TPU v7x, 32 devices: a whole 2x2x4 slice. The times are simulated.
32 devices in a mesh: groups: 2 (over y), cell: 4 (over z), gene: 2 (over x), sub: 2 (over core).
Axes of the slice: x: 2, y: 2, z: 4, core: 2. Of those that a mesh axis runs over, the one named last changes fastest.
Arguments:
- counts_x: bfloat16 [8192, 32768], P(('groups', 'cell'), ('gene', 'sub')), parts along dimension 0, may hold values from 0 to 4, as said below
- tile_mask: int32 [32, 128], P(('groups', 'cell'), ('gene', 'sub')), parts along dimension 0, may hold values from 0 to 1, as said below
- tile_counts: int32 [32, 128], P(('groups', 'cell'), ('gene', 'sub')), parts along dimension 0, may hold values from 1 to 4
- gene_factor: bfloat16 [512, 32768], P('groups', ('gene', 'sub')), parts along dimension 0, as said below
- prev_factor: bfloat16 [8192, 256], P(('groups', 'cell')), parts along dimension 0, may hold values from 0 to 2, as said below
Outputs:
- new_factor: bfloat16 [8192, 256], P(('groups', 'cell')), parts along dimension 0
- factor_gram: float32 [512, 256], P('groups'), parts along dimension 0
- data_products: float32 [65536, 256], P(('groups', 'gene', 'sub', 'cell')), parts along dimension 0
There are 2 independent parts, one for each index of `groups`. A program takes and returns all parts, laid end to end along the dimension named above; each array names one. Nothing has to cross between parts.
Inputs may be any that keep to these rules, and one draw needn't show every extreme that they name: `tile_mask`: 1 marks a stored tile, 0 an empty one. `gene_factor`: nonnegative. `counts_x`: nonnegative. `prev_factor`: nonnegative.
All inputs are finite; a program needn't handle non-finite values.
Results may differ from a plain program's by a relative error of at most 0.008.
Values may be sent and summed in bfloat16 or wider, within the bound.
No kernel may reach another device: no remote copies, remote signals or barrier semaphores. Data moves between devices by JAX's collectives and lax.ppermute only.
A program may use at most 192 MiB of HBM per device.

v0:
```python
import jax
import jax.numpy as jnp
from jax import lax
from jax.sharding import PartitionSpec as P

ITERS = 3


def scale_tiles(counts_x, tile_mask, tile_counts):
    row_tiles, gene_tiles = tile_mask.shape
    tile = counts_x.shape[0] // row_tiles
    factor = tile_mask.astype(jnp.float32) / tile_counts.astype(jnp.float32)
    shaped = counts_x.reshape(row_tiles, tile, gene_tiles, tile).astype(jnp.float32)
    return (shaped * factor[:, None, :, None]).reshape(counts_x.shape).astype(jnp.bfloat16)


def shifted_inverse(gram):
    width = gram.shape[0]
    rho = jnp.trace(gram) / width
    eye = jnp.eye(width, dtype=jnp.float32)
    lower = jnp.linalg.cholesky(gram + rho * eye)
    return (rho, jax.scipy.linalg.cho_solve((lower, True), eye))


def admm_steps(cross, inverse, rho, start_rows):
    zvalue = start_rows.astype(jnp.float32)
    uvalue = jnp.zeros_like(zvalue)
    for step in range(ITERS):
        vvalue = jnp.dot(cross + rho * (zvalue - uvalue), inverse, precision=lax.Precision.HIGHEST)
        zvalue = jnp.maximum(vvalue + uvalue, 0.0)
        uvalue = uvalue + vvalue - zvalue
    return zvalue.astype(jnp.bfloat16)


def contract_last(left, right):
    return lax.dot_general(
        left, right, (((1,), (1,)), ((), ())), preferred_element_type=jnp.float32
    )


def contract_first(left, right):
    return lax.dot_general(
        left, right, (((0,), (0,)), ((), ())), preferred_element_type=jnp.float32
    )


def shards(counts_x, tile_mask, tile_counts, gene_factor, prev_factor):
    scaled = scale_tiles(counts_x, tile_mask, tile_counts)
    gram_part = contract_last(gene_factor, gene_factor)
    cross_part = contract_last(scaled, gene_factor)
    gram = lax.psum(gram_part, ("gene", "sub"))
    cross = lax.psum(cross_part, ("gene", "sub"))
    rho, inverse = shifted_inverse(gram)
    new_factor = admm_steps(cross, inverse, rho, prev_factor)
    factor_gram = lax.psum(
        contract_first(new_factor, new_factor).astype(jnp.bfloat16), "cell"
    ).astype(jnp.float32)
    data_products = lax.psum_scatter(
        contract_first(scaled, new_factor), "cell", scatter_dimension=0, tiled=True
    )
    return (new_factor, factor_gram, data_products)


def solution(mesh):
    return jax.shard_map(
        shards,
        mesh=mesh,
        in_specs=(
            P(("groups", "cell"), ("gene", "sub")),
            P(("groups", "cell"), ("gene", "sub")),
            P(("groups", "cell"), ("gene", "sub")),
            P("groups", ("gene", "sub")),
            P(("groups", "cell"), None),
        ),
        out_specs=(
            P(("groups", "cell"), None),
            P("groups", None),
            P(("groups", "gene", "sub", "cell"), None),
        ),
        check_vma=False,
    )
```

profile of v0, /device:TPU:0, one launch (start us, length us, event | category | flops | bytes accessed | tf_op | source)
XLA Modules:
  0.0 373.4 jit_solution(18265011223606709398)
XLA Ops:
  7.2 0.0 all-reduce.7.cloned.1.call-start
  7.2 0.7 convert_divide_fusion
  7.9 4.8 %mul.31 = f32[4,256,32,256]{3,2,1,0:T(8,128)S(1)} broadcast(f32[4,32]{1,0:T(4,128)S(1)} %convert_divide_fusion), dimensions={0,2} | broadcast | bytes 33554944 | tf_op jit(solution)/shard_map/mul | solution.py:14
  12.8 0.0 copy-start
  12.8 34.0 %copy.16 = f32[128,8,32,256]{3,1,2,0:T(8,128)} copy(f32[128,8,32,256]{3,2,1,0:T(8,128)S(1)} %bitcast.45) | data formatting | bytes 67108864
  46.8 0.0 copy-done
  46.8 2.0 fusion.38
  48.7 0.0 copy-start.2
  48.7 19.8 %fusion.36 = f32[1024,256]{1,0:T(8,128)} fusion(bf16[256,8192]{1,0:T(8,128)(2,1)} %param.8, f32[1024,8192]{1,0:T(8,128)} %bitcast.43, bf16[1024,8192]{1,0:T(8,128)(2,1)} %param.5), kind=kOutput, calls=%fused_computation.65 | convolution fusion | flops 4320133120 | bytes 55574528 | tf_op jit(solution)/shard_map/dot_general | solution.py:36
  68.6 0.0 all-reduce.7.cloned.1.call-update
  68.6 0.2 all-reduce.5.cloned.1.call-start
  68.9 41.7 %all-reduce.7.cloned.1.call-done = (f32[1024,256]{1,0:T(8,128)}, f32[256,256]{0,1:T(8,128)}) async-done(((f32[1024,256]{1,0:T(8,128)}, f32[256,256]{0,1:T(8,128)}), (f32[1024,256]{1,0:T(8,128)}, f32[256,256]{0,1:T(8,128)})) %all-reduce.7.cloned.1.call-update) | async-done | bytes 1310736 | tf_op jit(solution)/shard_map/psum | solution.py:52
  110.5 1.6 select_reduce_fusion
  112.8 1.0 select_add_fusion
  113.8 0.1 copy.9
  113.9 1.0 fusion.19
  114.9 11.7 %cholesky.49 = f32[128,128]{1,0:T(8,128)S(1)} custom-call(f32[128,128]{1,0:T(8,128)S(1)} %cholesky.115), custom_call_target="Cholesky" | custom-call | tf_op jit(solution)/shard_map/jit(cholesky)/cholesky | solution.py:21
  126.7 9.8 %custom-call.18 = f32[1,128,128]{1,2,0:T(8,128)S(1)} custom-call(f32[1,128,128]{2,1,0:T(8,128)S(1)} %get-tuple-element.28), custom_call_target="InvertDiagBlocksLowerTriangular" | custom-call | tf_op jit(solution)/shard_map/jit(cholesky)/cholesky | solution.py:21
  136.5 0.2 fusion.22
  136.7 0.3 convolution_subtract_fusion.2
  137.0 11.7 %cholesky.103 = f32[128,128]{1,0:T(8,128)S(1)} custom-call(f32[128,128]{1,0:T(8,128)S(1)} %convolution_subtract_fusion.2), custom_call_target="Cholesky" | custom-call | tf_op jit(solution)/shard_map/jit(cholesky)/cholesky | solution.py:21
  148.7 0.1 copy.12
  148.8 0.1 copy.11
  148.9 0.1 copy.10
  149.0 0.6 compare_reduce_fusion
  151.1 0.1 triangular_solve.63
  151.1 4.4 %while.1 = (s32[]{:T(128)}, f32[256,256]{0,1:T(8,128)S(1)}, s32[2,2]{1,0:T(2,128)S(1)}, f32[2,128,128]{2,1,0:T(8,128)S(1)}, s32[]{:T(128)}) while((s32[]{:T(128)}, f32[256,256]{0,1:T(8,128)S(1)}, s32[2,2]{1,0:T(2,128)S(1)}, f32[2,128,128]{2,1,0:T(8,128)S(1)}, s32[]{:T(128)}) %tuple.26), condition=%wide.while_cond, body=%wide.while_body.sunk | while | flops 2 | bytes 393321 | solution.py:22
  151.3 0.6 fusion.53
  151.9 1.4 dynamic-slice.7
  153.3 0.1 copy.18
  153.4 0.6 fusion.53
  154.0 1.4 dynamic-slice.7
  155.4 0.1 copy.18
  155.5 19.7 %custom-call.19 = f32[2,128,128]{1,2,0:T(8,128)S(1)} custom-call(f32[2,128,128]{2,1,0:T(8,128)S(1)} %get-tuple-element.10), custom_call_target="InvertDiagBlocksLowerTriangular" | custom-call | tf_op jit(solution)/shard_map/jit(_cho_solve)/triangular_solve | solution.py:22
  175.2 0.3 fusion.20
  175.5 0.4 convolution_subtract_fusion.1
  175.9 0.3 fusion.27
  176.2 0.3 fusion.26
  176.5 0.3 convolution_subtract_fusion
  176.7 0.3 fusion.25
  177.0 0.0 copy-done.2
  177.0 2.2 fusion.10
  179.3 2.3 fusion
  181.6 2.3 fusion.3
  183.9 0.0 copy-start.1
  183.9 1.0 convolution_convert_fusion
  185.0 0.0 all-reduce.5.cloned.1.call-update
  185.0 0.0 reduce-scatter.2.cloned.1.call-start
  185.0 21.7 %fusion.35 = f32[8192,256]{1,0:T(8,128)} fusion(bf16[1024,256]{1,0:T(8,128)(2,1)S(1)} %fusion.3, f32[1024,8192]{1,0:T(8,128)} %bitcast.44, bf16[1024,8192]{1,0:T(8,128)(2,1)} %param.5), kind=kOutput, calls=%fused_computation.64 | convolution fusion | flops 4320133120 | bytes 59244544 | tf_op jit(solution)/shard_map/dot_general | solution.py:42
  206.7 0.0 copy-done.1
  206.7 0.0 reduce-scatter.2.cloned.1.call-update
  206.7 12.9 %all-reduce.5.cloned.1.call-done = bf16[256,256]{1,0:T(8,128)(2,1)} async-done(((bf16[256,256]{1,0:T(8,128)(2,1)}), bf16[256,256]{1,0:T(8,128)(2,1)}) %all-reduce.5.cloned.1.call-update) | async-done | bytes 131088 | tf_op jit(solution)/shard_map/psum | solution.py:55
  219.6 1.6 convert_element_type.33
  221.3 145.6 %reduce-scatter.2.cloned.1.call-done = f32[2048,256]{1,0:T(8,128)} async-done(((f32[8192,256]{1,0:T(8,128)}), f32[2048,256]{1,0:T(8,128)}) %reduce-scatter.2.cloned.1.call-update) | async-done | bytes 2097168 | tf_op jit(solution)/shard_map/reduce_scatter | solution.py:58
  (14 shorter events, 0.2 us)
Async XLA Ops:
  7.2 103.4 %all-reduce.7.cloned.1.call-start = ((), (), s32[]{:S(2)}) async-start(), calls=%async_computation.3 | async-start | bytes 2621440 | tf_op jit(solution)/shard_map/psum | solution.py:52
  12.8 34.0 %copy-start = (bf16[256,8192]{1,0:T(8,128)(2,1)S(1)}, bf16[256,8192]{1,0:T(8,128)(2,1)}, u32[]{:S(2)}) copy-start(bf16[256,8192]{1,0:T(8,128)(2,1)} %param.8) | copy-start | bytes 12582916
  48.7 128.3 %copy-start.2 = (bf16[1024,256]{1,0:T(8,128)(2,1)S(1)}, bf16[1024,256]{1,0:T(8,128)(2,1)}, u32[]{:S(2)}) copy-start(bf16[1024,256]{1,0:T(8,128)(2,1)} %param.9) | copy-start | bytes 1572868
  68.6 151.1 %all-reduce.5.cloned.1.call-start = ((), (), s32[]{:S(2)}) async-start(), calls=%async_computation.1 | async-start | bytes 262144 | tf_op jit(solution)/shard_map/psum | solution.py:55
  183.9 22.8 %copy-start.1 = (bf16[1024,256]{1,0:T(8,128)(2,1)}, bf16[1024,256]{1,0:T(8,128)(2,1)S(1)}, u32[]{:S(2)}) copy-start(bf16[1024,256]{1,0:T(8,128)(2,1)S(1)} %fusion.3) | copy-start | bytes 1572868
  185.0 181.9 %reduce-scatter.2.cloned.1.call-start = ((), (), s32[]{:S(2)}) async-start(), calls=%async_computation.2 | async-start | bytes 10485760 | tf_op jit(solution)/shard_map/reduce_scatter | solution.py:58
Sparse Core Ops, SparseCore 0:
  68.7 41.8 all-reduce.6
  185.1 34.5 all-reduce.4
  222.7 144.0 reduce-scatter.1
where the time goes:
time: 374 us; the launch traced here: 373 us
  waiting for transfers between devices  200 us (53%)
  other arithmetic  59.6 us (16%)
  matrix products  53.6 us (14%)
  local copies, waits for them, and re-layouts  43.5 us (12%)
  between operations  15.9 us (4%)
    reduce_scatter x1, waiting for transfers between devices, shards(): lax.psum_scatter(contract_first(scaled, new_factor), 'cell', scatter_dime...  146 us
    psum x1, waiting for transfers between devices, shards(): cross = lax.psum(cross_part, ('gene', 'sub'))  41.7 us
    unnamed x7, local copies, waits for them, and re-layouts  34 us
    another operation x6, other arithmetic, shifted_inverse(): lower = jnp.linalg.cholesky(gram + rho * eye)  34 us
    dot_general x2, matrix products, contract_first(): lax.dot_general(left, right, (((0,), (0,)), ((), ())), preferred_element_...  22.7 us
    dot_general x2, matrix products, contract_last(): lax.dot_general(left, right, (((1,), (1,)), ((), ())), preferred_element_...  21.8 us
    another operation x3, other arithmetic, shifted_inverse(): return (rho, jax.scipy.linalg.cho_solve((lower, True), eye))  19.7 us
    psum x1, waiting for transfers between devices, shards(): lax.psum(contract_first(new_factor, new_factor).astype(jnp.bfloat16), 'ce...  12.9 us
  transfers between devices with their start and end apart: 3, of which 3 were waited for; matrix products, arithmetic and copies ran while one was open for 6% of the time, Pallas kernels for 0%

commit v1 on v0

v1 whole, which is shorter than its diff:
```python
import functools

import jax
import jax.numpy as jnp
from jax import lax
from jax.experimental import pallas as pl
from jax.experimental.pallas import tpu as pltpu
from jax.sharding import PartitionSpec as P

ITERS = 3
F32 = jnp.float32
BF16 = jnp.bfloat16
VMEM_LIMIT = 48 * 1024 * 1024


def params():
    return pltpu.CompilerParams(vmem_limit_bytes=VMEM_LIMIT)


def cost(flops, bytes_accessed):
    return pl.CostEstimate(flops=flops, bytes_accessed=bytes_accessed, transcendentals=0)


def contract_last(left, right):
    return lax.dot_general(
        left, right, (((1,), (1,)), ((), ())), preferred_element_type=F32
    )


def cross_kernel(tile, meta, factor, counts, genes, theirs, mine, total):
    step = pl.program_id(0)
    row_tiles = counts.shape[0] // tile
    gene_tiles = counts.shape[1] // tile
    half = counts.shape[0] // 2
    for row in range(row_tiles):
        rows = pl.ds(row * tile, tile)
        parts = [
            (
                counts[rows, pl.ds(col * tile, tile)].astype(F32)
                * factor[row, step * gene_tiles + col]
            ).astype(BF16)
            for col in range(gene_tiles)
        ]
        part = contract_last(jnp.concatenate(parts, axis=1), genes[...])

        @pl.when(step == 0)
        def _(rows=rows, part=part):
            total[rows, :] = part

        @pl.when(step > 0)
        def _(rows=rows, part=part):
            total[rows, :] += part

    @pl.when(step == pl.num_programs(0) - 1)
    def _():
        sub = meta[0]
        mine[...] = total[pl.ds(pl.multiple_of(sub * half, half), half), :]
        theirs[...] = total[pl.ds(pl.multiple_of((1 - sub) * half, half), half), :]


def cross_parts(meta, factor, counts, genes, tile):
    rows, columns = counts.shape
    width = genes.shape[0]
    wide = min(1024, columns)
    half = jax.ShapeDtypeStruct((rows // 2, width), F32)
    return pl.pallas_call(
        functools.partial(cross_kernel, tile),
        out_shape=(half, half),
        grid_spec=pltpu.PrefetchScalarGridSpec(
            num_scalar_prefetch=1,
            grid=(columns // wide,),
            in_specs=[
                pl.BlockSpec(memory_space=pltpu.SMEM),
                pl.BlockSpec((rows, wide), lambda i, m: (0, i)),
                pl.BlockSpec((width, wide), lambda i, m: (0, i)),
            ],
            out_specs=(
                pl.BlockSpec((rows // 2, width), lambda i, m: (0, 0)),
                pl.BlockSpec((rows // 2, width), lambda i, m: (0, 0)),
            ),
            scratch_shapes=[pltpu.VMEM((rows, width), F32)],
        ),
        compiler_params=params(),
        cost_estimate=cost(2 * rows * columns * width, 2 * rows * columns),
        name="cross",
    )(meta, factor, counts, genes)


def halves(value):
    high = value.astype(BF16)
    return high, (value - high.astype(F32)).astype(BF16)


def product3(left, right):
    left_high, left_low = left
    right_high, right_low = right
    dot = functools.partial(jnp.dot, preferred_element_type=F32)
    return dot(left_high, right_high) + (
        dot(left_high, right_low) + dot(left_low, right_high)
    )


def inverse_kernel(gram_a, gram_b, inverse, rho_out):
    gram = gram_a[...] + gram_b[...]
    width = gram.shape[0]
    shape = (width, width)
    diagonal = lax.broadcasted_iota(jnp.int32, shape, 0) == lax.broadcasted_iota(
        jnp.int32, shape, 1
    )
    eye = jnp.where(diagonal, 1.0, 0.0).astype(F32)
    rho = jnp.sum(gram * eye) / width
    rho_out[0, 0] = rho
    scale = 1.0 / jnp.full((1, 1), rho, F32)
    matrix = gram * scale + eye
    low = 2.0 / (width + 2.0)
    guess = low * eye
    image = low * matrix
    first = True
    while True:
        low = low * (2.0 - low)
        gain = 2.0 / (1.0 + low)
        low = gain * low
        done = 1.0 - low < 2e-3
        step = halves(gain * (2.0 * eye - image))
        if first:
            guess = guess[0:1, 0:1] * (gain * (2.0 * eye - image))
        else:
            guess = product3(halves(guess), step)
        first = False
        if done:
            break
        image = product3(halves(image), step)
    rest = eye - jnp.dot(
        matrix, guess, preferred_element_type=F32, precision=lax.Precision.HIGHEST
    )
    rest_halves = halves(rest)
    series = rest + product3(rest_halves, rest_halves)
    inverse[...] = (guess + product3(halves(guess), halves(series))) * scale


def shifted_inverse(gram_a, gram_b):
    width = gram_a.shape[0]
    whole = pl.BlockSpec(memory_space=pltpu.VMEM)
    return pl.pallas_call(
        inverse_kernel,
        out_shape=(
            jax.ShapeDtypeStruct((width, width), F32),
            jax.ShapeDtypeStruct((1, 1), F32),
        ),
        in_specs=[whole, whole],
        out_specs=(whole, pl.BlockSpec(memory_space=pltpu.SMEM)),
        compiler_params=params(),
        cost_estimate=cost(2 * 60 * width**3, 12 * width**2),
        name="inverse",
    )(gram_a, gram_b)


def admm_kernel(meta, rho_ref, cross_a, cross_b, inverse, start, rows_out, columns_out):
    rho = rho_ref[0, 0]
    cross = cross_a[...] + cross_b[...]
    inverse_halves = halves(inverse[...])
    zvalue = start[...].astype(F32)
    uvalue = jnp.zeros_like(zvalue)
    for _ in range(ITERS):
        vvalue = product3(halves(cross + rho * (zvalue - uvalue)), inverse_halves)
        zvalue = jnp.maximum(vvalue + uvalue, 0.0)
        uvalue = uvalue + vvalue - zvalue
    rows_out[...] = zvalue.astype(BF16)
    columns_out[...] = zvalue.T.astype(BF16)


def admm(meta, rho, cross_a, cross_b, inverse, start):
    rows, width = cross_a.shape
    tall = lambda: pl.BlockSpec((rows, width), lambda i, m: (0, 0))
    return pl.pallas_call(
        admm_kernel,
        out_shape=(
            jax.ShapeDtypeStruct((rows, width), BF16),
            jax.ShapeDtypeStruct((width, rows), BF16),
        ),
        grid_spec=pltpu.PrefetchScalarGridSpec(
            num_scalar_prefetch=1,
            grid=(1,),
            in_specs=[
                pl.BlockSpec(memory_space=pltpu.SMEM),
                tall(),
                tall(),
                pl.BlockSpec((width, width), lambda i, m: (0, 0)),
                pl.BlockSpec((rows, width), lambda i, m: (m[0], 0)),
            ],
            out_specs=(
                tall(),
                pl.BlockSpec((width, rows), lambda i, m: (0, 0)),
            ),
        ),
        compiler_params=params(),
        cost_estimate=cost(2 * 9 * rows * width**2, 12 * rows * width),
        name="admm",
    )(meta, rho, cross_a, cross_b, inverse, start)


def chunk_product(tile, gene, meta, factor, counts, own, other):
    half = counts.shape[0] // 2
    sub = meta[0]
    column = gene // tile
    total = None
    for first, left in ((sub, own), (1 - sub, other)):
        parts = [
            (
                counts[pl.ds(pl.multiple_of(first * half + r * tile, tile), tile), :].astype(F32)
                * factor[first * (half // tile) + r, column]
            ).astype(BF16)
            for r in range(half // tile)
        ]
        part = jnp.dot(
            left[...], jnp.concatenate(parts, axis=0), preferred_element_type=F32
        )
        total = part if total is None else total + part
    return total


class Plan:
    def __init__(self, cells, columns, tile):
        self.cells = cells
        self.block = columns // cells
        self.chunks = 2 if self.block % (4 * tile) == 0 else 1
        self.chunk = self.block // self.chunks
        self.wide = min(tile, self.chunk)
        self.steps = self.chunk // self.wide

    def valid(self, shift, meta):
        target = meta[1] + shift
        return jnp.logical_and(target >= 0, target < self.cells)

    def place(self, shift, chunk, step, meta):
        target = lax.rem(meta[1] + shift + self.cells, self.cells)
        place = target * (self.block // self.wide) + chunk * self.steps + step
        return jnp.where(self.valid(shift, meta), place, 0)


def send_kernel(plan, tile, shift, chunk, with_arrived, meta, factor, counts, own, other, *refs):
    out = refs[-1]

    @pl.when(plan.valid(shift, meta))
    def _():
        gene = plan.place(shift, chunk, pl.program_id(0), meta) * plan.wide
        total = chunk_product(tile, gene, meta, factor, counts, own, other)
        if with_arrived:
            total = total + refs[0][...].astype(F32)
        out[...] = total.astype(BF16)


def send_chunk(plan, tile, shift, chunk, meta, factor, counts, own, other, arrived):
    rows = counts.shape[0]
    width = own.shape[0]
    wide = plan.wide
    halved = lambda: pl.BlockSpec((width, rows // 2), lambda i, m: (0, 0))
    piece = lambda: pl.BlockSpec((width, wide), lambda i, m: (0, i))
    extra = [] if arrived is None else [arrived]
    return pl.pallas_call(
        functools.partial(send_kernel, plan, tile, shift, chunk, arrived is not None),
        out_shape=jax.ShapeDtypeStruct((width, plan.chunk), BF16),
        grid_spec=pltpu.PrefetchScalarGridSpec(
            num_scalar_prefetch=1,
            grid=(plan.steps,),
            in_specs=[
                pl.BlockSpec(memory_space=pltpu.SMEM),
                pl.BlockSpec(
                    (rows, wide), lambda i, m: (0, plan.place(shift, chunk, i, m))
                ),
                halved(),
                halved(),
            ]
            + [piece() for _ in extra],
            out_specs=piece(),
        ),
        compiler_params=params(),
        cost_estimate=cost(2 * rows * width * plan.chunk, 2 * rows * plan.chunk),
        name="products_send",
    )(meta, factor, counts, own, other, *extra)


def keep_kernel(plan, tile, chunk, meta, factor, counts, own, other, from_left, from_right, *refs):
    gene = plan.place(0, chunk, pl.program_id(0), meta) * plan.wide
    total = chunk_product(tile, gene, meta, factor, counts, own, other)
    total = total + (from_left[...].astype(F32) + from_right[...].astype(F32))
    refs[-1][...] = total.T


def keep_chunk(plan, tile, chunk, meta, factor, counts, own, other, from_left, from_right, out):
    rows = counts.shape[0]
    width = own.shape[0]
    wide = plan.wide
    halved = lambda: pl.BlockSpec((width, rows // 2), lambda i, m: (0, 0))
    piece = lambda: pl.BlockSpec((width, wide), lambda i, m: (0, i))
    extra = [] if out is None else [out]
    return pl.pallas_call(
        functools.partial(keep_kernel, plan, tile, chunk),
        out_shape=jax.ShapeDtypeStruct((plan.block, width), F32),
        grid_spec=pltpu.PrefetchScalarGridSpec(
            num_scalar_prefetch=1,
            grid=(plan.steps,),
            in_specs=[
                pl.BlockSpec(memory_space=pltpu.SMEM),
                pl.BlockSpec(
                    (rows, wide), lambda i, m: (0, plan.place(0, chunk, i, m))
                ),
                halved(),
                halved(),
                piece(),
                piece(),
            ]
            + [pl.BlockSpec(memory_space=pl.ANY) for _ in extra],
            out_specs=pl.BlockSpec((wide, width), lambda i, m: (chunk * plan.steps + i, 0)),
        ),
        input_output_aliases={7: 0} if extra else {},
        compiler_params=params(),
        cost_estimate=cost(2 * rows * width * plan.chunk, 2 * rows * plan.chunk),
        name="products_keep",
    )(meta, factor, counts, own, other, from_left, from_right, *extra)


def swap(value, axis, size, step):
    return lax.ppermute(value, axis, [(i, i ^ step) for i in range(size)])


def pair_sums(value, axis, size, last):
    step = 1
    while step < size:
        arrived = swap(value, axis, size, step)
        step *= 2
        if step >= size and not last:
            return value, arrived
        value = value + arrived
    return value


def shards(sizes, counts, tile_mask, tile_counts, gene_factor, prev_factor):
    cells, genes, subs = sizes
    rows, columns = counts.shape
    width = gene_factor.shape[0]
    tile = rows // tile_mask.shape[0]
    sub = lax.axis_index("sub")
    cell = lax.axis_index("cell")
    meta = jnp.stack([sub, cell]).astype(jnp.int32)
    factor = tile_mask.astype(F32) / tile_counts.astype(F32)

    gram = contract_last(gene_factor, gene_factor)
    gram = pair_sums(gram, "sub", subs, True)
    gram_a, gram_b = pair_sums(gram, "gene", genes, False)
    theirs, mine = cross_parts(meta, factor, counts, gene_factor, tile)
    cross = mine + swap(theirs, "sub", subs, 1)
    cross_a, cross_b = pair_sums(cross, "gene", genes, False)
    inverse, rho = shifted_inverse(gram_a, gram_b)
    own_rows, own = admm(meta, rho, cross_a, cross_b, inverse, prev_factor)
    other = swap(own, "sub", subs, 1)

    plan = Plan(cells, columns, tile)
    rightward = [(i, i + 1) for i in range(cells - 1)]
    leftward = [(i + 1, i) for i in range(cells - 1)]
    from_left = [None] * plan.chunks
    from_right = [None] * plan.chunks
    for phase in range(1, cells):
        for chunk in range(plan.chunks):
            right = send_chunk(
                plan, tile, cells - phase, chunk, meta, factor, counts, own, other, from_left[chunk]
            )
            left = send_chunk(
                plan, tile, phase - cells, chunk, meta, factor, counts, own, other, from_right[chunk]
            )
            pairs = [pair for pair in rightward if pair[0] < phase]
            from_left[chunk] = lax.ppermute(right, "cell", pairs)
            pairs = [pair for pair in leftward if pair[0] >= cells - phase]
            from_right[chunk] = lax.ppermute(left, "cell", pairs)
    data_products = None
    for chunk in range(plan.chunks):
        data_products = keep_chunk(
            plan, tile, chunk, meta, factor, counts, own, other,
            from_left[chunk], from_right[chunk], data_products,
        )

    other_rows = swap(own_rows, "sub", subs, 1)
    new_factor = jnp.where(
        sub == 0,
        jnp.concatenate([own_rows, other_rows], axis=0),
        jnp.concatenate([other_rows, own_rows], axis=0),
    )
    share = width // (genes * subs)
    first = (lax.axis_index("gene") * subs + sub) * share
    gram_rows = contract_last(lax.dynamic_slice_in_dim(own, first, share, 0), own)
    gram_rows += contract_last(lax.dynamic_slice_in_dim(other, first, share, 0), other)
    gram_rows = pair_sums(gram_rows, "cell", cells, True)
    factor_gram = lax.all_gather(gram_rows, ("gene", "sub"), axis=0, tiled=True)
    return (new_factor, factor_gram, data_products)


def solution(mesh):
    sizes = (mesh.shape["cell"], mesh.shape["gene"], mesh.shape["sub"])
    return jax.shard_map(
        functools.partial(shards, sizes),
        mesh=mesh,
        in_specs=(
            P(("groups", "cell"), ("gene", "sub")),
            P(("groups", "cell"), ("gene", "sub")),
            P(("groups", "cell"), ("gene", "sub")),
            P("groups", ("gene", "sub")),
            P(("groups", "cell"), None),
        ),
        out_specs=(
            P(("groups", "cell"), None),
            P("groups", None),
            P(("groups", "gene", "sub", "cell"), None),
        ),
        check_vma=False,
    )
```

time: 374 us -> 156 us (0.42)
  waiting for transfers between devices: 200 us -> 28.2 us
  Pallas kernels: 0 us -> 73 us
  other arithmetic: 59.6 us -> 2.92 us
  matrix products: 53.6 us -> 1.69 us
  local copies, waits for them, and re-layouts: 43.5 us -> 2.9 us
  starting transfers between devices: 0.3 us -> 37.4 us
  between operations: 15.9 us -> 0.94 us
  blocking collectives: 0 us -> 5.79 us
    reduce_scatter x1 -> x0, waiting for transfers between devices: 146 us -> none  [shards(): lax.psum_scatter(contract_first(scaled, new_factor), 'cell', scatter_dime...]
    pallas_call x0 -> x17, Pallas kernels: none -> 73 us  [the longest x12 39.4 us: send_chunk(): pl.pallas_call(functools.partial(send_kernel, plan, tile, shift, chunk, a...]
    psum x2 -> x0, waiting for transfers between devices: 54.6 us -> none  [the longest x1 41.7 us: shards(): cross = lax.psum(cross_part, ('gene', 'sub'))]
    another operation x9 -> x1, other arithmetic: 53.7 us -> 0.08 us  [shards(): meta = jnp.stack([sub, cell]).astype(jnp.int32)]
    ppermute x0 -> x20, starting transfers between devices: none -> 37.4 us  [the longest x6 24.2 us: shards(): from_left[chunk] = lax.ppermute(right, 'cell', pairs)]
    unnamed x7 -> x5, local copies, waits for them, and re-layouts: 34 us -> 2.9 us
    dot_general x5 -> x0, matrix products: 29.6 us -> none  [the longest x2 22.7 us: contract_first(): lax.dot_general(left, right, (((0,), (0,)), ((), ())), preferred_element_...]
    ppermute x0 -> x20, waiting for transfers between devices: none -> 28.2 us  [the longest x8 26.6 us: swap(): return lax.ppermute(value, axis, [(i, i ^ step) for i in range(size)])]
  transfers between devices with their start and end apart: 3 -> 20, of which waited for: 3 -> 6; matrix products, arithmetic and copies ran while one was open for 6% -> 3% of each run, Pallas kernels for 0% -> 29%
where the time goes in v1:
time: 156 us; the launch traced here: 153 us
  Pallas kernels  73 us (47%)
  starting transfers between devices  37.4 us (24%)
  waiting for transfers between devices  28.2 us (18%)
  blocking collectives  5.79 us (4%)
  other arithmetic  2.92 us (2%)
  local copies, waits for them, and re-layouts  2.9 us (2%)
  matrix products  1.69 us (1%)
    pallas_call x12, Pallas kernels, send_chunk(): pl.pallas_call(functools.partial(send_kernel, plan, tile, shift, chunk, a...  39.4 us
    ppermute x8, waiting for transfers between devices, swap(): return lax.ppermute(value, axis, [(i, i ^ step) for i in range(size)])  26.6 us
    ppermute x6, starting transfers between devices, shards(): from_left[chunk] = lax.ppermute(right, 'cell', pairs)  24.2 us
    pallas_call x1, Pallas kernels, cross_parts(): pl.pallas_call(functools.partial(cross_kernel, tile), out_shape=(half, ha...  17.7 us
    pallas_call x2, Pallas kernels, keep_chunk(): pl.pallas_call(functools.partial(keep_kernel, plan, tile, chunk), out_sha...  9.92 us
    ppermute x8, starting transfers between devices, swap(): return lax.ppermute(value, axis, [(i, i ^ step) for i in range(size)])  7.09 us
    ppermute x6, starting transfers between devices, shards(): from_right[chunk] = lax.ppermute(left, 'cell', pairs)  6.12 us
    all_gather x1, blocking collectives, shards(): factor_gram = lax.all_gather(gram_rows, ('gene', 'sub'), axis=0, tiled=True)  5.79 us
  transfers between devices with their start and end apart: 20, of which 6 were waited for; matrix products, arithmetic and copies ran while one was open for 3% of the time, Pallas kernels for 29%

profile of v1, /device:TPU:0, one launch (start us, length us, event | category | flops | bytes accessed | tf_op | source)
XLA Modules:
  0.0 152.9 jit_solution(17897228685062348107)
XLA Ops:
  0.6 0.1 pad_add_fusion.meta
  0.7 0.7 convert_divide_fusion.factor
  1.4 2.2 %copy-done = bf16[256,8192]{1,0:T(8,128)(2,1)S(1)} copy-done((bf16[256,8192]{1,0:T(8,128)(2,1)S(1)}, bf16[256,8192]{1,0:T(8,128)(2,1)}, u32[]{:S(2)}) %copy-start) | copy-done | bytes 4194328
  3.6 17.7 %cross.1 = (f32[512,256]{1,0:T(8,128)S(1)}, f32[512,256]{1,0:T(8,128)S(1)}) custom-call(s32[2]{0:T(128)S(1)} %pad_add_fusion.meta, f32[4,32]{1,0:T(4,128)S(1)} %convert_divide_fusion.factor, bf16[1024,8192]{1,0:T(8,128)(2,1)} %counts.29, bf16[256,8192]{1,0:T(8,128)(2,1)S(1)} %copy-done), custom_call_target="tpu_custom_call" | custom-call | flops 4294967296 | bytes 16777216 | tf_op jit(solution)/shard_map/cross/pallas_call | solution.py:66
  21.4 0.5 collective-permute-start.2
  21.9 1.3 fusion.5
  23.2 0.1 collective-permute-start
  23.3 0.1 collective-permute-done.2
  23.4 0.1 add.23.cross_a
  23.5 0.0 copy-start.1
  23.5 2.9 %collective-permute-start.3 = (f32[512,256]{1,0:T(8,128)S(1)}, f32[512,256]{1,0:T(8,128)S(1)}, u32[]{:S(2)}, u32[]{:S(2)}) collective-permute-start(f32[512,256]{1,0:T(8,128)S(1)} %add.23.cross_a), channel_id=1, source_target_pairs={{0,2},{2,0},{1,3},{3,1},{4,6},{6,4},{5,7},{7,5},{8,10},{10,8},{9,1... | collective-permute-start | bytes 1572872 | tf_op jit(solution)/shard_map/ppermute | solution.py:324
  26.4 0.0 collective-permute-done
  26.5 1.0 collective-permute-start.1
  27.5 16.8 %collective-permute-done.1.gram_b = f32[256,256]{1,0:T(8,128)S(1)} collective-permute-done((f32[256,256]{1,0:T(8,128)S(1)}, f32[256,256]{1,0:T(8,128)S(1)}, u32[]{:S(2)}, u32[]{:S(2)}) %collective-permute-start.1) | collective-permute-done | bytes 262176 | tf_op jit(solution)/shard_map/ppermute | solution.py:324
  44.3 3.5 %inverse.1 = (f32[256,256]{1,0:T(8,128)S(1)}, f32[1,1]{1,0:T(1,128)}) custom-call(f32[256,256]{1,0:T(8,128)S(1)} %add.22.gram_a, f32[256,256]{1,0:T(8,128)S(1)} %collective-permute-done.1.gram_b), custom_call_target="tpu_custom_call" | custom-call | flops 2013265920 | bytes 786432 | tf_op jit(solution)/shard_map/inverse/pallas_call | solution.py:144
  47.8 0.0 collective-permute-done.3.cross_b
  47.8 2.5 %admm.1 = (bf16[512,256]{1,0:T(8,128)(2,1)S(1)}, bf16[256,512]{1,0:T(8,128)(2,1)S(1)}) custom-call(s32[2]{0:T(128)S(1)} %pad_add_fusion.meta, f32[1,1]{1,0:T(1,128)} %get-tuple-element.9.rho_ref, f32[512,256]{1,0:T(8,128)S(1)} %add.23.cross_a, f32[512,256]{1,0:T(8,128)S(1)} %collective-permute-done.3.cross_b, f32[256,256]{1,0:T(8,128)S(1)} %get-tuple-element.12.inverse, ...), custom_call_target="tpu_custom_call" | custom-call | flops 603979776 | bytes 1572864 | tf_op jit(solution)/shard_map/admm/pallas_call | solution.py:175
  50.3 0.1 collective-permute-start.5
  50.4 1.5 collective-permute-done.5.other
  51.9 3.0 %products_send.21 = bf16[256,1024]{1,0:T(8,128)(2,1)} custom-call(s32[2]{0:T(128)S(1)} %pad_add_fusion.meta, f32[4,32]{1,0:T(4,128)S(1)} %convert_divide_fusion.factor, bf16[1024,8192]{1,0:T(8,128)(2,1)} %counts.29, bf16[256,512]{1,0:T(8,128)(2,1)S(1)} %get-tuple-element.14.own, bf16[256,512]{1,0:T(8,128)(2,1)S(1)} %collective-permute-done.5.other), custom_call_target="tpu_custom_call" | custom-call | flops 536870912 | bytes 2097152 | tf_op jit(solution)/shard_map/products_send/pallas_call | solution.py:260
  54.9 1.5 collective-permute-start.17
  56.4 4.7 %products_send.18 = bf16[256,1024]{1,0:T(8,128)(2,1)} custom-call(s32[2]{0:T(128)S(1)} %pad_add_fusion.meta, f32[4,32]{1,0:T(4,128)S(1)} %convert_divide_fusion.factor, bf16[1024,8192]{1,0:T(8,128)(2,1)} %counts.29, bf16[256,512]{1,0:T(8,128)(2,1)S(1)} %get-tuple-element.14.own, bf16[256,512]{1,0:T(8,128)(2,1)S(1)} %collective-permute-done.5.other), custom_call_target="tpu_custom_call" | custom-call | flops 536870912 | bytes 2097152 | tf_op jit(solution)/shard_map/products_send/pallas_call | solution.py:260
  61.1 2.1 %collective-permute-start.14 = (bf16[256,1024]{1,0:T(8,128)(2,1)}, bf16[256,1024]{1,0:T(8,128)(2,1)S(1)}, u32[]{:S(2)}, u32[]{:S(2)}) collective-permute-start(bf16[256,1024]{1,0:T(8,128)(2,1)} %products_send.18), channel_id=1, source_target_pairs={{0,4},{1,5},{2,6},{3,7},{16,20},{17,21},{18,22},{19,23}} | collective-permute-start | bytes 1572872 | tf_op jit(solution)/shard_map/ppermute | solution.py:372
  63.1 1.8 %products_send.15 = bf16[256,1024]{1,0:T(8,128)(2,1)S(1)} custom-call(s32[2]{0:T(128)S(1)} %pad_add_fusion.meta, f32[4,32]{1,0:T(4,128)S(1)} %convert_divide_fusion.factor, bf16[1024,8192]{1,0:T(8,128)(2,1)} %counts.29, bf16[256,512]{1,0:T(8,128)(2,1)S(1)} %get-tuple-element.14.own, bf16[256,512]{1,0:T(8,128)(2,1)S(1)} %collective-permute-done.5.other), custom_call_target="tpu_custom_call" | custom-call | flops 536870912 | bytes 2097152 | tf_op jit(solution)/shard_map/products_send/pallas_call | solution.py:260
  64.9 0.7 collective-permute-start.11
  65.6 3.8 %products_send.12 = bf16[256,1024]{1,0:T(8,128)(2,1)S(1)} custom-call(s32[2]{0:T(128)S(1)} %pad_add_fusion.meta, f32[4,32]{1,0:T(4,128)S(1)} %convert_divide_fusion.factor, bf16[1024,8192]{1,0:T(8,128)(2,1)} %counts.29, bf16[256,512]{1,0:T(8,128)(2,1)S(1)} %get-tuple-element.14.own, bf16[256,512]{1,0:T(8,128)(2,1)S(1)} %collective-permute-done.5.other), custom_call_target="tpu_custom_call" | custom-call | flops 536870912 | bytes 2097152 | tf_op jit(solution)/shard_map/products_send/pallas_call | solution.py:260
  69.5 1.3 collective-permute-start.8
  70.8 0.1 collective-permute-start.4
  70.9 0.0 collective-permute-done.17.refs_0_
  70.9 2.7 %products_send.22 = bf16[256,1024]{1,0:T(8,128)(2,1)S(1)} custom-call(s32[2]{0:T(128)S(1)} %pad_add_fusion.meta, f32[4,32]{1,0:T(4,128)S(1)} %convert_divide_fusion.factor, bf16[1024,8192]{1,0:T(8,128)(2,1)} %counts.29, bf16[256,512]{1,0:T(8,128)(2,1)S(1)} %get-tuple-element.14.own, bf16[256,512]{1,0:T(8,128)(2,1)S(1)} %collective-permute-done.5.other, ...), custom_call_target="tpu_custom_call" | custom-call | flops 536870912 | bytes 2097152 | tf_op jit(solution)/shard_map/products_send/pallas_call | solution.py:260
  73.7 0.7 collective-permute-start.18
  74.4 1.3 collective-permute-done.14.refs_0_
  75.7 3.9 %products_send.19 = bf16[256,1024]{1,0:T(8,128)(2,1)S(1)} custom-call(s32[2]{0:T(128)S(1)} %pad_add_fusion.meta, f32[4,32]{1,0:T(4,128)S(1)} %convert_divide_fusion.factor, bf16[1024,8192]{1,0:T(8,128)(2,1)} %counts.29, bf16[256,512]{1,0:T(8,128)(2,1)S(1)} %get-tuple-element.14.own, bf16[256,512]{1,0:T(8,128)(2,1)S(1)} %collective-permute-done.5.other, ...), custom_call_target="tpu_custom_call" | custom-call | flops 536870912 | bytes 2097152 | tf_op jit(solution)/shard_map/products_send/pallas_call | solution.py:260
  79.6 4.3 %collective-permute-start.15 = (bf16[256,1024]{1,0:T(8,128)(2,1)S(1)}, bf16[256,1024]{1,0:T(8,128)(2,1)S(1)}, u32[]{:S(2)}, u32[]{:S(2)}) collective-permute-start(bf16[256,1024]{1,0:T(8,128)(2,1)S(1)} %products_send.19), channel_id=1, source_target_pairs={{0,4},{4,8},{1,5},{5,9},{2,6},{6,10},{3,7},{7,11},{16,20},{20,24},... | collective-permute-start | bytes 1572872 | tf_op jit(solution)/shard_map/ppermute | solution.py:372
  83.9 0.0 collective-permute-done.11.refs_0_
  83.9 1.9 %products_send.16 = bf16[256,1024]{1,0:T(8,128)(2,1)S(1)} custom-call(s32[2]{0:T(128)S(1)} %pad_add_fusion.meta, f32[4,32]{1,0:T(4,128)S(1)} %convert_divide_fusion.factor, bf16[1024,8192]{1,0:T(8,128)(2,1)} %counts.29, bf16[256,512]{1,0:T(8,128)(2,1)S(1)} %get-tuple-element.14.own, bf16[256,512]{1,0:T(8,128)(2,1)S(1)} %collective-permute-done.5.other, ...), custom_call_target="tpu_custom_call" | custom-call | flops 536870912 | bytes 2097152 | tf_op jit(solution)/shard_map/products_send/pallas_call | solution.py:260
  85.8 0.7 collective-permute-start.12
  86.5 0.3 collective-permute-done.8.refs_0_
  86.8 3.9 %products_send.13 = bf16[256,1024]{1,0:T(8,128)(2,1)S(1)} custom-call(s32[2]{0:T(128)S(1)} %pad_add_fusion.meta, f32[4,32]{1,0:T(4,128)S(1)} %convert_divide_fusion.factor, bf16[1024,8192]{1,0:T(8,128)(2,1)} %counts.29, bf16[256,512]{1,0:T(8,128)(2,1)S(1)} %get-tuple-element.14.own, bf16[256,512]{1,0:T(8,128)(2,1)S(1)} %collective-permute-done.5.other, ...), custom_call_target="tpu_custom_call" | custom-call | flops 536870912 | bytes 2097152 | tf_op jit(solution)/shard_map/products_send/pallas_call | solution.py:260
  90.7 4.4 %collective-permute-start.9 = (bf16[256,1024]{1,0:T(8,128)(2,1)S(1)}, bf16[256,1024]{1,0:T(8,128)(2,1)S(1)}, u32[]{:S(2)}, u32[]{:S(2)}) collective-permute-start(bf16[256,1024]{1,0:T(8,128)(2,1)S(1)} %products_send.13), channel_id=1, source_target_pairs={{0,4},{4,8},{1,5},{5,9},{2,6},{6,10},{3,7},{7,11},{16,20},{20,24},... | collective-permute-start | bytes 1572872 | tf_op jit(solution)/shard_map/ppermute | solution.py:372
  95.1 0.2 fusion
  95.3 0.2 convolution_add_fusion
  95.5 0.0 collective-permute-done.18.refs_0_
  95.6 1.6 %collective-permute-start.6 = (f32[64,256]{1,0:T(8,128)S(1)}, f32[64,256]{1,0:T(8,128)S(1)}, u32[]{:S(2)}, u32[]{:S(2)}) collective-permute-start(f32[64,256]{1,0:T(8,128)S(1)} %convolution_add_fusion), channel_id=1, source_target_pairs={{0,4},{4,0},{8,12},{12,8},{1,5},{5,1},{9,13},{13,9},{2,6},{6,2},{1... | collective-permute-start | bytes 196616 | tf_op jit(solution)/shard_map/ppermute | solution.py:324
  97.2 1.9 %products_send.23 = bf16[256,1024]{1,0:T(8,128)(2,1)S(1)} custom-call(s32[2]{0:T(128)S(1)} %pad_add_fusion.meta, f32[4,32]{1,0:T(4,128)S(1)} %convert_divide_fusion.factor, bf16[1024,8192]{1,0:T(8,128)(2,1)} %counts.29, bf16[256,512]{1,0:T(8,128)(2,1)S(1)} %get-tuple-element.14.own, bf16[256,512]{1,0:T(8,128)(2,1)S(1)} %collective-permute-done.5.other, ...), custom_call_target="tpu_custom_call" | custom-call | flops 536870912 | bytes 2097152 | tf_op jit(solution)/shard_map/products_send/pallas_call | solution.py:260
  99.1 0.0 collective-permute-done.15.refs_0_
  99.1 1.3 collective-permute-start.19
  100.4 3.9 %products_send.20 = bf16[256,1024]{1,0:T(8,128)(2,1)S(1)} custom-call(s32[2]{0:T(128)S(1)} %pad_add_fusion.meta, f32[4,32]{1,0:T(4,128)S(1)} %convert_divide_fusion.factor, bf16[1024,8192]{1,0:T(8,128)(2,1)} %counts.29, bf16[256,512]{1,0:T(8,128)(2,1)S(1)} %get-tuple-element.14.own, bf16[256,512]{1,0:T(8,128)(2,1)S(1)} %collective-permute-done.5.other, ...), custom_call_target="tpu_custom_call" | custom-call | flops 536870912 | bytes 2097152 | tf_op jit(solution)/shard_map/products_send/pallas_call | solution.py:260
  104.3 0.0 collective-permute-done.12.refs_0_
  104.3 5.0 %collective-permute-start.16 = (bf16[256,1024]{1,0:T(8,128)(2,1)S(1)}, bf16[256,1024]{1,0:T(8,128)(2,1)S(1)}, u32[]{:S(2)}, u32[]{:S(2)}) collective-permute-start(bf16[256,1024]{1,0:T(8,128)(2,1)S(1)} %products_send.20), channel_id=1, source_target_pairs={{0,4},{4,8},{8,12},{1,5},{5,9},{9,13},{2,6},{6,10},{10,14},{3,7},{... | collective-permute-start | bytes 1572872 | tf_op jit(solution)/shard_map/ppermute | solution.py:372
  109.3 3.1 %products_send.17 = bf16[256,1024]{1,0:T(8,128)(2,1)} custom-call(s32[2]{0:T(128)S(1)} %pad_add_fusion.meta, f32[4,32]{1,0:T(4,128)S(1)} %convert_divide_fusion.factor, bf16[1024,8192]{1,0:T(8,128)(2,1)} %counts.29, bf16[256,512]{1,0:T(8,128)(2,1)S(1)} %get-tuple-element.14.own, bf16[256,512]{1,0:T(8,128)(2,1)S(1)} %collective-permute-done.5.other, ...), custom_call_target="tpu_custom_call" | custom-call | flops 536870912 | bytes 2097152 | tf_op jit(solution)/shard_map/products_send/pallas_call | solution.py:260
  112.4 1.3 collective-permute-start.13
  113.7 4.7 %products_send.14 = bf16[256,1024]{1,0:T(8,128)(2,1)} custom-call(s32[2]{0:T(128)S(1)} %pad_add_fusion.meta, f32[4,32]{1,0:T(4,128)S(1)} %convert_divide_fusion.factor, bf16[1024,8192]{1,0:T(8,128)(2,1)} %counts.29, bf16[256,512]{1,0:T(8,128)(2,1)S(1)} %get-tuple-element.14.own, bf16[256,512]{1,0:T(8,128)(2,1)S(1)} %collective-permute-done.5.other, ...), custom_call_target="tpu_custom_call" | custom-call | flops 536870912 | bytes 2097152 | tf_op jit(solution)/shard_map/products_send/pallas_call | solution.py:260
  118.5 7.0 %collective-permute-start.10 = (bf16[256,1024]{1,0:T(8,128)(2,1)}, bf16[256,1024]{1,0:T(8,128)(2,1)}, u32[]{:S(2)}, u32[]{:S(2)}) collective-permute-start(bf16[256,1024]{1,0:T(8,128)(2,1)} %products_send.14), channel_id=1, source_target_pairs={{0,4},{4,8},{8,12},{1,5},{5,9},{9,13},{2,6},{6,10},{10,14},{3,7},{... | collective-permute-start | bytes 1572872 | tf_op jit(solution)/shard_map/ppermute | solution.py:372
  125.5 0.7 collective-permute-start.7
  126.3 2.0 %maximum_select_fusion = bf16[1024,256]{1,0:T(8,128)(2,1)} fusion(bf16[512,256]{1,0:T(8,128)(2,1)} %collective-permute-done.4, bf16[512,256]{1,0:T(8,128)(2,1)S(1)} %get-tuple-element.13, pred[]{:T(512)S(6)} %eq.3), kind=kLoop, calls=%fused_computation.1 | loop fusion | flops 2359296 | bytes 1048577 | tf_op jit(solution)/shard_map/jit(_where)/select_n | solution.py:383
  128.3 8.2 %collective-permute-done.7 = f32[64,256]{1,0:T(8,128)S(1)} collective-permute-done((f32[64,256]{1,0:T(8,128)S(1)}, f32[64,256]{1,0:T(8,128)S(1)}, u32[]{:S(2)}, u32[]{:S(2)}) %collective-permute-start.7) | collective-permute-done | bytes 65568 | tf_op jit(solution)/shard_map/ppermute | solution.py:324
  136.5 5.8 %all_gather.3 = f32[256,256]{1,0:T(8,128)S(1)} all-gather(f32[64,256]{1,0:T(8,128)S(1)} %add.28), channel_id=1, replica_groups=mesh['groups'=2,'cell'=4,'gene'=2,'sub'=2] {'gene','sub'}, dimensions={0}, use_global_device_ids=true | all-gather | bytes 327680 | tf_op jit(solution)/shard_map/all_gather | solution.py:393
  142.3 0.0 collective-permute-done.19.from_right
  142.3 0.0 collective-permute-done.16.from_left
  142.3 4.9 %products_keep.2.refs_0_ = f32[2048,256]{1,0:T(8,128)} custom-call(s32[2]{0:T(128)S(1)} %pad_add_fusion.meta, f32[4,32]{1,0:T(4,128)S(1)} %convert_divide_fusion.factor, bf16[1024,8192]{1,0:T(8,128)(2,1)} %counts.29, bf16[256,512]{1,0:T(8,128)(2,1)S(1)} %get-tuple-element.14.own, bf16[256,512]{1,0:T(8,128)(2,1)S(1)} %collective-permute-done.5.other, ...), custom_call_target="tpu_custom_call" | custom-call | flops 536870912 | bytes 2097152 | tf_op jit(solution)/shard_map/products_keep/pallas_call | solution.py:297
  147.2 0.0 collective-permute-done.13.from_right
  147.2 5.0 %products_keep.3 = f32[2048,256]{1,0:T(8,128)} custom-call(s32[2]{0:T(128)S(1)} %pad_add_fusion.meta, f32[4,32]{1,0:T(4,128)S(1)} %convert_divide_fusion.factor, bf16[1024,8192]{1,0:T(8,128)(2,1)} %counts.29, bf16[256,512]{1,0:T(8,128)(2,1)S(1)} %get-tuple-element.14.own, ...), custom_call_target="tpu_custom_call", output_to_operand_aliasing={{}: (7, {})} | custom-call | flops 536870912 | bytes 2097152 | tf_op jit(solution)/shard_map/products_keep/pallas_call | solution.py:297
  152.2 0.7 copy.11
  (9 shorter events, 0.1 us)
Async XLA Ops:
  1.4 2.2 %copy-start = (bf16[256,8192]{1,0:T(8,128)(2,1)S(1)}, bf16[256,8192]{1,0:T(8,128)(2,1)}, u32[]{:S(2)}) copy-start(bf16[256,8192]{1,0:T(8,128)(2,1)} %genes.1) | copy-start | bytes 12582916
  21.4 2.1 %collective-permute-start.2 = (f32[512,256]{1,0:T(8,128)S(1)}, f32[512,256]{1,0:T(8,128)S(1)}, u32[]{:S(2)}, u32[]{:S(2)}) collective-permute-start(f32[512,256]{1,0:T(8,128)S(1)} %get-tuple-element.11), channel_id=1, source_target_pairs={{0,1},{1,0},{2,3},{3,2},{4,5},{5,4},{6,7},{7,6},{8,9},{9,8},{10,11... | collective-permute-start | bytes 1572872 | tf_op jit(solution)/shard_map/ppermute | solution.py:324
  23.2 3.3 %collective-permute-start = (f32[256,256]{1,0:T(8,128)S(1)}, f32[256,256]{1,0:T(8,128)S(1)}, u32[]{:S(2)}, u32[]{:S(2)}) collective-permute-start(f32[256,256]{1,0:T(8,128)S(1)} %fusion.5), channel_id=1, source_target_pairs={{0,1},{1,0},{2,3},{3,2},{4,5},{5,4},{6,7},{7,6},{8,9},{9,8},{10,11... | collective-permute-start | bytes 786440 | tf_op jit(solution)/shard_map/ppermute | solution.py:324
  23.5 24.3 %copy-start.1 = (bf16[1024,256]{1,0:T(8,128)(2,1)S(1)}, bf16[1024,256]{1,0:T(8,128)(2,1)}, u32[]{:S(2)}) copy-start(bf16[1024,256]{1,0:T(8,128)(2,1)} %start.1) | copy-start | bytes 1572868
  23.5 24.3 %collective-permute-start.3 = (f32[512,256]{1,0:T(8,128)S(1)}, f32[512,256]{1,0:T(8,128)S(1)}, u32[]{:S(2)}, u32[]{:S(2)}) collective-permute-start(f32[512,256]{1,0:T(8,128)S(1)} %add.23.cross_a), channel_id=1, source_target_pairs={{0,2},{2,0},{1,3},{3,1},{4,6},{6,4},{5,7},{7,5},{8,10},{10,8},{9,1... | collective-permute-start | bytes 1572872 | tf_op jit(solution)/shard_map/ppermute | solution.py:324
  26.5 17.8 %collective-permute-start.1 = (f32[256,256]{1,0:T(8,128)S(1)}, f32[256,256]{1,0:T(8,128)S(1)}, u32[]{:S(2)}, u32[]{:S(2)}) collective-permute-start(f32[256,256]{1,0:T(8,128)S(1)} %add.22.gram_a), channel_id=1, source_target_pairs={{0,2},{2,0},{1,3},{3,1},{4,6},{6,4},{5,7},{7,5},{8,10},{10,8},{9,1... | collective-permute-start | bytes 786440 | tf_op jit(solution)/shard_map/ppermute | solution.py:324
  50.3 1.6 %collective-permute-start.5 = (bf16[256,512]{1,0:T(8,128)(2,1)S(1)}, bf16[256,512]{1,0:T(8,128)(2,1)S(1)}, u32[]{:S(2)}, u32[]{:S(2)}) collective-permute-start(bf16[256,512]{1,0:T(8,128)(2,1)S(1)} %get-tuple-element.14.own), channel_id=1, source_target_pairs={{0,1},{1,0},{2,3},{3,2},{4,5},{5,4},{6,7},{7,6},{8,9},{9,8},{10,11... | collective-permute-start | bytes 786440 | tf_op jit(solution)/shard_map/ppermute | solution.py:324
  54.9 16.0 %collective-permute-start.17 = (bf16[256,1024]{1,0:T(8,128)(2,1)}, bf16[256,1024]{1,0:T(8,128)(2,1)}, u32[]{:S(2)}, u32[]{:S(2)}) collective-permute-start(bf16[256,1024]{1,0:T(8,128)(2,1)} %products_send.21), channel_id=1, source_target_pairs={{12,8},{13,9},{14,10},{15,11},{28,24},{29,25},{30,26},{31,27}} | collective-permute-start | bytes 1572872 | tf_op jit(solution)/shard_map/ppermute | solution.py:374
  61.1 14.6 %collective-permute-start.14 = (bf16[256,1024]{1,0:T(8,128)(2,1)}, bf16[256,1024]{1,0:T(8,128)(2,1)S(1)}, u32[]{:S(2)}, u32[]{:S(2)}) collective-permute-start(bf16[256,1024]{1,0:T(8,128)(2,1)} %products_send.18), channel_id=1, source_target_pairs={{0,4},{1,5},{2,6},{3,7},{16,20},{17,21},{18,22},{19,23}} | collective-permute-start | bytes 1572872 | tf_op jit(solution)/shard_map/ppermute | solution.py:372
  64.9 19.0 %collective-permute-start.11 = (bf16[256,1024]{1,0:T(8,128)(2,1)S(1)}, bf16[256,1024]{1,0:T(8,128)(2,1)S(1)}, u32[]{:S(2)}, u32[]{:S(2)}) collective-permute-start(bf16[256,1024]{1,0:T(8,128)(2,1)S(1)} %products_send.15), channel_id=1, source_target_pairs={{12,8},{13,9},{14,10},{15,11},{28,24},{29,25},{30,26},{31,27}} | collective-permute-start | bytes 1572872 | tf_op jit(solution)/shard_map/ppermute | solution.py:374
  69.5 17.3 %collective-permute-start.8 = (bf16[256,1024]{1,0:T(8,128)(2,1)S(1)}, bf16[256,1024]{1,0:T(8,128)(2,1)S(1)}, u32[]{:S(2)}, u32[]{:S(2)}) collective-permute-start(bf16[256,1024]{1,0:T(8,128)(2,1)S(1)} %products_send.12), channel_id=1, source_target_pairs={{0,4},{1,5},{2,6},{3,7},{16,20},{17,21},{18,22},{19,23}} | collective-permute-start | bytes 1572872 | tf_op jit(solution)/shard_map/ppermute | solution.py:372
  70.8 54.7 %collective-permute-start.4 = (bf16[512,256]{1,0:T(8,128)(2,1)S(1)}, bf16[512,256]{1,0:T(8,128)(2,1)}, u32[]{:S(2)}, u32[]{:S(2)}) collective-permute-start(bf16[512,256]{1,0:T(8,128)(2,1)S(1)} %get-tuple-element.13), channel_id=1, source_target_pairs={{0,1},{1,0},{2,3},{3,2},{4,5},{5,4},{6,7},{7,6},{8,9},{9,8},{10,11... | collective-permute-start | bytes 786440 | tf_op jit(solution)/shard_map/ppermute | solution.py:324
  73.7 21.9 %collective-permute-start.18 = (bf16[256,1024]{1,0:T(8,128)(2,1)S(1)}, bf16[256,1024]{1,0:T(8,128)(2,1)S(1)}, u32[]{:S(2)}, u32[]{:S(2)}) collective-permute-start(bf16[256,1024]{1,0:T(8,128)(2,1)S(1)} %products_send.22), channel_id=1, source_target_pairs={{8,4},{12,8},{9,5},{13,9},{10,6},{14,10},{11,7},{15,11},{24,20},{2... | collective-permute-start | bytes 1572872 | tf_op jit(solution)/shard_map/ppermute | solution.py:374
  79.6 19.5 %collective-permute-start.15 = (bf16[256,1024]{1,0:T(8,128)(2,1)S(1)}, bf16[256,1024]{1,0:T(8,128)(2,1)S(1)}, u32[]{:S(2)}, u32[]{:S(2)}) collective-permute-start(bf16[256,1024]{1,0:T(8,128)(2,1)S(1)} %products_send.19), channel_id=1, source_target_pairs={{0,4},{4,8},{1,5},{5,9},{2,6},{6,10},{3,7},{7,11},{16,20},{20,24},... | collective-permute-start | bytes 1572872 | tf_op jit(solution)/shard_map/ppermute | solution.py:372
  85.8 18.5 %collective-permute-start.12 = (bf16[256,1024]{1,0:T(8,128)(2,1)S(1)}, bf16[256,1024]{1,0:T(8,128)(2,1)S(1)}, u32[]{:S(2)}, u32[]{:S(2)}) collective-permute-start(bf16[256,1024]{1,0:T(8,128)(2,1)S(1)} %products_send.16), channel_id=1, source_target_pairs={{8,4},{12,8},{9,5},{13,9},{10,6},{14,10},{11,7},{15,11},{24,20},{2... | collective-permute-start | bytes 1572872 | tf_op jit(solution)/shard_map/ppermute | solution.py:374
  90.7 21.7 %collective-permute-start.9 = (bf16[256,1024]{1,0:T(8,128)(2,1)S(1)}, bf16[256,1024]{1,0:T(8,128)(2,1)S(1)}, u32[]{:S(2)}, u32[]{:S(2)}) collective-permute-start(bf16[256,1024]{1,0:T(8,128)(2,1)S(1)} %products_send.13), channel_id=1, source_target_pairs={{0,4},{4,8},{1,5},{5,9},{2,6},{6,10},{3,7},{7,11},{16,20},{20,24},... | collective-permute-start | bytes 1572872 | tf_op jit(solution)/shard_map/ppermute | solution.py:372
  95.6 22.9 %collective-permute-start.6 = (f32[64,256]{1,0:T(8,128)S(1)}, f32[64,256]{1,0:T(8,128)S(1)}, u32[]{:S(2)}, u32[]{:S(2)}) collective-permute-start(f32[64,256]{1,0:T(8,128)S(1)} %convolution_add_fusion), channel_id=1, source_target_pairs={{0,4},{4,0},{8,12},{12,8},{1,5},{5,1},{9,13},{13,9},{2,6},{6,2},{1... | collective-permute-start | bytes 196616 | tf_op jit(solution)/shard_map/ppermute | solution.py:324
  99.1 43.2 %collective-permute-start.19 = (bf16[256,1024]{1,0:T(8,128)(2,1)S(1)}, bf16[256,1024]{1,0:T(8,128)(2,1)S(1)}, u32[]{:S(2)}, u32[]{:S(2)}) collective-permute-start(bf16[256,1024]{1,0:T(8,128)(2,1)S(1)} %products_send.23), channel_id=1, source_target_pairs={{4,0},{8,4},{12,8},{5,1},{9,5},{13,9},{6,2},{10,6},{14,10},{7,3},{... | collective-permute-start | bytes 1572872 | tf_op jit(solution)/shard_map/ppermute | solution.py:374
  104.3 38.0 %collective-permute-start.16 = (bf16[256,1024]{1,0:T(8,128)(2,1)S(1)}, bf16[256,1024]{1,0:T(8,128)(2,1)S(1)}, u32[]{:S(2)}, u32[]{:S(2)}) collective-permute-start(bf16[256,1024]{1,0:T(8,128)(2,1)S(1)} %products_send.20), channel_id=1, source_target_pairs={{0,4},{4,8},{8,12},{1,5},{5,9},{9,13},{2,6},{6,10},{10,14},{3,7},{... | collective-permute-start | bytes 1572872 | tf_op jit(solution)/shard_map/ppermute | solution.py:372
  112.4 34.8 %collective-permute-start.13 = (bf16[256,1024]{1,0:T(8,128)(2,1)}, bf16[256,1024]{1,0:T(8,128)(2,1)S(1)}, u32[]{:S(2)}, u32[]{:S(2)}) collective-permute-start(bf16[256,1024]{1,0:T(8,128)(2,1)} %products_send.17), channel_id=1, source_target_pairs={{4,0},{8,4},{12,8},{5,1},{9,5},{13,9},{6,2},{10,6},{14,10},{7,3},{... | collective-permute-start | bytes 1572872 | tf_op jit(solution)/shard_map/ppermute | solution.py:374
  118.5 28.8 %collective-permute-start.10 = (bf16[256,1024]{1,0:T(8,128)(2,1)}, bf16[256,1024]{1,0:T(8,128)(2,1)}, u32[]{:S(2)}, u32[]{:S(2)}) collective-permute-start(bf16[256,1024]{1,0:T(8,128)(2,1)} %products_send.14), channel_id=1, source_target_pairs={{0,4},{4,8},{8,12},{1,5},{5,9},{9,13},{2,6},{6,10},{10,14},{3,7},{... | collective-permute-start | bytes 1572872 | tf_op jit(solution)/shard_map/ppermute | solution.py:372
  125.5 11.0 %collective-permute-start.7 = (f32[64,256]{1,0:T(8,128)S(1)}, f32[64,256]{1,0:T(8,128)S(1)}, u32[]{:S(2)}, u32[]{:S(2)}) collective-permute-start(f32[64,256]{1,0:T(8,128)S(1)} %add.27), channel_id=1, source_target_pairs={{0,8},{4,12},{8,0},{12,4},{1,9},{5,13},{9,1},{13,5},{2,10},{6,14},... | collective-permute-start | bytes 196616 | tf_op jit(solution)/shard_map/ppermute | solution.py:324

commit v2 on v1

v2 whole, which is shorter than its diff:
```python
import functools

import jax
import jax.numpy as jnp
from jax import lax
from jax.experimental import pallas as pl
from jax.experimental.pallas import tpu as pltpu
from jax.sharding import PartitionSpec as P

ITERS = 3
F32 = jnp.float32
BF16 = jnp.bfloat16
MIB = 1024 * 1024


def params(limit=48):
    return pltpu.CompilerParams(vmem_limit_bytes=limit * MIB)


def cost(flops, bytes_accessed):
    return pl.CostEstimate(flops=flops, bytes_accessed=bytes_accessed, transcendentals=0)


def contract_last(left, right):
    return lax.dot_general(
        left, right, (((1,), (1,)), ((), ())), preferred_element_type=F32
    )


def gram_kernel(genes, tile_mask, tile_counts, gram, turned, factor):
    step = pl.program_id(0)
    turned[...] = genes[...].T
    part = jnp.dot(genes[...], turned[...], preferred_element_type=F32)

    @pl.when(step == 0)
    def _():
        gram[...] = part
        factor[...] = tile_mask[...].astype(F32) / tile_counts[...].astype(F32)

    @pl.when(step > 0)
    def _():
        gram[...] += part


def gram_parts(genes, tile_mask, tile_counts):
    width, columns = genes.shape
    wide = min(1024, columns)
    tiles = pl.BlockSpec(tile_mask.shape, lambda i: (0, 0))
    return pl.pallas_call(
        gram_kernel,
        out_shape=(
            jax.ShapeDtypeStruct((width, width), F32),
            jax.ShapeDtypeStruct((columns, width), BF16),
            jax.ShapeDtypeStruct(tile_mask.shape, F32),
        ),
        grid=(columns // wide,),
        in_specs=[pl.BlockSpec((width, wide), lambda i: (0, i)), tiles, tiles],
        out_specs=(
            pl.BlockSpec((width, width), lambda i: (0, 0)),
            pl.BlockSpec((wide, width), lambda i: (i, 0)),
            tiles,
        ),
        compiler_params=params(60),
        cost_estimate=cost(2 * width * width * columns, 4 * width * columns),
        name="gram",
    )(genes, tile_mask, tile_counts)


def cross_kernel(tile, meta, factor, counts, turned, theirs, mine, total, scaled):
    step = pl.program_id(0)
    row_tiles = counts.shape[0] // tile
    gene_tiles = counts.shape[1] // tile
    half = counts.shape[0] // 2
    for row in range(row_tiles):
        for col in range(gene_tiles):
            at = (pl.ds(row * tile, tile), pl.ds(col * tile, tile))
            scale = factor[row, step * gene_tiles + col]
            scaled[at] = (counts[at].astype(F32) * scale).astype(BF16)
    part = jnp.dot(scaled[...], turned[...], preferred_element_type=F32)

    @pl.when(step == 0)
    def _():
        total[...] = part

    @pl.when(step > 0)
    def _():
        total[...] += part

    @pl.when(step == pl.num_programs(0) - 1)
    def _():
        sub = meta[0]
        mine[...] = total[pl.ds(pl.multiple_of(sub * half, half), half), :]
        theirs[...] = total[pl.ds(pl.multiple_of((1 - sub) * half, half), half), :]


def cross_parts(meta, factor, counts, turned, tile):
    rows, columns = counts.shape
    width = turned.shape[1]
    wide = min(1024, columns)
    half = jax.ShapeDtypeStruct((rows // 2, width), F32)
    return pl.pallas_call(
        functools.partial(cross_kernel, tile),
        out_shape=(half, half),
        grid_spec=pltpu.PrefetchScalarGridSpec(
            num_scalar_prefetch=1,
            grid=(columns // wide,),
            in_specs=[
                pl.BlockSpec(memory_space=pltpu.SMEM),
                pl.BlockSpec((rows, wide), lambda i, m: (0, i)),
                pl.BlockSpec((wide, width), lambda i, m: (i, 0)),
            ],
            out_specs=(
                pl.BlockSpec((rows // 2, width), lambda i, m: (0, 0)),
                pl.BlockSpec((rows // 2, width), lambda i, m: (0, 0)),
            ),
            scratch_shapes=[
                pltpu.VMEM((rows, width), F32),
                pltpu.VMEM((rows, wide), BF16),
            ],
        ),
        compiler_params=params(60),
        cost_estimate=cost(2 * rows * columns * width, 2 * rows * columns),
        name="cross",
    )(meta, factor, counts, turned)


def halves(value):
    high = value.astype(BF16)
    return high, (value - high.astype(F32)).astype(BF16)


def product3(left, right):
    left_high, left_low = left
    right_high, right_low = right
    dot = functools.partial(jnp.dot, preferred_element_type=F32)
    return dot(left_high, right_high) + (
        dot(left_high, right_low) + dot(left_low, right_high)
    )


def inverse_kernel(gram_a, gram_b, inverse, rho_out):
    gram = gram_a[...] + gram_b[...]
    width = gram.shape[0]
    shape = (width, width)
    diagonal = lax.broadcasted_iota(jnp.int32, shape, 0) == lax.broadcasted_iota(
        jnp.int32, shape, 1
    )
    eye = jnp.where(diagonal, 1.0, 0.0).astype(F32)
    rho = jnp.sum(gram * eye) / width
    rho_out[0, 0] = rho
    scale = 1.0 / jnp.full((1, 1), rho, F32)
    matrix = gram * scale + eye
    low = 2.0 / (width + 2.0)
    guess = low * eye
    image = low * matrix
    first = True
    while True:
        low = low * (2.0 - low)
        gain = 2.0 / (1.0 + low)
        low = gain * low
        done = 1.0 - low < 2e-3
        step = halves(gain * (2.0 * eye - image))
        if first:
            guess = guess[0:1, 0:1] * (gain * (2.0 * eye - image))
        else:
            guess = product3(halves(guess), step)
        first = False
        if done:
            break
        image = product3(halves(image), step)
    rest = eye - jnp.dot(
        matrix, guess, preferred_element_type=F32, precision=lax.Precision.HIGHEST
    )
    rest_halves = halves(rest)
    series = rest + product3(rest_halves, rest_halves)
    inverse[...] = (guess + product3(halves(guess), halves(series))) * scale


def shifted_inverse(gram_a, gram_b):
    width = gram_a.shape[0]
    whole = pl.BlockSpec(memory_space=pltpu.VMEM)
    return pl.pallas_call(
        inverse_kernel,
        out_shape=(
            jax.ShapeDtypeStruct((width, width), F32),
            jax.ShapeDtypeStruct((1, 1), F32),
        ),
        in_specs=[whole, whole],
        out_specs=(whole, pl.BlockSpec(memory_space=pltpu.SMEM)),
        compiler_params=params(),
        cost_estimate=cost(2 * 60 * width**3, 12 * width**2),
        name="inverse",
    )(gram_a, gram_b)


def admm_kernel(meta, rho_ref, cross_a, cross_b, inverse, start, columns_out):
    rho = rho_ref[0, 0]
    cross = cross_a[...] + cross_b[...]
    inverse_halves = halves(inverse[...])
    zvalue = start[...].astype(F32)
    uvalue = jnp.zeros_like(zvalue)
    for _ in range(ITERS):
        vvalue = product3(halves(cross + rho * (zvalue - uvalue)), inverse_halves)
        zvalue = jnp.maximum(vvalue + uvalue, 0.0)
        uvalue = uvalue + vvalue - zvalue
    columns_out[...] = zvalue.T.astype(BF16)


def admm(meta, rho, cross_a, cross_b, inverse, start):
    rows, width = cross_a.shape
    tall = lambda: pl.BlockSpec((rows, width), lambda i, m: (0, 0))
    return pl.pallas_call(
        admm_kernel,
        out_shape=jax.ShapeDtypeStruct((width, rows), BF16),
        grid_spec=pltpu.PrefetchScalarGridSpec(
            num_scalar_prefetch=1,
            grid=(1,),
            in_specs=[
                pl.BlockSpec(memory_space=pltpu.SMEM),
                tall(),
                tall(),
                pl.BlockSpec((width, width), lambda i, m: (0, 0)),
                pl.BlockSpec((rows, width), lambda i, m: (m[2], 0)),
            ],
            out_specs=pl.BlockSpec((width, rows), lambda i, m: (0, 0)),
        ),
        compiler_params=params(),
        cost_estimate=cost(2 * 9 * rows * width**2, 12 * rows * width),
        name="admm",
    )(meta, rho, cross_a, cross_b, inverse, start)


def chunk_product(tile, gene, meta, factor, counts, own, other):
    half = counts.shape[0] // 2
    sub = meta[0]
    column = gene // tile
    total = None
    for first, left in ((sub, own), (1 - sub, other)):
        parts = [
            (
                counts[pl.ds(pl.multiple_of(first * half + r * tile, tile), tile), :].astype(F32)
                * factor[first * (half // tile) + r, column]
            ).astype(BF16)
            for r in range(half // tile)
        ]
        part = jnp.dot(
            left[...], jnp.concatenate(parts, axis=0), preferred_element_type=F32
        )
        total = part if total is None else total + part
    return total


def products_kernel(tile, wide, place, meta, factor, counts, own, other, out):
    gene = place(pl.program_id(0), pl.program_id(1)) * wide
    total = chunk_product(tile, gene, meta, factor, counts, own, other)
    out[...] = total.astype(BF16).reshape(out.shape)


def products(cells, chunks, chunk, tile, meta, factor, counts, own, other):
    rows, columns = counts.shape
    width = own.shape[0]
    block = columns // cells
    part = block // chunks
    wide = min(tile, part)
    place = lambda o, i: o * (block // wide) + chunk * (part // wide) + i
    halved = lambda: pl.BlockSpec((width, rows // 2), lambda o, i, m: (0, 0))
    return pl.pallas_call(
        functools.partial(products_kernel, tile, wide, place),
        out_shape=jax.ShapeDtypeStruct((cells, width, part), BF16),
        grid_spec=pltpu.PrefetchScalarGridSpec(
            num_scalar_prefetch=1,
            grid=(cells, part // wide),
            in_specs=[
                pl.BlockSpec(memory_space=pltpu.SMEM),
                pl.BlockSpec((rows, wide), lambda o, i, m: (0, place(o, i))),
                halved(),
                halved(),
            ],
            out_specs=pl.BlockSpec((1, width, wide), lambda o, i, m: (o, 0, i)),
        ),
        compiler_params=params(),
        cost_estimate=cost(2 * rows * width * part * cells, 2 * rows * part * cells),
        name="products",
    )(meta, factor, counts, own, other)


def swap(value, axis, size, step):
    return lax.ppermute(value, axis, [(i, i ^ step) for i in range(size)])


def pair_sums(value, axis, size):
    step = 1
    while step < size:
        value = value + swap(value, axis, size, step)
        step *= 2
    return value


def split_sums(value, axis, size):
    index = lax.axis_index(axis)
    step = size // 2
    while True:
        upper = (index // step) % 2 == 1
        low, high = jnp.split(value, 2, axis=0)
        kept = jnp.where(upper, high, low)
        arrived = swap(jnp.where(upper, low, high), axis, size, step)
        step //= 2
        if step == 0:
            return kept, arrived
        value = kept + arrived


def join_columns(value, axis, size):
    index = lax.axis_index(axis)
    step = 1
    while step < size:
        arrived = swap(value, axis, size, step)
        value = jnp.where(
            (index // step) % 2 == 0,
            jnp.concatenate([value, arrived], axis=1),
            jnp.concatenate([arrived, value], axis=1),
        )
        step *= 2
    return value


def shards(sizes, counts, tile_mask, tile_counts, gene_factor, prev_factor):
    cells, genes, subs = sizes
    rows, columns = counts.shape
    width = gene_factor.shape[0]
    tile = rows // tile_mask.shape[0]
    sub = lax.axis_index("sub")
    cell = lax.axis_index("cell")
    place = sub * genes + lax.axis_index("gene")
    meta = jnp.stack([sub, cell, place]).astype(jnp.int32)

    gram, turned, factor = gram_parts(gene_factor, tile_mask, tile_counts)
    gram = pair_sums(gram, "gene", genes)
    gram_other = swap(gram, "sub", subs, 1)
    theirs, mine = cross_parts(meta, factor, counts, turned, tile)
    cross = mine + swap(theirs, "sub", subs, 1)
    cross_a, cross_b = split_sums(cross, "gene", genes)
    inverse, rho = shifted_inverse(gram, gram_other)
    share = admm(meta, rho, cross_a, cross_b, inverse, prev_factor)
    own = join_columns(share, "gene", genes)
    other = swap(own, "sub", subs, 1)

    block = columns // cells
    chunks = 2 if block % (2 * tile) == 0 else 1
    pieces = []
    for chunk in range(chunks):
        part = products(cells, chunks, chunk, tile, meta, factor, counts, own, other)
        part = lax.psum_scatter(part, "cell", scatter_dimension=0)
        pieces.append(part.T.astype(F32))
    data_products = jnp.concatenate(pieces, axis=0)

    whole = jnp.where(
        sub == 0,
        jnp.concatenate([own, other], axis=1),
        jnp.concatenate([other, own], axis=1),
    )
    new_factor = whole.T
    part = width // (genes * subs)
    first = (lax.axis_index("gene") * subs + sub) * part
    gram_rows = contract_last(lax.dynamic_slice_in_dim(whole, first, part, 0), whole)
    gram_rows = pair_sums(gram_rows, "cell", cells)
    factor_gram = lax.all_gather(gram_rows, ("gene", "sub"), axis=0, tiled=True)
    return (new_factor, factor_gram, data_products)


def solution(mesh):
    sizes = (mesh.shape["cell"], mesh.shape["gene"], mesh.shape["sub"])
    return jax.shard_map(
        functools.partial(shards, sizes),
        mesh=mesh,
        in_specs=(
            P(("groups", "cell"), ("gene", "sub")),
            P(("groups", "cell"), ("gene", "sub")),
            P(("groups", "cell"), ("gene", "sub")),
            P("groups", ("gene", "sub")),
            P(("groups", "cell"), None),
        ),
        out_specs=(
            P(("groups", "cell"), None),
            P("groups", None),
            P(("groups", "gene", "sub", "cell"), None),
        ),
        check_vma=False,
    )
```

time: 156 us -> 178 us (1.14)
  waiting for transfers between devices: 28.2 us -> 85 us
  starting transfers between devices: 37.4 us -> 9.93 us
  Pallas kernels: 73 us -> 54.2 us
  between operations: 0.94 us -> 14.2 us
    reduce_scatter x0 -> x2, waiting for transfers between devices: none -> 54.6 us  [shards(): part = lax.psum_scatter(part, 'cell', scatter_dimension=0)]
    ppermute x12 -> x0, starting transfers between devices: 30.3 us -> none  [the longest x6 24.2 us: shards(): from_left[chunk] = lax.ppermute(right, 'cell', pairs)]
    pallas_call x15 -> x4, Pallas kernels: 51.8 us -> 37.4 us  [the longest x2 27.3 us: products(): pl.pallas_call(functools.partial(products_kernel, tile, wide, place), out...]
    pallas_call x1, Pallas kernels: 17.7 us -> 13.3 us  [cross_parts(): pl.pallas_call(functools.partial(cross_kernel, tile), out_shape=(half, ha...]
    ppermute x8, waiting for transfers between devices: 26.6 us -> 30.4 us  [swap(): return lax.ppermute(value, axis, [(i, i ^ step) for i in range(size)])]
    ppermute x8, starting transfers between devices: 7.09 us -> 9.85 us  [swap(): return lax.ppermute(value, axis, [(i, i ^ step) for i in range(size)])]
  transfers between devices with their start and end apart: 20 -> 10, of which waited for: 6 -> 8; matrix products, arithmetic and copies ran while one was open for 3% -> 1% of each run, Pallas kernels for 29% -> 10%
where the time goes in v2:
time: 178 us; the launch traced here: 176 us
  waiting for transfers between devices  85 us (48%)
  Pallas kernels  54.2 us (30%)
  between operations  14.2 us (8%)
  starting transfers between devices  9.93 us (6%)
  blocking collectives  5.81 us (3%)
  local copies, waits for them, and re-layouts  3.53 us (2%)
  other arithmetic  3.49 us (2%)
    reduce_scatter x2, waiting for transfers between devices, shards(): part = lax.psum_scatter(part, 'cell', scatter_dimension=0)  54.6 us
    ppermute x8, waiting for transfers between devices, swap(): return lax.ppermute(value, axis, [(i, i ^ step) for i in range(size)])  30.4 us
    pallas_call x2, Pallas kernels, products(): pl.pallas_call(functools.partial(products_kernel, tile, wide, place), out...  27.3 us
    pallas_call x1, Pallas kernels, cross_parts(): pl.pallas_call(functools.partial(cross_kernel, tile), out_shape=(half, ha...  13.3 us
    ppermute x8, starting transfers between devices, swap(): return lax.ppermute(value, axis, [(i, i ^ step) for i in range(size)])  9.85 us
    pallas_call x1, Pallas kernels, gram_parts(): pl.pallas_call(gram_kernel, out_shape=(jax.ShapeDtypeStruct((width, width...  8.04 us
    all_gather x1, blocking collectives, shards(): factor_gram = lax.all_gather(gram_rows, ('gene', 'sub'), axis=0, tiled=True)  5.81 us
  transfers between devices with their start and end apart: 10, of which 8 were waited for; matrix products, arithmetic and copies ran while one was open for 1% of the time, Pallas kernels for 10%

profile of v2, /device:TPU:0, one launch (start us, length us, event | category | flops | bytes accessed | tf_op | source)
XLA Modules:
  0.0 176.4 jit_solution(4798885939566280242)
XLA Ops:
  7.2 0.0 reduce-scatter.5.cloned.1.call-start
  7.2 0.6 pad_add_fusion.meta
  7.8 8.0 %gram.1 = (f32[256,256]{1,0:T(8,128)}, bf16[8192,256]{1,0:T(8,128)(2,1)}, f32[4,32]{1,0:T(4,128)}) custom-call(bf16[256,8192]{1,0:T(8,128)(2,1)} %genes.1, s32[4,32]{1,0:T(4,128)} %tile_mask.1, s32[4,32]{1,0:T(4,128)} %tile_counts.1), custom_call_target="tpu_custom_call" | custom-call | flops 1073741824 | bytes 8388608 | tf_op jit(solution)/shard_map/gram/pallas_call | solution.py:49
  15.9 0.0 copy-start.3
  15.9 13.3 %cross.1 = (f32[512,256]{1,0:T(8,128)}, f32[512,256]{1,0:T(8,128)}) custom-call(s32[3]{0:T(128)} %pad_add_fusion.meta, f32[4,32]{1,0:T(4,128)} %get-tuple-element.12.factor, bf16[1024,8192]{1,0:T(8,128)(2,1)} %counts.5, bf16[8192,256]{1,0:T(8,128)(2,1)} %get-tuple-element.13.turned), custom_call_target="tpu_custom_call" | custom-call | flops 4294967296 | bytes 16777216 | tf_op jit(solution)/shard_map/cross/pallas_call | solution.py:101
  29.1 0.5 collective-permute-start.2
  29.6 0.0 copy-done.3
  29.6 2.6 %collective-permute-start = (f32[256,256]{1,0:T(8,128)S(1)}, f32[256,256]{1,0:T(8,128)S(1)}, u32[]{:S(2)}, u32[]{:S(2)}) collective-permute-start(f32[256,256]{1,0:T(8,128)S(1)} %copy-done.3), channel_id=1, source_target_pairs={{0,2},{2,0},{1,3},{3,1},{4,6},{6,4},{5,7},{7,5},{8,10},{10,8},{9,1... | collective-permute-start | bytes 786440 | tf_op jit(solution)/shard_map/ppermute | solution.py:288
  32.1 6.9 %collective-permute-done = f32[256,256]{1,0:T(8,128)S(1)} collective-permute-done((f32[256,256]{1,0:T(8,128)S(1)}, f32[256,256]{1,0:T(8,128)S(1)}, u32[]{:S(2)}, u32[]{:S(2)}) %collective-permute-start) | collective-permute-done | bytes 262176 | tf_op jit(solution)/shard_map/ppermute | solution.py:288
  39.1 0.1 collective-permute-start.1
  39.2 0.0 collective-permute-done.2
  39.2 1.1 add.34
  40.3 0.0 copy-start
  40.3 0.0 copy-start.2
  40.3 0.0 copy-start.1
  40.4 1.8 %collective-permute-start.3 = (f32[256,256]{1,0:T(8,128)S(1)}, f32[256,256]{1,0:T(8,128)S(1)}, u32[]{:S(2)}, u32[]{:S(2)}) collective-permute-start(f32[256,256]{1,0:T(8,128)S(1)} %get-tuple-element.20), channel_id=1, source_target_pairs={{0,2},{2,0},{1,3},{3,1},{4,6},{6,4},{5,7},{7,5},{8,10},{10,8},{9,1... | collective-permute-start | bytes 786440 | tf_op jit(solution)/shard_map/ppermute | solution.py:288
  42.2 0.0 collective-permute-done.1.gram_b
  42.2 3.5 %inverse.1 = (f32[256,256]{1,0:T(8,128)S(1)}, f32[1,1]{1,0:T(1,128)}) custom-call(f32[256,256]{1,0:T(8,128)S(1)} %add.33.gram_a, f32[256,256]{1,0:T(8,128)S(1)} %collective-permute-done.1.gram_b), custom_call_target="tpu_custom_call" | custom-call | flops 2013265920 | bytes 786432 | tf_op jit(solution)/shard_map/inverse/pallas_call | solution.py:182
  45.7 3.4 %collective-permute-done.3.cross_b = f32[256,256]{1,0:T(8,128)S(1)} collective-permute-done((f32[256,256]{1,0:T(8,128)S(1)}, f32[256,256]{1,0:T(8,128)S(1)}, u32[]{:S(2)}, u32[]{:S(2)}) %collective-permute-start.3) | collective-permute-done | bytes 262176 | tf_op jit(solution)/shard_map/ppermute | solution.py:288
  49.1 0.0 copy-done
  49.1 0.0 copy-done.2
  49.1 2.1 %admm.1 = bf16[256,256]{1,0:T(8,128)(2,1)S(1)} custom-call(s32[3]{0:T(128)S(1)} %copy-done.2, f32[1,1]{1,0:T(1,128)} %get-tuple-element.11.rho_ref, f32[256,256]{1,0:T(8,128)S(1)} %get-tuple-element.21.cross_a, f32[256,256]{1,0:T(8,128)S(1)} %collective-permute-done.3.cross_b, f32[256,256]{1,0:T(8,128)S(1)} %get-tuple-element.16.inverse, ...), custom_call_target="tpu_custom_call" | custom-call | flops 301989888 | bytes 786432 | tf_op jit(solution)/shard_map/admm/pallas_call | solution.py:212
  51.2 1.8 %collective-permute-start.4 = (bf16[256,256]{1,0:T(8,128)(2,1)S(1)}, bf16[256,256]{1,0:T(8,128)(2,1)S(1)}, u32[]{:S(2)}, u32[]{:S(2)}) collective-permute-start(bf16[256,256]{1,0:T(8,128)(2,1)S(1)} %admm.1), channel_id=1, source_target_pairs={{0,2},{2,0},{1,3},{3,1},{4,6},{6,4},{5,7},{7,5},{8,10},{10,8},{9,1... | collective-permute-start | bytes 393224 | tf_op jit(solution)/shard_map/ppermute | solution.py:288
  53.0 3.4 %collective-permute-done.4 = bf16[256,256]{1,0:T(8,128)(2,1)S(1)} collective-permute-done((bf16[256,256]{1,0:T(8,128)(2,1)S(1)}, bf16[256,256]{1,0:T(8,128)(2,1)S(1)}, u32[]{:S(2)}, u32[]{:S(2)}) %collective-permute-start.4) | collective-permute-done | bytes 131104 | tf_op jit(solution)/shard_map/ppermute | solution.py:288
  56.4 0.1 maximum_select_fusion.1.own
  56.5 0.1 collective-permute-start.5
  56.6 1.5 collective-permute-done.5.other
  58.1 0.0 copy-done.1
  58.1 13.6 %products.3 = bf16[4,256,1024]{2,1,0:T(8,128)(2,1)} custom-call(s32[3]{0:T(128)S(1)} %copy-done.2, f32[4,32]{1,0:T(4,128)S(1)} %copy-done.1, bf16[1024,8192]{1,0:T(8,128)(2,1)} %counts.5, bf16[256,512]{1,0:T(8,128)(2,1)S(1)} %maximum_select_fusion.1.own, bf16[256,512]{1,0:T(8,128)(2,1)S(1)} %collective-permute-done.5.other), custom_call_target="tpu_custom_call" | custom-call | flops 2147483648 | bytes 8388608 | tf_op jit(solution)/shard_map/products/pallas_call | solution.py:267
  71.7 0.0 reduce-scatter.5.cloned.1.call-update
  71.7 0.0 reduce-scatter.3.cloned.1.call-start
  71.7 13.7 %products.2 = bf16[4,256,1024]{2,1,0:T(8,128)(2,1)} custom-call(s32[3]{0:T(128)S(1)} %copy-done.2, f32[4,32]{1,0:T(4,128)S(1)} %copy-done.1, bf16[1024,8192]{1,0:T(8,128)(2,1)} %counts.5, bf16[256,512]{1,0:T(8,128)(2,1)S(1)} %maximum_select_fusion.1.own, bf16[256,512]{1,0:T(8,128)(2,1)S(1)} %collective-permute-done.5.other), custom_call_target="tpu_custom_call" | custom-call | flops 2147483648 | bytes 8388608 | tf_op jit(solution)/shard_map/products/pallas_call | solution.py:267
  85.5 0.0 reduce-scatter.3.cloned.1.call-update
  85.5 0.1 maximum_select_fusion
  85.6 0.3 fusion
  85.9 1.9 %collective-permute-start.6 = (f32[64,256]{1,0:T(8,128)S(1)}, f32[64,256]{1,0:T(8,128)S(1)}, u32[]{:S(2)}, u32[]{:S(2)}) collective-permute-start(f32[64,256]{1,0:T(8,128)S(1)} %fusion), channel_id=1, source_target_pairs={{0,4},{4,0},{8,12},{12,8},{1,5},{5,1},{9,13},{13,9},{2,6},{6,2},{1... | collective-permute-start | bytes 196616 | tf_op jit(solution)/shard_map/ppermute | solution.py:288
  87.8 6.4 %collective-permute-done.6 = f32[64,256]{1,0:T(8,128)S(1)} collective-permute-done((f32[64,256]{1,0:T(8,128)S(1)}, f32[64,256]{1,0:T(8,128)S(1)}, u32[]{:S(2)}, u32[]{:S(2)}) %collective-permute-start.6) | collective-permute-done | bytes 65568 | tf_op jit(solution)/shard_map/ppermute | solution.py:288
  94.3 1.2 collective-permute-start.7
  95.5 1.0 copy.8
  96.5 8.7 %collective-permute-done.7 = f32[64,256]{1,0:T(8,128)S(1)} collective-permute-done((f32[64,256]{1,0:T(8,128)S(1)}, f32[64,256]{1,0:T(8,128)S(1)}, u32[]{:S(2)}, u32[]{:S(2)}) %collective-permute-start.7) | collective-permute-done | bytes 65568 | tf_op jit(solution)/shard_map/ppermute | solution.py:288
  105.2 5.8 %all_gather.3 = f32[256,256]{1,0:T(8,128)S(1)} all-gather(f32[64,256]{1,0:T(8,128)S(1)} %add.38), channel_id=1, replica_groups=mesh['groups'=2,'cell'=4,'gene'=2,'sub'=2] {'gene','sub'}, dimensions={0}, use_global_device_ids=true | all-gather | bytes 327680 | tf_op jit(solution)/shard_map/all_gather | solution.py:367
  111.0 8.7 %reduce-scatter.5.cloned.1.call-done = bf16[1,256,1024]{2,1,0:T(8,128)(2,1)} async-done(((bf16[4,256,1024]{2,1,0:T(8,128)(2,1)}), bf16[1,256,1024]{2,1,0:T(8,128)(2,1)}) %reduce-scatter.5.cloned.1.call-update) | async-done | bytes 524304 | tf_op jit(solution)/shard_map/reduce_scatter | solution.py:353
  119.7 46.0 %reduce-scatter.3.cloned.1.call-done = bf16[1,256,1024]{2,1,0:T(8,128)(2,1)} async-done(((bf16[4,256,1024]{2,1,0:T(8,128)(2,1)}), bf16[1,256,1024]{2,1,0:T(8,128)(2,1)}) %reduce-scatter.3.cloned.1.call-update) | async-done | bytes 524304 | tf_op jit(solution)/shard_map/reduce_scatter | solution.py:353
  165.6 1.4 maximum_convert_fusion
  167.1 1.8 %copy.9 = f32[2048,256]{1,0:T(8,128)} copy(f32[2048,256]{0,1:T(8,128)S(1)} %maximum_convert_fusion) | data formatting | bytes 4194304
  168.9 0.7 copy.11
  (4 shorter events, 0.1 us)
Async XLA Ops:
  7.2 112.5 %reduce-scatter.5.cloned.1.call-start = ((), (), s32[]{:S(2)}) async-start(), calls=%async_computation.3 | async-start | bytes 2621440 | tf_op jit(solution)/shard_map/reduce_scatter | solution.py:353
  15.9 13.7 %copy-start.3 = (f32[256,256]{1,0:T(8,128)S(1)}, f32[256,256]{1,0:T(8,128)}, u32[]{:S(2)}) copy-start(f32[256,256]{1,0:T(8,128)} %get-tuple-element.10) | copy-start | bytes 786436
  29.1 10.0 %collective-permute-start.2 = (f32[512,256]{1,0:T(8,128)}, f32[512,256]{1,0:T(8,128)S(1)}, u32[]{:S(2)}, u32[]{:S(2)}) collective-permute-start(f32[512,256]{1,0:T(8,128)} %get-tuple-element.15), channel_id=1, source_target_pairs={{0,1},{1,0},{2,3},{3,2},{4,5},{5,4},{6,7},{7,6},{8,9},{9,8},{10,11... | collective-permute-start | bytes 1572872 | tf_op jit(solution)/shard_map/ppermute | solution.py:288
  29.6 9.5 %collective-permute-start = (f32[256,256]{1,0:T(8,128)S(1)}, f32[256,256]{1,0:T(8,128)S(1)}, u32[]{:S(2)}, u32[]{:S(2)}) collective-permute-start(f32[256,256]{1,0:T(8,128)S(1)} %copy-done.3), channel_id=1, source_target_pairs={{0,2},{2,0},{1,3},{3,1},{4,6},{6,4},{5,7},{7,5},{8,10},{10,8},{9,1... | collective-permute-start | bytes 786440 | tf_op jit(solution)/shard_map/ppermute | solution.py:288
  39.1 3.1 %collective-permute-start.1 = (f32[256,256]{1,0:T(8,128)S(1)}, f32[256,256]{1,0:T(8,128)S(1)}, u32[]{:S(2)}, u32[]{:S(2)}) collective-permute-start(f32[256,256]{1,0:T(8,128)S(1)} %add.33.gram_a), channel_id=1, source_target_pairs={{0,1},{1,0},{2,3},{3,2},{4,5},{5,4},{6,7},{7,6},{8,9},{9,8},{10,11... | collective-permute-start | bytes 786440 | tf_op jit(solution)/shard_map/ppermute | solution.py:288
  40.3 8.8 %copy-start = (bf16[1024,256]{1,0:T(8,128)(2,1)S(1)}, bf16[1024,256]{1,0:T(8,128)(2,1)}, u32[]{:S(2)}) copy-start(bf16[1024,256]{1,0:T(8,128)(2,1)} %start.1) | copy-start | bytes 1572868
  40.3 8.8 %copy-start.2 = (s32[3]{0:T(128)S(1)}, s32[3]{0:T(128)}, u32[]{:S(2)}) copy-start(s32[3]{0:T(128)} %pad_add_fusion.meta) | copy-start | bytes 40
  40.3 17.8 %copy-start.1 = (f32[4,32]{1,0:T(4,128)S(1)}, f32[4,32]{1,0:T(4,128)}, u32[]{:S(2)}) copy-start(f32[4,32]{1,0:T(4,128)} %get-tuple-element.12.factor) | copy-start | bytes 1540
  40.4 8.8 %collective-permute-start.3 = (f32[256,256]{1,0:T(8,128)S(1)}, f32[256,256]{1,0:T(8,128)S(1)}, u32[]{:S(2)}, u32[]{:S(2)}) collective-permute-start(f32[256,256]{1,0:T(8,128)S(1)} %get-tuple-element.20), channel_id=1, source_target_pairs={{0,2},{2,0},{1,3},{3,1},{4,6},{6,4},{5,7},{7,5},{8,10},{10,8},{9,1... | collective-permute-start | bytes 786440 | tf_op jit(solution)/shard_map/ppermute | solution.py:288
  51.2 5.2 %collective-permute-start.4 = (bf16[256,256]{1,0:T(8,128)(2,1)S(1)}, bf16[256,256]{1,0:T(8,128)(2,1)S(1)}, u32[]{:S(2)}, u32[]{:S(2)}) collective-permute-start(bf16[256,256]{1,0:T(8,128)(2,1)S(1)} %admm.1), channel_id=1, source_target_pairs={{0,2},{2,0},{1,3},{3,1},{4,6},{6,4},{5,7},{7,5},{8,10},{10,8},{9,1... | collective-permute-start | bytes 393224 | tf_op jit(solution)/shard_map/ppermute | solution.py:288
  56.5 1.6 collective-permute-start.5
  71.7 93.9 %reduce-scatter.3.cloned.1.call-start = ((), (), s32[]{:S(2)}) async-start(), calls=%async_computation.2 | async-start | bytes 2621440 | tf_op jit(solution)/shard_map/reduce_scatter | solution.py:353
  85.9 8.3 %collective-permute-start.6 = (f32[64,256]{1,0:T(8,128)S(1)}, f32[64,256]{1,0:T(8,128)S(1)}, u32[]{:S(2)}, u32[]{:S(2)}) collective-permute-start(f32[64,256]{1,0:T(8,128)S(1)} %fusion), channel_id=1, source_target_pairs={{0,4},{4,0},{8,12},{12,8},{1,5},{5,1},{9,13},{13,9},{2,6},{6,2},{1... | collective-permute-start | bytes 196616 | tf_op jit(solution)/shard_map/ppermute | solution.py:288
  94.3 10.9 %collective-permute-start.7 = (f32[64,256]{1,0:T(8,128)S(1)}, f32[64,256]{1,0:T(8,128)S(1)}, u32[]{:S(2)}, u32[]{:S(2)}) collective-permute-start(f32[64,256]{1,0:T(8,128)S(1)} %add.37), channel_id=1, source_target_pairs={{0,8},{4,12},{8,0},{12,4},{1,9},{5,13},{9,1},{13,5},{2,10},{6,14},... | collective-permute-start | bytes 196616 | tf_op jit(solution)/shard_map/ppermute | solution.py:288
Sparse Core Ops, SparseCore 0:
  71.8 47.7 reduce-scatter.4
  122.0 43.5 reduce-scatter.2

commit v3 on v2

v3 whole, which is shorter than its diff:
```python
import functools

import jax
import jax.numpy as jnp
from jax import lax
from jax.experimental import pallas as pl
from jax.experimental.pallas import tpu as pltpu
from jax.sharding import PartitionSpec as P

ITERS = 3
F32 = jnp.float32
BF16 = jnp.bfloat16
MIB = 1024 * 1024


def params(limit=48):
    return pltpu.CompilerParams(vmem_limit_bytes=limit * MIB)


def cost(flops, bytes_accessed):
    return pl.CostEstimate(flops=flops, bytes_accessed=bytes_accessed, transcendentals=0)


def contract_last(left, right):
    return lax.dot_general(
        left, right, (((1,), (1,)), ((), ())), preferred_element_type=F32
    )


def cross_tile(counts, scales, genes, row):
    tile = counts.shape[0] // scales.shape[0]
    block = counts[row * tile : (row + 1) * tile].astype(F32)
    return contract_last((block * scales[row : row + 1]).astype(BF16), genes)


def halves(value):
    high = value.astype(BF16)
    return high, (value - high.astype(F32)).astype(BF16)


def product3(left, right):
    left_high, left_low = left
    right_high, right_low = right
    dot = functools.partial(jnp.dot, preferred_element_type=F32)
    return dot(left_high, right_high) + (
        dot(left_high, right_low) + dot(left_low, right_high)
    )


def inverse_kernel(gram_a, gram_b, inverse, rho_out):
    gram = gram_a[...] + gram_b[...]
    width = gram.shape[0]
    shape = (width, width)
    diagonal = lax.broadcasted_iota(jnp.int32, shape, 0) == lax.broadcasted_iota(
        jnp.int32, shape, 1
    )
    eye = jnp.where(diagonal, 1.0, 0.0).astype(F32)
    rho = jnp.sum(gram * eye) / width
    rho_out[0, 0] = rho
    scale = 1.0 / jnp.full((1, 1), rho, F32)
    matrix = gram * scale + eye
    low = 2.0 / (width + 2.0)
    guess = low * eye
    image = low * matrix
    first = True
    while True:
        low = low * (2.0 - low)
        gain = 2.0 / (1.0 + low)
        low = gain * low
        done = 1.0 - low < 2e-3
        step = halves(gain * (2.0 * eye - image))
        if first:
            guess = guess[0:1, 0:1] * (gain * (2.0 * eye - image))
        else:
            guess = product3(halves(guess), step)
        first = False
        if done:
            break
        image = product3(halves(image), step)
    rest = eye - jnp.dot(
        matrix, guess, preferred_element_type=F32, precision=lax.Precision.HIGHEST
    )
    rest_halves = halves(rest)
    series = rest + product3(rest_halves, rest_halves)
    inverse[...] = (guess + product3(halves(guess), halves(series))) * scale


def shifted_inverse(gram_a, gram_b):
    width = gram_a.shape[0]
    whole = pl.BlockSpec(memory_space=pltpu.VMEM)
    return pl.pallas_call(
        inverse_kernel,
        out_shape=(
            jax.ShapeDtypeStruct((width, width), F32),
            jax.ShapeDtypeStruct((1, 1), F32),
        ),
        in_specs=[whole, whole],
        out_specs=(whole, pl.BlockSpec(memory_space=pltpu.SMEM)),
        compiler_params=params(),
        cost_estimate=cost(2 * 60 * width**3, 12 * width**2),
        name="inverse",
    )(gram_a, gram_b)


def admm_kernel(meta, rho_ref, cross_a, cross_b, inverse, start, columns_out):
    rho = rho_ref[0, 0]
    cross = cross_a[...] + cross_b[...]
    inverse_halves = halves(inverse[...])
    zvalue = start[...].astype(F32)
    uvalue = jnp.zeros_like(zvalue)
    for _ in range(ITERS):
        vvalue = product3(halves(cross + rho * (zvalue - uvalue)), inverse_halves)
        zvalue = jnp.maximum(vvalue + uvalue, 0.0)
        uvalue = uvalue + vvalue - zvalue
    columns_out[...] = zvalue.T.astype(BF16)


def admm(meta, rho, cross_a, cross_b, inverse, start):
    rows, width = cross_a.shape
    tall = lambda: pl.BlockSpec((rows, width), lambda i, m: (0, 0))
    return pl.pallas_call(
        admm_kernel,
        out_shape=jax.ShapeDtypeStruct((width, rows), BF16),
        grid_spec=pltpu.PrefetchScalarGridSpec(
            num_scalar_prefetch=1,
            grid=(1,),
            in_specs=[
                pl.BlockSpec(memory_space=pltpu.SMEM),
                tall(),
                tall(),
                pl.BlockSpec((width, width), lambda i, m: (0, 0)),
                pl.BlockSpec((rows, width), lambda i, m: (m[2], 0)),
            ],
            out_specs=pl.BlockSpec((width, rows), lambda i, m: (0, 0)),
        ),
        compiler_params=params(),
        cost_estimate=cost(2 * 9 * rows * width**2, 12 * rows * width),
        name="admm",
    )(meta, rho, cross_a, cross_b, inverse, start)


def tile_products(tile, gene, meta, factor, counts, own, other):
    rows, wide = counts.shape
    half = rows // 2
    sub = meta[0]
    span = min(tile, wide)
    total = None
    for first, left in ((sub, own), (1 - sub, other)):
        parts = [
            [
                (
                    counts[
                        pl.ds(pl.multiple_of(first * half + r * tile, tile), tile),
                        pl.ds(c * span, span),
                    ].astype(F32)
                    * factor[first * (half // tile) + r, gene // tile + c]
                ).astype(BF16)
                for c in range(wide // span)
            ]
            for r in range(half // tile)
        ]
        right = jnp.concatenate([jnp.concatenate(row, axis=1) for row in parts], axis=0)
        part = jnp.dot(left[...], right, preferred_element_type=F32)
        total = part if total is None else total + part
    return total


def products_kernel(tile, wide, place, meta, factor, counts, own, other, out):
    gene = place(pl.program_id(0), pl.program_id(1), meta) * wide
    total = tile_products(tile, gene, meta, factor, counts, own, other)
    out[...] = total.astype(out.dtype).reshape(out.shape)


def products(block_of, blocks, block, start, chunk, dtype, tile, meta, factor, counts, own, other):
    rows = counts.shape[0]
    width = own.shape[0]
    wide = 2 * tile if chunk % (2 * tile) == 0 else min(tile, chunk)

    def place(o, i, m):
        return block_of(o, m) * (block // wide) + start // wide + i

    halved = lambda: pl.BlockSpec((width, rows // 2), lambda o, i, m: (0, 0))
    return pl.pallas_call(
        functools.partial(products_kernel, tile, wide, place),
        out_shape=jax.ShapeDtypeStruct((blocks, width, chunk), dtype),
        grid_spec=pltpu.PrefetchScalarGridSpec(
            num_scalar_prefetch=1,
            grid=(blocks, chunk // wide),
            in_specs=[
                pl.BlockSpec(memory_space=pltpu.SMEM),
                pl.BlockSpec((rows, wide), lambda o, i, m: (0, place(o, i, m))),
                halved(),
                halved(),
            ],
            out_specs=pl.BlockSpec((1, width, wide), lambda o, i, m: (o, 0, i)),
        ),
        compiler_params=params(40),
        cost_estimate=cost(1, 1),
        name="products",
    )(meta, factor, counts, own, other)


def keep_kernel(meta, total, first, second, *refs):
    value = total[0] + (first[...].astype(F32) + second[...].astype(F32))
    refs[-1][...] = value.T


def keep(block, start, meta, totals, first, second, out):
    width, chunk = first.shape
    wide = min(512, chunk)
    piece = lambda: pl.BlockSpec((width, wide), lambda i, m: (0, i))
    extra = [] if out is None else [out]
    return pl.pallas_call(
        keep_kernel,
        out_shape=jax.ShapeDtypeStruct((block, width), F32),
        grid_spec=pltpu.PrefetchScalarGridSpec(
            num_scalar_prefetch=1,
            grid=(chunk // wide,),
            in_specs=[
                pl.BlockSpec((1, width, wide), lambda i, m: (m[1], 0, i)),
                piece(),
                piece(),
            ]
            + [pl.BlockSpec(memory_space=pl.ANY) for _ in extra],
            out_specs=pl.BlockSpec((wide, width), lambda i, m: (start // wide + i, 0)),
        ),
        input_output_aliases={4: 0} if extra else {},
        compiler_params=params(40),
        cost_estimate=cost(3 * width * chunk, 12 * width * chunk),
        name="keep",
    )(meta, totals, first, second, *extra)


class Line:
    def __init__(self, size, cell):
        self.size = size
        self.cell = cell

    def pairs(self, phase, parity):
        links = range(parity, self.size - 1, 2)
        right = [(i, i + 1) for i in links if i < phase]
        left = [(i + 1, i) for i in links if i + 1 >= self.size - phase]
        return right + left

    def block(self, phase, parity):
        to_right = (self.cell & 1) == parity
        block = self.cell + jnp.where(to_right, self.size - phase, phase)
        return jnp.where(block >= self.size, block - self.size, block)

    def send(self, value, phase, parity):
        return lax.ppermute(value, "cell", self.pairs(phase, parity))


def swap(value, axis, size, step):
    return lax.ppermute(value, axis, [(i, i ^ step) for i in range(size)])


def pair_sums(value, axis, size):
    step = 1
    while step < size:
        value = value + swap(value, axis, size, step)
        step *= 2
    return value


def split_sums(value, axis, size):
    index = lax.axis_index(axis)
    step = size // 2
    while True:
        upper = (index & step) != 0
        low, high = jnp.split(value, 2, axis=0)
        kept = jnp.where(upper, high, low)
        arrived = swap(jnp.where(upper, low, high), axis, size, step)
        step //= 2
        if step == 0:
            return kept, arrived
        value = kept + arrived


def join(value, axis, size, dim):
    index = lax.axis_index(axis)
    step = 1
    while step < size:
        arrived = swap(value, axis, size, step)
        value = jnp.where(
            (index & step) == 0,
            jnp.concatenate([value, arrived], axis=dim),
            jnp.concatenate([arrived, value], axis=dim),
        )
        step *= 2
    return value


def after(value, event):
    return lax.optimization_barrier((value, event))


def chunk_sizes(block):
    if block % 2048 == 0:
        return [block // 4, block // 4, block // 2]
    return [block]


def shards(sizes, counts, tile_mask, tile_counts, gene_factor, prev_factor):
    cells, genes, subs = sizes
    rows, columns = counts.shape
    width = gene_factor.shape[0]
    tile = rows // tile_mask.shape[0]
    sub = lax.axis_index("sub")
    cell = lax.axis_index("cell")
    gene = lax.axis_index("gene")
    line = Line(cells, cell)
    meta = jnp.stack([sub, cell, sub * genes + gene, line.block(1, 0)]).astype(jnp.int32)
    factor = tile_mask.astype(F32) / tile_counts.astype(F32)

    gram = contract_last(gene_factor, gene_factor)
    factor, gram = after(factor, gram)
    gram = pair_sums(gram, "gene", genes)
    row_tiles = rows // tile
    early = row_tiles // 4 * 3
    scales = jnp.broadcast_to(factor[:, :, None], factor.shape + (tile,))
    scales = scales.reshape(row_tiles, columns)
    cross = [cross_tile(counts, scales, gene_factor, row) for row in range(early)]
    scales, gram = after(scales, gram)
    gram_other = swap(gram, "sub", subs, 1)
    cross += [cross_tile(counts, scales, gene_factor, row) for row in range(early, row_tiles)]
    low = jnp.concatenate(cross[: row_tiles // 2], axis=0)
    high = jnp.concatenate(cross[row_tiles // 2 :], axis=0)
    arrived = swap(jnp.where(sub == 0, high, low), "sub", subs, 1)
    cross = jnp.where(sub == 0, low, high) + arrived
    cross_a, cross_b = split_sums(cross, "gene", genes)
    inverse, rho = shifted_inverse(gram, gram_other)
    share = admm(meta, rho, cross_a, cross_b, inverse, prev_factor)
    own = join(share, "gene", genes, 1)
    other = swap(own, "sub", subs, 1)

    block = columns // cells
    chunks = chunk_sizes(block)
    starts = [sum(chunks[:i]) for i in range(len(chunks))]
    arrived = [[], []]
    for start, chunk in zip(starts, chunks):
        first = products(
            lambda o, m: m[3], 1, block, start, chunk, BF16, tile, meta, factor, counts, own, other
        )[0]
        meta, first = after(meta, first)
        for parity in (0, 1):
            sends = line.pairs(1, parity)
            arrived[parity].append(line.send(first, 1, parity) if sends else None)
    totals = []
    for index, (start, chunk) in enumerate(zip(starts, chunks)):
        meta, arrived[0][index] = after(meta, arrived[0][index])
        total = products(
            lambda o, m: o, cells, block, start, chunk, F32, tile, meta, factor, counts, own, other
        )
        meta, total = after(meta, total)
        totals.append(total)
    for phase in range(2, cells):
        for index, total in enumerate(totals):
            values = []
            for parity in (0, 1):
                value = lax.dynamic_index_in_dim(total, line.block(phase, parity), 0, False)
                before = arrived[1 - parity][index]
                if before is not None:
                    value = value + before.astype(F32)
                values.append(value.astype(BF16))
            for parity in (0, 1):
                arrived[parity][index] = line.send(values[parity], phase, parity)
    data_products = None
    for index, start in enumerate(starts):
        data_products = keep(
            block, start, meta, totals[index], arrived[0][index], arrived[1][index], data_products
        )

    own, _ = after(own, totals[0])
    whole = jnp.where(
        sub == 0,
        jnp.concatenate([own, other], axis=1),
        jnp.concatenate([other, own], axis=1),
    )
    new_factor = whole.T
    part = width // (genes * subs)
    gram_rows = contract_last(
        lax.dynamic_slice_in_dim(whole, (gene * subs + sub) * part, part, 0), whole
    )
    step = 1
    while step < cells:
        gram_rows = gram_rows.astype(BF16)
        gram_rows = gram_rows.astype(F32) + swap(gram_rows, "cell", cells, step).astype(F32)
        step *= 2
    factor_gram = join(join(gram_rows, "sub", subs, 0), "gene", genes, 0)
    return (new_factor, factor_gram, data_products)


def solution(mesh):
    sizes = (mesh.shape["cell"], mesh.shape["gene"], mesh.shape["sub"])
    return jax.shard_map(
        functools.partial(shards, sizes),
        mesh=mesh,
        in_specs=(
            P(("groups", "cell"), ("gene", "sub")),
            P(("groups", "cell"), ("gene", "sub")),
            P(("groups", "cell"), ("gene", "sub")),
            P("groups", ("gene", "sub")),
            P(("groups", "cell"), None),
        ),
        out_specs=(
            P(("groups", "cell"), None),
            P("groups", None),
            P(("groups", "gene", "sub", "cell"), None),
        ),
        check_vma=False,
    )
```

time: 178 us -> 158 us (0.89)
  waiting for transfers between devices: 85 us -> 27 us
  starting transfers between devices: 9.93 us -> 62 us
  Pallas kernels: 54.2 us -> 37.2 us
  matrix products: 0.29 us -> 16.7 us
  between operations: 14.2 us -> 1.19 us
  other arithmetic: 3.49 us -> 10.2 us
  blocking collectives: 5.81 us -> 0 us
    reduce_scatter x2 -> x0, waiting for transfers between devices: 54.6 us -> none  [shards(): part = lax.psum_scatter(part, 'cell', scatter_dimension=0)]
    ppermute x0 -> x15, starting transfers between devices: none -> 54.1 us  [send(): return lax.ppermute(value, 'cell', self.pairs(phase, parity))]
    dot_general x1 -> x6, matrix products: 0.29 us -> 16.7 us  [contract_last(): lax.dot_general(left, right, (((1,), (1,)), ((), ())), preferred_element_...]
    pallas_call x2 -> x3, Pallas kernels: 21.3 us -> 7.02 us  [keep(): pl.pallas_call(keep_kernel, out_shape=jax.ShapeDtypeStruct((block, width)...]
    ppermute x8 -> x10, waiting for transfers between devices: 30.4 us -> 17.9 us  [swap(): return lax.ppermute(value, axis, [(i, i ^ step) for i in range(size)])]
    ppermute x0 -> x15, waiting for transfers between devices: none -> 9.06 us  [send(): return lax.ppermute(value, 'cell', self.pairs(phase, parity))]
    convert_element_type x0 -> x7, other arithmetic: none -> 7.71 us  [the longest x6 7.7 us: shards(): values.append(value.astype(BF16))]
    all_gather x1 -> x0, blocking collectives: 5.81 us -> none  [shards(): factor_gram = lax.all_gather(gram_rows, ('gene', 'sub'), axis=0, tiled=True)]
  transfers between devices with their start and end apart: 10 -> 25, of which waited for: 8 -> 8; matrix products, arithmetic and copies ran while one was open for 1% -> 12% of each run, Pallas kernels for 10% -> 20%
where the time goes in v3:
time: 158 us; the launch traced here: 157 us
  starting transfers between devices  62 us (39%)
  Pallas kernels  37.2 us (24%)
  waiting for transfers between devices  27 us (17%)
  matrix products  16.7 us (11%)
  other arithmetic  10.2 us (6%)
  local copies, waits for them, and re-layouts  2.66 us (2%)
    ppermute x15, starting transfers between devices, send(): return lax.ppermute(value, 'cell', self.pairs(phase, parity))  54.1 us
    pallas_call x6, Pallas kernels, products(): pl.pallas_call(functools.partial(products_kernel, tile, wide, place), out...  24.6 us
    ppermute x10, waiting for transfers between devices, swap(): return lax.ppermute(value, axis, [(i, i ^ step) for i in range(size)])  17.9 us
    dot_general x6, matrix products, contract_last(): lax.dot_general(left, right, (((1,), (1,)), ((), ())), preferred_element_...  16.7 us
    ppermute x15, waiting for transfers between devices, send(): return lax.ppermute(value, 'cell', self.pairs(phase, parity))  9.06 us
    ppermute x10, starting transfers between devices, swap(): return lax.ppermute(value, axis, [(i, i ^ step) for i in range(size)])  7.95 us
    convert_element_type x6, other arithmetic, shards(): values.append(value.astype(BF16))  7.7 us
    pallas_call x3, Pallas kernels, keep(): pl.pallas_call(keep_kernel, out_shape=jax.ShapeDtypeStruct((block, width)...  7.02 us
  transfers between devices with their start and end apart: 25, of which 8 were waited for; matrix products, arithmetic and copies ran while one was open for 12% of the time, Pallas kernels for 20%

profile of v3, /device:TPU:0, one launch (start us, length us, event | category | flops | bytes accessed | tf_op | source)
XLA Modules:
  0.0 156.9 jit_solution(17684293971360558662)
XLA Ops:
  0.7 4.9 %fusion.24 = f32[256,256]{1,0:T(8,128)S(1)} fusion(bf16[256,8192]{1,0:T(8,128)(2,1)} %param.8), kind=kOutput, calls=%fused_computation.61 | convolution fusion | flops 1073741824 | bytes 4456448 | tf_op jit(solution)/shard_map/dot_general | solution.py:25
  5.6 3.0 %collective-permute-start = (f32[256,256]{1,0:T(8,128)S(1)}, f32[256,256]{1,0:T(8,128)S(1)}, u32[]{:S(2)}, u32[]{:S(2)}) collective-permute-start(f32[256,256]{1,0:T(8,128)S(1)} %fusion.24), channel_id=1, source_target_pairs={{0,2},{2,0},{1,3},{3,1},{4,6},{6,4},{5,7},{7,5},{8,10},{10,8},{9,1... | collective-permute-start | bytes 786440 | tf_op jit(solution)/shard_map/ppermute | solution.py:255
  8.6 0.1 broadcast_bitcast_fusion.3
  8.7 0.1 broadcast_bitcast_fusion.1
  8.8 4.2 %fusion.1 = f32[256,256]{1,0:T(8,128)S(1)} fusion(bf16[256,8192]{1,0:T(8,128)(2,1)S(1)} %copy-done.10, f32[8192]{0:T(1024)S(1)} %bitcast.80, bf16[1024,8192]{1,0:T(8,128)(2,1)} %counts.11), kind=kOutput, calls=%fused_computation.5 | convolution fusion | flops 1080033280 | bytes 8683520 | tf_op jit(solution)/shard_map/dot_general | solution.py:25
  13.0 1.3 fusion.2
  14.3 1.3 fusion
  15.6 0.1 broadcast_bitcast_fusion
  15.7 0.1 copy.11
  15.9 4.8 %fusion.3 = f32[256,256]{1,0:T(8,128)S(1)} fusion(bf16[256,8192]{1,0:T(8,128)(2,1)} %param.8, f32[8192]{0:T(1024)S(1)} %bitcast.81, bf16[1024,8192]{1,0:T(8,128)(2,1)} %counts.11), kind=kOutput, calls=%fused_computation.7 | convolution fusion | flops 1080033280 | bytes 8683520 | tf_op jit(solution)/shard_map/dot_general | solution.py:25
  20.8 0.1 collective-permute-start.2
  20.9 0.5 collective-permute-start.1
  21.4 1.4 collective-permute-done.2
  22.8 0.1 select_add_fusion
  22.9 1.4 collective-permute-start.3
  24.3 0.1 pad_add_fusion.meta
  24.4 3.5 %inverse.1 = (f32[256,256]{1,0:T(8,128)S(1)}, f32[1,1]{1,0:T(1,128)}) custom-call(f32[256,256]{1,0:T(8,128)S(1)} %add.98.gram_a, f32[256,256]{1,0:T(8,128)S(1)} %collective-permute-done.1.gram_b), custom_call_target="tpu_custom_call" | custom-call | flops 2013265920 | bytes 786432 | tf_op jit(solution)/shard_map/inverse/pallas_call | solution.py:91
  27.9 3.4 %collective-permute-done.3.cross_b = f32[256,256]{1,0:T(8,128)S(1)} collective-permute-done((f32[256,256]{1,0:T(8,128)S(1)}, f32[256,256]{1,0:T(8,128)S(1)}, u32[]{:S(2)}, u32[]{:S(2)}) %collective-permute-start.3) | collective-permute-done | bytes 262176 | tf_op jit(solution)/shard_map/ppermute | solution.py:255
  31.3 2.1 %admm.1 = bf16[256,256]{1,0:T(8,128)(2,1)S(1)} custom-call(s32[4]{0:T(128)S(1)} %pad_add_fusion.meta, f32[1,1]{1,0:T(1,128)} %get-tuple-element.31.rho_ref, f32[256,256]{1,0:T(8,128)S(1)} %get-tuple-element.63.cross_a, f32[256,256]{1,0:T(8,128)S(1)} %collective-permute-done.3.cross_b, f32[256,256]{1,0:T(8,128)S(1)} %get-tuple-element.33.inverse, ...), custom_call_target="tpu_custom_call" | custom-call | flops 301989888 | bytes 786432 | tf_op jit(solution)/shard_map/admm/pallas_call | solution.py:121
  33.4 1.4 collective-permute-start.4
  34.8 3.6 %collective-permute-done.4 = bf16[256,256]{1,0:T(8,128)(2,1)S(1)} collective-permute-done((bf16[256,256]{1,0:T(8,128)(2,1)S(1)}, bf16[256,256]{1,0:T(8,128)(2,1)S(1)}, u32[]{:S(2)}, u32[]{:S(2)}) %collective-permute-start.4) | collective-permute-done | bytes 131104 | tf_op jit(solution)/shard_map/ppermute | solution.py:255
  38.5 0.1 maximum_select_fusion.1.own
  38.7 1.5 collective-permute-done.5.other
  40.2 2.2 %products.6 = bf16[1,256,512]{2,1,0:T(8,128)(2,1)S(1)} custom-call(s32[4]{0:T(128)S(1)} %pad_add_fusion.meta, f32[4,32]{1,0:T(4,128)S(1)} %convert_divide_fusion.factor, bf16[1024,8192]{1,0:T(8,128)(2,1)} %counts.11, bf16[256,512]{1,0:T(8,128)(2,1)S(1)} %maximum_select_fusion.1.own, bf16[256,512]{1,0:T(8,128)(2,1)S(1)} %collective-permute-done.5.other), custom_call_target="tpu_custom_call" | custom-call | flops 1 | bytes 1 | tf_op jit(solution)/shard_map/products/pallas_call | solution.py:183
  42.4 4.6 %collective-permute-start.6 = (bf16[256,512]{1,0:T(8,128)(2,1)S(1)}, bf16[256,512]{1,0:T(8,128)(2,1)}, u32[]{:S(2)}, u32[]{:S(2)}) collective-permute-start(bf16[256,512]{1,0:T(8,128)(2,1)S(1)} %bitcast.74), channel_id=1, source_target_pairs={{0,4},{12,8},{1,5},{13,9},{2,6},{14,10},{3,7},{15,11},{16,20},{28,... | collective-permute-start | bytes 786440 | tf_op jit(solution)/shard_map/ppermute | solution.py:251
  47.0 2.2 %products.7 = bf16[1,256,512]{2,1,0:T(8,128)(2,1)S(1)} custom-call(s32[4]{0:T(128)S(1)} %pad_add_fusion.meta, f32[4,32]{1,0:T(4,128)S(1)} %convert_divide_fusion.factor, bf16[1024,8192]{1,0:T(8,128)(2,1)} %counts.11, bf16[256,512]{1,0:T(8,128)(2,1)S(1)} %maximum_select_fusion.1.own, bf16[256,512]{1,0:T(8,128)(2,1)S(1)} %collective-permute-done.5.other), custom_call_target="tpu_custom_call" | custom-call | flops 1 | bytes 1 | tf_op jit(solution)/shard_map/products/pallas_call | solution.py:183
  49.3 2.0 %collective-permute-start.11 = (bf16[256,512]{1,0:T(8,128)(2,1)S(1)}, bf16[256,512]{1,0:T(8,128)(2,1)}, u32[]{:S(2)}, u32[]{:S(2)}) collective-permute-start(bf16[256,512]{1,0:T(8,128)(2,1)S(1)} %bitcast.75), channel_id=1, source_target_pairs={{0,4},{12,8},{1,5},{13,9},{2,6},{14,10},{3,7},{15,11},{16,20},{28,... | collective-permute-start | bytes 786440 | tf_op jit(solution)/shard_map/ppermute | solution.py:251
  51.3 2.8 %products.8 = bf16[1,256,1024]{2,1,0:T(8,128)(2,1)S(1)} custom-call(s32[4]{0:T(128)S(1)} %pad_add_fusion.meta, f32[4,32]{1,0:T(4,128)S(1)} %convert_divide_fusion.factor, bf16[1024,8192]{1,0:T(8,128)(2,1)} %counts.11, bf16[256,512]{1,0:T(8,128)(2,1)S(1)} %maximum_select_fusion.1.own, bf16[256,512]{1,0:T(8,128)(2,1)S(1)} %collective-permute-done.5.other), custom_call_target="tpu_custom_call" | custom-call | flops 1 | bytes 1 | tf_op jit(solution)/shard_map/products/pallas_call | solution.py:183
  54.1 2.1 %collective-permute-start.12 = (bf16[256,1024]{1,0:T(8,128)(2,1)S(1)}, bf16[256,1024]{1,0:T(8,128)(2,1)}, u32[]{:S(2)}, u32[]{:S(2)}) collective-permute-start(bf16[256,1024]{1,0:T(8,128)(2,1)S(1)} %bitcast.73), channel_id=1, source_target_pairs={{0,4},{12,8},{1,5},{13,9},{2,6},{14,10},{3,7},{15,11},{16,20},{28,... | collective-permute-start | bytes 1572872 | tf_op jit(solution)/shard_map/ppermute | solution.py:251
  56.2 4.5 %products.9.total = f32[4,256,512]{2,1,0:T(8,128)S(1)} custom-call(s32[4]{0:T(128)S(1)} %pad_add_fusion.meta, f32[4,32]{1,0:T(4,128)S(1)} %convert_divide_fusion.factor, bf16[1024,8192]{1,0:T(8,128)(2,1)} %counts.11, bf16[256,512]{1,0:T(8,128)(2,1)S(1)} %maximum_select_fusion.1.own, bf16[256,512]{1,0:T(8,128)(2,1)S(1)} %collective-permute-done.5.other), custom_call_target="tpu_custom_call" | custom-call | flops 1 | bytes 1 | tf_op jit(solution)/shard_map/products/pallas_call | solution.py:183
  60.8 2.5 %collective-permute-start.23 = (bf16[256,512]{1,0:T(8,128)(2,1)S(1)}, bf16[256,512]{1,0:T(8,128)(2,1)S(1)}, u32[]{:S(2)}, u32[]{:S(2)}) collective-permute-start(bf16[256,512]{1,0:T(8,128)(2,1)S(1)} %bitcast_convert_fusion.1), channel_id=1, source_target_pairs={{0,4},{12,8},{1,5},{13,9},{2,6},{14,10},{3,7},{15,11},{16,20},{28,... | collective-permute-start | bytes 786440 | tf_op jit(solution)/shard_map/ppermute | solution.py:251
  63.3 0.1 maximum_select_fusion
  63.5 0.3 convolution_convert_fusion
  63.9 4.6 %products.10.total = f32[4,256,512]{2,1,0:T(8,128)S(1)} custom-call(s32[4]{0:T(128)S(1)} %pad_add_fusion.meta, f32[4,32]{1,0:T(4,128)S(1)} %convert_divide_fusion.factor, bf16[1024,8192]{1,0:T(8,128)(2,1)} %counts.11, bf16[256,512]{1,0:T(8,128)(2,1)S(1)} %maximum_select_fusion.1.own, bf16[256,512]{1,0:T(8,128)(2,1)S(1)} %collective-permute-done.5.other), custom_call_target="tpu_custom_call" | custom-call | flops 1 | bytes 1 | tf_op jit(solution)/shard_map/products/pallas_call | solution.py:183
  68.4 1.4 collective-permute-done.12
  69.8 8.3 %products.11.total = f32[4,256,1024]{2,1,0:T(8,128)S(1)} custom-call(s32[4]{0:T(128)S(1)} %pad_add_fusion.meta, f32[4,32]{1,0:T(4,128)S(1)} %convert_divide_fusion.factor, bf16[1024,8192]{1,0:T(8,128)(2,1)} %counts.11, bf16[256,512]{1,0:T(8,128)(2,1)S(1)} %maximum_select_fusion.1.own, bf16[256,512]{1,0:T(8,128)(2,1)S(1)} %collective-permute-done.5.other), custom_call_target="tpu_custom_call" | custom-call | flops 1 | bytes 1 | tf_op jit(solution)/shard_map/products/pallas_call | solution.py:183
  78.2 0.1 bitcast_convert_fusion
  78.2 4.6 %collective-permute-start.15 = (bf16[256,1024]{1,0:T(8,128)(2,1)S(1)}, bf16[256,1024]{1,0:T(8,128)(2,1)S(1)}, u32[]{:S(2)}, u32[]{:S(2)}) collective-permute-start(bf16[256,1024]{1,0:T(8,128)(2,1)S(1)} %bitcast_convert_fusion), channel_id=1, source_target_pairs={{0,4},{12,8},{1,5},{13,9},{2,6},{14,10},{3,7},{15,11},{16,20},{28,... | collective-permute-start | bytes 1572872 | tf_op jit(solution)/shard_map/ppermute | solution.py:251
  82.8 0.4 collective-permute-start.8
  83.3 4.6 %collective-permute-start.19 = (bf16[256,512]{1,0:T(8,128)(2,1)S(1)}, bf16[256,512]{1,0:T(8,128)(2,1)S(1)}, u32[]{:S(2)}, u32[]{:S(2)}) collective-permute-start(bf16[256,512]{1,0:T(8,128)(2,1)S(1)} %bitcast_convert_fusion.2), channel_id=1, source_target_pairs={{0,4},{12,8},{1,5},{13,9},{2,6},{14,10},{3,7},{15,11},{16,20},{28,... | collective-permute-start | bytes 786440 | tf_op jit(solution)/shard_map/ppermute | solution.py:251
  87.9 8.0 %collective-permute-done.8 = bf16[64,256]{1,0:T(8,128)(2,1)S(1)} collective-permute-done((bf16[64,256]{1,0:T(8,128)(2,1)S(1)}, bf16[64,256]{1,0:T(8,128)(2,1)S(1)}, u32[]{:S(2)}, u32[]{:S(2)}) %collective-permute-start.8) | collective-permute-done | bytes 32800 | tf_op jit(solution)/shard_map/ppermute | solution.py:255
  95.9 2.2 %fusion.12 = (bf16[256,1024]{1,0:T(8,128)(2,1)}, bf16[256,1024]{1,0:T(8,128)(2,1)S(1)}) fusion(bf16[256,1024]{1,0:T(8,128)(2,1)S(1)} %collective-permute-done.15, f32[4,256,1024]{2,1,0:T(8,128)S(1)} %products.11.total, s32[]{:T(128)S(6)} %select_n.143, bf16[256,1024]{1,0:T(8,128)(2,1)} %collective-permute-done.12, s32[]{:T(128)S(6)} %select_n.140), kind=kLoop, calls=%fused_computation.18 | loop fusion | flops 1572864 | bytes 4194312 | tf_op jit(solution)/shard_map/convert_element_type | solution.py:365
  98.1 0.7 collective-permute-start.13
  98.9 1.0 collective-permute-start.10
  99.8 1.1 fusion.15
  101.0 0.7 collective-permute-start.24
  101.6 0.7 collective-permute-start.21
  102.3 1.8 %fusion.18 = (bf16[256,512]{1,0:T(8,128)(2,1)}, bf16[256,512]{1,0:T(8,128)(2,1)S(1)}) fusion(bf16[256,512]{1,0:T(8,128)(2,1)S(1)} %collective-permute-done.19, f32[4,256,512]{2,1,0:T(8,128)S(1)} %products.10.total, s32[]{:T(128)S(6)} %select_n.143, bf16[256,512]{1,0:T(8,128)(2,1)} %collective-permute-done.11, s32[]{:T(128)S(6)} %select_n.140), kind=kLoop, calls=%fused_computation.35 | loop fusion | flops 786432 | bytes 2097160 | tf_op jit(solution)/shard_map/convert_element_type | solution.py:365
  104.2 0.7 collective-permute-start.17
  104.8 0.7 collective-permute-start.16
  105.5 1.0 fusion.14
  106.5 22.9 %collective-permute-start.14 = (bf16[256,1024]{1,0:T(8,128)(2,1)}, bf16[256,1024]{1,0:T(8,128)(2,1)S(1)}, u32[]{:S(2)}, u32[]{:S(2)}) collective-permute-start(bf16[256,1024]{1,0:T(8,128)(2,1)} %fusion.14), channel_id=1, source_target_pairs={{0,4},{8,12},{4,0},{12,8},{1,5},{9,13},{5,1},{13,9},{2,6},{10,14},... | collective-permute-start | bytes 1572872 | tf_op jit(solution)/shard_map/ppermute | solution.py:251
  129.4 0.8 fusion.17
  130.3 4.8 %collective-permute-start.22 = (bf16[256,512]{1,0:T(8,128)(2,1)}, bf16[256,512]{1,0:T(8,128)(2,1)}, u32[]{:S(2)}, u32[]{:S(2)}) collective-permute-start(bf16[256,512]{1,0:T(8,128)(2,1)} %fusion.17), channel_id=1, source_target_pairs={{0,4},{8,12},{4,0},{12,8},{1,5},{9,13},{5,1},{13,9},{2,6},{10,14},... | collective-permute-start | bytes 786440 | tf_op jit(solution)/shard_map/ppermute | solution.py:251
  135.1 0.8 fusion.20
  135.9 1.4 collective-permute-start.20
  137.3 1.1 collective-permute-start.18
  138.4 2.0 %copy.10 = bf16[1024,256]{1,0:T(8,128)(2,1)} copy(bf16[1024,256]{0,1:T(8,128)(2,1)} %bitcast.76) | data formatting | bytes 1048576
  140.4 1.9 %maximum_select_fusion.2 = f32[256,256]{1,0:T(8,128)} fusion(f32[128,256]{1,0:T(8,128)} %copy-done.7, f32[128,256]{1,0:T(8,128)S(1)} %maximum_select_fusion.3, pred[]{:T(512)S(6)} %eq.11), kind=kLoop, calls=%fused_computation.44 | loop fusion | flops 196608 | bytes 524289 | tf_op jit(solution)/shard_map/jit(_where)/select_n | solution.py:285
  142.2 6.0 %collective-permute-done.22.first = bf16[256,512]{1,0:T(8,128)(2,1)} collective-permute-done((bf16[256,512]{1,0:T(8,128)(2,1)}, bf16[256,512]{1,0:T(8,128)(2,1)}, u32[]{:S(2)}, u32[]{:S(2)}) %collective-permute-start.22) | collective-permute-done | bytes 262176 | tf_op jit(solution)/shard_map/ppermute | solution.py:251
  148.2 2.5 %keep.3.refs_0_ = f32[2048,256]{1,0:T(8,128)} custom-call(s32[4]{0:T(128)S(1)} %pad_add_fusion.meta, f32[4,256,512]{2,1,0:T(8,128)S(1)} %products.9.total, bf16[256,512]{1,0:T(8,128)(2,1)} %collective-permute-done.22.first, bf16[256,512]{1,0:T(8,128)(2,1)S(1)} %collective-permute-done.24.second), custom_call_target="tpu_custom_call" | custom-call | flops 393216 | bytes 1572864 | tf_op jit(solution)/shard_map/keep/pallas_call | solution.py:213
  150.7 1.7 %collective-permute-done.18.first = bf16[256,512]{1,0:T(8,128)(2,1)} collective-permute-done((bf16[256,512]{1,0:T(8,128)(2,1)}, bf16[256,512]{1,0:T(8,128)(2,1)}, u32[]{:S(2)}, u32[]{:S(2)}) %collective-permute-start.18) | collective-permute-done | bytes 262176 | tf_op jit(solution)/shard_map/ppermute | solution.py:251
  152.4 2.6 %keep.4.refs_0_ = f32[2048,256]{1,0:T(8,128)} custom-call(s32[4]{0:T(128)S(1)} %pad_add_fusion.meta, f32[4,256,512]{2,1,0:T(8,128)S(1)} %copy-done.3, bf16[256,512]{1,0:T(8,128)(2,1)} %collective-permute-done.18.first, bf16[256,512]{1,0:T(8,128)(2,1)} %collective-permute-done.20.second, f32[2048,256]{1,0:T(8,128)} %keep.3.refs_0_), custom_call_target="tpu_custom_call", output_to_operand_aliasing={{}: (4, {})} | custom-call | flops 393216 | bytes 1572864 | tf_op jit(solution)/shard_map/keep/pallas_call | solution.py:213
  155.0 2.0 %keep.5 = f32[2048,256]{1,0:T(8,128)} custom-call(s32[4]{0:T(128)S(1)} %pad_add_fusion.meta, f32[4,256,1024]{2,1,0:T(8,128)S(1)} %copy-done.1, bf16[256,1024]{1,0:T(8,128)(2,1)S(1)} %collective-permute-done.14.first, bf16[256,1024]{1,0:T(8,128)(2,1)S(1)} %collective-permute-done.16.second, f32[2048,256]{1,0:T(8,128)} %keep.4.refs_0_), custom_call_target="tpu_custom_call", output_to_operand_aliasing={{}: (4, {})} | custom-call | flops 786432 | bytes 3145728 | tf_op jit(solution)/shard_map/keep/pallas_call | solution.py:213
  (56 shorter events, 0.7 us)
Async XLA Ops:
  0.6 8.2 %copy-start.10 = (bf16[256,8192]{1,0:T(8,128)(2,1)S(1)}, bf16[256,8192]{1,0:T(8,128)(2,1)}, u32[]{:S(2)}) copy-start(bf16[256,8192]{1,0:T(8,128)(2,1)} %param.8) | copy-start | bytes 12582916
  0.6 4.9 %copy-start.8 = (s32[4,32]{1,0:T(4,128)S(1)}, s32[4,32]{1,0:T(4,128)}, u32[]{:S(2)}) copy-start(s32[4,32]{1,0:T(4,128)} %param.7) | copy-start | bytes 1540
  0.7 4.9 %copy-start.9 = (s32[4,32]{1,0:T(4,128)S(1)}, s32[4,32]{1,0:T(4,128)}, u32[]{:S(2)}) copy-start(s32[4,32]{1,0:T(4,128)} %param.6) | copy-start | bytes 1540
  0.7 12.3 %copy-start.5 = (bf16[1024,8192]{1,0:T(8,128)(2,1)S(1)}, bf16[1024,8192]{1,0:T(8,128)(2,1)}, u32[]{:S(2)}) copy-start(bf16[1024,8192]{1,0:T(8,128)(2,1)} %counts.11) | copy-start | bytes 50331652
  5.6 10.2 %collective-permute-start = (f32[256,256]{1,0:T(8,128)S(1)}, f32[256,256]{1,0:T(8,128)S(1)}, u32[]{:S(2)}, u32[]{:S(2)}) collective-permute-start(f32[256,256]{1,0:T(8,128)S(1)} %fusion.24), channel_id=1, source_target_pairs={{0,2},{2,0},{1,3},{3,1},{4,6},{6,4},{5,7},{7,5},{8,10},{10,8},{9,1... | collective-permute-start | bytes 786440 | tf_op jit(solution)/shard_map/ppermute | solution.py:255
  20.8 2.0 %collective-permute-start.2 = (f32[512,256]{1,0:T(8,128)S(1)}, f32[512,256]{1,0:T(8,128)S(1)}, u32[]{:S(2)}, u32[]{:S(2)}) collective-permute-start(f32[512,256]{1,0:T(8,128)S(1)} %fusion.21), channel_id=1, source_target_pairs={{0,1},{1,0},{2,3},{3,2},{4,5},{5,4},{6,7},{7,6},{8,9},{9,8},{10,11... | collective-permute-start | bytes 1572872 | tf_op jit(solution)/shard_map/ppermute | solution.py:255
  20.9 3.5 %collective-permute-start.1 = (f32[256,256]{1,0:T(8,128)S(1)}, f32[256,256]{1,0:T(8,128)S(1)}, u32[]{:S(2)}, u32[]{:S(2)}) collective-permute-start(f32[256,256]{1,0:T(8,128)S(1)} %add.98.gram_a), channel_id=1, source_target_pairs={{0,1},{1,0},{2,3},{3,2},{4,5},{5,4},{6,7},{7,6},{8,9},{9,8},{10,11... | collective-permute-start | bytes 786440 | tf_op jit(solution)/shard_map/ppermute | solution.py:255
  22.9 8.5 %copy-start.4 = (bf16[1024,256]{1,0:T(8,128)(2,1)S(1)}, bf16[1024,256]{1,0:T(8,128)(2,1)}, u32[]{:S(2)}) copy-start(bf16[1024,256]{1,0:T(8,128)(2,1)} %start.1) | copy-start | bytes 1572868
  22.9 8.4 %collective-permute-start.3 = (f32[256,256]{1,0:T(8,128)S(1)}, f32[256,256]{1,0:T(8,128)S(1)}, u32[]{:S(2)}, u32[]{:S(2)}) collective-permute-start(f32[256,256]{1,0:T(8,128)S(1)} %get-tuple-element.62), channel_id=1, source_target_pairs={{0,2},{2,0},{1,3},{3,1},{4,6},{6,4},{5,7},{7,5},{8,10},{10,8},{9,1... | collective-permute-start | bytes 786440 | tf_op jit(solution)/shard_map/ppermute | solution.py:255
  33.4 5.0 %collective-permute-start.4 = (bf16[256,256]{1,0:T(8,128)(2,1)S(1)}, bf16[256,256]{1,0:T(8,128)(2,1)S(1)}, u32[]{:S(2)}, u32[]{:S(2)}) collective-permute-start(bf16[256,256]{1,0:T(8,128)(2,1)S(1)} %admm.1), channel_id=1, source_target_pairs={{0,2},{2,0},{1,3},{3,1},{4,6},{6,4},{5,7},{7,5},{8,10},{10,8},{9,1... | collective-permute-start | bytes 393224 | tf_op jit(solution)/shard_map/ppermute | solution.py:255
  38.6 1.6 %collective-permute-start.5 = (bf16[256,512]{1,0:T(8,128)(2,1)S(1)}, bf16[256,512]{1,0:T(8,128)(2,1)S(1)}, u32[]{:S(2)}, u32[]{:S(2)}) collective-permute-start(bf16[256,512]{1,0:T(8,128)(2,1)S(1)} %maximum_select_fusion.1.own), channel_id=1, source_target_pairs={{0,1},{1,0},{2,3},{3,2},{4,5},{5,4},{6,7},{7,6},{8,9},{9,8},{10,11... | collective-permute-start | bytes 786440 | tf_op jit(solution)/shard_map/ppermute | solution.py:255
  42.4 13.8 %collective-permute-start.6 = (bf16[256,512]{1,0:T(8,128)(2,1)S(1)}, bf16[256,512]{1,0:T(8,128)(2,1)}, u32[]{:S(2)}, u32[]{:S(2)}) collective-permute-start(bf16[256,512]{1,0:T(8,128)(2,1)S(1)} %bitcast.74), channel_id=1, source_target_pairs={{0,4},{12,8},{1,5},{13,9},{2,6},{14,10},{3,7},{15,11},{16,20},{28,... | collective-permute-start | bytes 786440 | tf_op jit(solution)/shard_map/ppermute | solution.py:251
  49.3 11.5 %collective-permute-start.11 = (bf16[256,512]{1,0:T(8,128)(2,1)S(1)}, bf16[256,512]{1,0:T(8,128)(2,1)}, u32[]{:S(2)}, u32[]{:S(2)}) collective-permute-start(bf16[256,512]{1,0:T(8,128)(2,1)S(1)} %bitcast.75), channel_id=1, source_target_pairs={{0,4},{12,8},{1,5},{13,9},{2,6},{14,10},{3,7},{15,11},{16,20},{28,... | collective-permute-start | bytes 786440 | tf_op jit(solution)/shard_map/ppermute | solution.py:251
  54.1 15.7 %collective-permute-start.12 = (bf16[256,1024]{1,0:T(8,128)(2,1)S(1)}, bf16[256,1024]{1,0:T(8,128)(2,1)}, u32[]{:S(2)}, u32[]{:S(2)}) collective-permute-start(bf16[256,1024]{1,0:T(8,128)(2,1)S(1)} %bitcast.73), channel_id=1, source_target_pairs={{0,4},{12,8},{1,5},{13,9},{2,6},{14,10},{3,7},{15,11},{16,20},{28,... | collective-permute-start | bytes 1572872 | tf_op jit(solution)/shard_map/ppermute | solution.py:251
  60.8 39.0 %collective-permute-start.23 = (bf16[256,512]{1,0:T(8,128)(2,1)S(1)}, bf16[256,512]{1,0:T(8,128)(2,1)S(1)}, u32[]{:S(2)}, u32[]{:S(2)}) collective-permute-start(bf16[256,512]{1,0:T(8,128)(2,1)S(1)} %bitcast_convert_fusion.1), channel_id=1, source_target_pairs={{0,4},{12,8},{1,5},{13,9},{2,6},{14,10},{3,7},{15,11},{16,20},{28,... | collective-permute-start | bytes 786440 | tf_op jit(solution)/shard_map/ppermute | solution.py:251
  63.5 4.9 %copy-start.6 = (bf16[256,1024]{1,0:T(8,128)(2,1)}, bf16[256,1024]{1,0:T(8,128)(2,1)S(1)}, u32[]{:S(2)}) copy-start(bf16[256,1024]{1,0:T(8,128)(2,1)S(1)} %maximum_select_fusion) | copy-start | bytes 1572868
  63.8 19.0 %collective-permute-start.7 = (bf16[64,256]{1,0:T(8,128)(2,1)S(1)}, bf16[64,256]{1,0:T(8,128)(2,1)S(1)}, u32[]{:S(2)}, u32[]{:S(2)}) collective-permute-start(bf16[64,256]{1,0:T(8,128)(2,1)S(1)} %convolution_convert_fusion), channel_id=1, source_target_pairs={{0,4},{4,0},{8,12},{12,8},{1,5},{5,1},{9,13},{13,9},{2,6},{6,2},{1... | collective-permute-start | bytes 98312 | tf_op jit(solution)/shard_map/ppermute | solution.py:255
  68.4 66.6 %copy-start.2 = (f32[4,256,512]{2,1,0:T(8,128)}, f32[4,256,512]{2,1,0:T(8,128)S(1)}, u32[]{:S(2)}) copy-start(f32[4,256,512]{2,1,0:T(8,128)S(1)} %products.10.total) | copy-start | bytes 6291460
  78.1 27.4 %copy-start = (f32[4,256,1024]{2,1,0:T(8,128)}, f32[4,256,1024]{2,1,0:T(8,128)S(1)}, u32[]{:S(2)}) copy-start(f32[4,256,1024]{2,1,0:T(8,128)S(1)} %products.11.total) | copy-start | bytes 12582916
  78.2 17.7 %collective-permute-start.15 = (bf16[256,1024]{1,0:T(8,128)(2,1)S(1)}, bf16[256,1024]{1,0:T(8,128)(2,1)S(1)}, u32[]{:S(2)}, u32[]{:S(2)}) collective-permute-start(bf16[256,1024]{1,0:T(8,128)(2,1)S(1)} %bitcast_convert_fusion), channel_id=1, source_target_pairs={{0,4},{12,8},{1,5},{13,9},{2,6},{14,10},{3,7},{15,11},{16,20},{28,... | collective-permute-start | bytes 1572872 | tf_op jit(solution)/shard_map/ppermute | solution.py:251
  82.8 13.0 %collective-permute-start.8 = (bf16[64,256]{1,0:T(8,128)(2,1)S(1)}, bf16[64,256]{1,0:T(8,128)(2,1)S(1)}, u32[]{:S(2)}, u32[]{:S(2)}) collective-permute-start(bf16[64,256]{1,0:T(8,128)(2,1)S(1)} %add_convert_fusion), channel_id=1, source_target_pairs={{0,8},{4,12},{8,0},{12,4},{1,9},{5,13},{9,1},{13,5},{2,10},{6,14},... | collective-permute-start | bytes 98312 | tf_op jit(solution)/shard_map/ppermute | solution.py:255
  83.3 19.0 %collective-permute-start.19 = (bf16[256,512]{1,0:T(8,128)(2,1)S(1)}, bf16[256,512]{1,0:T(8,128)(2,1)S(1)}, u32[]{:S(2)}, u32[]{:S(2)}) collective-permute-start(bf16[256,512]{1,0:T(8,128)(2,1)S(1)} %bitcast_convert_fusion.2), channel_id=1, source_target_pairs={{0,4},{12,8},{1,5},{13,9},{2,6},{14,10},{3,7},{15,11},{16,20},{28,... | collective-permute-start | bytes 786440 | tf_op jit(solution)/shard_map/ppermute | solution.py:251
  95.8 3.0 %collective-permute-start.9 = (f32[64,256]{1,0:T(8,128)S(1)}, f32[64,256]{1,0:T(8,128)S(1)}, u32[]{:S(2)}, u32[]{:S(2)}) collective-permute-start(f32[64,256]{1,0:T(8,128)S(1)} %convert_add_fusion), channel_id=1, source_target_pairs={{0,1},{1,0},{2,3},{3,2},{4,5},{5,4},{6,7},{7,6},{8,9},{9,8},{10,11... | collective-permute-start | bytes 196616 | tf_op jit(solution)/shard_map/ppermute | solution.py:255
  98.1 6.7 %collective-permute-start.13 = (bf16[256,1024]{1,0:T(8,128)(2,1)S(1)}, bf16[256,1024]{1,0:T(8,128)(2,1)S(1)}, u32[]{:S(2)}, u32[]{:S(2)}) collective-permute-start(bf16[256,1024]{1,0:T(8,128)(2,1)S(1)} %get-tuple-element.57), channel_id=1, source_target_pairs={{4,8},{8,4},{5,9},{9,5},{6,10},{10,6},{7,11},{11,7},{20,24},{24,20... | collective-permute-start | bytes 1572872 | tf_op jit(solution)/shard_map/ppermute | solution.py:251
  98.9 37.0 %collective-permute-start.10 = (f32[128,256]{1,0:T(8,128)S(1)}, f32[128,256]{1,0:T(8,128)S(1)}, u32[]{:S(2)}, u32[]{:S(2)}) collective-permute-start(f32[128,256]{1,0:T(8,128)S(1)} %maximum_select_fusion.3), channel_id=1, source_target_pairs={{0,2},{2,0},{1,3},{3,1},{4,6},{6,4},{5,7},{7,5},{8,10},{10,8},{9,1... | collective-permute-start | bytes 393224 | tf_op jit(solution)/shard_map/ppermute | solution.py:255
  101.0 36.3 %collective-permute-start.24 = (bf16[256,512]{1,0:T(8,128)(2,1)S(1)}, bf16[256,512]{1,0:T(8,128)(2,1)S(1)}, u32[]{:S(2)}, u32[]{:S(2)}) collective-permute-start(bf16[256,512]{1,0:T(8,128)(2,1)S(1)} %get-tuple-element.58), channel_id=1, source_target_pairs={{4,8},{8,4},{5,9},{9,5},{6,10},{10,6},{7,11},{11,7},{20,24},{24,20... | collective-permute-start | bytes 786440 | tf_op jit(solution)/shard_map/ppermute | solution.py:251
  101.6 4.9 %collective-permute-start.21 = (bf16[256,512]{1,0:T(8,128)(2,1)S(1)}, bf16[256,512]{1,0:T(8,128)(2,1)S(1)}, u32[]{:S(2)}, u32[]{:S(2)}) collective-permute-start(bf16[256,512]{1,0:T(8,128)(2,1)S(1)} %get-tuple-element.59), channel_id=1, source_target_pairs={{4,8},{8,4},{5,9},{9,5},{6,10},{10,6},{7,11},{11,7},{20,24},{24,20... | collective-permute-start | bytes 786440 | tf_op jit(solution)/shard_map/ppermute | solution.py:251
  104.2 26.1 %collective-permute-start.17 = (bf16[256,512]{1,0:T(8,128)(2,1)S(1)}, bf16[256,512]{1,0:T(8,128)(2,1)S(1)}, u32[]{:S(2)}, u32[]{:S(2)}) collective-permute-start(bf16[256,512]{1,0:T(8,128)(2,1)S(1)} %get-tuple-element.61), channel_id=1, source_target_pairs={{4,8},{8,4},{5,9},{9,5},{6,10},{10,6},{7,11},{11,7},{20,24},{24,20... | collective-permute-start | bytes 786440 | tf_op jit(solution)/shard_map/ppermute | solution.py:251
  104.8 50.1 %collective-permute-start.16 = (bf16[256,1024]{1,0:T(8,128)(2,1)}, bf16[256,1024]{1,0:T(8,128)(2,1)S(1)}, u32[]{:S(2)}, u32[]{:S(2)}) collective-permute-start(bf16[256,1024]{1,0:T(8,128)(2,1)} %get-tuple-element.56), channel_id=1, source_target_pairs={{4,8},{8,4},{5,9},{9,5},{6,10},{10,6},{7,11},{11,7},{20,24},{24,20... | collective-permute-start | bytes 1572872 | tf_op jit(solution)/shard_map/ppermute | solution.py:251
  106.5 48.4 %collective-permute-start.14 = (bf16[256,1024]{1,0:T(8,128)(2,1)}, bf16[256,1024]{1,0:T(8,128)(2,1)S(1)}, u32[]{:S(2)}, u32[]{:S(2)}) collective-permute-start(bf16[256,1024]{1,0:T(8,128)(2,1)} %fusion.14), channel_id=1, source_target_pairs={{0,4},{8,12},{4,0},{12,8},{1,5},{9,13},{5,1},{13,9},{2,6},{10,14},... | collective-permute-start | bytes 1572872 | tf_op jit(solution)/shard_map/ppermute | solution.py:251
  130.3 18.0 %collective-permute-start.22 = (bf16[256,512]{1,0:T(8,128)(2,1)}, bf16[256,512]{1,0:T(8,128)(2,1)}, u32[]{:S(2)}, u32[]{:S(2)}) collective-permute-start(bf16[256,512]{1,0:T(8,128)(2,1)} %fusion.17), channel_id=1, source_target_pairs={{0,4},{8,12},{4,0},{12,8},{1,5},{9,13},{5,1},{13,9},{2,6},{10,14},... | collective-permute-start | bytes 786440 | tf_op jit(solution)/shard_map/ppermute | solution.py:251
  135.9 1.4 copy-start.7
  135.9 14.8 %collective-permute-start.20 = (bf16[256,512]{1,0:T(8,128)(2,1)}, bf16[256,512]{1,0:T(8,128)(2,1)}, u32[]{:S(2)}, u32[]{:S(2)}) collective-permute-start(bf16[256,512]{1,0:T(8,128)(2,1)} %get-tuple-element.60), channel_id=1, source_target_pairs={{4,8},{8,4},{5,9},{9,5},{6,10},{10,6},{7,11},{11,7},{20,24},{24,20... | collective-permute-start | bytes 786440 | tf_op jit(solution)/shard_map/ppermute | solution.py:251
  137.3 15.1 %collective-permute-start.18 = (bf16[256,512]{1,0:T(8,128)(2,1)}, bf16[256,512]{1,0:T(8,128)(2,1)}, u32[]{:S(2)}, u32[]{:S(2)}) collective-permute-start(bf16[256,512]{1,0:T(8,128)(2,1)} %fusion.20), channel_id=1, source_target_pairs={{0,4},{8,12},{4,0},{12,8},{1,5},{9,13},{5,1},{13,9},{2,6},{10,14},... | collective-permute-start | bytes 786440 | tf_op jit(solution)/shard_map/ppermute | solution.py:251
  140.4 12.0 %copy-start.3 = (f32[4,256,512]{2,1,0:T(8,128)S(1)}, f32[4,256,512]{2,1,0:T(8,128)}, u32[]{:S(2)}) copy-start(f32[4,256,512]{2,1,0:T(8,128)} %copy-done.2) | copy-start | bytes 6291460
  150.7 4.2 %copy-start.1 = (f32[4,256,1024]{2,1,0:T(8,128)S(1)}, f32[4,256,1024]{2,1,0:T(8,128)}, u32[]{:S(2)}) copy-start(f32[4,256,1024]{2,1,0:T(8,128)} %copy-done) | copy-start | bytes 12582916

commit v4 on v3

--- a/solution.py
+++ b/solution.py
@@ -165,39 +165,79 @@
     return total
 
 
-def products_kernel(tile, wide, place, meta, factor, counts, own, other, out):
-    gene = place(pl.program_id(0), pl.program_id(1), meta) * wide
+def products_kernel(tile, wide, place, meta, factor, counts, own, other, *outs):
+    step, order = pl.program_id(0), pl.program_id(1)
+    gene = place(step, order, meta) * wide
     total = tile_products(tile, gene, meta, factor, counts, own, other)
-    out[...] = total.astype(out.dtype).reshape(out.shape)
-
-
-def products(block_of, blocks, block, start, chunk, dtype, tile, meta, factor, counts, own, other):
-    rows = counts.shape[0]
+    outs[0][...] = total.astype(outs[0].dtype).reshape(outs[0].shape)
+    if len(outs) > 1:
+
+        @pl.when(order == meta[4])
+        def _():
+            outs[1][...] = total.astype(outs[1].dtype)
+
+
+def products(only_first, cells, start, chunk, tile, meta, factor, counts, own, other):
+    rows, columns = counts.shape
     width = own.shape[0]
+    block = columns // cells
+    blocks = 1 if only_first else cells
     wide = 2 * tile if chunk % (2 * tile) == 0 else min(tile, chunk)
 
-    def place(o, i, m):
-        return block_of(o, m) * (block // wide) + start // wide + i
-
-    halved = lambda: pl.BlockSpec((width, rows // 2), lambda o, i, m: (0, 0))
+    def place(i, o, m):
+        return (m[3] if only_first else o) * (block // wide) + start // wide + i
+
+    halved = lambda: pl.BlockSpec((width, rows // 2), lambda i, o, m: (0, 0))
+    flat = pl.BlockSpec((width, wide), lambda i, o, m: (0, i))
+    operand = jax.ShapeDtypeStruct((width, chunk), BF16)
+    if only_first:
+        out_shape, out_specs = (operand,), (flat,)
+    else:
+        out_shape = (jax.ShapeDtypeStruct((cells, width, chunk), F32), operand)
+        out_specs = (pl.BlockSpec((1, width, wide), lambda i, o, m: (o, 0, i)), flat)
     return pl.pallas_call(
         functools.partial(products_kernel, tile, wide, place),
-        out_shape=jax.ShapeDtypeStruct((blocks, width, chunk), dtype),
+        out_shape=out_shape,
         grid_spec=pltpu.PrefetchScalarGridSpec(
             num_scalar_prefetch=1,
-            grid=(blocks, chunk // wide),
+            grid=(chunk // wide, blocks),
             in_specs=[
                 pl.BlockSpec(memory_space=pltpu.SMEM),
-                pl.BlockSpec((rows, wide), lambda o, i, m: (0, place(o, i, m))),
+                pl.BlockSpec((rows, wide), lambda i, o, m: (0, place(i, o, m))),
                 halved(),
                 halved(),
             ],
-            out_specs=pl.BlockSpec((1, width, wide), lambda o, i, m: (o, 0, i)),
-        ),
-        compiler_params=params(40),
+            out_specs=out_specs,
+        ),
+        compiler_params=params(48),
         cost_estimate=cost(1, 1),
         name="products",
     )(meta, factor, counts, own, other)
+
+
+def operand_kernel(meta, total, before, out):
+    out[...] = (total[0] + before[...].astype(F32)).astype(BF16)
+
+
+def operand(slot, meta, total, before):
+    width, chunk = before.shape
+    flat = lambda: pl.BlockSpec((width, chunk), lambda i, m: (0, 0))
+    return pl.pallas_call(
+        operand_kernel,
+        out_shape=jax.ShapeDtypeStruct((width, chunk), BF16),
+        grid_spec=pltpu.PrefetchScalarGridSpec(
+            num_scalar_prefetch=1,
+            grid=(1,),
+            in_specs=[
+                pl.BlockSpec((1, width, chunk), lambda i, m: (m[slot], 0, 0)),
+                flat(),
+            ],
+            out_specs=flat(),
+        ),
+        compiler_params=params(24),
+        cost_estimate=cost(1, 1),
+        name="operand",
+    )(meta, total, before)
 
 
 def keep_kernel(meta, total, first, second, *refs):
@@ -225,8 +265,8 @@
             out_specs=pl.BlockSpec((wide, width), lambda i, m: (start // wide + i, 0)),
         ),
         input_output_aliases={4: 0} if extra else {},
-        compiler_params=params(40),
-        cost_estimate=cost(3 * width * chunk, 12 * width * chunk),
+        compiler_params=params(24),
+        cost_estimate=cost(1, 1),
         name="keep",
     )(meta, totals, first, second, *extra)
 
@@ -296,9 +336,7 @@
 
 
 def chunk_sizes(block):
-    if block % 2048 == 0:
-        return [block // 4, block // 4, block // 2]
-    return [block]
+    return [block // 2, block // 2] if block % 1024 == 0 else [block]
 
 
 def shards(sizes, counts, tile_mask, tile_counts, gene_factor, prev_factor):
@@ -310,7 +348,9 @@
     cell = lax.axis_index("cell")
     gene = lax.axis_index("gene")
     line = Line(cells, cell)
-    meta = jnp.stack([sub, cell, sub * genes + gene, line.block(1, 0)]).astype(jnp.int32)
+    places = [sub, cell, sub * genes + gene, line.block(1, 0), line.block(2, 0)]
+    places += [line.block(phase, parity) for phase in range(2, cells) for parity in (0, 1)]
+    meta = jnp.stack(places).astype(jnp.int32)
     factor = tile_mask.astype(F32) / tile_counts.astype(F32)
 
     gram = contract_last(gene_factor, gene_factor)
@@ -337,57 +377,85 @@
     block = columns // cells
     chunks = chunk_sizes(block)
     starts = [sum(chunks[:i]) for i in range(len(chunks))]
-    arrived = [[], []]
-    for start, chunk in zip(starts, chunks):
-        first = products(
-            lambda o, m: m[3], 1, block, start, chunk, BF16, tile, meta, factor, counts, own, other
-        )[0]
+    every = range(len(chunks))
+    part = width // (genes * subs)
+
+    arrived = {}
+
+    def send(value, phase, parity, index):
+        pairs = line.pairs(phase, parity)
+        arrived[phase, parity, index] = lax.ppermute(value, "cell", pairs) if pairs else None
+
+    def resend(meta, phase, parity, index):
+        before = arrived[phase - 1, 1 - parity, index]
+        if before is None:
+            value = seconds[index]
+        else:
+            value = operand(5 + 2 * (phase - 2) + parity, meta, totals[index], before)
+            meta, value = after(meta, value)
+        send(value, phase, parity, index)
+        return meta
+
+    steps = [1 << i for i in range((cells - 1).bit_length())]
+
+    def add_rows(meta, rows_sum):
+        rows_arrived = swap(rows_sum, "cell", cells, steps.pop(0))
+        rows_arrived, meta = after(rows_arrived, meta)
+        total = rows_sum.astype(F32) + rows_arrived.astype(F32)
+        return after(meta, total.astype(BF16) if steps else total)
+
+    def gram_rows(half):
+        rows_here = lax.dynamic_slice_in_dim(half, (gene * subs + sub) * part, part, 0)
+        return contract_last(rows_here, half)
+
+    meta, rows_sum = after(meta, (gram_rows(own) + gram_rows(other)).astype(BF16))
+    for index in every:
+        (first,) = products(
+            True, cells, starts[index], chunks[index], tile, meta, factor, counts, own, other
+        )
         meta, first = after(meta, first)
         for parity in (0, 1):
-            sends = line.pairs(1, parity)
-            arrived[parity].append(line.send(first, 1, parity) if sends else None)
-    totals = []
-    for index, (start, chunk) in enumerate(zip(starts, chunks)):
-        meta, arrived[0][index] = after(meta, arrived[0][index])
-        total = products(
-            lambda o, m: o, cells, block, start, chunk, F32, tile, meta, factor, counts, own, other
+            send(first, 1, parity, index)
+        if index == 0:
+            meta, rows_sum = add_rows(meta, rows_sum)
+    totals, seconds = [], []
+    for index in every:
+        total, second = products(
+            False, cells, starts[index], chunks[index], tile, meta, factor, counts, own, other
         )
-        meta, total = after(meta, total)
+        meta, second = after(meta, second)
         totals.append(total)
-    for phase in range(2, cells):
-        for index, total in enumerate(totals):
-            values = []
+        seconds.append(second)
+        if cells > 2:
             for parity in (0, 1):
-                value = lax.dynamic_index_in_dim(total, line.block(phase, parity), 0, False)
-                before = arrived[1 - parity][index]
-                if before is not None:
-                    value = value + before.astype(F32)
-                values.append(value.astype(BF16))
+                meta = resend(meta, 2, parity, index)
+    while steps:
+        meta, rows_sum = add_rows(meta, rows_sum)
+    new_factor = factor_gram = None
+    for phase in range(3, cells):
+        for index in every:
             for parity in (0, 1):
-                arrived[parity][index] = line.send(values[parity], phase, parity)
+                meta = resend(meta, phase, parity, index)
+                if new_factor is None:
+                    rows_sum = join(rows_sum, "sub", subs, 0)
+                    own_late, meta = after(own, meta)
+                    whole = jnp.where(
+                        sub == 0,
+                        jnp.concatenate([own_late, other], axis=1),
+                        jnp.concatenate([other, own_late], axis=1),
+                    )
+                    new_factor = whole.T
+                    meta, new_factor = after(meta, new_factor)
+                    factor_gram = join(rows_sum, "gene", genes, 0)
+                    meta, factor_gram = after(meta, factor_gram)
     data_products = None
-    for index, start in enumerate(starts):
+    last = cells - 1
+    for index in every:
         data_products = keep(
-            block, start, meta, totals[index], arrived[0][index], arrived[1][index], data_products
+            block, starts[index], meta, totals[index],
+            arrived[last, 0, index], arrived[last, 1, index], data_products,
         )
-
-    own, _ = after(own, totals[0])
-    whole = jnp.where(
-        sub == 0,
-        jnp.concatenate([own, other], axis=1),
-        jnp.concatenate([other, own], axis=1),
-    )
-    new_factor = whole.T
-    part = width // (genes * subs)
-    gram_rows = contract_last(
-        lax.dynamic_slice_in_dim(whole, (gene * subs + sub) * part, part, 0), whole
-    )
-    step = 1
-    while step < cells:
-        gram_rows = gram_rows.astype(BF16)
-        gram_rows = gram_rows.astype(F32) + swap(gram_rows, "cell", cells, step).astype(F32)
-        step *= 2
-    factor_gram = join(join(gram_rows, "sub", subs, 0), "gene", genes, 0)
+        meta, data_products = after(meta, data_products)
     return (new_factor, factor_gram, data_products)
 
 

time: 158 us -> 132 us (0.84)
  starting transfers between devices: 62 us -> 32.4 us
  local copies, waits for them, and re-layouts: 2.66 us -> 10.9 us
  other arithmetic: 10.2 us -> 2.06 us
  Pallas kernels: 37.2 us -> 41.1 us
    ppermute x15 -> x10, starting transfers between devices: 54.1 us -> 19.8 us  [send(): lax.ppermute(value, 'cell', pairs)]
    unnamed x30, local copies, waits for them, and re-layouts: 2.46 us -> 10.8 us
    convert_element_type x7 -> x1, other arithmetic: 7.71 us -> 0.01 us  [add_rows(): return after(meta, total.astype(BF16) if steps else total)]
    pallas_call x0 -> x6, Pallas kernels: none -> 6.49 us  [operand(): pl.pallas_call(operand_kernel, out_shape=jax.ShapeDtypeStruct((width, chu...]
    ppermute x15 -> x10, waiting for transfers between devices: 9.06 us -> 14.3 us  [send(): lax.ppermute(value, 'cell', pairs)]
    ppermute x10, starting transfers between devices: 7.95 us -> 12.6 us  [swap(): return lax.ppermute(value, axis, [(i, i ^ step) for i in range(size)])]
    ppermute x10, waiting for transfers between devices: 17.9 us -> 13.3 us  [swap(): return lax.ppermute(value, axis, [(i, i ^ step) for i in range(size)])]
    pallas_call x3 -> x2, Pallas kernels: 7.02 us -> 4.99 us  [keep(): pl.pallas_call(keep_kernel, out_shape=jax.ShapeDtypeStruct((block, width)...]
  transfers between devices with their start and end apart: 25 -> 20, of which waited for: 8 -> 8; matrix products, arithmetic and copies ran while one was open for 12% -> 8% of each run, Pallas kernels for 20% -> 28%
where the time goes in v4:
time: 132 us
  Pallas kernels  41.1 us (31%)
  starting transfers between devices  32.4 us (25%)
  waiting for transfers between devices  27.5 us (21%)
  matrix products  16.4 us (12%)
  local copies, waits for them, and re-layouts  10.9 us (8%)
  other arithmetic  2.06 us (2%)
    pallas_call x4, Pallas kernels, products(): pl.pallas_call(functools.partial(products_kernel, tile, wide, place), out...  24 us
    ppermute x10, starting transfers between devices, send(): lax.ppermute(value, 'cell', pairs)  19.8 us
    dot_general x7, matrix products, contract_last(): lax.dot_general(left, right, (((1,), (1,)), ((), ())), preferred_element_...  16.4 us
    ppermute x10, waiting for transfers between devices, send(): lax.ppermute(value, 'cell', pairs)  14.3 us
    ppermute x10, waiting for transfers between devices, swap(): return lax.ppermute(value, axis, [(i, i ^ step) for i in range(size)])  13.3 us
    ppermute x10, starting transfers between devices, swap(): return lax.ppermute(value, axis, [(i, i ^ step) for i in range(size)])  12.6 us
    unnamed x30, local copies, waits for them, and re-layouts  10.8 us
    pallas_call x6, Pallas kernels, operand(): pl.pallas_call(operand_kernel, out_shape=jax.ShapeDtypeStruct((width, chu...  6.49 us
  transfers between devices with their start and end apart: 20, of which 8 were waited for; matrix products, arithmetic and copies ran while one was open for 8% of the time, Pallas kernels for 28%

profile of v4, /device:TPU:0, one launch (start us, length us, event | category | flops | bytes accessed | tf_op | source)
XLA Modules:
  0.0 131.6 jit_solution(10034902419204738877)
XLA Ops:
  0.7 4.9 %fusion.20 = f32[256,256]{1,0:T(8,128)S(1)} fusion(bf16[256,8192]{1,0:T(8,128)(2,1)} %param.8), kind=kOutput, calls=%fused_computation.44 | convolution fusion | flops 1073741824 | bytes 4456448 | tf_op jit(solution)/shard_map/dot_general | solution.py:25
  5.6 3.0 %collective-permute-start = (f32[256,256]{1,0:T(8,128)S(1)}, f32[256,256]{1,0:T(8,128)S(1)}, u32[]{:S(2)}, u32[]{:S(2)}) collective-permute-start(f32[256,256]{1,0:T(8,128)S(1)} %fusion.20), channel_id=1, source_target_pairs={{0,2},{2,0},{1,3},{3,1},{4,6},{6,4},{5,7},{7,5},{8,10},{10,8},{9,1... | collective-permute-start | bytes 786440 | tf_op jit(solution)/shard_map/ppermute | solution.py:295
  8.6 0.1 broadcast_bitcast_fusion.3
  8.7 0.1 broadcast_bitcast_fusion.1
  8.8 3.8 %fusion.1 = f32[256,256]{1,0:T(8,128)S(1)} fusion(bf16[256,8192]{1,0:T(8,128)(2,1)S(1)} %copy-done.10, f32[8192]{0:T(1024)S(1)} %bitcast.39, bf16[1024,8192]{1,0:T(8,128)(2,1)} %counts.7), kind=kOutput, calls=%fused_computation.5 | convolution fusion | flops 1080033280 | bytes 8683520 | tf_op jit(solution)/shard_map/dot_general | solution.py:25
  12.7 1.3 fusion.2
  14.0 1.3 fusion
  15.3 0.1 broadcast_bitcast_fusion
  15.4 0.1 copy.10
  15.6 4.8 %fusion.3 = f32[256,256]{1,0:T(8,128)S(1)} fusion(bf16[256,8192]{1,0:T(8,128)(2,1)} %param.8, f32[8192]{0:T(1024)S(1)} %bitcast.40, bf16[1024,8192]{1,0:T(8,128)(2,1)} %counts.7), kind=kOutput, calls=%fused_computation.7 | convolution fusion | flops 1080033280 | bytes 8683520 | tf_op jit(solution)/shard_map/dot_general | solution.py:25
  20.3 0.1 fusion.14
  20.4 0.1 collective-permute-start.2
  20.5 0.5 collective-permute-start.1
  21.0 1.4 %collective-permute-done.2 = f32[512,256]{1,0:T(8,128)S(1)} collective-permute-done((f32[512,256]{1,0:T(8,128)S(1)}, f32[512,256]{1,0:T(8,128)S(1)}, u32[]{:S(2)}, u32[]{:S(2)}) %collective-permute-start.2) | collective-permute-done | bytes 524320 | tf_op jit(solution)/shard_map/ppermute | solution.py:295
  22.4 0.1 select_add_fusion
  22.5 1.8 %collective-permute-start.3 = (f32[256,256]{1,0:T(8,128)S(1)}, f32[256,256]{1,0:T(8,128)S(1)}, u32[]{:S(2)}, u32[]{:S(2)}) collective-permute-start(f32[256,256]{1,0:T(8,128)S(1)} %get-tuple-element.104), channel_id=1, source_target_pairs={{0,2},{2,0},{1,3},{3,1},{4,6},{6,4},{5,7},{7,5},{8,10},{10,8},{9,1... | collective-permute-start | bytes 786440 | tf_op jit(solution)/shard_map/ppermute | solution.py:295
  24.3 0.1 stack.33.meta
  24.4 3.5 %inverse.1 = (f32[256,256]{1,0:T(8,128)S(1)}, f32[1,1]{1,0:T(1,128)}) custom-call(f32[256,256]{1,0:T(8,128)S(1)} %add.52.gram_a, f32[256,256]{1,0:T(8,128)S(1)} %collective-permute-done.1.gram_b), custom_call_target="tpu_custom_call" | custom-call | flops 2013265920 | bytes 786432 | tf_op jit(solution)/shard_map/inverse/pallas_call | solution.py:91
  27.9 3.0 %collective-permute-done.3.cross_b = f32[256,256]{1,0:T(8,128)S(1)} collective-permute-done((f32[256,256]{1,0:T(8,128)S(1)}, f32[256,256]{1,0:T(8,128)S(1)}, u32[]{:S(2)}, u32[]{:S(2)}) %collective-permute-start.3) | collective-permute-done | bytes 262176 | tf_op jit(solution)/shard_map/ppermute | solution.py:295
  31.0 2.1 %admm.1 = bf16[256,256]{1,0:T(8,128)(2,1)S(1)} custom-call(s32[9]{0:T(128)S(1)} %stack.33.meta, f32[1,1]{1,0:T(1,128)} %get-tuple-element.55.rho_ref, f32[256,256]{1,0:T(8,128)S(1)} %get-tuple-element.105.cross_a, f32[256,256]{1,0:T(8,128)S(1)} %collective-permute-done.3.cross_b, f32[256,256]{1,0:T(8,128)S(1)} %get-tuple-element.57.inverse, ...), custom_call_target="tpu_custom_call" | custom-call | flops 301989888 | bytes 786432 | tf_op jit(solution)/shard_map/admm/pallas_call | solution.py:121
  33.0 1.8 %collective-permute-start.4 = (bf16[256,256]{1,0:T(8,128)(2,1)S(1)}, bf16[256,256]{1,0:T(8,128)(2,1)S(1)}, u32[]{:S(2)}, u32[]{:S(2)}) collective-permute-start(bf16[256,256]{1,0:T(8,128)(2,1)S(1)} %admm.1), channel_id=1, source_target_pairs={{0,2},{2,0},{1,3},{3,1},{4,6},{6,4},{5,7},{7,5},{8,10},{10,8},{9,1... | collective-permute-start | bytes 393224 | tf_op jit(solution)/shard_map/ppermute | solution.py:295
  34.8 3.3 %collective-permute-done.4 = bf16[256,256]{1,0:T(8,128)(2,1)S(1)} collective-permute-done((bf16[256,256]{1,0:T(8,128)(2,1)S(1)}, bf16[256,256]{1,0:T(8,128)(2,1)S(1)}, u32[]{:S(2)}, u32[]{:S(2)}) %collective-permute-start.4) | collective-permute-done | bytes 131104 | tf_op jit(solution)/shard_map/ppermute | solution.py:295
  38.1 0.1 maximum_select_fusion.1.own
  38.2 0.1 collective-permute-start.5
  38.3 1.5 %collective-permute-done.5.other = bf16[256,512]{1,0:T(8,128)(2,1)S(1)} collective-permute-done((bf16[256,512]{1,0:T(8,128)(2,1)S(1)}, bf16[256,512]{1,0:T(8,128)(2,1)S(1)}, u32[]{:S(2)}, u32[]{:S(2)}) %collective-permute-start.5) | collective-permute-done | bytes 262176 | tf_op jit(solution)/shard_map/ppermute | solution.py:295
  39.8 0.2 fusion.15
  40.0 0.2 fusion.12
  40.2 2.1 %collective-permute-start.6 = (bf16[64,256]{1,0:T(8,128)(2,1)S(1)}, bf16[64,256]{1,0:T(8,128)(2,1)S(1)}, u32[]{:S(2)}, u32[]{:S(2)}) collective-permute-start(bf16[64,256]{1,0:T(8,128)(2,1)S(1)} %fusion.12), channel_id=1, source_target_pairs={{0,4},{4,0},{8,12},{12,8},{1,5},{5,1},{9,13},{13,9},{2,6},{6,2},{1... | collective-permute-start | bytes 98312 | tf_op jit(solution)/shard_map/ppermute | solution.py:295
  42.3 2.8 %products.4 = bf16[256,1024]{1,0:T(8,128)(2,1)S(1)} custom-call(s32[9]{0:T(128)S(1)} %stack.33.meta, f32[4,32]{1,0:T(4,128)S(1)} %convert_divide_fusion.factor, bf16[1024,8192]{1,0:T(8,128)(2,1)} %counts.7, bf16[256,512]{1,0:T(8,128)(2,1)S(1)} %maximum_select_fusion.1.own, bf16[256,512]{1,0:T(8,128)(2,1)S(1)} %collective-permute-done.5.other), custom_call_target="tpu_custom_call" | custom-call | flops 1 | bytes 1 | tf_op jit(solution)/shard_map/products/pallas_call | solution.py:198
  45.1 2.0 %collective-permute-start.8 = (bf16[256,1024]{1,0:T(8,128)(2,1)S(1)}, bf16[256,1024]{1,0:T(8,128)(2,1)S(1)}, u32[]{:S(2)}, u32[]{:S(2)}) collective-permute-start(bf16[256,1024]{1,0:T(8,128)(2,1)S(1)} %products.4), channel_id=1, source_target_pairs={{0,4},{12,8},{1,5},{13,9},{2,6},{14,10},{3,7},{15,11},{16,20},{28,... | collective-permute-start | bytes 1572872 | tf_op jit(solution)/shard_map/ppermute | solution.py:387
  47.1 2.8 %products.5 = bf16[256,1024]{1,0:T(8,128)(2,1)S(1)} custom-call(s32[9]{0:T(128)S(1)} %stack.33.meta, f32[4,32]{1,0:T(4,128)S(1)} %convert_divide_fusion.factor, bf16[1024,8192]{1,0:T(8,128)(2,1)} %counts.7, bf16[256,512]{1,0:T(8,128)(2,1)S(1)} %maximum_select_fusion.1.own, bf16[256,512]{1,0:T(8,128)(2,1)S(1)} %collective-permute-done.5.other), custom_call_target="tpu_custom_call" | custom-call | flops 1 | bytes 1 | tf_op jit(solution)/shard_map/products/pallas_call | solution.py:198
  49.9 1.5 %collective-permute-start.9 = (bf16[256,1024]{1,0:T(8,128)(2,1)S(1)}, bf16[256,1024]{1,0:T(8,128)(2,1)S(1)}, u32[]{:S(2)}, u32[]{:S(2)}) collective-permute-start(bf16[256,1024]{1,0:T(8,128)(2,1)S(1)} %products.5), channel_id=1, source_target_pairs={{0,4},{12,8},{1,5},{13,9},{2,6},{14,10},{3,7},{15,11},{16,20},{28,... | collective-permute-start | bytes 1572872 | tf_op jit(solution)/shard_map/ppermute | solution.py:387
  51.4 2.0 %collective-permute-start.7 = (bf16[64,256]{1,0:T(8,128)(2,1)S(1)}, bf16[64,256]{1,0:T(8,128)(2,1)S(1)}, u32[]{:S(2)}, u32[]{:S(2)}) collective-permute-start(bf16[64,256]{1,0:T(8,128)(2,1)S(1)} %add_convert_fusion), channel_id=1, source_target_pairs={{0,8},{4,12},{8,0},{12,4},{1,9},{5,13},{9,1},{13,5},{2,10},{6,14},... | collective-permute-start | bytes 98312 | tf_op jit(solution)/shard_map/ppermute | solution.py:295
  53.4 9.2 %products.6 = (f32[4,256,1024]{2,1,0:T(8,128)S(1)}, bf16[256,1024]{1,0:T(8,128)(2,1)}) custom-call(s32[9]{0:T(128)S(1)} %stack.33.meta, f32[4,32]{1,0:T(4,128)S(1)} %convert_divide_fusion.factor, bf16[1024,8192]{1,0:T(8,128)(2,1)} %counts.7, bf16[256,512]{1,0:T(8,128)(2,1)S(1)} %maximum_select_fusion.1.own, bf16[256,512]{1,0:T(8,128)(2,1)S(1)} %collective-permute-done.5.other), custom_call_target="tpu_custom_call" | custom-call | flops 1 | bytes 1 | tf_op jit(solution)/shard_map/products/pallas_call | solution.py:198
  62.6 0.6 operand.6
  63.2 2.0 %copy-done = f32[4,256,1024]{2,1,0:T(8,128)} copy-done((f32[4,256,1024]{2,1,0:T(8,128)}, f32[4,256,1024]{2,1,0:T(8,128)S(1)}, u32[]{:S(2)}) %copy-start) | copy-done | bytes 4194328
  65.3 0.7 collective-permute-start.10
  65.9 9.2 %products.7 = (f32[4,256,1024]{2,1,0:T(8,128)S(1)}, bf16[256,1024]{1,0:T(8,128)(2,1)}) custom-call(s32[9]{0:T(128)S(1)} %stack.33.meta, f32[4,32]{1,0:T(4,128)S(1)} %convert_divide_fusion.factor, bf16[1024,8192]{1,0:T(8,128)(2,1)} %counts.7, bf16[256,512]{1,0:T(8,128)(2,1)S(1)} %maximum_select_fusion.1.own, bf16[256,512]{1,0:T(8,128)(2,1)S(1)} %collective-permute-done.5.other), custom_call_target="tpu_custom_call" | custom-call | flops 1 | bytes 1 | tf_op jit(solution)/shard_map/products/pallas_call | solution.py:198
  75.2 0.6 operand.7
  75.8 2.0 %copy-done.3 = f32[4,256,1024]{2,1,0:T(8,128)} copy-done((f32[4,256,1024]{2,1,0:T(8,128)}, f32[4,256,1024]{2,1,0:T(8,128)S(1)}, u32[]{:S(2)}) %copy-start.3) | copy-done | bytes 4194328
  77.8 0.1 collective-permute-start.11
  77.8 6.7 %collective-permute-start.13 = (bf16[256,1024]{1,0:T(8,128)(2,1)}, bf16[256,1024]{1,0:T(8,128)(2,1)}, u32[]{:S(2)}, u32[]{:S(2)}) collective-permute-start(bf16[256,1024]{1,0:T(8,128)(2,1)} %get-tuple-element.88), channel_id=1, source_target_pairs={{0,4},{12,8},{1,5},{13,9},{2,6},{14,10},{3,7},{15,11},{16,20},{28,... | collective-permute-start | bytes 1572872 | tf_op jit(solution)/shard_map/ppermute | solution.py:387
  84.5 0.7 collective-permute-start.14
  85.2 3.8 %collective-permute-start.15 = (bf16[256,1024]{1,0:T(8,128)(2,1)}, bf16[256,1024]{1,0:T(8,128)(2,1)S(1)}, u32[]{:S(2)}, u32[]{:S(2)}) collective-permute-start(bf16[256,1024]{1,0:T(8,128)(2,1)} %get-tuple-element.92), channel_id=1, source_target_pairs={{0,4},{12,8},{1,5},{13,9},{2,6},{14,10},{3,7},{15,11},{16,20},{28,... | collective-permute-start | bytes 1572872 | tf_op jit(solution)/shard_map/ppermute | solution.py:387
  89.0 1.3 %collective-permute-start.12 = (f32[128,256]{1,0:T(8,128)S(1)}, f32[128,256]{1,0:T(8,128)S(1)}, u32[]{:S(2)}, u32[]{:S(2)}) collective-permute-start(f32[128,256]{1,0:T(8,128)S(1)} %maximum_select_fusion.3), channel_id=1, source_target_pairs={{0,2},{2,0},{1,3},{3,1},{4,6},{6,4},{5,7},{7,5},{8,10},{10,8},{9,1... | collective-permute-start | bytes 393224 | tf_op jit(solution)/shard_map/ppermute | solution.py:295
  90.4 4.0 %collective-permute-done.12 = f32[128,256]{1,0:T(8,128)S(1)} collective-permute-done((f32[128,256]{1,0:T(8,128)S(1)}, f32[128,256]{1,0:T(8,128)S(1)}, u32[]{:S(2)}, u32[]{:S(2)}) %collective-permute-start.12) | collective-permute-done | bytes 131104 | tf_op jit(solution)/shard_map/ppermute | solution.py:295
  94.4 0.7 maximum_select_fusion.2
  95.2 2.2 %copy-done.1 = f32[4,256,1024]{2,1,0:T(8,128)S(1)} copy-done((f32[4,256,1024]{2,1,0:T(8,128)S(1)}, f32[4,256,1024]{2,1,0:T(8,128)}, u32[]{:S(2)}) %copy-start.1) | copy-done | bytes 4194328
  97.3 0.6 operand.8
  98.0 0.9 fusion.13
  98.9 2.5 %operand.9 = bf16[256,1024]{1,0:T(8,128)(2,1)} custom-call(s32[9]{0:T(128)S(1)} %stack.33.meta, f32[4,256,1024]{2,1,0:T(8,128)S(1)} %copy-done.1, bf16[256,1024]{1,0:T(8,128)(2,1)} %collective-permute-done.13.before), custom_call_target="tpu_custom_call" | custom-call | flops 1 | bytes 1 | tf_op jit(solution)/shard_map/operand/pallas_call | solution.py:225
  101.4 0.7 collective-permute-start.17
  102.1 3.1 %collective-permute-start.16 = (bf16[256,1024]{1,0:T(8,128)(2,1)S(1)}, bf16[256,1024]{1,0:T(8,128)(2,1)}, u32[]{:S(2)}, u32[]{:S(2)}) collective-permute-start(bf16[256,1024]{1,0:T(8,128)(2,1)S(1)} %operand.8), channel_id=1, source_target_pairs={{0,4},{8,12},{4,0},{12,8},{1,5},{9,13},{5,1},{13,9},{2,6},{10,14},... | collective-permute-start | bytes 1572872 | tf_op jit(solution)/shard_map/ppermute | solution.py:387
  105.2 1.5 %operand.10 = bf16[256,1024]{1,0:T(8,128)(2,1)} custom-call(s32[9]{0:T(128)S(1)} %stack.33.meta, f32[4,256,1024]{2,1,0:T(8,128)S(1)} %copy-done.4, bf16[256,1024]{1,0:T(8,128)(2,1)S(1)} %collective-permute-done.14.before), custom_call_target="tpu_custom_call" | custom-call | flops 1 | bytes 1 | tf_op jit(solution)/shard_map/operand/pallas_call | solution.py:225
  106.7 0.0 collective-permute-start.18
  106.7 0.8 collective-permute-done.15.before
  107.5 0.6 operand.11
  108.2 0.7 collective-permute-start.19
  108.9 2.0 %copy.9 = bf16[1024,256]{1,0:T(8,128)(2,1)} copy(bf16[1024,256]{0,1:T(8,128)(2,1)} %fusion.13) | data formatting | bytes 1048576
  110.9 7.7 %collective-permute-done.16.first = bf16[256,1024]{1,0:T(8,128)(2,1)} collective-permute-done((bf16[256,1024]{1,0:T(8,128)(2,1)S(1)}, bf16[256,1024]{1,0:T(8,128)(2,1)}, u32[]{:S(2)}, u32[]{:S(2)}) %collective-permute-start.16) | collective-permute-done | bytes 524320 | tf_op jit(solution)/shard_map/ppermute | solution.py:387
  118.7 2.2 %copy-done.2 = f32[4,256,1024]{2,1,0:T(8,128)S(1)} copy-done((f32[4,256,1024]{2,1,0:T(8,128)S(1)}, f32[4,256,1024]{2,1,0:T(8,128)}, u32[]{:S(2)}) %copy-start.2) | copy-done | bytes 4194328
  120.9 3.0 %keep.2.refs_0_ = f32[2048,256]{1,0:T(8,128)} custom-call(s32[9]{0:T(128)S(1)} %stack.33.meta, f32[4,256,1024]{2,1,0:T(8,128)S(1)} %copy-done.2, bf16[256,1024]{1,0:T(8,128)(2,1)} %collective-permute-done.16.first, bf16[256,1024]{1,0:T(8,128)(2,1)S(1)} %collective-permute-done.17.second), custom_call_target="tpu_custom_call" | custom-call | flops 1 | bytes 1 | tf_op jit(solution)/shard_map/keep/pallas_call | solution.py:253
  123.9 5.7 %collective-permute-done.18.first = bf16[256,1024]{1,0:T(8,128)(2,1)S(1)} collective-permute-done((bf16[256,1024]{1,0:T(8,128)(2,1)}, bf16[256,1024]{1,0:T(8,128)(2,1)S(1)}, u32[]{:S(2)}, u32[]{:S(2)}) %collective-permute-start.18) | collective-permute-done | bytes 524320 | tf_op jit(solution)/shard_map/ppermute | solution.py:387
  129.6 1.9 %keep.3 = f32[2048,256]{1,0:T(8,128)} custom-call(s32[9]{0:T(128)S(1)} %stack.33.meta, f32[4,256,1024]{2,1,0:T(8,128)S(1)} %copy-done.5, bf16[256,1024]{1,0:T(8,128)(2,1)S(1)} %collective-permute-done.18.first, bf16[256,1024]{1,0:T(8,128)(2,1)S(1)} %collective-permute-done.19.second, f32[2048,256]{1,0:T(8,128)} %keep.2.refs_0_), custom_call_target="tpu_custom_call", output_to_operand_aliasing={{}: (4, {})} | custom-call | flops 1 | bytes 1 | tf_op jit(solution)/shard_map/keep/pallas_call | solution.py:253
  (41 shorter events, 0.3 us)
Async XLA Ops:
  0.6 8.2 %copy-start.10 = (bf16[256,8192]{1,0:T(8,128)(2,1)S(1)}, bf16[256,8192]{1,0:T(8,128)(2,1)}, u32[]{:S(2)}) copy-start(bf16[256,8192]{1,0:T(8,128)(2,1)} %param.8) | copy-start | bytes 12582916
  0.6 4.9 %copy-start.8 = (s32[4,32]{1,0:T(4,128)S(1)}, s32[4,32]{1,0:T(4,128)}, u32[]{:S(2)}) copy-start(s32[4,32]{1,0:T(4,128)} %param.7) | copy-start | bytes 1540
  0.7 4.9 %copy-start.9 = (s32[4,32]{1,0:T(4,128)S(1)}, s32[4,32]{1,0:T(4,128)}, u32[]{:S(2)}) copy-start(s32[4,32]{1,0:T(4,128)} %param.6) | copy-start | bytes 1540
  0.7 12.0 %copy-start.7 = (bf16[1024,8192]{1,0:T(8,128)(2,1)S(1)}, bf16[1024,8192]{1,0:T(8,128)(2,1)}, u32[]{:S(2)}) copy-start(bf16[1024,8192]{1,0:T(8,128)(2,1)} %counts.7) | copy-start | bytes 50331652
  5.6 9.9 %collective-permute-start = (f32[256,256]{1,0:T(8,128)S(1)}, f32[256,256]{1,0:T(8,128)S(1)}, u32[]{:S(2)}, u32[]{:S(2)}) collective-permute-start(f32[256,256]{1,0:T(8,128)S(1)} %fusion.20), channel_id=1, source_target_pairs={{0,2},{2,0},{1,3},{3,1},{4,6},{6,4},{5,7},{7,5},{8,10},{10,8},{9,1... | collective-permute-start | bytes 786440 | tf_op jit(solution)/shard_map/ppermute | solution.py:295
  20.4 2.0 %collective-permute-start.2 = (f32[512,256]{1,0:T(8,128)S(1)}, f32[512,256]{1,0:T(8,128)S(1)}, u32[]{:S(2)}, u32[]{:S(2)}) collective-permute-start(f32[512,256]{1,0:T(8,128)S(1)} %fusion.14), channel_id=1, source_target_pairs={{0,1},{1,0},{2,3},{3,2},{4,5},{5,4},{6,7},{7,6},{8,9},{9,8},{10,11... | collective-permute-start | bytes 1572872 | tf_op jit(solution)/shard_map/ppermute | solution.py:295
  20.5 3.9 %collective-permute-start.1 = (f32[256,256]{1,0:T(8,128)S(1)}, f32[256,256]{1,0:T(8,128)S(1)}, u32[]{:S(2)}, u32[]{:S(2)}) collective-permute-start(f32[256,256]{1,0:T(8,128)S(1)} %add.52.gram_a), channel_id=1, source_target_pairs={{0,1},{1,0},{2,3},{3,2},{4,5},{5,4},{6,7},{7,6},{8,9},{9,8},{10,11... | collective-permute-start | bytes 786440 | tf_op jit(solution)/shard_map/ppermute | solution.py:295
  22.5 8.5 %copy-start.6 = (bf16[1024,256]{1,0:T(8,128)(2,1)S(1)}, bf16[1024,256]{1,0:T(8,128)(2,1)}, u32[]{:S(2)}) copy-start(bf16[1024,256]{1,0:T(8,128)(2,1)} %start.1) | copy-start | bytes 1572868
  22.5 8.4 %collective-permute-start.3 = (f32[256,256]{1,0:T(8,128)S(1)}, f32[256,256]{1,0:T(8,128)S(1)}, u32[]{:S(2)}, u32[]{:S(2)}) collective-permute-start(f32[256,256]{1,0:T(8,128)S(1)} %get-tuple-element.104), channel_id=1, source_target_pairs={{0,2},{2,0},{1,3},{3,1},{4,6},{6,4},{5,7},{7,5},{8,10},{10,8},{9,1... | collective-permute-start | bytes 786440 | tf_op jit(solution)/shard_map/ppermute | solution.py:295
  33.0 5.0 %collective-permute-start.4 = (bf16[256,256]{1,0:T(8,128)(2,1)S(1)}, bf16[256,256]{1,0:T(8,128)(2,1)S(1)}, u32[]{:S(2)}, u32[]{:S(2)}) collective-permute-start(bf16[256,256]{1,0:T(8,128)(2,1)S(1)} %admm.1), channel_id=1, source_target_pairs={{0,2},{2,0},{1,3},{3,1},{4,6},{6,4},{5,7},{7,5},{8,10},{10,8},{9,1... | collective-permute-start | bytes 393224 | tf_op jit(solution)/shard_map/ppermute | solution.py:295
  38.2 1.6 %collective-permute-start.5 = (bf16[256,512]{1,0:T(8,128)(2,1)S(1)}, bf16[256,512]{1,0:T(8,128)(2,1)S(1)}, u32[]{:S(2)}, u32[]{:S(2)}) collective-permute-start(bf16[256,512]{1,0:T(8,128)(2,1)S(1)} %maximum_select_fusion.1.own), channel_id=1, source_target_pairs={{0,1},{1,0},{2,3},{3,2},{4,5},{5,4},{6,7},{7,6},{8,9},{9,8},{10,11... | collective-permute-start | bytes 786440 | tf_op jit(solution)/shard_map/ppermute | solution.py:295
  40.2 6.9 %collective-permute-start.6 = (bf16[64,256]{1,0:T(8,128)(2,1)S(1)}, bf16[64,256]{1,0:T(8,128)(2,1)S(1)}, u32[]{:S(2)}, u32[]{:S(2)}) collective-permute-start(bf16[64,256]{1,0:T(8,128)(2,1)S(1)} %fusion.12), channel_id=1, source_target_pairs={{0,4},{4,0},{8,12},{12,8},{1,5},{5,1},{9,13},{13,9},{2,6},{6,2},{1... | collective-permute-start | bytes 98312 | tf_op jit(solution)/shard_map/ppermute | solution.py:295
  45.1 17.5 %collective-permute-start.8 = (bf16[256,1024]{1,0:T(8,128)(2,1)S(1)}, bf16[256,1024]{1,0:T(8,128)(2,1)S(1)}, u32[]{:S(2)}, u32[]{:S(2)}) collective-permute-start(bf16[256,1024]{1,0:T(8,128)(2,1)S(1)} %products.4), channel_id=1, source_target_pairs={{0,4},{12,8},{1,5},{13,9},{2,6},{14,10},{3,7},{15,11},{16,20},{28,... | collective-permute-start | bytes 1572872 | tf_op jit(solution)/shard_map/ppermute | solution.py:387
  49.9 25.3 %collective-permute-start.9 = (bf16[256,1024]{1,0:T(8,128)(2,1)S(1)}, bf16[256,1024]{1,0:T(8,128)(2,1)S(1)}, u32[]{:S(2)}, u32[]{:S(2)}) collective-permute-start(bf16[256,1024]{1,0:T(8,128)(2,1)S(1)} %products.5), channel_id=1, source_target_pairs={{0,4},{12,8},{1,5},{13,9},{2,6},{14,10},{3,7},{15,11},{16,20},{28,... | collective-permute-start | bytes 1572872 | tf_op jit(solution)/shard_map/ppermute | solution.py:387
  51.4 26.3 %collective-permute-start.7 = (bf16[64,256]{1,0:T(8,128)(2,1)S(1)}, bf16[64,256]{1,0:T(8,128)(2,1)S(1)}, u32[]{:S(2)}, u32[]{:S(2)}) collective-permute-start(bf16[64,256]{1,0:T(8,128)(2,1)S(1)} %add_convert_fusion), channel_id=1, source_target_pairs={{0,8},{4,12},{8,0},{12,4},{1,9},{5,13},{9,1},{13,5},{2,10},{6,14},... | collective-permute-start | bytes 98312 | tf_op jit(solution)/shard_map/ppermute | solution.py:295
  63.2 2.0 %copy-start = (f32[4,256,1024]{2,1,0:T(8,128)}, f32[4,256,1024]{2,1,0:T(8,128)S(1)}, u32[]{:S(2)}) copy-start(f32[4,256,1024]{2,1,0:T(8,128)S(1)} %get-tuple-element.68.total) | copy-start | bytes 12582916
  65.3 29.9 %collective-permute-start.10 = (bf16[256,1024]{1,0:T(8,128)(2,1)S(1)}, bf16[256,1024]{1,0:T(8,128)(2,1)S(1)}, u32[]{:S(2)}, u32[]{:S(2)}) collective-permute-start(bf16[256,1024]{1,0:T(8,128)(2,1)S(1)} %operand.6), channel_id=1, source_target_pairs={{4,8},{8,4},{5,9},{9,5},{6,10},{10,6},{7,11},{11,7},{20,24},{24,20... | collective-permute-start | bytes 1572872 | tf_op jit(solution)/shard_map/ppermute | solution.py:387
  75.8 2.0 %copy-start.3 = (f32[4,256,1024]{2,1,0:T(8,128)}, f32[4,256,1024]{2,1,0:T(8,128)S(1)}, u32[]{:S(2)}) copy-start(f32[4,256,1024]{2,1,0:T(8,128)S(1)} %get-tuple-element.73.total) | copy-start | bytes 12582916
  77.8 11.2 %collective-permute-start.11 = (f32[64,256]{1,0:T(8,128)S(1)}, f32[64,256]{1,0:T(8,128)S(1)}, u32[]{:S(2)}, u32[]{:S(2)}) collective-permute-start(f32[64,256]{1,0:T(8,128)S(1)} %convert_add_fusion), channel_id=1, source_target_pairs={{0,1},{1,0},{2,3},{3,2},{4,5},{5,4},{6,7},{7,6},{8,9},{9,8},{10,11... | collective-permute-start | bytes 196616 | tf_op jit(solution)/shard_map/ppermute | solution.py:295
  77.8 21.1 %collective-permute-start.13 = (bf16[256,1024]{1,0:T(8,128)(2,1)}, bf16[256,1024]{1,0:T(8,128)(2,1)}, u32[]{:S(2)}, u32[]{:S(2)}) collective-permute-start(bf16[256,1024]{1,0:T(8,128)(2,1)} %get-tuple-element.88), channel_id=1, source_target_pairs={{0,4},{12,8},{1,5},{13,9},{2,6},{14,10},{3,7},{15,11},{16,20},{28,... | collective-permute-start | bytes 1572872 | tf_op jit(solution)/shard_map/ppermute | solution.py:387
  84.5 20.7 %collective-permute-start.14 = (bf16[256,1024]{1,0:T(8,128)(2,1)S(1)}, bf16[256,1024]{1,0:T(8,128)(2,1)S(1)}, u32[]{:S(2)}, u32[]{:S(2)}) collective-permute-start(bf16[256,1024]{1,0:T(8,128)(2,1)S(1)} %operand.7), channel_id=1, source_target_pairs={{4,8},{8,4},{5,9},{9,5},{6,10},{10,6},{7,11},{11,7},{20,24},{24,20... | collective-permute-start | bytes 1572872 | tf_op jit(solution)/shard_map/ppermute | solution.py:387
  85.2 22.3 %collective-permute-start.15 = (bf16[256,1024]{1,0:T(8,128)(2,1)}, bf16[256,1024]{1,0:T(8,128)(2,1)S(1)}, u32[]{:S(2)}, u32[]{:S(2)}) collective-permute-start(bf16[256,1024]{1,0:T(8,128)(2,1)} %get-tuple-element.92), channel_id=1, source_target_pairs={{0,4},{12,8},{1,5},{13,9},{2,6},{14,10},{3,7},{15,11},{16,20},{28,... | collective-permute-start | bytes 1572872 | tf_op jit(solution)/shard_map/ppermute | solution.py:387
  89.0 5.4 %collective-permute-start.12 = (f32[128,256]{1,0:T(8,128)S(1)}, f32[128,256]{1,0:T(8,128)S(1)}, u32[]{:S(2)}, u32[]{:S(2)}) collective-permute-start(f32[128,256]{1,0:T(8,128)S(1)} %maximum_select_fusion.3), channel_id=1, source_target_pairs={{0,2},{2,0},{1,3},{3,1},{4,6},{6,4},{5,7},{7,5},{8,10},{10,8},{9,1... | collective-permute-start | bytes 393224 | tf_op jit(solution)/shard_map/ppermute | solution.py:295
  95.2 2.2 %copy-start.1 = (f32[4,256,1024]{2,1,0:T(8,128)S(1)}, f32[4,256,1024]{2,1,0:T(8,128)}, u32[]{:S(2)}) copy-start(f32[4,256,1024]{2,1,0:T(8,128)} %copy-done) | copy-start | bytes 12582916
  98.0 7.2 %copy-start.4 = (f32[4,256,1024]{2,1,0:T(8,128)S(1)}, f32[4,256,1024]{2,1,0:T(8,128)}, u32[]{:S(2)}) copy-start(f32[4,256,1024]{2,1,0:T(8,128)} %copy-done.3) | copy-start | bytes 12582916
  101.4 9.5 %collective-permute-start.17 = (bf16[256,1024]{1,0:T(8,128)(2,1)}, bf16[256,1024]{1,0:T(8,128)(2,1)S(1)}, u32[]{:S(2)}, u32[]{:S(2)}) collective-permute-start(bf16[256,1024]{1,0:T(8,128)(2,1)} %operand.9), channel_id=1, source_target_pairs={{4,8},{8,4},{5,9},{9,5},{6,10},{10,6},{7,11},{11,7},{20,24},{24,20... | collective-permute-start | bytes 1572872 | tf_op jit(solution)/shard_map/ppermute | solution.py:387
  102.1 16.6 %collective-permute-start.16 = (bf16[256,1024]{1,0:T(8,128)(2,1)S(1)}, bf16[256,1024]{1,0:T(8,128)(2,1)}, u32[]{:S(2)}, u32[]{:S(2)}) collective-permute-start(bf16[256,1024]{1,0:T(8,128)(2,1)S(1)} %operand.8), channel_id=1, source_target_pairs={{0,4},{8,12},{4,0},{12,8},{1,5},{9,13},{5,1},{13,9},{2,6},{10,14},... | collective-permute-start | bytes 1572872 | tf_op jit(solution)/shard_map/ppermute | solution.py:387
  106.7 22.9 %collective-permute-start.18 = (bf16[256,1024]{1,0:T(8,128)(2,1)}, bf16[256,1024]{1,0:T(8,128)(2,1)S(1)}, u32[]{:S(2)}, u32[]{:S(2)}) collective-permute-start(bf16[256,1024]{1,0:T(8,128)(2,1)} %operand.10), channel_id=1, source_target_pairs={{0,4},{8,12},{4,0},{12,8},{1,5},{9,13},{5,1},{13,9},{2,6},{10,14},... | collective-permute-start | bytes 1572872 | tf_op jit(solution)/shard_map/ppermute | solution.py:387
  108.2 21.4 %collective-permute-start.19 = (bf16[256,1024]{1,0:T(8,128)(2,1)S(1)}, bf16[256,1024]{1,0:T(8,128)(2,1)S(1)}, u32[]{:S(2)}, u32[]{:S(2)}) collective-permute-start(bf16[256,1024]{1,0:T(8,128)(2,1)S(1)} %operand.11), channel_id=1, source_target_pairs={{4,8},{8,4},{5,9},{9,5},{6,10},{10,6},{7,11},{11,7},{20,24},{24,20... | collective-permute-start | bytes 1572872 | tf_op jit(solution)/shard_map/ppermute | solution.py:387
  118.7 2.2 %copy-start.2 = (f32[4,256,1024]{2,1,0:T(8,128)S(1)}, f32[4,256,1024]{2,1,0:T(8,128)}, u32[]{:S(2)}) copy-start(f32[4,256,1024]{2,1,0:T(8,128)} %copy-done) | copy-start | bytes 12582916
  120.9 8.8 %copy-start.5 = (f32[4,256,1024]{2,1,0:T(8,128)S(1)}, f32[4,256,1024]{2,1,0:T(8,128)}, u32[]{:S(2)}) copy-start(f32[4,256,1024]{2,1,0:T(8,128)} %copy-done.3) | copy-start | bytes 12582916

commit v5 on v4

--- a/solution.py
+++ b/solution.py
@@ -27,10 +27,76 @@
     )
 
 
-def cross_tile(counts, scales, genes, row):
-    tile = counts.shape[0] // scales.shape[0]
-    block = counts[row * tile : (row + 1) * tile].astype(F32)
-    return contract_last((block * scales[row : row + 1]).astype(BF16), genes)
+def row_tile_specs(row_tiles, tile, wide, place):
+    return [
+        pl.BlockSpec((tile, wide), lambda *ids, r=r: (r, place(*ids)))
+        for r in range(row_tiles)
+    ]
+
+
+def scaled_rows(tile, row, gene_tile, factor, counts):
+    wide = counts.shape[1]
+    span = min(tile, wide)
+    parts = [
+        (
+            counts[:, pl.ds(c * span, span)].astype(F32) * factor[row, gene_tile + c]
+        ).astype(BF16)
+        for c in range(wide // span)
+    ]
+    return jnp.concatenate(parts, axis=1)
+
+
+def cross_kernel(tile, first, row_tiles, last, meta, factor, *refs):
+    counts, refs = refs[:row_tiles], refs[row_tiles:]
+    genes, refs = refs[0], refs[1:]
+    before, outs, total = (None, refs[:1], refs[1]) if not last else (refs[0], refs[1:3], refs[3])
+    step = pl.program_id(0)
+    gene_tile = (first + step) * (genes.shape[1] // tile)
+
+    @pl.when(step == 0)
+    def _():
+        total[...] = jnp.zeros_like(total) if before is None else before[...]
+
+    for row in range(row_tiles):
+        rows = pl.ds(row * tile, tile)
+        scaled = scaled_rows(tile, row, gene_tile, factor, counts[row])
+        total[rows, :] += contract_last(scaled, genes[...])
+
+    @pl.when(step == pl.num_programs(0) - 1)
+    def _():
+        if not last:
+            outs[0][...] = total[...]
+        else:
+            half = total.shape[0] // 2
+            sub = meta[0]
+            outs[0][...] = total[pl.ds(pl.multiple_of((1 - sub) * half, half), half), :]
+            outs[1][...] = total[pl.ds(pl.multiple_of(sub * half, half), half), :]
+
+
+def cross_part(first, steps, wide, tile, meta, factor, counts, genes, before):
+    rows, columns = counts.shape
+    width = genes.shape[0]
+    row_tiles = rows // tile
+    last = before is not None
+    whole = lambda n: pl.BlockSpec((n, width), lambda i, m: (0, 0))
+    sizes = (rows // 2, rows // 2) if last else (rows,)
+    return pl.pallas_call(
+        functools.partial(cross_kernel, tile, first, row_tiles, last),
+        out_shape=tuple(jax.ShapeDtypeStruct((n, width), F32) for n in sizes),
+        grid_spec=pltpu.PrefetchScalarGridSpec(
+            num_scalar_prefetch=1,
+            grid=(steps,),
+            in_specs=[pl.BlockSpec(memory_space=pltpu.SMEM)]
+            + row_tile_specs(row_tiles, tile, wide, lambda i, m: first + i)
+            + [pl.BlockSpec((width, wide), lambda i, m: (0, first + i))]
+            + ([whole(rows)] if last else []),
+            out_specs=tuple(whole(n) for n in sizes),
+            scratch_shapes=[pltpu.VMEM((rows, width), F32)],
+        ),
+        compiler_params=params(56),
+        cost_estimate=cost(1, 1),
+        name="cross",
+    )(meta, factor, *[counts] * row_tiles, genes, *([before] if last else []))
 
 
 def halves(value):
@@ -139,84 +205,122 @@
     )(meta, rho, cross_a, cross_b, inverse, start)
 
 
-def tile_products(tile, gene, meta, factor, counts, own, other):
-    rows, wide = counts.shape
-    half = rows // 2
-    sub = meta[0]
-    span = min(tile, wide)
-    total = None
-    for first, left in ((sub, own), (1 - sub, other)):
-        parts = [
-            [
-                (
-                    counts[
-                        pl.ds(pl.multiple_of(first * half + r * tile, tile), tile),
-                        pl.ds(c * span, span),
-                    ].astype(F32)
-                    * factor[first * (half // tile) + r, gene // tile + c]
-                ).astype(BF16)
-                for c in range(wide // span)
-            ]
-            for r in range(half // tile)
-        ]
-        right = jnp.concatenate([jnp.concatenate(row, axis=1) for row in parts], axis=0)
-        part = jnp.dot(left[...], right, preferred_element_type=F32)
-        total = part if total is None else total + part
-    return total
-
-
-def products_kernel(tile, wide, place, meta, factor, counts, own, other, *outs):
+def products_kernel(tile, wide, place, row_tiles, meta, factor, *refs):
+    counts, columns, outs = refs[:row_tiles], refs[row_tiles], refs[row_tiles + 1 :]
     step, order = pl.program_id(0), pl.program_id(1)
-    gene = place(step, order, meta) * wide
-    total = tile_products(tile, gene, meta, factor, counts, own, other)
-    outs[0][...] = total.astype(outs[0].dtype).reshape(outs[0].shape)
+    gene_tile = place(step, order, meta) * wide // tile
+    scaled = [
+        scaled_rows(tile, row, gene_tile, factor, counts[row]) for row in range(row_tiles)
+    ]
+    total = jnp.dot(
+        columns[...], jnp.concatenate(scaled, axis=0), preferred_element_type=F32
+    ).astype(BF16)
+    outs[0][...] = total.reshape(outs[0].shape)
     if len(outs) > 1:
 
         @pl.when(order == meta[4])
         def _():
-            outs[1][...] = total.astype(outs[1].dtype)
-
-
-def products(only_first, cells, start, chunk, tile, meta, factor, counts, own, other):
-    rows, columns = counts.shape
-    width = own.shape[0]
-    block = columns // cells
+            outs[1][...] = total
+
+
+def products(only_first, cells, start, chunk, tile, meta, factor, counts, columns):
+    rows = counts.shape[0]
+    width = columns.shape[0]
+    block = counts.shape[1] // cells
     blocks = 1 if only_first else cells
     wide = 2 * tile if chunk % (2 * tile) == 0 else min(tile, chunk)
+    row_tiles = rows // tile
 
     def place(i, o, m):
         return (m[3] if only_first else o) * (block // wide) + start // wide + i
 
-    halved = lambda: pl.BlockSpec((width, rows // 2), lambda i, o, m: (0, 0))
     flat = pl.BlockSpec((width, wide), lambda i, o, m: (0, i))
     operand = jax.ShapeDtypeStruct((width, chunk), BF16)
     if only_first:
         out_shape, out_specs = (operand,), (flat,)
     else:
-        out_shape = (jax.ShapeDtypeStruct((cells, width, chunk), F32), operand)
+        out_shape = (jax.ShapeDtypeStruct((cells, width, chunk), BF16), operand)
         out_specs = (pl.BlockSpec((1, width, wide), lambda i, o, m: (o, 0, i)), flat)
     return pl.pallas_call(
-        functools.partial(products_kernel, tile, wide, place),
+        functools.partial(products_kernel, tile, wide, place, row_tiles),
         out_shape=out_shape,
         grid_spec=pltpu.PrefetchScalarGridSpec(
             num_scalar_prefetch=1,
             grid=(chunk // wide, blocks),
-            in_specs=[
-                pl.BlockSpec(memory_space=pltpu.SMEM),
-                pl.BlockSpec((rows, wide), lambda i, o, m: (0, place(i, o, m))),
-                halved(),
-                halved(),
-            ],
+            in_specs=[pl.BlockSpec(memory_space=pltpu.SMEM)]
+            + row_tile_specs(row_tiles, tile, wide, place)
+            + [pl.BlockSpec((width, rows), lambda i, o, m: (0, 0))],
             out_specs=out_specs,
         ),
-        compiler_params=params(48),
+        compiler_params=params(50),
         cost_estimate=cost(1, 1),
         name="products",
-    )(meta, factor, counts, own, other)
+    )(meta, factor, *[counts] * row_tiles, columns)
+
+
+def small(kernel, name, out_shape, meta, *args, specs=None):
+    whole = lambda shape: pl.BlockSpec(shape, lambda i, m: (0,) * len(shape))
+    return pl.pallas_call(
+        kernel,
+        out_shape=out_shape,
+        grid_spec=pltpu.PrefetchScalarGridSpec(
+            num_scalar_prefetch=1,
+            grid=(1,),
+            in_specs=specs or [whole(arg.shape) for arg in args],
+            out_specs=whole(out_shape.shape),
+        ),
+        compiler_params=params(24),
+        cost_estimate=cost(1, 1),
+        name=name,
+    )(meta, *args)
+
+
+def turn_kernel(meta, value, out):
+    out[...] = value[...].astype(F32).T.astype(out.dtype)
+
+
+def turn(meta, value):
+    shape = jax.ShapeDtypeStruct(value.shape[::-1], value.dtype)
+    return small(turn_kernel, "turn", shape, meta, value)
+
+
+def row_share_kernel(meta, share, columns, out):
+    out[...] = contract_last(share[...], columns[...]).astype(out.dtype)
+
+
+def row_share(slot, part, meta, columns):
+    width, rows = columns.shape
+    specs = [
+        pl.BlockSpec((part, rows), lambda i, m: (m[slot], 0)),
+        pl.BlockSpec((width, rows), lambda i, m: (0, 0)),
+    ]
+    shape = jax.ShapeDtypeStruct((part, width), BF16)
+    return small(row_share_kernel, "row_share", shape, meta, columns, columns, specs=specs)
+
+
+def plus_kernel(meta, left, right, out):
+    out[...] = (left[...].astype(F32) + right[...].astype(F32)).astype(out.dtype)
+
+
+def plus(dtype, meta, left, right):
+    shape = jax.ShapeDtypeStruct(left.shape, dtype)
+    return small(plus_kernel, "plus", shape, meta, left, right)
+
+
+def stack_kernel(slot, bit, meta, mine, theirs, out):
+    rows = mine.shape[0]
+    upper = (meta[slot] & bit) != 0
+    out[:rows] = jnp.where(upper, theirs[...], mine[...])
+    out[rows:] = jnp.where(upper, mine[...], theirs[...])
+
+
+def stack(slot, bit, meta, mine, theirs):
+    shape = jax.ShapeDtypeStruct((2 * mine.shape[0],) + mine.shape[1:], mine.dtype)
+    return small(functools.partial(stack_kernel, slot, bit), "stack", shape, meta, mine, theirs)
 
 
 def operand_kernel(meta, total, before, out):
-    out[...] = (total[0] + before[...].astype(F32)).astype(BF16)
+    out[...] = (total[0].astype(F32) + before[...].astype(F32)).astype(BF16)
 
 
 def operand(slot, meta, total, before):
@@ -241,7 +345,7 @@
 
 
 def keep_kernel(meta, total, first, second, *refs):
-    value = total[0] + (first[...].astype(F32) + second[...].astype(F32))
+    value = total[0].astype(F32) + (first[...].astype(F32) + second[...].astype(F32))
     refs[-1][...] = value.T
 
 
@@ -349,6 +453,8 @@
     gene = lax.axis_index("gene")
     line = Line(cells, cell)
     places = [sub, cell, sub * genes + gene, line.block(1, 0), line.block(2, 0)]
+    places += [gene * subs + sub, gene]
+    at_phases = len(places)
     places += [line.block(phase, parity) for phase in range(2, cells) for parity in (0, 1)]
     meta = jnp.stack(places).astype(jnp.int32)
     factor = tile_mask.astype(F32) / tile_counts.astype(F32)
@@ -356,29 +462,33 @@
     gram = contract_last(gene_factor, gene_factor)
     factor, gram = after(factor, gram)
     gram = pair_sums(gram, "gene", genes)
-    row_tiles = rows // tile
-    early = row_tiles // 4 * 3
-    scales = jnp.broadcast_to(factor[:, :, None], factor.shape + (tile,))
-    scales = scales.reshape(row_tiles, columns)
-    cross = [cross_tile(counts, scales, gene_factor, row) for row in range(early)]
-    scales, gram = after(scales, gram)
+    wide = min(1024, columns)
+    steps = columns // wide
+    early = max(steps * 3 // 4, 1)
+    (early_total,) = cross_part(
+        0, early, wide, tile, meta, factor, counts, gene_factor, None
+    )
+    early_total, gram = after(early_total, gram)
     gram_other = swap(gram, "sub", subs, 1)
-    cross += [cross_tile(counts, scales, gene_factor, row) for row in range(early, row_tiles)]
-    low = jnp.concatenate(cross[: row_tiles // 2], axis=0)
-    high = jnp.concatenate(cross[row_tiles // 2 :], axis=0)
-    arrived = swap(jnp.where(sub == 0, high, low), "sub", subs, 1)
-    cross = jnp.where(sub == 0, low, high) + arrived
+    theirs, mine = cross_part(
+        early, steps - early, wide, tile, meta, factor, counts, gene_factor, early_total
+    )
+    cross = mine + swap(theirs, "sub", subs, 1)
     cross_a, cross_b = split_sums(cross, "gene", genes)
     inverse, rho = shifted_inverse(gram, gram_other)
     share = admm(meta, rho, cross_a, cross_b, inverse, prev_factor)
     own = join(share, "gene", genes, 1)
     other = swap(own, "sub", subs, 1)
+    whole = jnp.where(
+        sub == 0,
+        jnp.concatenate([own, other], axis=1),
+        jnp.concatenate([other, own], axis=1),
+    )
 
     block = columns // cells
     chunks = chunk_sizes(block)
     starts = [sum(chunks[:i]) for i in range(len(chunks))]
     every = range(len(chunks))
-    part = width // (genes * subs)
 
     arrived = {}
 
@@ -391,27 +501,26 @@
         if before is None:
             value = seconds[index]
         else:
-            value = operand(5 + 2 * (phase - 2) + parity, meta, totals[index], before)
+            slot = at_phases + 2 * (phase - 2) + parity
+            value = operand(slot, meta, totals[index], before)
             meta, value = after(meta, value)
         send(value, phase, parity, index)
         return meta
 
-    steps = [1 << i for i in range((cells - 1).bit_length())]
+    hops = [1 << i for i in range((cells - 1).bit_length())]
 
     def add_rows(meta, rows_sum):
-        rows_arrived = swap(rows_sum, "cell", cells, steps.pop(0))
-        rows_arrived, meta = after(rows_arrived, meta)
-        total = rows_sum.astype(F32) + rows_arrived.astype(F32)
-        return after(meta, total.astype(BF16) if steps else total)
-
-    def gram_rows(half):
-        rows_here = lax.dynamic_slice_in_dim(half, (gene * subs + sub) * part, part, 0)
-        return contract_last(rows_here, half)
-
-    meta, rows_sum = after(meta, (gram_rows(own) + gram_rows(other)).astype(BF16))
+        rows_arrived = swap(rows_sum, "cell", cells, hops.pop(0))
+        return after(meta, plus(BF16 if hops else F32, meta, rows_sum, rows_arrived))
+
+    def stack_rows(meta, rows_sum, axis, size, slot, bit):
+        rows_arrived = swap(rows_sum, axis, size, bit)
+        return after(meta, stack(slot, bit, meta, rows_sum, rows_arrived))
+
+    meta, rows_sum = after(meta, row_share(5, width // (genes * subs), meta, whole))
     for index in every:
         (first,) = products(
-            True, cells, starts[index], chunks[index], tile, meta, factor, counts, own, other
+            True, cells, starts[index], chunks[index], tile, meta, factor, counts, whole
         )
         meta, first = after(meta, first)
         for parity in (0, 1):
@@ -421,33 +530,25 @@
     totals, seconds = [], []
     for index in every:
         total, second = products(
-            False, cells, starts[index], chunks[index], tile, meta, factor, counts, own, other
+            False, cells, starts[index], chunks[index], tile, meta, factor, counts, whole
         )
         meta, second = after(meta, second)
         totals.append(total)
         seconds.append(second)
-        if cells > 2:
-            for parity in (0, 1):
-                meta = resend(meta, 2, parity, index)
-    while steps:
+        for parity in (0, 1):
+            meta = resend(meta, 2, parity, index)
+    while hops:
         meta, rows_sum = add_rows(meta, rows_sum)
-    new_factor = factor_gram = None
+    new_factor = turn(meta, whole)
+    meta, new_factor = after(meta, new_factor)
+    meta, rows_sum = stack_rows(meta, rows_sum, "sub", subs, 0, 1)
+    bits = [1 << i for i in range((genes - 1).bit_length())]
     for phase in range(3, cells):
         for index in every:
             for parity in (0, 1):
                 meta = resend(meta, phase, parity, index)
-                if new_factor is None:
-                    rows_sum = join(rows_sum, "sub", subs, 0)
-                    own_late, meta = after(own, meta)
-                    whole = jnp.where(
-                        sub == 0,
-                        jnp.concatenate([own_late, other], axis=1),
-                        jnp.concatenate([other, own_late], axis=1),
-                    )
-                    new_factor = whole.T
-                    meta, new_factor = after(meta, new_factor)
-                    factor_gram = join(rows_sum, "gene", genes, 0)
-                    meta, factor_gram = after(meta, factor_gram)
+                if bits:
+                    meta, rows_sum = stack_rows(meta, rows_sum, "gene", genes, 6, bits.pop(0))
     data_products = None
     last = cells - 1
     for index in every:
@@ -456,7 +557,7 @@
             arrived[last, 0, index], arrived[last, 1, index], data_products,
         )
         meta, data_products = after(meta, data_products)
-    return (new_factor, factor_gram, data_products)
+    return (new_factor, rows_sum, data_products)
 
 
 def solution(mesh):

time: 132 us -> 143 us (1.083)
  waiting for transfers between devices: 27.5 us -> 47 us
  Pallas kernels: 41.1 us -> 57 us
  matrix products: 16.4 us -> 4.75 us
  local copies, waits for them, and re-layouts: 10.9 us -> 0.71 us
  starting transfers between devices: 32.4 us -> 29.5 us
    pallas_call x4 -> x12, Pallas kernels: 24 us -> 43.5 us  [the longest x4 22.2 us: products(): pl.pallas_call(functools.partial(products_kernel, tile, wide, place, row_...]
    ppermute x10, waiting for transfers between devices: 13.3 us -> 28 us  [swap(): return lax.ppermute(value, axis, [(i, i ^ step) for i in range(size)])]
    dot_general x7 -> x1, matrix products: 16.4 us -> 4.75 us  [contract_last(): lax.dot_general(left, right, (((1,), (1,)), ((), ())), preferred_element_...]
    unnamed x30 -> x10, local copies, waits for them, and re-layouts: 10.8 us -> 0.03 us
    ppermute x10, starting transfers between devices: 12.6 us -> 6.98 us  [swap(): return lax.ppermute(value, axis, [(i, i ^ step) for i in range(size)])]
    ppermute x10, waiting for transfers between devices: 14.3 us -> 19 us  [send(): lax.ppermute(value, 'cell', pairs)]
    ppermute x10, starting transfers between devices: 19.8 us -> 22.6 us  [send(): lax.ppermute(value, 'cell', pairs)]
    pallas_call x6, Pallas kernels: 6.49 us -> 3.98 us  [operand(): pl.pallas_call(operand_kernel, out_shape=jax.ShapeDtypeStruct((width, chu...]
  transfers between devices with their start and end apart: 20 -> 20, of which waited for: 8 -> 8; matrix products, arithmetic and copies ran while one was open for 8% -> 1% of each run, Pallas kernels for 28% -> 33%
where the time goes in v5:
time: 143 us; the launch traced here: 142 us
  Pallas kernels  57 us (40%)
  waiting for transfers between devices  47 us (33%)
  starting transfers between devices  29.5 us (21%)
  matrix products  4.75 us (3%)
  other arithmetic  2.04 us (1%)
    ppermute x10, waiting for transfers between devices, swap(): return lax.ppermute(value, axis, [(i, i ^ step) for i in range(size)])  28 us
    ppermute x10, starting transfers between devices, send(): lax.ppermute(value, 'cell', pairs)  22.6 us
    pallas_call x4, Pallas kernels, products(): pl.pallas_call(functools.partial(products_kernel, tile, wide, place, row_...  22.2 us
    ppermute x10, waiting for transfers between devices, send(): lax.ppermute(value, 'cell', pairs)  19 us
    pallas_call x2, Pallas kernels, cross_part(): pl.pallas_call(functools.partial(cross_kernel, tile, first, row_tiles, la...  16 us
    ppermute x10, starting transfers between devices, swap(): return lax.ppermute(value, axis, [(i, i ^ step) for i in range(size)])  6.98 us
    pallas_call x6, Pallas kernels, small(): pl.pallas_call(kernel, out_shape=out_shape, grid_spec=pltpu.PrefetchScala...  5.27 us
    dot_general x1, matrix products, contract_last(): lax.dot_general(left, right, (((1,), (1,)), ((), ())), preferred_element_...  4.75 us
  transfers between devices with their start and end apart: 20, of which 8 were waited for; matrix products, arithmetic and copies ran while one was open for 1% of the time, Pallas kernels for 33%

profile of v5, /device:TPU:0, one launch (start us, length us, event | category | flops | bytes accessed | tf_op | source)
XLA Modules:
  0.0 142.0 jit_solution(12819335662995845136)
XLA Ops:
  0.7 4.8 %fusion = f32[256,256]{1,0:T(8,128)S(1)} fusion(bf16[256,8192]{1,0:T(8,128)(2,1)} %refs_4_.3), kind=kOutput, calls=%fused_computation.5 | convolution fusion | flops 1073741824 | bytes 4456448 | tf_op jit(solution)/shard_map/dot_general | solution.py:25
  5.4 0.6 convert_divide_fusion.factor
  6.0 2.9 %collective-permute-start = (f32[256,256]{1,0:T(8,128)S(1)}, f32[256,256]{1,0:T(8,128)S(1)}, u32[]{:S(2)}, u32[]{:S(2)}) collective-permute-start(f32[256,256]{1,0:T(8,128)S(1)} %fusion), channel_id=1, source_target_pairs={{0,2},{2,0},{1,3},{3,1},{4,6},{6,4},{5,7},{7,5},{8,10},{10,8},{9,1... | collective-permute-start | bytes 786440 | tf_op jit(solution)/shard_map/ppermute | solution.py:399
  9.0 0.7 stack.43.meta
  9.6 10.3 %cross.2.refs_5_ = f32[1024,256]{1,0:T(8,128)} custom-call(s32[11]{0:T(128)} %stack.43.meta, f32[4,32]{1,0:T(4,128)} %convert_divide_fusion.factor, bf16[1024,8192]{1,0:T(8,128)(2,1)} %refs_3_.11, bf16[1024,8192]{1,0:T(8,128)(2,1)} %refs_3_.11, bf16[1024,8192]{1,0:T(8,128)(2,1)} %refs_3_.11, bf16[1024,8192]{1,0:T(8,128)(2,1)} %refs_3_.11, ...), custom_call_target="tpu_custom_call" | custom-call | flops 1 | bytes 1 | tf_op jit(solution)/shard_map/cross/pallas_call | solution.py:83
  19.9 0.0 collective-permute-done
  20.0 5.7 %cross.3 = (f32[512,256]{1,0:T(8,128)}, f32[512,256]{1,0:T(8,128)}) custom-call(s32[11]{0:T(128)} %stack.43.meta, f32[4,32]{1,0:T(4,128)} %convert_divide_fusion.factor, bf16[1024,8192]{1,0:T(8,128)(2,1)} %refs_3_.11, bf16[1024,8192]{1,0:T(8,128)(2,1)} %refs_3_.11, bf16[1024,8192]{1,0:T(8,128)(2,1)} %refs_3_.11, bf16[1024,8192]{1,0:T(8,128)(2,1)} %refs_3_.11, ...), custom_call_target="tpu_custom_call" | custom-call | flops 1 | bytes 1 | tf_op jit(solution)/shard_map/cross/pallas_call | solution.py:83
  25.7 0.0 collective-permute-start.2
  25.7 0.5 collective-permute-start.1
  26.2 1.7 %collective-permute-done.2 = f32[512,256]{1,0:T(8,128)S(1)} collective-permute-done((f32[512,256]{1,0:T(8,128)}, f32[512,256]{1,0:T(8,128)S(1)}, u32[]{:S(2)}, u32[]{:S(2)}) %collective-permute-start.2) | collective-permute-done | bytes 524320 | tf_op jit(solution)/shard_map/ppermute | solution.py:399
  27.9 1.1 add.40
  29.1 0.0 copy-start
  29.1 0.0 copy-start.2
  29.1 0.1 collective-permute-start.3
  29.2 0.0 collective-permute-done.1.gram_b
  29.2 3.5 %inverse.1 = (f32[256,256]{1,0:T(8,128)S(1)}, f32[1,1]{1,0:T(1,128)}) custom-call(f32[256,256]{1,0:T(8,128)S(1)} %add.39.gram_a, f32[256,256]{1,0:T(8,128)S(1)} %collective-permute-done.1.gram_b), custom_call_target="tpu_custom_call" | custom-call | flops 2013265920 | bytes 786432 | tf_op jit(solution)/shard_map/inverse/pallas_call | solution.py:157
  32.8 4.8 %collective-permute-done.3.cross_b = f32[256,256]{1,0:T(8,128)S(1)} collective-permute-done((f32[256,256]{1,0:T(8,128)S(1)}, f32[256,256]{1,0:T(8,128)S(1)}, u32[]{:S(2)}, u32[]{:S(2)}) %collective-permute-start.3) | collective-permute-done | bytes 262176 | tf_op jit(solution)/shard_map/ppermute | solution.py:399
  37.6 2.1 %admm.1 = bf16[256,256]{1,0:T(8,128)(2,1)S(1)} custom-call(s32[11]{0:T(128)S(1)} %copy-done.1, f32[1,1]{1,0:T(1,128)} %get-tuple-element.53.rho_ref, f32[256,256]{1,0:T(8,128)S(1)} %get-tuple-element.98.cross_a, f32[256,256]{1,0:T(8,128)S(1)} %collective-permute-done.3.cross_b, f32[256,256]{1,0:T(8,128)S(1)} %get-tuple-element.57.inverse, ...), custom_call_target="tpu_custom_call" | custom-call | flops 301989888 | bytes 786432 | tf_op jit(solution)/shard_map/admm/pallas_call | solution.py:187
  39.6 0.4 collective-permute-start.4
  40.0 4.7 %collective-permute-done.4 = bf16[256,256]{1,0:T(8,128)(2,1)S(1)} collective-permute-done((bf16[256,256]{1,0:T(8,128)(2,1)S(1)}, bf16[256,256]{1,0:T(8,128)(2,1)S(1)}, u32[]{:S(2)}, u32[]{:S(2)}) %collective-permute-start.4) | collective-permute-done | bytes 131104 | tf_op jit(solution)/shard_map/ppermute | solution.py:399
  44.7 0.1 maximum_select_fusion.1
  44.8 0.1 collective-permute-start.5
  44.9 1.5 %collective-permute-done.5 = bf16[256,512]{1,0:T(8,128)(2,1)S(1)} collective-permute-done((bf16[256,512]{1,0:T(8,128)(2,1)S(1)}, bf16[256,512]{1,0:T(8,128)(2,1)S(1)}, u32[]{:S(2)}, u32[]{:S(2)}) %collective-permute-start.5) | collective-permute-done | bytes 262176 | tf_op jit(solution)/shard_map/ppermute | solution.py:399
  46.4 0.2 maximum_select_fusion.share.columns.refs_4_.value
  46.6 0.8 row_share.1.left
  47.4 1.6 %collective-permute-start.6 = (bf16[64,256]{1,0:T(8,128)(2,1)S(1)}, bf16[64,256]{1,0:T(8,128)(2,1)S(1)}, u32[]{:S(2)}, u32[]{:S(2)}) collective-permute-start(bf16[64,256]{1,0:T(8,128)(2,1)S(1)} %row_share.1.left), channel_id=1, source_target_pairs={{0,4},{4,0},{8,12},{12,8},{1,5},{5,1},{9,13},{13,9},{2,6},{6,2},{1... | collective-permute-start | bytes 98312 | tf_op jit(solution)/shard_map/ppermute | solution.py:399
  49.0 2.8 %products.4 = bf16[256,1024]{1,0:T(8,128)(2,1)S(1)} custom-call(s32[11]{0:T(128)S(1)} %copy-done.1, f32[4,32]{1,0:T(4,128)S(1)} %copy-done.2, bf16[1024,8192]{1,0:T(8,128)(2,1)} %refs_3_.11, bf16[1024,8192]{1,0:T(8,128)(2,1)} %refs_3_.11, bf16[1024,8192]{1,0:T(8,128)(2,1)} %refs_3_.11, bf16[1024,8192]{1,0:T(8,128)(2,1)} %refs_3_.11, ...), custom_call_target="tpu_custom_call" | custom-call | flops 1 | bytes 1 | tf_op jit(solution)/shard_map/products/pallas_call | solution.py:244
  51.9 2.4 %collective-permute-start.7 = (bf16[256,1024]{1,0:T(8,128)(2,1)S(1)}, bf16[256,1024]{1,0:T(8,128)(2,1)S(1)}, u32[]{:S(2)}, u32[]{:S(2)}) collective-permute-start(bf16[256,1024]{1,0:T(8,128)(2,1)S(1)} %products.4), channel_id=1, source_target_pairs={{0,4},{12,8},{1,5},{13,9},{2,6},{14,10},{3,7},{15,11},{16,20},{28,... | collective-permute-start | bytes 1572872 | tf_op jit(solution)/shard_map/ppermute | solution.py:497
  54.3 0.0 collective-permute-done.6.right
  54.3 0.6 plus.2.left
  54.8 2.9 %products.5 = bf16[256,1024]{1,0:T(8,128)(2,1)S(1)} custom-call(s32[11]{0:T(128)S(1)} %copy-done.1, f32[4,32]{1,0:T(4,128)S(1)} %copy-done.2, bf16[1024,8192]{1,0:T(8,128)(2,1)} %refs_3_.11, bf16[1024,8192]{1,0:T(8,128)(2,1)} %refs_3_.11, bf16[1024,8192]{1,0:T(8,128)(2,1)} %refs_3_.11, bf16[1024,8192]{1,0:T(8,128)(2,1)} %refs_3_.11, ...), custom_call_target="tpu_custom_call" | custom-call | flops 1 | bytes 1 | tf_op jit(solution)/shard_map/products/pallas_call | solution.py:244
  57.7 1.3 collective-permute-start.8
  59.0 8.3 %products.6 = (bf16[4,256,1024]{2,1,0:T(8,128)(2,1)S(1)}, bf16[256,1024]{1,0:T(8,128)(2,1)S(1)}) custom-call(s32[11]{0:T(128)S(1)} %copy-done.1, f32[4,32]{1,0:T(4,128)S(1)} %copy-done.2, bf16[1024,8192]{1,0:T(8,128)(2,1)} %refs_3_.11, bf16[1024,8192]{1,0:T(8,128)(2,1)} %refs_3_.11, bf16[1024,8192]{1,0:T(8,128)(2,1)} %refs_3_.11, ...), custom_call_target="tpu_custom_call" | custom-call | flops 1 | bytes 1 | tf_op jit(solution)/shard_map/products/pallas_call | solution.py:244
  67.3 0.0 collective-permute-done.7.before
  67.3 0.7 operand.6
  68.0 0.7 collective-permute-start.11
  68.7 7.6 %collective-permute-start.13 = (bf16[256,1024]{1,0:T(8,128)(2,1)S(1)}, bf16[256,1024]{1,0:T(8,128)(2,1)S(1)}, u32[]{:S(2)}, u32[]{:S(2)}) collective-permute-start(bf16[256,1024]{1,0:T(8,128)(2,1)S(1)} %get-tuple-element.84), channel_id=1, source_target_pairs={{0,4},{12,8},{1,5},{13,9},{2,6},{14,10},{3,7},{15,11},{16,20},{28,... | collective-permute-start | bytes 1572872 | tf_op jit(solution)/shard_map/ppermute | solution.py:497
  76.3 8.3 %products.7 = (bf16[4,256,1024]{2,1,0:T(8,128)(2,1)S(1)}, bf16[256,1024]{1,0:T(8,128)(2,1)S(1)}) custom-call(s32[11]{0:T(128)S(1)} %copy-done.1, f32[4,32]{1,0:T(4,128)S(1)} %copy-done.2, bf16[1024,8192]{1,0:T(8,128)(2,1)} %refs_3_.11, bf16[1024,8192]{1,0:T(8,128)(2,1)} %refs_3_.11, bf16[1024,8192]{1,0:T(8,128)(2,1)} %refs_3_.11, ...), custom_call_target="tpu_custom_call" | custom-call | flops 1 | bytes 1 | tf_op jit(solution)/shard_map/products/pallas_call | solution.py:244
  84.6 0.7 operand.7
  85.2 0.7 collective-permute-start.14
  85.9 2.5 %collective-permute-start.15 = (bf16[256,1024]{1,0:T(8,128)(2,1)S(1)}, bf16[256,1024]{1,0:T(8,128)(2,1)S(1)}, u32[]{:S(2)}, u32[]{:S(2)}) collective-permute-start(bf16[256,1024]{1,0:T(8,128)(2,1)S(1)} %get-tuple-element.88), channel_id=1, source_target_pairs={{0,4},{12,8},{1,5},{13,9},{2,6},{14,10},{3,7},{15,11},{16,20},{28,... | collective-permute-start | bytes 1572872 | tf_op jit(solution)/shard_map/ppermute | solution.py:497
  88.5 0.9 collective-permute-start.9
  89.3 10.5 %collective-permute-done.9.right = bf16[64,256]{1,0:T(8,128)(2,1)S(1)} collective-permute-done((bf16[64,256]{1,0:T(8,128)(2,1)S(1)}, bf16[64,256]{1,0:T(8,128)(2,1)S(1)}, u32[]{:S(2)}, u32[]{:S(2)}) %collective-permute-start.9) | collective-permute-done | bytes 32800 | tf_op jit(solution)/shard_map/ppermute | solution.py:399
  99.8 0.5 plus.3.mine
  100.4 0.1 collective-permute-start.10
  100.5 1.5 %turn.1 = bf16[1024,256]{1,0:T(8,128)(2,1)} custom-call(s32[11]{0:T(128)S(1)} %copy-done.1, bf16[256,1024]{1,0:T(8,128)(2,1)S(1)} %maximum_select_fusion.share.columns.refs_4_.value), custom_call_target="tpu_custom_call" | custom-call | flops 1 | bytes 1 | tf_op jit(solution)/shard_map/turn/pallas_call | solution.py:263
  102.0 0.0 collective-permute-done.10.theirs
  102.0 0.6 stack.44.mine
  102.6 0.5 collective-permute-start.12
  103.0 0.0 collective-permute-done.11.before
  103.0 0.7 operand.8
  103.7 4.8 %collective-permute-done.12.theirs = f32[128,256]{1,0:T(8,128)S(1)} collective-permute-done((f32[128,256]{1,0:T(8,128)S(1)}, f32[128,256]{1,0:T(8,128)S(1)}, u32[]{:S(2)}, u32[]{:S(2)}) %collective-permute-start.12) | collective-permute-done | bytes 131104 | tf_op jit(solution)/shard_map/ppermute | solution.py:399
  108.5 1.3 stack.45
  109.8 0.7 operand.9
  110.5 0.7 collective-permute-start.17
  111.2 5.9 %collective-permute-start.16 = (bf16[256,1024]{1,0:T(8,128)(2,1)S(1)}, bf16[256,1024]{1,0:T(8,128)(2,1)S(1)}, u32[]{:S(2)}, u32[]{:S(2)}) collective-permute-start(bf16[256,1024]{1,0:T(8,128)(2,1)S(1)} %operand.8), channel_id=1, source_target_pairs={{0,4},{8,12},{4,0},{12,8},{1,5},{9,13},{5,1},{13,9},{2,6},{10,14},... | collective-permute-start | bytes 1572872 | tf_op jit(solution)/shard_map/ppermute | solution.py:497
  117.1 0.7 operand.10
  117.7 0.1 collective-permute-start.18
  117.8 0.7 operand.11
  118.5 0.7 collective-permute-start.19
  119.2 10.6 %collective-permute-done.16.first = bf16[256,1024]{1,0:T(8,128)(2,1)S(1)} collective-permute-done((bf16[256,1024]{1,0:T(8,128)(2,1)S(1)}, bf16[256,1024]{1,0:T(8,128)(2,1)S(1)}, u32[]{:S(2)}, u32[]{:S(2)}) %collective-permute-start.16) | collective-permute-done | bytes 524320 | tf_op jit(solution)/shard_map/ppermute | solution.py:497
  129.8 1.9 %keep.2.refs_0_ = f32[2048,256]{1,0:T(8,128)} custom-call(s32[11]{0:T(128)S(1)} %copy-done.1, bf16[4,256,1024]{2,1,0:T(8,128)(2,1)S(1)} %get-tuple-element.65.total, bf16[256,1024]{1,0:T(8,128)(2,1)S(1)} %collective-permute-done.16.first, bf16[256,1024]{1,0:T(8,128)(2,1)S(1)} %collective-permute-done.17.second), custom_call_target="tpu_custom_call" | custom-call | flops 1 | bytes 1 | tf_op jit(solution)/shard_map/keep/pallas_call | solution.py:357
  131.7 8.4 %collective-permute-done.18.first = bf16[256,1024]{1,0:T(8,128)(2,1)S(1)} collective-permute-done((bf16[256,1024]{1,0:T(8,128)(2,1)S(1)}, bf16[256,1024]{1,0:T(8,128)(2,1)S(1)}, u32[]{:S(2)}, u32[]{:S(2)}) %collective-permute-start.18) | collective-permute-done | bytes 524320 | tf_op jit(solution)/shard_map/ppermute | solution.py:497
  140.1 1.9 %keep.3 = f32[2048,256]{1,0:T(8,128)} custom-call(s32[11]{0:T(128)S(1)} %copy-done.1, bf16[4,256,1024]{2,1,0:T(8,128)(2,1)S(1)} %get-tuple-element.70.total, bf16[256,1024]{1,0:T(8,128)(2,1)S(1)} %collective-permute-done.18.first, bf16[256,1024]{1,0:T(8,128)(2,1)S(1)} %collective-permute-done.19.second, ...), custom_call_target="tpu_custom_call", output_to_operand_aliasing={{}: (4, {})} | custom-call | flops 1 | bytes 1 | tf_op jit(solution)/shard_map/keep/pallas_call | solution.py:357
  (16 shorter events, 0.1 us)
Async XLA Ops:
  0.6 4.8 %copy-start.3 = (s32[4,32]{1,0:T(4,128)S(1)}, s32[4,32]{1,0:T(4,128)}, u32[]{:S(2)}) copy-start(s32[4,32]{1,0:T(4,128)} %param.7) | copy-start | bytes 1540
  0.6 4.8 %copy-start.4 = (s32[4,32]{1,0:T(4,128)S(1)}, s32[4,32]{1,0:T(4,128)}, u32[]{:S(2)}) copy-start(s32[4,32]{1,0:T(4,128)} %param.6) | copy-start | bytes 1540
  6.0 13.9 %collective-permute-start = (f32[256,256]{1,0:T(8,128)S(1)}, f32[256,256]{1,0:T(8,128)S(1)}, u32[]{:S(2)}, u32[]{:S(2)}) collective-permute-start(f32[256,256]{1,0:T(8,128)S(1)} %fusion), channel_id=1, source_target_pairs={{0,2},{2,0},{1,3},{3,1},{4,6},{6,4},{5,7},{7,5},{8,10},{10,8},{9,1... | collective-permute-start | bytes 786440 | tf_op jit(solution)/shard_map/ppermute | solution.py:399
  25.7 2.2 %collective-permute-start.2 = (f32[512,256]{1,0:T(8,128)}, f32[512,256]{1,0:T(8,128)S(1)}, u32[]{:S(2)}, u32[]{:S(2)}) collective-permute-start(f32[512,256]{1,0:T(8,128)} %get-tuple-element.56), channel_id=1, source_target_pairs={{0,1},{1,0},{2,3},{3,2},{4,5},{5,4},{6,7},{7,6},{8,9},{9,8},{10,11... | collective-permute-start | bytes 1572872 | tf_op jit(solution)/shard_map/ppermute | solution.py:399
  25.7 3.5 %collective-permute-start.1 = (f32[256,256]{1,0:T(8,128)S(1)}, f32[256,256]{1,0:T(8,128)S(1)}, u32[]{:S(2)}, u32[]{:S(2)}) collective-permute-start(f32[256,256]{1,0:T(8,128)S(1)} %add.39.gram_a), channel_id=1, source_target_pairs={{0,1},{1,0},{2,3},{3,2},{4,5},{5,4},{6,7},{7,6},{8,9},{9,8},{10,11... | collective-permute-start | bytes 786440 | tf_op jit(solution)/shard_map/ppermute | solution.py:399
  29.1 8.5 %copy-start = (bf16[1024,256]{1,0:T(8,128)(2,1)S(1)}, bf16[1024,256]{1,0:T(8,128)(2,1)}, u32[]{:S(2)}) copy-start(bf16[1024,256]{1,0:T(8,128)(2,1)} %start.1) | copy-start | bytes 1572868
  29.1 8.5 %copy-start.1 = (s32[11]{0:T(128)S(1)}, s32[11]{0:T(128)}, u32[]{:S(2)}) copy-start(s32[11]{0:T(128)} %stack.43.meta) | copy-start | bytes 136
  29.1 19.9 %copy-start.2 = (f32[4,32]{1,0:T(4,128)S(1)}, f32[4,32]{1,0:T(4,128)}, u32[]{:S(2)}) copy-start(f32[4,32]{1,0:T(4,128)} %convert_divide_fusion.factor) | copy-start | bytes 1540
  29.1 8.4 %collective-permute-start.3 = (f32[256,256]{1,0:T(8,128)S(1)}, f32[256,256]{1,0:T(8,128)S(1)}, u32[]{:S(2)}, u32[]{:S(2)}) collective-permute-start(f32[256,256]{1,0:T(8,128)S(1)} %get-tuple-element.97), channel_id=1, source_target_pairs={{0,2},{2,0},{1,3},{3,1},{4,6},{6,4},{5,7},{7,5},{8,10},{10,8},{9,1... | collective-permute-start | bytes 786440 | tf_op jit(solution)/shard_map/ppermute | solution.py:399
  39.6 5.0 %collective-permute-start.4 = (bf16[256,256]{1,0:T(8,128)(2,1)S(1)}, bf16[256,256]{1,0:T(8,128)(2,1)S(1)}, u32[]{:S(2)}, u32[]{:S(2)}) collective-permute-start(bf16[256,256]{1,0:T(8,128)(2,1)S(1)} %admm.1), channel_id=1, source_target_pairs={{0,2},{2,0},{1,3},{3,1},{4,6},{6,4},{5,7},{7,5},{8,10},{10,8},{9,1... | collective-permute-start | bytes 393224 | tf_op jit(solution)/shard_map/ppermute | solution.py:399
  44.8 1.6 %collective-permute-start.5 = (bf16[256,512]{1,0:T(8,128)(2,1)S(1)}, bf16[256,512]{1,0:T(8,128)(2,1)S(1)}, u32[]{:S(2)}, u32[]{:S(2)}) collective-permute-start(bf16[256,512]{1,0:T(8,128)(2,1)S(1)} %maximum_select_fusion.1), channel_id=1, source_target_pairs={{0,1},{1,0},{2,3},{3,2},{4,5},{5,4},{6,7},{7,6},{8,9},{9,8},{10,11... | collective-permute-start | bytes 786440 | tf_op jit(solution)/shard_map/ppermute | solution.py:399
  47.4 6.9 %collective-permute-start.6 = (bf16[64,256]{1,0:T(8,128)(2,1)S(1)}, bf16[64,256]{1,0:T(8,128)(2,1)S(1)}, u32[]{:S(2)}, u32[]{:S(2)}) collective-permute-start(bf16[64,256]{1,0:T(8,128)(2,1)S(1)} %row_share.1.left), channel_id=1, source_target_pairs={{0,4},{4,0},{8,12},{12,8},{1,5},{5,1},{9,13},{13,9},{2,6},{6,2},{1... | collective-permute-start | bytes 98312 | tf_op jit(solution)/shard_map/ppermute | solution.py:399
  51.9 15.4 %collective-permute-start.7 = (bf16[256,1024]{1,0:T(8,128)(2,1)S(1)}, bf16[256,1024]{1,0:T(8,128)(2,1)S(1)}, u32[]{:S(2)}, u32[]{:S(2)}) collective-permute-start(bf16[256,1024]{1,0:T(8,128)(2,1)S(1)} %products.4), channel_id=1, source_target_pairs={{0,4},{12,8},{1,5},{13,9},{2,6},{14,10},{3,7},{15,11},{16,20},{28,... | collective-permute-start | bytes 1572872 | tf_op jit(solution)/shard_map/ppermute | solution.py:497
  57.7 26.9 %collective-permute-start.8 = (bf16[256,1024]{1,0:T(8,128)(2,1)S(1)}, bf16[256,1024]{1,0:T(8,128)(2,1)S(1)}, u32[]{:S(2)}, u32[]{:S(2)}) collective-permute-start(bf16[256,1024]{1,0:T(8,128)(2,1)S(1)} %products.5), channel_id=1, source_target_pairs={{0,4},{12,8},{1,5},{13,9},{2,6},{14,10},{3,7},{15,11},{16,20},{28,... | collective-permute-start | bytes 1572872 | tf_op jit(solution)/shard_map/ppermute | solution.py:497
  68.0 35.0 %collective-permute-start.11 = (bf16[256,1024]{1,0:T(8,128)(2,1)S(1)}, bf16[256,1024]{1,0:T(8,128)(2,1)S(1)}, u32[]{:S(2)}, u32[]{:S(2)}) collective-permute-start(bf16[256,1024]{1,0:T(8,128)(2,1)S(1)} %operand.6), channel_id=1, source_target_pairs={{4,8},{8,4},{5,9},{9,5},{6,10},{10,6},{7,11},{11,7},{20,24},{24,20... | collective-permute-start | bytes 1572872 | tf_op jit(solution)/shard_map/ppermute | solution.py:497
  68.7 41.1 %collective-permute-start.13 = (bf16[256,1024]{1,0:T(8,128)(2,1)S(1)}, bf16[256,1024]{1,0:T(8,128)(2,1)S(1)}, u32[]{:S(2)}, u32[]{:S(2)}) collective-permute-start(bf16[256,1024]{1,0:T(8,128)(2,1)S(1)} %get-tuple-element.84), channel_id=1, source_target_pairs={{0,4},{12,8},{1,5},{13,9},{2,6},{14,10},{3,7},{15,11},{16,20},{28,... | collective-permute-start | bytes 1572872 | tf_op jit(solution)/shard_map/ppermute | solution.py:497
  85.2 31.8 %collective-permute-start.14 = (bf16[256,1024]{1,0:T(8,128)(2,1)S(1)}, bf16[256,1024]{1,0:T(8,128)(2,1)S(1)}, u32[]{:S(2)}, u32[]{:S(2)}) collective-permute-start(bf16[256,1024]{1,0:T(8,128)(2,1)S(1)} %operand.7), channel_id=1, source_target_pairs={{4,8},{8,4},{5,9},{9,5},{6,10},{10,6},{7,11},{11,7},{20,24},{24,20... | collective-permute-start | bytes 1572872 | tf_op jit(solution)/shard_map/ppermute | solution.py:497
  85.9 31.9 %collective-permute-start.15 = (bf16[256,1024]{1,0:T(8,128)(2,1)S(1)}, bf16[256,1024]{1,0:T(8,128)(2,1)S(1)}, u32[]{:S(2)}, u32[]{:S(2)}) collective-permute-start(bf16[256,1024]{1,0:T(8,128)(2,1)S(1)} %get-tuple-element.88), channel_id=1, source_target_pairs={{0,4},{12,8},{1,5},{13,9},{2,6},{14,10},{3,7},{15,11},{16,20},{28,... | collective-permute-start | bytes 1572872 | tf_op jit(solution)/shard_map/ppermute | solution.py:497
  88.5 11.3 %collective-permute-start.9 = (bf16[64,256]{1,0:T(8,128)(2,1)S(1)}, bf16[64,256]{1,0:T(8,128)(2,1)S(1)}, u32[]{:S(2)}, u32[]{:S(2)}) collective-permute-start(bf16[64,256]{1,0:T(8,128)(2,1)S(1)} %plus.2.left), channel_id=1, source_target_pairs={{0,8},{4,12},{8,0},{12,4},{1,9},{5,13},{9,1},{13,5},{2,10},{6,14},... | collective-permute-start | bytes 98312 | tf_op jit(solution)/shard_map/ppermute | solution.py:399
  100.4 1.6 %collective-permute-start.10 = (f32[64,256]{1,0:T(8,128)S(1)}, f32[64,256]{1,0:T(8,128)S(1)}, u32[]{:S(2)}, u32[]{:S(2)}) collective-permute-start(f32[64,256]{1,0:T(8,128)S(1)} %plus.3.mine), channel_id=1, source_target_pairs={{0,1},{1,0},{2,3},{3,2},{4,5},{5,4},{6,7},{7,6},{8,9},{9,8},{10,11... | collective-permute-start | bytes 196616 | tf_op jit(solution)/shard_map/ppermute | solution.py:399
  102.6 6.0 %collective-permute-start.12 = (f32[128,256]{1,0:T(8,128)S(1)}, f32[128,256]{1,0:T(8,128)S(1)}, u32[]{:S(2)}, u32[]{:S(2)}) collective-permute-start(f32[128,256]{1,0:T(8,128)S(1)} %stack.44.mine), channel_id=1, source_target_pairs={{0,2},{2,0},{1,3},{3,1},{4,6},{6,4},{5,7},{7,5},{8,10},{10,8},{9,1... | collective-permute-start | bytes 393224 | tf_op jit(solution)/shard_map/ppermute | solution.py:399
  110.5 8.7 %collective-permute-start.17 = (bf16[256,1024]{1,0:T(8,128)(2,1)S(1)}, bf16[256,1024]{1,0:T(8,128)(2,1)S(1)}, u32[]{:S(2)}, u32[]{:S(2)}) collective-permute-start(bf16[256,1024]{1,0:T(8,128)(2,1)S(1)} %operand.9), channel_id=1, source_target_pairs={{4,8},{8,4},{5,9},{9,5},{6,10},{10,6},{7,11},{11,7},{20,24},{24,20... | collective-permute-start | bytes 1572872 | tf_op jit(solution)/shard_map/ppermute | solution.py:497
  111.2 18.7 %collective-permute-start.16 = (bf16[256,1024]{1,0:T(8,128)(2,1)S(1)}, bf16[256,1024]{1,0:T(8,128)(2,1)S(1)}, u32[]{:S(2)}, u32[]{:S(2)}) collective-permute-start(bf16[256,1024]{1,0:T(8,128)(2,1)S(1)} %operand.8), channel_id=1, source_target_pairs={{0,4},{8,12},{4,0},{12,8},{1,5},{9,13},{5,1},{13,9},{2,6},{10,14},... | collective-permute-start | bytes 1572872 | tf_op jit(solution)/shard_map/ppermute | solution.py:497
  117.7 22.4 %collective-permute-start.18 = (bf16[256,1024]{1,0:T(8,128)(2,1)S(1)}, bf16[256,1024]{1,0:T(8,128)(2,1)S(1)}, u32[]{:S(2)}, u32[]{:S(2)}) collective-permute-start(bf16[256,1024]{1,0:T(8,128)(2,1)S(1)} %operand.10), channel_id=1, source_target_pairs={{0,4},{8,12},{4,0},{12,8},{1,5},{9,13},{5,1},{13,9},{2,6},{10,14},... | collective-permute-start | bytes 1572872 | tf_op jit(solution)/shard_map/ppermute | solution.py:497
  118.5 21.6 %collective-permute-start.19 = (bf16[256,1024]{1,0:T(8,128)(2,1)S(1)}, bf16[256,1024]{1,0:T(8,128)(2,1)S(1)}, u32[]{:S(2)}, u32[]{:S(2)}) collective-permute-start(bf16[256,1024]{1,0:T(8,128)(2,1)S(1)} %operand.11), channel_id=1, source_target_pairs={{4,8},{8,4},{5,9},{9,5},{6,10},{10,6},{7,11},{11,7},{20,24},{24,20... | collective-permute-start | bytes 1572872 | tf_op jit(solution)/shard_map/ppermute | solution.py:497

commit v6 on v5

--- a/solution.py
+++ b/solution.py
@@ -2,6 +2,7 @@
 
 import jax
 import jax.numpy as jnp
+import numpy as np
 from jax import lax
 from jax.experimental import pallas as pl
 from jax.experimental.pallas import tpu as pltpu
@@ -25,6 +26,47 @@
     return lax.dot_general(
         left, right, (((1,), (1,)), ((), ())), preferred_element_type=F32
     )
+
+
+def gram_kernel(pieces, *refs):
+    genes, (tile_mask, tile_counts, gram, factor) = refs[:pieces], refs[pieces:]
+    part = None
+    for piece in genes:
+        product = contract_last(piece[...], piece[...])
+        part = product if part is None else part + product
+
+    @pl.when(pl.program_id(0) == 0)
+    def _():
+        gram[...] = part
+        factor[...] = tile_mask[...].astype(F32) / tile_counts[...].astype(F32)
+
+    @pl.when(pl.program_id(0) > 0)
+    def _():
+        gram[...] += part
+
+
+def gram_part(genes, tile_mask, tile_counts):
+    width, columns = genes.shape
+    wide = min(1024, columns)
+    pieces = min(4, columns // wide)
+    tiles = pl.BlockSpec(tile_mask.shape, lambda i: (0, 0))
+    return pl.pallas_call(
+        functools.partial(gram_kernel, pieces),
+        out_shape=(
+            jax.ShapeDtypeStruct((width, width), F32),
+            jax.ShapeDtypeStruct(tile_mask.shape, F32),
+        ),
+        grid=(columns // (wide * pieces),),
+        in_specs=[
+            pl.BlockSpec((width, wide), lambda i, p=p: (0, i * pieces + p))
+            for p in range(pieces)
+        ]
+        + [tiles, tiles],
+        out_specs=(pl.BlockSpec((width, width), lambda i: (0, 0)), tiles),
+        compiler_params=params(60),
+        cost_estimate=cost(1, 1),
+        name="gram",
+    )(*[genes] * pieces, tile_mask, tile_counts)
 
 
 def row_tile_specs(row_tiles, tile, wide, place):
@@ -34,24 +76,12 @@
     ]
 
 
-def scaled_rows(tile, row, gene_tile, factor, counts):
-    wide = counts.shape[1]
-    span = min(tile, wide)
-    parts = [
-        (
-            counts[:, pl.ds(c * span, span)].astype(F32) * factor[row, gene_tile + c]
-        ).astype(BF16)
-        for c in range(wide // span)
-    ]
-    return jnp.concatenate(parts, axis=1)
-
-
 def cross_kernel(tile, first, row_tiles, last, meta, factor, *refs):
     counts, refs = refs[:row_tiles], refs[row_tiles:]
     genes, refs = refs[0], refs[1:]
     before, outs, total = (None, refs[:1], refs[1]) if not last else (refs[0], refs[1:3], refs[3])
     step = pl.program_id(0)
-    gene_tile = (first + step) * (genes.shape[1] // tile)
+    gene_tiles = genes.shape[1] // tile
 
     @pl.when(step == 0)
     def _():
@@ -59,8 +89,12 @@
 
     for row in range(row_tiles):
         rows = pl.ds(row * tile, tile)
-        scaled = scaled_rows(tile, row, gene_tile, factor, counts[row])
-        total[rows, :] += contract_last(scaled, genes[...])
+        part = total[rows, :]
+        for col in range(gene_tiles):
+            at = pl.ds(col * tile, tile)
+            scale = factor[row, (first + step) * gene_tiles + col]
+            part += scale * contract_last(counts[row][:, at], genes[:, at])
+        total[rows, :] = part
 
     @pl.when(step == pl.num_programs(0) - 1)
     def _():
@@ -209,18 +243,27 @@
     counts, columns, outs = refs[:row_tiles], refs[row_tiles], refs[row_tiles + 1 :]
     step, order = pl.program_id(0), pl.program_id(1)
     gene_tile = place(step, order, meta) * wide // tile
-    scaled = [
-        scaled_rows(tile, row, gene_tile, factor, counts[row]) for row in range(row_tiles)
-    ]
-    total = jnp.dot(
-        columns[...], jnp.concatenate(scaled, axis=0), preferred_element_type=F32
-    ).astype(BF16)
-    outs[0][...] = total.reshape(outs[0].shape)
-    if len(outs) > 1:
-
-        @pl.when(order == meta[4])
-        def _():
-            outs[1][...] = total
+    span = min(tile, wide)
+    for col in range(wide // span):
+        at = pl.ds(col * span, span)
+        total = None
+        for row in range(row_tiles):
+            part = jnp.dot(
+                columns[:, pl.ds(row * tile, tile)],
+                counts[row][:, at],
+                preferred_element_type=F32,
+            )
+            part = factor[row, gene_tile + col] * part
+            total = part if total is None else total + part
+        total = total.astype(BF16)
+        if len(outs) == 1:
+            outs[0][:, at] = total
+        else:
+            outs[0][0, :, at] = total
+
+            @pl.when(order == meta[4])
+            def _(at=at, total=total):
+                outs[1][:, at] = total
 
 
 def products(only_first, cells, start, chunk, tile, meta, factor, counts, columns):
@@ -298,13 +341,19 @@
     return small(row_share_kernel, "row_share", shape, meta, columns, columns, specs=specs)
 
 
-def plus_kernel(meta, left, right, out):
-    out[...] = (left[...].astype(F32) + right[...].astype(F32)).astype(out.dtype)
-
-
-def plus(dtype, meta, left, right):
-    shape = jax.ShapeDtypeStruct(left.shape, dtype)
-    return small(plus_kernel, "plus", shape, meta, left, right)
+def hop_kernel(kind, targets, meta, held, arrived, out):
+    reached = meta[1] == targets[0]
+    for target in targets[1:]:
+        reached = jnp.logical_or(reached, meta[1] == target)
+    more = arrived[...].astype(F32)
+    base = held[...].astype(F32)
+    value = base + more if kind == "sum" else more
+    out[...] = jnp.where(reached, value, base).astype(out.dtype)
+
+
+def hop(kind, targets, meta, held, arrived):
+    shape = jax.ShapeDtypeStruct(held.shape, held.dtype)
+    return small(functools.partial(hop_kernel, kind, targets), "hop", shape, meta, held, arrived)
 
 
 def stack_kernel(slot, bit, meta, mine, theirs, out):
@@ -452,15 +501,26 @@
     cell = lax.axis_index("cell")
     gene = lax.axis_index("gene")
     line = Line(cells, cell)
-    places = [sub, cell, sub * genes + gene, line.block(1, 0), line.block(2, 0)]
-    places += [gene * subs + sub, gene]
-    at_phases = len(places)
-    places += [line.block(phase, parity) for phase in range(2, cells) for parity in (0, 1)]
-    meta = jnp.stack(places).astype(jnp.int32)
-    factor = tile_mask.astype(F32) / tile_counts.astype(F32)
-
-    gram = contract_last(gene_factor, gene_factor)
-    factor, gram = after(factor, gram)
+    blocks = [(1, 0), (2, 0)]
+    blocks += [(phase, parity) for phase in range(2, cells) for parity in (0, 1)]
+    at_phases = 8
+    table = np.zeros((5, at_phases + len(blocks) - 2), np.int32)
+    table[1, [0, 5]] = 1
+    table[1, 2] = genes
+    table[2, 1] = 1
+    table[3, [2, 6]] = 1
+    table[3, 5] = subs
+    for slot, (phase, parity) in zip([3, 4, *range(at_phases, table.shape[1])], blocks):
+        ahead = cells - 2 * phase
+        table[:, slot] = [phase + (1 - parity) * ahead, 0, 1, 0, (2 * parity - 1) * ahead]
+    is_block = np.zeros(table.shape[1], bool)
+    is_block[[3, 4, *range(at_phases, table.shape[1])]] = True
+    meta = table[0] + sub * table[1] + cell * table[2] + gene * table[3]
+    meta = meta + (cell & 1) * table[4]
+    meta = jnp.where(is_block & (meta >= cells), meta - cells, meta).astype(jnp.int32)
+
+    gram, factor = gram_part(gene_factor, tile_mask, tile_counts)
+    meta, gram = after(meta, gram)
     gram = pair_sums(gram, "gene", genes)
     wide = min(1024, columns)
     steps = columns // wide
@@ -507,11 +567,17 @@
         send(value, phase, parity, index)
         return meta
 
-    hops = [1 << i for i in range((cells - 1).bit_length())]
-
-    def add_rows(meta, rows_sum):
-        rows_arrived = swap(rows_sum, "cell", cells, hops.pop(0))
-        return after(meta, plus(BF16 if hops else F32, meta, rows_sum, rows_arrived))
+    middle = cells // 2
+    inward = [[(i, i + 1), (cells - 1 - i, cells - 2 - i)] for i in range(middle - 1)]
+    outward = [[(b, a) for a, b in pairs] for pairs in reversed(inward)]
+    hops = [("sum", p) for p in inward] + [("sum", [(middle - 1, middle), (middle, middle - 1)])]
+    hops += [("copy", p) for p in outward]
+
+    def hop_rows(meta, rows_sum):
+        kind, pairs = hops.pop(0)
+        rows_arrived = lax.ppermute(rows_sum, "cell", pairs)
+        targets = [b for _, b in pairs]
+        return after(meta, hop(kind, targets, meta, rows_sum, rows_arrived))
 
     def stack_rows(meta, rows_sum, axis, size, slot, bit):
         rows_arrived = swap(rows_sum, axis, size, bit)
@@ -525,27 +591,29 @@
         meta, first = after(meta, first)
         for parity in (0, 1):
             send(first, 1, parity, index)
-        if index == 0:
-            meta, rows_sum = add_rows(meta, rows_sum)
+        if index == 0 and hops:
+            meta, rows_sum = hop_rows(meta, rows_sum)
     totals, seconds = [], []
     for index in every:
         total, second = products(
             False, cells, starts[index], chunks[index], tile, meta, factor, counts, whole
         )
         meta, second = after(meta, second)
+        if hops:
+            meta, rows_sum = hop_rows(meta, rows_sum)
         totals.append(total)
         seconds.append(second)
         for parity in (0, 1):
             meta = resend(meta, 2, parity, index)
     while hops:
-        meta, rows_sum = add_rows(meta, rows_sum)
+        meta, rows_sum = hop_rows(meta, rows_sum)
     new_factor = turn(meta, whole)
     meta, new_factor = after(meta, new_factor)
     meta, rows_sum = stack_rows(meta, rows_sum, "sub", subs, 0, 1)
     bits = [1 << i for i in range((genes - 1).bit_length())]
     for phase in range(3, cells):
         for index in every:
-            for parity in (0, 1):
+            for parity in (1, 0):
                 meta = resend(meta, phase, parity, index)
                 if bits:
                     meta, rows_sum = stack_rows(meta, rows_sum, "gene", genes, 6, bits.pop(0))
@@ -557,7 +625,7 @@
             arrived[last, 0, index], arrived[last, 1, index], data_products,
         )
         meta, data_products = after(meta, data_products)
-    return (new_factor, rows_sum, data_products)
+    return (new_factor, rows_sum.astype(F32), data_products)
 
 
 def solution(mesh):

time: 143 us -> 132 us (0.923)
  the two profiles are of different devices: /device:TPU:0 before, /device:TPU:12 now
where the time goes in v6:
time: 132 us; the launch traced here: 131 us
  Pallas kernels  62 us (47%)
  waiting for transfers between devices  37.9 us (29%)
  starting transfers between devices  27.5 us (21%)
  other arithmetic  2.74 us (2%)
    ppermute x10, waiting for transfers between devices, send(): lax.ppermute(value, 'cell', pairs)  25.6 us
    pallas_call x4, Pallas kernels, products(): pl.pallas_call(functools.partial(products_kernel, tile, wide, place, row_...  23.5 us
    ppermute x10, starting transfers between devices, send(): lax.ppermute(value, 'cell', pairs)  17 us
    pallas_call x2, Pallas kernels, cross_part(): pl.pallas_call(functools.partial(cross_kernel, tile, first, row_tiles, la...  16.1 us
    ppermute x8, waiting for transfers between devices, swap(): return lax.ppermute(value, axis, [(i, i ^ step) for i in range(size)])  12 us
    ppermute x3, starting transfers between devices, hop_rows(): rows_arrived = lax.ppermute(rows_sum, 'cell', pairs)  6.54 us
    pallas_call x7, Pallas kernels, small(): pl.pallas_call(kernel, out_shape=out_shape, grid_spec=pltpu.PrefetchScala...  5.11 us
    pallas_call x6, Pallas kernels, operand(): pl.pallas_call(operand_kernel, out_shape=jax.ShapeDtypeStruct((width, chu...  3.98 us
  transfers between devices with their start and end apart: 21, of which 10 were waited for; matrix products, arithmetic and copies ran while one was open for 1% of the time, Pallas kernels for 36%

profile of v6, /device:TPU:12, one launch (start us, length us, event | category | flops | bytes accessed | tf_op | source)
XLA Modules:
  0.0 131.3 jit_solution(13461944500948958848)
XLA Ops:
  0.6 0.0 copy-start.4
  0.7 0.0 copy-start.5
  0.7 0.0 copy-start.6
  0.7 0.0 copy-start.7
  0.7 0.0 copy-start.8
  0.7 3.9 %gram.1 = (f32[256,256]{1,0:T(8,128)}, f32[4,32]{1,0:T(4,128)}) custom-call(bf16[256,8192]{1,0:T(8,128)(2,1)} %refs_4_.5, bf16[256,8192]{1,0:T(8,128)(2,1)} %refs_4_.5, bf16[256,8192]{1,0:T(8,128)(2,1)} %refs_4_.5, bf16[256,8192]{1,0:T(8,128)(2,1)} %refs_4_.5, s32[4,32]{1,0:T(4,128)} %refs_4_.3, s32[4,32]{1,0:T(4,128)} %refs_5_.1), custom_call_target="tpu_custom_call" | custom-call | flops 1 | bytes 1 | tf_op jit(solution)/shard_map/gram/pallas_call | solution.py:53
  4.6 0.6 and_select_fusion.meta
  5.2 1.5 %collective-permute-start = (f32[256,256]{1,0:T(8,128)}, f32[256,256]{1,0:T(8,128)S(1)}, u32[]{:S(2)}, u32[]{:S(2)}) collective-permute-start(f32[256,256]{1,0:T(8,128)} %get-tuple-element.57), channel_id=1, source_target_pairs={{0,2},{2,0},{1,3},{3,1},{4,6},{6,4},{5,7},{7,5},{8,10},{10,8},{9,1... | collective-permute-start | bytes 786440 | tf_op jit(solution)/shard_map/ppermute | solution.py:448
  6.7 10.4 %cross.2.refs_5_ = f32[1024,256]{1,0:T(8,128)} custom-call(s32[12]{0:T(128)} %and_select_fusion.meta, f32[4,32]{1,0:T(4,128)} %get-tuple-element.56.factor, bf16[1024,8192]{1,0:T(8,128)(2,1)} %refs_3_.13, bf16[1024,8192]{1,0:T(8,128)(2,1)} %refs_3_.13, bf16[1024,8192]{1,0:T(8,128)(2,1)} %refs_3_.13, bf16[1024,8192]{1,0:T(8,128)(2,1)} %refs_3_.13, ...), custom_call_target="tpu_custom_call" | custom-call | flops 1 | bytes 1 | tf_op jit(solution)/shard_map/cross/pallas_call | solution.py:117
  17.2 5.7 %cross.3 = (f32[512,256]{1,0:T(8,128)}, f32[512,256]{1,0:T(8,128)}) custom-call(s32[12]{0:T(128)} %and_select_fusion.meta, f32[4,32]{1,0:T(4,128)} %get-tuple-element.56.factor, bf16[1024,8192]{1,0:T(8,128)(2,1)} %refs_3_.13, bf16[1024,8192]{1,0:T(8,128)(2,1)} %refs_3_.13, bf16[1024,8192]{1,0:T(8,128)(2,1)} %refs_3_.13, bf16[1024,8192]{1,0:T(8,128)(2,1)} %refs_3_.13, ...), custom_call_target="tpu_custom_call" | custom-call | flops 1 | bytes 1 | tf_op jit(solution)/shard_map/cross/pallas_call | solution.py:117
  22.9 0.5 collective-permute-start.1
  23.4 1.7 %collective-permute-done.2 = f32[512,256]{1,0:T(8,128)S(1)} collective-permute-done((f32[512,256]{1,0:T(8,128)}, f32[512,256]{1,0:T(8,128)S(1)}, u32[]{:S(2)}, u32[]{:S(2)}) %collective-permute-start.2) | collective-permute-done | bytes 524320 | tf_op jit(solution)/shard_map/ppermute | solution.py:448
  25.1 1.1 add.24
  26.3 0.6 collective-permute-start.3
  26.9 3.5 %inverse.1 = (f32[256,256]{1,0:T(8,128)S(1)}, f32[1,1]{1,0:T(1,128)}) custom-call(f32[256,256]{1,0:T(8,128)S(1)} %add.23.gram_a, f32[256,256]{1,0:T(8,128)S(1)} %collective-permute-done.1.gram_b), custom_call_target="tpu_custom_call" | custom-call | flops 2013265920 | bytes 786432 | tf_op jit(solution)/shard_map/inverse/pallas_call | solution.py:191
  30.4 4.3 %collective-permute-done.3.cross_b = f32[256,256]{1,0:T(8,128)S(1)} collective-permute-done((f32[256,256]{1,0:T(8,128)S(1)}, f32[256,256]{1,0:T(8,128)S(1)}, u32[]{:S(2)}, u32[]{:S(2)}) %collective-permute-start.3) | collective-permute-done | bytes 262176 | tf_op jit(solution)/shard_map/ppermute | solution.py:448
  34.7 2.1 %admm.1 = bf16[256,256]{1,0:T(8,128)(2,1)S(1)} custom-call(s32[12]{0:T(128)S(1)} %copy-done.1, f32[1,1]{1,0:T(1,128)} %get-tuple-element.59.rho_ref, f32[256,256]{1,0:T(8,128)S(1)} %get-tuple-element.106.cross_a, f32[256,256]{1,0:T(8,128)S(1)} %collective-permute-done.3.cross_b, f32[256,256]{1,0:T(8,128)S(1)} %get-tuple-element.63.inverse, ...), custom_call_target="tpu_custom_call" | custom-call | flops 301989888 | bytes 786432 | tf_op jit(solution)/shard_map/admm/pallas_call | solution.py:221
  36.8 0.6 collective-permute-start.4
  37.4 4.4 %collective-permute-done.4 = bf16[256,256]{1,0:T(8,128)(2,1)S(1)} collective-permute-done((bf16[256,256]{1,0:T(8,128)(2,1)S(1)}, bf16[256,256]{1,0:T(8,128)(2,1)S(1)}, u32[]{:S(2)}, u32[]{:S(2)}) %collective-permute-start.4) | collective-permute-done | bytes 131104 | tf_op jit(solution)/shard_map/ppermute | solution.py:448
  41.8 0.1 maximum_select_fusion.1
  42.0 0.1 collective-permute-start.5
  42.0 1.5 %collective-permute-done.5 = bf16[256,512]{1,0:T(8,128)(2,1)S(1)} collective-permute-done((bf16[256,512]{1,0:T(8,128)(2,1)S(1)}, bf16[256,512]{1,0:T(8,128)(2,1)S(1)}, u32[]{:S(2)}, u32[]{:S(2)}) %collective-permute-start.5) | collective-permute-done | bytes 262176 | tf_op jit(solution)/shard_map/ppermute | solution.py:448
  43.6 0.1 maximum_select_fusion.share.columns.refs_4_.value
  43.7 0.8 row_share.1.held
  44.5 1.3 collective-permute-start.6
  45.8 2.8 %products.4 = bf16[256,1024]{1,0:T(8,128)(2,1)S(1)} custom-call(s32[12]{0:T(128)S(1)} %copy-done.1, f32[4,32]{1,0:T(4,128)S(1)} %copy-done.2, bf16[1024,8192]{1,0:T(8,128)(2,1)} %refs_3_.13, bf16[1024,8192]{1,0:T(8,128)(2,1)} %refs_3_.13, bf16[1024,8192]{1,0:T(8,128)(2,1)} %refs_3_.13, bf16[1024,8192]{1,0:T(8,128)(2,1)} %refs_3_.13, ...), custom_call_target="tpu_custom_call" | custom-call | flops 1 | bytes 1 | tf_op jit(solution)/shard_map/products/pallas_call | solution.py:287
  48.6 1.3 collective-permute-start.8
  49.9 0.4 collective-permute-done.6.arrived
  50.3 0.6 hop.3.held
  50.9 2.8 %products.5 = bf16[256,1024]{1,0:T(8,128)(2,1)S(1)} custom-call(s32[12]{0:T(128)S(1)} %copy-done.1, f32[4,32]{1,0:T(4,128)S(1)} %copy-done.2, bf16[1024,8192]{1,0:T(8,128)(2,1)} %refs_3_.13, bf16[1024,8192]{1,0:T(8,128)(2,1)} %refs_3_.13, bf16[1024,8192]{1,0:T(8,128)(2,1)} %refs_3_.13, bf16[1024,8192]{1,0:T(8,128)(2,1)} %refs_3_.13, ...), custom_call_target="tpu_custom_call" | custom-call | flops 1 | bytes 1 | tf_op jit(solution)/shard_map/products/pallas_call | solution.py:287
  53.7 1.3 collective-permute-start.10
  55.0 3.5 %collective-permute-start.7 = (bf16[64,256]{1,0:T(8,128)(2,1)S(1)}, bf16[64,256]{1,0:T(8,128)(2,1)S(1)}, u32[]{:S(2)}, u32[]{:S(2)}) collective-permute-start(bf16[64,256]{1,0:T(8,128)(2,1)S(1)} %hop.3.held), channel_id=1, source_target_pairs={{4,8},{8,4},{5,9},{9,5},{6,10},{10,6},{7,11},{11,7},{20,24},{24,20... | collective-permute-start | bytes 98312 | tf_op jit(solution)/shard_map/ppermute | solution.py:578
  58.5 9.0 %products.6 = (bf16[4,256,1024]{2,1,0:T(8,128)(2,1)S(1)}, bf16[256,1024]{1,0:T(8,128)(2,1)S(1)}) custom-call(s32[12]{0:T(128)S(1)} %copy-done.1, f32[4,32]{1,0:T(4,128)S(1)} %copy-done.2, bf16[1024,8192]{1,0:T(8,128)(2,1)} %refs_3_.13, bf16[1024,8192]{1,0:T(8,128)(2,1)} %refs_3_.13, bf16[1024,8192]{1,0:T(8,128)(2,1)} %refs_3_.13, ...), custom_call_target="tpu_custom_call" | custom-call | flops 1 | bytes 1 | tf_op jit(solution)/shard_map/products/pallas_call | solution.py:287
  67.5 0.6 hop.4.held
  68.0 1.8 %collective-permute-start.9 = (bf16[64,256]{1,0:T(8,128)(2,1)S(1)}, bf16[64,256]{1,0:T(8,128)(2,1)S(1)}, u32[]{:S(2)}, u32[]{:S(2)}) collective-permute-start(bf16[64,256]{1,0:T(8,128)(2,1)S(1)} %hop.4.held), channel_id=1, source_target_pairs={{4,0},{8,12},{5,1},{9,13},{6,2},{10,14},{7,3},{11,15},{20,16},{24,... | collective-permute-start | bytes 98312 | tf_op jit(solution)/shard_map/ppermute | solution.py:578
  69.8 1.3 collective-permute-start.12
  71.1 0.7 operand.6
  71.8 9.0 %products.7 = (bf16[4,256,1024]{2,1,0:T(8,128)(2,1)S(1)}, bf16[256,1024]{1,0:T(8,128)(2,1)S(1)}) custom-call(s32[12]{0:T(128)S(1)} %copy-done.1, f32[4,32]{1,0:T(4,128)S(1)} %copy-done.2, bf16[1024,8192]{1,0:T(8,128)(2,1)} %refs_3_.13, bf16[1024,8192]{1,0:T(8,128)(2,1)} %refs_3_.13, bf16[1024,8192]{1,0:T(8,128)(2,1)} %refs_3_.13, ...), custom_call_target="tpu_custom_call" | custom-call | flops 1 | bytes 1 | tf_op jit(solution)/shard_map/products/pallas_call | solution.py:287
  80.8 3.5 %collective-permute-start.14 = (bf16[256,1024]{1,0:T(8,128)(2,1)S(1)}, bf16[256,1024]{1,0:T(8,128)(2,1)S(1)}, u32[]{:S(2)}, u32[]{:S(2)}) collective-permute-start(bf16[256,1024]{1,0:T(8,128)(2,1)S(1)} %operand.6), channel_id=1, source_target_pairs={{4,8},{8,4},{5,9},{9,5},{6,10},{10,6},{7,11},{11,7},{20,24},{24,20... | collective-permute-start | bytes 1572872 | tf_op jit(solution)/shard_map/ppermute | solution.py:557
  84.3 0.6 hop.5.mine
  84.8 1.3 collective-permute-start.15
  86.1 0.7 operand.7
  86.8 2.4 %collective-permute-start.16 = (bf16[256,1024]{1,0:T(8,128)(2,1)S(1)}, bf16[256,1024]{1,0:T(8,128)(2,1)S(1)}, u32[]{:S(2)}, u32[]{:S(2)}) collective-permute-start(bf16[256,1024]{1,0:T(8,128)(2,1)S(1)} %operand.7), channel_id=1, source_target_pairs={{4,8},{8,4},{5,9},{9,5},{6,10},{10,6},{7,11},{11,7},{20,24},{24,20... | collective-permute-start | bytes 1572872 | tf_op jit(solution)/shard_map/ppermute | solution.py:557
  89.2 0.1 collective-permute-start.11
  89.3 1.5 %turn.1 = bf16[1024,256]{1,0:T(8,128)(2,1)} custom-call(s32[12]{0:T(128)S(1)} %copy-done.1, bf16[256,1024]{1,0:T(8,128)(2,1)S(1)} %maximum_select_fusion.share.columns.refs_4_.value), custom_call_target="tpu_custom_call" | custom-call | flops 1 | bytes 1 | tf_op jit(solution)/shard_map/turn/pallas_call | solution.py:306
  90.8 0.5 stack.2.mine
  91.4 0.6 collective-permute-start.13
  92.0 0.7 operand.8
  92.6 3.5 %collective-permute-start.18 = (bf16[256,1024]{1,0:T(8,128)(2,1)S(1)}, bf16[256,1024]{1,0:T(8,128)(2,1)S(1)}, u32[]{:S(2)}, u32[]{:S(2)}) collective-permute-start(bf16[256,1024]{1,0:T(8,128)(2,1)S(1)} %operand.8), channel_id=1, source_target_pairs={{4,8},{8,4},{5,9},{9,5},{6,10},{10,6},{7,11},{11,7},{20,24},{24,20... | collective-permute-start | bytes 1572872 | tf_op jit(solution)/shard_map/ppermute | solution.py:557
  96.1 0.6 stack.3
  96.7 0.8 collective-permute-done.14.before
  97.5 0.7 operand.9
  98.2 1.3 collective-permute-done.15.before
  99.5 0.7 operand.10
  100.2 0.1 collective-permute-start.17
  100.2 2.4 %collective-permute-start.20 = (bf16[256,1024]{1,0:T(8,128)(2,1)S(1)}, bf16[256,1024]{1,0:T(8,128)(2,1)S(1)}, u32[]{:S(2)}, u32[]{:S(2)}) collective-permute-start(bf16[256,1024]{1,0:T(8,128)(2,1)S(1)} %operand.10), channel_id=1, source_target_pairs={{4,8},{8,4},{5,9},{9,5},{6,10},{10,6},{7,11},{11,7},{20,24},{24,20... | collective-permute-start | bytes 1572872 | tf_op jit(solution)/shard_map/ppermute | solution.py:557
  102.6 6.2 %collective-permute-done.16.before = bf16[256,1024]{1,0:T(8,128)(2,1)S(1)} collective-permute-done((bf16[256,1024]{1,0:T(8,128)(2,1)S(1)}, bf16[256,1024]{1,0:T(8,128)(2,1)S(1)}, u32[]{:S(2)}, u32[]{:S(2)}) %collective-permute-start.16) | collective-permute-done | bytes 524320 | tf_op jit(solution)/shard_map/ppermute | solution.py:557
  108.8 0.7 operand.11
  109.4 0.1 collective-permute-start.19
  109.5 0.7 convert_element_type.3
  110.2 9.8 %collective-permute-done.18.second = bf16[256,1024]{1,0:T(8,128)(2,1)S(1)} collective-permute-done((bf16[256,1024]{1,0:T(8,128)(2,1)S(1)}, bf16[256,1024]{1,0:T(8,128)(2,1)S(1)}, u32[]{:S(2)}, u32[]{:S(2)}) %collective-permute-start.18) | collective-permute-done | bytes 524320 | tf_op jit(solution)/shard_map/ppermute | solution.py:557
  120.0 1.9 %keep.2.refs_0_ = f32[2048,256]{1,0:T(8,128)} custom-call(s32[12]{0:T(128)S(1)} %copy-done.1, bf16[4,256,1024]{2,1,0:T(8,128)(2,1)S(1)} %get-tuple-element.73.total, bf16[256,1024]{1,0:T(8,128)(2,1)S(1)} %collective-permute-done.17.first, bf16[256,1024]{1,0:T(8,128)(2,1)S(1)} %collective-permute-done.18.second), custom_call_target="tpu_custom_call" | custom-call | flops 1 | bytes 1 | tf_op jit(solution)/shard_map/keep/pallas_call | solution.py:406
  121.9 7.5 %collective-permute-done.20.second = bf16[256,1024]{1,0:T(8,128)(2,1)S(1)} collective-permute-done((bf16[256,1024]{1,0:T(8,128)(2,1)S(1)}, bf16[256,1024]{1,0:T(8,128)(2,1)S(1)}, u32[]{:S(2)}, u32[]{:S(2)}) %collective-permute-start.20) | collective-permute-done | bytes 524320 | tf_op jit(solution)/shard_map/ppermute | solution.py:557
  129.4 1.9 %keep.3 = f32[2048,256]{1,0:T(8,128)} custom-call(s32[12]{0:T(128)S(1)} %copy-done.1, bf16[4,256,1024]{2,1,0:T(8,128)(2,1)S(1)} %get-tuple-element.80.total, bf16[256,1024]{1,0:T(8,128)(2,1)S(1)} %collective-permute-done.19.first, bf16[256,1024]{1,0:T(8,128)(2,1)S(1)} %collective-permute-done.20.second, ...), custom_call_target="tpu_custom_call", output_to_operand_aliasing={{}: (4, {})} | custom-call | flops 1 | bytes 1 | tf_op jit(solution)/shard_map/keep/pallas_call | solution.py:406
  (29 shorter events, 0.1 us)
Async XLA Ops:
  0.6 3.9 %copy-start.4 = (s32[12]{0:T(128)S(1)}, s32[12]{0:T(128)}, u32[]{:S(2)}) copy-start(s32[12]{0:T(128)} %constant.31.clone) | copy-start | bytes 148
  0.7 3.9 %copy-start.5 = (s32[12]{0:T(128)S(1)}, s32[12]{0:T(128)}, u32[]{:S(2)}) copy-start(s32[12]{0:T(128)} %constant.32.clone) | copy-start | bytes 148
  0.7 3.9 %copy-start.6 = (s32[12]{0:T(128)S(1)}, s32[12]{0:T(128)}, u32[]{:S(2)}) copy-start(s32[12]{0:T(128)} %constant.33.clone) | copy-start | bytes 148
  0.7 3.9 %copy-start.7 = (s32[12]{0:T(128)S(1)}, s32[12]{0:T(128)}, u32[]{:S(2)}) copy-start(s32[12]{0:T(128)} %constant.34.clone) | copy-start | bytes 148
  0.7 3.9 %copy-start.8 = (s32[12]{0:T(128)S(1)}, s32[12]{0:T(128)}, u32[]{:S(2)}) copy-start(s32[12]{0:T(128)} %constant.35.clone) | copy-start | bytes 148
  0.7 3.9 %copy-start.9 = (pred[12]{0:T(512)(128)(4,1)S(1)}, pred[12]{0:T(512)(128)(4,1)}, u32[]{:S(2)}) copy-start(pred[12]{0:T(512)(128)(4,1)} %constant.36.clone) | copy-start | bytes 40
  5.2 11.9 %collective-permute-start = (f32[256,256]{1,0:T(8,128)}, f32[256,256]{1,0:T(8,128)S(1)}, u32[]{:S(2)}, u32[]{:S(2)}) collective-permute-start(f32[256,256]{1,0:T(8,128)} %get-tuple-element.57), channel_id=1, source_target_pairs={{0,2},{2,0},{1,3},{3,1},{4,6},{6,4},{5,7},{7,5},{8,10},{10,8},{9,1... | collective-permute-start | bytes 786440 | tf_op jit(solution)/shard_map/ppermute | solution.py:448
  6.7 10.4 %copy-start.3 = (f32[256,256]{1,0:T(8,128)S(1)}, f32[256,256]{1,0:T(8,128)}, u32[]{:S(2)}) copy-start(f32[256,256]{1,0:T(8,128)} %get-tuple-element.57) | copy-start | bytes 786436
  22.9 2.2 %collective-permute-start.2 = (f32[512,256]{1,0:T(8,128)}, f32[512,256]{1,0:T(8,128)S(1)}, u32[]{:S(2)}, u32[]{:S(2)}) collective-permute-start(f32[512,256]{1,0:T(8,128)} %get-tuple-element.62), channel_id=1, source_target_pairs={{0,1},{1,0},{2,3},{3,2},{4,5},{5,4},{6,7},{7,6},{8,9},{9,8},{10,11... | collective-permute-start | bytes 1572872 | tf_op jit(solution)/shard_map/ppermute | solution.py:448
  22.9 4.0 %collective-permute-start.1 = (f32[256,256]{1,0:T(8,128)S(1)}, f32[256,256]{1,0:T(8,128)S(1)}, u32[]{:S(2)}, u32[]{:S(2)}) collective-permute-start(f32[256,256]{1,0:T(8,128)S(1)} %add.23.gram_a), channel_id=1, source_target_pairs={{0,1},{1,0},{2,3},{3,2},{4,5},{5,4},{6,7},{7,6},{8,9},{9,8},{10,11... | collective-permute-start | bytes 786440 | tf_op jit(solution)/shard_map/ppermute | solution.py:448
  26.3 8.4 %copy-start = (bf16[1024,256]{1,0:T(8,128)(2,1)S(1)}, bf16[1024,256]{1,0:T(8,128)(2,1)}, u32[]{:S(2)}) copy-start(bf16[1024,256]{1,0:T(8,128)(2,1)} %start.1) | copy-start | bytes 1572868
  26.3 8.4 %copy-start.1 = (s32[12]{0:T(128)S(1)}, s32[12]{0:T(128)}, u32[]{:S(2)}) copy-start(s32[12]{0:T(128)} %and_select_fusion.meta) | copy-start | bytes 148
  26.3 8.4 %collective-permute-start.3 = (f32[256,256]{1,0:T(8,128)S(1)}, f32[256,256]{1,0:T(8,128)S(1)}, u32[]{:S(2)}, u32[]{:S(2)}) collective-permute-start(f32[256,256]{1,0:T(8,128)S(1)} %get-tuple-element.105), channel_id=1, source_target_pairs={{0,2},{2,0},{1,3},{3,1},{4,6},{6,4},{5,7},{7,5},{8,10},{10,8},{9,1... | collective-permute-start | bytes 786440 | tf_op jit(solution)/shard_map/ppermute | solution.py:448
  30.4 15.4 %copy-start.2 = (f32[4,32]{1,0:T(4,128)S(1)}, f32[4,32]{1,0:T(4,128)}, u32[]{:S(2)}) copy-start(f32[4,32]{1,0:T(4,128)} %get-tuple-element.56.factor) | copy-start | bytes 1540
  36.8 5.0 %collective-permute-start.4 = (bf16[256,256]{1,0:T(8,128)(2,1)S(1)}, bf16[256,256]{1,0:T(8,128)(2,1)S(1)}, u32[]{:S(2)}, u32[]{:S(2)}) collective-permute-start(bf16[256,256]{1,0:T(8,128)(2,1)S(1)} %admm.1), channel_id=1, source_target_pairs={{0,2},{2,0},{1,3},{3,1},{4,6},{6,4},{5,7},{7,5},{8,10},{10,8},{9,1... | collective-permute-start | bytes 393224 | tf_op jit(solution)/shard_map/ppermute | solution.py:448
  42.0 1.6 %collective-permute-start.5 = (bf16[256,512]{1,0:T(8,128)(2,1)S(1)}, bf16[256,512]{1,0:T(8,128)(2,1)S(1)}, u32[]{:S(2)}, u32[]{:S(2)}) collective-permute-start(bf16[256,512]{1,0:T(8,128)(2,1)S(1)} %maximum_select_fusion.1), channel_id=1, source_target_pairs={{0,1},{1,0},{2,3},{3,2},{4,5},{5,4},{6,7},{7,6},{8,9},{9,8},{10,11... | collective-permute-start | bytes 786440 | tf_op jit(solution)/shard_map/ppermute | solution.py:448
  44.5 5.8 %collective-permute-start.6 = (bf16[64,256]{1,0:T(8,128)(2,1)S(1)}, bf16[64,256]{1,0:T(8,128)(2,1)S(1)}, u32[]{:S(2)}, u32[]{:S(2)}) collective-permute-start(bf16[64,256]{1,0:T(8,128)(2,1)S(1)} %row_share.1.held), channel_id=1, source_target_pairs={{0,4},{12,8},{1,5},{13,9},{2,6},{14,10},{3,7},{15,11},{16,20},{28,... | collective-permute-start | bytes 98312 | tf_op jit(solution)/shard_map/ppermute | solution.py:578
  48.6 22.5 %collective-permute-start.8 = (bf16[256,1024]{1,0:T(8,128)(2,1)S(1)}, bf16[256,1024]{1,0:T(8,128)(2,1)S(1)}, u32[]{:S(2)}, u32[]{:S(2)}) collective-permute-start(bf16[256,1024]{1,0:T(8,128)(2,1)S(1)} %products.4), channel_id=1, source_target_pairs={{0,4},{12,8},{1,5},{13,9},{2,6},{14,10},{3,7},{15,11},{16,20},{28,... | collective-permute-start | bytes 1572872 | tf_op jit(solution)/shard_map/ppermute | solution.py:557
  53.7 32.4 %collective-permute-start.10 = (bf16[256,1024]{1,0:T(8,128)(2,1)S(1)}, bf16[256,1024]{1,0:T(8,128)(2,1)S(1)}, u32[]{:S(2)}, u32[]{:S(2)}) collective-permute-start(bf16[256,1024]{1,0:T(8,128)(2,1)S(1)} %products.5), channel_id=1, source_target_pairs={{0,4},{12,8},{1,5},{13,9},{2,6},{14,10},{3,7},{15,11},{16,20},{28,... | collective-permute-start | bytes 1572872 | tf_op jit(solution)/shard_map/ppermute | solution.py:557
  55.0 12.5 %collective-permute-start.7 = (bf16[64,256]{1,0:T(8,128)(2,1)S(1)}, bf16[64,256]{1,0:T(8,128)(2,1)S(1)}, u32[]{:S(2)}, u32[]{:S(2)}) collective-permute-start(bf16[64,256]{1,0:T(8,128)(2,1)S(1)} %hop.3.held), channel_id=1, source_target_pairs={{4,8},{8,4},{5,9},{9,5},{6,10},{10,6},{7,11},{11,7},{20,24},{24,20... | collective-permute-start | bytes 98312 | tf_op jit(solution)/shard_map/ppermute | solution.py:578
  68.0 16.2 %collective-permute-start.9 = (bf16[64,256]{1,0:T(8,128)(2,1)S(1)}, bf16[64,256]{1,0:T(8,128)(2,1)S(1)}, u32[]{:S(2)}, u32[]{:S(2)}) collective-permute-start(bf16[64,256]{1,0:T(8,128)(2,1)S(1)} %hop.4.held), channel_id=1, source_target_pairs={{4,0},{8,12},{5,1},{9,13},{6,2},{10,14},{7,3},{11,15},{20,16},{24,... | collective-permute-start | bytes 98312 | tf_op jit(solution)/shard_map/ppermute | solution.py:578
  69.8 22.2 %collective-permute-start.12 = (bf16[256,1024]{1,0:T(8,128)(2,1)S(1)}, bf16[256,1024]{1,0:T(8,128)(2,1)S(1)}, u32[]{:S(2)}, u32[]{:S(2)}) collective-permute-start(bf16[256,1024]{1,0:T(8,128)(2,1)S(1)} %get-tuple-element.87), channel_id=1, source_target_pairs={{0,4},{12,8},{1,5},{13,9},{2,6},{14,10},{3,7},{15,11},{16,20},{28,... | collective-permute-start | bytes 1572872 | tf_op jit(solution)/shard_map/ppermute | solution.py:557
  80.8 16.8 %collective-permute-start.14 = (bf16[256,1024]{1,0:T(8,128)(2,1)S(1)}, bf16[256,1024]{1,0:T(8,128)(2,1)S(1)}, u32[]{:S(2)}, u32[]{:S(2)}) collective-permute-start(bf16[256,1024]{1,0:T(8,128)(2,1)S(1)} %operand.6), channel_id=1, source_target_pairs={{4,8},{8,4},{5,9},{9,5},{6,10},{10,6},{7,11},{11,7},{20,24},{24,20... | collective-permute-start | bytes 1572872 | tf_op jit(solution)/shard_map/ppermute | solution.py:557
  84.8 14.7 %collective-permute-start.15 = (bf16[256,1024]{1,0:T(8,128)(2,1)S(1)}, bf16[256,1024]{1,0:T(8,128)(2,1)S(1)}, u32[]{:S(2)}, u32[]{:S(2)}) collective-permute-start(bf16[256,1024]{1,0:T(8,128)(2,1)S(1)} %get-tuple-element.94), channel_id=1, source_target_pairs={{0,4},{12,8},{1,5},{13,9},{2,6},{14,10},{3,7},{15,11},{16,20},{28,... | collective-permute-start | bytes 1572872 | tf_op jit(solution)/shard_map/ppermute | solution.py:557
  86.8 22.0 %collective-permute-start.16 = (bf16[256,1024]{1,0:T(8,128)(2,1)S(1)}, bf16[256,1024]{1,0:T(8,128)(2,1)S(1)}, u32[]{:S(2)}, u32[]{:S(2)}) collective-permute-start(bf16[256,1024]{1,0:T(8,128)(2,1)S(1)} %operand.7), channel_id=1, source_target_pairs={{4,8},{8,4},{5,9},{9,5},{6,10},{10,6},{7,11},{11,7},{20,24},{24,20... | collective-permute-start | bytes 1572872 | tf_op jit(solution)/shard_map/ppermute | solution.py:557
  89.2 1.6 %collective-permute-start.11 = (bf16[64,256]{1,0:T(8,128)(2,1)S(1)}, bf16[64,256]{1,0:T(8,128)(2,1)S(1)}, u32[]{:S(2)}, u32[]{:S(2)}) collective-permute-start(bf16[64,256]{1,0:T(8,128)(2,1)S(1)} %hop.5.mine), channel_id=1, source_target_pairs={{0,1},{1,0},{2,3},{3,2},{4,5},{5,4},{6,7},{7,6},{8,9},{9,8},{10,11... | collective-permute-start | bytes 98312 | tf_op jit(solution)/shard_map/ppermute | solution.py:448
  91.4 4.8 %collective-permute-start.13 = (bf16[128,256]{1,0:T(8,128)(2,1)S(1)}, bf16[128,256]{1,0:T(8,128)(2,1)S(1)}, u32[]{:S(2)}, u32[]{:S(2)}) collective-permute-start(bf16[128,256]{1,0:T(8,128)(2,1)S(1)} %stack.2.mine), channel_id=1, source_target_pairs={{0,2},{2,0},{1,3},{3,1},{4,6},{6,4},{5,7},{7,5},{8,10},{10,8},{9,1... | collective-permute-start | bytes 196616 | tf_op jit(solution)/shard_map/ppermute | solution.py:448
  92.6 27.4 %collective-permute-start.18 = (bf16[256,1024]{1,0:T(8,128)(2,1)S(1)}, bf16[256,1024]{1,0:T(8,128)(2,1)S(1)}, u32[]{:S(2)}, u32[]{:S(2)}) collective-permute-start(bf16[256,1024]{1,0:T(8,128)(2,1)S(1)} %operand.8), channel_id=1, source_target_pairs={{4,8},{8,4},{5,9},{9,5},{6,10},{10,6},{7,11},{11,7},{20,24},{24,20... | collective-permute-start | bytes 1572872 | tf_op jit(solution)/shard_map/ppermute | solution.py:557
  100.2 19.8 %collective-permute-start.17 = (bf16[256,1024]{1,0:T(8,128)(2,1)S(1)}, bf16[256,1024]{1,0:T(8,128)(2,1)S(1)}, u32[]{:S(2)}, u32[]{:S(2)}) collective-permute-start(bf16[256,1024]{1,0:T(8,128)(2,1)S(1)} %operand.9), channel_id=1, source_target_pairs={{0,4},{8,12},{4,0},{12,8},{1,5},{9,13},{5,1},{13,9},{2,6},{10,14},... | collective-permute-start | bytes 1572872 | tf_op jit(solution)/shard_map/ppermute | solution.py:557
  100.2 29.2 %collective-permute-start.20 = (bf16[256,1024]{1,0:T(8,128)(2,1)S(1)}, bf16[256,1024]{1,0:T(8,128)(2,1)S(1)}, u32[]{:S(2)}, u32[]{:S(2)}) collective-permute-start(bf16[256,1024]{1,0:T(8,128)(2,1)S(1)} %operand.10), channel_id=1, source_target_pairs={{4,8},{8,4},{5,9},{9,5},{6,10},{10,6},{7,11},{11,7},{20,24},{24,20... | collective-permute-start | bytes 1572872 | tf_op jit(solution)/shard_map/ppermute | solution.py:557
  109.4 20.0 %collective-permute-start.19 = (bf16[256,1024]{1,0:T(8,128)(2,1)S(1)}, bf16[256,1024]{1,0:T(8,128)(2,1)S(1)}, u32[]{:S(2)}, u32[]{:S(2)}) collective-permute-start(bf16[256,1024]{1,0:T(8,128)(2,1)S(1)} %operand.11), channel_id=1, source_target_pairs={{0,4},{8,12},{4,0},{12,8},{1,5},{9,13},{5,1},{13,9},{2,6},{10,14},... | collective-permute-start | bytes 1572872 | tf_op jit(solution)/shard_map/ppermute | solution.py:557

commit v7 on v6

--- a/solution.py
+++ b/solution.py
@@ -14,8 +14,16 @@
 MIB = 1024 * 1024
 
 
-def params(limit=48):
+def params(limit=16):
     return pltpu.CompilerParams(vmem_limit_bytes=limit * MIB)
+
+
+def away(value):
+    return pltpu.with_memory_space_constraint(value, pltpu.HBM)
+
+
+def held(value):
+    return pltpu.with_memory_space_constraint(value, pltpu.VMEM)
 
 
 def cost(flops, bytes_accessed):
@@ -28,109 +36,149 @@
     )
 
 
-def gram_kernel(pieces, *refs):
-    genes, (tile_mask, tile_counts, gram, factor) = refs[:pieces], refs[pieces:]
+def row_copies(source, target, first, sems):
+    rows = target.shape[0]
+    piece = max(rows // sems.shape[0], 16)
+    return [
+        pltpu.make_async_copy(
+            source.at[pl.ds(first + i * piece, piece)],
+            target.at[pl.ds(i * piece, piece)],
+            sems.at[i],
+        )
+        for i in range(rows // piece)
+    ]
+
+
+def gram_kernel(tile, genes, counts, tile_mask, tile_counts, gram, factor, genes_held, head, sems_a, sems_b):
+    gene_copies = row_copies(genes, genes_held, 0, sems_a)
+    head_copies = row_copies(counts, head, 0, sems_b)
+    for copy in gene_copies + head_copies:
+        copy.start()
+    factor[...] = tile_mask[...].astype(F32) / tile_counts[...].astype(F32)
+    for copy in gene_copies:
+        copy.wait()
+    columns = genes.shape[1]
+    wide = min(1024, columns)
     part = None
-    for piece in genes:
-        product = contract_last(piece[...], piece[...])
+    for start in range(0, columns, wide):
+        piece = genes_held[:, start : start + wide]
+        product = contract_last(piece, piece)
         part = product if part is None else part + product
-
-    @pl.when(pl.program_id(0) == 0)
-    def _():
-        gram[...] = part
-        factor[...] = tile_mask[...].astype(F32) / tile_counts[...].astype(F32)
-
-    @pl.when(pl.program_id(0) > 0)
-    def _():
-        gram[...] += part
-
-
-def gram_part(genes, tile_mask, tile_counts):
+    gram[...] = part
+    for copy in head_copies:
+        copy.wait()
+
+
+def gram_part(genes, counts, tile, tile_mask, tile_counts):
     width, columns = genes.shape
-    wide = min(1024, columns)
-    pieces = min(4, columns // wide)
-    tiles = pl.BlockSpec(tile_mask.shape, lambda i: (0, 0))
-    return pl.pallas_call(
-        functools.partial(gram_kernel, pieces),
+    here = pl.BlockSpec(memory_space=pltpu.VMEM)
+    there = pl.BlockSpec(memory_space=pltpu.HBM)
+    return pl.pallas_call(
+        functools.partial(gram_kernel, tile),
         out_shape=(
             jax.ShapeDtypeStruct((width, width), F32),
             jax.ShapeDtypeStruct(tile_mask.shape, F32),
-        ),
-        grid=(columns // (wide * pieces),),
-        in_specs=[
-            pl.BlockSpec((width, wide), lambda i, p=p: (0, i * pieces + p))
-            for p in range(pieces)
-        ]
-        + [tiles, tiles],
-        out_specs=(pl.BlockSpec((width, width), lambda i: (0, 0)), tiles),
-        compiler_params=params(60),
+            pltpu.VMEM((width, columns), BF16),
+            pltpu.VMEM((tile, columns), BF16),
+        ),
+        in_specs=[there, there, here, here],
+        out_specs=(here,) * 4,
+        scratch_shapes=[pltpu.SemaphoreType.DMA((4,)), pltpu.SemaphoreType.DMA((4,))],
+        compiler_params=params(16),
         cost_estimate=cost(1, 1),
         name="gram",
-    )(*[genes] * pieces, tile_mask, tile_counts)
-
-
-def row_tile_specs(row_tiles, tile, wide, place):
-    return [
-        pl.BlockSpec((tile, wide), lambda *ids, r=r: (r, place(*ids)))
-        for r in range(row_tiles)
-    ]
-
-
-def cross_kernel(tile, first, row_tiles, last, meta, factor, *refs):
-    counts, refs = refs[:row_tiles], refs[row_tiles:]
-    genes, refs = refs[0], refs[1:]
-    before, outs, total = (None, refs[:1], refs[1]) if not last else (refs[0], refs[1:3], refs[3])
-    step = pl.program_id(0)
-    gene_tiles = genes.shape[1] // tile
-
-    @pl.when(step == 0)
-    def _():
-        total[...] = jnp.zeros_like(total) if before is None else before[...]
-
-    for row in range(row_tiles):
-        rows = pl.ds(row * tile, tile)
-        part = total[rows, :]
-        for col in range(gene_tiles):
-            at = pl.ds(col * tile, tile)
-            scale = factor[row, (first + step) * gene_tiles + col]
-            part += scale * contract_last(counts[row][:, at], genes[:, at])
-        total[rows, :] = part
-
-    @pl.when(step == pl.num_programs(0) - 1)
-    def _():
-        if not last:
-            outs[0][...] = total[...]
-        else:
-            half = total.shape[0] // 2
-            sub = meta[0]
-            outs[0][...] = total[pl.ds(pl.multiple_of((1 - sub) * half, half), half), :]
-            outs[1][...] = total[pl.ds(pl.multiple_of(sub * half, half), half), :]
-
-
-def cross_part(first, steps, wide, tile, meta, factor, counts, genes, before):
+    )(away(genes), away(counts), tile_mask, tile_counts)
+
+
+def cross_rows(tile, row, factor, counts, genes):
+    gene_tiles = counts.shape[1] // tile
+    at_once = min(4, gene_tiles)
+
+    def body(step, part):
+        for col in range(at_once):
+            place = step * at_once + col
+            at = pl.ds(pl.multiple_of(place * tile, tile), tile)
+            part += factor[row, place] * contract_last(counts[:, at], genes[:, at])
+        return part
+
+    start = jnp.zeros((tile, genes.shape[0]), F32)
+    return lax.fori_loop(0, gene_tiles // at_once, body, start)
+
+
+def cross_early_kernel(tile, factor, head, counts, genes, total, tail, sems):
+    rows = tail.shape[0]
+    copies = row_copies(counts, tail, tile, sems)
+    per_tile = len(copies) // (rows // tile)
+    for copy in copies:
+        copy.start()
+    total[:tile] = cross_rows(tile, 0, factor, head, genes)
+    for row in range(1, rows // tile + 1):
+        for copy in copies[(row - 1) * per_tile : row * per_tile]:
+            copy.wait()
+        if row * tile < rows:
+            at = slice((row - 1) * tile, row * tile)
+            total[row * tile : (row + 1) * tile] = cross_rows(
+                tile, row, factor, tail.at[at], genes
+            )
+
+
+def cross_early(tile, factor, head, counts, genes):
     rows, columns = counts.shape
     width = genes.shape[0]
-    row_tiles = rows // tile
-    last = before is not None
-    whole = lambda n: pl.BlockSpec((n, width), lambda i, m: (0, 0))
-    sizes = (rows // 2, rows // 2) if last else (rows,)
-    return pl.pallas_call(
-        functools.partial(cross_kernel, tile, first, row_tiles, last),
-        out_shape=tuple(jax.ShapeDtypeStruct((n, width), F32) for n in sizes),
-        grid_spec=pltpu.PrefetchScalarGridSpec(
-            num_scalar_prefetch=1,
-            grid=(steps,),
-            in_specs=[pl.BlockSpec(memory_space=pltpu.SMEM)]
-            + row_tile_specs(row_tiles, tile, wide, lambda i, m: first + i)
-            + [pl.BlockSpec((width, wide), lambda i, m: (0, first + i))]
-            + ([whole(rows)] if last else []),
-            out_specs=tuple(whole(n) for n in sizes),
-            scratch_shapes=[pltpu.VMEM((rows, width), F32)],
-        ),
-        compiler_params=params(56),
+    here = pl.BlockSpec(memory_space=pltpu.VMEM)
+    return pl.pallas_call(
+        functools.partial(cross_early_kernel, tile),
+        out_shape=(
+            jax.ShapeDtypeStruct((rows - tile, width), F32),
+            pltpu.VMEM((rows - tile, columns), BF16),
+        ),
+        in_specs=[
+            pl.BlockSpec(memory_space=pltpu.SMEM),
+            here,
+            pl.BlockSpec(memory_space=pltpu.HBM),
+            here,
+        ],
+        out_specs=(here, here),
+        scratch_shapes=[pltpu.SemaphoreType.DMA((4 * (rows // tile - 1),))],
+        compiler_params=params(16),
         cost_estimate=cost(1, 1),
-        name="cross",
-    )(meta, factor, *[counts] * row_tiles, genes, *([before] if last else []))
+        name="cross_early",
+    )(factor, held(head), away(counts), held(genes))
+
+
+def cross_late_kernel(tile, meta, factor, early, tail, genes, theirs, mine):
+    rows = early.shape[0]
+    half = theirs.shape[0]
+    last = cross_rows(tile, rows // tile, factor, tail.at[rows - tile :], genes)
+
+    def put(low, high):
+        low[...] = early[:half]
+        high[: half - tile] = early[half:]
+        high[half - tile :] = last
+
+    @pl.when(meta[0] == 0)
+    def _():
+        put(mine, theirs)
+
+    @pl.when(meta[0] != 0)
+    def _():
+        put(theirs, mine)
+
+
+def cross_late(tile, meta, factor, early, tail, genes):
+    rows, width = early.shape
+    half = jax.ShapeDtypeStruct(((rows + tile) // 2, width), F32)
+    here = pl.BlockSpec(memory_space=pltpu.VMEM)
+    there = pl.BlockSpec(memory_space=pltpu.SMEM)
+    return pl.pallas_call(
+        functools.partial(cross_late_kernel, tile),
+        out_shape=(half, half),
+        in_specs=[there, there, here, here, here],
+        out_specs=(here, here),
+        compiler_params=params(16),
+        cost_estimate=cost(1, 1),
+        name="cross_late",
+    )(meta, factor, early, held(tail), held(genes))
 
 
 def halves(value):
@@ -239,66 +287,60 @@
     )(meta, rho, cross_a, cross_b, inverse, start)
 
 
-def products_kernel(tile, wide, place, row_tiles, meta, factor, *refs):
-    counts, columns, outs = refs[:row_tiles], refs[row_tiles], refs[row_tiles + 1 :]
-    step, order = pl.program_id(0), pl.program_id(1)
-    gene_tile = place(step, order, meta) * wide // tile
-    span = min(tile, wide)
-    for col in range(wide // span):
-        at = pl.ds(col * span, span)
-        total = None
-        for row in range(row_tiles):
-            part = jnp.dot(
-                columns[:, pl.ds(row * tile, tile)],
-                counts[row][:, at],
-                preferred_element_type=F32,
-            )
-            part = factor[row, gene_tile + col] * part
-            total = part if total is None else total + part
-        total = total.astype(BF16)
-        if len(outs) == 1:
-            outs[0][:, at] = total
-        else:
-            outs[0][0, :, at] = total
-
-            @pl.when(order == meta[4])
-            def _(at=at, total=total):
-                outs[1][:, at] = total
-
-
-def products(only_first, cells, start, chunk, tile, meta, factor, counts, columns):
-    rows = counts.shape[0]
+def products_kernel(tile, block, start, chunk, meta, factor, head, tail, columns, *outs):
+    only_first = len(outs) == 1
+    span = min(tile, chunk)
+    wide = 2 * span if chunk % (2 * span) == 0 else span
+    steps = chunk // wide
+    row_tiles = columns.shape[1] // tile
+    blocks = 1 if only_first else outs[0].shape[0]
+
+    @pl.loop(0, blocks * steps)
+    def _(turn):
+        order, step = (0, turn) if only_first else (turn // steps, lax.rem(turn, steps))
+        place = meta[3] if only_first else order
+        first = place * block + start + step * wide
+        for col in range(wide // span):
+            gene = pl.multiple_of(first + col * span, span)
+            total = None
+            for row in range(row_tiles):
+                counts = head if row == 0 else tail.at[(row - 1) * tile : row * tile]
+                part = jnp.dot(
+                    columns[:, row * tile : (row + 1) * tile],
+                    counts[:, pl.ds(gene, span)],
+                    preferred_element_type=F32,
+                )
+                part = factor[row, gene // tile] * part
+                total = part if total is None else total + part
+            total = total.astype(BF16)
+            at = pl.ds(pl.multiple_of(step * wide + col * span, span), span)
+            if only_first:
+                outs[0][:, at] = total
+            else:
+                outs[0][order, :, at] = total
+
+                @pl.when(order == meta[4])
+                def _(at=at, total=total):
+                    outs[1][:, at] = total
+
+
+def products(only_first, cells, start, chunk, tile, meta, factor, head, tail, columns):
     width = columns.shape[0]
-    block = counts.shape[1] // cells
-    blocks = 1 if only_first else cells
-    wide = 2 * tile if chunk % (2 * tile) == 0 else min(tile, chunk)
-    row_tiles = rows // tile
-
-    def place(i, o, m):
-        return (m[3] if only_first else o) * (block // wide) + start // wide + i
-
-    flat = pl.BlockSpec((width, wide), lambda i, o, m: (0, i))
-    operand = jax.ShapeDtypeStruct((width, chunk), BF16)
-    if only_first:
-        out_shape, out_specs = (operand,), (flat,)
-    else:
-        out_shape = (jax.ShapeDtypeStruct((cells, width, chunk), BF16), operand)
-        out_specs = (pl.BlockSpec((1, width, wide), lambda i, o, m: (o, 0, i)), flat)
-    return pl.pallas_call(
-        functools.partial(products_kernel, tile, wide, place, row_tiles),
+    block = head.shape[1] // cells
+    out_shape = (jax.ShapeDtypeStruct((width, chunk), BF16),)
+    if not only_first:
+        out_shape = (jax.ShapeDtypeStruct((cells, width, chunk), BF16),) + out_shape
+    here = pl.BlockSpec(memory_space=pltpu.VMEM)
+    there = pl.BlockSpec(memory_space=pltpu.SMEM)
+    return pl.pallas_call(
+        functools.partial(products_kernel, tile, block, start, chunk),
         out_shape=out_shape,
-        grid_spec=pltpu.PrefetchScalarGridSpec(
-            num_scalar_prefetch=1,
-            grid=(chunk // wide, blocks),
-            in_specs=[pl.BlockSpec(memory_space=pltpu.SMEM)]
-            + row_tile_specs(row_tiles, tile, wide, place)
-            + [pl.BlockSpec((width, rows), lambda i, o, m: (0, 0))],
-            out_specs=out_specs,
-        ),
-        compiler_params=params(50),
+        in_specs=[there, there, here, here, here],
+        out_specs=(here,) * len(out_shape),
+        compiler_params=params(16),
         cost_estimate=cost(1, 1),
         name="products",
-    )(meta, factor, *[counts] * row_tiles, columns)
+    )(meta, factor, held(head), held(tail), columns)
 
 
 def small(kernel, name, out_shape, meta, *args, specs=None):
@@ -312,7 +354,7 @@
             in_specs=specs or [whole(arg.shape) for arg in args],
             out_specs=whole(out_shape.shape),
         ),
-        compiler_params=params(24),
+        compiler_params=params(16),
         cost_estimate=cost(1, 1),
         name=name,
     )(meta, *args)
@@ -387,7 +429,7 @@
             ],
             out_specs=flat(),
         ),
-        compiler_params=params(24),
+        compiler_params=params(16),
         cost_estimate=cost(1, 1),
         name="operand",
     )(meta, total, before)
@@ -418,7 +460,7 @@
             out_specs=pl.BlockSpec((wide, width), lambda i, m: (start // wide + i, 0)),
         ),
         input_output_aliases={4: 0} if extra else {},
-        compiler_params=params(24),
+        compiler_params=params(16),
         cost_estimate=cost(1, 1),
         name="keep",
     )(meta, totals, first, second, *extra)
@@ -519,20 +561,14 @@
     meta = meta + (cell & 1) * table[4]
     meta = jnp.where(is_block & (meta >= cells), meta - cells, meta).astype(jnp.int32)
 
-    gram, factor = gram_part(gene_factor, tile_mask, tile_counts)
-    meta, gram = after(meta, gram)
+    gram, factor, genes_held, head = gram_part(
+        gene_factor, counts, tile, tile_mask, tile_counts
+    )
     gram = pair_sums(gram, "gene", genes)
-    wide = min(1024, columns)
-    steps = columns // wide
-    early = max(steps * 3 // 4, 1)
-    (early_total,) = cross_part(
-        0, early, wide, tile, meta, factor, counts, gene_factor, None
-    )
-    early_total, gram = after(early_total, gram)
+    early, tail = cross_early(tile, factor, head, counts, genes_held)
+    early, gram = after(early, gram)
     gram_other = swap(gram, "sub", subs, 1)
-    theirs, mine = cross_part(
-        early, steps - early, wide, tile, meta, factor, counts, gene_factor, early_total
-    )
+    theirs, mine = cross_late(tile, meta, factor, early, tail, genes_held)
     cross = mine + swap(theirs, "sub", subs, 1)
     cross_a, cross_b = split_sums(cross, "gene", genes)
     inverse, rho = shifted_inverse(gram, gram_other)
@@ -586,7 +622,7 @@
     meta, rows_sum = after(meta, row_share(5, width // (genes * subs), meta, whole))
     for index in every:
         (first,) = products(
-            True, cells, starts[index], chunks[index], tile, meta, factor, counts, whole
+            True, cells, starts[index], chunks[index], tile, meta, factor, head, tail, whole
         )
         meta, first = after(meta, first)
         for parity in (0, 1):
@@ -596,7 +632,7 @@
     totals, seconds = [], []
     for index in every:
         total, second = products(
-            False, cells, starts[index], chunks[index], tile, meta, factor, counts, whole
+            False, cells, starts[index], chunks[index], tile, meta, factor, head, tail, whole
         )
         meta, second = after(meta, second)
         if hops:
@@ -613,7 +649,7 @@
     bits = [1 << i for i in range((genes - 1).bit_length())]
     for phase in range(3, cells):
         for index in every:
-            for parity in (1, 0):
+            for parity in (0, 1):
                 meta = resend(meta, phase, parity, index)
                 if bits:
                     meta, rows_sum = stack_rows(meta, rows_sum, "gene", genes, 6, bits.pop(0))

time: 132 us -> 137 us (1.038)
  the two profiles are of different devices: /device:TPU:12 before, /device:TPU:0 now
where the time goes in v7:
time: 137 us
  Pallas kernels  50.2 us (37%)
  starting transfers between devices  35.7 us (26%)
  waiting for transfers between devices  29.1 us (21%)
  local copies, waits for them, and re-layouts  19.4 us (14%)
    ppermute x10, starting transfers between devices, send(): lax.ppermute(value, 'cell', pairs)  21.6 us
    unnamed x34, local copies, waits for them, and re-layouts  19.4 us
    ppermute x10, waiting for transfers between devices, send(): lax.ppermute(value, 'cell', pairs)  17.3 us
    pallas_call x4, Pallas kernels, products(): pl.pallas_call(functools.partial(products_kernel, tile, block, start, chu...  14.5 us
    ppermute x8, waiting for transfers between devices, swap(): return lax.ppermute(value, axis, [(i, i ^ step) for i in range(size)])  11.8 us
    pallas_call x1, Pallas kernels, cross_early(): pl.pallas_call(functools.partial(cross_early_kernel, tile), out_shape=(ja...  9.27 us
    ppermute x8, starting transfers between devices, swap(): return lax.ppermute(value, axis, [(i, i ^ step) for i in range(size)])  8.67 us
    ppermute x3, starting transfers between devices, hop_rows(): rows_arrived = lax.ppermute(rows_sum, 'cell', pairs)  5.42 us
  transfers between devices with their start and end apart: 21, of which 9 were waited for; matrix products, arithmetic and copies ran while one was open for 1% of the time, Pallas kernels for 27%

profile of v7, /device:TPU:0, one launch (start us, length us, event | category | flops | bytes accessed | tf_op | source)
XLA Modules:
  0.0 136.6 jit_solution(17438198952219078201)
XLA Ops:
  0.6 0.7 copy-done.9
  1.3 0.7 copy-done.10
  2.0 4.5 %gram.1 = (f32[256,256]{1,0:T(8,128)S(1)}, f32[4,32]{1,0:T(4,128)S(1)}, bf16[256,8192]{1,0:T(8,128)(2,1)S(1)}, bf16[256,8192]{1,0:T(8,128)(2,1)S(1)}) custom-call(bf16[256,8192]{1,0:T(8,128)(2,1)} %genes.1, bf16[1024,8192]{1,0:T(8,128)(2,1)} %counts.3, s32[4,32]{1,0:T(4,128)S(1)} %copy-done.9, s32[4,32]{1,0:T(4,128)S(1)} %copy-done.10), custom_call_target="tpu_custom_call" | custom-call | flops 1 | bytes 1 | tf_op jit(solution)/shard_map/gram/pallas_call | solution.py:76
  6.5 3.0 %collective-permute-start = (f32[256,256]{1,0:T(8,128)S(1)}, f32[256,256]{1,0:T(8,128)S(1)}, u32[]{:S(2)}, u32[]{:S(2)}) collective-permute-start(f32[256,256]{1,0:T(8,128)S(1)} %get-tuple-element.60), channel_id=1, source_target_pairs={{0,2},{2,0},{1,3},{3,1},{4,6},{6,4},{5,7},{7,5},{8,10},{10,8},{9,1... | collective-permute-start | bytes 786440 | tf_op jit(solution)/shard_map/ppermute | solution.py:490
  9.5 9.3 %cross_early.1 = (f32[768,256]{1,0:T(8,128)S(1)}, bf16[768,8192]{1,0:T(8,128)(2,1)S(1)}) custom-call(f32[4,32]{1,0:T(4,128)S(1)} %get-tuple-element.56.factor, bf16[256,8192]{1,0:T(8,128)(2,1)S(1)} %get-tuple-element.57.head, bf16[1024,8192]{1,0:T(8,128)(2,1)} %counts.3, bf16[256,8192]{1,0:T(8,128)(2,1)S(1)} %get-tuple-element.58.genes), custom_call_target="tpu_custom_call" | custom-call | flops 1 | bytes 1 | tf_op jit(solution)/shard_map/cross_early/pallas_call | solution.py:129
  18.8 4.5 %copy-done = bf16[768,8192]{1,0:T(8,128)(2,1)} copy-done((bf16[768,8192]{1,0:T(8,128)(2,1)}, bf16[768,8192]{1,0:T(8,128)(2,1)S(1)}, u32[]{:S(2)}) %copy-start) | copy-done | bytes 12582936
  23.5 4.6 %copy-done.1 = bf16[768,8192]{1,0:T(8,128)(2,1)S(1)} copy-done((bf16[768,8192]{1,0:T(8,128)(2,1)S(1)}, bf16[768,8192]{1,0:T(8,128)(2,1)}, u32[]{:S(2)}) %copy-start.1) | copy-done | bytes 12582936
  28.0 2.2 %copy-done.7 = bf16[256,8192]{1,0:T(8,128)(2,1)S(1)} copy-done((bf16[256,8192]{1,0:T(8,128)(2,1)S(1)}, bf16[256,8192]{1,0:T(8,128)(2,1)}, u32[]{:S(2)}) %copy-start.7) | copy-done | bytes 4194328
  30.2 3.5 %cross_late.1 = (f32[512,256]{1,0:T(8,128)S(1)}, f32[512,256]{1,0:T(8,128)S(1)}) custom-call(s32[12]{0:T(128)S(1)} %and_select_fusion.meta, f32[4,32]{1,0:T(4,128)S(1)} %get-tuple-element.56.factor, f32[768,256]{1,0:T(8,128)S(1)} %get-tuple-element.63.early, bf16[768,8192]{1,0:T(8,128)(2,1)S(1)} %copy-done.1, bf16[256,8192]{1,0:T(8,128)(2,1)S(1)} %copy-done.7), custom_call_target="tpu_custom_call" | custom-call | flops 1 | bytes 1 | tf_op jit(solution)/shard_map/cross_late/pallas_call | solution.py:173
  33.7 0.1 collective-permute-start.2
  33.8 0.5 collective-permute-start.1
  34.3 1.4 %collective-permute-done.2 = f32[512,256]{1,0:T(8,128)S(1)} collective-permute-done((f32[512,256]{1,0:T(8,128)S(1)}, f32[512,256]{1,0:T(8,128)S(1)}, u32[]{:S(2)}, u32[]{:S(2)}) %collective-permute-start.2) | collective-permute-done | bytes 524320 | tf_op jit(solution)/shard_map/ppermute | solution.py:490
  35.8 1.7 %collective-permute-start.3 = (f32[256,256]{1,0:T(8,128)S(1)}, f32[256,256]{1,0:T(8,128)S(1)}, u32[]{:S(2)}, u32[]{:S(2)}) collective-permute-start(f32[256,256]{1,0:T(8,128)S(1)} %get-tuple-element.109), channel_id=1, source_target_pairs={{0,2},{2,0},{1,3},{3,1},{4,6},{6,4},{5,7},{7,5},{8,10},{10,8},{9,1... | collective-permute-start | bytes 786440 | tf_op jit(solution)/shard_map/ppermute | solution.py:490
  37.5 3.5 %inverse.1 = (f32[256,256]{1,0:T(8,128)S(1)}, f32[1,1]{1,0:T(1,128)}) custom-call(f32[256,256]{1,0:T(8,128)S(1)} %add.23.gram_a, f32[256,256]{1,0:T(8,128)S(1)} %collective-permute-done.1.gram_b), custom_call_target="tpu_custom_call" | custom-call | flops 2013265920 | bytes 786432 | tf_op jit(solution)/shard_map/inverse/pallas_call | solution.py:239
  41.0 3.2 %collective-permute-done.3.cross_b = f32[256,256]{1,0:T(8,128)S(1)} collective-permute-done((f32[256,256]{1,0:T(8,128)S(1)}, f32[256,256]{1,0:T(8,128)S(1)}, u32[]{:S(2)}, u32[]{:S(2)}) %collective-permute-start.3) | collective-permute-done | bytes 262176 | tf_op jit(solution)/shard_map/ppermute | solution.py:490
  44.2 2.1 %admm.1 = bf16[256,256]{1,0:T(8,128)(2,1)S(1)} custom-call(s32[12]{0:T(128)S(1)} %and_select_fusion.meta, f32[1,1]{1,0:T(1,128)} %get-tuple-element.62.rho_ref, f32[256,256]{1,0:T(8,128)S(1)} %get-tuple-element.110.cross_a, f32[256,256]{1,0:T(8,128)S(1)} %collective-permute-done.3.cross_b, f32[256,256]{1,0:T(8,128)S(1)} %get-tuple-element.67.inverse, ...), custom_call_target="tpu_custom_call" | custom-call | flops 301989888 | bytes 786432 | tf_op jit(solution)/shard_map/admm/pallas_call | solution.py:269
  46.3 1.7 %collective-permute-start.4 = (bf16[256,256]{1,0:T(8,128)(2,1)S(1)}, bf16[256,256]{1,0:T(8,128)(2,1)S(1)}, u32[]{:S(2)}, u32[]{:S(2)}) collective-permute-start(bf16[256,256]{1,0:T(8,128)(2,1)S(1)} %admm.1), channel_id=1, source_target_pairs={{0,2},{2,0},{1,3},{3,1},{4,6},{6,4},{5,7},{7,5},{8,10},{10,8},{9,1... | collective-permute-start | bytes 393224 | tf_op jit(solution)/shard_map/ppermute | solution.py:490
  48.0 3.4 %collective-permute-done.4 = bf16[256,256]{1,0:T(8,128)(2,1)S(1)} collective-permute-done((bf16[256,256]{1,0:T(8,128)(2,1)S(1)}, bf16[256,256]{1,0:T(8,128)(2,1)S(1)}, u32[]{:S(2)}, u32[]{:S(2)}) %collective-permute-start.4) | collective-permute-done | bytes 131104 | tf_op jit(solution)/shard_map/ppermute | solution.py:490
  51.3 0.1 maximum_select_fusion.1
  51.5 0.1 collective-permute-start.5
  51.6 1.5 %collective-permute-done.5 = bf16[256,512]{1,0:T(8,128)(2,1)S(1)} collective-permute-done((bf16[256,512]{1,0:T(8,128)(2,1)S(1)}, bf16[256,512]{1,0:T(8,128)(2,1)S(1)}, u32[]{:S(2)}, u32[]{:S(2)}) %collective-permute-start.5) | collective-permute-done | bytes 262176 | tf_op jit(solution)/shard_map/ppermute | solution.py:490
  53.1 0.1 maximum_select_fusion.share.columns.value
  53.2 0.8 row_share.1.held
  54.0 3.5 %collective-permute-start.6 = (bf16[64,256]{1,0:T(8,128)(2,1)S(1)}, bf16[64,256]{1,0:T(8,128)(2,1)S(1)}, u32[]{:S(2)}, u32[]{:S(2)}) collective-permute-start(bf16[64,256]{1,0:T(8,128)(2,1)S(1)} %row_share.1.held), channel_id=1, source_target_pairs={{0,4},{12,8},{1,5},{13,9},{2,6},{14,10},{3,7},{15,11},{16,20},{28,... | collective-permute-start | bytes 98312 | tf_op jit(solution)/shard_map/ppermute | solution.py:614
  57.5 4.6 %copy-done.2 = bf16[768,8192]{1,0:T(8,128)(2,1)S(1)} copy-done((bf16[768,8192]{1,0:T(8,128)(2,1)S(1)}, bf16[768,8192]{1,0:T(8,128)(2,1)}, u32[]{:S(2)}) %copy-start.2) | copy-done | bytes 12582936
  62.1 2.2 %copy-done.4 = bf16[256,8192]{1,0:T(8,128)(2,1)S(1)} copy-done((bf16[256,8192]{1,0:T(8,128)(2,1)S(1)}, bf16[256,8192]{1,0:T(8,128)(2,1)}, u32[]{:S(2)}) %copy-start.4) | copy-done | bytes 4194328
  64.3 1.5 %products.4 = bf16[256,1024]{1,0:T(8,128)(2,1)S(1)} custom-call(s32[12]{0:T(128)S(1)} %and_select_fusion.meta, f32[4,32]{1,0:T(4,128)S(1)} %get-tuple-element.56.factor, bf16[256,8192]{1,0:T(8,128)(2,1)S(1)} %copy-done.4, bf16[768,8192]{1,0:T(8,128)(2,1)S(1)} %copy-done.2, bf16[256,1024]{1,0:T(8,128)(2,1)S(1)} %maximum_select_fusion.share.columns.value), custom_call_target="tpu_custom_call" | custom-call | flops 1 | bytes 1 | tf_op jit(solution)/shard_map/products/pallas_call | solution.py:335
  65.8 1.3 collective-permute-start.8
  67.1 0.6 hop.3.held
  67.7 1.5 %products.5 = bf16[256,1024]{1,0:T(8,128)(2,1)S(1)} custom-call(s32[12]{0:T(128)S(1)} %and_select_fusion.meta, f32[4,32]{1,0:T(4,128)S(1)} %get-tuple-element.56.factor, bf16[256,8192]{1,0:T(8,128)(2,1)S(1)} %copy-done.5, bf16[768,8192]{1,0:T(8,128)(2,1)S(1)} %copy-done.2, bf16[256,1024]{1,0:T(8,128)(2,1)S(1)} %maximum_select_fusion.share.columns.value), custom_call_target="tpu_custom_call" | custom-call | flops 1 | bytes 1 | tf_op jit(solution)/shard_map/products/pallas_call | solution.py:335
  69.2 1.3 collective-permute-start.10
  70.5 0.7 collective-permute-start.7
  71.2 5.7 %products.6 = (bf16[4,256,1024]{2,1,0:T(8,128)(2,1)S(1)}, bf16[256,1024]{1,0:T(8,128)(2,1)S(1)}) custom-call(s32[12]{0:T(128)S(1)} %and_select_fusion.meta, f32[4,32]{1,0:T(4,128)S(1)} %get-tuple-element.56.factor, bf16[256,8192]{1,0:T(8,128)(2,1)S(1)} %copy-done.5, bf16[768,8192]{1,0:T(8,128)(2,1)S(1)} %copy-done.2, ...), custom_call_target="tpu_custom_call" | custom-call | flops 1 | bytes 1 | tf_op jit(solution)/shard_map/products/pallas_call | solution.py:335
  77.0 0.6 hop.4.held
  77.5 1.3 collective-permute-start.9
  78.8 0.5 collective-permute-done.8.before
  79.3 0.7 operand.6
  80.0 0.7 collective-permute-start.12
  80.7 7.2 %collective-permute-start.14 = (bf16[256,1024]{1,0:T(8,128)(2,1)S(1)}, bf16[256,1024]{1,0:T(8,128)(2,1)S(1)}, u32[]{:S(2)}, u32[]{:S(2)}) collective-permute-start(bf16[256,1024]{1,0:T(8,128)(2,1)S(1)} %get-tuple-element.96), channel_id=1, source_target_pairs={{0,4},{12,8},{1,5},{13,9},{2,6},{14,10},{3,7},{15,11},{16,20},{28,... | collective-permute-start | bytes 1572872 | tf_op jit(solution)/shard_map/ppermute | solution.py:593
  87.9 5.7 %products.7 = (bf16[4,256,1024]{2,1,0:T(8,128)(2,1)S(1)}, bf16[256,1024]{1,0:T(8,128)(2,1)S(1)}) custom-call(s32[12]{0:T(128)S(1)} %and_select_fusion.meta, f32[4,32]{1,0:T(4,128)S(1)} %get-tuple-element.56.factor, bf16[256,8192]{1,0:T(8,128)(2,1)S(1)} %copy-done.5, bf16[768,8192]{1,0:T(8,128)(2,1)S(1)} %copy-done.2, ...), custom_call_target="tpu_custom_call" | custom-call | flops 1 | bytes 1 | tf_op jit(solution)/shard_map/products/pallas_call | solution.py:335
  93.7 0.6 hop.5.mine
  94.2 0.7 operand.7
  94.9 0.7 collective-permute-start.15
  95.6 3.5 %collective-permute-start.16 = (bf16[256,1024]{1,0:T(8,128)(2,1)S(1)}, bf16[256,1024]{1,0:T(8,128)(2,1)S(1)}, u32[]{:S(2)}, u32[]{:S(2)}) collective-permute-start(bf16[256,1024]{1,0:T(8,128)(2,1)S(1)} %get-tuple-element.100), channel_id=1, source_target_pairs={{0,4},{12,8},{1,5},{13,9},{2,6},{14,10},{3,7},{15,11},{16,20},{28,... | collective-permute-start | bytes 1572872 | tf_op jit(solution)/shard_map/ppermute | solution.py:593
  99.2 0.1 collective-permute-start.11
  99.2 1.5 %turn.1 = bf16[1024,256]{1,0:T(8,128)(2,1)} custom-call(s32[12]{0:T(128)S(1)} %and_select_fusion.meta, bf16[256,1024]{1,0:T(8,128)(2,1)S(1)} %maximum_select_fusion.share.columns.value), custom_call_target="tpu_custom_call" | custom-call | flops 1 | bytes 1 | tf_op jit(solution)/shard_map/turn/pallas_call | solution.py:348
  100.8 0.5 stack.2.mine
  101.3 1.6 %collective-permute-start.13 = (bf16[128,256]{1,0:T(8,128)(2,1)S(1)}, bf16[128,256]{1,0:T(8,128)(2,1)S(1)}, u32[]{:S(2)}, u32[]{:S(2)}) collective-permute-start(bf16[128,256]{1,0:T(8,128)(2,1)S(1)} %stack.2.mine), channel_id=1, source_target_pairs={{0,2},{2,0},{1,3},{3,1},{4,6},{6,4},{5,7},{7,5},{8,10},{10,8},{9,1... | collective-permute-start | bytes 196616 | tf_op jit(solution)/shard_map/ppermute | solution.py:490
  103.0 0.7 operand.8
  103.6 2.3 %collective-permute-done.13.theirs = bf16[128,256]{1,0:T(8,128)(2,1)S(1)} collective-permute-done((bf16[128,256]{1,0:T(8,128)(2,1)S(1)}, bf16[128,256]{1,0:T(8,128)(2,1)S(1)}, u32[]{:S(2)}, u32[]{:S(2)}) %collective-permute-start.13) | collective-permute-done | bytes 65568 | tf_op jit(solution)/shard_map/ppermute | solution.py:490
  105.9 0.6 stack.3
  106.5 0.1 collective-permute-start.17
  106.5 0.7 operand.9
  107.2 0.7 collective-permute-start.18
  107.9 0.7 operand.10
  108.6 4.4 %collective-permute-done.16.before = bf16[256,1024]{1,0:T(8,128)(2,1)S(1)} collective-permute-done((bf16[256,1024]{1,0:T(8,128)(2,1)S(1)}, bf16[256,1024]{1,0:T(8,128)(2,1)S(1)}, u32[]{:S(2)}, u32[]{:S(2)}) %collective-permute-start.16) | collective-permute-done | bytes 524320 | tf_op jit(solution)/shard_map/ppermute | solution.py:593
  113.1 0.7 operand.11
  113.7 0.7 collective-permute-start.20
  114.4 5.3 %collective-permute-start.19 = (bf16[256,1024]{1,0:T(8,128)(2,1)S(1)}, bf16[256,1024]{1,0:T(8,128)(2,1)S(1)}, u32[]{:S(2)}, u32[]{:S(2)}) collective-permute-start(bf16[256,1024]{1,0:T(8,128)(2,1)S(1)} %operand.10), channel_id=1, source_target_pairs={{0,4},{8,12},{4,0},{12,8},{1,5},{9,13},{5,1},{13,9},{2,6},{10,14},... | collective-permute-start | bytes 1572872 | tf_op jit(solution)/shard_map/ppermute | solution.py:593
  119.8 0.7 convert_element_type.3
  120.5 3.8 %collective-permute-done.17.first = bf16[256,1024]{1,0:T(8,128)(2,1)S(1)} collective-permute-done((bf16[256,1024]{1,0:T(8,128)(2,1)S(1)}, bf16[256,1024]{1,0:T(8,128)(2,1)S(1)}, u32[]{:S(2)}, u32[]{:S(2)}) %collective-permute-start.17) | collective-permute-done | bytes 524320 | tf_op jit(solution)/shard_map/ppermute | solution.py:593
  124.3 1.9 %keep.2.refs_0_ = f32[2048,256]{1,0:T(8,128)} custom-call(s32[12]{0:T(128)S(1)} %and_select_fusion.meta, bf16[4,256,1024]{2,1,0:T(8,128)(2,1)S(1)} %get-tuple-element.77.total, bf16[256,1024]{1,0:T(8,128)(2,1)S(1)} %collective-permute-done.17.first, bf16[256,1024]{1,0:T(8,128)(2,1)S(1)} %collective-permute-done.18.second), custom_call_target="tpu_custom_call" | custom-call | flops 1 | bytes 1 | tf_op jit(solution)/shard_map/keep/pallas_call | solution.py:448
  126.2 8.5 %collective-permute-done.19.first = bf16[256,1024]{1,0:T(8,128)(2,1)S(1)} collective-permute-done((bf16[256,1024]{1,0:T(8,128)(2,1)S(1)}, bf16[256,1024]{1,0:T(8,128)(2,1)S(1)}, u32[]{:S(2)}, u32[]{:S(2)}) %collective-permute-start.19) | collective-permute-done | bytes 524320 | tf_op jit(solution)/shard_map/ppermute | solution.py:593
  134.7 1.9 %keep.3 = f32[2048,256]{1,0:T(8,128)} custom-call(s32[12]{0:T(128)S(1)} %and_select_fusion.meta, bf16[4,256,1024]{2,1,0:T(8,128)(2,1)S(1)} %get-tuple-element.84.total, bf16[256,1024]{1,0:T(8,128)(2,1)S(1)} %collective-permute-done.19.first, bf16[256,1024]{1,0:T(8,128)(2,1)S(1)} %collective-permute-done.20.second, ...), custom_call_target="tpu_custom_call", output_to_operand_aliasing={{}: (4, {})} | custom-call | flops 1 | bytes 1 | tf_op jit(solution)/shard_map/keep/pallas_call | solution.py:448
  (43 shorter events, 0.2 us)
Async XLA Ops:
  0.6 0.7 copy-start.9
  1.3 0.7 copy-start.10
  6.5 12.3 %copy-start.3 = (bf16[256,8192]{1,0:T(8,128)(2,1)}, bf16[256,8192]{1,0:T(8,128)(2,1)S(1)}, u32[]{:S(2)}) copy-start(bf16[256,8192]{1,0:T(8,128)(2,1)S(1)} %get-tuple-element.57.head) | copy-start | bytes 12582916
  6.5 12.3 %copy-start.6 = (bf16[256,8192]{1,0:T(8,128)(2,1)}, bf16[256,8192]{1,0:T(8,128)(2,1)S(1)}, u32[]{:S(2)}) copy-start(bf16[256,8192]{1,0:T(8,128)(2,1)S(1)} %get-tuple-element.58.genes) | copy-start | bytes 12582916
  6.5 16.9 %collective-permute-start = (f32[256,256]{1,0:T(8,128)S(1)}, f32[256,256]{1,0:T(8,128)S(1)}, u32[]{:S(2)}, u32[]{:S(2)}) collective-permute-start(f32[256,256]{1,0:T(8,128)S(1)} %get-tuple-element.60), channel_id=1, source_target_pairs={{0,2},{2,0},{1,3},{3,1},{4,6},{6,4},{5,7},{7,5},{8,10},{10,8},{9,1... | collective-permute-start | bytes 786440 | tf_op jit(solution)/shard_map/ppermute | solution.py:490
  9.5 13.9 %copy-start.11 = (pred[12]{0:T(512)(128)(4,1)S(1)}, pred[12]{0:T(512)(128)(4,1)}, u32[]{:S(2)}) copy-start(pred[12]{0:T(512)(128)(4,1)} %constant.36.clone) | copy-start | bytes 40
  9.5 13.9 %copy-start.12 = (s32[12]{0:T(128)S(1)}, s32[12]{0:T(128)}, u32[]{:S(2)}) copy-start(s32[12]{0:T(128)} %constant.35.clone) | copy-start | bytes 148
  9.5 13.9 %copy-start.13 = (s32[12]{0:T(128)S(1)}, s32[12]{0:T(128)}, u32[]{:S(2)}) copy-start(s32[12]{0:T(128)} %constant.34.clone) | copy-start | bytes 148
  9.5 13.9 %copy-start.14 = (s32[12]{0:T(128)S(1)}, s32[12]{0:T(128)}, u32[]{:S(2)}) copy-start(s32[12]{0:T(128)} %constant.33.clone) | copy-start | bytes 148
  9.5 13.9 %copy-start.15 = (s32[12]{0:T(128)S(1)}, s32[12]{0:T(128)}, u32[]{:S(2)}) copy-start(s32[12]{0:T(128)} %constant.32.clone) | copy-start | bytes 148
  9.5 13.9 %copy-start.16 = (s32[12]{0:T(128)S(1)}, s32[12]{0:T(128)}, u32[]{:S(2)}) copy-start(s32[12]{0:T(128)} %constant.31.clone) | copy-start | bytes 148
  18.8 4.5 %copy-start = (bf16[768,8192]{1,0:T(8,128)(2,1)}, bf16[768,8192]{1,0:T(8,128)(2,1)S(1)}, u32[]{:S(2)}) copy-start(bf16[768,8192]{1,0:T(8,128)(2,1)S(1)} %get-tuple-element.64.tail) | copy-start | bytes 37748740
  23.5 4.6 %copy-start.1 = (bf16[768,8192]{1,0:T(8,128)(2,1)S(1)}, bf16[768,8192]{1,0:T(8,128)(2,1)}, u32[]{:S(2)}) copy-start(bf16[768,8192]{1,0:T(8,128)(2,1)} %copy-done) | copy-start | bytes 37748740
  28.0 2.2 %copy-start.7 = (bf16[256,8192]{1,0:T(8,128)(2,1)S(1)}, bf16[256,8192]{1,0:T(8,128)(2,1)}, u32[]{:S(2)}) copy-start(bf16[256,8192]{1,0:T(8,128)(2,1)} %copy-done.6) | copy-start | bytes 12582916
  33.7 2.0 %collective-permute-start.2 = (f32[512,256]{1,0:T(8,128)S(1)}, f32[512,256]{1,0:T(8,128)S(1)}, u32[]{:S(2)}, u32[]{:S(2)}) collective-permute-start(f32[512,256]{1,0:T(8,128)S(1)} %get-tuple-element.66), channel_id=1, source_target_pairs={{0,1},{1,0},{2,3},{3,2},{4,5},{5,4},{6,7},{7,6},{8,9},{9,8},{10,11... | collective-permute-start | bytes 1572872 | tf_op jit(solution)/shard_map/ppermute | solution.py:490
  33.8 3.7 %collective-permute-start.1 = (f32[256,256]{1,0:T(8,128)S(1)}, f32[256,256]{1,0:T(8,128)S(1)}, u32[]{:S(2)}, u32[]{:S(2)}) collective-permute-start(f32[256,256]{1,0:T(8,128)S(1)} %add.23.gram_a), channel_id=1, source_target_pairs={{0,1},{1,0},{2,3},{3,2},{4,5},{5,4},{6,7},{7,6},{8,9},{9,8},{10,11... | collective-permute-start | bytes 786440 | tf_op jit(solution)/shard_map/ppermute | solution.py:490
  35.8 8.5 %copy-start.8 = (bf16[1024,256]{1,0:T(8,128)(2,1)S(1)}, bf16[1024,256]{1,0:T(8,128)(2,1)}, u32[]{:S(2)}) copy-start(bf16[1024,256]{1,0:T(8,128)(2,1)} %start.1) | copy-start | bytes 1572868
  35.8 8.4 %collective-permute-start.3 = (f32[256,256]{1,0:T(8,128)S(1)}, f32[256,256]{1,0:T(8,128)S(1)}, u32[]{:S(2)}, u32[]{:S(2)}) collective-permute-start(f32[256,256]{1,0:T(8,128)S(1)} %get-tuple-element.109), channel_id=1, source_target_pairs={{0,2},{2,0},{1,3},{3,1},{4,6},{6,4},{5,7},{7,5},{8,10},{10,8},{9,1... | collective-permute-start | bytes 786440 | tf_op jit(solution)/shard_map/ppermute | solution.py:490
  46.3 5.0 %collective-permute-start.4 = (bf16[256,256]{1,0:T(8,128)(2,1)S(1)}, bf16[256,256]{1,0:T(8,128)(2,1)S(1)}, u32[]{:S(2)}, u32[]{:S(2)}) collective-permute-start(bf16[256,256]{1,0:T(8,128)(2,1)S(1)} %admm.1), channel_id=1, source_target_pairs={{0,2},{2,0},{1,3},{3,1},{4,6},{6,4},{5,7},{7,5},{8,10},{10,8},{9,1... | collective-permute-start | bytes 393224 | tf_op jit(solution)/shard_map/ppermute | solution.py:490
  51.5 1.6 %collective-permute-start.5 = (bf16[256,512]{1,0:T(8,128)(2,1)S(1)}, bf16[256,512]{1,0:T(8,128)(2,1)S(1)}, u32[]{:S(2)}, u32[]{:S(2)}) collective-permute-start(bf16[256,512]{1,0:T(8,128)(2,1)S(1)} %maximum_select_fusion.1), channel_id=1, source_target_pairs={{0,1},{1,0},{2,3},{3,2},{4,5},{5,4},{6,7},{7,6},{8,9},{9,8},{10,11... | collective-permute-start | bytes 786440 | tf_op jit(solution)/shard_map/ppermute | solution.py:490
  54.0 13.1 %collective-permute-start.6 = (bf16[64,256]{1,0:T(8,128)(2,1)S(1)}, bf16[64,256]{1,0:T(8,128)(2,1)S(1)}, u32[]{:S(2)}, u32[]{:S(2)}) collective-permute-start(bf16[64,256]{1,0:T(8,128)(2,1)S(1)} %row_share.1.held), channel_id=1, source_target_pairs={{0,4},{12,8},{1,5},{13,9},{2,6},{14,10},{3,7},{15,11},{16,20},{28,... | collective-permute-start | bytes 98312 | tf_op jit(solution)/shard_map/ppermute | solution.py:614
  57.5 4.6 %copy-start.2 = (bf16[768,8192]{1,0:T(8,128)(2,1)S(1)}, bf16[768,8192]{1,0:T(8,128)(2,1)}, u32[]{:S(2)}) copy-start(bf16[768,8192]{1,0:T(8,128)(2,1)} %copy-done) | copy-start | bytes 37748740
  62.1 2.2 %copy-start.4 = (bf16[256,8192]{1,0:T(8,128)(2,1)S(1)}, bf16[256,8192]{1,0:T(8,128)(2,1)}, u32[]{:S(2)}) copy-start(bf16[256,8192]{1,0:T(8,128)(2,1)} %copy-done.3) | copy-start | bytes 12582916
  64.3 3.4 %copy-start.5 = (bf16[256,8192]{1,0:T(8,128)(2,1)S(1)}, bf16[256,8192]{1,0:T(8,128)(2,1)}, u32[]{:S(2)}) copy-start(bf16[256,8192]{1,0:T(8,128)(2,1)} %copy-done.3) | copy-start | bytes 12582916
  65.8 13.6 %collective-permute-start.8 = (bf16[256,1024]{1,0:T(8,128)(2,1)S(1)}, bf16[256,1024]{1,0:T(8,128)(2,1)S(1)}, u32[]{:S(2)}, u32[]{:S(2)}) collective-permute-start(bf16[256,1024]{1,0:T(8,128)(2,1)S(1)} %products.4), channel_id=1, source_target_pairs={{0,4},{12,8},{1,5},{13,9},{2,6},{14,10},{3,7},{15,11},{16,20},{28,... | collective-permute-start | bytes 1572872 | tf_op jit(solution)/shard_map/ppermute | solution.py:593
  69.2 25.0 %collective-permute-start.10 = (bf16[256,1024]{1,0:T(8,128)(2,1)S(1)}, bf16[256,1024]{1,0:T(8,128)(2,1)S(1)}, u32[]{:S(2)}, u32[]{:S(2)}) collective-permute-start(bf16[256,1024]{1,0:T(8,128)(2,1)S(1)} %products.5), channel_id=1, source_target_pairs={{0,4},{12,8},{1,5},{13,9},{2,6},{14,10},{3,7},{15,11},{16,20},{28,... | collective-permute-start | bytes 1572872 | tf_op jit(solution)/shard_map/ppermute | solution.py:593
  70.5 6.4 %collective-permute-start.7 = (bf16[64,256]{1,0:T(8,128)(2,1)S(1)}, bf16[64,256]{1,0:T(8,128)(2,1)S(1)}, u32[]{:S(2)}, u32[]{:S(2)}) collective-permute-start(bf16[64,256]{1,0:T(8,128)(2,1)S(1)} %hop.3.held), channel_id=1, source_target_pairs={{4,8},{8,4},{5,9},{9,5},{6,10},{10,6},{7,11},{11,7},{20,24},{24,20... | collective-permute-start | bytes 98312 | tf_op jit(solution)/shard_map/ppermute | solution.py:614
  77.5 16.1 %collective-permute-start.9 = (bf16[64,256]{1,0:T(8,128)(2,1)S(1)}, bf16[64,256]{1,0:T(8,128)(2,1)S(1)}, u32[]{:S(2)}, u32[]{:S(2)}) collective-permute-start(bf16[64,256]{1,0:T(8,128)(2,1)S(1)} %hop.4.held), channel_id=1, source_target_pairs={{4,0},{8,12},{5,1},{9,13},{6,2},{10,14},{7,3},{11,15},{20,16},{24,... | collective-permute-start | bytes 98312 | tf_op jit(solution)/shard_map/ppermute | solution.py:614
  80.0 23.0 %collective-permute-start.12 = (bf16[256,1024]{1,0:T(8,128)(2,1)S(1)}, bf16[256,1024]{1,0:T(8,128)(2,1)S(1)}, u32[]{:S(2)}, u32[]{:S(2)}) collective-permute-start(bf16[256,1024]{1,0:T(8,128)(2,1)S(1)} %operand.6), channel_id=1, source_target_pairs={{4,8},{8,4},{5,9},{9,5},{6,10},{10,6},{7,11},{11,7},{20,24},{24,20... | collective-permute-start | bytes 1572872 | tf_op jit(solution)/shard_map/ppermute | solution.py:593
  80.7 25.8 %collective-permute-start.14 = (bf16[256,1024]{1,0:T(8,128)(2,1)S(1)}, bf16[256,1024]{1,0:T(8,128)(2,1)S(1)}, u32[]{:S(2)}, u32[]{:S(2)}) collective-permute-start(bf16[256,1024]{1,0:T(8,128)(2,1)S(1)} %get-tuple-element.96), channel_id=1, source_target_pairs={{0,4},{12,8},{1,5},{13,9},{2,6},{14,10},{3,7},{15,11},{16,20},{28,... | collective-permute-start | bytes 1572872 | tf_op jit(solution)/shard_map/ppermute | solution.py:593
  94.9 13.0 %collective-permute-start.15 = (bf16[256,1024]{1,0:T(8,128)(2,1)S(1)}, bf16[256,1024]{1,0:T(8,128)(2,1)S(1)}, u32[]{:S(2)}, u32[]{:S(2)}) collective-permute-start(bf16[256,1024]{1,0:T(8,128)(2,1)S(1)} %operand.7), channel_id=1, source_target_pairs={{4,8},{8,4},{5,9},{9,5},{6,10},{10,6},{7,11},{11,7},{20,24},{24,20... | collective-permute-start | bytes 1572872 | tf_op jit(solution)/shard_map/ppermute | solution.py:593
  95.6 17.4 %collective-permute-start.16 = (bf16[256,1024]{1,0:T(8,128)(2,1)S(1)}, bf16[256,1024]{1,0:T(8,128)(2,1)S(1)}, u32[]{:S(2)}, u32[]{:S(2)}) collective-permute-start(bf16[256,1024]{1,0:T(8,128)(2,1)S(1)} %get-tuple-element.100), channel_id=1, source_target_pairs={{0,4},{12,8},{1,5},{13,9},{2,6},{14,10},{3,7},{15,11},{16,20},{28,... | collective-permute-start | bytes 1572872 | tf_op jit(solution)/shard_map/ppermute | solution.py:593
  99.2 1.6 %collective-permute-start.11 = (bf16[64,256]{1,0:T(8,128)(2,1)S(1)}, bf16[64,256]{1,0:T(8,128)(2,1)S(1)}, u32[]{:S(2)}, u32[]{:S(2)}) collective-permute-start(bf16[64,256]{1,0:T(8,128)(2,1)S(1)} %hop.5.mine), channel_id=1, source_target_pairs={{0,1},{1,0},{2,3},{3,2},{4,5},{5,4},{6,7},{7,6},{8,9},{9,8},{10,11... | collective-permute-start | bytes 98312 | tf_op jit(solution)/shard_map/ppermute | solution.py:490
  101.3 4.6 %collective-permute-start.13 = (bf16[128,256]{1,0:T(8,128)(2,1)S(1)}, bf16[128,256]{1,0:T(8,128)(2,1)S(1)}, u32[]{:S(2)}, u32[]{:S(2)}) collective-permute-start(bf16[128,256]{1,0:T(8,128)(2,1)S(1)} %stack.2.mine), channel_id=1, source_target_pairs={{0,2},{2,0},{1,3},{3,1},{4,6},{6,4},{5,7},{7,5},{8,10},{10,8},{9,1... | collective-permute-start | bytes 196616 | tf_op jit(solution)/shard_map/ppermute | solution.py:490
  106.5 17.8 %collective-permute-start.17 = (bf16[256,1024]{1,0:T(8,128)(2,1)S(1)}, bf16[256,1024]{1,0:T(8,128)(2,1)S(1)}, u32[]{:S(2)}, u32[]{:S(2)}) collective-permute-start(bf16[256,1024]{1,0:T(8,128)(2,1)S(1)} %operand.8), channel_id=1, source_target_pairs={{0,4},{8,12},{4,0},{12,8},{1,5},{9,13},{5,1},{13,9},{2,6},{10,14},... | collective-permute-start | bytes 1572872 | tf_op jit(solution)/shard_map/ppermute | solution.py:593
  107.2 17.1 %collective-permute-start.18 = (bf16[256,1024]{1,0:T(8,128)(2,1)S(1)}, bf16[256,1024]{1,0:T(8,128)(2,1)S(1)}, u32[]{:S(2)}, u32[]{:S(2)}) collective-permute-start(bf16[256,1024]{1,0:T(8,128)(2,1)S(1)} %operand.9), channel_id=1, source_target_pairs={{4,8},{8,4},{5,9},{9,5},{6,10},{10,6},{7,11},{11,7},{20,24},{24,20... | collective-permute-start | bytes 1572872 | tf_op jit(solution)/shard_map/ppermute | solution.py:593
  113.7 12.5 %collective-permute-start.20 = (bf16[256,1024]{1,0:T(8,128)(2,1)S(1)}, bf16[256,1024]{1,0:T(8,128)(2,1)S(1)}, u32[]{:S(2)}, u32[]{:S(2)}) collective-permute-start(bf16[256,1024]{1,0:T(8,128)(2,1)S(1)} %operand.11), channel_id=1, source_target_pairs={{4,8},{8,4},{5,9},{9,5},{6,10},{10,6},{7,11},{11,7},{20,24},{24,20... | collective-permute-start | bytes 1572872 | tf_op jit(solution)/shard_map/ppermute | solution.py:593
  114.4 20.3 %collective-permute-start.19 = (bf16[256,1024]{1,0:T(8,128)(2,1)S(1)}, bf16[256,1024]{1,0:T(8,128)(2,1)S(1)}, u32[]{:S(2)}, u32[]{:S(2)}) collective-permute-start(bf16[256,1024]{1,0:T(8,128)(2,1)S(1)} %operand.10), channel_id=1, source_target_pairs={{0,4},{8,12},{4,0},{12,8},{1,5},{9,13},{5,1},{13,9},{2,6},{10,14},... | collective-permute-start | bytes 1572872 | tf_op jit(solution)/shard_map/ppermute | solution.py:593

commit v8 on v0

v8 whole, which is shorter than its diff:
```python
import functools

import jax
import jax.numpy as jnp
import numpy as np
from jax import lax
from jax.experimental import pallas as pl
from jax.experimental.pallas import tpu as pltpu
from jax.sharding import PartitionSpec as P

ITERS = 3
F32 = jnp.float32
BF16 = jnp.bfloat16
MIB = 1024 * 1024


def params(limit=16):
    return pltpu.CompilerParams(vmem_limit_bytes=limit * MIB)


def away(value):
    return pltpu.with_memory_space_constraint(value, pltpu.HBM)


def held(value):
    return pltpu.with_memory_space_constraint(value, pltpu.VMEM)


def cost(flops, bytes_accessed):
    return pl.CostEstimate(flops=flops, bytes_accessed=bytes_accessed, transcendentals=0)


def contract_last(left, right):
    return lax.dot_general(
        left, right, (((1,), (1,)), ((), ())), preferred_element_type=F32
    )


def row_copies(source, target, first, sems):
    rows = target.shape[0]
    piece = max(rows // sems.shape[0], 16)
    return [
        pltpu.make_async_copy(
            source.at[pl.ds(first + i * piece, piece)],
            target.at[pl.ds(i * piece, piece)],
            sems.at[i],
        )
        for i in range(rows // piece)
    ]


def load_kernel(
    tile, genes, counts, tile_mask, tile_counts,
    gram, factor, theirs, mine, genes_held, counts_held,
    mask_here, counts_here, mask_scalars, counts_scalars, gene_sems, row_sems, small_sems,
):
    small = [(tile_mask, mask_here), (tile_counts, counts_here)]
    small += [(tile_mask, mask_scalars), (tile_counts, counts_scalars)]
    small_copies = [
        pltpu.make_async_copy(source, target, small_sems.at[i])
        for i, (source, target) in enumerate(small)
    ]
    gene_copies = row_copies(genes, genes_held, 0, gene_sems)
    row_starts = row_copies(counts, counts_held, 0, row_sems)
    for copy in small_copies + gene_copies + row_starts:
        copy.start()
    for copy in small_copies:
        copy.wait()
    factor[...] = mask_here[...].astype(F32) / counts_here[...].astype(F32)
    for copy in gene_copies:
        copy.wait()
    columns = genes.shape[1]
    wide = min(1024, columns)
    part = None
    for start in range(0, columns, wide):
        piece = genes_held[:, start : start + wide]
        product = contract_last(piece, piece)
        part = product if part is None else part + product
    gram[...] = part

    rows = counts.shape[0]
    half = rows // 2
    at_once = min(4, columns // tile)

    def scale(row, place):
        above = jnp.full((1, tile), mask_scalars[row, place].astype(F32), F32)
        return above / jnp.full((1, tile), counts_scalars[row, place].astype(F32), F32)

    def half_cross(side, out):
        out[...] = jnp.zeros_like(out)

        @pl.loop(0, columns // (tile * at_once))
        def _(step):
            total = None
            for col in range(at_once):
                place = step * at_once + col
                at = pl.ds(pl.multiple_of(place * tile, tile), tile)
                product = contract_last(
                    genes_held[:, at], counts_held[side * half : (side + 1) * half, at]
                )
                first = side * (half // tile)
                scales = jnp.concatenate(
                    [scale(first + row, place) for row in range(half // tile)], axis=1
                )
                product = scales * product
                total = product if total is None else total + product
            out[...] += total

    core = lax.axis_index("sub")
    per_half = len(row_starts) // 2
    for side in (0, 1):
        for copy in row_starts[side * per_half : (side + 1) * per_half]:
            copy.wait()

        @pl.when(core == side)
        def _(side=side):
            half_cross(side, mine)

        @pl.when(core != side)
        def _(side=side):
            half_cross(side, theirs)


def load(genes, counts, tile_mask, tile_counts):
    width, columns = genes.shape
    rows = counts.shape[0]
    tile = rows // tile_mask.shape[0]
    here = pl.BlockSpec(memory_space=pltpu.VMEM)
    there = pl.BlockSpec(memory_space=pltpu.HBM)
    half = jax.ShapeDtypeStruct((width, rows // 2), F32)
    return pl.pallas_call(
        functools.partial(load_kernel, tile),
        out_shape=(
            jax.ShapeDtypeStruct((width, width), F32),
            jax.ShapeDtypeStruct(tile_mask.shape, F32),
            half,
            half,
            pltpu.VMEM((width, columns), BF16),
            pltpu.VMEM((rows, columns), BF16),
        ),
        in_specs=[there] * 4,
        out_specs=(here,) * 6,
        scratch_shapes=[
            pltpu.VMEM(tile_mask.shape, jnp.int32),
            pltpu.VMEM(tile_mask.shape, jnp.int32),
            pltpu.SMEM(tile_mask.shape, jnp.int32),
            pltpu.SMEM(tile_mask.shape, jnp.int32),
            pltpu.SemaphoreType.DMA((4,)),
            pltpu.SemaphoreType.DMA((16,)),
            pltpu.SemaphoreType.DMA((4,)),
        ],
        compiler_params=params(),
        cost_estimate=cost(1, 1),
        name="load",
    )(away(genes), away(counts), away(tile_mask), away(tile_counts))


def call(kernel, name, out_shape, token, *args, scratch=(), smem=0, aliases=None, out=None):
    here = pl.BlockSpec(memory_space=pltpu.VMEM)
    there = pl.BlockSpec(memory_space=pltpu.SMEM)
    wherever = pl.BlockSpec(memory_space=pl.ANY)
    single = not isinstance(out_shape, tuple)
    specs = [there] * smem + [here] * (len(args) - smem)
    if aliases:
        specs[-1] = wherever
    out = out or here
    return pl.pallas_call(
        lambda token, *refs: kernel(*refs),
        out_shape=out_shape,
        in_specs=[wherever] + specs,
        out_specs=out if single else (out,) * len(out_shape),
        scratch_shapes=list(scratch),
        input_output_aliases=aliases or {},
        compiler_params=params(),
        cost_estimate=cost(1, 1),
        name=name,
    )(token, *args)


def fold_kernel(axis, bit, left, right, kept, sent):
    half = kept.shape[1]
    upper = (lax.axis_index(axis) & bit) != 0

    @pl.when(upper)
    def _():
        kept[...] = left[:, half:] + right[:, half:]
        sent[...] = left[:, :half] + right[:, :half]

    @pl.when(jnp.logical_not(upper))
    def _():
        kept[...] = left[:, :half] + right[:, :half]
        sent[...] = left[:, half:] + right[:, half:]


def fold(axis, bit, token, left, right):
    shape = jax.ShapeDtypeStruct((left.shape[0], left.shape[1] // 2), F32)
    return call(
        functools.partial(fold_kernel, axis, bit), "fold", (shape, shape), token, left, right
    )


def side_kernel(axis, bit, dim, mine, theirs, out):
    size = mine.shape[dim]
    low = (slice(None),) * dim + (slice(0, size),)
    high = (slice(None),) * dim + (slice(size, 2 * size),)
    upper = (lax.axis_index(axis) & bit) != 0

    @pl.when(upper)
    def _():
        out[low], out[high] = theirs[...], mine[...]

    @pl.when(jnp.logical_not(upper))
    def _():
        out[low], out[high] = mine[...], theirs[...]


def side(axis, bit, dim, token, mine, theirs):
    shape = list(mine.shape)
    shape[dim] *= 2
    return call(
        functools.partial(side_kernel, axis, bit, dim),
        "side", jax.ShapeDtypeStruct(tuple(shape), mine.dtype), token, mine, theirs,
    )


def halves(value):
    high = value.astype(BF16)
    return high, (value - high.astype(F32)).astype(BF16)


def product3(left, right):
    left_high, left_low = left
    right_high, right_low = right
    dot = functools.partial(jnp.dot, preferred_element_type=F32)
    return dot(left_high, right_high) + (
        dot(left_high, right_low) + dot(left_low, right_high)
    )


def inverse_kernel(gram_a, gram_b, inverse, rho_out):
    gram = gram_a[...] + gram_b[...]
    width = gram.shape[0]
    shape = (width, width)
    diagonal = lax.broadcasted_iota(jnp.int32, shape, 0) == lax.broadcasted_iota(
        jnp.int32, shape, 1
    )
    eye = jnp.where(diagonal, 1.0, 0.0).astype(F32)
    rho = jnp.sum(gram * eye) / width
    rho_out[...] = jnp.full(rho_out.shape, rho, F32)
    scale = 1.0 / jnp.full((1, 1), rho, F32)
    matrix = gram * scale + eye
    low = 2.0 / (width + 2.0)
    guess = low * eye
    image = low * matrix
    first = True
    while True:
        low = low * (2.0 - low)
        gain = 2.0 / (1.0 + low)
        low = gain * low
        done = 1.0 - low < 2e-3
        step = halves(gain * (2.0 * eye - image))
        if first:
            guess = guess[0:1, 0:1] * (gain * (2.0 * eye - image))
        else:
            guess = product3(halves(guess), step)
        first = False
        if done:
            break
        image = product3(halves(image), step)
    rest = eye - jnp.dot(
        matrix, guess, preferred_element_type=F32, precision=lax.Precision.HIGHEST
    )
    rest_halves = halves(rest)
    series = rest + product3(rest_halves, rest_halves)
    inverse[...] = (guess + product3(halves(guess), halves(series))) * scale


def shifted_inverse(gram_a, gram_b):
    width = gram_a.shape[0]
    whole = pl.BlockSpec(memory_space=pltpu.VMEM)
    return pl.pallas_call(
        inverse_kernel,
        out_shape=(
            jax.ShapeDtypeStruct((width, width), F32),
            jax.ShapeDtypeStruct((8, 128), F32),
        ),
        in_specs=[whole, whole],
        out_specs=(whole, whole),
        compiler_params=params(),
        cost_estimate=cost(2 * 60 * width**3, 12 * width**2),
        name="inverse",
    )(gram_a, gram_b)


def admm_kernel(genes, rho_block, cross_a, cross_b, inverse, start, columns_out):
    rows = cross_a.shape[1]
    place = lax.axis_index("sub") * genes + lax.axis_index("gene")
    rho = rho_block[0:1, 0:1]
    cross = cross_a[...] + cross_b[...]
    inverse_halves = halves(inverse[...])
    zvalue = start[pl.ds(pl.multiple_of(place * rows, rows), rows), :].astype(F32).T
    uvalue = jnp.zeros_like(zvalue)
    for _ in range(ITERS):
        vvalue = product3(inverse_halves, halves(cross + rho * (zvalue - uvalue)))
        zvalue = jnp.maximum(vvalue + uvalue, 0.0)
        uvalue = uvalue + vvalue - zvalue
    columns_out[...] = zvalue.astype(BF16)


def products_kernel(tile, line, start, chunk, factor, counts, columns, *outs):
    only_first = len(outs) == 1
    block = line.block(1 if only_first else 2, 0)
    size = counts.shape[1] // line.size
    span = min(tile, chunk)
    wide = 2 * span if chunk % (2 * span) == 0 else span
    steps = chunk // wide
    row_tiles = columns.shape[1] // tile

    @pl.loop(0, steps if only_first else line.size * steps)
    def _(turn):
        order, step = (block, turn) if only_first else (turn // steps, lax.rem(turn, steps))
        first = pl.multiple_of(order * size + start + step * wide, span)
        total = None
        for row in range(row_tiles):
            part = jnp.dot(
                columns[:, row * tile : (row + 1) * tile],
                counts[row * tile : (row + 1) * tile, pl.ds(first, wide)],
                preferred_element_type=F32,
            )
            scales = [
                jnp.full((1, span), factor[row, (first + col * span) // tile], F32)
                for col in range(wide // span)
            ]
            part = jnp.concatenate(scales, axis=1) * part
            total = part if total is None else total + part
        total = total.astype(BF16)
        at = pl.ds(pl.multiple_of(step * wide, span), wide)
        if only_first:
            outs[0][:, at] = total
        else:
            outs[0][order, :, at] = total

            @pl.when(order == block)
            def _():
                outs[1][:, at] = total


def products(only_first, line, start, chunk, token, factor, counts, columns):
    width, rows = columns.shape
    tile = rows // factor.shape[0]
    out_shape = (jax.ShapeDtypeStruct((width, chunk), BF16),)
    if not only_first:
        out_shape = (jax.ShapeDtypeStruct((line.size, width, chunk), BF16),) + out_shape
    return call(
        functools.partial(products_kernel, tile, line, start, chunk),
        "products", out_shape, token, factor, held(counts), columns, smem=1,
    )


def turn_kernel(value, out):
    out[...] = value[...].astype(F32).T.astype(out.dtype)


def turn(token, value):
    shape = jax.ShapeDtypeStruct(value.shape[::-1], value.dtype)
    return call(turn_kernel, "turn", shape, token, value)


def row_share_kernel(subs, columns, out):
    part = out.shape[0]
    place = lax.axis_index("gene") * subs + lax.axis_index("sub")
    share = columns[pl.ds(pl.multiple_of(place * part, part), part), :]
    out[...] = contract_last(share, columns[...]).astype(out.dtype)


def row_share(subs, part, token, columns):
    shape = jax.ShapeDtypeStruct((part, columns.shape[0]), BF16)
    return call(functools.partial(row_share_kernel, subs), "row_share", shape, token, columns)


def hop_kernel(kind, targets, own, arrived, out):
    cell = lax.axis_index("cell")
    reached = cell == targets[0]
    for target in targets[1:]:
        reached = jnp.logical_or(reached, cell == target)
    more = arrived[...].astype(F32)
    base = own[...].astype(F32)
    value = base + more if kind == "sum" else more
    out[...] = jnp.where(reached, value, base).astype(out.dtype)


def hop(kind, targets, token, own, arrived):
    shape = jax.ShapeDtypeStruct(own.shape, own.dtype)
    return call(functools.partial(hop_kernel, kind, targets), "hop", shape, token, own, arrived)


def operand_kernel(line, phase, parity, total, before, out):
    own = total[line.block(phase, parity)].astype(F32)
    out[...] = (own + before[...].astype(F32)).astype(BF16)


def operand(line, phase, parity, token, total, before):
    shape = jax.ShapeDtypeStruct(before.shape, BF16)
    return call(
        functools.partial(operand_kernel, line, phase, parity),
        "operand", shape, token, total, before,
    )


def keep_kernel(start, total, first, second, *refs):
    out, turned, sems = refs[-3:]
    width, chunk = first.shape
    pieces = sems.shape[0]
    wide = chunk // pieces
    own = total.at[lax.axis_index("cell")]
    copies = []
    for piece in range(pieces):
        at = slice(piece * wide, (piece + 1) * wide)
        value = first[:, at].astype(F32) + second[:, at].astype(F32)
        turned[at] = (own[:, at].astype(F32) + value).T
        copies.append(
            pltpu.make_async_copy(
                turned.at[at], out.at[pl.ds(start + piece * wide, wide)], sems.at[piece]
            )
        )
        copies[-1].start()
    for copy in copies:
        copy.wait()


def keep(block, start, token, total, first, second, out):
    width, chunk = first.shape
    pieces = max(1, chunk // 256)
    return call(
        functools.partial(keep_kernel, start),
        "keep", jax.ShapeDtypeStruct((block, width), F32), token,
        total, first, second, *([] if out is None else [out]),
        scratch=[pltpu.VMEM((chunk, width), F32), pltpu.SemaphoreType.DMA((pieces,))],
        aliases=None if out is None else {4: 0},
        out=pl.BlockSpec(memory_space=pl.ANY),
    )


class Line:
    def __init__(self, size):
        self.size = size

    def pairs(self, phase, parity):
        links = range(parity, self.size - 1, 2)
        right = [(i, i + 1) for i in links if i < phase]
        left = [(i + 1, i) for i in links if i + 1 >= self.size - phase]
        return right + left

    def block(self, phase, parity):
        cell = lax.axis_index("cell")
        to_right = (cell & 1) == parity
        block = cell + jnp.where(to_right, self.size - phase, phase)
        return jnp.where(block >= self.size, block - self.size, block)

    def send(self, value, phase, parity):
        return lax.ppermute(value, "cell", self.pairs(phase, parity))


def swap(value, axis, size, step):
    return lax.ppermute(value, axis, [(i, i ^ step) for i in range(size)])


def pair_sums(value, axis, size, event):
    step = 1
    while step < size:
        arrived, event = after(swap(value, axis, size, step), event)
        value = value + arrived
        step *= 2
    return value


def after(value, event):
    return lax.optimization_barrier((value, event))


def chunk_sizes(block):
    return [block // 2, block // 2] if block % 1024 == 0 else [block]


def shards(sizes, counts, tile_mask, tile_counts, gene_factor, prev_factor):
    cells, genes, subs = sizes
    rows, columns = counts.shape
    width = gene_factor.shape[0]
    line = Line(cells)

    gram, factor, theirs, mine, _, counts_held = load(
        gene_factor, counts, tile_mask, tile_counts
    )
    token = factor
    arrived = swap(theirs, "sub", subs, 1)
    cross_a, cross_b = mine, arrived
    bit = genes // 2
    while bit:
        cross_a, sent = fold("gene", bit, token, cross_a, cross_b)
        cross_b = swap(sent, "gene", genes, bit)
        if bit == genes // 2:
            gram = pair_sums(gram, "gene", genes, cross_a)
        bit //= 2
    gram_other = swap(gram, "sub", subs, 1)
    inverse, rho = shifted_inverse(gram, gram_other)
    share = jax.ShapeDtypeStruct((width, rows // (genes * subs)), BF16)
    columns_held = call(
        functools.partial(admm_kernel, genes),
        "admm", share, token, rho, cross_a, cross_b, inverse, prev_factor,
    )
    bit = 1
    while bit < genes:
        columns_arrived = swap(columns_held, "gene", genes, bit)
        columns_held = side("gene", bit, 1, token, columns_held, columns_arrived)
        bit *= 2
    columns_arrived = swap(columns_held, "sub", subs, 1)
    whole = side("sub", 1, 1, token, columns_held, columns_arrived)

    block = columns // cells
    chunks = chunk_sizes(block)
    starts = [sum(chunks[:i]) for i in range(len(chunks))]
    every = range(len(chunks))

    arrived = {}

    def send(value, phase, parity, index):
        pairs = line.pairs(phase, parity)
        arrived[phase, parity, index] = lax.ppermute(value, "cell", pairs) if pairs else None

    def resend(token, phase, parity, index):
        before = arrived[phase - 1, 1 - parity, index]
        if before is None:
            value = seconds[index]
        else:
            value = operand(line, phase, parity, token, totals[index], before)
            token, value = after(token, value)
        send(value, phase, parity, index)
        return token

    middle = cells // 2
    inward = [[(i, i + 1), (cells - 1 - i, cells - 2 - i)] for i in range(middle - 1)]
    outward = [[(b, a) for a, b in pairs] for pairs in reversed(inward)]
    hops = [("sum", p) for p in inward] + [("sum", [(middle - 1, middle), (middle, middle - 1)])]
    hops += [("copy", p) for p in outward]

    def hop_rows(token, rows_sum):
        kind, pairs = hops.pop(0)
        rows_arrived = lax.ppermute(rows_sum, "cell", pairs)
        targets = [b for _, b in pairs]
        return after(token, hop(kind, targets, token, rows_sum, rows_arrived))

    def side_rows(token, rows_sum, axis, size, bit):
        rows_arrived = swap(rows_sum, axis, size, bit)
        return after(token, side(axis, bit, 0, token, rows_sum, rows_arrived))

    token, rows_sum = after(token, row_share(subs, width // (genes * subs), token, whole))
    for index in every:
        (first,) = products(
            True, line, starts[index], chunks[index], token, factor, counts_held, whole
        )
        token, first = after(token, first)
        for parity in (0, 1):
            send(first, 1, parity, index)
        if index == 0 and hops:
            token, rows_sum = hop_rows(token, rows_sum)
    totals, seconds = [], []
    for index in every:
        total, second = products(
            False, line, starts[index], chunks[index], token, factor, counts_held, whole
        )
        token, second = after(token, second)
        if hops:
            token, rows_sum = hop_rows(token, rows_sum)
        totals.append(total)
        seconds.append(second)
        for parity in (0, 1):
            token = resend(token, 2, parity, index)
    while hops:
        token, rows_sum = hop_rows(token, rows_sum)
    new_factor = turn(token, whole)
    token, new_factor = after(token, new_factor)
    token, rows_sum = side_rows(token, rows_sum, "sub", subs, 1)
    bits = [1 << i for i in range((genes - 1).bit_length())]
    for phase in range(3, cells):
        for index in every:
            for parity in (0, 1):
                token = resend(token, phase, parity, index)
                if bits:
                    token, rows_sum = side_rows(token, rows_sum, "gene", genes, bits.pop(0))
    data_products = None
    last = cells - 1
    for index in every:
        data_products = keep(
            block, starts[index], token, totals[index],
            arrived[last, 0, index], arrived[last, 1, index], data_products,
        )
        token, data_products = after(token, data_products)
    return (new_factor, rows_sum.astype(F32), data_products)


def solution(mesh):
    sizes = (mesh.shape["cell"], mesh.shape["gene"], mesh.shape["sub"])
    return jax.shard_map(
        functools.partial(shards, sizes),
        mesh=mesh,
        in_specs=(
            P(("groups", "cell"), ("gene", "sub")),
            P(("groups", "cell"), ("gene", "sub")),
            P(("groups", "cell"), ("gene", "sub")),
            P("groups", ("gene", "sub")),
            P(("groups", "cell"), None),
        ),
        out_specs=(
            P(("groups", "cell"), None),
            P("groups", None),
            P(("groups", "gene", "sub", "cell"), None),
        ),
        check_vma=False,
    )
```

time: 374 us -> 121 us (0.32)
  waiting for transfers between devices: 200 us -> 40.5 us
  other arithmetic: 59.6 us -> 0.76 us
  matrix products: 53.6 us -> 0 us
  local copies, waits for them, and re-layouts: 43.5 us -> 0.01 us
  starting transfers between devices: 0.3 us -> 40 us
  Pallas kernels: 0 us -> 38.6 us
  between operations: 15.9 us -> 0.96 us
    reduce_scatter x1 -> x0, waiting for transfers between devices: 146 us -> none  [shards(): lax.psum_scatter(contract_first(scaled, new_factor), 'cell', scatter_dime...]
    psum x2 -> x0, waiting for transfers between devices: 54.6 us -> none  [the longest x1 41.7 us: shards(): cross = lax.psum(cross_part, ('gene', 'sub'))]
    another operation x9 -> x0, other arithmetic: 53.7 us -> none  [the longest x6 34 us: shifted_inverse(): lower = jnp.linalg.cholesky(gram + rho * eye)]
    dot_general x7 -> x0, matrix products: 51.3 us -> none  [the longest x2 22.7 us: contract_first(): lax.dot_general(left, right, (((0,), (0,)), ((), ())), preferred_element_...]
    ppermute x0 -> x21, waiting for transfers between devices: none -> 40.5 us  [the longest x10 22.5 us: send(): lax.ppermute(value, 'cell', pairs)]
    ppermute x0 -> x21, starting transfers between devices: none -> 40 us  [the longest x10 25.9 us: send(): lax.ppermute(value, 'cell', pairs)]
    pallas_call x0 -> x25, Pallas kernels: none -> 38.6 us  [the longest x1 18 us: load(): pl.pallas_call(functools.partial(load_kernel, tile), out_shape=(jax.Shape...]
    unnamed x7 -> x2, local copies, waits for them, and re-layouts: 34 us -> 0.01 us
  transfers between devices with their start and end apart: 3 -> 21, of which waited for: 3 -> 10; matrix products, arithmetic and copies ran while one was open for 6% -> 1% of each run, Pallas kernels for 0% -> 15%
where the time goes in v8:
time: 121 us
  waiting for transfers between devices  40.5 us (33%)
  starting transfers between devices  40 us (33%)
  Pallas kernels  38.6 us (32%)
    ppermute x10, starting transfers between devices, send(): lax.ppermute(value, 'cell', pairs)  25.9 us
    ppermute x10, waiting for transfers between devices, send(): lax.ppermute(value, 'cell', pairs)  22.5 us
    ppermute x8, waiting for transfers between devices, swap(): return lax.ppermute(value, axis, [(i, i ^ step) for i in range(size)])  18 us
    pallas_call x1, Pallas kernels, load(): pl.pallas_call(functools.partial(load_kernel, tile), out_shape=(jax.Shape...  18 us
    pallas_call x23, Pallas kernels, call(): pl.pallas_call(lambda token, *refs: kernel(*refs), out_shape=out_shape, i...  17.1 us
    ppermute x8, starting transfers between devices, swap(): return lax.ppermute(value, axis, [(i, i ^ step) for i in range(size)])  8.38 us
    ppermute x3, starting transfers between devices, hop_rows(): rows_arrived = lax.ppermute(rows_sum, 'cell', pairs)  5.68 us
    pallas_call x1, Pallas kernels, shifted_inverse(): pl.pallas_call(inverse_kernel, out_shape=(jax.ShapeDtypeStruct((width, wi...  3.51 us
  transfers between devices with their start and end apart: 21, of which 10 were waited for; matrix products, arithmetic and copies ran while one was open for 1% of the time, Pallas kernels for 15%

profile of v8, /device:TPU:0, one launch (start us, length us, event | category | flops | bytes accessed | tf_op | source)
XLA Modules:
  0.0 120.9 jit_solution(4192395064621732883)
XLA Ops:
  0.6 18.0 %load.1 = (f32[256,256]{1,0:T(8,128)S(1)}, f32[4,32]{1,0:T(4,128)S(1)}, f32[256,512]{1,0:T(8,128)S(1)}, f32[256,512]{1,0:T(8,128)S(1)}, bf16[256,8192]{1,0:T(8,128)(2,1)}, /*index=5*/bf16[1024,8192]{1,0:T(8,128)(2,1)S(1)}) custom-call(bf16[256,8192]{1,0:T(8,128)(2,1)} %genes.1, bf16[1024,8192]{1,0:T(8,128)(2,1)} %counts.1, s32[4,32]{1,0:T(4,128)} %tile_mask.1, ...), custom_call_target="tpu_custom_call" | custom-call | flops 1 | bytes 1 | tf_op jit(solution)/shard_map/load/pallas_call | solution.py:131
  18.6 0.5 collective-permute-start.1
  19.2 2.5 %collective-permute-start = (f32[256,256]{1,0:T(8,128)S(1)}, f32[256,256]{1,0:T(8,128)S(1)}, u32[]{:S(2)}, u32[]{:S(2)}) collective-permute-start(f32[256,256]{1,0:T(8,128)S(1)} %get-tuple-element.55), channel_id=1, source_target_pairs={{0,2},{2,0},{1,3},{3,1},{4,6},{6,4},{5,7},{7,5},{8,10},{10,8},{9,1... | collective-permute-start | bytes 786440 | tf_op jit(solution)/shard_map/ppermute | solution.py:465
  21.7 0.0 collective-permute-done.1.refs_1_
  21.7 0.1 fold.1
  21.8 0.0 copy-start
  21.8 6.8 %collective-permute-done = f32[256,256]{1,0:T(8,128)S(1)} collective-permute-done((f32[256,256]{1,0:T(8,128)S(1)}, f32[256,256]{1,0:T(8,128)S(1)}, u32[]{:S(2)}, u32[]{:S(2)}) %collective-permute-start) | collective-permute-done | bytes 262176 | tf_op jit(solution)/shard_map/ppermute | solution.py:465
  28.7 0.1 collective-permute-start.2
  28.7 1.8 %collective-permute-start.3 = (f32[256,256]{1,0:T(8,128)S(1)}, f32[256,256]{1,0:T(8,128)S(1)}, u32[]{:S(2)}, u32[]{:S(2)}) collective-permute-start(f32[256,256]{1,0:T(8,128)S(1)} %get-tuple-element.61), channel_id=1, source_target_pairs={{0,2},{2,0},{1,3},{3,1},{4,6},{6,4},{5,7},{7,5},{8,10},{10,8},{9,1... | collective-permute-start | bytes 786440 | tf_op jit(solution)/shard_map/ppermute | solution.py:465
  30.6 0.0 collective-permute-done.2.gram_b
  30.6 3.5 %inverse.1 = (f32[256,256]{1,0:T(8,128)S(1)}, f32[8,128]{1,0:T(8,128)S(1)}) custom-call(f32[256,256]{1,0:T(8,128)S(1)} %add.3.gram_a, f32[256,256]{1,0:T(8,128)S(1)} %collective-permute-done.2.gram_b), custom_call_target="tpu_custom_call" | custom-call | flops 2013265920 | bytes 786432 | tf_op jit(solution)/shard_map/inverse/pallas_call | solution.py:281
  34.1 3.4 %collective-permute-done.3.refs_2_ = f32[256,256]{1,0:T(8,128)S(1)} collective-permute-done((f32[256,256]{1,0:T(8,128)S(1)}, f32[256,256]{1,0:T(8,128)S(1)}, u32[]{:S(2)}, u32[]{:S(2)}) %collective-permute-start.3) | collective-permute-done | bytes 262176 | tf_op jit(solution)/shard_map/ppermute | solution.py:465
  37.5 0.0 copy-done
  37.5 1.0 admm.1.refs_0_
  38.5 1.8 %collective-permute-start.4 = (bf16[256,256]{1,0:T(8,128)(2,1)S(1)}, bf16[256,256]{1,0:T(8,128)(2,1)S(1)}, u32[]{:S(2)}, u32[]{:S(2)}) collective-permute-start(bf16[256,256]{1,0:T(8,128)(2,1)S(1)} %admm.1.refs_0_), channel_id=1, source_target_pairs={{0,2},{2,0},{1,3},{3,1},{4,6},{6,4},{5,7},{7,5},{8,10},{10,8},{9,1... | collective-permute-start | bytes 393224 | tf_op jit(solution)/shard_map/ppermute | solution.py:465
  40.3 3.3 %collective-permute-done.4.refs_1_ = bf16[256,256]{1,0:T(8,128)(2,1)S(1)} collective-permute-done((bf16[256,256]{1,0:T(8,128)(2,1)S(1)}, bf16[256,256]{1,0:T(8,128)(2,1)S(1)}, u32[]{:S(2)}, u32[]{:S(2)}) %collective-permute-start.4) | collective-permute-done | bytes 131104 | tf_op jit(solution)/shard_map/ppermute | solution.py:465
  43.7 0.1 collective-permute-start.5
  43.8 1.5 %collective-permute-done.5.refs_1_ = bf16[256,512]{1,0:T(8,128)(2,1)S(1)} collective-permute-done((bf16[256,512]{1,0:T(8,128)(2,1)S(1)}, bf16[256,512]{1,0:T(8,128)(2,1)S(1)}, u32[]{:S(2)}, u32[]{:S(2)}) %collective-permute-start.5) | collective-permute-done | bytes 262176 | tf_op jit(solution)/shard_map/ppermute | solution.py:465
  45.3 0.3 row_share.1.refs_0_
  45.6 3.7 %collective-permute-start.6 = (bf16[64,256]{1,0:T(8,128)(2,1)S(1)}, bf16[64,256]{1,0:T(8,128)(2,1)S(1)}, u32[]{:S(2)}, u32[]{:S(2)}) collective-permute-start(bf16[64,256]{1,0:T(8,128)(2,1)S(1)} %row_share.1.refs_0_), channel_id=1, source_target_pairs={{0,4},{12,8},{1,5},{13,9},{2,6},{14,10},{3,7},{15,11},{16,20},{28,... | collective-permute-start | bytes 98312 | tf_op jit(solution)/shard_map/ppermute | solution.py:548
  49.3 1.5 %products.4 = bf16[256,1024]{1,0:T(8,128)(2,1)S(1)} custom-call(f32[4,32]{1,0:T(4,128)S(1)} %get-tuple-element.100.token.refs_0_, f32[4,32]{1,0:T(4,128)S(1)} %get-tuple-element.100.token.refs_0_, bf16[1024,8192]{1,0:T(8,128)(2,1)S(1)} %get-tuple-element.64.refs_1_, bf16[256,1024]{1,0:T(8,128)(2,1)S(1)} %side.5.refs_0_.refs_2_), custom_call_target="tpu_custom_call" | custom-call | flops 1 | bytes 1 | tf_op jit(solution)/shard_map/products/pallas_call | solution.py:167
  50.8 1.3 %collective-permute-start.8 = (bf16[256,1024]{1,0:T(8,128)(2,1)S(1)}, bf16[256,1024]{1,0:T(8,128)(2,1)S(1)}, u32[]{:S(2)}, u32[]{:S(2)}) collective-permute-start(bf16[256,1024]{1,0:T(8,128)(2,1)S(1)} %products.4), channel_id=1, source_target_pairs={{0,4},{12,8},{1,5},{13,9},{2,6},{14,10},{3,7},{15,11},{16,20},{28,... | collective-permute-start | bytes 1572872 | tf_op jit(solution)/shard_map/ppermute | solution.py:528
  52.1 0.0 collective-permute-done.6.refs_1_
  52.2 1.5 %products.5 = bf16[256,1024]{1,0:T(8,128)(2,1)S(1)} custom-call(f32[4,32]{1,0:T(4,128)S(1)} %get-tuple-element.100.token.refs_0_, f32[4,32]{1,0:T(4,128)S(1)} %get-tuple-element.100.token.refs_0_, bf16[1024,8192]{1,0:T(8,128)(2,1)S(1)} %get-tuple-element.64.refs_1_, bf16[256,1024]{1,0:T(8,128)(2,1)S(1)} %side.5.refs_0_.refs_2_), custom_call_target="tpu_custom_call" | custom-call | flops 1 | bytes 1 | tf_op jit(solution)/shard_map/products/pallas_call | solution.py:167
  53.7 3.0 %collective-permute-start.10 = (bf16[256,1024]{1,0:T(8,128)(2,1)S(1)}, bf16[256,1024]{1,0:T(8,128)(2,1)S(1)}, u32[]{:S(2)}, u32[]{:S(2)}) collective-permute-start(bf16[256,1024]{1,0:T(8,128)(2,1)S(1)} %products.5), channel_id=1, source_target_pairs={{0,4},{12,8},{1,5},{13,9},{2,6},{14,10},{3,7},{15,11},{16,20},{28,... | collective-permute-start | bytes 1572872 | tf_op jit(solution)/shard_map/ppermute | solution.py:528
  56.7 0.7 collective-permute-start.7
  57.3 4.2 %products.6 = (bf16[4,256,1024]{2,1,0:T(8,128)(2,1)S(1)}, bf16[256,1024]{1,0:T(8,128)(2,1)S(1)}) custom-call(f32[4,32]{1,0:T(4,128)S(1)} %get-tuple-element.100.token.refs_0_, f32[4,32]{1,0:T(4,128)S(1)} %get-tuple-element.100.token.refs_0_, bf16[1024,8192]{1,0:T(8,128)(2,1)S(1)} %get-tuple-element.64.refs_1_, bf16[256,1024]{1,0:T(8,128)(2,1)S(1)} %side.5.refs_0_.refs_2_), custom_call_target="tpu_custom_call" | custom-call | flops 1 | bytes 1 | tf_op jit(solution)/shard_map/products/pallas_call | solution.py:167
  61.6 0.0 collective-permute-done.7.refs_1_
  61.6 1.3 %collective-permute-start.9 = (bf16[64,256]{1,0:T(8,128)(2,1)S(1)}, bf16[64,256]{1,0:T(8,128)(2,1)S(1)}, u32[]{:S(2)}, u32[]{:S(2)}) collective-permute-start(bf16[64,256]{1,0:T(8,128)(2,1)S(1)} %hop.4.refs_0_), channel_id=1, source_target_pairs={{4,0},{8,12},{5,1},{9,13},{6,2},{10,14},{7,3},{11,15},{20,16},{24,... | collective-permute-start | bytes 98312 | tf_op jit(solution)/shard_map/ppermute | solution.py:548
  62.9 1.5 %collective-permute-done.8.refs_1_ = bf16[256,1024]{1,0:T(8,128)(2,1)S(1)} collective-permute-done((bf16[256,1024]{1,0:T(8,128)(2,1)S(1)}, bf16[256,1024]{1,0:T(8,128)(2,1)S(1)}, u32[]{:S(2)}, u32[]{:S(2)}) %collective-permute-start.8) | collective-permute-done | bytes 524320 | tf_op jit(solution)/shard_map/ppermute | solution.py:528
  64.4 0.1 operand.6
  64.5 0.7 collective-permute-start.12
  65.2 7.3 %collective-permute-start.14 = (bf16[256,1024]{1,0:T(8,128)(2,1)S(1)}, bf16[256,1024]{1,0:T(8,128)(2,1)S(1)}, u32[]{:S(2)}, u32[]{:S(2)}) collective-permute-start(bf16[256,1024]{1,0:T(8,128)(2,1)S(1)} %get-tuple-element.92), channel_id=1, source_target_pairs={{0,4},{12,8},{1,5},{13,9},{2,6},{14,10},{3,7},{15,11},{16,20},{28,... | collective-permute-start | bytes 1572872 | tf_op jit(solution)/shard_map/ppermute | solution.py:528
  72.5 4.2 %products.7 = (bf16[4,256,1024]{2,1,0:T(8,128)(2,1)S(1)}, bf16[256,1024]{1,0:T(8,128)(2,1)S(1)}) custom-call(f32[4,32]{1,0:T(4,128)S(1)} %get-tuple-element.100.token.refs_0_, f32[4,32]{1,0:T(4,128)S(1)} %get-tuple-element.100.token.refs_0_, bf16[1024,8192]{1,0:T(8,128)(2,1)S(1)} %get-tuple-element.64.refs_1_, bf16[256,1024]{1,0:T(8,128)(2,1)S(1)} %side.5.refs_0_.refs_2_), custom_call_target="tpu_custom_call" | custom-call | flops 1 | bytes 1 | tf_op jit(solution)/shard_map/products/pallas_call | solution.py:167
  76.8 0.0 collective-permute-done.9.refs_1_
  76.8 0.0 collective-permute-done.10.refs_1_
  76.8 0.2 operand.7
  77.0 0.7 collective-permute-start.15
  77.7 6.1 %collective-permute-start.16 = (bf16[256,1024]{1,0:T(8,128)(2,1)S(1)}, bf16[256,1024]{1,0:T(8,128)(2,1)S(1)}, u32[]{:S(2)}, u32[]{:S(2)}) collective-permute-start(bf16[256,1024]{1,0:T(8,128)(2,1)S(1)} %get-tuple-element.96), channel_id=1, source_target_pairs={{0,4},{12,8},{1,5},{13,9},{2,6},{14,10},{3,7},{15,11},{16,20},{28,... | collective-permute-start | bytes 1572872 | tf_op jit(solution)/shard_map/ppermute | solution.py:528
  83.8 0.1 collective-permute-start.11
  83.9 1.0 turn.1
  84.9 0.2 collective-permute-done.11.refs_1_
  85.1 1.4 %collective-permute-start.13 = (bf16[128,256]{1,0:T(8,128)(2,1)S(1)}, bf16[128,256]{1,0:T(8,128)(2,1)S(1)}, u32[]{:S(2)}, u32[]{:S(2)}) collective-permute-start(bf16[128,256]{1,0:T(8,128)(2,1)S(1)} %side.6.refs_0_), channel_id=1, source_target_pairs={{0,2},{2,0},{1,3},{3,1},{4,6},{6,4},{5,7},{7,5},{8,10},{10,8},{9,1... | collective-permute-start | bytes 196616 | tf_op jit(solution)/shard_map/ppermute | solution.py:465
  86.5 0.0 collective-permute-done.12.refs_1_
  86.5 0.1 operand.8
  86.6 2.8 %collective-permute-done.13.refs_1_ = bf16[128,256]{1,0:T(8,128)(2,1)S(1)} collective-permute-done((bf16[128,256]{1,0:T(8,128)(2,1)S(1)}, bf16[128,256]{1,0:T(8,128)(2,1)S(1)}, u32[]{:S(2)}, u32[]{:S(2)}) %collective-permute-start.13) | collective-permute-done | bytes 65568 | tf_op jit(solution)/shard_map/ppermute | solution.py:465
  89.4 0.1 collective-permute-start.17
  89.5 0.0 collective-permute-done.14.refs_1_
  89.5 0.2 operand.9
  89.7 0.7 collective-permute-start.18
  90.4 0.0 collective-permute-done.15.refs_1_
  90.4 0.2 operand.10
  90.6 7.5 %collective-permute-done.16.refs_1_ = bf16[256,1024]{1,0:T(8,128)(2,1)S(1)} collective-permute-done((bf16[256,1024]{1,0:T(8,128)(2,1)S(1)}, bf16[256,1024]{1,0:T(8,128)(2,1)S(1)}, u32[]{:S(2)}, u32[]{:S(2)}) %collective-permute-start.16) | collective-permute-done | bytes 524320 | tf_op jit(solution)/shard_map/ppermute | solution.py:528
  98.1 0.1 operand.11
  98.2 0.7 collective-permute-start.20
  98.9 5.4 %collective-permute-start.19 = (bf16[256,1024]{1,0:T(8,128)(2,1)S(1)}, bf16[256,1024]{1,0:T(8,128)(2,1)S(1)}, u32[]{:S(2)}, u32[]{:S(2)}) collective-permute-start(bf16[256,1024]{1,0:T(8,128)(2,1)S(1)} %operand.10), channel_id=1, source_target_pairs={{0,4},{8,12},{4,0},{12,8},{1,5},{9,13},{5,1},{13,9},{2,6},{10,14},... | collective-permute-start | bytes 1572872 | tf_op jit(solution)/shard_map/ppermute | solution.py:528
  104.3 0.7 convert_element_type.3
  105.1 4.3 %collective-permute-done.17.refs_1_ = bf16[256,1024]{1,0:T(8,128)(2,1)S(1)} collective-permute-done((bf16[256,1024]{1,0:T(8,128)(2,1)S(1)}, bf16[256,1024]{1,0:T(8,128)(2,1)S(1)}, u32[]{:S(2)}, u32[]{:S(2)}) %collective-permute-start.17) | collective-permute-done | bytes 524320 | tf_op jit(solution)/shard_map/ppermute | solution.py:528
  109.3 0.0 collective-permute-done.18.refs_2_
  109.3 1.1 keep.2.refs_3_
  110.5 0.0 collective-permute-done.20.refs_2_
  110.5 9.3 %collective-permute-done.19.refs_1_ = bf16[256,1024]{1,0:T(8,128)(2,1)S(1)} collective-permute-done((bf16[256,1024]{1,0:T(8,128)(2,1)S(1)}, bf16[256,1024]{1,0:T(8,128)(2,1)S(1)}, u32[]{:S(2)}, u32[]{:S(2)}) %collective-permute-start.19) | collective-permute-done | bytes 524320 | tf_op jit(solution)/shard_map/ppermute | solution.py:528
  119.8 1.1 keep.3
  (8 shorter events, 0.2 us)
Async XLA Ops:
  18.6 3.1 %collective-permute-start.1 = (f32[256,512]{1,0:T(8,128)S(1)}, f32[256,512]{1,0:T(8,128)S(1)}, u32[]{:S(2)}, u32[]{:S(2)}) collective-permute-start(f32[256,512]{1,0:T(8,128)S(1)} %get-tuple-element.57), channel_id=1, source_target_pairs={{0,1},{1,0},{2,3},{3,2},{4,5},{5,4},{6,7},{7,6},{8,9},{9,8},{10,11... | collective-permute-start | bytes 1572872 | tf_op jit(solution)/shard_map/ppermute | solution.py:465
  19.2 9.4 %collective-permute-start = (f32[256,256]{1,0:T(8,128)S(1)}, f32[256,256]{1,0:T(8,128)S(1)}, u32[]{:S(2)}, u32[]{:S(2)}) collective-permute-start(f32[256,256]{1,0:T(8,128)S(1)} %get-tuple-element.55), channel_id=1, source_target_pairs={{0,2},{2,0},{1,3},{3,1},{4,6},{6,4},{5,7},{7,5},{8,10},{10,8},{9,1... | collective-permute-start | bytes 786440 | tf_op jit(solution)/shard_map/ppermute | solution.py:465
  21.8 15.7 %copy-start = (bf16[1024,256]{1,0:T(8,128)(2,1)S(1)}, bf16[1024,256]{1,0:T(8,128)(2,1)}, u32[]{:S(2)}) copy-start(bf16[1024,256]{1,0:T(8,128)(2,1)} %refs_4_.1) | copy-start | bytes 1572868
  28.7 1.9 %collective-permute-start.2 = (f32[256,256]{1,0:T(8,128)S(1)}, f32[256,256]{1,0:T(8,128)S(1)}, u32[]{:S(2)}, u32[]{:S(2)}) collective-permute-start(f32[256,256]{1,0:T(8,128)S(1)} %add.3.gram_a), channel_id=1, source_target_pairs={{0,1},{1,0},{2,3},{3,2},{4,5},{5,4},{6,7},{7,6},{8,9},{9,8},{10,11... | collective-permute-start | bytes 786440 | tf_op jit(solution)/shard_map/ppermute | solution.py:465
  28.7 8.7 %collective-permute-start.3 = (f32[256,256]{1,0:T(8,128)S(1)}, f32[256,256]{1,0:T(8,128)S(1)}, u32[]{:S(2)}, u32[]{:S(2)}) collective-permute-start(f32[256,256]{1,0:T(8,128)S(1)} %get-tuple-element.61), channel_id=1, source_target_pairs={{0,2},{2,0},{1,3},{3,1},{4,6},{6,4},{5,7},{7,5},{8,10},{10,8},{9,1... | collective-permute-start | bytes 786440 | tf_op jit(solution)/shard_map/ppermute | solution.py:465
  38.5 5.1 %collective-permute-start.4 = (bf16[256,256]{1,0:T(8,128)(2,1)S(1)}, bf16[256,256]{1,0:T(8,128)(2,1)S(1)}, u32[]{:S(2)}, u32[]{:S(2)}) collective-permute-start(bf16[256,256]{1,0:T(8,128)(2,1)S(1)} %admm.1.refs_0_), channel_id=1, source_target_pairs={{0,2},{2,0},{1,3},{3,1},{4,6},{6,4},{5,7},{7,5},{8,10},{10,8},{9,1... | collective-permute-start | bytes 393224 | tf_op jit(solution)/shard_map/ppermute | solution.py:465
  43.7 1.6 %collective-permute-start.5 = (bf16[256,512]{1,0:T(8,128)(2,1)S(1)}, bf16[256,512]{1,0:T(8,128)(2,1)S(1)}, u32[]{:S(2)}, u32[]{:S(2)}) collective-permute-start(bf16[256,512]{1,0:T(8,128)(2,1)S(1)} %side.4.refs_0_), channel_id=1, source_target_pairs={{0,1},{1,0},{2,3},{3,2},{4,5},{5,4},{6,7},{7,6},{8,9},{9,8},{10,11... | collective-permute-start | bytes 786440 | tf_op jit(solution)/shard_map/ppermute | solution.py:465
  45.6 6.5 %collective-permute-start.6 = (bf16[64,256]{1,0:T(8,128)(2,1)S(1)}, bf16[64,256]{1,0:T(8,128)(2,1)S(1)}, u32[]{:S(2)}, u32[]{:S(2)}) collective-permute-start(bf16[64,256]{1,0:T(8,128)(2,1)S(1)} %row_share.1.refs_0_), channel_id=1, source_target_pairs={{0,4},{12,8},{1,5},{13,9},{2,6},{14,10},{3,7},{15,11},{16,20},{28,... | collective-permute-start | bytes 98312 | tf_op jit(solution)/shard_map/ppermute | solution.py:548
  50.8 13.6 %collective-permute-start.8 = (bf16[256,1024]{1,0:T(8,128)(2,1)S(1)}, bf16[256,1024]{1,0:T(8,128)(2,1)S(1)}, u32[]{:S(2)}, u32[]{:S(2)}) collective-permute-start(bf16[256,1024]{1,0:T(8,128)(2,1)S(1)} %products.4), channel_id=1, source_target_pairs={{0,4},{12,8},{1,5},{13,9},{2,6},{14,10},{3,7},{15,11},{16,20},{28,... | collective-permute-start | bytes 1572872 | tf_op jit(solution)/shard_map/ppermute | solution.py:528
  53.7 23.2 %collective-permute-start.10 = (bf16[256,1024]{1,0:T(8,128)(2,1)S(1)}, bf16[256,1024]{1,0:T(8,128)(2,1)S(1)}, u32[]{:S(2)}, u32[]{:S(2)}) collective-permute-start(bf16[256,1024]{1,0:T(8,128)(2,1)S(1)} %products.5), channel_id=1, source_target_pairs={{0,4},{12,8},{1,5},{13,9},{2,6},{14,10},{3,7},{15,11},{16,20},{28,... | collective-permute-start | bytes 1572872 | tf_op jit(solution)/shard_map/ppermute | solution.py:528
  56.7 4.9 %collective-permute-start.7 = (bf16[64,256]{1,0:T(8,128)(2,1)S(1)}, bf16[64,256]{1,0:T(8,128)(2,1)S(1)}, u32[]{:S(2)}, u32[]{:S(2)}) collective-permute-start(bf16[64,256]{1,0:T(8,128)(2,1)S(1)} %hop.3.refs_0_), channel_id=1, source_target_pairs={{4,8},{8,4},{5,9},{9,5},{6,10},{10,6},{7,11},{11,7},{20,24},{24,20... | collective-permute-start | bytes 98312 | tf_op jit(solution)/shard_map/ppermute | solution.py:548
  61.6 15.2 %collective-permute-start.9 = (bf16[64,256]{1,0:T(8,128)(2,1)S(1)}, bf16[64,256]{1,0:T(8,128)(2,1)S(1)}, u32[]{:S(2)}, u32[]{:S(2)}) collective-permute-start(bf16[64,256]{1,0:T(8,128)(2,1)S(1)} %hop.4.refs_0_), channel_id=1, source_target_pairs={{4,0},{8,12},{5,1},{9,13},{6,2},{10,14},{7,3},{11,15},{20,16},{24,... | collective-permute-start | bytes 98312 | tf_op jit(solution)/shard_map/ppermute | solution.py:548
  64.5 22.0 %collective-permute-start.12 = (bf16[256,1024]{1,0:T(8,128)(2,1)S(1)}, bf16[256,1024]{1,0:T(8,128)(2,1)S(1)}, u32[]{:S(2)}, u32[]{:S(2)}) collective-permute-start(bf16[256,1024]{1,0:T(8,128)(2,1)S(1)} %operand.6), channel_id=1, source_target_pairs={{4,8},{8,4},{5,9},{9,5},{6,10},{10,6},{7,11},{11,7},{20,24},{24,20... | collective-permute-start | bytes 1572872 | tf_op jit(solution)/shard_map/ppermute | solution.py:528
  65.2 24.3 %collective-permute-start.14 = (bf16[256,1024]{1,0:T(8,128)(2,1)S(1)}, bf16[256,1024]{1,0:T(8,128)(2,1)S(1)}, u32[]{:S(2)}, u32[]{:S(2)}) collective-permute-start(bf16[256,1024]{1,0:T(8,128)(2,1)S(1)} %get-tuple-element.92), channel_id=1, source_target_pairs={{0,4},{12,8},{1,5},{13,9},{2,6},{14,10},{3,7},{15,11},{16,20},{28,... | collective-permute-start | bytes 1572872 | tf_op jit(solution)/shard_map/ppermute | solution.py:528
  77.0 13.4 %collective-permute-start.15 = (bf16[256,1024]{1,0:T(8,128)(2,1)S(1)}, bf16[256,1024]{1,0:T(8,128)(2,1)S(1)}, u32[]{:S(2)}, u32[]{:S(2)}) collective-permute-start(bf16[256,1024]{1,0:T(8,128)(2,1)S(1)} %operand.7), channel_id=1, source_target_pairs={{4,8},{8,4},{5,9},{9,5},{6,10},{10,6},{7,11},{11,7},{20,24},{24,20... | collective-permute-start | bytes 1572872 | tf_op jit(solution)/shard_map/ppermute | solution.py:528
  77.7 20.4 %collective-permute-start.16 = (bf16[256,1024]{1,0:T(8,128)(2,1)S(1)}, bf16[256,1024]{1,0:T(8,128)(2,1)S(1)}, u32[]{:S(2)}, u32[]{:S(2)}) collective-permute-start(bf16[256,1024]{1,0:T(8,128)(2,1)S(1)} %get-tuple-element.96), channel_id=1, source_target_pairs={{0,4},{12,8},{1,5},{13,9},{2,6},{14,10},{3,7},{15,11},{16,20},{28,... | collective-permute-start | bytes 1572872 | tf_op jit(solution)/shard_map/ppermute | solution.py:528
  83.8 1.3 %collective-permute-start.11 = (bf16[64,256]{1,0:T(8,128)(2,1)S(1)}, bf16[64,256]{1,0:T(8,128)(2,1)S(1)}, u32[]{:S(2)}, u32[]{:S(2)}) collective-permute-start(bf16[64,256]{1,0:T(8,128)(2,1)S(1)} %hop.5.refs_0_), channel_id=1, source_target_pairs={{0,1},{1,0},{2,3},{3,2},{4,5},{5,4},{6,7},{7,6},{8,9},{9,8},{10,11... | collective-permute-start | bytes 98312 | tf_op jit(solution)/shard_map/ppermute | solution.py:465
  85.1 4.4 %collective-permute-start.13 = (bf16[128,256]{1,0:T(8,128)(2,1)S(1)}, bf16[128,256]{1,0:T(8,128)(2,1)S(1)}, u32[]{:S(2)}, u32[]{:S(2)}) collective-permute-start(bf16[128,256]{1,0:T(8,128)(2,1)S(1)} %side.6.refs_0_), channel_id=1, source_target_pairs={{0,2},{2,0},{1,3},{3,1},{4,6},{6,4},{5,7},{7,5},{8,10},{10,8},{9,1... | collective-permute-start | bytes 196616 | tf_op jit(solution)/shard_map/ppermute | solution.py:465
  89.4 19.9 %collective-permute-start.17 = (bf16[256,1024]{1,0:T(8,128)(2,1)S(1)}, bf16[256,1024]{1,0:T(8,128)(2,1)S(1)}, u32[]{:S(2)}, u32[]{:S(2)}) collective-permute-start(bf16[256,1024]{1,0:T(8,128)(2,1)S(1)} %operand.8), channel_id=1, source_target_pairs={{0,4},{8,12},{4,0},{12,8},{1,5},{9,13},{5,1},{13,9},{2,6},{10,14},... | collective-permute-start | bytes 1572872 | tf_op jit(solution)/shard_map/ppermute | solution.py:528
  89.7 19.6 %collective-permute-start.18 = (bf16[256,1024]{1,0:T(8,128)(2,1)S(1)}, bf16[256,1024]{1,0:T(8,128)(2,1)S(1)}, u32[]{:S(2)}, u32[]{:S(2)}) collective-permute-start(bf16[256,1024]{1,0:T(8,128)(2,1)S(1)} %operand.9), channel_id=1, source_target_pairs={{4,8},{8,4},{5,9},{9,5},{6,10},{10,6},{7,11},{11,7},{20,24},{24,20... | collective-permute-start | bytes 1572872 | tf_op jit(solution)/shard_map/ppermute | solution.py:528
  98.2 12.3 %collective-permute-start.20 = (bf16[256,1024]{1,0:T(8,128)(2,1)S(1)}, bf16[256,1024]{1,0:T(8,128)(2,1)S(1)}, u32[]{:S(2)}, u32[]{:S(2)}) collective-permute-start(bf16[256,1024]{1,0:T(8,128)(2,1)S(1)} %operand.11), channel_id=1, source_target_pairs={{4,8},{8,4},{5,9},{9,5},{6,10},{10,6},{7,11},{11,7},{20,24},{24,20... | collective-permute-start | bytes 1572872 | tf_op jit(solution)/shard_map/ppermute | solution.py:528
  98.9 20.8 %collective-permute-start.19 = (bf16[256,1024]{1,0:T(8,128)(2,1)S(1)}, bf16[256,1024]{1,0:T(8,128)(2,1)S(1)}, u32[]{:S(2)}, u32[]{:S(2)}) collective-permute-start(bf16[256,1024]{1,0:T(8,128)(2,1)S(1)} %operand.10), channel_id=1, source_target_pairs={{0,4},{8,12},{4,0},{12,8},{1,5},{9,13},{5,1},{13,9},{2,6},{10,14},... | collective-permute-start | bytes 1572872 | tf_op jit(solution)/shard_map/ppermute | solution.py:528

commit v9 on v8

--- a/solution.py
+++ b/solution.py
@@ -50,19 +50,16 @@
 
 
 def load_kernel(
-    tile, genes, counts, tile_mask, tile_counts,
-    gram, factor, theirs, mine, genes_held, counts_held,
-    mask_here, counts_here, mask_scalars, counts_scalars, gene_sems, row_sems, small_sems,
+    genes, counts, tile_mask, tile_counts, gram, factor, turned, upper,
+    genes_here, mask_here, counts_here, gene_sems, row_sems, small_sems,
 ):
-    small = [(tile_mask, mask_here), (tile_counts, counts_here)]
-    small += [(tile_mask, mask_scalars), (tile_counts, counts_scalars)]
     small_copies = [
-        pltpu.make_async_copy(source, target, small_sems.at[i])
-        for i, (source, target) in enumerate(small)
+        pltpu.make_async_copy(tile_mask, mask_here, small_sems.at[0]),
+        pltpu.make_async_copy(tile_counts, counts_here, small_sems.at[1]),
     ]
-    gene_copies = row_copies(genes, genes_held, 0, gene_sems)
-    row_starts = row_copies(counts, counts_held, 0, row_sems)
-    for copy in small_copies + gene_copies + row_starts:
+    gene_copies = row_copies(genes, genes_here, 0, gene_sems)
+    upper_copies = row_copies(counts, upper, 0, row_sems)
+    for copy in gene_copies + small_copies + upper_copies:
         copy.start()
     for copy in small_copies:
         copy.wait()
@@ -71,88 +68,123 @@
         copy.wait()
     columns = genes.shape[1]
     wide = min(1024, columns)
-    part = None
-    for start in range(0, columns, wide):
-        piece = genes_held[:, start : start + wide]
-        product = contract_last(piece, piece)
-        part = product if part is None else part + product
-    gram[...] = part
-
-    rows = counts.shape[0]
-    half = rows // 2
-    at_once = min(4, columns // tile)
-
-    def scale(row, place):
-        above = jnp.full((1, tile), mask_scalars[row, place].astype(F32), F32)
-        return above / jnp.full((1, tile), counts_scalars[row, place].astype(F32), F32)
-
-    def half_cross(side, out):
-        out[...] = jnp.zeros_like(out)
-
-        @pl.loop(0, columns // (tile * at_once))
-        def _(step):
-            total = None
-            for col in range(at_once):
-                place = step * at_once + col
-                at = pl.ds(pl.multiple_of(place * tile, tile), tile)
-                product = contract_last(
-                    genes_held[:, at], counts_held[side * half : (side + 1) * half, at]
-                )
-                first = side * (half // tile)
-                scales = jnp.concatenate(
-                    [scale(first + row, place) for row in range(half // tile)], axis=1
-                )
-                product = scales * product
-                total = product if total is None else total + product
-            out[...] += total
-
-    core = lax.axis_index("sub")
-    per_half = len(row_starts) // 2
-    for side in (0, 1):
-        for copy in row_starts[side * per_half : (side + 1) * per_half]:
-            copy.wait()
-
-        @pl.when(core == side)
-        def _(side=side):
-            half_cross(side, mine)
-
-        @pl.when(core != side)
-        def _(side=side):
-            half_cross(side, theirs)
+    gram[...] = jnp.zeros_like(gram)
+
+    @pl.loop(0, columns // wide)
+    def _(step):
+        at = pl.ds(pl.multiple_of(step * wide, wide), wide)
+        piece = genes_here[:, at]
+        turned[at, :] = piece.T
+        gram[...] += jnp.dot(piece, turned[at, :], preferred_element_type=F32)
+
+    for copy in upper_copies:
+        copy.wait()
 
 
 def load(genes, counts, tile_mask, tile_counts):
     width, columns = genes.shape
     rows = counts.shape[0]
-    tile = rows // tile_mask.shape[0]
     here = pl.BlockSpec(memory_space=pltpu.VMEM)
     there = pl.BlockSpec(memory_space=pltpu.HBM)
-    half = jax.ShapeDtypeStruct((width, rows // 2), F32)
     return pl.pallas_call(
-        functools.partial(load_kernel, tile),
+        load_kernel,
         out_shape=(
             jax.ShapeDtypeStruct((width, width), F32),
             jax.ShapeDtypeStruct(tile_mask.shape, F32),
-            half,
-            half,
-            pltpu.VMEM((width, columns), BF16),
-            pltpu.VMEM((rows, columns), BF16),
+            pltpu.VMEM((columns, width), BF16),
+            pltpu.VMEM((rows // 2, columns), BF16),
         ),
         in_specs=[there] * 4,
-        out_specs=(here,) * 6,
+        out_specs=(here,) * 4,
         scratch_shapes=[
+            pltpu.VMEM((width, columns), BF16),
             pltpu.VMEM(tile_mask.shape, jnp.int32),
             pltpu.VMEM(tile_mask.shape, jnp.int32),
-            pltpu.SMEM(tile_mask.shape, jnp.int32),
-            pltpu.SMEM(tile_mask.shape, jnp.int32),
             pltpu.SemaphoreType.DMA((4,)),
-            pltpu.SemaphoreType.DMA((16,)),
-            pltpu.SemaphoreType.DMA((4,)),
+            pltpu.SemaphoreType.DMA((8,)),
+            pltpu.SemaphoreType.DMA((2,)),
         ],
         compiler_params=params(),
         cost_estimate=cost(1, 1),
         name="load",
     )(away(genes), away(counts), away(tile_mask), away(tile_counts))
+
+
+def add_cross(first_row, start, stop, factor, counts, turned, total):
+    tile = counts.shape[1] // factor.shape[1]
+    at_once = min(4, stop - start)
+
+    @pl.loop(start // at_once, stop // at_once)
+    def _(step):
+        sums = None
+        for col in range(at_once):
+            place = step * at_once + col
+            at = pl.ds(pl.multiple_of(place * tile, tile), tile)
+            product = jnp.dot(counts[:, at], turned[at, :], preferred_element_type=F32)
+            product = jnp.concatenate(
+                [
+                    product[row * tile : (row + 1) * tile] * factor[first_row + row, place]
+                    for row in range(counts.shape[0] // tile)
+                ],
+                axis=0,
+            )
+            sums = product if sums is None else sums + product
+        total[...] += sums
+
+
+def cross_early_kernel(split, factor, upper, turned, counts, high, low, lower, total, sems):
+    half = upper.shape[0]
+    copies = row_copies(counts, lower, half, sems)
+    for copy in copies:
+        copy.start()
+    gene_tiles = factor.shape[1]
+    total[...] = jnp.zeros_like(total)
+    add_cross(0, 0, gene_tiles, factor, upper, turned, total)
+    high[...] = total[...].T
+    for copy in copies:
+        copy.wait()
+    low[...] = jnp.zeros_like(low)
+    add_cross(factor.shape[0] // 2, 0, split, factor, lower, turned, low)
+
+
+def cross_early(split, factor, upper, turned, counts):
+    half, columns = upper.shape
+    width = turned.shape[1]
+    here = pl.BlockSpec(memory_space=pltpu.VMEM)
+    return pl.pallas_call(
+        functools.partial(cross_early_kernel, split),
+        out_shape=(
+            jax.ShapeDtypeStruct((width, half), F32),
+            jax.ShapeDtypeStruct((half, width), F32),
+            pltpu.VMEM((half, columns), BF16),
+        ),
+        in_specs=[
+            pl.BlockSpec(memory_space=pltpu.SMEM),
+            here,
+            here,
+            pl.BlockSpec(memory_space=pltpu.HBM),
+        ],
+        out_specs=(here,) * 3,
+        scratch_shapes=[pltpu.VMEM((half, width), F32), pltpu.SemaphoreType.DMA((8,))],
+        compiler_params=params(),
+        cost_estimate=cost(1, 1),
+        name="cross_early",
+    )(factor, held(upper), held(turned), away(counts))
+
+
+def cross_late_kernel(split, factor, high, low, lower, turned, theirs, mine, total):
+    total[...] = low[...]
+    add_cross(factor.shape[0] // 2, split, factor.shape[1], factor, lower, turned, total)
+
+    @pl.when(lax.axis_index("sub") == 0)
+    def _():
+        mine[...] = high[...]
+        theirs[...] = total[...].T
+
+    @pl.when(lax.axis_index("sub") != 0)
+    def _():
+        theirs[...] = high[...]
+        mine[...] = total[...].T
 
 
 def call(kernel, name, out_shape, token, *args, scratch=(), smem=0, aliases=None, out=None):
@@ -307,10 +339,10 @@
     columns_out[...] = zvalue.astype(BF16)
 
 
-def products_kernel(tile, line, start, chunk, factor, counts, columns, *outs):
+def products_kernel(tile, line, start, chunk, factor, upper, lower, columns, *outs):
     only_first = len(outs) == 1
     block = line.block(1 if only_first else 2, 0)
-    size = counts.shape[1] // line.size
+    size = upper.shape[1] // line.size
     span = min(tile, chunk)
     wide = 2 * span if chunk % (2 * span) == 0 else span
     steps = chunk // wide
@@ -322,9 +354,10 @@
         first = pl.multiple_of(order * size + start + step * wide, span)
         total = None
         for row in range(row_tiles):
+            counts, place = (upper, row) if row < row_tiles // 2 else (lower, row - row_tiles // 2)
             part = jnp.dot(
                 columns[:, row * tile : (row + 1) * tile],
-                counts[row * tile : (row + 1) * tile, pl.ds(first, wide)],
+                counts[place * tile : (place + 1) * tile, pl.ds(first, wide)],
                 preferred_element_type=F32,
             )
             scales = [
@@ -345,7 +378,7 @@
                 outs[1][:, at] = total
 
 
-def products(only_first, line, start, chunk, token, factor, counts, columns):
+def products(only_first, line, start, chunk, token, factor, upper, lower, columns):
     width, rows = columns.shape
     tile = rows // factor.shape[0]
     out_shape = (jax.ShapeDtypeStruct((width, chunk), BF16),)
@@ -353,7 +386,7 @@
         out_shape = (jax.ShapeDtypeStruct((line.size, width, chunk), BF16),) + out_shape
     return call(
         functools.partial(products_kernel, tile, line, start, chunk),
-        "products", out_shape, token, factor, held(counts), columns, smem=1,
+        "products", out_shape, token, factor, held(upper), held(lower), columns, smem=1,
     )
 
 
@@ -366,16 +399,20 @@
     return call(turn_kernel, "turn", shape, token, value)
 
 
-def row_share_kernel(subs, columns, out):
+def row_share_kernel(columns, out):
     part = out.shape[0]
-    place = lax.axis_index("gene") * subs + lax.axis_index("sub")
+    place = lax.axis_index("gene")
     share = columns[pl.ds(pl.multiple_of(place * part, part), part), :]
     out[...] = contract_last(share, columns[...]).astype(out.dtype)
 
 
-def row_share(subs, part, token, columns):
+def row_share(part, token, columns):
     shape = jax.ShapeDtypeStruct((part, columns.shape[0]), BF16)
-    return call(functools.partial(row_share_kernel, subs), "row_share", shape, token, columns)
+    return call(row_share_kernel, "row_share", shape, token, columns)
+
+
+def plus_kernel(left, right, out):
+    out[...] = (left[...].astype(F32) + right[...].astype(F32)).astype(out.dtype)
 
 
 def hop_kernel(kind, targets, own, arrived, out):
@@ -471,7 +508,7 @@
         arrived, event = after(swap(value, axis, size, step), event)
         value = value + arrived
         step *= 2
-    return value
+    return value, event
 
 
 def after(value, event):
@@ -488,18 +525,23 @@
     width = gene_factor.shape[0]
     line = Line(cells)
 
-    gram, factor, theirs, mine, _, counts_held = load(
-        gene_factor, counts, tile_mask, tile_counts
-    )
+    gram, factor, turned, upper = load(gene_factor, counts, tile_mask, tile_counts)
     token = factor
+    split = tile_mask.shape[1] // 8 * 4
+    high, low, lower = cross_early(split, factor, upper, turned, counts)
+    gram, low = pair_sums(gram, "gene", genes, low)
+    half = jax.ShapeDtypeStruct((width, rows // 2), F32)
+    theirs, mine = call(
+        functools.partial(cross_late_kernel, split), "cross_late", (half, half), token,
+        factor, high, low, held(lower), held(turned),
+        smem=1, scratch=[pltpu.VMEM((rows // 2, width), F32)],
+    )
     arrived = swap(theirs, "sub", subs, 1)
     cross_a, cross_b = mine, arrived
     bit = genes // 2
     while bit:
         cross_a, sent = fold("gene", bit, token, cross_a, cross_b)
         cross_b = swap(sent, "gene", genes, bit)
-        if bit == genes // 2:
-            gram = pair_sums(gram, "gene", genes, cross_a)
         bit //= 2
     gram_other = swap(gram, "sub", subs, 1)
     inverse, rho = shifted_inverse(gram, gram_other)
@@ -513,6 +555,7 @@
         columns_arrived = swap(columns_held, "gene", genes, bit)
         columns_held = side("gene", bit, 1, token, columns_held, columns_arrived)
         bit *= 2
+    token, rows_sum = after(token, row_share(width // genes, token, columns_held))
     columns_arrived = swap(columns_held, "sub", subs, 1)
     whole = side("sub", 1, 1, token, columns_held, columns_arrived)
 
@@ -553,10 +596,9 @@
         rows_arrived = swap(rows_sum, axis, size, bit)
         return after(token, side(axis, bit, 0, token, rows_sum, rows_arrived))
 
-    token, rows_sum = after(token, row_share(subs, width // (genes * subs), token, whole))
     for index in every:
         (first,) = products(
-            True, line, starts[index], chunks[index], token, factor, counts_held, whole
+            True, line, starts[index], chunks[index], token, factor, upper, lower, whole
         )
         token, first = after(token, first)
         for parity in (0, 1):
@@ -566,7 +608,7 @@
     totals, seconds = [], []
     for index in every:
         total, second = products(
-            False, line, starts[index], chunks[index], token, factor, counts_held, whole
+            False, line, starts[index], chunks[index], token, factor, upper, lower, whole
         )
         token, second = after(token, second)
         if hops:
@@ -579,7 +621,9 @@
         token, rows_sum = hop_rows(token, rows_sum)
     new_factor = turn(token, whole)
     token, new_factor = after(token, new_factor)
-    token, rows_sum = side_rows(token, rows_sum, "sub", subs, 1)
+    rows_arrived = swap(rows_sum, "sub", subs, 1)
+    shape = jax.ShapeDtypeStruct(rows_sum.shape, F32)
+    token, rows_sum = after(token, call(plus_kernel, "plus", shape, token, rows_sum, rows_arrived))
     bits = [1 << i for i in range((genes - 1).bit_length())]
     for phase in range(3, cells):
         for index in every:
@@ -595,7 +639,7 @@
             arrived[last, 0, index], arrived[last, 1, index], data_products,
         )
         token, data_products = after(token, data_products)
-    return (new_factor, rows_sum.astype(F32), data_products)
+    return (new_factor, rows_sum, data_products)
 
 
 def solution(mesh):

time: 121 us -> 113 us (0.934)
  waiting for transfers between devices: 40.5 us -> 34.7 us
    ppermute x8, waiting for transfers between devices: 18 us -> 11.9 us  [swap(): return lax.ppermute(value, axis, [(i, i ^ step) for i in range(size)])]
    pallas_call x1 -> x2, Pallas kernels: 18 us -> 14 us  [the longest x1 7.69 us: load(): pl.pallas_call(load_kernel, out_shape=(jax.ShapeDtypeStruct((width, width...]
    pallas_call x23 -> x24, Pallas kernels: 17.1 us -> 20.3 us  [call(): pl.pallas_call(lambda token, *refs: kernel(*refs), out_shape=out_shape, i...]
    ppermute x10, starting transfers between devices: 25.9 us -> 24.7 us  [send(): lax.ppermute(value, 'cell', pairs)]
  transfers between devices with their start and end apart: 21 -> 21, of which waited for: 10 -> 9; matrix products, arithmetic and copies ran while one was open for 1% -> 0% of each run, Pallas kernels for 15% -> 22%
where the time goes in v9:
time: 113 us
  starting transfers between devices  39.4 us (35%)
  Pallas kernels  37.8 us (33%)
  waiting for transfers between devices  34.7 us (31%)
    ppermute x10, starting transfers between devices, send(): lax.ppermute(value, 'cell', pairs)  24.7 us
    ppermute x10, waiting for transfers between devices, send(): lax.ppermute(value, 'cell', pairs)  22.7 us
    pallas_call x24, Pallas kernels, call(): pl.pallas_call(lambda token, *refs: kernel(*refs), out_shape=out_shape, i...  20.3 us
    ppermute x8, waiting for transfers between devices, swap(): return lax.ppermute(value, axis, [(i, i ^ step) for i in range(size)])  11.9 us
    ppermute x8, starting transfers between devices, swap(): return lax.ppermute(value, axis, [(i, i ^ step) for i in range(size)])  8.95 us
    pallas_call x1, Pallas kernels, load(): pl.pallas_call(load_kernel, out_shape=(jax.ShapeDtypeStruct((width, width...  7.69 us
    pallas_call x1, Pallas kernels, cross_early(): pl.pallas_call(functools.partial(cross_early_kernel, split), out_shape=(j...  6.26 us
    ppermute x3, starting transfers between devices, hop_rows(): rows_arrived = lax.ppermute(rows_sum, 'cell', pairs)  5.69 us
  transfers between devices with their start and end apart: 21, of which 9 were waited for; matrix products, arithmetic and copies ran while one was open for 0% of the time, Pallas kernels for 22%

profile of v9, /device:TPU:0, one launch (start us, length us, event | category | flops | bytes accessed | tf_op | source)
XLA Modules:
  0.0 112.8 jit_solution(4674371383652085143)
XLA Ops:
  0.6 7.7 %load.1 = (f32[256,256]{1,0:T(8,128)S(1)}, f32[4,32]{1,0:T(4,128)S(1)}, bf16[8192,256]{1,0:T(8,128)(2,1)S(1)}, bf16[512,8192]{1,0:T(8,128)(2,1)S(1)}) custom-call(bf16[256,8192]{1,0:T(8,128)(2,1)} %genes.1, bf16[1024,8192]{1,0:T(8,128)(2,1)} %counts.3, s32[4,32]{1,0:T(4,128)} %tile_mask.1, s32[4,32]{1,0:T(4,128)} %tile_counts.1), custom_call_target="tpu_custom_call" | custom-call | flops 1 | bytes 1 | tf_op jit(solution)/shard_map/load/pallas_call | solution.py:89
  8.3 3.0 %collective-permute-start = (f32[256,256]{1,0:T(8,128)S(1)}, f32[256,256]{1,0:T(8,128)S(1)}, u32[]{:S(2)}, u32[]{:S(2)}) collective-permute-start(f32[256,256]{1,0:T(8,128)S(1)} %get-tuple-element.60), channel_id=1, source_target_pairs={{0,2},{2,0},{1,3},{3,1},{4,6},{6,4},{5,7},{7,5},{8,10},{10,8},{9,1... | collective-permute-start | bytes 786440 | tf_op jit(solution)/shard_map/ppermute | solution.py:502
  11.3 6.3 %cross_early.1 = (f32[256,512]{1,0:T(8,128)S(1)}, f32[512,256]{1,0:T(8,128)S(1)}, bf16[512,8192]{1,0:T(8,128)(2,1)S(1)}) custom-call(f32[4,32]{1,0:T(4,128)S(1)} %get-tuple-element.110.factor.token.refs_0_, bf16[512,8192]{1,0:T(8,128)(2,1)S(1)} %get-tuple-element.61.upper.refs_1_, bf16[8192,256]{1,0:T(8,128)(2,1)S(1)} %get-tuple-element.62.turned.refs_4_, ...), custom_call_target="tpu_custom_call" | custom-call | flops 1 | bytes 1 | tf_op jit(solution)/shard_map/cross_early/pallas_call | solution.py:154
  17.6 0.0 collective-permute-done
  17.6 2.6 %cross_late.1 = (f32[256,512]{1,0:T(8,128)S(1)}, f32[256,512]{1,0:T(8,128)S(1)}) custom-call(f32[4,32]{1,0:T(4,128)S(1)} %get-tuple-element.110.factor.token.refs_0_, f32[4,32]{1,0:T(4,128)S(1)} %get-tuple-element.110.factor.token.refs_0_, f32[256,512]{1,0:T(8,128)S(1)} %get-tuple-element.66.refs_1_, f32[512,256]{1,0:T(8,128)S(1)} %get-tuple-element.67.refs_2_, ...), custom_call_target="tpu_custom_call" | custom-call | flops 1 | bytes 1 | tf_op jit(solution)/shard_map/cross_late/pallas_call | solution.py:199
  20.2 0.1 collective-permute-start.2
  20.4 0.6 collective-permute-start.1
  20.9 1.3 %collective-permute-done.2.refs_1_ = f32[256,512]{1,0:T(8,128)S(1)} collective-permute-done((f32[256,512]{1,0:T(8,128)S(1)}, f32[256,512]{1,0:T(8,128)S(1)}, u32[]{:S(2)}, u32[]{:S(2)}) %collective-permute-start.2) | collective-permute-done | bytes 524320 | tf_op jit(solution)/shard_map/ppermute | solution.py:502
  22.2 0.1 fold.1
  22.3 1.8 %collective-permute-start.3 = (f32[256,256]{1,0:T(8,128)S(1)}, f32[256,256]{1,0:T(8,128)S(1)}, u32[]{:S(2)}, u32[]{:S(2)}) collective-permute-start(f32[256,256]{1,0:T(8,128)S(1)} %get-tuple-element.72), channel_id=1, source_target_pairs={{0,2},{2,0},{1,3},{3,1},{4,6},{6,4},{5,7},{7,5},{8,10},{10,8},{9,1... | collective-permute-start | bytes 786440 | tf_op jit(solution)/shard_map/ppermute | solution.py:502
  24.1 0.0 collective-permute-done.1.gram_b
  24.1 3.5 %inverse.1 = (f32[256,256]{1,0:T(8,128)S(1)}, f32[8,128]{1,0:T(8,128)S(1)}) custom-call(f32[256,256]{1,0:T(8,128)S(1)} %add.3.gram_a, f32[256,256]{1,0:T(8,128)S(1)} %collective-permute-done.1.gram_b), custom_call_target="tpu_custom_call" | custom-call | flops 2013265920 | bytes 786432 | tf_op jit(solution)/shard_map/inverse/pallas_call | solution.py:313
  27.6 3.1 %collective-permute-done.3.refs_2_ = f32[256,256]{1,0:T(8,128)S(1)} collective-permute-done((f32[256,256]{1,0:T(8,128)S(1)}, f32[256,256]{1,0:T(8,128)S(1)}, u32[]{:S(2)}, u32[]{:S(2)}) %collective-permute-start.3) | collective-permute-done | bytes 262176 | tf_op jit(solution)/shard_map/ppermute | solution.py:502
  30.7 0.0 copy-done
  30.7 1.0 admm.1.refs_0_
  31.8 1.8 %collective-permute-start.4 = (bf16[256,256]{1,0:T(8,128)(2,1)S(1)}, bf16[256,256]{1,0:T(8,128)(2,1)S(1)}, u32[]{:S(2)}, u32[]{:S(2)}) collective-permute-start(bf16[256,256]{1,0:T(8,128)(2,1)S(1)} %admm.1.refs_0_), channel_id=1, source_target_pairs={{0,2},{2,0},{1,3},{3,1},{4,6},{6,4},{5,7},{7,5},{8,10},{10,8},{9,1... | collective-permute-start | bytes 393224 | tf_op jit(solution)/shard_map/ppermute | solution.py:502
  33.6 3.2 %collective-permute-done.4.refs_1_ = bf16[256,256]{1,0:T(8,128)(2,1)S(1)} collective-permute-done((bf16[256,256]{1,0:T(8,128)(2,1)S(1)}, bf16[256,256]{1,0:T(8,128)(2,1)S(1)}, u32[]{:S(2)}, u32[]{:S(2)}) %collective-permute-start.4) | collective-permute-done | bytes 131104 | tf_op jit(solution)/shard_map/ppermute | solution.py:502
  36.8 0.1 collective-permute-start.5
  36.9 0.2 row_share.1.refs_0_
  37.1 3.7 %collective-permute-start.6 = (bf16[128,256]{1,0:T(8,128)(2,1)S(1)}, bf16[128,256]{1,0:T(8,128)(2,1)S(1)}, u32[]{:S(2)}, u32[]{:S(2)}) collective-permute-start(bf16[128,256]{1,0:T(8,128)(2,1)S(1)} %row_share.1.refs_0_), channel_id=1, source_target_pairs={{0,4},{12,8},{1,5},{13,9},{2,6},{14,10},{3,7},{15,11},{16,20},{28,... | collective-permute-start | bytes 196616 | tf_op jit(solution)/shard_map/ppermute | solution.py:591
  40.9 0.0 collective-permute-done.5.refs_1_
  40.9 1.5 %products.4 = bf16[256,1024]{1,0:T(8,128)(2,1)S(1)} custom-call(f32[4,32]{1,0:T(4,128)S(1)} %get-tuple-element.110.factor.token.refs_0_, f32[4,32]{1,0:T(4,128)S(1)} %get-tuple-element.110.factor.token.refs_0_, bf16[512,8192]{1,0:T(8,128)(2,1)S(1)} %get-tuple-element.61.upper.refs_1_, bf16[512,8192]{1,0:T(8,128)(2,1)S(1)} %get-tuple-element.68.refs_3_.refs_2_, ...), custom_call_target="tpu_custom_call" | custom-call | flops 1 | bytes 1 | tf_op jit(solution)/shard_map/products/pallas_call | solution.py:199
  42.4 1.3 %collective-permute-start.8 = (bf16[256,1024]{1,0:T(8,128)(2,1)S(1)}, bf16[256,1024]{1,0:T(8,128)(2,1)S(1)}, u32[]{:S(2)}, u32[]{:S(2)}) collective-permute-start(bf16[256,1024]{1,0:T(8,128)(2,1)S(1)} %products.4), channel_id=1, source_target_pairs={{0,4},{12,8},{1,5},{13,9},{2,6},{14,10},{3,7},{15,11},{16,20},{28,... | collective-permute-start | bytes 1572872 | tf_op jit(solution)/shard_map/ppermute | solution.py:571
  43.7 0.0 collective-permute-done.6.refs_1_
  43.8 1.5 %products.5 = bf16[256,1024]{1,0:T(8,128)(2,1)S(1)} custom-call(f32[4,32]{1,0:T(4,128)S(1)} %get-tuple-element.110.factor.token.refs_0_, f32[4,32]{1,0:T(4,128)S(1)} %get-tuple-element.110.factor.token.refs_0_, bf16[512,8192]{1,0:T(8,128)(2,1)S(1)} %get-tuple-element.61.upper.refs_1_, bf16[512,8192]{1,0:T(8,128)(2,1)S(1)} %get-tuple-element.68.refs_3_.refs_2_, ...), custom_call_target="tpu_custom_call" | custom-call | flops 1 | bytes 1 | tf_op jit(solution)/shard_map/products/pallas_call | solution.py:199
  45.3 3.5 %collective-permute-start.10 = (bf16[256,1024]{1,0:T(8,128)(2,1)S(1)}, bf16[256,1024]{1,0:T(8,128)(2,1)S(1)}, u32[]{:S(2)}, u32[]{:S(2)}) collective-permute-start(bf16[256,1024]{1,0:T(8,128)(2,1)S(1)} %products.5), channel_id=1, source_target_pairs={{0,4},{12,8},{1,5},{13,9},{2,6},{14,10},{3,7},{15,11},{16,20},{28,... | collective-permute-start | bytes 1572872 | tf_op jit(solution)/shard_map/ppermute | solution.py:571
  48.8 0.7 collective-permute-start.7
  49.5 4.2 %products.6 = (bf16[4,256,1024]{2,1,0:T(8,128)(2,1)S(1)}, bf16[256,1024]{1,0:T(8,128)(2,1)S(1)}) custom-call(f32[4,32]{1,0:T(4,128)S(1)} %get-tuple-element.110.factor.token.refs_0_, f32[4,32]{1,0:T(4,128)S(1)} %get-tuple-element.110.factor.token.refs_0_, bf16[512,8192]{1,0:T(8,128)(2,1)S(1)} %get-tuple-element.61.upper.refs_1_, ...), custom_call_target="tpu_custom_call" | custom-call | flops 1 | bytes 1 | tf_op jit(solution)/shard_map/products/pallas_call | solution.py:199
  53.7 0.0 collective-permute-done.7.refs_1_
  53.8 1.3 %collective-permute-start.9 = (bf16[128,256]{1,0:T(8,128)(2,1)S(1)}, bf16[128,256]{1,0:T(8,128)(2,1)S(1)}, u32[]{:S(2)}, u32[]{:S(2)}) collective-permute-start(bf16[128,256]{1,0:T(8,128)(2,1)S(1)} %hop.4.refs_0_), channel_id=1, source_target_pairs={{4,0},{8,12},{5,1},{9,13},{6,2},{10,14},{7,3},{11,15},{20,16},{24,... | collective-permute-start | bytes 196616 | tf_op jit(solution)/shard_map/ppermute | solution.py:591
  55.1 4.6 %collective-permute-start.14 = (bf16[256,1024]{1,0:T(8,128)(2,1)S(1)}, bf16[256,1024]{1,0:T(8,128)(2,1)S(1)}, u32[]{:S(2)}, u32[]{:S(2)}) collective-permute-start(bf16[256,1024]{1,0:T(8,128)(2,1)S(1)} %get-tuple-element.102), channel_id=1, source_target_pairs={{0,4},{12,8},{1,5},{13,9},{2,6},{14,10},{3,7},{15,11},{16,20},{28,... | collective-permute-start | bytes 1572872 | tf_op jit(solution)/shard_map/ppermute | solution.py:571
  59.7 0.0 collective-permute-done.8.refs_1_
  59.7 0.1 operand.6
  59.8 0.7 collective-permute-start.12
  60.5 4.3 %products.7 = (bf16[4,256,1024]{2,1,0:T(8,128)(2,1)S(1)}, bf16[256,1024]{1,0:T(8,128)(2,1)S(1)}) custom-call(f32[4,32]{1,0:T(4,128)S(1)} %get-tuple-element.110.factor.token.refs_0_, f32[4,32]{1,0:T(4,128)S(1)} %get-tuple-element.110.factor.token.refs_0_, bf16[512,8192]{1,0:T(8,128)(2,1)S(1)} %get-tuple-element.61.upper.refs_1_, ...), custom_call_target="tpu_custom_call" | custom-call | flops 1 | bytes 1 | tf_op jit(solution)/shard_map/products/pallas_call | solution.py:199
  64.8 0.0 collective-permute-done.9.refs_1_
  64.8 2.4 %collective-permute-done.10.refs_1_ = bf16[256,1024]{1,0:T(8,128)(2,1)S(1)} collective-permute-done((bf16[256,1024]{1,0:T(8,128)(2,1)S(1)}, bf16[256,1024]{1,0:T(8,128)(2,1)S(1)}, u32[]{:S(2)}, u32[]{:S(2)}) %collective-permute-start.10) | collective-permute-done | bytes 524320 | tf_op jit(solution)/shard_map/ppermute | solution.py:571
  67.2 0.1 operand.7
  67.3 0.7 collective-permute-start.15
  68.0 7.2 %collective-permute-start.16 = (bf16[256,1024]{1,0:T(8,128)(2,1)S(1)}, bf16[256,1024]{1,0:T(8,128)(2,1)S(1)}, u32[]{:S(2)}, u32[]{:S(2)}) collective-permute-start(bf16[256,1024]{1,0:T(8,128)(2,1)S(1)} %get-tuple-element.106), channel_id=1, source_target_pairs={{0,4},{12,8},{1,5},{13,9},{2,6},{14,10},{3,7},{15,11},{16,20},{28,... | collective-permute-start | bytes 1572872 | tf_op jit(solution)/shard_map/ppermute | solution.py:571
  75.2 0.1 collective-permute-start.11
  75.3 1.0 turn.1
  76.3 0.2 collective-permute-done.11.refs_1_
  76.6 1.6 %collective-permute-start.13 = (f32[128,256]{1,0:T(8,128)S(1)}, f32[128,256]{1,0:T(8,128)S(1)}, u32[]{:S(2)}, u32[]{:S(2)}) collective-permute-start(f32[128,256]{1,0:T(8,128)S(1)} %plus.1.refs_0_), channel_id=1, source_target_pairs={{0,2},{2,0},{1,3},{3,1},{4,6},{6,4},{5,7},{7,5},{8,10},{10,8},{9,1... | collective-permute-start | bytes 393224 | tf_op jit(solution)/shard_map/ppermute | solution.py:502
  78.1 0.0 collective-permute-done.12.refs_1_
  78.1 0.1 operand.8
  78.3 4.0 %collective-permute-done.13.refs_1_ = f32[128,256]{1,0:T(8,128)S(1)} collective-permute-done((f32[128,256]{1,0:T(8,128)S(1)}, f32[128,256]{1,0:T(8,128)S(1)}, u32[]{:S(2)}, u32[]{:S(2)}) %collective-permute-start.13) | collective-permute-done | bytes 131104 | tf_op jit(solution)/shard_map/ppermute | solution.py:502
  82.3 0.7 side.5
  83.0 0.0 collective-permute-start.17
  83.0 0.0 collective-permute-done.14.refs_1_
  83.0 0.1 operand.9
  83.1 0.0 collective-permute-done.15.refs_1_
  83.2 0.1 operand.10
  83.3 0.7 collective-permute-start.18
  84.0 5.6 %collective-permute-done.16.refs_1_ = bf16[256,1024]{1,0:T(8,128)(2,1)S(1)} collective-permute-done((bf16[256,1024]{1,0:T(8,128)(2,1)S(1)}, bf16[256,1024]{1,0:T(8,128)(2,1)S(1)}, u32[]{:S(2)}, u32[]{:S(2)}) %collective-permute-start.16) | collective-permute-done | bytes 524320 | tf_op jit(solution)/shard_map/ppermute | solution.py:571
  89.6 0.1 operand.11
  89.8 0.7 collective-permute-start.20
  90.5 5.3 %collective-permute-start.19 = (bf16[256,1024]{1,0:T(8,128)(2,1)S(1)}, bf16[256,1024]{1,0:T(8,128)(2,1)S(1)}, u32[]{:S(2)}, u32[]{:S(2)}) collective-permute-start(bf16[256,1024]{1,0:T(8,128)(2,1)S(1)} %operand.10), channel_id=1, source_target_pairs={{0,4},{8,12},{4,0},{12,8},{1,5},{9,13},{5,1},{13,9},{2,6},{10,14},... | collective-permute-start | bytes 1572872 | tf_op jit(solution)/shard_map/ppermute | solution.py:571
  95.8 5.1 %collective-permute-done.17.refs_1_ = bf16[256,1024]{1,0:T(8,128)(2,1)S(1)} collective-permute-done((bf16[256,1024]{1,0:T(8,128)(2,1)S(1)}, bf16[256,1024]{1,0:T(8,128)(2,1)S(1)}, u32[]{:S(2)}, u32[]{:S(2)}) %collective-permute-start.17) | collective-permute-done | bytes 524320 | tf_op jit(solution)/shard_map/ppermute | solution.py:571
  100.9 0.0 collective-permute-done.18.refs_2_
  100.9 1.1 %keep.2.refs_3_ = f32[2048,256]{1,0:T(8,128)} custom-call(f32[4,32]{1,0:T(4,128)S(1)} %get-tuple-element.110.factor.token.refs_0_, bf16[4,256,1024]{2,1,0:T(8,128)(2,1)S(1)} %get-tuple-element.83.refs_0_, bf16[256,1024]{1,0:T(8,128)(2,1)S(1)} %collective-permute-done.17.refs_1_, bf16[256,1024]{1,0:T(8,128)(2,1)S(1)} %collective-permute-done.18.refs_2_), custom_call_target="tpu_custom_call" | custom-call | flops 1 | bytes 1 | tf_op jit(solution)/shard_map/keep/pallas_call | solution.py:199
  102.0 0.0 collective-permute-done.20.refs_2_
  102.0 9.7 %collective-permute-done.19.refs_1_ = bf16[256,1024]{1,0:T(8,128)(2,1)S(1)} collective-permute-done((bf16[256,1024]{1,0:T(8,128)(2,1)S(1)}, bf16[256,1024]{1,0:T(8,128)(2,1)S(1)}, u32[]{:S(2)}, u32[]{:S(2)}) %collective-permute-start.19) | collective-permute-done | bytes 524320 | tf_op jit(solution)/shard_map/ppermute | solution.py:571
  111.7 1.1 %keep.3 = f32[2048,256]{1,0:T(8,128)} custom-call(f32[4,32]{1,0:T(4,128)S(1)} %get-tuple-element.110.factor.token.refs_0_, bf16[4,256,1024]{2,1,0:T(8,128)(2,1)S(1)} %get-tuple-element.90.refs_0_, bf16[256,1024]{1,0:T(8,128)(2,1)S(1)} %collective-permute-done.19.refs_1_, ...), custom_call_target="tpu_custom_call", output_to_operand_aliasing={{}: (4, {})} | custom-call | flops 1 | bytes 1 | tf_op jit(solution)/shard_map/keep/pallas_call | solution.py:199
  (8 shorter events, 0.2 us)
Async XLA Ops:
  8.3 9.3 %collective-permute-start = (f32[256,256]{1,0:T(8,128)S(1)}, f32[256,256]{1,0:T(8,128)S(1)}, u32[]{:S(2)}, u32[]{:S(2)}) collective-permute-start(f32[256,256]{1,0:T(8,128)S(1)} %get-tuple-element.60), channel_id=1, source_target_pairs={{0,2},{2,0},{1,3},{3,1},{4,6},{6,4},{5,7},{7,5},{8,10},{10,8},{9,1... | collective-permute-start | bytes 786440 | tf_op jit(solution)/shard_map/ppermute | solution.py:502
  20.2 2.0 %collective-permute-start.2 = (f32[256,512]{1,0:T(8,128)S(1)}, f32[256,512]{1,0:T(8,128)S(1)}, u32[]{:S(2)}, u32[]{:S(2)}) collective-permute-start(f32[256,512]{1,0:T(8,128)S(1)} %get-tuple-element.70), channel_id=1, source_target_pairs={{0,1},{1,0},{2,3},{3,2},{4,5},{5,4},{6,7},{7,6},{8,9},{9,8},{10,11... | collective-permute-start | bytes 1572872 | tf_op jit(solution)/shard_map/ppermute | solution.py:502
  20.4 3.7 %collective-permute-start.1 = (f32[256,256]{1,0:T(8,128)S(1)}, f32[256,256]{1,0:T(8,128)S(1)}, u32[]{:S(2)}, u32[]{:S(2)}) collective-permute-start(f32[256,256]{1,0:T(8,128)S(1)} %add.3.gram_a), channel_id=1, source_target_pairs={{0,1},{1,0},{2,3},{3,2},{4,5},{5,4},{6,7},{7,6},{8,9},{9,8},{10,11... | collective-permute-start | bytes 786440 | tf_op jit(solution)/shard_map/ppermute | solution.py:502
  22.2 8.5 %copy-start = (bf16[1024,256]{1,0:T(8,128)(2,1)S(1)}, bf16[1024,256]{1,0:T(8,128)(2,1)}, u32[]{:S(2)}) copy-start(bf16[1024,256]{1,0:T(8,128)(2,1)} %refs_4_.1) | copy-start | bytes 1572868
  22.3 8.4 %collective-permute-start.3 = (f32[256,256]{1,0:T(8,128)S(1)}, f32[256,256]{1,0:T(8,128)S(1)}, u32[]{:S(2)}, u32[]{:S(2)}) collective-permute-start(f32[256,256]{1,0:T(8,128)S(1)} %get-tuple-element.72), channel_id=1, source_target_pairs={{0,2},{2,0},{1,3},{3,1},{4,6},{6,4},{5,7},{7,5},{8,10},{10,8},{9,1... | collective-permute-start | bytes 786440 | tf_op jit(solution)/shard_map/ppermute | solution.py:502
  31.8 5.0 %collective-permute-start.4 = (bf16[256,256]{1,0:T(8,128)(2,1)S(1)}, bf16[256,256]{1,0:T(8,128)(2,1)S(1)}, u32[]{:S(2)}, u32[]{:S(2)}) collective-permute-start(bf16[256,256]{1,0:T(8,128)(2,1)S(1)} %admm.1.refs_0_), channel_id=1, source_target_pairs={{0,2},{2,0},{1,3},{3,1},{4,6},{6,4},{5,7},{7,5},{8,10},{10,8},{9,1... | collective-permute-start | bytes 393224 | tf_op jit(solution)/shard_map/ppermute | solution.py:502
  36.8 4.0 %collective-permute-start.5 = (bf16[256,512]{1,0:T(8,128)(2,1)S(1)}, bf16[256,512]{1,0:T(8,128)(2,1)S(1)}, u32[]{:S(2)}, u32[]{:S(2)}) collective-permute-start(bf16[256,512]{1,0:T(8,128)(2,1)S(1)} %side.3.refs_0_), channel_id=1, source_target_pairs={{0,1},{1,0},{2,3},{3,2},{4,5},{5,4},{6,7},{7,6},{8,9},{9,8},{10,11... | collective-permute-start | bytes 786440 | tf_op jit(solution)/shard_map/ppermute | solution.py:502
  37.1 6.6 %collective-permute-start.6 = (bf16[128,256]{1,0:T(8,128)(2,1)S(1)}, bf16[128,256]{1,0:T(8,128)(2,1)S(1)}, u32[]{:S(2)}, u32[]{:S(2)}) collective-permute-start(bf16[128,256]{1,0:T(8,128)(2,1)S(1)} %row_share.1.refs_0_), channel_id=1, source_target_pairs={{0,4},{12,8},{1,5},{13,9},{2,6},{14,10},{3,7},{15,11},{16,20},{28,... | collective-permute-start | bytes 196616 | tf_op jit(solution)/shard_map/ppermute | solution.py:591
  42.4 17.2 %collective-permute-start.8 = (bf16[256,1024]{1,0:T(8,128)(2,1)S(1)}, bf16[256,1024]{1,0:T(8,128)(2,1)S(1)}, u32[]{:S(2)}, u32[]{:S(2)}) collective-permute-start(bf16[256,1024]{1,0:T(8,128)(2,1)S(1)} %products.4), channel_id=1, source_target_pairs={{0,4},{12,8},{1,5},{13,9},{2,6},{14,10},{3,7},{15,11},{16,20},{28,... | collective-permute-start | bytes 1572872 | tf_op jit(solution)/shard_map/ppermute | solution.py:571
  45.3 21.9 %collective-permute-start.10 = (bf16[256,1024]{1,0:T(8,128)(2,1)S(1)}, bf16[256,1024]{1,0:T(8,128)(2,1)S(1)}, u32[]{:S(2)}, u32[]{:S(2)}) collective-permute-start(bf16[256,1024]{1,0:T(8,128)(2,1)S(1)} %products.5), channel_id=1, source_target_pairs={{0,4},{12,8},{1,5},{13,9},{2,6},{14,10},{3,7},{15,11},{16,20},{28,... | collective-permute-start | bytes 1572872 | tf_op jit(solution)/shard_map/ppermute | solution.py:571
  48.8 4.9 %collective-permute-start.7 = (bf16[128,256]{1,0:T(8,128)(2,1)S(1)}, bf16[128,256]{1,0:T(8,128)(2,1)S(1)}, u32[]{:S(2)}, u32[]{:S(2)}) collective-permute-start(bf16[128,256]{1,0:T(8,128)(2,1)S(1)} %hop.3.refs_0_), channel_id=1, source_target_pairs={{4,8},{8,4},{5,9},{9,5},{6,10},{10,6},{7,11},{11,7},{20,24},{24,20... | collective-permute-start | bytes 196616 | tf_op jit(solution)/shard_map/ppermute | solution.py:591
  53.8 11.0 %collective-permute-start.9 = (bf16[128,256]{1,0:T(8,128)(2,1)S(1)}, bf16[128,256]{1,0:T(8,128)(2,1)S(1)}, u32[]{:S(2)}, u32[]{:S(2)}) collective-permute-start(bf16[128,256]{1,0:T(8,128)(2,1)S(1)} %hop.4.refs_0_), channel_id=1, source_target_pairs={{4,0},{8,12},{5,1},{9,13},{6,2},{10,14},{7,3},{11,15},{20,16},{24,... | collective-permute-start | bytes 196616 | tf_op jit(solution)/shard_map/ppermute | solution.py:591
  55.1 27.9 %collective-permute-start.14 = (bf16[256,1024]{1,0:T(8,128)(2,1)S(1)}, bf16[256,1024]{1,0:T(8,128)(2,1)S(1)}, u32[]{:S(2)}, u32[]{:S(2)}) collective-permute-start(bf16[256,1024]{1,0:T(8,128)(2,1)S(1)} %get-tuple-element.102), channel_id=1, source_target_pairs={{0,4},{12,8},{1,5},{13,9},{2,6},{14,10},{3,7},{15,11},{16,20},{28,... | collective-permute-start | bytes 1572872 | tf_op jit(solution)/shard_map/ppermute | solution.py:571
  59.8 18.3 %collective-permute-start.12 = (bf16[256,1024]{1,0:T(8,128)(2,1)S(1)}, bf16[256,1024]{1,0:T(8,128)(2,1)S(1)}, u32[]{:S(2)}, u32[]{:S(2)}) collective-permute-start(bf16[256,1024]{1,0:T(8,128)(2,1)S(1)} %operand.6), channel_id=1, source_target_pairs={{4,8},{8,4},{5,9},{9,5},{6,10},{10,6},{7,11},{11,7},{20,24},{24,20... | collective-permute-start | bytes 1572872 | tf_op jit(solution)/shard_map/ppermute | solution.py:571
  67.3 15.8 %collective-permute-start.15 = (bf16[256,1024]{1,0:T(8,128)(2,1)S(1)}, bf16[256,1024]{1,0:T(8,128)(2,1)S(1)}, u32[]{:S(2)}, u32[]{:S(2)}) collective-permute-start(bf16[256,1024]{1,0:T(8,128)(2,1)S(1)} %operand.7), channel_id=1, source_target_pairs={{4,8},{8,4},{5,9},{9,5},{6,10},{10,6},{7,11},{11,7},{20,24},{24,20... | collective-permute-start | bytes 1572872 | tf_op jit(solution)/shard_map/ppermute | solution.py:571
  68.0 21.6 %collective-permute-start.16 = (bf16[256,1024]{1,0:T(8,128)(2,1)S(1)}, bf16[256,1024]{1,0:T(8,128)(2,1)S(1)}, u32[]{:S(2)}, u32[]{:S(2)}) collective-permute-start(bf16[256,1024]{1,0:T(8,128)(2,1)S(1)} %get-tuple-element.106), channel_id=1, source_target_pairs={{0,4},{12,8},{1,5},{13,9},{2,6},{14,10},{3,7},{15,11},{16,20},{28,... | collective-permute-start | bytes 1572872 | tf_op jit(solution)/shard_map/ppermute | solution.py:571
  75.2 1.3 %collective-permute-start.11 = (bf16[128,256]{1,0:T(8,128)(2,1)S(1)}, bf16[128,256]{1,0:T(8,128)(2,1)S(1)}, u32[]{:S(2)}, u32[]{:S(2)}) collective-permute-start(bf16[128,256]{1,0:T(8,128)(2,1)S(1)} %hop.5.refs_0_), channel_id=1, source_target_pairs={{0,1},{1,0},{2,3},{3,2},{4,5},{5,4},{6,7},{7,6},{8,9},{9,8},{10,11... | collective-permute-start | bytes 196616 | tf_op jit(solution)/shard_map/ppermute | solution.py:502
  76.6 5.7 %collective-permute-start.13 = (f32[128,256]{1,0:T(8,128)S(1)}, f32[128,256]{1,0:T(8,128)S(1)}, u32[]{:S(2)}, u32[]{:S(2)}) collective-permute-start(f32[128,256]{1,0:T(8,128)S(1)} %plus.1.refs_0_), channel_id=1, source_target_pairs={{0,2},{2,0},{1,3},{3,1},{4,6},{6,4},{5,7},{7,5},{8,10},{10,8},{9,1... | collective-permute-start | bytes 393224 | tf_op jit(solution)/shard_map/ppermute | solution.py:502
  83.0 17.9 %collective-permute-start.17 = (bf16[256,1024]{1,0:T(8,128)(2,1)S(1)}, bf16[256,1024]{1,0:T(8,128)(2,1)S(1)}, u32[]{:S(2)}, u32[]{:S(2)}) collective-permute-start(bf16[256,1024]{1,0:T(8,128)(2,1)S(1)} %operand.8), channel_id=1, source_target_pairs={{0,4},{8,12},{4,0},{12,8},{1,5},{9,13},{5,1},{13,9},{2,6},{10,14},... | collective-permute-start | bytes 1572872 | tf_op jit(solution)/shard_map/ppermute | solution.py:571
  83.3 17.6 %collective-permute-start.18 = (bf16[256,1024]{1,0:T(8,128)(2,1)S(1)}, bf16[256,1024]{1,0:T(8,128)(2,1)S(1)}, u32[]{:S(2)}, u32[]{:S(2)}) collective-permute-start(bf16[256,1024]{1,0:T(8,128)(2,1)S(1)} %operand.9), channel_id=1, source_target_pairs={{4,8},{8,4},{5,9},{9,5},{6,10},{10,6},{7,11},{11,7},{20,24},{24,20... | collective-permute-start | bytes 1572872 | tf_op jit(solution)/shard_map/ppermute | solution.py:571
  89.8 12.3 %collective-permute-start.20 = (bf16[256,1024]{1,0:T(8,128)(2,1)S(1)}, bf16[256,1024]{1,0:T(8,128)(2,1)S(1)}, u32[]{:S(2)}, u32[]{:S(2)}) collective-permute-start(bf16[256,1024]{1,0:T(8,128)(2,1)S(1)} %operand.11), channel_id=1, source_target_pairs={{4,8},{8,4},{5,9},{9,5},{6,10},{10,6},{7,11},{11,7},{20,24},{24,20... | collective-permute-start | bytes 1572872 | tf_op jit(solution)/shard_map/ppermute | solution.py:571
  90.5 21.2 %collective-permute-start.19 = (bf16[256,1024]{1,0:T(8,128)(2,1)S(1)}, bf16[256,1024]{1,0:T(8,128)(2,1)S(1)}, u32[]{:S(2)}, u32[]{:S(2)}) collective-permute-start(bf16[256,1024]{1,0:T(8,128)(2,1)S(1)} %operand.10), channel_id=1, source_target_pairs={{0,4},{8,12},{4,0},{12,8},{1,5},{9,13},{5,1},{13,9},{2,6},{10,14},... | collective-permute-start | bytes 1572872 | tf_op jit(solution)/shard_map/ppermute | solution.py:571

commit v10 on v9

--- a/solution.py
+++ b/solution.py
@@ -50,7 +50,7 @@
 
 
 def load_kernel(
-    genes, counts, tile_mask, tile_counts, gram, factor, turned, upper,
+    genes, counts, tile_mask, tile_counts, gram, factor, turned, theirs,
     genes_here, mask_here, counts_here, gene_sems, row_sems, small_sems,
 ):
     small_copies = [
@@ -58,14 +58,18 @@
         pltpu.make_async_copy(tile_counts, counts_here, small_sems.at[1]),
     ]
     gene_copies = row_copies(genes, genes_here, 0, gene_sems)
-    upper_copies = row_copies(counts, upper, 0, row_sems)
-    for copy in gene_copies + small_copies + upper_copies:
+    half = theirs.shape[0]
+    other_core = 1 - lax.axis_index("sub")
+    row_starts = row_copies(counts, theirs, pl.multiple_of(other_core * half, half), row_sems)
+    for copy in gene_copies + small_copies:
         copy.start()
     for copy in small_copies:
         copy.wait()
     factor[...] = mask_here[...].astype(F32) / counts_here[...].astype(F32)
     for copy in gene_copies:
         copy.wait()
+    for copy in row_starts:
+        copy.start()
     columns = genes.shape[1]
     wide = min(1024, columns)
     gram[...] = jnp.zeros_like(gram)
@@ -77,7 +81,7 @@
         turned[at, :] = piece.T
         gram[...] += jnp.dot(piece, turned[at, :], preferred_element_type=F32)
 
-    for copy in upper_copies:
+    for copy in row_starts:
         copy.wait()
 
 
@@ -132,29 +136,35 @@
         total[...] += sums
 
 
-def cross_early_kernel(split, factor, upper, turned, counts, high, low, lower, total, sems):
-    half = upper.shape[0]
-    copies = row_copies(counts, lower, half, sems)
+def cross_early_kernel(
+    split, factor, theirs, turned, counts, cross_a, cross_b, low, mine, total, sems
+):
+    half = theirs.shape[0]
+    core = lax.axis_index("sub")
+    copies = row_copies(counts, mine, pl.multiple_of(core * half, half), sems)
     for copy in copies:
         copy.start()
     gene_tiles = factor.shape[1]
+    row_tiles = factor.shape[0] // 2
     total[...] = jnp.zeros_like(total)
-    add_cross(0, 0, gene_tiles, factor, upper, turned, total)
-    high[...] = total[...].T
+    add_cross((1 - core) * row_tiles, 0, gene_tiles, factor, theirs, turned, total)
+    cross_a[...] = total[: half // 2].T
+    cross_b[...] = total[half // 2 :].T
     for copy in copies:
         copy.wait()
     low[...] = jnp.zeros_like(low)
-    add_cross(factor.shape[0] // 2, 0, split, factor, lower, turned, low)
-
-
-def cross_early(split, factor, upper, turned, counts):
-    half, columns = upper.shape
+    add_cross(core * row_tiles, 0, split, factor, mine, turned, low)
+
+
+def cross_early(split, factor, theirs, turned, counts):
+    half, columns = theirs.shape
     width = turned.shape[1]
     here = pl.BlockSpec(memory_space=pltpu.VMEM)
     return pl.pallas_call(
         functools.partial(cross_early_kernel, split),
         out_shape=(
-            jax.ShapeDtypeStruct((width, half), F32),
+            jax.ShapeDtypeStruct((width, half // 2), F32),
+            jax.ShapeDtypeStruct((width, half // 2), F32),
             jax.ShapeDtypeStruct((half, width), F32),
             pltpu.VMEM((half, columns), BF16),
         ),
@@ -164,27 +174,19 @@
             here,
             pl.BlockSpec(memory_space=pltpu.HBM),
         ],
-        out_specs=(here,) * 3,
+        out_specs=(here,) * 4,
         scratch_shapes=[pltpu.VMEM((half, width), F32), pltpu.SemaphoreType.DMA((8,))],
         compiler_params=params(),
         cost_estimate=cost(1, 1),
         name="cross_early",
-    )(factor, held(upper), held(turned), away(counts))
-
-
-def cross_late_kernel(split, factor, high, low, lower, turned, theirs, mine, total):
+    )(factor, held(theirs), held(turned), away(counts))
+
+
+def cross_late_kernel(split, factor, low, counts, turned, cross, total):
     total[...] = low[...]
-    add_cross(factor.shape[0] // 2, split, factor.shape[1], factor, lower, turned, total)
-
-    @pl.when(lax.axis_index("sub") == 0)
-    def _():
-        mine[...] = high[...]
-        theirs[...] = total[...].T
-
-    @pl.when(lax.axis_index("sub") != 0)
-    def _():
-        theirs[...] = high[...]
-        mine[...] = total[...].T
+    first_row = lax.axis_index("sub") * (factor.shape[0] // 2)
+    add_cross(first_row, split, factor.shape[1], factor, counts, turned, total)
+    cross[...] = total[...].T
 
 
 def call(kernel, name, out_shape, token, *args, scratch=(), smem=0, aliases=None, out=None):
@@ -222,6 +224,29 @@
     def _():
         kept[...] = left[:, :half] + right[:, :half]
         sent[...] = left[:, half:] + right[:, half:]
+
+
+def first_fold_kernel(axis, bit, left, right_low, right_high, kept, sent):
+    half = kept.shape[1]
+    upper = (lax.axis_index(axis) & bit) != 0
+
+    @pl.when(upper)
+    def _():
+        kept[...] = left[:, half:] + right_high[...]
+        sent[...] = left[:, :half] + right_low[...]
+
+    @pl.when(jnp.logical_not(upper))
+    def _():
+        kept[...] = left[:, :half] + right_low[...]
+        sent[...] = left[:, half:] + right_high[...]
+
+
+def first_fold(axis, bit, token, left, right_low, right_high):
+    shape = jax.ShapeDtypeStruct(right_low.shape, F32)
+    return call(
+        functools.partial(first_fold_kernel, axis, bit),
+        "fold", (shape, shape), token, left, right_low, right_high,
+    )
 
 
 def fold(axis, bit, token, left, right):
@@ -339,24 +364,29 @@
     columns_out[...] = zvalue.astype(BF16)
 
 
-def products_kernel(tile, line, start, chunk, factor, upper, lower, columns, *outs):
+def products_kernel(tile, line, start, chunk, factor, theirs, mine, columns, *outs):
     only_first = len(outs) == 1
     block = line.block(1 if only_first else 2, 0)
-    size = upper.shape[1] // line.size
+    size = mine.shape[1] // line.size
     span = min(tile, chunk)
     wide = 2 * span if chunk % (2 * span) == 0 else span
     steps = chunk // wide
-    row_tiles = columns.shape[1] // tile
+    row_tiles = columns.shape[1] // tile // 2
+    core = lax.axis_index("sub")
 
     @pl.loop(0, steps if only_first else line.size * steps)
     def _(turn):
         order, step = (block, turn) if only_first else (turn // steps, lax.rem(turn, steps))
         first = pl.multiple_of(order * size + start + step * wide, span)
         total = None
-        for row in range(row_tiles):
-            counts, place = (upper, row) if row < row_tiles // 2 else (lower, row - row_tiles // 2)
+        for counts, side, place in [
+            (counts, side, place)
+            for counts, side in ((theirs, 1 - core), (mine, core))
+            for place in range(row_tiles)
+        ]:
+            row = side * row_tiles + place
             part = jnp.dot(
-                columns[:, row * tile : (row + 1) * tile],
+                columns[:, pl.ds(pl.multiple_of(row * tile, tile), tile)],
                 counts[place * tile : (place + 1) * tile, pl.ds(first, wide)],
                 preferred_element_type=F32,
             )
@@ -378,7 +408,7 @@
                 outs[1][:, at] = total
 
 
-def products(only_first, line, start, chunk, token, factor, upper, lower, columns):
+def products(only_first, line, start, chunk, token, factor, theirs, mine, columns):
     width, rows = columns.shape
     tile = rows // factor.shape[0]
     out_shape = (jax.ShapeDtypeStruct((width, chunk), BF16),)
@@ -386,7 +416,7 @@
         out_shape = (jax.ShapeDtypeStruct((line.size, width, chunk), BF16),) + out_shape
     return call(
         functools.partial(products_kernel, tile, line, start, chunk),
-        "products", out_shape, token, factor, held(upper), held(lower), columns, smem=1,
+        "products", out_shape, token, factor, held(theirs), held(mine), columns, smem=1,
     )
 
 
@@ -484,9 +514,8 @@
 
     def pairs(self, phase, parity):
         links = range(parity, self.size - 1, 2)
-        right = [(i, i + 1) for i in links if i < phase]
-        left = [(i + 1, i) for i in links if i + 1 >= self.size - phase]
-        return right + left
+        used = [i for i in links if i < phase or i + 1 >= self.size - phase]
+        return [(i, i + 1) for i in used] + [(i + 1, i) for i in used]
 
     def block(self, phase, parity):
         cell = lax.axis_index("cell")
@@ -525,20 +554,23 @@
     width = gene_factor.shape[0]
     line = Line(cells)
 
-    gram, factor, turned, upper = load(gene_factor, counts, tile_mask, tile_counts)
+    gram, factor, turned, theirs = load(gene_factor, counts, tile_mask, tile_counts)
     token = factor
     split = tile_mask.shape[1] // 8 * 4
-    high, low, lower = cross_early(split, factor, upper, turned, counts)
+    theirs_low, theirs_high, low, mine = cross_early(split, factor, theirs, turned, counts)
     gram, low = pair_sums(gram, "gene", genes, low)
     half = jax.ShapeDtypeStruct((width, rows // 2), F32)
-    theirs, mine = call(
-        functools.partial(cross_late_kernel, split), "cross_late", (half, half), token,
-        factor, high, low, held(lower), held(turned),
+    cross_a = call(
+        functools.partial(cross_late_kernel, split), "cross_late", half, token,
+        factor, low, held(mine), held(turned),
         smem=1, scratch=[pltpu.VMEM((rows // 2, width), F32)],
     )
-    arrived = swap(theirs, "sub", subs, 1)
-    cross_a, cross_b = mine, arrived
+    arrived_low = swap(theirs_low, "sub", subs, 1)
+    arrived_high = swap(theirs_high, "sub", subs, 1)
     bit = genes // 2
+    cross_a, sent = first_fold("gene", bit, token, cross_a, arrived_low, arrived_high)
+    cross_b = swap(sent, "gene", genes, bit)
+    bit //= 2
     while bit:
         cross_a, sent = fold("gene", bit, token, cross_a, cross_b)
         cross_b = swap(sent, "gene", genes, bit)
@@ -588,7 +620,8 @@
 
     def hop_rows(token, rows_sum):
         kind, pairs = hops.pop(0)
-        rows_arrived = lax.ppermute(rows_sum, "cell", pairs)
+        both = sorted(set(pairs) | {(b, a) for a, b in pairs})
+        rows_arrived = lax.ppermute(rows_sum, "cell", both)
         targets = [b for _, b in pairs]
         return after(token, hop(kind, targets, token, rows_sum, rows_arrived))
 
@@ -598,7 +631,7 @@
 
     for index in every:
         (first,) = products(
-            True, line, starts[index], chunks[index], token, factor, upper, lower, whole
+            True, line, starts[index], chunks[index], token, factor, theirs, mine, whole
         )
         token, first = after(token, first)
         for parity in (0, 1):
@@ -608,7 +641,7 @@
     totals, seconds = [], []
     for index in every:
         total, second = products(
-            False, line, starts[index], chunks[index], token, factor, upper, lower, whole
+            False, line, starts[index], chunks[index], token, factor, theirs, mine, whole
         )
         token, second = after(token, second)
         if hops:

time: 113 us -> 111 us (0.982)
  starting transfers between devices: 39.4 us -> 29.1 us
  waiting for transfers between devices: 34.7 us -> 44.4 us
  Pallas kernels: 37.8 us -> 35.8 us
    ppermute x10, starting transfers between devices: 24.7 us -> 14.8 us  [send(): lax.ppermute(value, 'cell', pairs)]
    ppermute x3, waiting for transfers between devices: 0.01 us -> 7.64 us  [hop_rows(): rows_arrived = lax.ppermute(rows_sum, 'cell', both)]
    pallas_call x1, Pallas kernels: 7.69 us -> 5.72 us  [load(): pl.pallas_call(load_kernel, out_shape=(jax.ShapeDtypeStruct((width, width...]
    ppermute x10, waiting for transfers between devices: 22.7 us -> 24.4 us  [send(): lax.ppermute(value, 'cell', pairs)]
    ppermute x8 -> x9, starting transfers between devices: 8.95 us -> 7.57 us  [swap(): return lax.ppermute(value, axis, [(i, i ^ step) for i in range(size)])]
    ppermute x8 -> x9, waiting for transfers between devices: 11.9 us -> 12.4 us  [swap(): return lax.ppermute(value, axis, [(i, i ^ step) for i in range(size)])]
  transfers between devices with their start and end apart: 21 -> 22, of which waited for: 9 -> 10; matrix products, arithmetic and copies ran while one was open for 0% -> 0% of each run, Pallas kernels for 22% -> 25%
where the time goes in v10:
time: 111 us; the launch traced here: 110 us
  waiting for transfers between devices  44.4 us (40%)
  Pallas kernels  35.8 us (32%)
  starting transfers between devices  29.1 us (26%)
    ppermute x10, waiting for transfers between devices, send(): lax.ppermute(value, 'cell', pairs)  24.4 us
    pallas_call x24, Pallas kernels, call(): pl.pallas_call(lambda token, *refs: kernel(*refs), out_shape=out_shape, i...  20.3 us
    ppermute x10, starting transfers between devices, send(): lax.ppermute(value, 'cell', pairs)  14.8 us
    ppermute x9, waiting for transfers between devices, swap(): return lax.ppermute(value, axis, [(i, i ^ step) for i in range(size)])  12.4 us
    ppermute x3, waiting for transfers between devices, hop_rows(): rows_arrived = lax.ppermute(rows_sum, 'cell', both)  7.64 us
    ppermute x9, starting transfers between devices, swap(): return lax.ppermute(value, axis, [(i, i ^ step) for i in range(size)])  7.57 us
    ppermute x3, starting transfers between devices, hop_rows(): rows_arrived = lax.ppermute(rows_sum, 'cell', both)  6.76 us
    pallas_call x1, Pallas kernels, cross_early(): pl.pallas_call(functools.partial(cross_early_kernel, split), out_shape=(j...  6.25 us
  transfers between devices with their start and end apart: 22, of which 10 were waited for; matrix products, arithmetic and copies ran while one was open for 0% of the time, Pallas kernels for 25%

profile of v10, /device:TPU:0, one launch (start us, length us, event | category | flops | bytes accessed | tf_op | source)
XLA Modules:
  0.0 110.3 jit_solution(8045914348237321577)
XLA Ops:
  0.6 5.7 %load.1 = (f32[256,256]{1,0:T(8,128)S(1)}, f32[4,32]{1,0:T(4,128)S(1)}, bf16[8192,256]{1,0:T(8,128)(2,1)S(1)}, bf16[512,8192]{1,0:T(8,128)(2,1)S(1)}) custom-call(bf16[256,8192]{1,0:T(8,128)(2,1)} %genes.1, bf16[1024,8192]{1,0:T(8,128)(2,1)} %counts.3, s32[4,32]{1,0:T(4,128)} %tile_mask.1, s32[4,32]{1,0:T(4,128)} %tile_counts.1), custom_call_target="tpu_custom_call" | custom-call | flops 1 | bytes 1 | tf_op jit(solution)/shard_map/load/pallas_call | solution.py:93
  6.4 3.0 %collective-permute-start = (f32[256,256]{1,0:T(8,128)S(1)}, f32[256,256]{1,0:T(8,128)S(1)}, u32[]{:S(2)}, u32[]{:S(2)}) collective-permute-start(f32[256,256]{1,0:T(8,128)S(1)} %get-tuple-element.59), channel_id=1, source_target_pairs={{0,2},{2,0},{1,3},{3,1},{4,6},{6,4},{5,7},{7,5},{8,10},{10,8},{9,1... | collective-permute-start | bytes 786440 | tf_op jit(solution)/shard_map/ppermute | solution.py:531
  9.4 6.3 %cross_early.1 = (f32[256,256]{1,0:T(8,128)S(1)}, f32[256,256]{1,0:T(8,128)S(1)}, f32[512,256]{1,0:T(8,128)S(1)}, bf16[512,8192]{1,0:T(8,128)(2,1)S(1)}) custom-call(f32[4,32]{1,0:T(4,128)S(1)} %get-tuple-element.108.factor.token.refs_0_, bf16[512,8192]{1,0:T(8,128)(2,1)S(1)} %get-tuple-element.60.theirs.refs_1_, ...), custom_call_target="tpu_custom_call" | custom-call | flops 1 | bytes 1 | tf_op jit(solution)/shard_map/cross_early/pallas_call | solution.py:163
  15.6 0.1 collective-permute-start.2
  15.7 0.5 collective-permute-start.3
  16.2 0.0 collective-permute-done
  16.2 0.1 collective-permute-start.1
  16.4 2.6 %cross_late.1.refs_0_ = f32[256,512]{1,0:T(8,128)S(1)} custom-call(f32[4,32]{1,0:T(4,128)S(1)} %get-tuple-element.108.factor.token.refs_0_, f32[4,32]{1,0:T(4,128)S(1)} %get-tuple-element.108.factor.token.refs_0_, f32[512,256]{1,0:T(8,128)S(1)} %get-tuple-element.65.refs_1_, bf16[512,8192]{1,0:T(8,128)(2,1)S(1)} %get-tuple-element.66.refs_2_, ...), custom_call_target="tpu_custom_call" | custom-call | flops 1 | bytes 1 | tf_op jit(solution)/shard_map/cross_late/pallas_call | solution.py:201
  19.0 0.0 copy-start
  19.0 0.0 collective-permute-done.2.refs_1_
  19.0 0.0 collective-permute-done.3.refs_2_
  19.0 0.1 fold.1
  19.1 1.2 %collective-permute-start.4 = (f32[256,256]{1,0:T(8,128)S(1)}, f32[256,256]{1,0:T(8,128)S(1)}, u32[]{:S(2)}, u32[]{:S(2)}) collective-permute-start(f32[256,256]{1,0:T(8,128)S(1)} %get-tuple-element.70), channel_id=1, source_target_pairs={{0,2},{2,0},{1,3},{3,1},{4,6},{6,4},{5,7},{7,5},{8,10},{10,8},{9,1... | collective-permute-start | bytes 786440 | tf_op jit(solution)/shard_map/ppermute | solution.py:531
  20.3 0.0 collective-permute-done.1.gram_b
  20.3 3.5 %inverse.1 = (f32[256,256]{1,0:T(8,128)S(1)}, f32[8,128]{1,0:T(8,128)S(1)}) custom-call(f32[256,256]{1,0:T(8,128)S(1)} %add.3.gram_a, f32[256,256]{1,0:T(8,128)S(1)} %collective-permute-done.1.gram_b), custom_call_target="tpu_custom_call" | custom-call | flops 2013265920 | bytes 786432 | tf_op jit(solution)/shard_map/inverse/pallas_call | solution.py:338
  23.8 4.0 %collective-permute-done.4.refs_2_ = f32[256,256]{1,0:T(8,128)S(1)} collective-permute-done((f32[256,256]{1,0:T(8,128)S(1)}, f32[256,256]{1,0:T(8,128)S(1)}, u32[]{:S(2)}, u32[]{:S(2)}) %collective-permute-start.4) | collective-permute-done | bytes 262176 | tf_op jit(solution)/shard_map/ppermute | solution.py:531
  27.8 1.0 admm.1.refs_0_
  28.8 1.3 %collective-permute-start.5 = (bf16[256,256]{1,0:T(8,128)(2,1)S(1)}, bf16[256,256]{1,0:T(8,128)(2,1)S(1)}, u32[]{:S(2)}, u32[]{:S(2)}) collective-permute-start(bf16[256,256]{1,0:T(8,128)(2,1)S(1)} %admm.1.refs_0_), channel_id=1, source_target_pairs={{0,2},{2,0},{1,3},{3,1},{4,6},{6,4},{5,7},{7,5},{8,10},{10,8},{9,1... | collective-permute-start | bytes 393224 | tf_op jit(solution)/shard_map/ppermute | solution.py:531
  30.1 3.9 %collective-permute-done.5.refs_1_ = bf16[256,256]{1,0:T(8,128)(2,1)S(1)} collective-permute-done((bf16[256,256]{1,0:T(8,128)(2,1)S(1)}, bf16[256,256]{1,0:T(8,128)(2,1)S(1)}, u32[]{:S(2)}, u32[]{:S(2)}) %collective-permute-start.5) | collective-permute-done | bytes 131104 | tf_op jit(solution)/shard_map/ppermute | solution.py:531
  34.0 0.1 collective-permute-start.6
  34.1 0.2 row_share.1.refs_0_
  34.3 1.6 %collective-permute-start.7 = (bf16[128,256]{1,0:T(8,128)(2,1)S(1)}, bf16[128,256]{1,0:T(8,128)(2,1)S(1)}, u32[]{:S(2)}, u32[]{:S(2)}) collective-permute-start(bf16[128,256]{1,0:T(8,128)(2,1)S(1)} %row_share.1.refs_0_), channel_id=1, source_target_pairs={{0,4},{4,0},{8,12},{12,8},{1,5},{5,1},{9,13},{13,9},{2,6},{6,2},{1... | collective-permute-start | bytes 196616 | tf_op jit(solution)/shard_map/ppermute | solution.py:624
  35.9 0.0 collective-permute-done.6.refs_1_
  36.0 1.5 %products.4 = bf16[256,1024]{1,0:T(8,128)(2,1)S(1)} custom-call(f32[4,32]{1,0:T(4,128)S(1)} %get-tuple-element.108.factor.token.refs_0_, f32[4,32]{1,0:T(4,128)S(1)} %get-tuple-element.108.factor.token.refs_0_, bf16[512,8192]{1,0:T(8,128)(2,1)S(1)} %get-tuple-element.60.theirs.refs_1_, bf16[512,8192]{1,0:T(8,128)(2,1)S(1)} %get-tuple-element.66.refs_2_, ...), custom_call_target="tpu_custom_call" | custom-call | flops 1 | bytes 1 | tf_op jit(solution)/shard_map/products/pallas_call | solution.py:201
  37.5 1.3 %collective-permute-start.9 = (bf16[256,1024]{1,0:T(8,128)(2,1)S(1)}, bf16[256,1024]{1,0:T(8,128)(2,1)S(1)}, u32[]{:S(2)}, u32[]{:S(2)}) collective-permute-start(bf16[256,1024]{1,0:T(8,128)(2,1)S(1)} %products.4), channel_id=1, source_target_pairs={{0,4},{8,12},{4,0},{12,8},{1,5},{9,13},{5,1},{13,9},{2,6},{10,14},... | collective-permute-start | bytes 1572872 | tf_op jit(solution)/shard_map/ppermute | solution.py:603
  38.8 0.1 collective-permute-done.7.refs_1_
  38.9 1.5 %products.5 = bf16[256,1024]{1,0:T(8,128)(2,1)S(1)} custom-call(f32[4,32]{1,0:T(4,128)S(1)} %get-tuple-element.108.factor.token.refs_0_, f32[4,32]{1,0:T(4,128)S(1)} %get-tuple-element.108.factor.token.refs_0_, bf16[512,8192]{1,0:T(8,128)(2,1)S(1)} %get-tuple-element.60.theirs.refs_1_, bf16[512,8192]{1,0:T(8,128)(2,1)S(1)} %get-tuple-element.66.refs_2_, ...), custom_call_target="tpu_custom_call" | custom-call | flops 1 | bytes 1 | tf_op jit(solution)/shard_map/products/pallas_call | solution.py:201
  40.4 1.6 %collective-permute-start.11 = (bf16[256,1024]{1,0:T(8,128)(2,1)S(1)}, bf16[256,1024]{1,0:T(8,128)(2,1)S(1)}, u32[]{:S(2)}, u32[]{:S(2)}) collective-permute-start(bf16[256,1024]{1,0:T(8,128)(2,1)S(1)} %products.5), channel_id=1, source_target_pairs={{0,4},{8,12},{4,0},{12,8},{1,5},{9,13},{5,1},{13,9},{2,6},{10,14},... | collective-permute-start | bytes 1572872 | tf_op jit(solution)/shard_map/ppermute | solution.py:603
  42.0 0.7 collective-permute-start.8
  42.7 4.3 %products.6 = (bf16[4,256,1024]{2,1,0:T(8,128)(2,1)S(1)}, bf16[256,1024]{1,0:T(8,128)(2,1)S(1)}) custom-call(f32[4,32]{1,0:T(4,128)S(1)} %get-tuple-element.108.factor.token.refs_0_, f32[4,32]{1,0:T(4,128)S(1)} %get-tuple-element.108.factor.token.refs_0_, bf16[512,8192]{1,0:T(8,128)(2,1)S(1)} %get-tuple-element.60.theirs.refs_1_, ...), custom_call_target="tpu_custom_call" | custom-call | flops 1 | bytes 1 | tf_op jit(solution)/shard_map/products/pallas_call | solution.py:201
  46.9 0.0 collective-permute-done.8.refs_1_
  47.0 4.5 %collective-permute-start.10 = (bf16[128,256]{1,0:T(8,128)(2,1)S(1)}, bf16[128,256]{1,0:T(8,128)(2,1)S(1)}, u32[]{:S(2)}, u32[]{:S(2)}) collective-permute-start(bf16[128,256]{1,0:T(8,128)(2,1)S(1)} %hop.4.refs_0_), channel_id=1, source_target_pairs={{0,4},{4,0},{8,12},{12,8},{1,5},{5,1},{9,13},{13,9},{2,6},{6,2},{1... | collective-permute-start | bytes 196616 | tf_op jit(solution)/shard_map/ppermute | solution.py:624
  51.5 0.1 collective-permute-start.15
  51.5 0.8 collective-permute-done.9.refs_1_
  52.3 0.1 operand.6
  52.4 0.7 collective-permute-start.13
  53.1 4.3 %products.7 = (bf16[4,256,1024]{2,1,0:T(8,128)(2,1)S(1)}, bf16[256,1024]{1,0:T(8,128)(2,1)S(1)}) custom-call(f32[4,32]{1,0:T(4,128)S(1)} %get-tuple-element.108.factor.token.refs_0_, f32[4,32]{1,0:T(4,128)S(1)} %get-tuple-element.108.factor.token.refs_0_, bf16[512,8192]{1,0:T(8,128)(2,1)S(1)} %get-tuple-element.60.theirs.refs_1_, ...), custom_call_target="tpu_custom_call" | custom-call | flops 1 | bytes 1 | tf_op jit(solution)/shard_map/products/pallas_call | solution.py:201
  57.4 7.5 %collective-permute-done.10.refs_1_ = bf16[128,256]{1,0:T(8,128)(2,1)S(1)} collective-permute-done((bf16[128,256]{1,0:T(8,128)(2,1)S(1)}, bf16[128,256]{1,0:T(8,128)(2,1)S(1)}, u32[]{:S(2)}, u32[]{:S(2)}) %collective-permute-start.10) | collective-permute-done | bytes 65568 | tf_op jit(solution)/shard_map/ppermute | solution.py:624
  64.9 0.0 collective-permute-done.11.refs_1_
  65.0 0.1 operand.7
  65.1 0.7 collective-permute-start.16
  65.8 4.5 %collective-permute-start.17 = (bf16[256,1024]{1,0:T(8,128)(2,1)S(1)}, bf16[256,1024]{1,0:T(8,128)(2,1)S(1)}, u32[]{:S(2)}, u32[]{:S(2)}) collective-permute-start(bf16[256,1024]{1,0:T(8,128)(2,1)S(1)} %get-tuple-element.104), channel_id=1, source_target_pairs={{0,4},{8,12},{4,0},{12,8},{1,5},{9,13},{5,1},{13,9},{2,6},{10,14},... | collective-permute-start | bytes 1572872 | tf_op jit(solution)/shard_map/ppermute | solution.py:603
  70.3 0.0 collective-permute-start.12
  70.3 1.0 turn.1
  71.3 0.3 collective-permute-done.12.refs_1_
  71.5 1.3 %collective-permute-start.14 = (f32[128,256]{1,0:T(8,128)S(1)}, f32[128,256]{1,0:T(8,128)S(1)}, u32[]{:S(2)}, u32[]{:S(2)}) collective-permute-start(f32[128,256]{1,0:T(8,128)S(1)} %plus.1.refs_0_), channel_id=1, source_target_pairs={{0,2},{2,0},{1,3},{3,1},{4,6},{6,4},{5,7},{7,5},{8,10},{10,8},{9,1... | collective-permute-start | bytes 393224 | tf_op jit(solution)/shard_map/ppermute | solution.py:531
  72.8 0.0 collective-permute-done.13.refs_1_
  72.8 0.1 operand.8
  73.0 4.3 %collective-permute-done.14.refs_1_ = f32[128,256]{1,0:T(8,128)S(1)} collective-permute-done((f32[128,256]{1,0:T(8,128)S(1)}, f32[128,256]{1,0:T(8,128)S(1)}, u32[]{:S(2)}, u32[]{:S(2)}) %collective-permute-start.14) | collective-permute-done | bytes 131104 | tf_op jit(solution)/shard_map/ppermute | solution.py:531
  77.3 0.7 side.5
  78.0 0.1 collective-permute-start.18
  78.1 0.1 operand.9
  78.2 0.0 collective-permute-done.16.refs_1_
  78.2 0.1 operand.10
  78.4 0.7 collective-permute-start.19
  79.1 8.3 %collective-permute-done.17.refs_1_ = bf16[256,1024]{1,0:T(8,128)(2,1)S(1)} collective-permute-done((bf16[256,1024]{1,0:T(8,128)(2,1)S(1)}, bf16[256,1024]{1,0:T(8,128)(2,1)S(1)}, u32[]{:S(2)}, u32[]{:S(2)}) %collective-permute-start.17) | collective-permute-done | bytes 524320 | tf_op jit(solution)/shard_map/ppermute | solution.py:603
  87.4 0.1 operand.11
  87.5 0.7 collective-permute-start.21
  88.2 4.5 %collective-permute-start.20 = (bf16[256,1024]{1,0:T(8,128)(2,1)S(1)}, bf16[256,1024]{1,0:T(8,128)(2,1)S(1)}, u32[]{:S(2)}, u32[]{:S(2)}) collective-permute-start(bf16[256,1024]{1,0:T(8,128)(2,1)S(1)} %operand.10), channel_id=1, source_target_pairs={{0,4},{8,12},{4,0},{12,8},{1,5},{9,13},{5,1},{13,9},{2,6},{10,14},... | collective-permute-start | bytes 1572872 | tf_op jit(solution)/shard_map/ppermute | solution.py:603
  92.7 5.9 %collective-permute-done.18.refs_1_ = bf16[256,1024]{1,0:T(8,128)(2,1)S(1)} collective-permute-done((bf16[256,1024]{1,0:T(8,128)(2,1)S(1)}, bf16[256,1024]{1,0:T(8,128)(2,1)S(1)}, u32[]{:S(2)}, u32[]{:S(2)}) %collective-permute-start.18) | collective-permute-done | bytes 524320 | tf_op jit(solution)/shard_map/ppermute | solution.py:603
  98.6 0.0 collective-permute-done.19.refs_2_
  98.6 1.1 %keep.2.refs_3_ = f32[2048,256]{1,0:T(8,128)} custom-call(f32[4,32]{1,0:T(4,128)S(1)} %get-tuple-element.108.factor.token.refs_0_, bf16[4,256,1024]{2,1,0:T(8,128)(2,1)S(1)} %get-tuple-element.81.refs_0_, bf16[256,1024]{1,0:T(8,128)(2,1)S(1)} %collective-permute-done.18.refs_1_, bf16[256,1024]{1,0:T(8,128)(2,1)S(1)} %collective-permute-done.19.refs_2_), custom_call_target="tpu_custom_call" | custom-call | flops 1 | bytes 1 | tf_op jit(solution)/shard_map/keep/pallas_call | solution.py:201
  99.8 9.4 %collective-permute-done.20.refs_1_ = bf16[256,1024]{1,0:T(8,128)(2,1)S(1)} collective-permute-done((bf16[256,1024]{1,0:T(8,128)(2,1)S(1)}, bf16[256,1024]{1,0:T(8,128)(2,1)S(1)}, u32[]{:S(2)}, u32[]{:S(2)}) %collective-permute-start.20) | collective-permute-done | bytes 524320 | tf_op jit(solution)/shard_map/ppermute | solution.py:603
  109.2 1.1 %keep.3 = f32[2048,256]{1,0:T(8,128)} custom-call(f32[4,32]{1,0:T(4,128)S(1)} %get-tuple-element.108.factor.token.refs_0_, bf16[4,256,1024]{2,1,0:T(8,128)(2,1)S(1)} %get-tuple-element.88.refs_0_, bf16[256,1024]{1,0:T(8,128)(2,1)S(1)} %collective-permute-done.20.refs_1_, ...), custom_call_target="tpu_custom_call", output_to_operand_aliasing={{}: (4, {})} | custom-call | flops 1 | bytes 1 | tf_op jit(solution)/shard_map/keep/pallas_call | solution.py:201
  (10 shorter events, 0.2 us)
Async XLA Ops:
  6.4 9.8 %collective-permute-start = (f32[256,256]{1,0:T(8,128)S(1)}, f32[256,256]{1,0:T(8,128)S(1)}, u32[]{:S(2)}, u32[]{:S(2)}) collective-permute-start(f32[256,256]{1,0:T(8,128)S(1)} %get-tuple-element.59), channel_id=1, source_target_pairs={{0,2},{2,0},{1,3},{3,1},{4,6},{6,4},{5,7},{7,5},{8,10},{10,8},{9,1... | collective-permute-start | bytes 786440 | tf_op jit(solution)/shard_map/ppermute | solution.py:531
  15.6 3.4 %collective-permute-start.2 = (f32[256,256]{1,0:T(8,128)S(1)}, f32[256,256]{1,0:T(8,128)S(1)}, u32[]{:S(2)}, u32[]{:S(2)}) collective-permute-start(f32[256,256]{1,0:T(8,128)S(1)} %get-tuple-element.67), channel_id=1, source_target_pairs={{0,1},{1,0},{2,3},{3,2},{4,5},{5,4},{6,7},{7,6},{8,9},{9,8},{10,11... | collective-permute-start | bytes 786440 | tf_op jit(solution)/shard_map/ppermute | solution.py:531
  15.7 3.3 %collective-permute-start.3 = (f32[256,256]{1,0:T(8,128)S(1)}, f32[256,256]{1,0:T(8,128)S(1)}, u32[]{:S(2)}, u32[]{:S(2)}) collective-permute-start(f32[256,256]{1,0:T(8,128)S(1)} %get-tuple-element.68), channel_id=1, source_target_pairs={{0,1},{1,0},{2,3},{3,2},{4,5},{5,4},{6,7},{7,6},{8,9},{9,8},{10,11... | collective-permute-start | bytes 786440 | tf_op jit(solution)/shard_map/ppermute | solution.py:531
  16.2 4.1 %collective-permute-start.1 = (f32[256,256]{1,0:T(8,128)S(1)}, f32[256,256]{1,0:T(8,128)S(1)}, u32[]{:S(2)}, u32[]{:S(2)}) collective-permute-start(f32[256,256]{1,0:T(8,128)S(1)} %add.3.gram_a), channel_id=1, source_target_pairs={{0,1},{1,0},{2,3},{3,2},{4,5},{5,4},{6,7},{7,6},{8,9},{9,8},{10,11... | collective-permute-start | bytes 786440 | tf_op jit(solution)/shard_map/ppermute | solution.py:531
  19.0 8.8 %copy-start = (bf16[1024,256]{1,0:T(8,128)(2,1)S(1)}, bf16[1024,256]{1,0:T(8,128)(2,1)}, u32[]{:S(2)}) copy-start(bf16[1024,256]{1,0:T(8,128)(2,1)} %refs_4_.1) | copy-start | bytes 1572868
  19.1 8.7 %collective-permute-start.4 = (f32[256,256]{1,0:T(8,128)S(1)}, f32[256,256]{1,0:T(8,128)S(1)}, u32[]{:S(2)}, u32[]{:S(2)}) collective-permute-start(f32[256,256]{1,0:T(8,128)S(1)} %get-tuple-element.70), channel_id=1, source_target_pairs={{0,2},{2,0},{1,3},{3,1},{4,6},{6,4},{5,7},{7,5},{8,10},{10,8},{9,1... | collective-permute-start | bytes 786440 | tf_op jit(solution)/shard_map/ppermute | solution.py:531
  28.8 5.1 %collective-permute-start.5 = (bf16[256,256]{1,0:T(8,128)(2,1)S(1)}, bf16[256,256]{1,0:T(8,128)(2,1)S(1)}, u32[]{:S(2)}, u32[]{:S(2)}) collective-permute-start(bf16[256,256]{1,0:T(8,128)(2,1)S(1)} %admm.1.refs_0_), channel_id=1, source_target_pairs={{0,2},{2,0},{1,3},{3,1},{4,6},{6,4},{5,7},{7,5},{8,10},{10,8},{9,1... | collective-permute-start | bytes 393224 | tf_op jit(solution)/shard_map/ppermute | solution.py:531
  34.0 1.9 %collective-permute-start.6 = (bf16[256,512]{1,0:T(8,128)(2,1)S(1)}, bf16[256,512]{1,0:T(8,128)(2,1)S(1)}, u32[]{:S(2)}, u32[]{:S(2)}) collective-permute-start(bf16[256,512]{1,0:T(8,128)(2,1)S(1)} %side.3.refs_0_), channel_id=1, source_target_pairs={{0,1},{1,0},{2,3},{3,2},{4,5},{5,4},{6,7},{7,6},{8,9},{9,8},{10,11... | collective-permute-start | bytes 786440 | tf_op jit(solution)/shard_map/ppermute | solution.py:531
  34.3 4.6 %collective-permute-start.7 = (bf16[128,256]{1,0:T(8,128)(2,1)S(1)}, bf16[128,256]{1,0:T(8,128)(2,1)S(1)}, u32[]{:S(2)}, u32[]{:S(2)}) collective-permute-start(bf16[128,256]{1,0:T(8,128)(2,1)S(1)} %row_share.1.refs_0_), channel_id=1, source_target_pairs={{0,4},{4,0},{8,12},{12,8},{1,5},{5,1},{9,13},{13,9},{2,6},{6,2},{1... | collective-permute-start | bytes 196616 | tf_op jit(solution)/shard_map/ppermute | solution.py:624
  37.5 14.8 %collective-permute-start.9 = (bf16[256,1024]{1,0:T(8,128)(2,1)S(1)}, bf16[256,1024]{1,0:T(8,128)(2,1)S(1)}, u32[]{:S(2)}, u32[]{:S(2)}) collective-permute-start(bf16[256,1024]{1,0:T(8,128)(2,1)S(1)} %products.4), channel_id=1, source_target_pairs={{0,4},{8,12},{4,0},{12,8},{1,5},{9,13},{5,1},{13,9},{2,6},{10,14},... | collective-permute-start | bytes 1572872 | tf_op jit(solution)/shard_map/ppermute | solution.py:603
  40.4 24.6 %collective-permute-start.11 = (bf16[256,1024]{1,0:T(8,128)(2,1)S(1)}, bf16[256,1024]{1,0:T(8,128)(2,1)S(1)}, u32[]{:S(2)}, u32[]{:S(2)}) collective-permute-start(bf16[256,1024]{1,0:T(8,128)(2,1)S(1)} %products.5), channel_id=1, source_target_pairs={{0,4},{8,12},{4,0},{12,8},{1,5},{9,13},{5,1},{13,9},{2,6},{10,14},... | collective-permute-start | bytes 1572872 | tf_op jit(solution)/shard_map/ppermute | solution.py:603
  42.0 4.9 %collective-permute-start.8 = (bf16[128,256]{1,0:T(8,128)(2,1)S(1)}, bf16[128,256]{1,0:T(8,128)(2,1)S(1)}, u32[]{:S(2)}, u32[]{:S(2)}) collective-permute-start(bf16[128,256]{1,0:T(8,128)(2,1)S(1)} %hop.3.refs_0_), channel_id=1, source_target_pairs={{4,8},{8,4},{5,9},{9,5},{6,10},{10,6},{7,11},{11,7},{20,24},{24,20... | collective-permute-start | bytes 196616 | tf_op jit(solution)/shard_map/ppermute | solution.py:624
  47.0 17.9 %collective-permute-start.10 = (bf16[128,256]{1,0:T(8,128)(2,1)S(1)}, bf16[128,256]{1,0:T(8,128)(2,1)S(1)}, u32[]{:S(2)}, u32[]{:S(2)}) collective-permute-start(bf16[128,256]{1,0:T(8,128)(2,1)S(1)} %hop.4.refs_0_), channel_id=1, source_target_pairs={{0,4},{4,0},{8,12},{12,8},{1,5},{5,1},{9,13},{13,9},{2,6},{6,2},{1... | collective-permute-start | bytes 196616 | tf_op jit(solution)/shard_map/ppermute | solution.py:624
  51.5 26.6 %collective-permute-start.15 = (bf16[256,1024]{1,0:T(8,128)(2,1)S(1)}, bf16[256,1024]{1,0:T(8,128)(2,1)S(1)}, u32[]{:S(2)}, u32[]{:S(2)}) collective-permute-start(bf16[256,1024]{1,0:T(8,128)(2,1)S(1)} %get-tuple-element.100), channel_id=1, source_target_pairs={{0,4},{8,12},{4,0},{12,8},{1,5},{9,13},{5,1},{13,9},{2,6},{10,14},... | collective-permute-start | bytes 1572872 | tf_op jit(solution)/shard_map/ppermute | solution.py:603
  52.4 20.4 %collective-permute-start.13 = (bf16[256,1024]{1,0:T(8,128)(2,1)S(1)}, bf16[256,1024]{1,0:T(8,128)(2,1)S(1)}, u32[]{:S(2)}, u32[]{:S(2)}) collective-permute-start(bf16[256,1024]{1,0:T(8,128)(2,1)S(1)} %operand.6), channel_id=1, source_target_pairs={{4,8},{8,4},{5,9},{9,5},{6,10},{10,6},{7,11},{11,7},{20,24},{24,20... | collective-permute-start | bytes 1572872 | tf_op jit(solution)/shard_map/ppermute | solution.py:603
  65.1 13.1 %collective-permute-start.16 = (bf16[256,1024]{1,0:T(8,128)(2,1)S(1)}, bf16[256,1024]{1,0:T(8,128)(2,1)S(1)}, u32[]{:S(2)}, u32[]{:S(2)}) collective-permute-start(bf16[256,1024]{1,0:T(8,128)(2,1)S(1)} %operand.7), channel_id=1, source_target_pairs={{4,8},{8,4},{5,9},{9,5},{6,10},{10,6},{7,11},{11,7},{20,24},{24,20... | collective-permute-start | bytes 1572872 | tf_op jit(solution)/shard_map/ppermute | solution.py:603
  65.8 21.6 %collective-permute-start.17 = (bf16[256,1024]{1,0:T(8,128)(2,1)S(1)}, bf16[256,1024]{1,0:T(8,128)(2,1)S(1)}, u32[]{:S(2)}, u32[]{:S(2)}) collective-permute-start(bf16[256,1024]{1,0:T(8,128)(2,1)S(1)} %get-tuple-element.104), channel_id=1, source_target_pairs={{0,4},{8,12},{4,0},{12,8},{1,5},{9,13},{5,1},{13,9},{2,6},{10,14},... | collective-permute-start | bytes 1572872 | tf_op jit(solution)/shard_map/ppermute | solution.py:603
  70.3 1.3 %collective-permute-start.12 = (bf16[128,256]{1,0:T(8,128)(2,1)S(1)}, bf16[128,256]{1,0:T(8,128)(2,1)S(1)}, u32[]{:S(2)}, u32[]{:S(2)}) collective-permute-start(bf16[128,256]{1,0:T(8,128)(2,1)S(1)} %hop.5.refs_0_), channel_id=1, source_target_pairs={{0,1},{1,0},{2,3},{3,2},{4,5},{5,4},{6,7},{7,6},{8,9},{9,8},{10,11... | collective-permute-start | bytes 196616 | tf_op jit(solution)/shard_map/ppermute | solution.py:531
  71.5 5.7 %collective-permute-start.14 = (f32[128,256]{1,0:T(8,128)S(1)}, f32[128,256]{1,0:T(8,128)S(1)}, u32[]{:S(2)}, u32[]{:S(2)}) collective-permute-start(f32[128,256]{1,0:T(8,128)S(1)} %plus.1.refs_0_), channel_id=1, source_target_pairs={{0,2},{2,0},{1,3},{3,1},{4,6},{6,4},{5,7},{7,5},{8,10},{10,8},{9,1... | collective-permute-start | bytes 393224 | tf_op jit(solution)/shard_map/ppermute | solution.py:531
  78.0 20.7 %collective-permute-start.18 = (bf16[256,1024]{1,0:T(8,128)(2,1)S(1)}, bf16[256,1024]{1,0:T(8,128)(2,1)S(1)}, u32[]{:S(2)}, u32[]{:S(2)}) collective-permute-start(bf16[256,1024]{1,0:T(8,128)(2,1)S(1)} %operand.8), channel_id=1, source_target_pairs={{0,4},{8,12},{4,0},{12,8},{1,5},{9,13},{5,1},{13,9},{2,6},{10,14},... | collective-permute-start | bytes 1572872 | tf_op jit(solution)/shard_map/ppermute | solution.py:603
  78.4 20.3 %collective-permute-start.19 = (bf16[256,1024]{1,0:T(8,128)(2,1)S(1)}, bf16[256,1024]{1,0:T(8,128)(2,1)S(1)}, u32[]{:S(2)}, u32[]{:S(2)}) collective-permute-start(bf16[256,1024]{1,0:T(8,128)(2,1)S(1)} %operand.9), channel_id=1, source_target_pairs={{4,8},{8,4},{5,9},{9,5},{6,10},{10,6},{7,11},{11,7},{20,24},{24,20... | collective-permute-start | bytes 1572872 | tf_op jit(solution)/shard_map/ppermute | solution.py:603
  87.5 12.3 %collective-permute-start.21 = (bf16[256,1024]{1,0:T(8,128)(2,1)S(1)}, bf16[256,1024]{1,0:T(8,128)(2,1)S(1)}, u32[]{:S(2)}, u32[]{:S(2)}) collective-permute-start(bf16[256,1024]{1,0:T(8,128)(2,1)S(1)} %operand.11), channel_id=1, source_target_pairs={{4,8},{8,4},{5,9},{9,5},{6,10},{10,6},{7,11},{11,7},{20,24},{24,20... | collective-permute-start | bytes 1572872 | tf_op jit(solution)/shard_map/ppermute | solution.py:603
  88.2 20.9 %collective-permute-start.20 = (bf16[256,1024]{1,0:T(8,128)(2,1)S(1)}, bf16[256,1024]{1,0:T(8,128)(2,1)S(1)}, u32[]{:S(2)}, u32[]{:S(2)}) collective-permute-start(bf16[256,1024]{1,0:T(8,128)(2,1)S(1)} %operand.10), channel_id=1, source_target_pairs={{0,4},{8,12},{4,0},{12,8},{1,5},{9,13},{5,1},{13,9},{2,6},{10,14},... | collective-permute-start | bytes 1572872 | tf_op jit(solution)/shard_map/ppermute | solution.py:603

commit v11 on v10

--- a/solution.py
+++ b/solution.py
@@ -114,79 +114,120 @@
     )(away(genes), away(counts), away(tile_mask), away(tile_counts))
 
 
-def add_cross(first_row, start, stop, factor, counts, turned, total):
-    tile = counts.shape[1] // factor.shape[1]
-    at_once = min(4, stop - start)
-
-    @pl.loop(start // at_once, stop // at_once)
+def scaled(counts, factors):
+    tile_rows = counts.shape[0] // len(factors)
+    tile_columns = counts.shape[1] // len(factors[0])
+    rows = []
+    for row, scales in enumerate(factors):
+        part = counts[row * tile_rows : (row + 1) * tile_rows]
+        rows.append(
+            jnp.concatenate(
+                [
+                    (
+                        part[:, col * tile_columns : (col + 1) * tile_columns].astype(F32) * scale
+                    ).astype(BF16)
+                    for col, scale in enumerate(scales)
+                ],
+                axis=1,
+            )
+        )
+    return jnp.concatenate(rows, axis=0)
+
+
+def add_cross(first_row, factor, counts, turned, total):
+    gene_tiles = factor.shape[1]
+    tile = counts.shape[1] // gene_tiles
+    row_tiles = counts.shape[0] // tile
+    at_once = min(4, gene_tiles)
+
+    @pl.loop(0, gene_tiles // at_once)
     def _(step):
-        sums = None
-        for col in range(at_once):
-            place = step * at_once + col
-            at = pl.ds(pl.multiple_of(place * tile, tile), tile)
-            product = jnp.dot(counts[:, at], turned[at, :], preferred_element_type=F32)
-            product = jnp.concatenate(
-                [
-                    product[row * tile : (row + 1) * tile] * factor[first_row + row, place]
-                    for row in range(counts.shape[0] // tile)
-                ],
-                axis=0,
-            )
-            sums = product if sums is None else sums + product
-        total[...] += sums
-
-
-def cross_early_kernel(
-    split, factor, theirs, turned, counts, cross_a, cross_b, low, mine, total, sems
-):
+        at = pl.ds(pl.multiple_of(step * at_once * tile, at_once * tile), at_once * tile)
+        factors = [
+            [factor[first_row + row, step * at_once + col] for col in range(at_once)]
+            for row in range(row_tiles)
+        ]
+        total[...] += jnp.dot(
+            scaled(counts[:, at], factors), turned[at, :], preferred_element_type=F32
+        )
+
+
+def cross_theirs_kernel(factor, theirs, turned, counts, low, high, mine, total, sems):
     half = theirs.shape[0]
     core = lax.axis_index("sub")
     copies = row_copies(counts, mine, pl.multiple_of(core * half, half), sems)
     for copy in copies:
         copy.start()
-    gene_tiles = factor.shape[1]
-    row_tiles = factor.shape[0] // 2
     total[...] = jnp.zeros_like(total)
-    add_cross((1 - core) * row_tiles, 0, gene_tiles, factor, theirs, turned, total)
-    cross_a[...] = total[: half // 2].T
-    cross_b[...] = total[half // 2 :].T
+    add_cross((1 - core) * (factor.shape[0] // 2), factor, theirs, turned, total)
+    low[...] = total[: half // 2].T
+    high[...] = total[half // 2 :].T
     for copy in copies:
         copy.wait()
-    low[...] = jnp.zeros_like(low)
-    add_cross(core * row_tiles, 0, split, factor, mine, turned, low)
-
-
-def cross_early(split, factor, theirs, turned, counts):
+
+
+def cross_theirs(factor, theirs, turned, counts):
     half, columns = theirs.shape
     width = turned.shape[1]
     here = pl.BlockSpec(memory_space=pltpu.VMEM)
+    piece = jax.ShapeDtypeStruct((width, half // 2), F32)
     return pl.pallas_call(
-        functools.partial(cross_early_kernel, split),
-        out_shape=(
-            jax.ShapeDtypeStruct((width, half // 2), F32),
-            jax.ShapeDtypeStruct((width, half // 2), F32),
-            jax.ShapeDtypeStruct((half, width), F32),
-            pltpu.VMEM((half, columns), BF16),
-        ),
+        cross_theirs_kernel,
+        out_shape=(piece, piece, pltpu.VMEM((half, columns), BF16)),
         in_specs=[
             pl.BlockSpec(memory_space=pltpu.SMEM),
             here,
             here,
             pl.BlockSpec(memory_space=pltpu.HBM),
         ],
-        out_specs=(here,) * 4,
+        out_specs=(here,) * 3,
         scratch_shapes=[pltpu.VMEM((half, width), F32), pltpu.SemaphoreType.DMA((8,))],
         compiler_params=params(),
         cost_estimate=cost(1, 1),
-        name="cross_early",
+        name="cross_theirs",
     )(factor, held(theirs), held(turned), away(counts))
 
 
-def cross_late_kernel(split, factor, low, counts, turned, cross, total):
-    total[...] = low[...]
-    first_row = lax.axis_index("sub") * (factor.shape[0] // 2)
-    add_cross(first_row, split, factor.shape[1], factor, counts, turned, total)
+def cross_piece_kernel(bit, kept, factor, mine, turned, cross, total):
+    rows = total.shape[0]
+    upper = ((lax.axis_index("gene") & bit) != 0) == kept
+    piece = jnp.where(upper, 1, 0)
+    first = lax.axis_index("sub") * (factor.shape[0] // 2)
+    first += piece * (factor.shape[0] // 4)
+    total[...] = jnp.zeros_like(total)
+    counts = mine.at[pl.ds(pl.multiple_of(piece * rows, rows), rows)]
+    add_cross(first, factor, counts, turned, total)
     cross[...] = total[...].T
+
+
+def cross_piece(bit, kept, token, factor, mine, turned):
+    rows = mine.shape[0] // 2
+    width = turned.shape[1]
+    return call(
+        functools.partial(cross_piece_kernel, bit, kept),
+        "cross_piece", jax.ShapeDtypeStruct((width, rows), F32), token,
+        factor, held(mine), held(turned),
+        smem=1, scratch=[pltpu.VMEM((rows, width), F32)],
+    )
+
+
+def add_piece_kernel(bit, kept, left, low, high, out):
+    upper = ((lax.axis_index("gene") & bit) != 0) == kept
+
+    @pl.when(upper)
+    def _():
+        out[...] = left[...] + high[...]
+
+    @pl.when(jnp.logical_not(upper))
+    def _():
+        out[...] = left[...] + low[...]
+
+
+def add_piece(bit, kept, token, left, low, high):
+    shape = jax.ShapeDtypeStruct(left.shape, F32)
+    return call(
+        functools.partial(add_piece_kernel, bit, kept), "add_piece", shape, token, left, low, high
+    )
 
 
 def call(kernel, name, out_shape, token, *args, scratch=(), smem=0, aliases=None, out=None):
@@ -224,29 +265,6 @@
     def _():
         kept[...] = left[:, :half] + right[:, :half]
         sent[...] = left[:, half:] + right[:, half:]
-
-
-def first_fold_kernel(axis, bit, left, right_low, right_high, kept, sent):
-    half = kept.shape[1]
-    upper = (lax.axis_index(axis) & bit) != 0
-
-    @pl.when(upper)
-    def _():
-        kept[...] = left[:, half:] + right_high[...]
-        sent[...] = left[:, :half] + right_low[...]
-
-    @pl.when(jnp.logical_not(upper))
-    def _():
-        kept[...] = left[:, :half] + right_low[...]
-        sent[...] = left[:, half:] + right_high[...]
-
-
-def first_fold(axis, bit, token, left, right_low, right_high):
-    shape = jax.ShapeDtypeStruct(right_low.shape, F32)
-    return call(
-        functools.partial(first_fold_kernel, axis, bit),
-        "fold", (shape, shape), token, left, right_low, right_high,
-    )
 
 
 def fold(axis, bit, token, left, right):
@@ -379,22 +397,20 @@
         order, step = (block, turn) if only_first else (turn // steps, lax.rem(turn, steps))
         first = pl.multiple_of(order * size + start + step * wide, span)
         total = None
-        for counts, side, place in [
-            (counts, side, place)
-            for counts, side in ((theirs, 1 - core), (mine, core))
-            for place in range(row_tiles)
-        ]:
-            row = side * row_tiles + place
+        for counts, side in ((theirs, 1 - core), (mine, core)):
+            factors = [
+                [
+                    factor[side * row_tiles + row, (first + col * span) // tile]
+                    for col in range(wide // span)
+                ]
+                for row in range(row_tiles)
+            ]
+            cells = row_tiles * tile
             part = jnp.dot(
-                columns[:, pl.ds(pl.multiple_of(row * tile, tile), tile)],
-                counts[place * tile : (place + 1) * tile, pl.ds(first, wide)],
+                columns[:, pl.ds(pl.multiple_of(side * cells, cells), cells)],
+                scaled(counts[:, pl.ds(first, wide)], factors),
                 preferred_element_type=F32,
             )
-            scales = [
-                jnp.full((1, span), factor[row, (first + col * span) // tile], F32)
-                for col in range(wide // span)
-            ]
-            part = jnp.concatenate(scales, axis=1) * part
             total = part if total is None else total + part
         total = total.astype(BF16)
         at = pl.ds(pl.multiple_of(step * wide, span), wide)
@@ -512,10 +528,14 @@
     def __init__(self, size):
         self.size = size
 
-    def pairs(self, phase, parity):
+    def pairs(self, phase, parity, exchange=False):
         links = range(parity, self.size - 1, 2)
-        used = [i for i in links if i < phase or i + 1 >= self.size - phase]
-        return [(i, i + 1) for i in used] + [(i + 1, i) for i in used]
+        right = [(i, i + 1) for i in links if i < phase]
+        left = [(i + 1, i) for i in links if i + 1 >= self.size - phase]
+        pairs = right + left
+        if exchange:
+            pairs = sorted(set(pairs) | {(b, a) for a, b in pairs})
+        return pairs
 
     def block(self, phase, parity):
         cell = lax.axis_index("cell")
@@ -556,20 +576,16 @@
 
     gram, factor, turned, theirs = load(gene_factor, counts, tile_mask, tile_counts)
     token = factor
-    split = tile_mask.shape[1] // 8 * 4
-    theirs_low, theirs_high, low, mine = cross_early(split, factor, theirs, turned, counts)
-    gram, low = pair_sums(gram, "gene", genes, low)
-    half = jax.ShapeDtypeStruct((width, rows // 2), F32)
-    cross_a = call(
-        functools.partial(cross_late_kernel, split), "cross_late", half, token,
-        factor, low, held(mine), held(turned),
-        smem=1, scratch=[pltpu.VMEM((rows // 2, width), F32)],
-    )
+    theirs_low, theirs_high, mine = cross_theirs(factor, theirs, turned, counts)
     arrived_low = swap(theirs_low, "sub", subs, 1)
     arrived_high = swap(theirs_high, "sub", subs, 1)
     bit = genes // 2
-    cross_a, sent = first_fold("gene", bit, token, cross_a, arrived_low, arrived_high)
+    own_sent = cross_piece(bit, False, token, factor, mine, turned)
+    sent = add_piece(bit, False, token, own_sent, arrived_low, arrived_high)
     cross_b = swap(sent, "gene", genes, bit)
+    gram, (factor_late, _) = pair_sums(gram, "gene", genes, (factor, own_sent))
+    cross_a = cross_piece(bit, True, token, factor_late, mine, turned)
+    cross_a = add_piece(bit, True, token, cross_a, arrived_low, arrived_high)
     bit //= 2
     while bit:
         cross_a, sent = fold("gene", bit, token, cross_a, cross_b)
@@ -599,7 +615,7 @@
     arrived = {}
 
     def send(value, phase, parity, index):
-        pairs = line.pairs(phase, parity)
+        pairs = line.pairs(phase, parity, exchange=phase == 1 and index == 0)
         arrived[phase, parity, index] = lax.ppermute(value, "cell", pairs) if pairs else None
 
     def resend(token, phase, parity, index):

time: 111 us -> 108 us (0.973)
  waiting for transfers between devices: 44.4 us -> 36.2 us
  starting transfers between devices: 29.1 us -> 32.4 us
  Pallas kernels: 35.8 us -> 38.1 us
    ppermute x10, starting transfers between devices: 14.8 us -> 22.8 us  [send(): lax.ppermute(value, 'cell', pairs)]
    ppermute x10, waiting for transfers between devices: 24.4 us -> 19.2 us  [send(): lax.ppermute(value, 'cell', pairs)]
    pallas_call x24 -> x26, Pallas kernels: 20.3 us -> 24.5 us  [call(): pl.pallas_call(lambda token, *refs: kernel(*refs), out_shape=out_shape, i...]
    ppermute x9, starting transfers between devices: 7.57 us -> 5.03 us  [swap(): return lax.ppermute(value, axis, [(i, i ^ step) for i in range(size)])]
    ppermute x3, waiting for transfers between devices: 7.64 us -> 5.29 us  [hop_rows(): rows_arrived = lax.ppermute(rows_sum, 'cell', both)]
    ppermute x3, starting transfers between devices: 6.76 us -> 4.55 us  [hop_rows(): rows_arrived = lax.ppermute(rows_sum, 'cell', both)]
    pallas_call x1, Pallas kernels: 6.25 us -> 4.44 us  [cross_theirs(): pl.pallas_call(cross_theirs_kernel, out_shape=(piece, piece, pltpu.VMEM((...]
  transfers between devices with their start and end apart: 22 -> 22, of which waited for: 10 -> 9; matrix products, arithmetic and copies ran while one was open for 0% -> 0% of each run, Pallas kernels for 25% -> 28%
where the time goes in v11:
time: 108 us
  Pallas kernels  38.1 us (35%)
  waiting for transfers between devices  36.2 us (34%)
  starting transfers between devices  32.4 us (30%)
    pallas_call x26, Pallas kernels, call(): pl.pallas_call(lambda token, *refs: kernel(*refs), out_shape=out_shape, i...  24.5 us
    ppermute x10, starting transfers between devices, send(): lax.ppermute(value, 'cell', pairs)  22.8 us
    ppermute x10, waiting for transfers between devices, send(): lax.ppermute(value, 'cell', pairs)  19.2 us
    ppermute x9, waiting for transfers between devices, swap(): return lax.ppermute(value, axis, [(i, i ^ step) for i in range(size)])  11.7 us
    pallas_call x1, Pallas kernels, load(): pl.pallas_call(load_kernel, out_shape=(jax.ShapeDtypeStruct((width, width...  5.72 us
    ppermute x3, waiting for transfers between devices, hop_rows(): rows_arrived = lax.ppermute(rows_sum, 'cell', both)  5.29 us
    ppermute x9, starting transfers between devices, swap(): return lax.ppermute(value, axis, [(i, i ^ step) for i in range(size)])  5.03 us
    ppermute x3, starting transfers between devices, hop_rows(): rows_arrived = lax.ppermute(rows_sum, 'cell', both)  4.55 us
  transfers between devices with their start and end apart: 22, of which 9 were waited for; matrix products, arithmetic and copies ran while one was open for 0% of the time, Pallas kernels for 28%

profile of v11, /device:TPU:0, one launch (start us, length us, event | category | flops | bytes accessed | tf_op | source)
XLA Modules:
  0.0 107.7 jit_solution(17764768607697836674)
XLA Ops:
  0.6 5.7 %load.1 = (f32[256,256]{1,0:T(8,128)S(1)}, f32[4,32]{1,0:T(4,128)S(1)}, bf16[8192,256]{1,0:T(8,128)(2,1)S(1)}, bf16[512,8192]{1,0:T(8,128)(2,1)S(1)}) custom-call(bf16[256,8192]{1,0:T(8,128)(2,1)} %genes.1, bf16[1024,8192]{1,0:T(8,128)(2,1)} %counts.3, s32[4,32]{1,0:T(4,128)} %tile_mask.1, s32[4,32]{1,0:T(4,128)} %tile_counts.1), custom_call_target="tpu_custom_call" | custom-call | flops 1 | bytes 1 | tf_op jit(solution)/shard_map/load/pallas_call | solution.py:93
  6.4 3.0 %collective-permute-start = (f32[256,256]{1,0:T(8,128)S(1)}, f32[256,256]{1,0:T(8,128)S(1)}, u32[]{:S(2)}, u32[]{:S(2)}) collective-permute-start(f32[256,256]{1,0:T(8,128)S(1)} %get-tuple-element.56), channel_id=1, source_target_pairs={{0,2},{2,0},{1,3},{3,1},{4,6},{6,4},{5,7},{7,5},{8,10},{10,8},{9,1... | collective-permute-start | bytes 786440 | tf_op jit(solution)/shard_map/ppermute | solution.py:551
  9.4 4.4 %cross_theirs.1 = (f32[256,256]{1,0:T(8,128)S(1)}, f32[256,256]{1,0:T(8,128)S(1)}, bf16[512,8192]{1,0:T(8,128)(2,1)S(1)}) custom-call(f32[4,32]{1,0:T(4,128)S(1)} %get-tuple-element.102.factor.token.refs_0_, bf16[512,8192]{1,0:T(8,128)(2,1)S(1)} %get-tuple-element.57.theirs.refs_1_, bf16[8192,256]{1,0:T(8,128)(2,1)S(1)} %get-tuple-element.58.turned.refs_2_, ...), custom_call_target="tpu_custom_call" | custom-call | flops 1 | bytes 1 | tf_op jit(solution)/shard_map/cross_theirs/pallas_call | solution.py:174
  13.8 0.1 collective-permute-start.2
  13.9 0.5 collective-permute-start.3
  14.4 3.2 %cross_piece.2.refs_0_ = f32[256,256]{1,0:T(8,128)S(1)} custom-call(f32[4,32]{1,0:T(4,128)S(1)} %get-tuple-element.102.factor.token.refs_0_, f32[4,32]{1,0:T(4,128)S(1)} %get-tuple-element.102.factor.token.refs_0_, bf16[512,8192]{1,0:T(8,128)(2,1)S(1)} %get-tuple-element.59.refs_1_.refs_2_, bf16[8192,256]{1,0:T(8,128)(2,1)S(1)} %get-tuple-element.58.turned.refs_2_), custom_call_target="tpu_custom_call" | custom-call | flops 1 | bytes 1 | tf_op jit(solution)/shard_map/cross_piece/pallas_call | solution.py:242
  17.6 0.0 collective-permute-done
  17.6 0.1 collective-permute-start.1
  17.8 0.0 collective-permute-done.2.refs_1_
  17.8 0.0 collective-permute-done.3.refs_2_
  17.8 0.1 collective-permute-start.4
  17.9 3.2 %cross_piece.3.refs_0_ = f32[256,256]{1,0:T(8,128)S(1)} custom-call(f32[4,32]{1,0:T(4,128)S(1)} %get-tuple-element.102.factor.token.refs_0_, f32[4,32]{1,0:T(4,128)S(1)} %get-tuple-element.102.factor.token.refs_0_, bf16[512,8192]{1,0:T(8,128)(2,1)S(1)} %get-tuple-element.59.refs_1_.refs_2_, bf16[8192,256]{1,0:T(8,128)(2,1)S(1)} %get-tuple-element.58.turned.refs_2_), custom_call_target="tpu_custom_call" | custom-call | flops 1 | bytes 1 | tf_op jit(solution)/shard_map/cross_piece/pallas_call | solution.py:242
  21.1 0.0 copy-start
  21.1 0.1 add_piece.2.refs_1_
  21.2 0.0 collective-permute-done.1.gram_b
  21.2 3.5 %inverse.1 = (f32[256,256]{1,0:T(8,128)S(1)}, f32[8,128]{1,0:T(8,128)S(1)}) custom-call(f32[256,256]{1,0:T(8,128)S(1)} %add.3.gram_a, f32[256,256]{1,0:T(8,128)S(1)} %collective-permute-done.1.gram_b), custom_call_target="tpu_custom_call" | custom-call | flops 2013265920 | bytes 786432 | tf_op jit(solution)/shard_map/inverse/pallas_call | solution.py:356
  24.7 1.8 %collective-permute-done.4.refs_2_ = f32[256,256]{1,0:T(8,128)S(1)} collective-permute-done((f32[256,256]{1,0:T(8,128)S(1)}, f32[256,256]{1,0:T(8,128)S(1)}, u32[]{:S(2)}, u32[]{:S(2)}) %collective-permute-start.4) | collective-permute-done | bytes 262176 | tf_op jit(solution)/shard_map/ppermute | solution.py:551
  26.5 1.0 admm.1.refs_0_
  27.6 0.3 collective-permute-start.5
  27.9 4.8 %collective-permute-done.5.refs_1_ = bf16[256,256]{1,0:T(8,128)(2,1)S(1)} collective-permute-done((bf16[256,256]{1,0:T(8,128)(2,1)S(1)}, bf16[256,256]{1,0:T(8,128)(2,1)S(1)}, u32[]{:S(2)}, u32[]{:S(2)}) %collective-permute-start.5) | collective-permute-done | bytes 131104 | tf_op jit(solution)/shard_map/ppermute | solution.py:551
  32.7 0.1 collective-permute-start.6
  32.8 0.2 row_share.1.refs_0_
  33.0 1.6 %collective-permute-start.7 = (bf16[128,256]{1,0:T(8,128)(2,1)S(1)}, bf16[128,256]{1,0:T(8,128)(2,1)S(1)}, u32[]{:S(2)}, u32[]{:S(2)}) collective-permute-start(bf16[128,256]{1,0:T(8,128)(2,1)S(1)} %row_share.1.refs_0_), channel_id=1, source_target_pairs={{0,4},{4,0},{8,12},{12,8},{1,5},{5,1},{9,13},{13,9},{2,6},{6,2},{1... | collective-permute-start | bytes 196616 | tf_op jit(solution)/shard_map/ppermute | solution.py:640
  34.7 0.0 collective-permute-done.6.refs_1_
  34.7 1.5 %products.4 = bf16[256,1024]{1,0:T(8,128)(2,1)S(1)} custom-call(f32[4,32]{1,0:T(4,128)S(1)} %get-tuple-element.102.factor.token.refs_0_, f32[4,32]{1,0:T(4,128)S(1)} %get-tuple-element.102.factor.token.refs_0_, bf16[512,8192]{1,0:T(8,128)(2,1)S(1)} %get-tuple-element.57.theirs.refs_1_, bf16[512,8192]{1,0:T(8,128)(2,1)S(1)} %get-tuple-element.59.refs_1_.refs_2_, ...), custom_call_target="tpu_custom_call" | custom-call | flops 1 | bytes 1 | tf_op jit(solution)/shard_map/products/pallas_call | solution.py:242
  36.2 1.3 %collective-permute-start.9 = (bf16[256,1024]{1,0:T(8,128)(2,1)S(1)}, bf16[256,1024]{1,0:T(8,128)(2,1)S(1)}, u32[]{:S(2)}, u32[]{:S(2)}) collective-permute-start(bf16[256,1024]{1,0:T(8,128)(2,1)S(1)} %products.4), channel_id=1, source_target_pairs={{0,4},{4,0},{8,12},{12,8},{1,5},{5,1},{9,13},{13,9},{2,6},{6,2},{1... | collective-permute-start | bytes 1572872 | tf_op jit(solution)/shard_map/ppermute | solution.py:619
  37.5 0.1 collective-permute-done.7.refs_1_
  37.6 1.5 %products.5 = bf16[256,1024]{1,0:T(8,128)(2,1)S(1)} custom-call(f32[4,32]{1,0:T(4,128)S(1)} %get-tuple-element.102.factor.token.refs_0_, f32[4,32]{1,0:T(4,128)S(1)} %get-tuple-element.102.factor.token.refs_0_, bf16[512,8192]{1,0:T(8,128)(2,1)S(1)} %get-tuple-element.57.theirs.refs_1_, bf16[512,8192]{1,0:T(8,128)(2,1)S(1)} %get-tuple-element.59.refs_1_.refs_2_, ...), custom_call_target="tpu_custom_call" | custom-call | flops 1 | bytes 1 | tf_op jit(solution)/shard_map/products/pallas_call | solution.py:242
  39.2 3.5 %collective-permute-start.11 = (bf16[256,1024]{1,0:T(8,128)(2,1)S(1)}, bf16[256,1024]{1,0:T(8,128)(2,1)S(1)}, u32[]{:S(2)}, u32[]{:S(2)}) collective-permute-start(bf16[256,1024]{1,0:T(8,128)(2,1)S(1)} %products.5), channel_id=1, source_target_pairs={{0,4},{12,8},{1,5},{13,9},{2,6},{14,10},{3,7},{15,11},{16,20},{28,... | collective-permute-start | bytes 1572872 | tf_op jit(solution)/shard_map/ppermute | solution.py:619
  42.6 0.7 collective-permute-start.8
  43.3 4.4 %products.6 = (bf16[4,256,1024]{2,1,0:T(8,128)(2,1)S(1)}, bf16[256,1024]{1,0:T(8,128)(2,1)S(1)}) custom-call(f32[4,32]{1,0:T(4,128)S(1)} %get-tuple-element.102.factor.token.refs_0_, f32[4,32]{1,0:T(4,128)S(1)} %get-tuple-element.102.factor.token.refs_0_, bf16[512,8192]{1,0:T(8,128)(2,1)S(1)} %get-tuple-element.57.theirs.refs_1_, ...), custom_call_target="tpu_custom_call" | custom-call | flops 1 | bytes 1 | tf_op jit(solution)/shard_map/products/pallas_call | solution.py:242
  47.7 0.0 collective-permute-done.8.refs_1_
  47.8 2.3 %collective-permute-start.10 = (bf16[128,256]{1,0:T(8,128)(2,1)S(1)}, bf16[128,256]{1,0:T(8,128)(2,1)S(1)}, u32[]{:S(2)}, u32[]{:S(2)}) collective-permute-start(bf16[128,256]{1,0:T(8,128)(2,1)S(1)} %hop.4.refs_0_), channel_id=1, source_target_pairs={{0,4},{4,0},{8,12},{12,8},{1,5},{5,1},{9,13},{13,9},{2,6},{6,2},{1... | collective-permute-start | bytes 196616 | tf_op jit(solution)/shard_map/ppermute | solution.py:640
  50.0 1.9 %collective-permute-start.15 = (bf16[256,1024]{1,0:T(8,128)(2,1)S(1)}, bf16[256,1024]{1,0:T(8,128)(2,1)S(1)}, u32[]{:S(2)}, u32[]{:S(2)}) collective-permute-start(bf16[256,1024]{1,0:T(8,128)(2,1)S(1)} %get-tuple-element.94), channel_id=1, source_target_pairs={{0,4},{12,8},{1,5},{13,9},{2,6},{14,10},{3,7},{15,11},{16,20},{28,... | collective-permute-start | bytes 1572872 | tf_op jit(solution)/shard_map/ppermute | solution.py:619
  52.0 0.0 collective-permute-done.9.refs_1_
  52.0 0.1 operand.6
  52.1 0.7 collective-permute-start.13
  52.8 4.4 %products.7 = (bf16[4,256,1024]{2,1,0:T(8,128)(2,1)S(1)}, bf16[256,1024]{1,0:T(8,128)(2,1)S(1)}) custom-call(f32[4,32]{1,0:T(4,128)S(1)} %get-tuple-element.102.factor.token.refs_0_, f32[4,32]{1,0:T(4,128)S(1)} %get-tuple-element.102.factor.token.refs_0_, bf16[512,8192]{1,0:T(8,128)(2,1)S(1)} %get-tuple-element.57.theirs.refs_1_, ...), custom_call_target="tpu_custom_call" | custom-call | flops 1 | bytes 1 | tf_op jit(solution)/shard_map/products/pallas_call | solution.py:242
  57.2 5.2 %collective-permute-done.10.refs_1_ = bf16[128,256]{1,0:T(8,128)(2,1)S(1)} collective-permute-done((bf16[128,256]{1,0:T(8,128)(2,1)S(1)}, bf16[128,256]{1,0:T(8,128)(2,1)S(1)}, u32[]{:S(2)}, u32[]{:S(2)}) %collective-permute-start.10) | collective-permute-done | bytes 65568 | tf_op jit(solution)/shard_map/ppermute | solution.py:640
  62.5 0.0 collective-permute-done.11.refs_1_
  62.5 0.1 operand.7
  62.6 0.7 collective-permute-start.16
  63.3 7.6 %collective-permute-start.17 = (bf16[256,1024]{1,0:T(8,128)(2,1)S(1)}, bf16[256,1024]{1,0:T(8,128)(2,1)S(1)}, u32[]{:S(2)}, u32[]{:S(2)}) collective-permute-start(bf16[256,1024]{1,0:T(8,128)(2,1)S(1)} %get-tuple-element.98), channel_id=1, source_target_pairs={{0,4},{12,8},{1,5},{13,9},{2,6},{14,10},{3,7},{15,11},{16,20},{28,... | collective-permute-start | bytes 1572872 | tf_op jit(solution)/shard_map/ppermute | solution.py:619
  70.9 0.1 collective-permute-start.12
  71.0 1.0 turn.1
  72.0 0.2 collective-permute-done.12.refs_1_
  72.2 0.8 collective-permute-start.14
  73.0 0.0 collective-permute-done.13.refs_1_
  73.0 0.1 operand.8
  73.2 4.8 %collective-permute-done.14.refs_1_ = f32[128,256]{1,0:T(8,128)S(1)} collective-permute-done((f32[128,256]{1,0:T(8,128)S(1)}, f32[128,256]{1,0:T(8,128)S(1)}, u32[]{:S(2)}, u32[]{:S(2)}) %collective-permute-start.14) | collective-permute-done | bytes 131104 | tf_op jit(solution)/shard_map/ppermute | solution.py:551
  78.0 0.7 side.5
  78.7 0.1 operand.9
  78.8 0.1 operand.10
  79.0 0.7 collective-permute-start.19
  79.7 5.2 %collective-permute-done.17.refs_1_ = bf16[256,1024]{1,0:T(8,128)(2,1)S(1)} collective-permute-done((bf16[256,1024]{1,0:T(8,128)(2,1)S(1)}, bf16[256,1024]{1,0:T(8,128)(2,1)S(1)}, u32[]{:S(2)}, u32[]{:S(2)}) %collective-permute-start.17) | collective-permute-done | bytes 524320 | tf_op jit(solution)/shard_map/ppermute | solution.py:619
  84.9 0.1 operand.11
  85.1 0.7 collective-permute-start.21
  85.8 5.7 %collective-permute-start.20 = (bf16[256,1024]{1,0:T(8,128)(2,1)S(1)}, bf16[256,1024]{1,0:T(8,128)(2,1)S(1)}, u32[]{:S(2)}, u32[]{:S(2)}) collective-permute-start(bf16[256,1024]{1,0:T(8,128)(2,1)S(1)} %operand.10), channel_id=1, source_target_pairs={{0,4},{8,12},{4,0},{12,8},{1,5},{9,13},{5,1},{13,9},{2,6},{10,14},... | collective-permute-start | bytes 1572872 | tf_op jit(solution)/shard_map/ppermute | solution.py:619
  91.5 4.7 %collective-permute-done.18.refs_1_ = bf16[256,1024]{1,0:T(8,128)(2,1)S(1)} collective-permute-done((bf16[256,1024]{1,0:T(8,128)(2,1)S(1)}, bf16[256,1024]{1,0:T(8,128)(2,1)S(1)}, u32[]{:S(2)}, u32[]{:S(2)}) %collective-permute-start.18) | collective-permute-done | bytes 524320 | tf_op jit(solution)/shard_map/ppermute | solution.py:619
  96.2 0.0 collective-permute-done.19.refs_2_
  96.2 1.1 %keep.2.refs_3_ = f32[2048,256]{1,0:T(8,128)} custom-call(f32[4,32]{1,0:T(4,128)S(1)} %get-tuple-element.102.factor.token.refs_0_, bf16[4,256,1024]{2,1,0:T(8,128)(2,1)S(1)} %get-tuple-element.75.refs_0_, bf16[256,1024]{1,0:T(8,128)(2,1)S(1)} %collective-permute-done.18.refs_1_, bf16[256,1024]{1,0:T(8,128)(2,1)S(1)} %collective-permute-done.19.refs_2_), custom_call_target="tpu_custom_call" | custom-call | flops 1 | bytes 1 | tf_op jit(solution)/shard_map/keep/pallas_call | solution.py:242
  97.3 0.0 collective-permute-done.21.refs_2_
  97.3 9.3 %collective-permute-done.20.refs_1_ = bf16[256,1024]{1,0:T(8,128)(2,1)S(1)} collective-permute-done((bf16[256,1024]{1,0:T(8,128)(2,1)S(1)}, bf16[256,1024]{1,0:T(8,128)(2,1)S(1)}, u32[]{:S(2)}, u32[]{:S(2)}) %collective-permute-start.20) | collective-permute-done | bytes 524320 | tf_op jit(solution)/shard_map/ppermute | solution.py:619
  106.6 1.1 %keep.3 = f32[2048,256]{1,0:T(8,128)} custom-call(f32[4,32]{1,0:T(4,128)S(1)} %get-tuple-element.102.factor.token.refs_0_, bf16[4,256,1024]{2,1,0:T(8,128)(2,1)S(1)} %get-tuple-element.82.refs_0_, bf16[256,1024]{1,0:T(8,128)(2,1)S(1)} %collective-permute-done.20.refs_1_, ...), custom_call_target="tpu_custom_call", output_to_operand_aliasing={{}: (4, {})} | custom-call | flops 1 | bytes 1 | tf_op jit(solution)/shard_map/keep/pallas_call | solution.py:242
  (12 shorter events, 0.2 us)
Async XLA Ops:
  6.4 11.2 %collective-permute-start = (f32[256,256]{1,0:T(8,128)S(1)}, f32[256,256]{1,0:T(8,128)S(1)}, u32[]{:S(2)}, u32[]{:S(2)}) collective-permute-start(f32[256,256]{1,0:T(8,128)S(1)} %get-tuple-element.56), channel_id=1, source_target_pairs={{0,2},{2,0},{1,3},{3,1},{4,6},{6,4},{5,7},{7,5},{8,10},{10,8},{9,1... | collective-permute-start | bytes 786440 | tf_op jit(solution)/shard_map/ppermute | solution.py:551
  13.8 4.0 %collective-permute-start.2 = (f32[256,256]{1,0:T(8,128)S(1)}, f32[256,256]{1,0:T(8,128)S(1)}, u32[]{:S(2)}, u32[]{:S(2)}) collective-permute-start(f32[256,256]{1,0:T(8,128)S(1)} %get-tuple-element.63), channel_id=1, source_target_pairs={{0,1},{1,0},{2,3},{3,2},{4,5},{5,4},{6,7},{7,6},{8,9},{9,8},{10,11... | collective-permute-start | bytes 786440 | tf_op jit(solution)/shard_map/ppermute | solution.py:551
  13.9 3.9 %collective-permute-start.3 = (f32[256,256]{1,0:T(8,128)S(1)}, f32[256,256]{1,0:T(8,128)S(1)}, u32[]{:S(2)}, u32[]{:S(2)}) collective-permute-start(f32[256,256]{1,0:T(8,128)S(1)} %get-tuple-element.64), channel_id=1, source_target_pairs={{0,1},{1,0},{2,3},{3,2},{4,5},{5,4},{6,7},{7,6},{8,9},{9,8},{10,11... | collective-permute-start | bytes 786440 | tf_op jit(solution)/shard_map/ppermute | solution.py:551
  17.6 3.5 %collective-permute-start.1 = (f32[256,256]{1,0:T(8,128)S(1)}, f32[256,256]{1,0:T(8,128)S(1)}, u32[]{:S(2)}, u32[]{:S(2)}) collective-permute-start(f32[256,256]{1,0:T(8,128)S(1)} %add.3.gram_a), channel_id=1, source_target_pairs={{0,1},{1,0},{2,3},{3,2},{4,5},{5,4},{6,7},{7,6},{8,9},{9,8},{10,11... | collective-permute-start | bytes 786440 | tf_op jit(solution)/shard_map/ppermute | solution.py:551
  17.8 8.7 %collective-permute-start.4 = (f32[256,256]{1,0:T(8,128)S(1)}, f32[256,256]{1,0:T(8,128)S(1)}, u32[]{:S(2)}, u32[]{:S(2)}) collective-permute-start(f32[256,256]{1,0:T(8,128)S(1)} %add_piece.3), channel_id=1, source_target_pairs={{0,2},{2,0},{1,3},{3,1},{4,6},{6,4},{5,7},{7,5},{8,10},{10,8},{9,1... | collective-permute-start | bytes 786440 | tf_op jit(solution)/shard_map/ppermute | solution.py:551
  21.1 5.4 %copy-start = (bf16[1024,256]{1,0:T(8,128)(2,1)S(1)}, bf16[1024,256]{1,0:T(8,128)(2,1)}, u32[]{:S(2)}) copy-start(bf16[1024,256]{1,0:T(8,128)(2,1)} %refs_4_.1) | copy-start | bytes 1572868
  27.6 5.1 %collective-permute-start.5 = (bf16[256,256]{1,0:T(8,128)(2,1)S(1)}, bf16[256,256]{1,0:T(8,128)(2,1)S(1)}, u32[]{:S(2)}, u32[]{:S(2)}) collective-permute-start(bf16[256,256]{1,0:T(8,128)(2,1)S(1)} %admm.1.refs_0_), channel_id=1, source_target_pairs={{0,2},{2,0},{1,3},{3,1},{4,6},{6,4},{5,7},{7,5},{8,10},{10,8},{9,1... | collective-permute-start | bytes 393224 | tf_op jit(solution)/shard_map/ppermute | solution.py:551
  32.7 1.9 %collective-permute-start.6 = (bf16[256,512]{1,0:T(8,128)(2,1)S(1)}, bf16[256,512]{1,0:T(8,128)(2,1)S(1)}, u32[]{:S(2)}, u32[]{:S(2)}) collective-permute-start(bf16[256,512]{1,0:T(8,128)(2,1)S(1)} %side.3.refs_0_), channel_id=1, source_target_pairs={{0,1},{1,0},{2,3},{3,2},{4,5},{5,4},{6,7},{7,6},{8,9},{9,8},{10,11... | collective-permute-start | bytes 786440 | tf_op jit(solution)/shard_map/ppermute | solution.py:551
  33.0 4.6 %collective-permute-start.7 = (bf16[128,256]{1,0:T(8,128)(2,1)S(1)}, bf16[128,256]{1,0:T(8,128)(2,1)S(1)}, u32[]{:S(2)}, u32[]{:S(2)}) collective-permute-start(bf16[128,256]{1,0:T(8,128)(2,1)S(1)} %row_share.1.refs_0_), channel_id=1, source_target_pairs={{0,4},{4,0},{8,12},{12,8},{1,5},{5,1},{9,13},{13,9},{2,6},{6,2},{1... | collective-permute-start | bytes 196616 | tf_op jit(solution)/shard_map/ppermute | solution.py:640
  36.2 15.8 %collective-permute-start.9 = (bf16[256,1024]{1,0:T(8,128)(2,1)S(1)}, bf16[256,1024]{1,0:T(8,128)(2,1)S(1)}, u32[]{:S(2)}, u32[]{:S(2)}) collective-permute-start(bf16[256,1024]{1,0:T(8,128)(2,1)S(1)} %products.4), channel_id=1, source_target_pairs={{0,4},{4,0},{8,12},{12,8},{1,5},{5,1},{9,13},{13,9},{2,6},{6,2},{1... | collective-permute-start | bytes 1572872 | tf_op jit(solution)/shard_map/ppermute | solution.py:619
  39.2 23.3 %collective-permute-start.11 = (bf16[256,1024]{1,0:T(8,128)(2,1)S(1)}, bf16[256,1024]{1,0:T(8,128)(2,1)S(1)}, u32[]{:S(2)}, u32[]{:S(2)}) collective-permute-start(bf16[256,1024]{1,0:T(8,128)(2,1)S(1)} %products.5), channel_id=1, source_target_pairs={{0,4},{12,8},{1,5},{13,9},{2,6},{14,10},{3,7},{15,11},{16,20},{28,... | collective-permute-start | bytes 1572872 | tf_op jit(solution)/shard_map/ppermute | solution.py:619
  42.6 5.1 %collective-permute-start.8 = (bf16[128,256]{1,0:T(8,128)(2,1)S(1)}, bf16[128,256]{1,0:T(8,128)(2,1)S(1)}, u32[]{:S(2)}, u32[]{:S(2)}) collective-permute-start(bf16[128,256]{1,0:T(8,128)(2,1)S(1)} %hop.3.refs_0_), channel_id=1, source_target_pairs={{4,8},{8,4},{5,9},{9,5},{6,10},{10,6},{7,11},{11,7},{20,24},{24,20... | collective-permute-start | bytes 196616 | tf_op jit(solution)/shard_map/ppermute | solution.py:640
  47.8 14.7 %collective-permute-start.10 = (bf16[128,256]{1,0:T(8,128)(2,1)S(1)}, bf16[128,256]{1,0:T(8,128)(2,1)S(1)}, u32[]{:S(2)}, u32[]{:S(2)}) collective-permute-start(bf16[128,256]{1,0:T(8,128)(2,1)S(1)} %hop.4.refs_0_), channel_id=1, source_target_pairs={{0,4},{4,0},{8,12},{12,8},{1,5},{5,1},{9,13},{13,9},{2,6},{6,2},{1... | collective-permute-start | bytes 196616 | tf_op jit(solution)/shard_map/ppermute | solution.py:640
  50.0 28.7 %collective-permute-start.15 = (bf16[256,1024]{1,0:T(8,128)(2,1)S(1)}, bf16[256,1024]{1,0:T(8,128)(2,1)S(1)}, u32[]{:S(2)}, u32[]{:S(2)}) collective-permute-start(bf16[256,1024]{1,0:T(8,128)(2,1)S(1)} %get-tuple-element.94), channel_id=1, source_target_pairs={{0,4},{12,8},{1,5},{13,9},{2,6},{14,10},{3,7},{15,11},{16,20},{28,... | collective-permute-start | bytes 1572872 | tf_op jit(solution)/shard_map/ppermute | solution.py:619
  52.1 20.9 %collective-permute-start.13 = (bf16[256,1024]{1,0:T(8,128)(2,1)S(1)}, bf16[256,1024]{1,0:T(8,128)(2,1)S(1)}, u32[]{:S(2)}, u32[]{:S(2)}) collective-permute-start(bf16[256,1024]{1,0:T(8,128)(2,1)S(1)} %operand.6), channel_id=1, source_target_pairs={{4,8},{8,4},{5,9},{9,5},{6,10},{10,6},{7,11},{11,7},{20,24},{24,20... | collective-permute-start | bytes 1572872 | tf_op jit(solution)/shard_map/ppermute | solution.py:619
  62.6 16.2 %collective-permute-start.16 = (bf16[256,1024]{1,0:T(8,128)(2,1)S(1)}, bf16[256,1024]{1,0:T(8,128)(2,1)S(1)}, u32[]{:S(2)}, u32[]{:S(2)}) collective-permute-start(bf16[256,1024]{1,0:T(8,128)(2,1)S(1)} %operand.7), channel_id=1, source_target_pairs={{4,8},{8,4},{5,9},{9,5},{6,10},{10,6},{7,11},{11,7},{20,24},{24,20... | collective-permute-start | bytes 1572872 | tf_op jit(solution)/shard_map/ppermute | solution.py:619
  63.3 21.6 %collective-permute-start.17 = (bf16[256,1024]{1,0:T(8,128)(2,1)S(1)}, bf16[256,1024]{1,0:T(8,128)(2,1)S(1)}, u32[]{:S(2)}, u32[]{:S(2)}) collective-permute-start(bf16[256,1024]{1,0:T(8,128)(2,1)S(1)} %get-tuple-element.98), channel_id=1, source_target_pairs={{0,4},{12,8},{1,5},{13,9},{2,6},{14,10},{3,7},{15,11},{16,20},{28,... | collective-permute-start | bytes 1572872 | tf_op jit(solution)/shard_map/ppermute | solution.py:619
  70.9 1.3 %collective-permute-start.12 = (bf16[128,256]{1,0:T(8,128)(2,1)S(1)}, bf16[128,256]{1,0:T(8,128)(2,1)S(1)}, u32[]{:S(2)}, u32[]{:S(2)}) collective-permute-start(bf16[128,256]{1,0:T(8,128)(2,1)S(1)} %hop.5.refs_0_), channel_id=1, source_target_pairs={{0,1},{1,0},{2,3},{3,2},{4,5},{5,4},{6,7},{7,6},{8,9},{9,8},{10,11... | collective-permute-start | bytes 196616 | tf_op jit(solution)/shard_map/ppermute | solution.py:551
  72.2 5.7 %collective-permute-start.14 = (f32[128,256]{1,0:T(8,128)S(1)}, f32[128,256]{1,0:T(8,128)S(1)}, u32[]{:S(2)}, u32[]{:S(2)}) collective-permute-start(f32[128,256]{1,0:T(8,128)S(1)} %plus.1.refs_0_), channel_id=1, source_target_pairs={{0,2},{2,0},{1,3},{3,1},{4,6},{6,4},{5,7},{7,5},{8,10},{10,8},{9,1... | collective-permute-start | bytes 393224 | tf_op jit(solution)/shard_map/ppermute | solution.py:551
  78.7 17.5 %collective-permute-start.18 = (bf16[256,1024]{1,0:T(8,128)(2,1)S(1)}, bf16[256,1024]{1,0:T(8,128)(2,1)S(1)}, u32[]{:S(2)}, u32[]{:S(2)}) collective-permute-start(bf16[256,1024]{1,0:T(8,128)(2,1)S(1)} %operand.8), channel_id=1, source_target_pairs={{0,4},{8,12},{4,0},{12,8},{1,5},{9,13},{5,1},{13,9},{2,6},{10,14},... | collective-permute-start | bytes 1572872 | tf_op jit(solution)/shard_map/ppermute | solution.py:619
  79.0 17.2 %collective-permute-start.19 = (bf16[256,1024]{1,0:T(8,128)(2,1)S(1)}, bf16[256,1024]{1,0:T(8,128)(2,1)S(1)}, u32[]{:S(2)}, u32[]{:S(2)}) collective-permute-start(bf16[256,1024]{1,0:T(8,128)(2,1)S(1)} %operand.9), channel_id=1, source_target_pairs={{4,8},{8,4},{5,9},{9,5},{6,10},{10,6},{7,11},{11,7},{20,24},{24,20... | collective-permute-start | bytes 1572872 | tf_op jit(solution)/shard_map/ppermute | solution.py:619
  85.1 12.3 %collective-permute-start.21 = (bf16[256,1024]{1,0:T(8,128)(2,1)S(1)}, bf16[256,1024]{1,0:T(8,128)(2,1)S(1)}, u32[]{:S(2)}, u32[]{:S(2)}) collective-permute-start(bf16[256,1024]{1,0:T(8,128)(2,1)S(1)} %operand.11), channel_id=1, source_target_pairs={{4,8},{8,4},{5,9},{9,5},{6,10},{10,6},{7,11},{11,7},{20,24},{24,20... | collective-permute-start | bytes 1572872 | tf_op jit(solution)/shard_map/ppermute | solution.py:619
  85.8 20.8 %collective-permute-start.20 = (bf16[256,1024]{1,0:T(8,128)(2,1)S(1)}, bf16[256,1024]{1,0:T(8,128)(2,1)S(1)}, u32[]{:S(2)}, u32[]{:S(2)}) collective-permute-start(bf16[256,1024]{1,0:T(8,128)(2,1)S(1)} %operand.10), channel_id=1, source_target_pairs={{0,4},{8,12},{4,0},{12,8},{1,5},{9,13},{5,1},{13,9},{2,6},{10,14},... | collective-permute-start | bytes 1572872 | tf_op jit(solution)/shard_map/ppermute | solution.py:619

commit v12 on v11

--- a/solution.py
+++ b/solution.py
@@ -49,28 +49,49 @@
     ]
 
 
+def pieces_of(rows, bit):
+    core = lax.axis_index("sub")
+    upper = (lax.axis_index("gene") & bit) != 0
+    half, quarter = rows // 2, rows // 4
+    mine = core * half
+    kept = jnp.where(upper, quarter, 0)
+    return [
+        pl.multiple_of((1 - core) * half, quarter),
+        pl.multiple_of(mine + quarter - kept, quarter),
+        pl.multiple_of(mine + kept, quarter),
+    ]
+
+
 def load_kernel(
-    genes, counts, tile_mask, tile_counts, gram, factor, turned, theirs,
-    genes_here, mask_here, counts_here, gene_sems, row_sems, small_sems,
+    bit, genes, counts, tile_mask, tile_counts, gram, scales, turned, first,
+    genes_here, mask_here, counts_here, gene_sems, row_sems, sent_sems, small_sems,
 ):
     small_copies = [
         pltpu.make_async_copy(tile_mask, mask_here, small_sems.at[0]),
         pltpu.make_async_copy(tile_counts, counts_here, small_sems.at[1]),
     ]
     gene_copies = row_copies(genes, genes_here, 0, gene_sems)
-    half = theirs.shape[0]
-    other_core = 1 - lax.axis_index("sub")
-    row_starts = row_copies(counts, theirs, pl.multiple_of(other_core * half, half), row_sems)
+    rows = counts.shape[0]
+    half = rows // 2
+    theirs, sent, _ = pieces_of(rows, bit)
+    row_starts = row_copies(counts, first.at[:half], theirs, row_sems)
+    row_starts += row_copies(counts, first.at[half:], sent, sent_sems)
     for copy in gene_copies + small_copies:
         copy.start()
     for copy in small_copies:
         copy.wait()
-    factor[...] = mask_here[...].astype(F32) / counts_here[...].astype(F32)
+    ratio = mask_here[...].astype(F32) / counts_here[...].astype(F32)
+    columns = genes.shape[1]
+    tile = columns // ratio.shape[1]
+    for row in range(ratio.shape[0]):
+        for col in range(ratio.shape[1]):
+            scales[row * 8 : row * 8 + 8, col * tile : (col + 1) * tile] = jnp.broadcast_to(
+                ratio[row : row + 1, col : col + 1], (8, tile)
+            )
     for copy in gene_copies:
         copy.wait()
     for copy in row_starts:
         copy.start()
-    columns = genes.shape[1]
     wide = min(1024, columns)
     gram[...] = jnp.zeros_like(gram)
 
@@ -85,18 +106,18 @@
         copy.wait()
 
 
-def load(genes, counts, tile_mask, tile_counts):
+def load(bit, genes, counts, tile_mask, tile_counts):
     width, columns = genes.shape
     rows = counts.shape[0]
     here = pl.BlockSpec(memory_space=pltpu.VMEM)
     there = pl.BlockSpec(memory_space=pltpu.HBM)
     return pl.pallas_call(
-        load_kernel,
+        functools.partial(load_kernel, bit),
         out_shape=(
             jax.ShapeDtypeStruct((width, width), F32),
-            jax.ShapeDtypeStruct(tile_mask.shape, F32),
+            jax.ShapeDtypeStruct((tile_mask.shape[0] * 8, columns), F32),
             pltpu.VMEM((columns, width), BF16),
-            pltpu.VMEM((rows // 2, columns), BF16),
+            pltpu.VMEM((rows // 4 * 3, columns), BF16),
         ),
         in_specs=[there] * 4,
         out_specs=(here,) * 4,
@@ -106,6 +127,7 @@
             pltpu.VMEM(tile_mask.shape, jnp.int32),
             pltpu.SemaphoreType.DMA((4,)),
             pltpu.SemaphoreType.DMA((8,)),
+            pltpu.SemaphoreType.DMA((4,)),
             pltpu.SemaphoreType.DMA((2,)),
         ],
         compiler_params=params(),
@@ -114,100 +136,84 @@
     )(away(genes), away(counts), away(tile_mask), away(tile_counts))
 
 
-def scaled(counts, factors):
-    tile_rows = counts.shape[0] // len(factors)
-    tile_columns = counts.shape[1] // len(factors[0])
-    rows = []
-    for row, scales in enumerate(factors):
-        part = counts[row * tile_rows : (row + 1) * tile_rows]
-        rows.append(
-            jnp.concatenate(
-                [
-                    (
-                        part[:, col * tile_columns : (col + 1) * tile_columns].astype(F32) * scale
-                    ).astype(BF16)
-                    for col, scale in enumerate(scales)
-                ],
-                axis=1,
-            )
+def scaled(counts, at, row_tiles, scales):
+    tile = counts.shape[0] // len(row_tiles)
+    return jnp.concatenate(
+        [
+            (
+                counts[i * tile : (i + 1) * tile, at].astype(F32)
+                * scales[pl.ds(pl.multiple_of(row * 8, 8), 8), at][0:1]
+            ).astype(BF16)
+            for i, row in enumerate(row_tiles)
+        ],
+        axis=0,
+    )
+
+
+def cross_rows(row_tiles, scales, counts, turned, total):
+    columns = counts.shape[1]
+    wide = min(1024, columns)
+    total[...] = jnp.zeros_like(total)
+
+    @pl.loop(0, columns // wide)
+    def _(step):
+        at = pl.ds(pl.multiple_of(step * wide, wide), wide)
+        total[...] += jnp.dot(
+            scaled(counts, at, row_tiles, scales), turned[at, :], preferred_element_type=F32
         )
-    return jnp.concatenate(rows, axis=0)
-
-
-def add_cross(first_row, factor, counts, turned, total):
-    gene_tiles = factor.shape[1]
-    tile = counts.shape[1] // gene_tiles
-    row_tiles = counts.shape[0] // tile
-    at_once = min(4, gene_tiles)
-
-    @pl.loop(0, gene_tiles // at_once)
-    def _(step):
-        at = pl.ds(pl.multiple_of(step * at_once * tile, at_once * tile), at_once * tile)
-        factors = [
-            [factor[first_row + row, step * at_once + col] for col in range(at_once)]
-            for row in range(row_tiles)
-        ]
-        total[...] += jnp.dot(
-            scaled(counts[:, at], factors), turned[at, :], preferred_element_type=F32
-        )
-
-
-def cross_theirs_kernel(factor, theirs, turned, counts, low, high, mine, total, sems):
-    half = theirs.shape[0]
-    core = lax.axis_index("sub")
-    copies = row_copies(counts, mine, pl.multiple_of(core * half, half), sems)
+
+
+def tiles_from(start, rows, tile):
+    return [start // tile + i for i in range(rows // tile)]
+
+
+def cross_first_kernel(bit, scales, first, turned, counts, low, high, sent, kept, total, sems):
+    rows = counts.shape[0]
+    half, quarter, tile = rows // 2, rows // 4, rows // (scales.shape[0] // 8)
+    theirs_at, sent_at, kept_at = pieces_of(rows, bit)
+    copies = row_copies(counts, kept, kept_at, sems)
     for copy in copies:
         copy.start()
-    total[...] = jnp.zeros_like(total)
-    add_cross((1 - core) * (factor.shape[0] // 2), factor, theirs, turned, total)
-    low[...] = total[: half // 2].T
-    high[...] = total[half // 2 :].T
+    row_tiles = tiles_from(theirs_at, half, tile) + tiles_from(sent_at, quarter, tile)
+    cross_rows(row_tiles, scales, first, turned, total)
+    low[...] = total[:quarter].T
+    high[...] = total[quarter:half].T
+    sent[...] = total[half:].T
     for copy in copies:
         copy.wait()
 
 
-def cross_theirs(factor, theirs, turned, counts):
-    half, columns = theirs.shape
+def cross_first(bit, scales, first, turned, counts):
+    rows, columns = counts.shape
     width = turned.shape[1]
     here = pl.BlockSpec(memory_space=pltpu.VMEM)
-    piece = jax.ShapeDtypeStruct((width, half // 2), F32)
+    piece = jax.ShapeDtypeStruct((width, rows // 4), F32)
     return pl.pallas_call(
-        cross_theirs_kernel,
-        out_shape=(piece, piece, pltpu.VMEM((half, columns), BF16)),
-        in_specs=[
-            pl.BlockSpec(memory_space=pltpu.SMEM),
-            here,
-            here,
-            pl.BlockSpec(memory_space=pltpu.HBM),
-        ],
-        out_specs=(here,) * 3,
-        scratch_shapes=[pltpu.VMEM((half, width), F32), pltpu.SemaphoreType.DMA((8,))],
+        functools.partial(cross_first_kernel, bit),
+        out_shape=(piece, piece, piece, pltpu.VMEM((rows // 4, columns), BF16)),
+        in_specs=[here, here, here, pl.BlockSpec(memory_space=pltpu.HBM)],
+        out_specs=(here,) * 4,
+        scratch_shapes=[pltpu.VMEM(first.shape[:1] + (width,), F32), pltpu.SemaphoreType.DMA((4,))],
         compiler_params=params(),
         cost_estimate=cost(1, 1),
-        name="cross_theirs",
-    )(factor, held(theirs), held(turned), away(counts))
-
-
-def cross_piece_kernel(bit, kept, factor, mine, turned, cross, total):
-    rows = total.shape[0]
-    upper = ((lax.axis_index("gene") & bit) != 0) == kept
-    piece = jnp.where(upper, 1, 0)
-    first = lax.axis_index("sub") * (factor.shape[0] // 2)
-    first += piece * (factor.shape[0] // 4)
-    total[...] = jnp.zeros_like(total)
-    counts = mine.at[pl.ds(pl.multiple_of(piece * rows, rows), rows)]
-    add_cross(first, factor, counts, turned, total)
+        name="cross_first",
+    )(scales, held(first), held(turned), away(counts))
+
+
+def cross_kept_kernel(bit, scales, kept, turned, cross, total):
+    rows = kept.shape[0] * 4
+    tile = rows // (scales.shape[0] // 8)
+    row_tiles = tiles_from(pieces_of(rows, bit)[2], rows // 4, tile)
+    cross_rows(row_tiles, scales, kept, turned, total)
     cross[...] = total[...].T
 
 
-def cross_piece(bit, kept, token, factor, mine, turned):
-    rows = mine.shape[0] // 2
-    width = turned.shape[1]
+def cross_kept(bit, token, scales, kept, turned):
+    rows, width = kept.shape[0], turned.shape[1]
     return call(
-        functools.partial(cross_piece_kernel, bit, kept),
-        "cross_piece", jax.ShapeDtypeStruct((width, rows), F32), token,
-        factor, held(mine), held(turned),
-        smem=1, scratch=[pltpu.VMEM((rows, width), F32)],
+        functools.partial(cross_kept_kernel, bit),
+        "cross_kept", jax.ShapeDtypeStruct((width, rows), F32), token,
+        scales, held(kept), held(turned), scratch=[pltpu.VMEM((rows, width), F32)],
     )
 
 
@@ -230,12 +236,11 @@
     )
 
 
-def call(kernel, name, out_shape, token, *args, scratch=(), smem=0, aliases=None, out=None):
+def call(kernel, name, out_shape, token, *args, scratch=(), aliases=None, out=None):
     here = pl.BlockSpec(memory_space=pltpu.VMEM)
-    there = pl.BlockSpec(memory_space=pltpu.SMEM)
     wherever = pl.BlockSpec(memory_space=pl.ANY)
     single = not isinstance(out_shape, tuple)
-    specs = [there] * smem + [here] * (len(args) - smem)
+    specs = [here] * len(args)
     if aliases:
         specs[-1] = wherever
     out = out or here
@@ -382,33 +387,32 @@
     columns_out[...] = zvalue.astype(BF16)
 
 
-def products_kernel(tile, line, start, chunk, factor, theirs, mine, columns, *outs):
+def products_kernel(tile, bit, line, start, chunk, scales, first, kept, columns, *outs):
     only_first = len(outs) == 1
     block = line.block(1 if only_first else 2, 0)
-    size = mine.shape[1] // line.size
+    size = first.shape[1] // line.size
     span = min(tile, chunk)
     wide = 2 * span if chunk % (2 * span) == 0 else span
     steps = chunk // wide
-    row_tiles = columns.shape[1] // tile // 2
-    core = lax.axis_index("sub")
+    rows = columns.shape[1]
+    half = rows // 2
+    theirs_at, sent_at, kept_at = pieces_of(rows, bit)
+    groups = [
+        (first.at[:half], theirs_at),
+        (first.at[half:], sent_at),
+        (kept, kept_at),
+    ]
 
     @pl.loop(0, steps if only_first else line.size * steps)
     def _(turn):
         order, step = (block, turn) if only_first else (turn // steps, lax.rem(turn, steps))
-        first = pl.multiple_of(order * size + start + step * wide, span)
+        genes = pl.ds(pl.multiple_of(order * size + start + step * wide, span), wide)
         total = None
-        for counts, side in ((theirs, 1 - core), (mine, core)):
-            factors = [
-                [
-                    factor[side * row_tiles + row, (first + col * span) // tile]
-                    for col in range(wide // span)
-                ]
-                for row in range(row_tiles)
-            ]
-            cells = row_tiles * tile
+        for counts, place in groups:
+            cells = counts.shape[0]
             part = jnp.dot(
-                columns[:, pl.ds(pl.multiple_of(side * cells, cells), cells)],
-                scaled(counts[:, pl.ds(first, wide)], factors),
+                columns[:, pl.ds(place, cells)],
+                scaled(counts, genes, tiles_from(place, cells, tile), scales),
                 preferred_element_type=F32,
             )
             total = part if total is None else total + part
@@ -424,15 +428,15 @@
                 outs[1][:, at] = total
 
 
-def products(only_first, line, start, chunk, token, factor, theirs, mine, columns):
+def products(only_first, bit, line, start, chunk, token, scales, first, kept, columns):
     width, rows = columns.shape
-    tile = rows // factor.shape[0]
+    tile = rows // (scales.shape[0] // 8)
     out_shape = (jax.ShapeDtypeStruct((width, chunk), BF16),)
     if not only_first:
         out_shape = (jax.ShapeDtypeStruct((line.size, width, chunk), BF16),) + out_shape
     return call(
-        functools.partial(products_kernel, tile, line, start, chunk),
-        "products", out_shape, token, factor, held(theirs), held(mine), columns, smem=1,
+        functools.partial(products_kernel, tile, bit, line, start, chunk),
+        "products", out_shape, token, scales, held(first), held(kept), columns,
     )
 
 
@@ -574,17 +578,18 @@
     width = gene_factor.shape[0]
     line = Line(cells)
 
-    gram, factor, turned, theirs = load(gene_factor, counts, tile_mask, tile_counts)
-    token = factor
-    theirs_low, theirs_high, mine = cross_theirs(factor, theirs, turned, counts)
+    half_bit = bit = genes // 2
+    gram, scales, turned, first_rows = load(bit, gene_factor, counts, tile_mask, tile_counts)
+    token = scales
+    theirs_low, theirs_high, own_sent, kept = cross_first(
+        bit, scales, first_rows, turned, counts
+    )
     arrived_low = swap(theirs_low, "sub", subs, 1)
     arrived_high = swap(theirs_high, "sub", subs, 1)
-    bit = genes // 2
-    own_sent = cross_piece(bit, False, token, factor, mine, turned)
     sent = add_piece(bit, False, token, own_sent, arrived_low, arrived_high)
     cross_b = swap(sent, "gene", genes, bit)
-    gram, (factor_late, _) = pair_sums(gram, "gene", genes, (factor, own_sent))
-    cross_a = cross_piece(bit, True, token, factor_late, mine, turned)
+    gram, (scales_late, _) = pair_sums(gram, "gene", genes, (scales, own_sent))
+    cross_a = cross_kept(bit, token, scales_late, kept, turned)
     cross_a = add_piece(bit, True, token, cross_a, arrived_low, arrived_high)
     bit //= 2
     while bit:
@@ -647,7 +652,7 @@
 
     for index in every:
         (first,) = products(
-            True, line, starts[index], chunks[index], token, factor, theirs, mine, whole
+            True, half_bit, line, starts[index], chunks[index], token, scales, first_rows, kept, whole
         )
         token, first = after(token, first)
         for parity in (0, 1):
@@ -657,7 +662,7 @@
     totals, seconds = [], []
     for index in every:
         total, second = products(
-            False, line, starts[index], chunks[index], token, factor, theirs, mine, whole
+            False, half_bit, line, starts[index], chunks[index], token, scales, first_rows, kept, whole
         )
         token, second = after(token, second)
         if hops:

time: 108 us -> 107 us (level)
  Pallas kernels: 38.1 us -> 34 us
  starting transfers between devices: 32.4 us -> 35.7 us
    pallas_call x26 -> x25, Pallas kernels: 24.5 us -> 18.5 us  [call(): pl.pallas_call(lambda token, *refs: kernel(*refs), out_shape=out_shape, i...]
    ppermute x9, starting transfers between devices: 5.03 us -> 8.32 us  [swap(): return lax.ppermute(value, axis, [(i, i ^ step) for i in range(size)])]
    ppermute x9, waiting for transfers between devices: 11.7 us -> 9.79 us  [swap(): return lax.ppermute(value, axis, [(i, i ^ step) for i in range(size)])]
    pallas_call x2, Pallas kernels: 10.2 us -> 12 us  [the longest x1 7.04 us: load(): pl.pallas_call(functools.partial(load_kernel, bit), out_shape=(jax.ShapeD...]
    ppermute x3, waiting for transfers between devices: 5.29 us -> 6.92 us  [hop_rows(): rows_arrived = lax.ppermute(rows_sum, 'cell', both)]
  transfers between devices with their start and end apart: 22 -> 22, of which waited for: 9 -> 12; matrix products, arithmetic and copies ran while one was open for 0% -> 0% of each run, Pallas kernels for 28% -> 23%
where the time goes in v12:
time: 107 us
  waiting for transfers between devices  36 us (34%)
  starting transfers between devices  35.7 us (33%)
  Pallas kernels  34 us (32%)
    ppermute x10, starting transfers between devices, send(): lax.ppermute(value, 'cell', pairs)  22.8 us
    ppermute x10, waiting for transfers between devices, send(): lax.ppermute(value, 'cell', pairs)  19.2 us
    pallas_call x25, Pallas kernels, call(): pl.pallas_call(lambda token, *refs: kernel(*refs), out_shape=out_shape, i...  18.5 us
    ppermute x9, waiting for transfers between devices, swap(): return lax.ppermute(value, axis, [(i, i ^ step) for i in range(size)])  9.79 us
    ppermute x9, starting transfers between devices, swap(): return lax.ppermute(value, axis, [(i, i ^ step) for i in range(size)])  8.32 us
    pallas_call x1, Pallas kernels, load(): pl.pallas_call(functools.partial(load_kernel, bit), out_shape=(jax.ShapeD...  7.04 us
    ppermute x3, waiting for transfers between devices, hop_rows(): rows_arrived = lax.ppermute(rows_sum, 'cell', both)  6.92 us
    pallas_call x1, Pallas kernels, cross_first(): pl.pallas_call(functools.partial(cross_first_kernel, bit), out_shape=(pie...  5 us
  transfers between devices with their start and end apart: 22, of which 12 were waited for; matrix products, arithmetic and copies ran while one was open for 0% of the time, Pallas kernels for 23%

profile of v12, /device:TPU:0, one launch (start us, length us, event | category | flops | bytes accessed | tf_op | source)
XLA Modules:
  0.0 106.7 jit_solution(10646308792501622208)
XLA Ops:
  0.6 7.0 %load.1 = (f32[256,256]{1,0:T(8,128)S(1)}, f32[32,8192]{1,0:T(8,128)S(1)}, bf16[8192,256]{1,0:T(8,128)(2,1)S(1)}, bf16[768,8192]{1,0:T(8,128)(2,1)S(1)}) custom-call(bf16[256,8192]{1,0:T(8,128)(2,1)} %genes.1, bf16[1024,8192]{1,0:T(8,128)(2,1)} %counts.3, s32[4,32]{1,0:T(4,128)} %tile_mask.1, s32[4,32]{1,0:T(4,128)} %tile_counts.1), custom_call_target="tpu_custom_call" | custom-call | flops 1 | bytes 1 | tf_op jit(solution)/shard_map/load/pallas_call | solution.py:114
  7.7 3.0 %collective-permute-start = (f32[256,256]{1,0:T(8,128)S(1)}, f32[256,256]{1,0:T(8,128)S(1)}, u32[]{:S(2)}, u32[]{:S(2)}) collective-permute-start(f32[256,256]{1,0:T(8,128)S(1)} %get-tuple-element.57), channel_id=1, source_target_pairs={{0,2},{2,0},{1,3},{3,1},{4,6},{6,4},{5,7},{7,5},{8,10},{10,8},{9,1... | collective-permute-start | bytes 786440 | tf_op jit(solution)/shard_map/ppermute | solution.py:555
  10.7 5.0 %cross_first.1 = (f32[256,256]{1,0:T(8,128)S(1)}, f32[256,256]{1,0:T(8,128)S(1)}, f32[256,256]{1,0:T(8,128)S(1)}, bf16[256,8192]{1,0:T(8,128)(2,1)S(1)}) custom-call(f32[32,8192]{1,0:T(8,128)S(1)} %get-tuple-element.104.scales.token.refs_0_, bf16[768,8192]{1,0:T(8,128)(2,1)S(1)} %get-tuple-element.58.first.refs_1_, ...), custom_call_target="tpu_custom_call" | custom-call | flops 1 | bytes 1 | tf_op jit(solution)/shard_map/cross_first/pallas_call | solution.py:191
  15.7 0.1 collective-permute-start.2
  15.8 0.5 collective-permute-start.3
  16.3 0.7 collective-permute-done
  17.0 0.1 collective-permute-start.1
  17.1 0.2 collective-permute-done.2.refs_1_
  17.3 0.4 collective-permute-done.3.refs_2_
  17.7 1.3 %collective-permute-start.4 = (f32[256,256]{1,0:T(8,128)S(1)}, f32[256,256]{1,0:T(8,128)S(1)}, u32[]{:S(2)}, u32[]{:S(2)}) collective-permute-start(f32[256,256]{1,0:T(8,128)S(1)} %add_piece.3), channel_id=1, source_target_pairs={{0,2},{2,0},{1,3},{3,1},{4,6},{6,4},{5,7},{7,5},{8,10},{10,8},{9,1... | collective-permute-start | bytes 786440 | tf_op jit(solution)/shard_map/ppermute | solution.py:555
  19.0 2.6 %cross_kept.1.refs_0_ = f32[256,256]{1,0:T(8,128)S(1)} custom-call(f32[32,8192]{1,0:T(8,128)S(1)} %get-tuple-element.104.scales.token.refs_0_, f32[32,8192]{1,0:T(8,128)S(1)} %get-tuple-element.104.scales.token.refs_0_, bf16[256,8192]{1,0:T(8,128)(2,1)S(1)} %get-tuple-element.64.refs_1_.refs_2_, bf16[8192,256]{1,0:T(8,128)(2,1)S(1)} %get-tuple-element.59.turned.refs_2_), custom_call_target="tpu_custom_call" | custom-call | flops 1 | bytes 1 | tf_op jit(solution)/shard_map/cross_kept/pallas_call | solution.py:247
  21.7 0.0 copy-start
  21.7 0.0 collective-permute-done.1.gram_b
  21.7 3.5 %inverse.1 = (f32[256,256]{1,0:T(8,128)S(1)}, f32[8,128]{1,0:T(8,128)S(1)}) custom-call(f32[256,256]{1,0:T(8,128)S(1)} %add.3.gram_a, f32[256,256]{1,0:T(8,128)S(1)} %collective-permute-done.1.gram_b), custom_call_target="tpu_custom_call" | custom-call | flops 2013265920 | bytes 786432 | tf_op jit(solution)/shard_map/inverse/pallas_call | solution.py:361
  25.2 0.9 collective-permute-done.4.refs_2_
  26.1 1.0 admm.1.refs_0_
  27.2 1.6 %collective-permute-start.5 = (bf16[256,256]{1,0:T(8,128)(2,1)S(1)}, bf16[256,256]{1,0:T(8,128)(2,1)S(1)}, u32[]{:S(2)}, u32[]{:S(2)}) collective-permute-start(bf16[256,256]{1,0:T(8,128)(2,1)S(1)} %admm.1.refs_0_), channel_id=1, source_target_pairs={{0,2},{2,0},{1,3},{3,1},{4,6},{6,4},{5,7},{7,5},{8,10},{10,8},{9,1... | collective-permute-start | bytes 393224 | tf_op jit(solution)/shard_map/ppermute | solution.py:555
  28.8 3.4 %collective-permute-done.5.refs_1_ = bf16[256,256]{1,0:T(8,128)(2,1)S(1)} collective-permute-done((bf16[256,256]{1,0:T(8,128)(2,1)S(1)}, bf16[256,256]{1,0:T(8,128)(2,1)S(1)}, u32[]{:S(2)}, u32[]{:S(2)}) %collective-permute-start.5) | collective-permute-done | bytes 131104 | tf_op jit(solution)/shard_map/ppermute | solution.py:555
  32.2 0.1 collective-permute-start.6
  32.3 0.2 row_share.1.refs_0_
  32.5 1.7 %collective-permute-start.7 = (bf16[128,256]{1,0:T(8,128)(2,1)S(1)}, bf16[128,256]{1,0:T(8,128)(2,1)S(1)}, u32[]{:S(2)}, u32[]{:S(2)}) collective-permute-start(bf16[128,256]{1,0:T(8,128)(2,1)S(1)} %row_share.1.refs_0_), channel_id=1, source_target_pairs={{0,4},{4,0},{8,12},{12,8},{1,5},{5,1},{9,13},{13,9},{2,6},{6,2},{1... | collective-permute-start | bytes 196616 | tf_op jit(solution)/shard_map/ppermute | solution.py:645
  34.2 0.0 collective-permute-done.6.refs_1_
  34.3 1.0 products.4
  35.2 1.3 %collective-permute-start.9 = (bf16[256,1024]{1,0:T(8,128)(2,1)S(1)}, bf16[256,1024]{1,0:T(8,128)(2,1)S(1)}, u32[]{:S(2)}, u32[]{:S(2)}) collective-permute-start(bf16[256,1024]{1,0:T(8,128)(2,1)S(1)} %products.4), channel_id=1, source_target_pairs={{0,4},{4,0},{8,12},{12,8},{1,5},{5,1},{9,13},{13,9},{2,6},{6,2},{1... | collective-permute-start | bytes 1572872 | tf_op jit(solution)/shard_map/ppermute | solution.py:624
  36.5 0.6 collective-permute-done.7.refs_1_
  37.1 1.0 products.5
  38.1 3.6 %collective-permute-start.11 = (bf16[256,1024]{1,0:T(8,128)(2,1)S(1)}, bf16[256,1024]{1,0:T(8,128)(2,1)S(1)}, u32[]{:S(2)}, u32[]{:S(2)}) collective-permute-start(bf16[256,1024]{1,0:T(8,128)(2,1)S(1)} %products.5), channel_id=1, source_target_pairs={{0,4},{12,8},{1,5},{13,9},{2,6},{14,10},{3,7},{15,11},{16,20},{28,... | collective-permute-start | bytes 1572872 | tf_op jit(solution)/shard_map/ppermute | solution.py:624
  41.6 0.7 collective-permute-start.8
  42.3 3.8 %products.6 = (bf16[4,256,1024]{2,1,0:T(8,128)(2,1)S(1)}, bf16[256,1024]{1,0:T(8,128)(2,1)S(1)}) custom-call(f32[32,8192]{1,0:T(8,128)S(1)} %get-tuple-element.104.scales.token.refs_0_, f32[32,8192]{1,0:T(8,128)S(1)} %get-tuple-element.104.scales.token.refs_0_, bf16[768,8192]{1,0:T(8,128)(2,1)S(1)} %get-tuple-element.58.first.refs_1_, ...), custom_call_target="tpu_custom_call" | custom-call | flops 1 | bytes 1 | tf_op jit(solution)/shard_map/products/pallas_call | solution.py:247
  46.1 0.0 collective-permute-done.8.refs_1_
  46.2 2.2 %collective-permute-start.10 = (bf16[128,256]{1,0:T(8,128)(2,1)S(1)}, bf16[128,256]{1,0:T(8,128)(2,1)S(1)}, u32[]{:S(2)}, u32[]{:S(2)}) collective-permute-start(bf16[128,256]{1,0:T(8,128)(2,1)S(1)} %hop.4.refs_0_), channel_id=1, source_target_pairs={{0,4},{4,0},{8,12},{12,8},{1,5},{5,1},{9,13},{13,9},{2,6},{6,2},{1... | collective-permute-start | bytes 196616 | tf_op jit(solution)/shard_map/ppermute | solution.py:645
  48.4 1.9 %collective-permute-start.15 = (bf16[256,1024]{1,0:T(8,128)(2,1)S(1)}, bf16[256,1024]{1,0:T(8,128)(2,1)S(1)}, u32[]{:S(2)}, u32[]{:S(2)}) collective-permute-start(bf16[256,1024]{1,0:T(8,128)(2,1)S(1)} %get-tuple-element.96), channel_id=1, source_target_pairs={{0,4},{12,8},{1,5},{13,9},{2,6},{14,10},{3,7},{15,11},{16,20},{28,... | collective-permute-start | bytes 1572872 | tf_op jit(solution)/shard_map/ppermute | solution.py:624
  50.4 0.0 collective-permute-done.9.refs_1_
  50.4 0.1 operand.6
  50.5 0.7 collective-permute-start.13
  51.2 3.8 %products.7 = (bf16[4,256,1024]{2,1,0:T(8,128)(2,1)S(1)}, bf16[256,1024]{1,0:T(8,128)(2,1)S(1)}) custom-call(f32[32,8192]{1,0:T(8,128)S(1)} %get-tuple-element.104.scales.token.refs_0_, f32[32,8192]{1,0:T(8,128)S(1)} %get-tuple-element.104.scales.token.refs_0_, bf16[768,8192]{1,0:T(8,128)(2,1)S(1)} %get-tuple-element.58.first.refs_1_, ...), custom_call_target="tpu_custom_call" | custom-call | flops 1 | bytes 1 | tf_op jit(solution)/shard_map/products/pallas_call | solution.py:247
  55.1 6.4 %collective-permute-done.10.refs_1_ = bf16[128,256]{1,0:T(8,128)(2,1)S(1)} collective-permute-done((bf16[128,256]{1,0:T(8,128)(2,1)S(1)}, bf16[128,256]{1,0:T(8,128)(2,1)S(1)}, u32[]{:S(2)}, u32[]{:S(2)}) %collective-permute-start.10) | collective-permute-done | bytes 65568 | tf_op jit(solution)/shard_map/ppermute | solution.py:645
  61.5 0.0 collective-permute-done.11.refs_1_
  61.5 0.1 operand.7
  61.6 0.7 collective-permute-start.16
  62.3 7.6 %collective-permute-start.17 = (bf16[256,1024]{1,0:T(8,128)(2,1)S(1)}, bf16[256,1024]{1,0:T(8,128)(2,1)S(1)}, u32[]{:S(2)}, u32[]{:S(2)}) collective-permute-start(bf16[256,1024]{1,0:T(8,128)(2,1)S(1)} %get-tuple-element.100), channel_id=1, source_target_pairs={{0,4},{12,8},{1,5},{13,9},{2,6},{14,10},{3,7},{15,11},{16,20},{28,... | collective-permute-start | bytes 1572872 | tf_op jit(solution)/shard_map/ppermute | solution.py:624
  69.9 0.1 collective-permute-start.12
  70.0 1.0 turn.1
  71.0 0.2 collective-permute-done.12.refs_1_
  71.2 1.7 %collective-permute-start.14 = (f32[128,256]{1,0:T(8,128)S(1)}, f32[128,256]{1,0:T(8,128)S(1)}, u32[]{:S(2)}, u32[]{:S(2)}) collective-permute-start(f32[128,256]{1,0:T(8,128)S(1)} %plus.1.refs_0_), channel_id=1, source_target_pairs={{0,2},{2,0},{1,3},{3,1},{4,6},{6,4},{5,7},{7,5},{8,10},{10,8},{9,1... | collective-permute-start | bytes 393224 | tf_op jit(solution)/shard_map/ppermute | solution.py:555
  72.9 0.0 collective-permute-done.13.refs_1_
  72.9 0.1 operand.8
  73.0 3.9 %collective-permute-done.14.refs_1_ = f32[128,256]{1,0:T(8,128)S(1)} collective-permute-done((f32[128,256]{1,0:T(8,128)S(1)}, f32[128,256]{1,0:T(8,128)S(1)}, u32[]{:S(2)}, u32[]{:S(2)}) %collective-permute-start.14) | collective-permute-done | bytes 131104 | tf_op jit(solution)/shard_map/ppermute | solution.py:555
  77.0 0.7 side.5
  77.7 0.0 collective-permute-start.18
  77.7 0.0 collective-permute-done.15.refs_1_
  77.7 0.1 operand.9
  77.8 0.0 collective-permute-done.16.refs_1_
  77.8 0.1 operand.10
  78.0 0.7 collective-permute-start.19
  78.7 5.2 %collective-permute-done.17.refs_1_ = bf16[256,1024]{1,0:T(8,128)(2,1)S(1)} collective-permute-done((bf16[256,1024]{1,0:T(8,128)(2,1)S(1)}, bf16[256,1024]{1,0:T(8,128)(2,1)S(1)}, u32[]{:S(2)}, u32[]{:S(2)}) %collective-permute-start.17) | collective-permute-done | bytes 524320 | tf_op jit(solution)/shard_map/ppermute | solution.py:624
  83.9 0.1 operand.11
  84.1 0.7 collective-permute-start.21
  84.8 5.7 %collective-permute-start.20 = (bf16[256,1024]{1,0:T(8,128)(2,1)S(1)}, bf16[256,1024]{1,0:T(8,128)(2,1)S(1)}, u32[]{:S(2)}, u32[]{:S(2)}) collective-permute-start(bf16[256,1024]{1,0:T(8,128)(2,1)S(1)} %operand.10), channel_id=1, source_target_pairs={{0,4},{8,12},{4,0},{12,8},{1,5},{9,13},{5,1},{13,9},{2,6},{10,14},... | collective-permute-start | bytes 1572872 | tf_op jit(solution)/shard_map/ppermute | solution.py:624
  90.4 4.7 %collective-permute-done.18.refs_1_ = bf16[256,1024]{1,0:T(8,128)(2,1)S(1)} collective-permute-done((bf16[256,1024]{1,0:T(8,128)(2,1)S(1)}, bf16[256,1024]{1,0:T(8,128)(2,1)S(1)}, u32[]{:S(2)}, u32[]{:S(2)}) %collective-permute-start.18) | collective-permute-done | bytes 524320 | tf_op jit(solution)/shard_map/ppermute | solution.py:624
  95.2 1.1 %keep.2.refs_3_ = f32[2048,256]{1,0:T(8,128)} custom-call(f32[32,8192]{1,0:T(8,128)S(1)} %get-tuple-element.104.scales.token.refs_0_, bf16[4,256,1024]{2,1,0:T(8,128)(2,1)S(1)} %get-tuple-element.77.refs_0_, bf16[256,1024]{1,0:T(8,128)(2,1)S(1)} %collective-permute-done.18.refs_1_, bf16[256,1024]{1,0:T(8,128)(2,1)S(1)} %collective-permute-done.19.refs_2_), custom_call_target="tpu_custom_call" | custom-call | flops 1 | bytes 1 | tf_op jit(solution)/shard_map/keep/pallas_call | solution.py:247
  96.3 0.0 collective-permute-done.21.refs_2_
  96.3 9.3 %collective-permute-done.20.refs_1_ = bf16[256,1024]{1,0:T(8,128)(2,1)S(1)} collective-permute-done((bf16[256,1024]{1,0:T(8,128)(2,1)S(1)}, bf16[256,1024]{1,0:T(8,128)(2,1)S(1)}, u32[]{:S(2)}, u32[]{:S(2)}) %collective-permute-start.20) | collective-permute-done | bytes 524320 | tf_op jit(solution)/shard_map/ppermute | solution.py:624
  105.6 1.1 %keep.3 = f32[2048,256]{1,0:T(8,128)} custom-call(f32[32,8192]{1,0:T(8,128)S(1)} %get-tuple-element.104.scales.token.refs_0_, bf16[4,256,1024]{2,1,0:T(8,128)(2,1)S(1)} %get-tuple-element.84.refs_0_, bf16[256,1024]{1,0:T(8,128)(2,1)S(1)} %collective-permute-done.20.refs_1_, ...), custom_call_target="tpu_custom_call", output_to_operand_aliasing={{}: (4, {})} | custom-call | flops 1 | bytes 1 | tf_op jit(solution)/shard_map/keep/pallas_call | solution.py:247
  (11 shorter events, 0.3 us)
Async XLA Ops:
  7.7 9.3 %collective-permute-start = (f32[256,256]{1,0:T(8,128)S(1)}, f32[256,256]{1,0:T(8,128)S(1)}, u32[]{:S(2)}, u32[]{:S(2)}) collective-permute-start(f32[256,256]{1,0:T(8,128)S(1)} %get-tuple-element.57), channel_id=1, source_target_pairs={{0,2},{2,0},{1,3},{3,1},{4,6},{6,4},{5,7},{7,5},{8,10},{10,8},{9,1... | collective-permute-start | bytes 786440 | tf_op jit(solution)/shard_map/ppermute | solution.py:555
  15.7 1.6 %collective-permute-start.2 = (f32[256,256]{1,0:T(8,128)S(1)}, f32[256,256]{1,0:T(8,128)S(1)}, u32[]{:S(2)}, u32[]{:S(2)}) collective-permute-start(f32[256,256]{1,0:T(8,128)S(1)} %get-tuple-element.65), channel_id=1, source_target_pairs={{0,1},{1,0},{2,3},{3,2},{4,5},{5,4},{6,7},{7,6},{8,9},{9,8},{10,11... | collective-permute-start | bytes 786440 | tf_op jit(solution)/shard_map/ppermute | solution.py:555
  15.8 1.9 %collective-permute-start.3 = (f32[256,256]{1,0:T(8,128)S(1)}, f32[256,256]{1,0:T(8,128)S(1)}, u32[]{:S(2)}, u32[]{:S(2)}) collective-permute-start(f32[256,256]{1,0:T(8,128)S(1)} %get-tuple-element.66), channel_id=1, source_target_pairs={{0,1},{1,0},{2,3},{3,2},{4,5},{5,4},{6,7},{7,6},{8,9},{9,8},{10,11... | collective-permute-start | bytes 786440 | tf_op jit(solution)/shard_map/ppermute | solution.py:555
  17.0 4.7 %collective-permute-start.1 = (f32[256,256]{1,0:T(8,128)S(1)}, f32[256,256]{1,0:T(8,128)S(1)}, u32[]{:S(2)}, u32[]{:S(2)}) collective-permute-start(f32[256,256]{1,0:T(8,128)S(1)} %add.3.gram_a), channel_id=1, source_target_pairs={{0,1},{1,0},{2,3},{3,2},{4,5},{5,4},{6,7},{7,6},{8,9},{9,8},{10,11... | collective-permute-start | bytes 786440 | tf_op jit(solution)/shard_map/ppermute | solution.py:555
  17.7 8.4 %collective-permute-start.4 = (f32[256,256]{1,0:T(8,128)S(1)}, f32[256,256]{1,0:T(8,128)S(1)}, u32[]{:S(2)}, u32[]{:S(2)}) collective-permute-start(f32[256,256]{1,0:T(8,128)S(1)} %add_piece.3), channel_id=1, source_target_pairs={{0,2},{2,0},{1,3},{3,1},{4,6},{6,4},{5,7},{7,5},{8,10},{10,8},{9,1... | collective-permute-start | bytes 786440 | tf_op jit(solution)/shard_map/ppermute | solution.py:555
  21.7 4.5 %copy-start = (bf16[1024,256]{1,0:T(8,128)(2,1)S(1)}, bf16[1024,256]{1,0:T(8,128)(2,1)}, u32[]{:S(2)}) copy-start(bf16[1024,256]{1,0:T(8,128)(2,1)} %refs_4_.1) | copy-start | bytes 1572868
  27.2 5.0 %collective-permute-start.5 = (bf16[256,256]{1,0:T(8,128)(2,1)S(1)}, bf16[256,256]{1,0:T(8,128)(2,1)S(1)}, u32[]{:S(2)}, u32[]{:S(2)}) collective-permute-start(bf16[256,256]{1,0:T(8,128)(2,1)S(1)} %admm.1.refs_0_), channel_id=1, source_target_pairs={{0,2},{2,0},{1,3},{3,1},{4,6},{6,4},{5,7},{7,5},{8,10},{10,8},{9,1... | collective-permute-start | bytes 393224 | tf_op jit(solution)/shard_map/ppermute | solution.py:555
  32.2 2.0 %collective-permute-start.6 = (bf16[256,512]{1,0:T(8,128)(2,1)S(1)}, bf16[256,512]{1,0:T(8,128)(2,1)S(1)}, u32[]{:S(2)}, u32[]{:S(2)}) collective-permute-start(bf16[256,512]{1,0:T(8,128)(2,1)S(1)} %side.3.refs_0_), channel_id=1, source_target_pairs={{0,1},{1,0},{2,3},{3,2},{4,5},{5,4},{6,7},{7,6},{8,9},{9,8},{10,11... | collective-permute-start | bytes 786440 | tf_op jit(solution)/shard_map/ppermute | solution.py:555
  32.5 4.6 %collective-permute-start.7 = (bf16[128,256]{1,0:T(8,128)(2,1)S(1)}, bf16[128,256]{1,0:T(8,128)(2,1)S(1)}, u32[]{:S(2)}, u32[]{:S(2)}) collective-permute-start(bf16[128,256]{1,0:T(8,128)(2,1)S(1)} %row_share.1.refs_0_), channel_id=1, source_target_pairs={{0,4},{4,0},{8,12},{12,8},{1,5},{5,1},{9,13},{13,9},{2,6},{6,2},{1... | collective-permute-start | bytes 196616 | tf_op jit(solution)/shard_map/ppermute | solution.py:645
  35.2 15.2 %collective-permute-start.9 = (bf16[256,1024]{1,0:T(8,128)(2,1)S(1)}, bf16[256,1024]{1,0:T(8,128)(2,1)S(1)}, u32[]{:S(2)}, u32[]{:S(2)}) collective-permute-start(bf16[256,1024]{1,0:T(8,128)(2,1)S(1)} %products.4), channel_id=1, source_target_pairs={{0,4},{4,0},{8,12},{12,8},{1,5},{5,1},{9,13},{13,9},{2,6},{6,2},{1... | collective-permute-start | bytes 1572872 | tf_op jit(solution)/shard_map/ppermute | solution.py:624
  38.1 23.4 %collective-permute-start.11 = (bf16[256,1024]{1,0:T(8,128)(2,1)S(1)}, bf16[256,1024]{1,0:T(8,128)(2,1)S(1)}, u32[]{:S(2)}, u32[]{:S(2)}) collective-permute-start(bf16[256,1024]{1,0:T(8,128)(2,1)S(1)} %products.5), channel_id=1, source_target_pairs={{0,4},{12,8},{1,5},{13,9},{2,6},{14,10},{3,7},{15,11},{16,20},{28,... | collective-permute-start | bytes 1572872 | tf_op jit(solution)/shard_map/ppermute | solution.py:624
  41.6 4.5 %collective-permute-start.8 = (bf16[128,256]{1,0:T(8,128)(2,1)S(1)}, bf16[128,256]{1,0:T(8,128)(2,1)S(1)}, u32[]{:S(2)}, u32[]{:S(2)}) collective-permute-start(bf16[128,256]{1,0:T(8,128)(2,1)S(1)} %hop.3.refs_0_), channel_id=1, source_target_pairs={{4,8},{8,4},{5,9},{9,5},{6,10},{10,6},{7,11},{11,7},{20,24},{24,20... | collective-permute-start | bytes 196616 | tf_op jit(solution)/shard_map/ppermute | solution.py:645
  46.2 15.3 %collective-permute-start.10 = (bf16[128,256]{1,0:T(8,128)(2,1)S(1)}, bf16[128,256]{1,0:T(8,128)(2,1)S(1)}, u32[]{:S(2)}, u32[]{:S(2)}) collective-permute-start(bf16[128,256]{1,0:T(8,128)(2,1)S(1)} %hop.4.refs_0_), channel_id=1, source_target_pairs={{0,4},{4,0},{8,12},{12,8},{1,5},{5,1},{9,13},{13,9},{2,6},{6,2},{1... | collective-permute-start | bytes 196616 | tf_op jit(solution)/shard_map/ppermute | solution.py:645
  48.4 29.2 %collective-permute-start.15 = (bf16[256,1024]{1,0:T(8,128)(2,1)S(1)}, bf16[256,1024]{1,0:T(8,128)(2,1)S(1)}, u32[]{:S(2)}, u32[]{:S(2)}) collective-permute-start(bf16[256,1024]{1,0:T(8,128)(2,1)S(1)} %get-tuple-element.96), channel_id=1, source_target_pairs={{0,4},{12,8},{1,5},{13,9},{2,6},{14,10},{3,7},{15,11},{16,20},{28,... | collective-permute-start | bytes 1572872 | tf_op jit(solution)/shard_map/ppermute | solution.py:624
  50.5 22.3 %collective-permute-start.13 = (bf16[256,1024]{1,0:T(8,128)(2,1)S(1)}, bf16[256,1024]{1,0:T(8,128)(2,1)S(1)}, u32[]{:S(2)}, u32[]{:S(2)}) collective-permute-start(bf16[256,1024]{1,0:T(8,128)(2,1)S(1)} %operand.6), channel_id=1, source_target_pairs={{4,8},{8,4},{5,9},{9,5},{6,10},{10,6},{7,11},{11,7},{20,24},{24,20... | collective-permute-start | bytes 1572872 | tf_op jit(solution)/shard_map/ppermute | solution.py:624
  61.6 16.2 %collective-permute-start.16 = (bf16[256,1024]{1,0:T(8,128)(2,1)S(1)}, bf16[256,1024]{1,0:T(8,128)(2,1)S(1)}, u32[]{:S(2)}, u32[]{:S(2)}) collective-permute-start(bf16[256,1024]{1,0:T(8,128)(2,1)S(1)} %operand.7), channel_id=1, source_target_pairs={{4,8},{8,4},{5,9},{9,5},{6,10},{10,6},{7,11},{11,7},{20,24},{24,20... | collective-permute-start | bytes 1572872 | tf_op jit(solution)/shard_map/ppermute | solution.py:624
  62.3 21.6 %collective-permute-start.17 = (bf16[256,1024]{1,0:T(8,128)(2,1)S(1)}, bf16[256,1024]{1,0:T(8,128)(2,1)S(1)}, u32[]{:S(2)}, u32[]{:S(2)}) collective-permute-start(bf16[256,1024]{1,0:T(8,128)(2,1)S(1)} %get-tuple-element.100), channel_id=1, source_target_pairs={{0,4},{12,8},{1,5},{13,9},{2,6},{14,10},{3,7},{15,11},{16,20},{28,... | collective-permute-start | bytes 1572872 | tf_op jit(solution)/shard_map/ppermute | solution.py:624
  69.9 1.3 %collective-permute-start.12 = (bf16[128,256]{1,0:T(8,128)(2,1)S(1)}, bf16[128,256]{1,0:T(8,128)(2,1)S(1)}, u32[]{:S(2)}, u32[]{:S(2)}) collective-permute-start(bf16[128,256]{1,0:T(8,128)(2,1)S(1)} %hop.5.refs_0_), channel_id=1, source_target_pairs={{0,1},{1,0},{2,3},{3,2},{4,5},{5,4},{6,7},{7,6},{8,9},{9,8},{10,11... | collective-permute-start | bytes 196616 | tf_op jit(solution)/shard_map/ppermute | solution.py:555
  71.2 5.7 %collective-permute-start.14 = (f32[128,256]{1,0:T(8,128)S(1)}, f32[128,256]{1,0:T(8,128)S(1)}, u32[]{:S(2)}, u32[]{:S(2)}) collective-permute-start(f32[128,256]{1,0:T(8,128)S(1)} %plus.1.refs_0_), channel_id=1, source_target_pairs={{0,2},{2,0},{1,3},{3,1},{4,6},{6,4},{5,7},{7,5},{8,10},{10,8},{9,1... | collective-permute-start | bytes 393224 | tf_op jit(solution)/shard_map/ppermute | solution.py:555
  77.7 17.5 %collective-permute-start.18 = (bf16[256,1024]{1,0:T(8,128)(2,1)S(1)}, bf16[256,1024]{1,0:T(8,128)(2,1)S(1)}, u32[]{:S(2)}, u32[]{:S(2)}) collective-permute-start(bf16[256,1024]{1,0:T(8,128)(2,1)S(1)} %operand.8), channel_id=1, source_target_pairs={{0,4},{8,12},{4,0},{12,8},{1,5},{9,13},{5,1},{13,9},{2,6},{10,14},... | collective-permute-start | bytes 1572872 | tf_op jit(solution)/shard_map/ppermute | solution.py:624
  78.0 17.2 %collective-permute-start.19 = (bf16[256,1024]{1,0:T(8,128)(2,1)S(1)}, bf16[256,1024]{1,0:T(8,128)(2,1)S(1)}, u32[]{:S(2)}, u32[]{:S(2)}) collective-permute-start(bf16[256,1024]{1,0:T(8,128)(2,1)S(1)} %operand.9), channel_id=1, source_target_pairs={{4,8},{8,4},{5,9},{9,5},{6,10},{10,6},{7,11},{11,7},{20,24},{24,20... | collective-permute-start | bytes 1572872 | tf_op jit(solution)/shard_map/ppermute | solution.py:624
  84.1 12.3 %collective-permute-start.21 = (bf16[256,1024]{1,0:T(8,128)(2,1)S(1)}, bf16[256,1024]{1,0:T(8,128)(2,1)S(1)}, u32[]{:S(2)}, u32[]{:S(2)}) collective-permute-start(bf16[256,1024]{1,0:T(8,128)(2,1)S(1)} %operand.11), channel_id=1, source_target_pairs={{4,8},{8,4},{5,9},{9,5},{6,10},{10,6},{7,11},{11,7},{20,24},{24,20... | collective-permute-start | bytes 1572872 | tf_op jit(solution)/shard_map/ppermute | solution.py:624
  84.8 20.8 %collective-permute-start.20 = (bf16[256,1024]{1,0:T(8,128)(2,1)S(1)}, bf16[256,1024]{1,0:T(8,128)(2,1)S(1)}, u32[]{:S(2)}, u32[]{:S(2)}) collective-permute-start(bf16[256,1024]{1,0:T(8,128)(2,1)S(1)} %operand.10), channel_id=1, source_target_pairs={{0,4},{8,12},{4,0},{12,8},{1,5},{9,13},{5,1},{13,9},{2,6},{10,14},... | collective-permute-start | bytes 1572872 | tf_op jit(solution)/shard_map/ppermute | solution.py:624

commit v13 on v12

--- a/solution.py
+++ b/solution.py
@@ -49,33 +49,37 @@
     ]
 
 
-def pieces_of(rows, bit):
+def pieces_of(rows, bit, kept):
     core = lax.axis_index("sub")
-    upper = (lax.axis_index("gene") & bit) != 0
+    upper = ((lax.axis_index("gene") & bit) != 0) == kept
     half, quarter = rows // 2, rows // 4
-    mine = core * half
-    kept = jnp.where(upper, quarter, 0)
+    place = jnp.where(upper, quarter, 0)
     return [
-        pl.multiple_of((1 - core) * half, quarter),
-        pl.multiple_of(mine + quarter - kept, quarter),
-        pl.multiple_of(mine + kept, quarter),
+        pl.multiple_of((1 - core) * half + place, quarter),
+        pl.multiple_of(core * half + place, quarter),
     ]
+
+
+def piece_copies(bit, kept, counts, target, sems):
+    quarter = counts.shape[0] // 4
+    copies = []
+    for i, place in enumerate(pieces_of(counts.shape[0], bit, kept)):
+        copies += row_copies(
+            counts, target.at[i * quarter : (i + 1) * quarter], place, sems.at[i * 4 : i * 4 + 4]
+        )
+    return copies
 
 
 def load_kernel(
     bit, genes, counts, tile_mask, tile_counts, gram, scales, turned, first,
-    genes_here, mask_here, counts_here, gene_sems, row_sems, sent_sems, small_sems,
+    genes_here, mask_here, counts_here, gene_sems, row_sems, small_sems,
 ):
     small_copies = [
         pltpu.make_async_copy(tile_mask, mask_here, small_sems.at[0]),
         pltpu.make_async_copy(tile_counts, counts_here, small_sems.at[1]),
     ]
     gene_copies = row_copies(genes, genes_here, 0, gene_sems)
-    rows = counts.shape[0]
-    half = rows // 2
-    theirs, sent, _ = pieces_of(rows, bit)
-    row_starts = row_copies(counts, first.at[:half], theirs, row_sems)
-    row_starts += row_copies(counts, first.at[half:], sent, sent_sems)
+    row_starts = piece_copies(bit, False, counts, first, row_sems)
     for copy in gene_copies + small_copies:
         copy.start()
     for copy in small_copies:
@@ -117,7 +121,7 @@
             jax.ShapeDtypeStruct((width, width), F32),
             jax.ShapeDtypeStruct((tile_mask.shape[0] * 8, columns), F32),
             pltpu.VMEM((columns, width), BF16),
-            pltpu.VMEM((rows // 4 * 3, columns), BF16),
+            pltpu.VMEM((rows // 2, columns), BF16),
         ),
         in_specs=[there] * 4,
         out_specs=(here,) * 4,
@@ -127,7 +131,6 @@
             pltpu.VMEM(tile_mask.shape, jnp.int32),
             pltpu.SemaphoreType.DMA((4,)),
             pltpu.SemaphoreType.DMA((8,)),
-            pltpu.SemaphoreType.DMA((4,)),
             pltpu.SemaphoreType.DMA((2,)),
         ],
         compiler_params=params(),
@@ -163,77 +166,59 @@
         )
 
 
-def tiles_from(start, rows, tile):
-    return [start // tile + i for i in range(rows // tile)]
-
-
-def cross_first_kernel(bit, scales, first, turned, counts, low, high, sent, kept, total, sems):
-    rows = counts.shape[0]
-    half, quarter, tile = rows // 2, rows // 4, rows // (scales.shape[0] // 8)
-    theirs_at, sent_at, kept_at = pieces_of(rows, bit)
-    copies = row_copies(counts, kept, kept_at, sems)
-    for copy in copies:
-        copy.start()
-    row_tiles = tiles_from(theirs_at, half, tile) + tiles_from(sent_at, quarter, tile)
-    cross_rows(row_tiles, scales, first, turned, total)
-    low[...] = total[:quarter].T
-    high[...] = total[quarter:half].T
-    sent[...] = total[half:].T
-    for copy in copies:
-        copy.wait()
-
-
-def cross_first(bit, scales, first, turned, counts):
+def tiles_of(bit, kept, rows, tile):
+    quarter = rows // 4
+    return [
+        place // tile + i
+        for place in pieces_of(rows, bit, kept)
+        for i in range(quarter // tile)
+    ]
+
+
+def cross_kernel(bit, kept, rows, scales, held_rows, turned, *refs):
+    (low, high, mine), total = refs[-5:-2] if kept else refs[1:4], refs[-2]
+    if not kept:
+        copies = piece_copies(bit, True, refs[0], refs[4], refs[-1])
+        for copy in copies:
+            copy.start()
+    quarter, tile = rows // 4, rows // (scales.shape[0] // 8)
+    cross_rows(tiles_of(bit, kept, rows, tile), scales, held_rows, turned, total)
+    low[...] = total[: quarter // 2].T
+    high[...] = total[quarter // 2 : quarter].T
+    mine[...] = total[quarter:].T
+    if not kept:
+        for copy in copies:
+            copy.wait()
+
+
+def cross(bit, kept, scales, held_rows, turned, counts):
     rows, columns = counts.shape
     width = turned.shape[1]
     here = pl.BlockSpec(memory_space=pltpu.VMEM)
     piece = jax.ShapeDtypeStruct((width, rows // 4), F32)
+    small_piece = jax.ShapeDtypeStruct((width, rows // 8), F32)
+    out_shape = (small_piece, small_piece, piece)
+    in_specs, args = [here] * 3, [scales, held(held_rows), held(turned)]
+    if not kept:
+        out_shape += (pltpu.VMEM((rows // 2, columns), BF16),)
+        in_specs.append(pl.BlockSpec(memory_space=pltpu.HBM))
+        args.append(away(counts))
     return pl.pallas_call(
-        functools.partial(cross_first_kernel, bit),
-        out_shape=(piece, piece, piece, pltpu.VMEM((rows // 4, columns), BF16)),
-        in_specs=[here, here, here, pl.BlockSpec(memory_space=pltpu.HBM)],
-        out_specs=(here,) * 4,
-        scratch_shapes=[pltpu.VMEM(first.shape[:1] + (width,), F32), pltpu.SemaphoreType.DMA((4,))],
+        functools.partial(cross_kernel, bit, kept, rows),
+        out_shape=out_shape,
+        in_specs=in_specs,
+        out_specs=(here,) * len(out_shape),
+        scratch_shapes=[pltpu.VMEM((rows // 2, width), F32), pltpu.SemaphoreType.DMA((8,))],
         compiler_params=params(),
         cost_estimate=cost(1, 1),
-        name="cross_first",
-    )(scales, held(first), held(turned), away(counts))
-
-
-def cross_kept_kernel(bit, scales, kept, turned, cross, total):
-    rows = kept.shape[0] * 4
-    tile = rows // (scales.shape[0] // 8)
-    row_tiles = tiles_from(pieces_of(rows, bit)[2], rows // 4, tile)
-    cross_rows(row_tiles, scales, kept, turned, total)
-    cross[...] = total[...].T
-
-
-def cross_kept(bit, token, scales, kept, turned):
-    rows, width = kept.shape[0], turned.shape[1]
-    return call(
-        functools.partial(cross_kept_kernel, bit),
-        "cross_kept", jax.ShapeDtypeStruct((width, rows), F32), token,
-        scales, held(kept), held(turned), scratch=[pltpu.VMEM((rows, width), F32)],
-    )
-
-
-def add_piece_kernel(bit, kept, left, low, high, out):
-    upper = ((lax.axis_index("gene") & bit) != 0) == kept
-
-    @pl.when(upper)
-    def _():
-        out[...] = left[...] + high[...]
-
-    @pl.when(jnp.logical_not(upper))
-    def _():
-        out[...] = left[...] + low[...]
-
-
-def add_piece(bit, kept, token, left, low, high):
-    shape = jax.ShapeDtypeStruct(left.shape, F32)
-    return call(
-        functools.partial(add_piece_kernel, bit, kept), "add_piece", shape, token, left, low, high
-    )
+        name="cross_kept" if kept else "cross_sent",
+    )(*args)
+
+
+def plus_pieces_kernel(left, low, high, out):
+    half = low.shape[1]
+    out[:, :half] = left[:, :half] + low[...]
+    out[:, half:] = left[:, half:] + high[...]
 
 
 def call(kernel, name, out_shape, token, *args, scratch=(), aliases=None, out=None):
@@ -367,7 +352,7 @@
         in_specs=[whole, whole],
         out_specs=(whole, whole),
         compiler_params=params(),
-        cost_estimate=cost(2 * 60 * width**3, 12 * width**2),
+        cost_estimate=cost(1, 1),
         name="inverse",
     )(gram_a, gram_b)
 
@@ -387,32 +372,27 @@
     columns_out[...] = zvalue.astype(BF16)
 
 
-def products_kernel(tile, bit, line, start, chunk, scales, first, kept, columns, *outs):
+def products_kernel(tile, bit, line, start, chunk, scales, sent, kept, columns, *outs):
     only_first = len(outs) == 1
     block = line.block(1 if only_first else 2, 0)
-    size = first.shape[1] // line.size
+    size = kept.shape[1] // line.size
     span = min(tile, chunk)
     wide = 2 * span if chunk % (2 * span) == 0 else span
     steps = chunk // wide
     rows = columns.shape[1]
-    half = rows // 2
-    theirs_at, sent_at, kept_at = pieces_of(rows, bit)
-    groups = [
-        (first.at[:half], theirs_at),
-        (first.at[half:], sent_at),
-        (kept, kept_at),
-    ]
+    quarter = rows // 4
+    groups = [(sent, False), (kept, True)]
 
     @pl.loop(0, steps if only_first else line.size * steps)
     def _(turn):
         order, step = (block, turn) if only_first else (turn // steps, lax.rem(turn, steps))
         genes = pl.ds(pl.multiple_of(order * size + start + step * wide, span), wide)
         total = None
-        for counts, place in groups:
-            cells = counts.shape[0]
+        for counts, stays in groups:
+            cells = [columns[:, pl.ds(at, quarter)] for at in pieces_of(rows, bit, stays)]
             part = jnp.dot(
-                columns[:, pl.ds(place, cells)],
-                scaled(counts, genes, tiles_from(place, cells, tile), scales),
+                jnp.concatenate(cells, axis=1),
+                scaled(counts, genes, tiles_of(bit, stays, rows, tile), scales),
                 preferred_element_type=F32,
             )
             total = part if total is None else total + part
@@ -428,7 +408,7 @@
                 outs[1][:, at] = total
 
 
-def products(only_first, bit, line, start, chunk, token, scales, first, kept, columns):
+def products(only_first, bit, line, start, chunk, token, scales, sent, kept, columns):
     width, rows = columns.shape
     tile = rows // (scales.shape[0] // 8)
     out_shape = (jax.ShapeDtypeStruct((width, chunk), BF16),)
@@ -436,7 +416,7 @@
         out_shape = (jax.ShapeDtypeStruct((line.size, width, chunk), BF16),) + out_shape
     return call(
         functools.partial(products_kernel, tile, bit, line, start, chunk),
-        "products", out_shape, token, scales, held(first), held(kept), columns,
+        "products", out_shape, token, scales, held(sent), held(kept), columns,
     )
 
 
@@ -579,25 +559,25 @@
     line = Line(cells)
 
     half_bit = bit = genes // 2
-    gram, scales, turned, first_rows = load(bit, gene_factor, counts, tile_mask, tile_counts)
+    gram, scales, turned, sent_rows = load(bit, gene_factor, counts, tile_mask, tile_counts)
     token = scales
-    theirs_low, theirs_high, own_sent, kept = cross_first(
-        bit, scales, first_rows, turned, counts
-    )
-    arrived_low = swap(theirs_low, "sub", subs, 1)
-    arrived_high = swap(theirs_high, "sub", subs, 1)
-    sent = add_piece(bit, False, token, own_sent, arrived_low, arrived_high)
+    piece = jax.ShapeDtypeStruct((width, rows // 4), F32)
+    low, high, mine, kept_rows = cross(bit, False, scales, sent_rows, turned, counts)
+    low, high = [swap(value, "sub", subs, 1) for value in (low, high)]
+    sent = call(plus_pieces_kernel, "plus", piece, token, mine, low, high)
     cross_b = swap(sent, "gene", genes, bit)
-    gram, (scales_late, _) = pair_sums(gram, "gene", genes, (scales, own_sent))
-    cross_a = cross_kept(bit, token, scales_late, kept, turned)
-    cross_a = add_piece(bit, True, token, cross_a, arrived_low, arrived_high)
+    gram, (scales_late, _) = pair_sums(gram, "gene", genes, (scales, sent))
+    low, high, mine = cross(bit, True, scales_late, kept_rows, turned, counts)
+    low, high = [swap(value, "sub", subs, 1) for value in (low, high)]
+    gram_other = swap(gram, "sub", subs, 1)
+    inverse, rho = shifted_inverse(gram, gram_other)
+    token_late, inverse = after(token, inverse)
+    cross_a = call(plus_pieces_kernel, "plus", piece, token_late, mine, low, high)
     bit //= 2
     while bit:
         cross_a, sent = fold("gene", bit, token, cross_a, cross_b)
         cross_b = swap(sent, "gene", genes, bit)
         bit //= 2
-    gram_other = swap(gram, "sub", subs, 1)
-    inverse, rho = shifted_inverse(gram, gram_other)
     share = jax.ShapeDtypeStruct((width, rows // (genes * subs)), BF16)
     columns_held = call(
         functools.partial(admm_kernel, genes),
@@ -652,7 +632,7 @@
 
     for index in every:
         (first,) = products(
-            True, half_bit, line, starts[index], chunks[index], token, scales, first_rows, kept, whole
+            True, half_bit, line, starts[index], chunks[index], token, scales, sent_rows, kept_rows, whole
         )
         token, first = after(token, first)
         for parity in (0, 1):
@@ -662,7 +642,7 @@
     totals, seconds = [], []
     for index in every:
         total, second = products(
-            False, half_bit, line, starts[index], chunks[index], token, scales, first_rows, kept, whole
+            False, half_bit, line, starts[index], chunks[index], token, scales, sent_rows, kept_rows, whole
         )
         token, second = after(token, second)
         if hops:

time: 107 us -> 107 us (level)
  waiting for transfers between devices: 36 us -> 38 us
    pallas_call x1 -> x2, Pallas kernels: 5 us -> 7.74 us  [cross(): pl.pallas_call(functools.partial(cross_kernel, bit, kept, rows), out_shap...]
    pallas_call x25 -> x24, Pallas kernels: 18.5 us -> 16.1 us  [call(): pl.pallas_call(lambda token, *refs: kernel(*refs), out_shape=out_shape, i...]
    ppermute x9 -> x11, waiting for transfers between devices: 9.79 us -> 12 us  [swap(): return lax.ppermute(value, axis, [(i, i ^ step) for i in range(size)])]
    pallas_call x1, Pallas kernels: 7.04 us -> 5.81 us  [load(): pl.pallas_call(functools.partial(load_kernel, bit), out_shape=(jax.ShapeD...]
    ppermute x9 -> x11, starting transfers between devices: 8.32 us -> 7.43 us  [swap(): return lax.ppermute(value, axis, [(i, i ^ step) for i in range(size)])]
  transfers between devices with their start and end apart: 22 -> 24, of which waited for: 12 -> 11; matrix products, arithmetic and copies ran while one was open for 0% -> 0% of each run, Pallas kernels for 23% -> 24%
where the time goes in v13:
time: 107 us
  waiting for transfers between devices  38 us (36%)
  starting transfers between devices  34.7 us (32%)
  Pallas kernels  33.1 us (31%)
    ppermute x10, starting transfers between devices, send(): lax.ppermute(value, 'cell', pairs)  22.8 us
    ppermute x10, waiting for transfers between devices, send(): lax.ppermute(value, 'cell', pairs)  19.2 us
    pallas_call x24, Pallas kernels, call(): pl.pallas_call(lambda token, *refs: kernel(*refs), out_shape=out_shape, i...  16.1 us
    ppermute x11, waiting for transfers between devices, swap(): return lax.ppermute(value, axis, [(i, i ^ step) for i in range(size)])  12 us
    pallas_call x2, Pallas kernels, cross(): pl.pallas_call(functools.partial(cross_kernel, bit, kept, rows), out_shap...  7.74 us
    ppermute x11, starting transfers between devices, swap(): return lax.ppermute(value, axis, [(i, i ^ step) for i in range(size)])  7.43 us
    ppermute x3, waiting for transfers between devices, hop_rows(): rows_arrived = lax.ppermute(rows_sum, 'cell', both)  6.76 us
    pallas_call x1, Pallas kernels, load(): pl.pallas_call(functools.partial(load_kernel, bit), out_shape=(jax.ShapeD...  5.81 us
  transfers between devices with their start and end apart: 24, of which 11 were waited for; matrix products, arithmetic and copies ran while one was open for 0% of the time, Pallas kernels for 24%

profile of v13, /device:TPU:0, one launch (start us, length us, event | category | flops | bytes accessed | tf_op | source)
XLA Modules:
  0.0 106.9 jit_solution(2945101334518425271)
XLA Ops:
  0.6 5.8 %load.1 = (f32[256,256]{1,0:T(8,128)S(1)}, f32[32,8192]{1,0:T(8,128)S(1)}, bf16[8192,256]{1,0:T(8,128)(2,1)S(1)}, bf16[512,8192]{1,0:T(8,128)(2,1)S(1)}) custom-call(bf16[256,8192]{1,0:T(8,128)(2,1)} %genes.1, bf16[1024,8192]{1,0:T(8,128)(2,1)} %refs_0_.1, s32[4,32]{1,0:T(4,128)} %tile_mask.1, s32[4,32]{1,0:T(4,128)} %tile_counts.1), custom_call_target="tpu_custom_call" | custom-call | flops 1 | bytes 1 | tf_op jit(solution)/shard_map/load/pallas_call | solution.py:118
  6.4 3.0 %collective-permute-start = (f32[256,256]{1,0:T(8,128)S(1)}, f32[256,256]{1,0:T(8,128)S(1)}, u32[]{:S(2)}, u32[]{:S(2)}) collective-permute-start(f32[256,256]{1,0:T(8,128)S(1)} %get-tuple-element.62), channel_id=1, source_target_pairs={{0,2},{2,0},{1,3},{3,1},{4,6},{6,4},{5,7},{7,5},{8,10},{10,8},{9,1... | collective-permute-start | bytes 786440 | tf_op jit(solution)/shard_map/ppermute | solution.py:535
  9.4 3.9 %cross_sent.1 = (f32[256,128]{1,0:T(8,128)S(1)}, f32[256,128]{1,0:T(8,128)S(1)}, f32[256,256]{1,0:T(8,128)S(1)}, bf16[512,8192]{1,0:T(8,128)(2,1)S(1)}) custom-call(f32[32,8192]{1,0:T(8,128)S(1)} %get-tuple-element.114.scales.token.refs_0_, bf16[512,8192]{1,0:T(8,128)(2,1)S(1)} %get-tuple-element.63.held_rows.refs_1_, ...), custom_call_target="tpu_custom_call" | custom-call | flops 1 | bytes 1 | tf_op jit(solution)/shard_map/cross_sent/pallas_call | solution.py:206
  13.3 0.1 collective-permute-start.1
  13.4 0.5 collective-permute-start.2
  13.9 0.8 collective-permute-done.1.refs_1_
  14.7 0.2 collective-permute-done.2.refs_2_
  15.0 0.8 collective-permute-done
  15.8 0.1 collective-permute-start.3
  15.9 1.8 %collective-permute-start.6 = (f32[256,256]{1,0:T(8,128)S(1)}, f32[256,256]{1,0:T(8,128)S(1)}, u32[]{:S(2)}, u32[]{:S(2)}) collective-permute-start(f32[256,256]{1,0:T(8,128)S(1)} %plus.3), channel_id=1, source_target_pairs={{0,2},{2,0},{1,3},{3,1},{4,6},{6,4},{5,7},{7,5},{8,10},{10,8},{9,1... | collective-permute-start | bytes 786440 | tf_op jit(solution)/shard_map/ppermute | solution.py:535
  17.7 3.9 %cross_kept.1 = (f32[256,128]{1,0:T(8,128)S(1)}, f32[256,128]{1,0:T(8,128)S(1)}, f32[256,256]{1,0:T(8,128)S(1)}) custom-call(f32[32,8192]{1,0:T(8,128)S(1)} %get-tuple-element.114.scales.token.refs_0_, bf16[512,8192]{1,0:T(8,128)(2,1)S(1)} %get-tuple-element.73.held_rows.refs_2_, bf16[8192,256]{1,0:T(8,128)(2,1)S(1)} %get-tuple-element.64.turned), custom_call_target="tpu_custom_call" | custom-call | flops 1 | bytes 1 | tf_op jit(solution)/shard_map/cross_kept/pallas_call | solution.py:206
  21.5 0.2 collective-permute-start.4
  21.8 0.3 collective-permute-start.5
  22.1 0.0 collective-permute-done.3.gram_b
  22.1 3.5 %inverse.1 = (f32[256,256]{1,0:T(8,128)S(1)}, f32[8,128]{1,0:T(8,128)S(1)}) custom-call(f32[256,256]{1,0:T(8,128)S(1)} %add.3.gram_a, f32[256,256]{1,0:T(8,128)S(1)} %collective-permute-done.3.gram_b), custom_call_target="tpu_custom_call" | custom-call | flops 1 | bytes 1 | tf_op jit(solution)/shard_map/inverse/pallas_call | solution.py:346
  25.7 0.0 collective-permute-done.4.refs_1_
  25.7 0.0 collective-permute-done.5.refs_2_
  25.7 1.0 admm.1.refs_0_
  26.8 0.7 collective-permute-start.7
  27.4 5.0 %collective-permute-done.7.refs_1_ = bf16[256,256]{1,0:T(8,128)(2,1)S(1)} collective-permute-done((bf16[256,256]{1,0:T(8,128)(2,1)S(1)}, bf16[256,256]{1,0:T(8,128)(2,1)S(1)}, u32[]{:S(2)}, u32[]{:S(2)}) %collective-permute-start.7) | collective-permute-done | bytes 131104 | tf_op jit(solution)/shard_map/ppermute | solution.py:535
  32.4 0.1 collective-permute-start.8
  32.5 0.2 row_share.1.refs_0_
  32.7 1.6 %collective-permute-start.9 = (bf16[128,256]{1,0:T(8,128)(2,1)S(1)}, bf16[128,256]{1,0:T(8,128)(2,1)S(1)}, u32[]{:S(2)}, u32[]{:S(2)}) collective-permute-start(bf16[128,256]{1,0:T(8,128)(2,1)S(1)} %row_share.1.refs_0_), channel_id=1, source_target_pairs={{0,4},{4,0},{8,12},{12,8},{1,5},{5,1},{9,13},{13,9},{2,6},{6,2},{1... | collective-permute-start | bytes 196616 | tf_op jit(solution)/shard_map/ppermute | solution.py:625
  34.4 1.0 products.4
  35.4 1.3 %collective-permute-start.11 = (bf16[256,1024]{1,0:T(8,128)(2,1)S(1)}, bf16[256,1024]{1,0:T(8,128)(2,1)S(1)}, u32[]{:S(2)}, u32[]{:S(2)}) collective-permute-start(bf16[256,1024]{1,0:T(8,128)(2,1)S(1)} %products.4), channel_id=1, source_target_pairs={{0,4},{4,0},{8,12},{12,8},{1,5},{5,1},{9,13},{13,9},{2,6},{6,2},{1... | collective-permute-start | bytes 1572872 | tf_op jit(solution)/shard_map/ppermute | solution.py:604
  36.7 0.6 collective-permute-done.9.refs_1_
  37.3 1.0 products.5
  38.3 3.5 %collective-permute-start.13 = (bf16[256,1024]{1,0:T(8,128)(2,1)S(1)}, bf16[256,1024]{1,0:T(8,128)(2,1)S(1)}, u32[]{:S(2)}, u32[]{:S(2)}) collective-permute-start(bf16[256,1024]{1,0:T(8,128)(2,1)S(1)} %products.5), channel_id=1, source_target_pairs={{0,4},{12,8},{1,5},{13,9},{2,6},{14,10},{3,7},{15,11},{16,20},{28,... | collective-permute-start | bytes 1572872 | tf_op jit(solution)/shard_map/ppermute | solution.py:604
  41.8 0.7 collective-permute-start.10
  42.5 3.9 %products.6 = (bf16[4,256,1024]{2,1,0:T(8,128)(2,1)S(1)}, bf16[256,1024]{1,0:T(8,128)(2,1)S(1)}) custom-call(f32[32,8192]{1,0:T(8,128)S(1)} %get-tuple-element.114.scales.token.refs_0_, f32[32,8192]{1,0:T(8,128)S(1)} %get-tuple-element.114.scales.token.refs_0_, bf16[512,8192]{1,0:T(8,128)(2,1)S(1)} %get-tuple-element.63.held_rows.refs_1_, ...), custom_call_target="tpu_custom_call" | custom-call | flops 1 | bytes 1 | tf_op jit(solution)/shard_map/products/pallas_call | solution.py:232
  46.4 0.0 collective-permute-done.10.refs_1_
  46.5 2.2 %collective-permute-start.12 = (bf16[128,256]{1,0:T(8,128)(2,1)S(1)}, bf16[128,256]{1,0:T(8,128)(2,1)S(1)}, u32[]{:S(2)}, u32[]{:S(2)}) collective-permute-start(bf16[128,256]{1,0:T(8,128)(2,1)S(1)} %hop.4.refs_0_), channel_id=1, source_target_pairs={{0,4},{4,0},{8,12},{12,8},{1,5},{5,1},{9,13},{13,9},{2,6},{6,2},{1... | collective-permute-start | bytes 196616 | tf_op jit(solution)/shard_map/ppermute | solution.py:625
  48.7 1.9 %collective-permute-start.17 = (bf16[256,1024]{1,0:T(8,128)(2,1)S(1)}, bf16[256,1024]{1,0:T(8,128)(2,1)S(1)}, u32[]{:S(2)}, u32[]{:S(2)}) collective-permute-start(bf16[256,1024]{1,0:T(8,128)(2,1)S(1)} %get-tuple-element.106), channel_id=1, source_target_pairs={{0,4},{12,8},{1,5},{13,9},{2,6},{14,10},{3,7},{15,11},{16,20},{28,... | collective-permute-start | bytes 1572872 | tf_op jit(solution)/shard_map/ppermute | solution.py:604
  50.7 0.1 operand.6
  50.8 0.7 collective-permute-start.15
  51.5 3.9 %products.7 = (bf16[4,256,1024]{2,1,0:T(8,128)(2,1)S(1)}, bf16[256,1024]{1,0:T(8,128)(2,1)S(1)}) custom-call(f32[32,8192]{1,0:T(8,128)S(1)} %get-tuple-element.114.scales.token.refs_0_, f32[32,8192]{1,0:T(8,128)S(1)} %get-tuple-element.114.scales.token.refs_0_, bf16[512,8192]{1,0:T(8,128)(2,1)S(1)} %get-tuple-element.63.held_rows.refs_1_, ...), custom_call_target="tpu_custom_call" | custom-call | flops 1 | bytes 1 | tf_op jit(solution)/shard_map/products/pallas_call | solution.py:232
  55.5 6.2 %collective-permute-done.12.refs_1_ = bf16[128,256]{1,0:T(8,128)(2,1)S(1)} collective-permute-done((bf16[128,256]{1,0:T(8,128)(2,1)S(1)}, bf16[128,256]{1,0:T(8,128)(2,1)S(1)}, u32[]{:S(2)}, u32[]{:S(2)}) %collective-permute-start.12) | collective-permute-done | bytes 65568 | tf_op jit(solution)/shard_map/ppermute | solution.py:625
  61.7 0.1 operand.7
  61.8 0.7 collective-permute-start.18
  62.5 7.6 %collective-permute-start.19 = (bf16[256,1024]{1,0:T(8,128)(2,1)S(1)}, bf16[256,1024]{1,0:T(8,128)(2,1)S(1)}, u32[]{:S(2)}, u32[]{:S(2)}) collective-permute-start(bf16[256,1024]{1,0:T(8,128)(2,1)S(1)} %get-tuple-element.110), channel_id=1, source_target_pairs={{0,4},{12,8},{1,5},{13,9},{2,6},{14,10},{3,7},{15,11},{16,20},{28,... | collective-permute-start | bytes 1572872 | tf_op jit(solution)/shard_map/ppermute | solution.py:604
  70.1 0.1 collective-permute-start.14
  70.2 1.0 turn.1
  71.2 0.2 collective-permute-done.14.refs_1_
  71.4 0.6 collective-permute-start.16
  72.0 0.0 collective-permute-done.15.refs_1_
  72.0 0.1 operand.8
  72.2 5.0 %collective-permute-done.16.refs_1_ = f32[128,256]{1,0:T(8,128)S(1)} collective-permute-done((f32[128,256]{1,0:T(8,128)S(1)}, f32[128,256]{1,0:T(8,128)S(1)}, u32[]{:S(2)}, u32[]{:S(2)}) %collective-permute-start.16) | collective-permute-done | bytes 131104 | tf_op jit(solution)/shard_map/ppermute | solution.py:535
  77.1 0.7 side.5
  77.9 0.0 collective-permute-start.20
  77.9 0.0 collective-permute-done.17.refs_1_
  77.9 0.1 operand.9
  78.0 0.0 collective-permute-done.18.refs_1_
  78.0 0.1 operand.10
  78.2 0.7 collective-permute-start.21
  78.9 5.2 %collective-permute-done.19.refs_1_ = bf16[256,1024]{1,0:T(8,128)(2,1)S(1)} collective-permute-done((bf16[256,1024]{1,0:T(8,128)(2,1)S(1)}, bf16[256,1024]{1,0:T(8,128)(2,1)S(1)}, u32[]{:S(2)}, u32[]{:S(2)}) %collective-permute-start.19) | collective-permute-done | bytes 524320 | tf_op jit(solution)/shard_map/ppermute | solution.py:604
  84.1 0.1 operand.11
  84.2 0.7 collective-permute-start.23
  85.0 5.7 %collective-permute-start.22 = (bf16[256,1024]{1,0:T(8,128)(2,1)S(1)}, bf16[256,1024]{1,0:T(8,128)(2,1)S(1)}, u32[]{:S(2)}, u32[]{:S(2)}) collective-permute-start(bf16[256,1024]{1,0:T(8,128)(2,1)S(1)} %operand.10), channel_id=1, source_target_pairs={{0,4},{8,12},{4,0},{12,8},{1,5},{9,13},{5,1},{13,9},{2,6},{10,14},... | collective-permute-start | bytes 1572872 | tf_op jit(solution)/shard_map/ppermute | solution.py:604
  90.6 4.7 %collective-permute-done.20.refs_1_ = bf16[256,1024]{1,0:T(8,128)(2,1)S(1)} collective-permute-done((bf16[256,1024]{1,0:T(8,128)(2,1)S(1)}, bf16[256,1024]{1,0:T(8,128)(2,1)S(1)}, u32[]{:S(2)}, u32[]{:S(2)}) %collective-permute-start.20) | collective-permute-done | bytes 524320 | tf_op jit(solution)/shard_map/ppermute | solution.py:604
  95.3 0.0 collective-permute-done.21.refs_2_
  95.3 1.1 %keep.2.refs_3_ = f32[2048,256]{1,0:T(8,128)} custom-call(f32[32,8192]{1,0:T(8,128)S(1)} %get-tuple-element.114.scales.token.refs_0_, bf16[4,256,1024]{2,1,0:T(8,128)(2,1)S(1)} %get-tuple-element.87.refs_0_, bf16[256,1024]{1,0:T(8,128)(2,1)S(1)} %collective-permute-done.20.refs_1_, bf16[256,1024]{1,0:T(8,128)(2,1)S(1)} %collective-permute-done.21.refs_2_), custom_call_target="tpu_custom_call" | custom-call | flops 1 | bytes 1 | tf_op jit(solution)/shard_map/keep/pallas_call | solution.py:232
  96.5 0.0 collective-permute-done.23.refs_2_
  96.5 9.3 %collective-permute-done.22.refs_1_ = bf16[256,1024]{1,0:T(8,128)(2,1)S(1)} collective-permute-done((bf16[256,1024]{1,0:T(8,128)(2,1)S(1)}, bf16[256,1024]{1,0:T(8,128)(2,1)S(1)}, u32[]{:S(2)}, u32[]{:S(2)}) %collective-permute-start.22) | collective-permute-done | bytes 524320 | tf_op jit(solution)/shard_map/ppermute | solution.py:604
  105.8 1.1 %keep.3 = f32[2048,256]{1,0:T(8,128)} custom-call(f32[32,8192]{1,0:T(8,128)S(1)} %get-tuple-element.114.scales.token.refs_0_, bf16[4,256,1024]{2,1,0:T(8,128)(2,1)S(1)} %get-tuple-element.94.refs_0_, bf16[256,1024]{1,0:T(8,128)(2,1)S(1)} %collective-permute-done.22.refs_1_, ...), custom_call_target="tpu_custom_call", output_to_operand_aliasing={{}: (4, {})} | custom-call | flops 1 | bytes 1 | tf_op jit(solution)/shard_map/keep/pallas_call | solution.py:232
  (15 shorter events, 0.2 us)
Async XLA Ops:
  6.4 9.3 %collective-permute-start = (f32[256,256]{1,0:T(8,128)S(1)}, f32[256,256]{1,0:T(8,128)S(1)}, u32[]{:S(2)}, u32[]{:S(2)}) collective-permute-start(f32[256,256]{1,0:T(8,128)S(1)} %get-tuple-element.62), channel_id=1, source_target_pairs={{0,2},{2,0},{1,3},{3,1},{4,6},{6,4},{5,7},{7,5},{8,10},{10,8},{9,1... | collective-permute-start | bytes 786440 | tf_op jit(solution)/shard_map/ppermute | solution.py:535
  13.3 1.4 %collective-permute-start.1 = (f32[256,128]{1,0:T(8,128)S(1)}, f32[256,128]{1,0:T(8,128)S(1)}, u32[]{:S(2)}, u32[]{:S(2)}) collective-permute-start(f32[256,128]{1,0:T(8,128)S(1)} %get-tuple-element.66), channel_id=1, source_target_pairs={{0,1},{1,0},{2,3},{3,2},{4,5},{5,4},{6,7},{7,6},{8,9},{9,8},{10,11... | collective-permute-start | bytes 393224 | tf_op jit(solution)/shard_map/ppermute | solution.py:535
  13.4 1.5 %collective-permute-start.2 = (f32[256,128]{1,0:T(8,128)S(1)}, f32[256,128]{1,0:T(8,128)S(1)}, u32[]{:S(2)}, u32[]{:S(2)}) collective-permute-start(f32[256,128]{1,0:T(8,128)S(1)} %get-tuple-element.67), channel_id=1, source_target_pairs={{0,1},{1,0},{2,3},{3,2},{4,5},{5,4},{6,7},{7,6},{8,9},{9,8},{10,11... | collective-permute-start | bytes 393224 | tf_op jit(solution)/shard_map/ppermute | solution.py:535
  15.8 6.3 %collective-permute-start.3 = (f32[256,256]{1,0:T(8,128)S(1)}, f32[256,256]{1,0:T(8,128)S(1)}, u32[]{:S(2)}, u32[]{:S(2)}) collective-permute-start(f32[256,256]{1,0:T(8,128)S(1)} %add.3.gram_a), channel_id=1, source_target_pairs={{0,1},{1,0},{2,3},{3,2},{4,5},{5,4},{6,7},{7,6},{8,9},{9,8},{10,11... | collective-permute-start | bytes 786440 | tf_op jit(solution)/shard_map/ppermute | solution.py:535
  15.9 9.8 %collective-permute-start.6 = (f32[256,256]{1,0:T(8,128)S(1)}, f32[256,256]{1,0:T(8,128)S(1)}, u32[]{:S(2)}, u32[]{:S(2)}) collective-permute-start(f32[256,256]{1,0:T(8,128)S(1)} %plus.3), channel_id=1, source_target_pairs={{0,2},{2,0},{1,3},{3,1},{4,6},{6,4},{5,7},{7,5},{8,10},{10,8},{9,1... | collective-permute-start | bytes 786440 | tf_op jit(solution)/shard_map/ppermute | solution.py:535
  17.7 8.1 %copy-start = (bf16[1024,256]{1,0:T(8,128)(2,1)S(1)}, bf16[1024,256]{1,0:T(8,128)(2,1)}, u32[]{:S(2)}) copy-start(bf16[1024,256]{1,0:T(8,128)(2,1)} %refs_4_.1) | copy-start | bytes 1572868
  21.5 4.1 %collective-permute-start.4 = (f32[256,128]{1,0:T(8,128)S(1)}, f32[256,128]{1,0:T(8,128)S(1)}, u32[]{:S(2)}, u32[]{:S(2)}) collective-permute-start(f32[256,128]{1,0:T(8,128)S(1)} %get-tuple-element.75), channel_id=1, source_target_pairs={{0,1},{1,0},{2,3},{3,2},{4,5},{5,4},{6,7},{7,6},{8,9},{9,8},{10,11... | collective-permute-start | bytes 393224 | tf_op jit(solution)/shard_map/ppermute | solution.py:535
  21.8 3.9 %collective-permute-start.5 = (f32[256,128]{1,0:T(8,128)S(1)}, f32[256,128]{1,0:T(8,128)S(1)}, u32[]{:S(2)}, u32[]{:S(2)}) collective-permute-start(f32[256,128]{1,0:T(8,128)S(1)} %get-tuple-element.76), channel_id=1, source_target_pairs={{0,1},{1,0},{2,3},{3,2},{4,5},{5,4},{6,7},{7,6},{8,9},{9,8},{10,11... | collective-permute-start | bytes 393224 | tf_op jit(solution)/shard_map/ppermute | solution.py:535
  26.8 5.6 %collective-permute-start.7 = (bf16[256,256]{1,0:T(8,128)(2,1)S(1)}, bf16[256,256]{1,0:T(8,128)(2,1)S(1)}, u32[]{:S(2)}, u32[]{:S(2)}) collective-permute-start(bf16[256,256]{1,0:T(8,128)(2,1)S(1)} %admm.1.refs_0_), channel_id=1, source_target_pairs={{0,2},{2,0},{1,3},{3,1},{4,6},{6,4},{5,7},{7,5},{8,10},{10,8},{9,1... | collective-permute-start | bytes 393224 | tf_op jit(solution)/shard_map/ppermute | solution.py:535
  32.4 2.0 %collective-permute-start.8 = (bf16[256,512]{1,0:T(8,128)(2,1)S(1)}, bf16[256,512]{1,0:T(8,128)(2,1)S(1)}, u32[]{:S(2)}, u32[]{:S(2)}) collective-permute-start(bf16[256,512]{1,0:T(8,128)(2,1)S(1)} %side.3.refs_0_), channel_id=1, source_target_pairs={{0,1},{1,0},{2,3},{3,2},{4,5},{5,4},{6,7},{7,6},{8,9},{9,8},{10,11... | collective-permute-start | bytes 786440 | tf_op jit(solution)/shard_map/ppermute | solution.py:535
  32.7 4.6 %collective-permute-start.9 = (bf16[128,256]{1,0:T(8,128)(2,1)S(1)}, bf16[128,256]{1,0:T(8,128)(2,1)S(1)}, u32[]{:S(2)}, u32[]{:S(2)}) collective-permute-start(bf16[128,256]{1,0:T(8,128)(2,1)S(1)} %row_share.1.refs_0_), channel_id=1, source_target_pairs={{0,4},{4,0},{8,12},{12,8},{1,5},{5,1},{9,13},{13,9},{2,6},{6,2},{1... | collective-permute-start | bytes 196616 | tf_op jit(solution)/shard_map/ppermute | solution.py:625
  35.4 15.3 %collective-permute-start.11 = (bf16[256,1024]{1,0:T(8,128)(2,1)S(1)}, bf16[256,1024]{1,0:T(8,128)(2,1)S(1)}, u32[]{:S(2)}, u32[]{:S(2)}) collective-permute-start(bf16[256,1024]{1,0:T(8,128)(2,1)S(1)} %products.4), channel_id=1, source_target_pairs={{0,4},{4,0},{8,12},{12,8},{1,5},{5,1},{9,13},{13,9},{2,6},{6,2},{1... | collective-permute-start | bytes 1572872 | tf_op jit(solution)/shard_map/ppermute | solution.py:604
  38.3 23.4 %collective-permute-start.13 = (bf16[256,1024]{1,0:T(8,128)(2,1)S(1)}, bf16[256,1024]{1,0:T(8,128)(2,1)S(1)}, u32[]{:S(2)}, u32[]{:S(2)}) collective-permute-start(bf16[256,1024]{1,0:T(8,128)(2,1)S(1)} %products.5), channel_id=1, source_target_pairs={{0,4},{12,8},{1,5},{13,9},{2,6},{14,10},{3,7},{15,11},{16,20},{28,... | collective-permute-start | bytes 1572872 | tf_op jit(solution)/shard_map/ppermute | solution.py:604
  41.8 4.6 %collective-permute-start.10 = (bf16[128,256]{1,0:T(8,128)(2,1)S(1)}, bf16[128,256]{1,0:T(8,128)(2,1)S(1)}, u32[]{:S(2)}, u32[]{:S(2)}) collective-permute-start(bf16[128,256]{1,0:T(8,128)(2,1)S(1)} %hop.3.refs_0_), channel_id=1, source_target_pairs={{4,8},{8,4},{5,9},{9,5},{6,10},{10,6},{7,11},{11,7},{20,24},{24,20... | collective-permute-start | bytes 196616 | tf_op jit(solution)/shard_map/ppermute | solution.py:625
  46.5 15.2 %collective-permute-start.12 = (bf16[128,256]{1,0:T(8,128)(2,1)S(1)}, bf16[128,256]{1,0:T(8,128)(2,1)S(1)}, u32[]{:S(2)}, u32[]{:S(2)}) collective-permute-start(bf16[128,256]{1,0:T(8,128)(2,1)S(1)} %hop.4.refs_0_), channel_id=1, source_target_pairs={{0,4},{4,0},{8,12},{12,8},{1,5},{5,1},{9,13},{13,9},{2,6},{6,2},{1... | collective-permute-start | bytes 196616 | tf_op jit(solution)/shard_map/ppermute | solution.py:625
  48.7 29.1 %collective-permute-start.17 = (bf16[256,1024]{1,0:T(8,128)(2,1)S(1)}, bf16[256,1024]{1,0:T(8,128)(2,1)S(1)}, u32[]{:S(2)}, u32[]{:S(2)}) collective-permute-start(bf16[256,1024]{1,0:T(8,128)(2,1)S(1)} %get-tuple-element.106), channel_id=1, source_target_pairs={{0,4},{12,8},{1,5},{13,9},{2,6},{14,10},{3,7},{15,11},{16,20},{28,... | collective-permute-start | bytes 1572872 | tf_op jit(solution)/shard_map/ppermute | solution.py:604
  50.8 21.2 %collective-permute-start.15 = (bf16[256,1024]{1,0:T(8,128)(2,1)S(1)}, bf16[256,1024]{1,0:T(8,128)(2,1)S(1)}, u32[]{:S(2)}, u32[]{:S(2)}) collective-permute-start(bf16[256,1024]{1,0:T(8,128)(2,1)S(1)} %operand.6), channel_id=1, source_target_pairs={{4,8},{8,4},{5,9},{9,5},{6,10},{10,6},{7,11},{11,7},{20,24},{24,20... | collective-permute-start | bytes 1572872 | tf_op jit(solution)/shard_map/ppermute | solution.py:604
  61.8 16.2 %collective-permute-start.18 = (bf16[256,1024]{1,0:T(8,128)(2,1)S(1)}, bf16[256,1024]{1,0:T(8,128)(2,1)S(1)}, u32[]{:S(2)}, u32[]{:S(2)}) collective-permute-start(bf16[256,1024]{1,0:T(8,128)(2,1)S(1)} %operand.7), channel_id=1, source_target_pairs={{4,8},{8,4},{5,9},{9,5},{6,10},{10,6},{7,11},{11,7},{20,24},{24,20... | collective-permute-start | bytes 1572872 | tf_op jit(solution)/shard_map/ppermute | solution.py:604
  62.5 21.6 %collective-permute-start.19 = (bf16[256,1024]{1,0:T(8,128)(2,1)S(1)}, bf16[256,1024]{1,0:T(8,128)(2,1)S(1)}, u32[]{:S(2)}, u32[]{:S(2)}) collective-permute-start(bf16[256,1024]{1,0:T(8,128)(2,1)S(1)} %get-tuple-element.110), channel_id=1, source_target_pairs={{0,4},{12,8},{1,5},{13,9},{2,6},{14,10},{3,7},{15,11},{16,20},{28,... | collective-permute-start | bytes 1572872 | tf_op jit(solution)/shard_map/ppermute | solution.py:604
  70.1 1.3 %collective-permute-start.14 = (bf16[128,256]{1,0:T(8,128)(2,1)S(1)}, bf16[128,256]{1,0:T(8,128)(2,1)S(1)}, u32[]{:S(2)}, u32[]{:S(2)}) collective-permute-start(bf16[128,256]{1,0:T(8,128)(2,1)S(1)} %hop.5.refs_0_), channel_id=1, source_target_pairs={{0,1},{1,0},{2,3},{3,2},{4,5},{5,4},{6,7},{7,6},{8,9},{9,8},{10,11... | collective-permute-start | bytes 196616 | tf_op jit(solution)/shard_map/ppermute | solution.py:535
  71.4 5.7 %collective-permute-start.16 = (f32[128,256]{1,0:T(8,128)S(1)}, f32[128,256]{1,0:T(8,128)S(1)}, u32[]{:S(2)}, u32[]{:S(2)}) collective-permute-start(f32[128,256]{1,0:T(8,128)S(1)} %plus.5.refs_0_), channel_id=1, source_target_pairs={{0,2},{2,0},{1,3},{3,1},{4,6},{6,4},{5,7},{7,5},{8,10},{10,8},{9,1... | collective-permute-start | bytes 393224 | tf_op jit(solution)/shard_map/ppermute | solution.py:535
  77.9 17.5 %collective-permute-start.20 = (bf16[256,1024]{1,0:T(8,128)(2,1)S(1)}, bf16[256,1024]{1,0:T(8,128)(2,1)S(1)}, u32[]{:S(2)}, u32[]{:S(2)}) collective-permute-start(bf16[256,1024]{1,0:T(8,128)(2,1)S(1)} %operand.8), channel_id=1, source_target_pairs={{0,4},{8,12},{4,0},{12,8},{1,5},{9,13},{5,1},{13,9},{2,6},{10,14},... | collective-permute-start | bytes 1572872 | tf_op jit(solution)/shard_map/ppermute | solution.py:604
  78.2 17.2 %collective-permute-start.21 = (bf16[256,1024]{1,0:T(8,128)(2,1)S(1)}, bf16[256,1024]{1,0:T(8,128)(2,1)S(1)}, u32[]{:S(2)}, u32[]{:S(2)}) collective-permute-start(bf16[256,1024]{1,0:T(8,128)(2,1)S(1)} %operand.9), channel_id=1, source_target_pairs={{4,8},{8,4},{5,9},{9,5},{6,10},{10,6},{7,11},{11,7},{20,24},{24,20... | collective-permute-start | bytes 1572872 | tf_op jit(solution)/shard_map/ppermute | solution.py:604
  84.2 12.3 %collective-permute-start.23 = (bf16[256,1024]{1,0:T(8,128)(2,1)S(1)}, bf16[256,1024]{1,0:T(8,128)(2,1)S(1)}, u32[]{:S(2)}, u32[]{:S(2)}) collective-permute-start(bf16[256,1024]{1,0:T(8,128)(2,1)S(1)} %operand.11), channel_id=1, source_target_pairs={{4,8},{8,4},{5,9},{9,5},{6,10},{10,6},{7,11},{11,7},{20,24},{24,20... | collective-permute-start | bytes 1572872 | tf_op jit(solution)/shard_map/ppermute | solution.py:604
  85.0 20.8 %collective-permute-start.22 = (bf16[256,1024]{1,0:T(8,128)(2,1)S(1)}, bf16[256,1024]{1,0:T(8,128)(2,1)S(1)}, u32[]{:S(2)}, u32[]{:S(2)}) collective-permute-start(bf16[256,1024]{1,0:T(8,128)(2,1)S(1)} %operand.10), channel_id=1, source_target_pairs={{0,4},{8,12},{4,0},{12,8},{1,5},{9,13},{5,1},{13,9},{2,6},{10,14},... | collective-permute-start | bytes 1572872 | tf_op jit(solution)/shard_map/ppermute | solution.py:604

commit v14 on v13

--- a/solution.py
+++ b/solution.py
@@ -297,9 +297,9 @@
     left_high, left_low = left
     right_high, right_low = right
     dot = functools.partial(jnp.dot, preferred_element_type=F32)
-    return dot(left_high, right_high) + (
-        dot(left_high, right_low) + dot(left_low, right_high)
-    )
+    rows = left_high.shape[0]
+    both = dot(jnp.concatenate([left_high, left_low], axis=0), right_high)
+    return both[:rows] + (dot(left_high, right_low) + both[rows:])
 
 
 def inverse_kernel(gram_a, gram_b, inverse, rho_out):
@@ -326,12 +326,14 @@
         step = halves(gain * (2.0 * eye - image))
         if first:
             guess = guess[0:1, 0:1] * (gain * (2.0 * eye - image))
+            image = product3(halves(image), step)
+        elif done:
+            guess = product3(halves(guess), step)
+            break
         else:
-            guess = product3(halves(guess), step)
+            both = product3(halves(jnp.concatenate([guess, image], axis=0)), step)
+            guess, image = both[:width], both[width:]
         first = False
-        if done:
-            break
-        image = product3(halves(image), step)
     rest = eye - jnp.dot(
         matrix, guess, preferred_element_type=F32, precision=lax.Precision.HIGHEST
     )
@@ -383,7 +385,9 @@
     quarter = rows // 4
     groups = [(sent, False), (kept, True)]
 
-    @pl.loop(0, steps if only_first else line.size * steps)
+    turns = jnp.where(line.sends(1, 0), steps, 0) if only_first else line.size * steps
+
+    @pl.loop(0, turns)
     def _(turn):
         order, step = (block, turn) if only_first else (turn // steps, lax.rem(turn, steps))
         genes = pl.ds(pl.multiple_of(order * size + start + step * wide, span), wide)
@@ -512,14 +516,17 @@
     def __init__(self, size):
         self.size = size
 
-    def pairs(self, phase, parity, exchange=False):
+    def pairs(self, phase, parity):
         links = range(parity, self.size - 1, 2)
         right = [(i, i + 1) for i in links if i < phase]
         left = [(i + 1, i) for i in links if i + 1 >= self.size - phase]
-        pairs = right + left
-        if exchange:
-            pairs = sorted(set(pairs) | {(b, a) for a, b in pairs})
-        return pairs
+        return right + left
+
+    def sends(self, phase, parity):
+        cell = lax.axis_index("cell")
+        ahead = self.size - phase
+        to_right = (cell & 1) == parity
+        return jnp.where(to_right, cell + ahead < self.size, cell >= ahead)
 
     def block(self, phase, parity):
         cell = lax.axis_index("cell")
@@ -600,7 +607,7 @@
     arrived = {}
 
     def send(value, phase, parity, index):
-        pairs = line.pairs(phase, parity, exchange=phase == 1 and index == 0)
+        pairs = line.pairs(phase, parity)
         arrived[phase, parity, index] = lax.ppermute(value, "cell", pairs) if pairs else None
 
     def resend(token, phase, parity, index):

time: 107 us -> 109 us (1.019)
  waiting for transfers between devices: 38 us -> 39.6 us
    ppermute x3, waiting for transfers between devices: 6.76 us -> 7.86 us  [hop_rows(): rows_arrived = lax.ppermute(rows_sum, 'cell', both)]
where the time goes in v14:
time: 109 us; the launch traced here: 108 us
  waiting for transfers between devices  39.6 us (36%)
  starting transfers between devices  34 us (31%)
  Pallas kernels  33.8 us (31%)
    ppermute x10, starting transfers between devices, send(): lax.ppermute(value, 'cell', pairs)  22.4 us
    ppermute x10, waiting for transfers between devices, send(): lax.ppermute(value, 'cell', pairs)  19.4 us
    pallas_call x24, Pallas kernels, call(): pl.pallas_call(lambda token, *refs: kernel(*refs), out_shape=out_shape, i...  16.1 us
    ppermute x11, waiting for transfers between devices, swap(): return lax.ppermute(value, axis, [(i, i ^ step) for i in range(size)])  12.3 us
    ppermute x3, waiting for transfers between devices, hop_rows(): rows_arrived = lax.ppermute(rows_sum, 'cell', both)  7.86 us
    pallas_call x2, Pallas kernels, cross(): pl.pallas_call(functools.partial(cross_kernel, bit, kept, rows), out_shap...  7.74 us
    ppermute x11, starting transfers between devices, swap(): return lax.ppermute(value, axis, [(i, i ^ step) for i in range(size)])  7.11 us
    pallas_call x1, Pallas kernels, load(): pl.pallas_call(functools.partial(load_kernel, bit), out_shape=(jax.ShapeD...  5.81 us
  transfers between devices with their start and end apart: 24, of which 11 were waited for; matrix products, arithmetic and copies ran while one was open for 0% of the time, Pallas kernels for 24%

profile of v14, /device:TPU:0, one launch (start us, length us, event | category | flops | bytes accessed | tf_op | source)
XLA Modules:
  0.0 108.5 jit_solution(17036023679102808135)
XLA Ops:
  0.6 5.8 %load.1 = (f32[256,256]{1,0:T(8,128)S(1)}, f32[32,8192]{1,0:T(8,128)S(1)}, bf16[8192,256]{1,0:T(8,128)(2,1)S(1)}, bf16[512,8192]{1,0:T(8,128)(2,1)S(1)}) custom-call(bf16[256,8192]{1,0:T(8,128)(2,1)} %genes.1, bf16[1024,8192]{1,0:T(8,128)(2,1)} %refs_0_.1, s32[4,32]{1,0:T(4,128)} %tile_mask.1, s32[4,32]{1,0:T(4,128)} %tile_counts.1), custom_call_target="tpu_custom_call" | custom-call | flops 1 | bytes 1 | tf_op jit(solution)/shard_map/load/pallas_call | solution.py:118
  6.4 3.0 %collective-permute-start = (f32[256,256]{1,0:T(8,128)S(1)}, f32[256,256]{1,0:T(8,128)S(1)}, u32[]{:S(2)}, u32[]{:S(2)}) collective-permute-start(f32[256,256]{1,0:T(8,128)S(1)} %get-tuple-element.62), channel_id=1, source_target_pairs={{0,2},{2,0},{1,3},{3,1},{4,6},{6,4},{5,7},{7,5},{8,10},{10,8},{9,1... | collective-permute-start | bytes 786440 | tf_op jit(solution)/shard_map/ppermute | solution.py:542
  9.4 3.9 %cross_sent.1 = (f32[256,128]{1,0:T(8,128)S(1)}, f32[256,128]{1,0:T(8,128)S(1)}, f32[256,256]{1,0:T(8,128)S(1)}, bf16[512,8192]{1,0:T(8,128)(2,1)S(1)}) custom-call(f32[32,8192]{1,0:T(8,128)S(1)} %get-tuple-element.114.scales.token.refs_0_, bf16[512,8192]{1,0:T(8,128)(2,1)S(1)} %get-tuple-element.63.held_rows.refs_1_, ...), custom_call_target="tpu_custom_call" | custom-call | flops 1 | bytes 1 | tf_op jit(solution)/shard_map/cross_sent/pallas_call | solution.py:206
  13.3 0.1 collective-permute-start.1
  13.4 0.5 collective-permute-start.2
  13.9 0.8 collective-permute-done.1.refs_1_
  14.7 0.2 collective-permute-done.2.refs_2_
  15.0 0.8 collective-permute-done
  15.8 0.1 collective-permute-start.3
  15.9 1.8 %collective-permute-start.6 = (f32[256,256]{1,0:T(8,128)S(1)}, f32[256,256]{1,0:T(8,128)S(1)}, u32[]{:S(2)}, u32[]{:S(2)}) collective-permute-start(f32[256,256]{1,0:T(8,128)S(1)} %plus.3), channel_id=1, source_target_pairs={{0,2},{2,0},{1,3},{3,1},{4,6},{6,4},{5,7},{7,5},{8,10},{10,8},{9,1... | collective-permute-start | bytes 786440 | tf_op jit(solution)/shard_map/ppermute | solution.py:542
  17.7 3.9 %cross_kept.1 = (f32[256,128]{1,0:T(8,128)S(1)}, f32[256,128]{1,0:T(8,128)S(1)}, f32[256,256]{1,0:T(8,128)S(1)}) custom-call(f32[32,8192]{1,0:T(8,128)S(1)} %get-tuple-element.114.scales.token.refs_0_, bf16[512,8192]{1,0:T(8,128)(2,1)S(1)} %get-tuple-element.73.held_rows.refs_2_, bf16[8192,256]{1,0:T(8,128)(2,1)S(1)} %get-tuple-element.64.turned), custom_call_target="tpu_custom_call" | custom-call | flops 1 | bytes 1 | tf_op jit(solution)/shard_map/cross_kept/pallas_call | solution.py:206
  21.5 0.2 collective-permute-start.4
  21.8 0.3 collective-permute-start.5
  22.1 0.0 collective-permute-done.3.gram_b
  22.1 4.2 %inverse.1 = (f32[256,256]{1,0:T(8,128)S(1)}, f32[8,128]{1,0:T(8,128)S(1)}) custom-call(f32[256,256]{1,0:T(8,128)S(1)} %add.3.gram_a, f32[256,256]{1,0:T(8,128)S(1)} %collective-permute-done.3.gram_b), custom_call_target="tpu_custom_call" | custom-call | flops 1 | bytes 1 | tf_op jit(solution)/shard_map/inverse/pallas_call | solution.py:348
  26.3 0.0 collective-permute-done.4.refs_1_
  26.3 0.0 collective-permute-done.5.refs_2_
  26.4 0.0 collective-permute-done.6.refs_2_
  26.4 1.0 admm.1.refs_0_
  27.5 0.3 collective-permute-start.7
  27.8 5.3 %collective-permute-done.7.refs_1_ = bf16[256,256]{1,0:T(8,128)(2,1)S(1)} collective-permute-done((bf16[256,256]{1,0:T(8,128)(2,1)S(1)}, bf16[256,256]{1,0:T(8,128)(2,1)S(1)}, u32[]{:S(2)}, u32[]{:S(2)}) %collective-permute-start.7) | collective-permute-done | bytes 131104 | tf_op jit(solution)/shard_map/ppermute | solution.py:542
  33.1 0.1 collective-permute-start.8
  33.2 0.2 row_share.1.refs_0_
  33.4 1.6 %collective-permute-start.9 = (bf16[128,256]{1,0:T(8,128)(2,1)S(1)}, bf16[128,256]{1,0:T(8,128)(2,1)S(1)}, u32[]{:S(2)}, u32[]{:S(2)}) collective-permute-start(bf16[128,256]{1,0:T(8,128)(2,1)S(1)} %row_share.1.refs_0_), channel_id=1, source_target_pairs={{0,4},{4,0},{8,12},{12,8},{1,5},{5,1},{9,13},{13,9},{2,6},{6,2},{1... | collective-permute-start | bytes 196616 | tf_op jit(solution)/shard_map/ppermute | solution.py:632
  35.1 1.0 products.4
  36.1 2.2 %collective-permute-start.11 = (bf16[256,1024]{1,0:T(8,128)(2,1)S(1)}, bf16[256,1024]{1,0:T(8,128)(2,1)S(1)}, u32[]{:S(2)}, u32[]{:S(2)}) collective-permute-start(bf16[256,1024]{1,0:T(8,128)(2,1)S(1)} %products.4), channel_id=1, source_target_pairs={{0,4},{12,8},{1,5},{13,9},{2,6},{14,10},{3,7},{15,11},{16,20},{28,... | collective-permute-start | bytes 1572872 | tf_op jit(solution)/shard_map/ppermute | solution.py:611
  38.4 1.0 products.5
  39.3 2.2 %collective-permute-start.13 = (bf16[256,1024]{1,0:T(8,128)(2,1)S(1)}, bf16[256,1024]{1,0:T(8,128)(2,1)S(1)}, u32[]{:S(2)}, u32[]{:S(2)}) collective-permute-start(bf16[256,1024]{1,0:T(8,128)(2,1)S(1)} %products.5), channel_id=1, source_target_pairs={{0,4},{12,8},{1,5},{13,9},{2,6},{14,10},{3,7},{15,11},{16,20},{28,... | collective-permute-start | bytes 1572872 | tf_op jit(solution)/shard_map/ppermute | solution.py:611
  41.6 0.7 collective-permute-start.10
  42.2 3.9 %products.6 = (bf16[4,256,1024]{2,1,0:T(8,128)(2,1)S(1)}, bf16[256,1024]{1,0:T(8,128)(2,1)S(1)}) custom-call(f32[32,8192]{1,0:T(8,128)S(1)} %get-tuple-element.114.scales.token.refs_0_, f32[32,8192]{1,0:T(8,128)S(1)} %get-tuple-element.114.scales.token.refs_0_, bf16[512,8192]{1,0:T(8,128)(2,1)S(1)} %get-tuple-element.63.held_rows.refs_1_, ...), custom_call_target="tpu_custom_call" | custom-call | flops 1 | bytes 1 | tf_op jit(solution)/shard_map/products/pallas_call | solution.py:232
  46.2 0.0 collective-permute-done.10.refs_1_
  46.2 2.2 %collective-permute-start.12 = (bf16[128,256]{1,0:T(8,128)(2,1)S(1)}, bf16[128,256]{1,0:T(8,128)(2,1)S(1)}, u32[]{:S(2)}, u32[]{:S(2)}) collective-permute-start(bf16[128,256]{1,0:T(8,128)(2,1)S(1)} %hop.4.refs_0_), channel_id=1, source_target_pairs={{0,4},{4,0},{8,12},{12,8},{1,5},{5,1},{9,13},{13,9},{2,6},{6,2},{1... | collective-permute-start | bytes 196616 | tf_op jit(solution)/shard_map/ppermute | solution.py:632
  48.5 1.9 %collective-permute-start.17 = (bf16[256,1024]{1,0:T(8,128)(2,1)S(1)}, bf16[256,1024]{1,0:T(8,128)(2,1)S(1)}, u32[]{:S(2)}, u32[]{:S(2)}) collective-permute-start(bf16[256,1024]{1,0:T(8,128)(2,1)S(1)} %get-tuple-element.106), channel_id=1, source_target_pairs={{0,4},{12,8},{1,5},{13,9},{2,6},{14,10},{3,7},{15,11},{16,20},{28,... | collective-permute-start | bytes 1572872 | tf_op jit(solution)/shard_map/ppermute | solution.py:611
  50.4 0.1 collective-permute-done.11.refs_1_
  50.6 0.1 operand.6
  50.7 0.7 collective-permute-start.15
  51.4 3.9 %products.7 = (bf16[4,256,1024]{2,1,0:T(8,128)(2,1)S(1)}, bf16[256,1024]{1,0:T(8,128)(2,1)S(1)}) custom-call(f32[32,8192]{1,0:T(8,128)S(1)} %get-tuple-element.114.scales.token.refs_0_, f32[32,8192]{1,0:T(8,128)S(1)} %get-tuple-element.114.scales.token.refs_0_, bf16[512,8192]{1,0:T(8,128)(2,1)S(1)} %get-tuple-element.63.held_rows.refs_1_, ...), custom_call_target="tpu_custom_call" | custom-call | flops 1 | bytes 1 | tf_op jit(solution)/shard_map/products/pallas_call | solution.py:232
  55.3 7.9 %collective-permute-done.12.refs_1_ = bf16[128,256]{1,0:T(8,128)(2,1)S(1)} collective-permute-done((bf16[128,256]{1,0:T(8,128)(2,1)S(1)}, bf16[128,256]{1,0:T(8,128)(2,1)S(1)}, u32[]{:S(2)}, u32[]{:S(2)}) %collective-permute-start.12) | collective-permute-done | bytes 65568 | tf_op jit(solution)/shard_map/ppermute | solution.py:632
  63.2 0.0 collective-permute-done.13.refs_1_
  63.2 0.1 operand.7
  63.4 0.7 collective-permute-start.18
  64.1 7.5 %collective-permute-start.19 = (bf16[256,1024]{1,0:T(8,128)(2,1)S(1)}, bf16[256,1024]{1,0:T(8,128)(2,1)S(1)}, u32[]{:S(2)}, u32[]{:S(2)}) collective-permute-start(bf16[256,1024]{1,0:T(8,128)(2,1)S(1)} %get-tuple-element.110), channel_id=1, source_target_pairs={{0,4},{12,8},{1,5},{13,9},{2,6},{14,10},{3,7},{15,11},{16,20},{28,... | collective-permute-start | bytes 1572872 | tf_op jit(solution)/shard_map/ppermute | solution.py:611
  71.6 0.1 collective-permute-start.14
  71.7 1.0 turn.1
  72.7 0.2 collective-permute-done.14.refs_1_
  73.0 0.6 collective-permute-start.16
  73.6 0.0 collective-permute-done.15.refs_1_
  73.6 0.1 operand.8
  73.7 5.0 %collective-permute-done.16.refs_1_ = f32[128,256]{1,0:T(8,128)S(1)} collective-permute-done((f32[128,256]{1,0:T(8,128)S(1)}, f32[128,256]{1,0:T(8,128)S(1)}, u32[]{:S(2)}, u32[]{:S(2)}) %collective-permute-start.16) | collective-permute-done | bytes 131104 | tf_op jit(solution)/shard_map/ppermute | solution.py:542
  78.7 0.7 side.5
  79.4 0.0 collective-permute-start.20
  79.4 0.0 collective-permute-done.17.refs_1_
  79.4 0.1 operand.9
  79.6 0.1 operand.10
  79.7 0.7 collective-permute-start.21
  80.4 5.2 %collective-permute-done.19.refs_1_ = bf16[256,1024]{1,0:T(8,128)(2,1)S(1)} collective-permute-done((bf16[256,1024]{1,0:T(8,128)(2,1)S(1)}, bf16[256,1024]{1,0:T(8,128)(2,1)S(1)}, u32[]{:S(2)}, u32[]{:S(2)}) %collective-permute-start.19) | collective-permute-done | bytes 524320 | tf_op jit(solution)/shard_map/ppermute | solution.py:611
  85.7 0.1 operand.11
  85.8 0.7 collective-permute-start.23
  86.5 5.7 %collective-permute-start.22 = (bf16[256,1024]{1,0:T(8,128)(2,1)S(1)}, bf16[256,1024]{1,0:T(8,128)(2,1)S(1)}, u32[]{:S(2)}, u32[]{:S(2)}) collective-permute-start(bf16[256,1024]{1,0:T(8,128)(2,1)S(1)} %operand.10), channel_id=1, source_target_pairs={{0,4},{8,12},{4,0},{12,8},{1,5},{9,13},{5,1},{13,9},{2,6},{10,14},... | collective-permute-start | bytes 1572872 | tf_op jit(solution)/shard_map/ppermute | solution.py:611
  92.2 4.7 %collective-permute-done.20.refs_1_ = bf16[256,1024]{1,0:T(8,128)(2,1)S(1)} collective-permute-done((bf16[256,1024]{1,0:T(8,128)(2,1)S(1)}, bf16[256,1024]{1,0:T(8,128)(2,1)S(1)}, u32[]{:S(2)}, u32[]{:S(2)}) %collective-permute-start.20) | collective-permute-done | bytes 524320 | tf_op jit(solution)/shard_map/ppermute | solution.py:611
  96.9 1.1 %keep.2.refs_3_ = f32[2048,256]{1,0:T(8,128)} custom-call(f32[32,8192]{1,0:T(8,128)S(1)} %get-tuple-element.114.scales.token.refs_0_, bf16[4,256,1024]{2,1,0:T(8,128)(2,1)S(1)} %get-tuple-element.87.refs_0_, bf16[256,1024]{1,0:T(8,128)(2,1)S(1)} %collective-permute-done.20.refs_1_, bf16[256,1024]{1,0:T(8,128)(2,1)S(1)} %collective-permute-done.21.refs_2_), custom_call_target="tpu_custom_call" | custom-call | flops 1 | bytes 1 | tf_op jit(solution)/shard_map/keep/pallas_call | solution.py:232
  98.1 0.0 collective-permute-done.23.refs_2_
  98.1 9.3 %collective-permute-done.22.refs_1_ = bf16[256,1024]{1,0:T(8,128)(2,1)S(1)} collective-permute-done((bf16[256,1024]{1,0:T(8,128)(2,1)S(1)}, bf16[256,1024]{1,0:T(8,128)(2,1)S(1)}, u32[]{:S(2)}, u32[]{:S(2)}) %collective-permute-start.22) | collective-permute-done | bytes 524320 | tf_op jit(solution)/shard_map/ppermute | solution.py:611
  107.3 1.1 %keep.3 = f32[2048,256]{1,0:T(8,128)} custom-call(f32[32,8192]{1,0:T(8,128)S(1)} %get-tuple-element.114.scales.token.refs_0_, bf16[4,256,1024]{2,1,0:T(8,128)(2,1)S(1)} %get-tuple-element.94.refs_0_, bf16[256,1024]{1,0:T(8,128)(2,1)S(1)} %collective-permute-done.22.refs_1_, ...), custom_call_target="tpu_custom_call", output_to_operand_aliasing={{}: (4, {})} | custom-call | flops 1 | bytes 1 | tf_op jit(solution)/shard_map/keep/pallas_call | solution.py:232
  (15 shorter events, 0.2 us)
Async XLA Ops:
  6.4 9.3 %collective-permute-start = (f32[256,256]{1,0:T(8,128)S(1)}, f32[256,256]{1,0:T(8,128)S(1)}, u32[]{:S(2)}, u32[]{:S(2)}) collective-permute-start(f32[256,256]{1,0:T(8,128)S(1)} %get-tuple-element.62), channel_id=1, source_target_pairs={{0,2},{2,0},{1,3},{3,1},{4,6},{6,4},{5,7},{7,5},{8,10},{10,8},{9,1... | collective-permute-start | bytes 786440 | tf_op jit(solution)/shard_map/ppermute | solution.py:542
  13.3 1.4 %collective-permute-start.1 = (f32[256,128]{1,0:T(8,128)S(1)}, f32[256,128]{1,0:T(8,128)S(1)}, u32[]{:S(2)}, u32[]{:S(2)}) collective-permute-start(f32[256,128]{1,0:T(8,128)S(1)} %get-tuple-element.66), channel_id=1, source_target_pairs={{0,1},{1,0},{2,3},{3,2},{4,5},{5,4},{6,7},{7,6},{8,9},{9,8},{10,11... | collective-permute-start | bytes 393224 | tf_op jit(solution)/shard_map/ppermute | solution.py:542
  13.4 1.5 %collective-permute-start.2 = (f32[256,128]{1,0:T(8,128)S(1)}, f32[256,128]{1,0:T(8,128)S(1)}, u32[]{:S(2)}, u32[]{:S(2)}) collective-permute-start(f32[256,128]{1,0:T(8,128)S(1)} %get-tuple-element.67), channel_id=1, source_target_pairs={{0,1},{1,0},{2,3},{3,2},{4,5},{5,4},{6,7},{7,6},{8,9},{9,8},{10,11... | collective-permute-start | bytes 393224 | tf_op jit(solution)/shard_map/ppermute | solution.py:542
  15.8 6.3 %collective-permute-start.3 = (f32[256,256]{1,0:T(8,128)S(1)}, f32[256,256]{1,0:T(8,128)S(1)}, u32[]{:S(2)}, u32[]{:S(2)}) collective-permute-start(f32[256,256]{1,0:T(8,128)S(1)} %add.3.gram_a), channel_id=1, source_target_pairs={{0,1},{1,0},{2,3},{3,2},{4,5},{5,4},{6,7},{7,6},{8,9},{9,8},{10,11... | collective-permute-start | bytes 786440 | tf_op jit(solution)/shard_map/ppermute | solution.py:542
  15.9 10.5 %collective-permute-start.6 = (f32[256,256]{1,0:T(8,128)S(1)}, f32[256,256]{1,0:T(8,128)S(1)}, u32[]{:S(2)}, u32[]{:S(2)}) collective-permute-start(f32[256,256]{1,0:T(8,128)S(1)} %plus.3), channel_id=1, source_target_pairs={{0,2},{2,0},{1,3},{3,1},{4,6},{6,4},{5,7},{7,5},{8,10},{10,8},{9,1... | collective-permute-start | bytes 786440 | tf_op jit(solution)/shard_map/ppermute | solution.py:542
  17.7 8.7 %copy-start = (bf16[1024,256]{1,0:T(8,128)(2,1)S(1)}, bf16[1024,256]{1,0:T(8,128)(2,1)}, u32[]{:S(2)}) copy-start(bf16[1024,256]{1,0:T(8,128)(2,1)} %refs_4_.1) | copy-start | bytes 1572868
  21.5 4.8 %collective-permute-start.4 = (f32[256,128]{1,0:T(8,128)S(1)}, f32[256,128]{1,0:T(8,128)S(1)}, u32[]{:S(2)}, u32[]{:S(2)}) collective-permute-start(f32[256,128]{1,0:T(8,128)S(1)} %get-tuple-element.75), channel_id=1, source_target_pairs={{0,1},{1,0},{2,3},{3,2},{4,5},{5,4},{6,7},{7,6},{8,9},{9,8},{10,11... | collective-permute-start | bytes 393224 | tf_op jit(solution)/shard_map/ppermute | solution.py:542
  21.8 4.6 %collective-permute-start.5 = (f32[256,128]{1,0:T(8,128)S(1)}, f32[256,128]{1,0:T(8,128)S(1)}, u32[]{:S(2)}, u32[]{:S(2)}) collective-permute-start(f32[256,128]{1,0:T(8,128)S(1)} %get-tuple-element.76), channel_id=1, source_target_pairs={{0,1},{1,0},{2,3},{3,2},{4,5},{5,4},{6,7},{7,6},{8,9},{9,8},{10,11... | collective-permute-start | bytes 393224 | tf_op jit(solution)/shard_map/ppermute | solution.py:542
  27.5 5.6 %collective-permute-start.7 = (bf16[256,256]{1,0:T(8,128)(2,1)S(1)}, bf16[256,256]{1,0:T(8,128)(2,1)S(1)}, u32[]{:S(2)}, u32[]{:S(2)}) collective-permute-start(bf16[256,256]{1,0:T(8,128)(2,1)S(1)} %admm.1.refs_0_), channel_id=1, source_target_pairs={{0,2},{2,0},{1,3},{3,1},{4,6},{6,4},{5,7},{7,5},{8,10},{10,8},{9,1... | collective-permute-start | bytes 393224 | tf_op jit(solution)/shard_map/ppermute | solution.py:542
  33.1 2.0 %collective-permute-start.8 = (bf16[256,512]{1,0:T(8,128)(2,1)S(1)}, bf16[256,512]{1,0:T(8,128)(2,1)S(1)}, u32[]{:S(2)}, u32[]{:S(2)}) collective-permute-start(bf16[256,512]{1,0:T(8,128)(2,1)S(1)} %side.3.refs_0_), channel_id=1, source_target_pairs={{0,1},{1,0},{2,3},{3,2},{4,5},{5,4},{6,7},{7,6},{8,9},{9,8},{10,11... | collective-permute-start | bytes 786440 | tf_op jit(solution)/shard_map/ppermute | solution.py:542
  33.4 4.9 %collective-permute-start.9 = (bf16[128,256]{1,0:T(8,128)(2,1)S(1)}, bf16[128,256]{1,0:T(8,128)(2,1)S(1)}, u32[]{:S(2)}, u32[]{:S(2)}) collective-permute-start(bf16[128,256]{1,0:T(8,128)(2,1)S(1)} %row_share.1.refs_0_), channel_id=1, source_target_pairs={{0,4},{4,0},{8,12},{12,8},{1,5},{5,1},{9,13},{13,9},{2,6},{6,2},{1... | collective-permute-start | bytes 196616 | tf_op jit(solution)/shard_map/ppermute | solution.py:632
  36.1 14.4 %collective-permute-start.11 = (bf16[256,1024]{1,0:T(8,128)(2,1)S(1)}, bf16[256,1024]{1,0:T(8,128)(2,1)S(1)}, u32[]{:S(2)}, u32[]{:S(2)}) collective-permute-start(bf16[256,1024]{1,0:T(8,128)(2,1)S(1)} %products.4), channel_id=1, source_target_pairs={{0,4},{12,8},{1,5},{13,9},{2,6},{14,10},{3,7},{15,11},{16,20},{28,... | collective-permute-start | bytes 1572872 | tf_op jit(solution)/shard_map/ppermute | solution.py:611
  39.3 23.9 %collective-permute-start.13 = (bf16[256,1024]{1,0:T(8,128)(2,1)S(1)}, bf16[256,1024]{1,0:T(8,128)(2,1)S(1)}, u32[]{:S(2)}, u32[]{:S(2)}) collective-permute-start(bf16[256,1024]{1,0:T(8,128)(2,1)S(1)} %products.5), channel_id=1, source_target_pairs={{0,4},{12,8},{1,5},{13,9},{2,6},{14,10},{3,7},{15,11},{16,20},{28,... | collective-permute-start | bytes 1572872 | tf_op jit(solution)/shard_map/ppermute | solution.py:611
  41.6 4.6 %collective-permute-start.10 = (bf16[128,256]{1,0:T(8,128)(2,1)S(1)}, bf16[128,256]{1,0:T(8,128)(2,1)S(1)}, u32[]{:S(2)}, u32[]{:S(2)}) collective-permute-start(bf16[128,256]{1,0:T(8,128)(2,1)S(1)} %hop.3.refs_0_), channel_id=1, source_target_pairs={{4,8},{8,4},{5,9},{9,5},{6,10},{10,6},{7,11},{11,7},{20,24},{24,20... | collective-permute-start | bytes 196616 | tf_op jit(solution)/shard_map/ppermute | solution.py:632
  46.2 17.0 %collective-permute-start.12 = (bf16[128,256]{1,0:T(8,128)(2,1)S(1)}, bf16[128,256]{1,0:T(8,128)(2,1)S(1)}, u32[]{:S(2)}, u32[]{:S(2)}) collective-permute-start(bf16[128,256]{1,0:T(8,128)(2,1)S(1)} %hop.4.refs_0_), channel_id=1, source_target_pairs={{0,4},{4,0},{8,12},{12,8},{1,5},{5,1},{9,13},{13,9},{2,6},{6,2},{1... | collective-permute-start | bytes 196616 | tf_op jit(solution)/shard_map/ppermute | solution.py:632
  48.5 31.0 %collective-permute-start.17 = (bf16[256,1024]{1,0:T(8,128)(2,1)S(1)}, bf16[256,1024]{1,0:T(8,128)(2,1)S(1)}, u32[]{:S(2)}, u32[]{:S(2)}) collective-permute-start(bf16[256,1024]{1,0:T(8,128)(2,1)S(1)} %get-tuple-element.106), channel_id=1, source_target_pairs={{0,4},{12,8},{1,5},{13,9},{2,6},{14,10},{3,7},{15,11},{16,20},{28,... | collective-permute-start | bytes 1572872 | tf_op jit(solution)/shard_map/ppermute | solution.py:611
  50.7 22.9 %collective-permute-start.15 = (bf16[256,1024]{1,0:T(8,128)(2,1)S(1)}, bf16[256,1024]{1,0:T(8,128)(2,1)S(1)}, u32[]{:S(2)}, u32[]{:S(2)}) collective-permute-start(bf16[256,1024]{1,0:T(8,128)(2,1)S(1)} %operand.6), channel_id=1, source_target_pairs={{4,8},{8,4},{5,9},{9,5},{6,10},{10,6},{7,11},{11,7},{20,24},{24,20... | collective-permute-start | bytes 1572872 | tf_op jit(solution)/shard_map/ppermute | solution.py:611
  63.4 16.2 %collective-permute-start.18 = (bf16[256,1024]{1,0:T(8,128)(2,1)S(1)}, bf16[256,1024]{1,0:T(8,128)(2,1)S(1)}, u32[]{:S(2)}, u32[]{:S(2)}) collective-permute-start(bf16[256,1024]{1,0:T(8,128)(2,1)S(1)} %operand.7), channel_id=1, source_target_pairs={{4,8},{8,4},{5,9},{9,5},{6,10},{10,6},{7,11},{11,7},{20,24},{24,20... | collective-permute-start | bytes 1572872 | tf_op jit(solution)/shard_map/ppermute | solution.py:611
  64.1 21.6 %collective-permute-start.19 = (bf16[256,1024]{1,0:T(8,128)(2,1)S(1)}, bf16[256,1024]{1,0:T(8,128)(2,1)S(1)}, u32[]{:S(2)}, u32[]{:S(2)}) collective-permute-start(bf16[256,1024]{1,0:T(8,128)(2,1)S(1)} %get-tuple-element.110), channel_id=1, source_target_pairs={{0,4},{12,8},{1,5},{13,9},{2,6},{14,10},{3,7},{15,11},{16,20},{28,... | collective-permute-start | bytes 1572872 | tf_op jit(solution)/shard_map/ppermute | solution.py:611
  71.6 1.3 %collective-permute-start.14 = (bf16[128,256]{1,0:T(8,128)(2,1)S(1)}, bf16[128,256]{1,0:T(8,128)(2,1)S(1)}, u32[]{:S(2)}, u32[]{:S(2)}) collective-permute-start(bf16[128,256]{1,0:T(8,128)(2,1)S(1)} %hop.5.refs_0_), channel_id=1, source_target_pairs={{0,1},{1,0},{2,3},{3,2},{4,5},{5,4},{6,7},{7,6},{8,9},{9,8},{10,11... | collective-permute-start | bytes 196616 | tf_op jit(solution)/shard_map/ppermute | solution.py:542
  73.0 5.7 %collective-permute-start.16 = (f32[128,256]{1,0:T(8,128)S(1)}, f32[128,256]{1,0:T(8,128)S(1)}, u32[]{:S(2)}, u32[]{:S(2)}) collective-permute-start(f32[128,256]{1,0:T(8,128)S(1)} %plus.5.refs_0_), channel_id=1, source_target_pairs={{0,2},{2,0},{1,3},{3,1},{4,6},{6,4},{5,7},{7,5},{8,10},{10,8},{9,1... | collective-permute-start | bytes 393224 | tf_op jit(solution)/shard_map/ppermute | solution.py:542
  79.4 17.5 %collective-permute-start.20 = (bf16[256,1024]{1,0:T(8,128)(2,1)S(1)}, bf16[256,1024]{1,0:T(8,128)(2,1)S(1)}, u32[]{:S(2)}, u32[]{:S(2)}) collective-permute-start(bf16[256,1024]{1,0:T(8,128)(2,1)S(1)} %operand.8), channel_id=1, source_target_pairs={{0,4},{8,12},{4,0},{12,8},{1,5},{9,13},{5,1},{13,9},{2,6},{10,14},... | collective-permute-start | bytes 1572872 | tf_op jit(solution)/shard_map/ppermute | solution.py:611
  79.7 17.2 %collective-permute-start.21 = (bf16[256,1024]{1,0:T(8,128)(2,1)S(1)}, bf16[256,1024]{1,0:T(8,128)(2,1)S(1)}, u32[]{:S(2)}, u32[]{:S(2)}) collective-permute-start(bf16[256,1024]{1,0:T(8,128)(2,1)S(1)} %operand.9), channel_id=1, source_target_pairs={{4,8},{8,4},{5,9},{9,5},{6,10},{10,6},{7,11},{11,7},{20,24},{24,20... | collective-permute-start | bytes 1572872 | tf_op jit(solution)/shard_map/ppermute | solution.py:611
  85.8 12.3 %collective-permute-start.23 = (bf16[256,1024]{1,0:T(8,128)(2,1)S(1)}, bf16[256,1024]{1,0:T(8,128)(2,1)S(1)}, u32[]{:S(2)}, u32[]{:S(2)}) collective-permute-start(bf16[256,1024]{1,0:T(8,128)(2,1)S(1)} %operand.11), channel_id=1, source_target_pairs={{4,8},{8,4},{5,9},{9,5},{6,10},{10,6},{7,11},{11,7},{20,24},{24,20... | collective-permute-start | bytes 1572872 | tf_op jit(solution)/shard_map/ppermute | solution.py:611
  86.5 20.8 %collective-permute-start.22 = (bf16[256,1024]{1,0:T(8,128)(2,1)S(1)}, bf16[256,1024]{1,0:T(8,128)(2,1)S(1)}, u32[]{:S(2)}, u32[]{:S(2)}) collective-permute-start(bf16[256,1024]{1,0:T(8,128)(2,1)S(1)} %operand.10), channel_id=1, source_target_pairs={{0,4},{8,12},{4,0},{12,8},{1,5},{9,13},{5,1},{13,9},{2,6},{10,14},... | collective-permute-start | bytes 1572872 | tf_op jit(solution)/shard_map/ppermute | solution.py:611

commit v15 on v13

--- a/solution.py
+++ b/solution.py
@@ -302,8 +302,8 @@
     )
 
 
-def inverse_kernel(gram_a, gram_b, inverse, rho_out):
-    gram = gram_a[...] + gram_b[...]
+def inverse_kernel(gram_in, inverse, rho_out):
+    gram = gram_in[...]
     width = gram.shape[0]
     shape = (width, width)
     diagonal = lax.broadcasted_iota(jnp.int32, shape, 0) == lax.broadcasted_iota(
@@ -340,8 +340,8 @@
     inverse[...] = (guess + product3(halves(guess), halves(series))) * scale
 
 
-def shifted_inverse(gram_a, gram_b):
-    width = gram_a.shape[0]
+def shifted_inverse(gram):
+    width = gram.shape[0]
     whole = pl.BlockSpec(memory_space=pltpu.VMEM)
     return pl.pallas_call(
         inverse_kernel,
@@ -349,12 +349,12 @@
             jax.ShapeDtypeStruct((width, width), F32),
             jax.ShapeDtypeStruct((8, 128), F32),
         ),
-        in_specs=[whole, whole],
+        in_specs=[whole],
         out_specs=(whole, whole),
         compiler_params=params(),
         cost_estimate=cost(1, 1),
         name="inverse",
-    )(gram_a, gram_b)
+    )(gram)
 
 
 def admm_kernel(genes, rho_block, cross_a, cross_b, inverse, start, columns_out):
@@ -461,33 +461,38 @@
     return call(functools.partial(hop_kernel, kind, targets), "hop", shape, token, own, arrived)
 
 
-def operand_kernel(line, phase, parity, total, before, out):
-    own = total[line.block(phase, parity)].astype(F32)
-    out[...] = (own + before[...].astype(F32)).astype(BF16)
-
-
-def operand(line, phase, parity, token, total, before):
-    shape = jax.ShapeDtypeStruct(before.shape, BF16)
+def operand_kernel(line, phase, parity, total, before, *outs):
+    own = total.at[line.block(phase, parity)]
+    start = 0
+    for out in outs:
+        at = slice(start, start + out.shape[1])
+        out[...] = (own[:, at].astype(F32) + before[:, at].astype(F32)).astype(BF16)
+        start += out.shape[1]
+
+
+def operand(line, phase, parity, parts, token, total, before):
+    width = before.shape[0]
     return call(
         functools.partial(operand_kernel, line, phase, parity),
-        "operand", shape, token, total, before,
-    )
-
-
-def keep_kernel(start, total, first, second, *refs):
+        "operand", tuple(jax.ShapeDtypeStruct((width, part), BF16) for part in parts),
+        token, total, before,
+    )
+
+
+def keep_kernel(start, skip, total, first, second, *refs):
     out, turned, sems = refs[-3:]
-    width, chunk = first.shape
     pieces = sems.shape[0]
-    wide = chunk // pieces
+    wide = first.shape[1] // pieces
     own = total.at[lax.axis_index("cell")]
     copies = []
     for piece in range(pieces):
         at = slice(piece * wide, (piece + 1) * wide)
-        value = first[:, at].astype(F32) + second[:, at].astype(F32)
-        turned[at] = (own[:, at].astype(F32) + value).T
+        there = slice(skip + piece * wide, skip + (piece + 1) * wide)
+        value = first[:, at].astype(F32) + second[:, there].astype(F32)
+        turned[at] = (own[:, there].astype(F32) + value).T
         copies.append(
             pltpu.make_async_copy(
-                turned.at[at], out.at[pl.ds(start + piece * wide, wide)], sems.at[piece]
+                turned.at[at], out.at[pl.ds(start + skip + piece * wide, wide)], sems.at[piece]
             )
         )
         copies[-1].start()
@@ -495,11 +500,11 @@
         copy.wait()
 
 
-def keep(block, start, token, total, first, second, out):
+def keep(block, start, skip, token, total, first, second, out):
     width, chunk = first.shape
     pieces = max(1, chunk // 256)
     return call(
-        functools.partial(keep_kernel, start),
+        functools.partial(keep_kernel, start, skip),
         "keep", jax.ShapeDtypeStruct((block, width), F32), token,
         total, first, second, *([] if out is None else [out]),
         scratch=[pltpu.VMEM((chunk, width), F32), pltpu.SemaphoreType.DMA((pieces,))],
@@ -562,15 +567,20 @@
     gram, scales, turned, sent_rows = load(bit, gene_factor, counts, tile_mask, tile_counts)
     token = scales
     piece = jax.ShapeDtypeStruct((width, rows // 4), F32)
+    gram_other = swap(gram, "sub", subs, 1)
     low, high, mine, kept_rows = cross(bit, False, scales, sent_rows, turned, counts)
     low, high = [swap(value, "sub", subs, 1) for value in (low, high)]
-    sent = call(plus_pieces_kernel, "plus", piece, token, mine, low, high)
+    token_sent, mine = after(token, mine)
+    gram_half, _ = fold("sub", 1, token_sent, gram, gram_other)
+    token_sent, gram_half = after(token, gram_half)
+    sent = call(plus_pieces_kernel, "plus", piece, token_sent, mine, low, high)
     cross_b = swap(sent, "gene", genes, bit)
-    gram, (scales_late, _) = pair_sums(gram, "gene", genes, (scales, sent))
+    scales_late, _ = after(scales, sent)
     low, high, mine = cross(bit, True, scales_late, kept_rows, turned, counts)
     low, high = [swap(value, "sub", subs, 1) for value in (low, high)]
-    gram_other = swap(gram, "sub", subs, 1)
-    inverse, rho = shifted_inverse(gram, gram_other)
+    gram_half, (mine, _) = pair_sums(gram_half, "gene", genes, (mine, scales))
+    gram = side("sub", 1, 1, token, gram_half, swap(gram_half, "sub", subs, 1))
+    inverse, rho = shifted_inverse(gram)
     token_late, inverse = after(token, inverse)
     cross_a = call(plus_pieces_kernel, "plus", piece, token_late, mine, low, high)
     bit //= 2
@@ -598,6 +608,7 @@
     every = range(len(chunks))
 
     arrived = {}
+    last_part = []
 
     def send(value, phase, parity, index):
         pairs = line.pairs(phase, parity, exchange=phase == 1 and index == 0)
@@ -608,8 +619,15 @@
         if before is None:
             value = seconds[index]
         else:
-            value = operand(line, phase, parity, token, totals[index], before)
-            token, value = after(token, value)
+            chunk = chunks[index]
+            parts = (chunk,)
+            if phase == cells - 1 and parity == 0 and index == every[-1] and chunk >= 1024:
+                parts = (chunk // 4 * 3, chunk // 4)
+            values = operand(line, phase, parity, parts, token, totals[index], before)
+            token, values = after(token, values)
+            value, rest = values[0], values[1:]
+            for part in rest:
+                last_part.append(lax.ppermute(part, "cell", line.pairs(phase, parity)))
         send(value, phase, parity, index)
         return token
 
@@ -668,11 +686,15 @@
     data_products = None
     last = cells - 1
     for index in every:
-        data_products = keep(
-            block, starts[index], token, totals[index],
-            arrived[last, 0, index], arrived[last, 1, index], data_products,
-        )
-        token, data_products = after(token, data_products)
+        parts = [arrived[last, 0, index]] + (last_part if index == every[-1] else [])
+        skip = 0
+        for part in parts:
+            data_products = keep(
+                block, starts[index], skip, token, totals[index],
+                part, arrived[last, 1, index], data_products,
+            )
+            token, data_products = after(token, data_products)
+            skip += part.shape[1]
     return (new_factor, rows_sum, data_products)
 
 

time: 107 us -> 106 us (level)
  waiting for transfers between devices: 38 us -> 33.6 us
  Pallas kernels: 33.1 us -> 34.6 us
  starting transfers between devices: 34.7 us -> 36.2 us
    ppermute x11 -> x12, waiting for transfers between devices: 12 us -> 8.84 us  [swap(): return lax.ppermute(value, axis, [(i, i ^ step) for i in range(size)])]
    ppermute x10, waiting for transfers between devices: 19.2 us -> 17.2 us  [send(): lax.ppermute(value, 'cell', pairs)]
    pallas_call x24 -> x27, Pallas kernels: 16.1 us -> 17.6 us  [call(): pl.pallas_call(lambda token, *refs: kernel(*refs), out_shape=out_shape, i...]
    ppermute x11 -> x12, starting transfers between devices: 7.43 us -> 8.46 us  [swap(): return lax.ppermute(value, axis, [(i, i ^ step) for i in range(size)])]
  transfers between devices with their start and end apart: 24 -> 26, of which waited for: 11 -> 11; matrix products, arithmetic and copies ran while one was open for 0% -> 0% of each run, Pallas kernels for 24% -> 26%
where the time goes in v15:
time: 106 us; the launch traced here: 105 us
  starting transfers between devices  36.2 us (34%)
  Pallas kernels  34.6 us (33%)
  waiting for transfers between devices  33.6 us (32%)
    ppermute x10, starting transfers between devices, send(): lax.ppermute(value, 'cell', pairs)  22.9 us
    pallas_call x27, Pallas kernels, call(): pl.pallas_call(lambda token, *refs: kernel(*refs), out_shape=out_shape, i...  17.6 us
    ppermute x10, waiting for transfers between devices, send(): lax.ppermute(value, 'cell', pairs)  17.2 us
    ppermute x12, waiting for transfers between devices, swap(): return lax.ppermute(value, axis, [(i, i ^ step) for i in range(size)])  8.84 us
    ppermute x12, starting transfers between devices, swap(): return lax.ppermute(value, axis, [(i, i ^ step) for i in range(size)])  8.46 us
    pallas_call x2, Pallas kernels, cross(): pl.pallas_call(functools.partial(cross_kernel, bit, kept, rows), out_shap...  7.74 us
    ppermute x3, waiting for transfers between devices, hop_rows(): rows_arrived = lax.ppermute(rows_sum, 'cell', both)  6.6 us
    pallas_call x1, Pallas kernels, load(): pl.pallas_call(functools.partial(load_kernel, bit), out_shape=(jax.ShapeD...  5.81 us
  transfers between devices with their start and end apart: 26, of which 11 were waited for; matrix products, arithmetic and copies ran while one was open for 0% of the time, Pallas kernels for 26%

profile of v15, /device:TPU:0, one launch (start us, length us, event | category | flops | bytes accessed | tf_op | source)
XLA Modules:
  0.0 105.4 jit_solution(8209943509543528967)
XLA Ops:
  0.6 5.8 %load.1 = (f32[256,256]{1,0:T(8,128)S(1)}, f32[32,8192]{1,0:T(8,128)S(1)}, bf16[8192,256]{1,0:T(8,128)(2,1)S(1)}, bf16[512,8192]{1,0:T(8,128)(2,1)S(1)}) custom-call(bf16[256,8192]{1,0:T(8,128)(2,1)} %genes.1, bf16[1024,8192]{1,0:T(8,128)(2,1)} %refs_0_.1, s32[4,32]{1,0:T(4,128)} %tile_mask.1, s32[4,32]{1,0:T(4,128)} %tile_counts.1), custom_call_target="tpu_custom_call" | custom-call | flops 1 | bytes 1 | tf_op jit(solution)/shard_map/load/pallas_call | solution.py:118
  6.4 0.5 collective-permute-start
  7.0 3.9 %cross_sent.1 = (f32[256,128]{1,0:T(8,128)S(1)}, f32[256,128]{1,0:T(8,128)S(1)}, f32[256,256]{1,0:T(8,128)S(1)}, bf16[512,8192]{1,0:T(8,128)(2,1)S(1)}) custom-call(f32[32,8192]{1,0:T(8,128)S(1)} %get-tuple-element.137.scales.token.refs_0_, bf16[512,8192]{1,0:T(8,128)(2,1)S(1)} %get-tuple-element.73.held_rows.refs_1_, ...), custom_call_target="tpu_custom_call" | custom-call | flops 1 | bytes 1 | tf_op jit(solution)/shard_map/cross_sent/pallas_call | solution.py:206
  10.8 0.1 collective-permute-start.2
  11.0 0.5 collective-permute-start.3
  11.4 0.7 fold.1
  12.1 2.6 %collective-permute-start.1 = (f32[256,128]{1,0:T(8,128)S(1)}, f32[256,128]{1,0:T(8,128)S(1)}, u32[]{:S(2)}, u32[]{:S(2)}) collective-permute-start(f32[256,128]{1,0:T(8,128)S(1)} %get-tuple-element.79), channel_id=1, source_target_pairs={{0,2},{2,0},{1,3},{3,1},{4,6},{6,4},{5,7},{7,5},{8,10},{10,8},{9,1... | collective-permute-start | bytes 393224 | tf_op jit(solution)/shard_map/ppermute | solution.py:540
  14.7 0.0 collective-permute-done.2.refs_1_
  14.7 0.0 collective-permute-done.3.refs_2_
  14.7 0.6 collective-permute-start.7
  15.4 3.9 %cross_kept.1 = (f32[256,128]{1,0:T(8,128)S(1)}, f32[256,128]{1,0:T(8,128)S(1)}, f32[256,256]{1,0:T(8,128)S(1)}) custom-call(f32[32,8192]{1,0:T(8,128)S(1)} %get-tuple-element.137.scales.token.refs_0_, bf16[512,8192]{1,0:T(8,128)(2,1)S(1)} %get-tuple-element.85.held_rows.refs_2_, bf16[8192,256]{1,0:T(8,128)(2,1)S(1)} %get-tuple-element.74.turned), custom_call_target="tpu_custom_call" | custom-call | flops 1 | bytes 1 | tf_op jit(solution)/shard_map/cross_kept/pallas_call | solution.py:206
  19.2 0.0 copy-start
  19.2 0.0 collective-permute-done.1
  19.3 0.1 collective-permute-start.4
  19.4 0.5 collective-permute-start.5
  19.8 0.1 collective-permute-start.6
  19.9 0.8 collective-permute-done.4.refs_1_
  20.7 3.5 %inverse.1 = (f32[256,256]{1,0:T(8,128)S(1)}, f32[8,128]{1,0:T(8,128)S(1)}) custom-call(f32[256,256]{1,0:T(8,128)S(1)} %side.4.gram_in), custom_call_target="tpu_custom_call" | custom-call | flops 1 | bytes 1 | tf_op jit(solution)/shard_map/inverse/pallas_call | solution.py:346
  24.3 0.1 collective-permute-done.7.refs_2_
  24.4 1.0 admm.1.refs_0_
  25.4 1.8 %collective-permute-start.8 = (bf16[256,256]{1,0:T(8,128)(2,1)S(1)}, bf16[256,256]{1,0:T(8,128)(2,1)S(1)}, u32[]{:S(2)}, u32[]{:S(2)}) collective-permute-start(bf16[256,256]{1,0:T(8,128)(2,1)S(1)} %admm.1.refs_0_), channel_id=1, source_target_pairs={{0,2},{2,0},{1,3},{3,1},{4,6},{6,4},{5,7},{7,5},{8,10},{10,8},{9,1... | collective-permute-start | bytes 393224 | tf_op jit(solution)/shard_map/ppermute | solution.py:540
  27.3 3.7 %collective-permute-done.8.refs_1_ = bf16[256,256]{1,0:T(8,128)(2,1)S(1)} collective-permute-done((bf16[256,256]{1,0:T(8,128)(2,1)S(1)}, bf16[256,256]{1,0:T(8,128)(2,1)S(1)}, u32[]{:S(2)}, u32[]{:S(2)}) %collective-permute-start.8) | collective-permute-done | bytes 131104 | tf_op jit(solution)/shard_map/ppermute | solution.py:540
  31.0 0.1 collective-permute-start.9
  31.1 0.2 row_share.1.refs_0_
  31.3 1.9 %collective-permute-start.10 = (bf16[128,256]{1,0:T(8,128)(2,1)S(1)}, bf16[128,256]{1,0:T(8,128)(2,1)S(1)}, u32[]{:S(2)}, u32[]{:S(2)}) collective-permute-start(bf16[128,256]{1,0:T(8,128)(2,1)S(1)} %row_share.1.refs_0_), channel_id=1, source_target_pairs={{0,4},{4,0},{8,12},{12,8},{1,5},{5,1},{9,13},{13,9},{2,6},{6,2},{1... | collective-permute-start | bytes 196616 | tf_op jit(solution)/shard_map/ppermute | solution.py:643
  33.2 1.0 products.4
  34.2 1.3 %collective-permute-start.12 = (bf16[256,1024]{1,0:T(8,128)(2,1)S(1)}, bf16[256,1024]{1,0:T(8,128)(2,1)S(1)}, u32[]{:S(2)}, u32[]{:S(2)}) collective-permute-start(bf16[256,1024]{1,0:T(8,128)(2,1)S(1)} %products.4), channel_id=1, source_target_pairs={{0,4},{4,0},{8,12},{12,8},{1,5},{5,1},{9,13},{13,9},{2,6},{6,2},{1... | collective-permute-start | bytes 1572872 | tf_op jit(solution)/shard_map/ppermute | solution.py:615
  35.5 0.4 collective-permute-done.10.refs_1_
  36.0 1.0 products.5
  36.9 3.7 %collective-permute-start.14 = (bf16[256,1024]{1,0:T(8,128)(2,1)S(1)}, bf16[256,1024]{1,0:T(8,128)(2,1)S(1)}, u32[]{:S(2)}, u32[]{:S(2)}) collective-permute-start(bf16[256,1024]{1,0:T(8,128)(2,1)S(1)} %products.5), channel_id=1, source_target_pairs={{0,4},{12,8},{1,5},{13,9},{2,6},{14,10},{3,7},{15,11},{16,20},{28,... | collective-permute-start | bytes 1572872 | tf_op jit(solution)/shard_map/ppermute | solution.py:615
  40.6 0.7 collective-permute-start.11
  41.3 3.9 %products.6 = (bf16[4,256,1024]{2,1,0:T(8,128)(2,1)S(1)}, bf16[256,1024]{1,0:T(8,128)(2,1)S(1)}) custom-call(f32[32,8192]{1,0:T(8,128)S(1)} %get-tuple-element.137.scales.token.refs_0_, f32[32,8192]{1,0:T(8,128)S(1)} %get-tuple-element.137.scales.token.refs_0_, bf16[512,8192]{1,0:T(8,128)(2,1)S(1)} %get-tuple-element.73.held_rows.refs_1_, ...), custom_call_target="tpu_custom_call" | custom-call | flops 1 | bytes 1 | tf_op jit(solution)/shard_map/products/pallas_call | solution.py:232
  45.3 2.2 %collective-permute-start.13 = (bf16[128,256]{1,0:T(8,128)(2,1)S(1)}, bf16[128,256]{1,0:T(8,128)(2,1)S(1)}, u32[]{:S(2)}, u32[]{:S(2)}) collective-permute-start(bf16[128,256]{1,0:T(8,128)(2,1)S(1)} %hop.4.refs_0_), channel_id=1, source_target_pairs={{0,4},{4,0},{8,12},{12,8},{1,5},{5,1},{9,13},{13,9},{2,6},{6,2},{1... | collective-permute-start | bytes 196616 | tf_op jit(solution)/shard_map/ppermute | solution.py:643
  47.5 1.9 %collective-permute-start.18 = (bf16[256,1024]{1,0:T(8,128)(2,1)S(1)}, bf16[256,1024]{1,0:T(8,128)(2,1)S(1)}, u32[]{:S(2)}, u32[]{:S(2)}) collective-permute-start(bf16[256,1024]{1,0:T(8,128)(2,1)S(1)} %get-tuple-element.123), channel_id=1, source_target_pairs={{0,4},{12,8},{1,5},{13,9},{2,6},{14,10},{3,7},{15,11},{16,20},{28,... | collective-permute-start | bytes 1572872 | tf_op jit(solution)/shard_map/ppermute | solution.py:615
  49.5 0.0 collective-permute-done.12.refs_1_
  49.5 0.1 operand.6
  49.6 0.7 collective-permute-start.16
  50.3 3.9 %products.7 = (bf16[4,256,1024]{2,1,0:T(8,128)(2,1)S(1)}, bf16[256,1024]{1,0:T(8,128)(2,1)S(1)}) custom-call(f32[32,8192]{1,0:T(8,128)S(1)} %get-tuple-element.137.scales.token.refs_0_, f32[32,8192]{1,0:T(8,128)S(1)} %get-tuple-element.137.scales.token.refs_0_, bf16[512,8192]{1,0:T(8,128)(2,1)S(1)} %get-tuple-element.73.held_rows.refs_1_, ...), custom_call_target="tpu_custom_call" | custom-call | flops 1 | bytes 1 | tf_op jit(solution)/shard_map/products/pallas_call | solution.py:232
  54.3 6.2 %collective-permute-done.13.refs_1_ = bf16[128,256]{1,0:T(8,128)(2,1)S(1)} collective-permute-done((bf16[128,256]{1,0:T(8,128)(2,1)S(1)}, bf16[128,256]{1,0:T(8,128)(2,1)S(1)}, u32[]{:S(2)}, u32[]{:S(2)}) %collective-permute-start.13) | collective-permute-done | bytes 65568 | tf_op jit(solution)/shard_map/ppermute | solution.py:643
  60.5 0.1 operand.7
  60.6 0.7 collective-permute-start.19
  61.3 7.5 %collective-permute-start.20 = (bf16[256,1024]{1,0:T(8,128)(2,1)S(1)}, bf16[256,1024]{1,0:T(8,128)(2,1)S(1)}, u32[]{:S(2)}, u32[]{:S(2)}) collective-permute-start(bf16[256,1024]{1,0:T(8,128)(2,1)S(1)} %get-tuple-element.129), channel_id=1, source_target_pairs={{0,4},{12,8},{1,5},{13,9},{2,6},{14,10},{3,7},{15,11},{16,20},{28,... | collective-permute-start | bytes 1572872 | tf_op jit(solution)/shard_map/ppermute | solution.py:615
  68.9 0.1 collective-permute-start.15
  68.9 1.0 turn.1
  69.9 0.2 collective-permute-done.15.refs_1_
  70.2 1.6 %collective-permute-start.17 = (f32[128,256]{1,0:T(8,128)S(1)}, f32[128,256]{1,0:T(8,128)S(1)}, u32[]{:S(2)}, u32[]{:S(2)}) collective-permute-start(f32[128,256]{1,0:T(8,128)S(1)} %plus.5.refs_0_), channel_id=1, source_target_pairs={{0,2},{2,0},{1,3},{3,1},{4,6},{6,4},{5,7},{7,5},{8,10},{10,8},{9,1... | collective-permute-start | bytes 393224 | tf_op jit(solution)/shard_map/ppermute | solution.py:540
  71.8 0.1 operand.8
  71.9 4.0 %collective-permute-done.17.refs_1_ = f32[128,256]{1,0:T(8,128)S(1)} collective-permute-done((f32[128,256]{1,0:T(8,128)S(1)}, f32[128,256]{1,0:T(8,128)S(1)}, u32[]{:S(2)}, u32[]{:S(2)}) %collective-permute-start.17) | collective-permute-done | bytes 131104 | tf_op jit(solution)/shard_map/ppermute | solution.py:540
  75.9 0.7 side.7
  76.6 0.0 collective-permute-start.21
  76.6 0.1 operand.9
  76.8 0.1 operand.10
  76.9 0.7 collective-permute-start.22
  77.6 5.3 %collective-permute-done.20.refs_1_ = bf16[256,1024]{1,0:T(8,128)(2,1)S(1)} collective-permute-done((bf16[256,1024]{1,0:T(8,128)(2,1)S(1)}, bf16[256,1024]{1,0:T(8,128)(2,1)S(1)}, u32[]{:S(2)}, u32[]{:S(2)}) %collective-permute-start.20) | collective-permute-done | bytes 524320 | tf_op jit(solution)/shard_map/ppermute | solution.py:615
  82.9 0.1 operand.11
  83.0 0.7 collective-permute-start.24
  83.7 5.7 %collective-permute-start.23 = (bf16[256,768]{1,0:T(8,128)(2,1)S(1)}, bf16[256,768]{1,0:T(8,128)(2,1)S(1)}, u32[]{:S(2)}, u32[]{:S(2)}) collective-permute-start(bf16[256,768]{1,0:T(8,128)(2,1)S(1)} %get-tuple-element.134), channel_id=1, source_target_pairs={{0,4},{8,12},{4,0},{12,8},{1,5},{9,13},{5,1},{13,9},{2,6},{10,14},... | collective-permute-start | bytes 1179656 | tf_op jit(solution)/shard_map/ppermute | solution.py:615
  89.4 0.1 collective-permute-start.25
  89.5 4.6 %collective-permute-done.21.refs_1_ = bf16[256,1024]{1,0:T(8,128)(2,1)S(1)} collective-permute-done((bf16[256,1024]{1,0:T(8,128)(2,1)S(1)}, bf16[256,1024]{1,0:T(8,128)(2,1)S(1)}, u32[]{:S(2)}, u32[]{:S(2)}) %collective-permute-start.21) | collective-permute-done | bytes 524320 | tf_op jit(solution)/shard_map/ppermute | solution.py:615
  94.1 1.1 %keep.3.refs_3_ = f32[2048,256]{1,0:T(8,128)} custom-call(f32[32,8192]{1,0:T(8,128)S(1)} %get-tuple-element.137.scales.token.refs_0_, bf16[4,256,1024]{2,1,0:T(8,128)(2,1)S(1)} %get-tuple-element.104.refs_0_, bf16[256,1024]{1,0:T(8,128)(2,1)S(1)} %collective-permute-done.21.refs_1_, bf16[256,1024]{1,0:T(8,128)(2,1)S(1)} %collective-permute-done.22.refs_2_), custom_call_target="tpu_custom_call" | custom-call | flops 1 | bytes 1 | tf_op jit(solution)/shard_map/keep/pallas_call | solution.py:232
  95.3 7.3 %collective-permute-done.23.refs_1_ = bf16[256,768]{1,0:T(8,128)(2,1)S(1)} collective-permute-done((bf16[256,768]{1,0:T(8,128)(2,1)S(1)}, bf16[256,768]{1,0:T(8,128)(2,1)S(1)}, u32[]{:S(2)}, u32[]{:S(2)}) %collective-permute-start.23) | collective-permute-done | bytes 393248 | tf_op jit(solution)/shard_map/ppermute | solution.py:615
  102.6 1.0 keep.4.refs_3_
  103.6 1.0 collective-permute-done.25.refs_1_
  104.6 0.9 keep.5
  (22 shorter events, 0.3 us)
Async XLA Ops:
  6.4 5.0 %collective-permute-start = (f32[256,256]{1,0:T(8,128)S(1)}, f32[256,256]{1,0:T(8,128)S(1)}, u32[]{:S(2)}, u32[]{:S(2)}) collective-permute-start(f32[256,256]{1,0:T(8,128)S(1)} %get-tuple-element.77.refs_0_), channel_id=1, source_target_pairs={{0,1},{1,0},{2,3},{3,2},{4,5},{5,4},{6,7},{7,6},{8,9},{9,8},{10,11... | collective-permute-start | bytes 786440 | tf_op jit(solution)/shard_map/ppermute | solution.py:540
  10.8 3.8 %collective-permute-start.2 = (f32[256,128]{1,0:T(8,128)S(1)}, f32[256,128]{1,0:T(8,128)S(1)}, u32[]{:S(2)}, u32[]{:S(2)}) collective-permute-start(f32[256,128]{1,0:T(8,128)S(1)} %get-tuple-element.82), channel_id=1, source_target_pairs={{0,1},{1,0},{2,3},{3,2},{4,5},{5,4},{6,7},{7,6},{8,9},{9,8},{10,11... | collective-permute-start | bytes 393224 | tf_op jit(solution)/shard_map/ppermute | solution.py:540
  11.0 3.7 %collective-permute-start.3 = (f32[256,128]{1,0:T(8,128)S(1)}, f32[256,128]{1,0:T(8,128)S(1)}, u32[]{:S(2)}, u32[]{:S(2)}) collective-permute-start(f32[256,128]{1,0:T(8,128)S(1)} %get-tuple-element.83), channel_id=1, source_target_pairs={{0,1},{1,0},{2,3},{3,2},{4,5},{5,4},{6,7},{7,6},{8,9},{9,8},{10,11... | collective-permute-start | bytes 393224 | tf_op jit(solution)/shard_map/ppermute | solution.py:540
  12.1 7.1 %collective-permute-start.1 = (f32[256,128]{1,0:T(8,128)S(1)}, f32[256,128]{1,0:T(8,128)S(1)}, u32[]{:S(2)}, u32[]{:S(2)}) collective-permute-start(f32[256,128]{1,0:T(8,128)S(1)} %get-tuple-element.79), channel_id=1, source_target_pairs={{0,2},{2,0},{1,3},{3,1},{4,6},{6,4},{5,7},{7,5},{8,10},{10,8},{9,1... | collective-permute-start | bytes 393224 | tf_op jit(solution)/shard_map/ppermute | solution.py:540
  14.7 9.7 %collective-permute-start.7 = (f32[256,256]{1,0:T(8,128)S(1)}, f32[256,256]{1,0:T(8,128)S(1)}, u32[]{:S(2)}, u32[]{:S(2)}) collective-permute-start(f32[256,256]{1,0:T(8,128)S(1)} %plus.3), channel_id=1, source_target_pairs={{0,2},{2,0},{1,3},{3,1},{4,6},{6,4},{5,7},{7,5},{8,10},{10,8},{9,1... | collective-permute-start | bytes 786440 | tf_op jit(solution)/shard_map/ppermute | solution.py:540
  19.2 5.2 %copy-start = (bf16[1024,256]{1,0:T(8,128)(2,1)S(1)}, bf16[1024,256]{1,0:T(8,128)(2,1)}, u32[]{:S(2)}) copy-start(bf16[1024,256]{1,0:T(8,128)(2,1)} %refs_4_.1) | copy-start | bytes 1572868
  19.3 1.4 %collective-permute-start.4 = (f32[256,128]{1,0:T(8,128)S(1)}, f32[256,128]{1,0:T(8,128)S(1)}, u32[]{:S(2)}, u32[]{:S(2)}) collective-permute-start(f32[256,128]{1,0:T(8,128)S(1)} %add.3.refs_0_), channel_id=1, source_target_pairs={{0,1},{1,0},{2,3},{3,2},{4,5},{5,4},{6,7},{7,6},{8,9},{9,8},{10,11... | collective-permute-start | bytes 393224 | tf_op jit(solution)/shard_map/ppermute | solution.py:540
  19.4 4.9 %collective-permute-start.5 = (f32[256,128]{1,0:T(8,128)S(1)}, f32[256,128]{1,0:T(8,128)S(1)}, u32[]{:S(2)}, u32[]{:S(2)}) collective-permute-start(f32[256,128]{1,0:T(8,128)S(1)} %get-tuple-element.92), channel_id=1, source_target_pairs={{0,1},{1,0},{2,3},{3,2},{4,5},{5,4},{6,7},{7,6},{8,9},{9,8},{10,11... | collective-permute-start | bytes 393224 | tf_op jit(solution)/shard_map/ppermute | solution.py:540
  19.8 4.4 %collective-permute-start.6 = (f32[256,128]{1,0:T(8,128)S(1)}, f32[256,128]{1,0:T(8,128)S(1)}, u32[]{:S(2)}, u32[]{:S(2)}) collective-permute-start(f32[256,128]{1,0:T(8,128)S(1)} %get-tuple-element.93), channel_id=1, source_target_pairs={{0,1},{1,0},{2,3},{3,2},{4,5},{5,4},{6,7},{7,6},{8,9},{9,8},{10,11... | collective-permute-start | bytes 393224 | tf_op jit(solution)/shard_map/ppermute | solution.py:540
  25.4 5.5 %collective-permute-start.8 = (bf16[256,256]{1,0:T(8,128)(2,1)S(1)}, bf16[256,256]{1,0:T(8,128)(2,1)S(1)}, u32[]{:S(2)}, u32[]{:S(2)}) collective-permute-start(bf16[256,256]{1,0:T(8,128)(2,1)S(1)} %admm.1.refs_0_), channel_id=1, source_target_pairs={{0,2},{2,0},{1,3},{3,1},{4,6},{6,4},{5,7},{7,5},{8,10},{10,8},{9,1... | collective-permute-start | bytes 393224 | tf_op jit(solution)/shard_map/ppermute | solution.py:540
  31.0 2.2 %collective-permute-start.9 = (bf16[256,512]{1,0:T(8,128)(2,1)S(1)}, bf16[256,512]{1,0:T(8,128)(2,1)S(1)}, u32[]{:S(2)}, u32[]{:S(2)}) collective-permute-start(bf16[256,512]{1,0:T(8,128)(2,1)S(1)} %side.5.refs_0_), channel_id=1, source_target_pairs={{0,1},{1,0},{2,3},{3,2},{4,5},{5,4},{6,7},{7,6},{8,9},{9,8},{10,11... | collective-permute-start | bytes 786440 | tf_op jit(solution)/shard_map/ppermute | solution.py:540
  31.3 4.6 %collective-permute-start.10 = (bf16[128,256]{1,0:T(8,128)(2,1)S(1)}, bf16[128,256]{1,0:T(8,128)(2,1)S(1)}, u32[]{:S(2)}, u32[]{:S(2)}) collective-permute-start(bf16[128,256]{1,0:T(8,128)(2,1)S(1)} %row_share.1.refs_0_), channel_id=1, source_target_pairs={{0,4},{4,0},{8,12},{12,8},{1,5},{5,1},{9,13},{13,9},{2,6},{6,2},{1... | collective-permute-start | bytes 196616 | tf_op jit(solution)/shard_map/ppermute | solution.py:643
  34.2 15.3 %collective-permute-start.12 = (bf16[256,1024]{1,0:T(8,128)(2,1)S(1)}, bf16[256,1024]{1,0:T(8,128)(2,1)S(1)}, u32[]{:S(2)}, u32[]{:S(2)}) collective-permute-start(bf16[256,1024]{1,0:T(8,128)(2,1)S(1)} %products.4), channel_id=1, source_target_pairs={{0,4},{4,0},{8,12},{12,8},{1,5},{5,1},{9,13},{13,9},{2,6},{6,2},{1... | collective-permute-start | bytes 1572872 | tf_op jit(solution)/shard_map/ppermute | solution.py:615
  36.9 23.5 %collective-permute-start.14 = (bf16[256,1024]{1,0:T(8,128)(2,1)S(1)}, bf16[256,1024]{1,0:T(8,128)(2,1)S(1)}, u32[]{:S(2)}, u32[]{:S(2)}) collective-permute-start(bf16[256,1024]{1,0:T(8,128)(2,1)S(1)} %products.5), channel_id=1, source_target_pairs={{0,4},{12,8},{1,5},{13,9},{2,6},{14,10},{3,7},{15,11},{16,20},{28,... | collective-permute-start | bytes 1572872 | tf_op jit(solution)/shard_map/ppermute | solution.py:615
  40.6 4.6 %collective-permute-start.11 = (bf16[128,256]{1,0:T(8,128)(2,1)S(1)}, bf16[128,256]{1,0:T(8,128)(2,1)S(1)}, u32[]{:S(2)}, u32[]{:S(2)}) collective-permute-start(bf16[128,256]{1,0:T(8,128)(2,1)S(1)} %hop.3.refs_0_), channel_id=1, source_target_pairs={{4,8},{8,4},{5,9},{9,5},{6,10},{10,6},{7,11},{11,7},{20,24},{24,20... | collective-permute-start | bytes 196616 | tf_op jit(solution)/shard_map/ppermute | solution.py:643
  45.3 15.2 %collective-permute-start.13 = (bf16[128,256]{1,0:T(8,128)(2,1)S(1)}, bf16[128,256]{1,0:T(8,128)(2,1)S(1)}, u32[]{:S(2)}, u32[]{:S(2)}) collective-permute-start(bf16[128,256]{1,0:T(8,128)(2,1)S(1)} %hop.4.refs_0_), channel_id=1, source_target_pairs={{0,4},{4,0},{8,12},{12,8},{1,5},{5,1},{9,13},{13,9},{2,6},{6,2},{1... | collective-permute-start | bytes 196616 | tf_op jit(solution)/shard_map/ppermute | solution.py:643
  47.5 29.1 %collective-permute-start.18 = (bf16[256,1024]{1,0:T(8,128)(2,1)S(1)}, bf16[256,1024]{1,0:T(8,128)(2,1)S(1)}, u32[]{:S(2)}, u32[]{:S(2)}) collective-permute-start(bf16[256,1024]{1,0:T(8,128)(2,1)S(1)} %get-tuple-element.123), channel_id=1, source_target_pairs={{0,4},{12,8},{1,5},{13,9},{2,6},{14,10},{3,7},{15,11},{16,20},{28,... | collective-permute-start | bytes 1572872 | tf_op jit(solution)/shard_map/ppermute | solution.py:615
  49.6 22.1 %collective-permute-start.16 = (bf16[256,1024]{1,0:T(8,128)(2,1)S(1)}, bf16[256,1024]{1,0:T(8,128)(2,1)S(1)}, u32[]{:S(2)}, u32[]{:S(2)}) collective-permute-start(bf16[256,1024]{1,0:T(8,128)(2,1)S(1)} %operand.6), channel_id=1, source_target_pairs={{4,8},{8,4},{5,9},{9,5},{6,10},{10,6},{7,11},{11,7},{20,24},{24,20... | collective-permute-start | bytes 1572872 | tf_op jit(solution)/shard_map/ppermute | solution.py:615
  60.6 16.2 %collective-permute-start.19 = (bf16[256,1024]{1,0:T(8,128)(2,1)S(1)}, bf16[256,1024]{1,0:T(8,128)(2,1)S(1)}, u32[]{:S(2)}, u32[]{:S(2)}) collective-permute-start(bf16[256,1024]{1,0:T(8,128)(2,1)S(1)} %operand.7), channel_id=1, source_target_pairs={{4,8},{8,4},{5,9},{9,5},{6,10},{10,6},{7,11},{11,7},{20,24},{24,20... | collective-permute-start | bytes 1572872 | tf_op jit(solution)/shard_map/ppermute | solution.py:615
  61.3 21.6 %collective-permute-start.20 = (bf16[256,1024]{1,0:T(8,128)(2,1)S(1)}, bf16[256,1024]{1,0:T(8,128)(2,1)S(1)}, u32[]{:S(2)}, u32[]{:S(2)}) collective-permute-start(bf16[256,1024]{1,0:T(8,128)(2,1)S(1)} %get-tuple-element.129), channel_id=1, source_target_pairs={{0,4},{12,8},{1,5},{13,9},{2,6},{14,10},{3,7},{15,11},{16,20},{28,... | collective-permute-start | bytes 1572872 | tf_op jit(solution)/shard_map/ppermute | solution.py:615
  68.9 1.3 %collective-permute-start.15 = (bf16[128,256]{1,0:T(8,128)(2,1)S(1)}, bf16[128,256]{1,0:T(8,128)(2,1)S(1)}, u32[]{:S(2)}, u32[]{:S(2)}) collective-permute-start(bf16[128,256]{1,0:T(8,128)(2,1)S(1)} %hop.5.refs_0_), channel_id=1, source_target_pairs={{0,1},{1,0},{2,3},{3,2},{4,5},{5,4},{6,7},{7,6},{8,9},{9,8},{10,11... | collective-permute-start | bytes 196616 | tf_op jit(solution)/shard_map/ppermute | solution.py:540
  70.2 5.7 %collective-permute-start.17 = (f32[128,256]{1,0:T(8,128)S(1)}, f32[128,256]{1,0:T(8,128)S(1)}, u32[]{:S(2)}, u32[]{:S(2)}) collective-permute-start(f32[128,256]{1,0:T(8,128)S(1)} %plus.5.refs_0_), channel_id=1, source_target_pairs={{0,2},{2,0},{1,3},{3,1},{4,6},{6,4},{5,7},{7,5},{8,10},{10,8},{9,1... | collective-permute-start | bytes 393224 | tf_op jit(solution)/shard_map/ppermute | solution.py:540
  76.6 17.5 %collective-permute-start.21 = (bf16[256,1024]{1,0:T(8,128)(2,1)S(1)}, bf16[256,1024]{1,0:T(8,128)(2,1)S(1)}, u32[]{:S(2)}, u32[]{:S(2)}) collective-permute-start(bf16[256,1024]{1,0:T(8,128)(2,1)S(1)} %operand.8), channel_id=1, source_target_pairs={{0,4},{8,12},{4,0},{12,8},{1,5},{9,13},{5,1},{13,9},{2,6},{10,14},... | collective-permute-start | bytes 1572872 | tf_op jit(solution)/shard_map/ppermute | solution.py:615
  76.9 17.2 %collective-permute-start.22 = (bf16[256,1024]{1,0:T(8,128)(2,1)S(1)}, bf16[256,1024]{1,0:T(8,128)(2,1)S(1)}, u32[]{:S(2)}, u32[]{:S(2)}) collective-permute-start(bf16[256,1024]{1,0:T(8,128)(2,1)S(1)} %operand.9), channel_id=1, source_target_pairs={{4,8},{8,4},{5,9},{9,5},{6,10},{10,6},{7,11},{11,7},{20,24},{24,20... | collective-permute-start | bytes 1572872 | tf_op jit(solution)/shard_map/ppermute | solution.py:615
  83.0 19.5 %collective-permute-start.24 = (bf16[256,1024]{1,0:T(8,128)(2,1)S(1)}, bf16[256,1024]{1,0:T(8,128)(2,1)S(1)}, u32[]{:S(2)}, u32[]{:S(2)}) collective-permute-start(bf16[256,1024]{1,0:T(8,128)(2,1)S(1)} %operand.11), channel_id=1, source_target_pairs={{4,8},{8,4},{5,9},{9,5},{6,10},{10,6},{7,11},{11,7},{20,24},{24,20... | collective-permute-start | bytes 1572872 | tf_op jit(solution)/shard_map/ppermute | solution.py:615
  83.7 18.8 %collective-permute-start.23 = (bf16[256,768]{1,0:T(8,128)(2,1)S(1)}, bf16[256,768]{1,0:T(8,128)(2,1)S(1)}, u32[]{:S(2)}, u32[]{:S(2)}) collective-permute-start(bf16[256,768]{1,0:T(8,128)(2,1)S(1)} %get-tuple-element.134), channel_id=1, source_target_pairs={{0,4},{8,12},{4,0},{12,8},{1,5},{9,13},{5,1},{13,9},{2,6},{10,14},... | collective-permute-start | bytes 1179656 | tf_op jit(solution)/shard_map/ppermute | solution.py:615
  89.4 15.2 %collective-permute-start.25 = (bf16[256,256]{1,0:T(8,128)(2,1)S(1)}, bf16[256,256]{1,0:T(8,128)(2,1)S(1)}, u32[]{:S(2)}, u32[]{:S(2)}) collective-permute-start(bf16[256,256]{1,0:T(8,128)(2,1)S(1)} %get-tuple-element.138), channel_id=1, source_target_pairs={{0,4},{8,12},{4,0},{12,8},{1,5},{9,13},{5,1},{13,9},{2,6},{10,14},... | collective-permute-start | bytes 393224 | tf_op jit(solution)/shard_map/ppermute | solution.py:630

commit v16 on v15

--- a/solution.py
+++ b/solution.py
@@ -257,6 +257,19 @@
         sent[...] = left[:, half:] + right[:, half:]
 
 
+def half_sum_kernel(axis, left, right, out):
+    half = out.shape[1]
+    upper = lax.axis_index(axis) != 0
+
+    @pl.when(upper)
+    def _():
+        out[...] = left[:, half:] + right[:, half:]
+
+    @pl.when(jnp.logical_not(upper))
+    def _():
+        out[...] = left[:, :half] + right[:, :half]
+
+
 def fold(axis, bit, token, left, right):
     shape = jax.ShapeDtypeStruct((left.shape[0], left.shape[1] // 2), F32)
     return call(
@@ -571,7 +584,10 @@
     low, high, mine, kept_rows = cross(bit, False, scales, sent_rows, turned, counts)
     low, high = [swap(value, "sub", subs, 1) for value in (low, high)]
     token_sent, mine = after(token, mine)
-    gram_half, _ = fold("sub", 1, token_sent, gram, gram_other)
+    half = jax.ShapeDtypeStruct((width, width // 2), F32)
+    gram_half = call(
+        functools.partial(half_sum_kernel, "sub"), "half_sum", half, token_sent, gram, gram_other
+    )
     token_sent, gram_half = after(token, gram_half)
     sent = call(plus_pieces_kernel, "plus", piece, token_sent, mine, low, high)
     cross_b = swap(sent, "gene", genes, bit)

time: 106 us -> 105 us (level)
  transfers between devices with their start and end apart: 26 -> 26, of which waited for: 11 -> 10; matrix products, arithmetic and copies ran while one was open for 0% -> 0% of each run, Pallas kernels for 26% -> 25%
where the time goes in v16:
time: 105 us
  starting transfers between devices  35.7 us (34%)
  waiting for transfers between devices  34.6 us (33%)
  Pallas kernels  33.9 us (32%)
    ppermute x10, starting transfers between devices, send(): lax.ppermute(value, 'cell', pairs)  22.8 us
    ppermute x10, waiting for transfers between devices, send(): lax.ppermute(value, 'cell', pairs)  17.1 us
    pallas_call x27, Pallas kernels, call(): pl.pallas_call(lambda token, *refs: kernel(*refs), out_shape=out_shape, i...  16.9 us
    ppermute x12, waiting for transfers between devices, swap(): return lax.ppermute(value, axis, [(i, i ^ step) for i in range(size)])  9.71 us
    ppermute x12, starting transfers between devices, swap(): return lax.ppermute(value, axis, [(i, i ^ step) for i in range(size)])  8.24 us
    pallas_call x2, Pallas kernels, cross(): pl.pallas_call(functools.partial(cross_kernel, bit, kept, rows), out_shap...  7.74 us
    ppermute x3, waiting for transfers between devices, hop_rows(): rows_arrived = lax.ppermute(rows_sum, 'cell', both)  6.76 us
    pallas_call x1, Pallas kernels, load(): pl.pallas_call(functools.partial(load_kernel, bit), out_shape=(jax.ShapeD...  5.81 us
  transfers between devices with their start and end apart: 26, of which 10 were waited for; matrix products, arithmetic and copies ran while one was open for 0% of the time, Pallas kernels for 25%

profile of v16, /device:TPU:0, one launch (start us, length us, event | category | flops | bytes accessed | tf_op | source)
XLA Modules:
  0.0 105.2 jit_solution(5460059019227571464)
XLA Ops:
  0.6 5.8 %load.1 = (f32[256,256]{1,0:T(8,128)S(1)}, f32[32,8192]{1,0:T(8,128)S(1)}, bf16[8192,256]{1,0:T(8,128)(2,1)S(1)}, bf16[512,8192]{1,0:T(8,128)(2,1)S(1)}) custom-call(bf16[256,8192]{1,0:T(8,128)(2,1)} %genes.1, bf16[1024,8192]{1,0:T(8,128)(2,1)} %refs_0_.1, s32[4,32]{1,0:T(4,128)} %tile_mask.1, s32[4,32]{1,0:T(4,128)} %tile_counts.1), custom_call_target="tpu_custom_call" | custom-call | flops 1 | bytes 1 | tf_op jit(solution)/shard_map/load/pallas_call | solution.py:118
  6.4 0.5 collective-permute-start
  7.0 3.9 %cross_sent.1 = (f32[256,128]{1,0:T(8,128)S(1)}, f32[256,128]{1,0:T(8,128)S(1)}, f32[256,256]{1,0:T(8,128)S(1)}, bf16[512,8192]{1,0:T(8,128)(2,1)S(1)}) custom-call(f32[32,8192]{1,0:T(8,128)S(1)} %get-tuple-element.135.scales.token.refs_0_, bf16[512,8192]{1,0:T(8,128)(2,1)S(1)} %get-tuple-element.72.held_rows.refs_1_, ...), custom_call_target="tpu_custom_call" | custom-call | flops 1 | bytes 1 | tf_op jit(solution)/shard_map/cross_sent/pallas_call | solution.py:206
  10.8 0.1 collective-permute-start.2
  11.0 0.5 collective-permute-start.3
  11.4 0.0 collective-permute-done.refs_1_
  11.5 2.6 %collective-permute-start.1 = (f32[256,128]{1,0:T(8,128)S(1)}, f32[256,128]{1,0:T(8,128)S(1)}, u32[]{:S(2)}, u32[]{:S(2)}) collective-permute-start(f32[256,128]{1,0:T(8,128)S(1)} %half_sum.1), channel_id=1, source_target_pairs={{0,2},{2,0},{1,3},{3,1},{4,6},{6,4},{5,7},{7,5},{8,10},{10,8},{9,1... | collective-permute-start | bytes 393224 | tf_op jit(solution)/shard_map/ppermute | solution.py:553
  14.1 0.0 collective-permute-done.3.refs_2_
  14.1 1.2 %collective-permute-start.7 = (f32[256,256]{1,0:T(8,128)S(1)}, f32[256,256]{1,0:T(8,128)S(1)}, u32[]{:S(2)}, u32[]{:S(2)}) collective-permute-start(f32[256,256]{1,0:T(8,128)S(1)} %plus.3), channel_id=1, source_target_pairs={{0,2},{2,0},{1,3},{3,1},{4,6},{6,4},{5,7},{7,5},{8,10},{10,8},{9,1... | collective-permute-start | bytes 786440 | tf_op jit(solution)/shard_map/ppermute | solution.py:553
  15.4 3.9 %cross_kept.1 = (f32[256,128]{1,0:T(8,128)S(1)}, f32[256,128]{1,0:T(8,128)S(1)}, f32[256,256]{1,0:T(8,128)S(1)}) custom-call(f32[32,8192]{1,0:T(8,128)S(1)} %get-tuple-element.135.scales.token.refs_0_, bf16[512,8192]{1,0:T(8,128)(2,1)S(1)} %get-tuple-element.83.held_rows.refs_2_, bf16[8192,256]{1,0:T(8,128)(2,1)S(1)} %get-tuple-element.73.turned), custom_call_target="tpu_custom_call" | custom-call | flops 1 | bytes 1 | tf_op jit(solution)/shard_map/cross_kept/pallas_call | solution.py:206
  19.2 0.0 copy-start
  19.2 0.0 collective-permute-done.1
  19.3 0.1 collective-permute-start.4
  19.4 0.5 collective-permute-start.5
  19.8 0.1 collective-permute-start.6
  19.9 0.8 collective-permute-done.4.refs_1_
  20.7 3.5 %inverse.1 = (f32[256,256]{1,0:T(8,128)S(1)}, f32[8,128]{1,0:T(8,128)S(1)}) custom-call(f32[256,256]{1,0:T(8,128)S(1)} %side.4.gram_in), custom_call_target="tpu_custom_call" | custom-call | flops 1 | bytes 1 | tf_op jit(solution)/shard_map/inverse/pallas_call | solution.py:359
  24.2 0.0 collective-permute-done.5.refs_1_
  24.3 1.0 admm.1.refs_0_
  25.4 1.3 %collective-permute-start.8 = (bf16[256,256]{1,0:T(8,128)(2,1)S(1)}, bf16[256,256]{1,0:T(8,128)(2,1)S(1)}, u32[]{:S(2)}, u32[]{:S(2)}) collective-permute-start(bf16[256,256]{1,0:T(8,128)(2,1)S(1)} %admm.1.refs_0_), channel_id=1, source_target_pairs={{0,2},{2,0},{1,3},{3,1},{4,6},{6,4},{5,7},{7,5},{8,10},{10,8},{9,1... | collective-permute-start | bytes 393224 | tf_op jit(solution)/shard_map/ppermute | solution.py:553
  26.7 4.3 %collective-permute-done.8.refs_1_ = bf16[256,256]{1,0:T(8,128)(2,1)S(1)} collective-permute-done((bf16[256,256]{1,0:T(8,128)(2,1)S(1)}, bf16[256,256]{1,0:T(8,128)(2,1)S(1)}, u32[]{:S(2)}, u32[]{:S(2)}) %collective-permute-start.8) | collective-permute-done | bytes 131104 | tf_op jit(solution)/shard_map/ppermute | solution.py:553
  31.0 0.1 collective-permute-start.9
  31.1 0.2 row_share.1.refs_0_
  31.3 1.6 %collective-permute-start.10 = (bf16[128,256]{1,0:T(8,128)(2,1)S(1)}, bf16[128,256]{1,0:T(8,128)(2,1)S(1)}, u32[]{:S(2)}, u32[]{:S(2)}) collective-permute-start(bf16[128,256]{1,0:T(8,128)(2,1)S(1)} %row_share.1.refs_0_), channel_id=1, source_target_pairs={{0,4},{4,0},{8,12},{12,8},{1,5},{5,1},{9,13},{13,9},{2,6},{6,2},{1... | collective-permute-start | bytes 196616 | tf_op jit(solution)/shard_map/ppermute | solution.py:659
  32.9 0.0 collective-permute-done.9.refs_1_
  33.0 1.0 products.4
  34.0 1.3 %collective-permute-start.12 = (bf16[256,1024]{1,0:T(8,128)(2,1)S(1)}, bf16[256,1024]{1,0:T(8,128)(2,1)S(1)}, u32[]{:S(2)}, u32[]{:S(2)}) collective-permute-start(bf16[256,1024]{1,0:T(8,128)(2,1)S(1)} %products.4), channel_id=1, source_target_pairs={{0,4},{4,0},{8,12},{12,8},{1,5},{5,1},{9,13},{13,9},{2,6},{6,2},{1... | collective-permute-start | bytes 1572872 | tf_op jit(solution)/shard_map/ppermute | solution.py:631
  35.3 0.6 collective-permute-done.10.refs_1_
  35.9 1.0 products.5
  36.9 3.5 %collective-permute-start.14 = (bf16[256,1024]{1,0:T(8,128)(2,1)S(1)}, bf16[256,1024]{1,0:T(8,128)(2,1)S(1)}, u32[]{:S(2)}, u32[]{:S(2)}) collective-permute-start(bf16[256,1024]{1,0:T(8,128)(2,1)S(1)} %products.5), channel_id=1, source_target_pairs={{0,4},{12,8},{1,5},{13,9},{2,6},{14,10},{3,7},{15,11},{16,20},{28,... | collective-permute-start | bytes 1572872 | tf_op jit(solution)/shard_map/ppermute | solution.py:631
  40.4 0.7 collective-permute-start.11
  41.0 3.9 %products.6 = (bf16[4,256,1024]{2,1,0:T(8,128)(2,1)S(1)}, bf16[256,1024]{1,0:T(8,128)(2,1)S(1)}) custom-call(f32[32,8192]{1,0:T(8,128)S(1)} %get-tuple-element.135.scales.token.refs_0_, f32[32,8192]{1,0:T(8,128)S(1)} %get-tuple-element.135.scales.token.refs_0_, bf16[512,8192]{1,0:T(8,128)(2,1)S(1)} %get-tuple-element.72.held_rows.refs_1_, ...), custom_call_target="tpu_custom_call" | custom-call | flops 1 | bytes 1 | tf_op jit(solution)/shard_map/products/pallas_call | solution.py:232
  45.0 0.0 collective-permute-done.11.refs_1_
  45.0 2.2 %collective-permute-start.13 = (bf16[128,256]{1,0:T(8,128)(2,1)S(1)}, bf16[128,256]{1,0:T(8,128)(2,1)S(1)}, u32[]{:S(2)}, u32[]{:S(2)}) collective-permute-start(bf16[128,256]{1,0:T(8,128)(2,1)S(1)} %hop.4.refs_0_), channel_id=1, source_target_pairs={{0,4},{4,0},{8,12},{12,8},{1,5},{5,1},{9,13},{13,9},{2,6},{6,2},{1... | collective-permute-start | bytes 196616 | tf_op jit(solution)/shard_map/ppermute | solution.py:659
  47.3 1.9 %collective-permute-start.18 = (bf16[256,1024]{1,0:T(8,128)(2,1)S(1)}, bf16[256,1024]{1,0:T(8,128)(2,1)S(1)}, u32[]{:S(2)}, u32[]{:S(2)}) collective-permute-start(bf16[256,1024]{1,0:T(8,128)(2,1)S(1)} %get-tuple-element.121), channel_id=1, source_target_pairs={{0,4},{12,8},{1,5},{13,9},{2,6},{14,10},{3,7},{15,11},{16,20},{28,... | collective-permute-start | bytes 1572872 | tf_op jit(solution)/shard_map/ppermute | solution.py:631
  49.2 0.1 operand.6
  49.4 0.7 collective-permute-start.16
  50.1 3.9 %products.7 = (bf16[4,256,1024]{2,1,0:T(8,128)(2,1)S(1)}, bf16[256,1024]{1,0:T(8,128)(2,1)S(1)}) custom-call(f32[32,8192]{1,0:T(8,128)S(1)} %get-tuple-element.135.scales.token.refs_0_, f32[32,8192]{1,0:T(8,128)S(1)} %get-tuple-element.135.scales.token.refs_0_, bf16[512,8192]{1,0:T(8,128)(2,1)S(1)} %get-tuple-element.72.held_rows.refs_1_, ...), custom_call_target="tpu_custom_call" | custom-call | flops 1 | bytes 1 | tf_op jit(solution)/shard_map/products/pallas_call | solution.py:232
  54.0 6.2 %collective-permute-done.13.refs_1_ = bf16[128,256]{1,0:T(8,128)(2,1)S(1)} collective-permute-done((bf16[128,256]{1,0:T(8,128)(2,1)S(1)}, bf16[128,256]{1,0:T(8,128)(2,1)S(1)}, u32[]{:S(2)}, u32[]{:S(2)}) %collective-permute-start.13) | collective-permute-done | bytes 65568 | tf_op jit(solution)/shard_map/ppermute | solution.py:659
  60.2 0.0 collective-permute-done.14.refs_1_
  60.2 0.1 operand.7
  60.4 0.7 collective-permute-start.19
  61.1 7.6 %collective-permute-start.20 = (bf16[256,1024]{1,0:T(8,128)(2,1)S(1)}, bf16[256,1024]{1,0:T(8,128)(2,1)S(1)}, u32[]{:S(2)}, u32[]{:S(2)}) collective-permute-start(bf16[256,1024]{1,0:T(8,128)(2,1)S(1)} %get-tuple-element.127), channel_id=1, source_target_pairs={{0,4},{12,8},{1,5},{13,9},{2,6},{14,10},{3,7},{15,11},{16,20},{28,... | collective-permute-start | bytes 1572872 | tf_op jit(solution)/shard_map/ppermute | solution.py:631
  68.6 0.1 collective-permute-start.15
  68.7 1.0 turn.1
  69.7 0.2 collective-permute-done.15.refs_1_
  70.0 1.2 %collective-permute-start.17 = (f32[128,256]{1,0:T(8,128)S(1)}, f32[128,256]{1,0:T(8,128)S(1)}, u32[]{:S(2)}, u32[]{:S(2)}) collective-permute-start(f32[128,256]{1,0:T(8,128)S(1)} %plus.5.refs_0_), channel_id=1, source_target_pairs={{0,2},{2,0},{1,3},{3,1},{4,6},{6,4},{5,7},{7,5},{8,10},{10,8},{9,1... | collective-permute-start | bytes 393224 | tf_op jit(solution)/shard_map/ppermute | solution.py:553
  71.2 0.1 operand.8
  71.3 4.4 %collective-permute-done.17.refs_1_ = f32[128,256]{1,0:T(8,128)S(1)} collective-permute-done((f32[128,256]{1,0:T(8,128)S(1)}, f32[128,256]{1,0:T(8,128)S(1)}, u32[]{:S(2)}, u32[]{:S(2)}) %collective-permute-start.17) | collective-permute-done | bytes 131104 | tf_op jit(solution)/shard_map/ppermute | solution.py:553
  75.7 0.7 side.7
  76.4 0.1 operand.9
  76.6 0.1 operand.10
  76.7 0.7 collective-permute-start.22
  77.4 5.2 %collective-permute-done.20.refs_1_ = bf16[256,1024]{1,0:T(8,128)(2,1)S(1)} collective-permute-done((bf16[256,1024]{1,0:T(8,128)(2,1)S(1)}, bf16[256,1024]{1,0:T(8,128)(2,1)S(1)}, u32[]{:S(2)}, u32[]{:S(2)}) %collective-permute-start.20) | collective-permute-done | bytes 524320 | tf_op jit(solution)/shard_map/ppermute | solution.py:631
  82.7 0.1 operand.11
  82.8 0.7 collective-permute-start.24
  83.5 5.7 %collective-permute-start.23 = (bf16[256,768]{1,0:T(8,128)(2,1)S(1)}, bf16[256,768]{1,0:T(8,128)(2,1)S(1)}, u32[]{:S(2)}, u32[]{:S(2)}) collective-permute-start(bf16[256,768]{1,0:T(8,128)(2,1)S(1)} %get-tuple-element.132), channel_id=1, source_target_pairs={{0,4},{8,12},{4,0},{12,8},{1,5},{9,13},{5,1},{13,9},{2,6},{10,14},... | collective-permute-start | bytes 1179656 | tf_op jit(solution)/shard_map/ppermute | solution.py:631
  89.2 0.1 collective-permute-start.25
  89.3 4.6 %collective-permute-done.21.refs_1_ = bf16[256,1024]{1,0:T(8,128)(2,1)S(1)} collective-permute-done((bf16[256,1024]{1,0:T(8,128)(2,1)S(1)}, bf16[256,1024]{1,0:T(8,128)(2,1)S(1)}, u32[]{:S(2)}, u32[]{:S(2)}) %collective-permute-start.21) | collective-permute-done | bytes 524320 | tf_op jit(solution)/shard_map/ppermute | solution.py:631
  93.9 1.1 %keep.3.refs_3_ = f32[2048,256]{1,0:T(8,128)} custom-call(f32[32,8192]{1,0:T(8,128)S(1)} %get-tuple-element.135.scales.token.refs_0_, bf16[4,256,1024]{2,1,0:T(8,128)(2,1)S(1)} %get-tuple-element.102.refs_0_, bf16[256,1024]{1,0:T(8,128)(2,1)S(1)} %collective-permute-done.21.refs_1_, bf16[256,1024]{1,0:T(8,128)(2,1)S(1)} %collective-permute-done.22.refs_2_), custom_call_target="tpu_custom_call" | custom-call | flops 1 | bytes 1 | tf_op jit(solution)/shard_map/keep/pallas_call | solution.py:232
  95.0 7.3 %collective-permute-done.23.refs_1_ = bf16[256,768]{1,0:T(8,128)(2,1)S(1)} collective-permute-done((bf16[256,768]{1,0:T(8,128)(2,1)S(1)}, bf16[256,768]{1,0:T(8,128)(2,1)S(1)}, u32[]{:S(2)}, u32[]{:S(2)}) %collective-permute-start.23) | collective-permute-done | bytes 393248 | tf_op jit(solution)/shard_map/ppermute | solution.py:631
  102.3 1.0 keep.4.refs_3_
  103.4 1.0 collective-permute-done.25.refs_1_
  104.3 0.9 keep.5
  (22 shorter events, 0.3 us)
Async XLA Ops:
  6.4 5.0 %collective-permute-start = (f32[256,256]{1,0:T(8,128)S(1)}, f32[256,256]{1,0:T(8,128)S(1)}, u32[]{:S(2)}, u32[]{:S(2)}) collective-permute-start(f32[256,256]{1,0:T(8,128)S(1)} %get-tuple-element.76.refs_0_), channel_id=1, source_target_pairs={{0,1},{1,0},{2,3},{3,2},{4,5},{5,4},{6,7},{7,6},{8,9},{9,8},{10,11... | collective-permute-start | bytes 786440 | tf_op jit(solution)/shard_map/ppermute | solution.py:553
  10.8 3.2 %collective-permute-start.2 = (f32[256,128]{1,0:T(8,128)S(1)}, f32[256,128]{1,0:T(8,128)S(1)}, u32[]{:S(2)}, u32[]{:S(2)}) collective-permute-start(f32[256,128]{1,0:T(8,128)S(1)} %get-tuple-element.80), channel_id=1, source_target_pairs={{0,1},{1,0},{2,3},{3,2},{4,5},{5,4},{6,7},{7,6},{8,9},{9,8},{10,11... | collective-permute-start | bytes 393224 | tf_op jit(solution)/shard_map/ppermute | solution.py:553
  11.0 3.1 %collective-permute-start.3 = (f32[256,128]{1,0:T(8,128)S(1)}, f32[256,128]{1,0:T(8,128)S(1)}, u32[]{:S(2)}, u32[]{:S(2)}) collective-permute-start(f32[256,128]{1,0:T(8,128)S(1)} %get-tuple-element.81), channel_id=1, source_target_pairs={{0,1},{1,0},{2,3},{3,2},{4,5},{5,4},{6,7},{7,6},{8,9},{9,8},{10,11... | collective-permute-start | bytes 393224 | tf_op jit(solution)/shard_map/ppermute | solution.py:553
  11.5 7.8 %collective-permute-start.1 = (f32[256,128]{1,0:T(8,128)S(1)}, f32[256,128]{1,0:T(8,128)S(1)}, u32[]{:S(2)}, u32[]{:S(2)}) collective-permute-start(f32[256,128]{1,0:T(8,128)S(1)} %half_sum.1), channel_id=1, source_target_pairs={{0,2},{2,0},{1,3},{3,1},{4,6},{6,4},{5,7},{7,5},{8,10},{10,8},{9,1... | collective-permute-start | bytes 393224 | tf_op jit(solution)/shard_map/ppermute | solution.py:553
  14.1 10.2 %collective-permute-start.7 = (f32[256,256]{1,0:T(8,128)S(1)}, f32[256,256]{1,0:T(8,128)S(1)}, u32[]{:S(2)}, u32[]{:S(2)}) collective-permute-start(f32[256,256]{1,0:T(8,128)S(1)} %plus.3), channel_id=1, source_target_pairs={{0,2},{2,0},{1,3},{3,1},{4,6},{6,4},{5,7},{7,5},{8,10},{10,8},{9,1... | collective-permute-start | bytes 786440 | tf_op jit(solution)/shard_map/ppermute | solution.py:553
  19.2 5.1 %copy-start = (bf16[1024,256]{1,0:T(8,128)(2,1)S(1)}, bf16[1024,256]{1,0:T(8,128)(2,1)}, u32[]{:S(2)}) copy-start(bf16[1024,256]{1,0:T(8,128)(2,1)} %refs_4_.1) | copy-start | bytes 1572868
  19.3 1.4 %collective-permute-start.4 = (f32[256,128]{1,0:T(8,128)S(1)}, f32[256,128]{1,0:T(8,128)S(1)}, u32[]{:S(2)}, u32[]{:S(2)}) collective-permute-start(f32[256,128]{1,0:T(8,128)S(1)} %add.3.refs_0_), channel_id=1, source_target_pairs={{0,1},{1,0},{2,3},{3,2},{4,5},{5,4},{6,7},{7,6},{8,9},{9,8},{10,11... | collective-permute-start | bytes 393224 | tf_op jit(solution)/shard_map/ppermute | solution.py:553
  19.4 4.9 %collective-permute-start.5 = (f32[256,128]{1,0:T(8,128)S(1)}, f32[256,128]{1,0:T(8,128)S(1)}, u32[]{:S(2)}, u32[]{:S(2)}) collective-permute-start(f32[256,128]{1,0:T(8,128)S(1)} %get-tuple-element.90), channel_id=1, source_target_pairs={{0,1},{1,0},{2,3},{3,2},{4,5},{5,4},{6,7},{7,6},{8,9},{9,8},{10,11... | collective-permute-start | bytes 393224 | tf_op jit(solution)/shard_map/ppermute | solution.py:553
  19.8 4.4 %collective-permute-start.6 = (f32[256,128]{1,0:T(8,128)S(1)}, f32[256,128]{1,0:T(8,128)S(1)}, u32[]{:S(2)}, u32[]{:S(2)}) collective-permute-start(f32[256,128]{1,0:T(8,128)S(1)} %get-tuple-element.91), channel_id=1, source_target_pairs={{0,1},{1,0},{2,3},{3,2},{4,5},{5,4},{6,7},{7,6},{8,9},{9,8},{10,11... | collective-permute-start | bytes 393224 | tf_op jit(solution)/shard_map/ppermute | solution.py:553
  25.4 5.6 %collective-permute-start.8 = (bf16[256,256]{1,0:T(8,128)(2,1)S(1)}, bf16[256,256]{1,0:T(8,128)(2,1)S(1)}, u32[]{:S(2)}, u32[]{:S(2)}) collective-permute-start(bf16[256,256]{1,0:T(8,128)(2,1)S(1)} %admm.1.refs_0_), channel_id=1, source_target_pairs={{0,2},{2,0},{1,3},{3,1},{4,6},{6,4},{5,7},{7,5},{8,10},{10,8},{9,1... | collective-permute-start | bytes 393224 | tf_op jit(solution)/shard_map/ppermute | solution.py:553
  31.0 2.0 %collective-permute-start.9 = (bf16[256,512]{1,0:T(8,128)(2,1)S(1)}, bf16[256,512]{1,0:T(8,128)(2,1)S(1)}, u32[]{:S(2)}, u32[]{:S(2)}) collective-permute-start(bf16[256,512]{1,0:T(8,128)(2,1)S(1)} %side.5.refs_0_), channel_id=1, source_target_pairs={{0,1},{1,0},{2,3},{3,2},{4,5},{5,4},{6,7},{7,6},{8,9},{9,8},{10,11... | collective-permute-start | bytes 786440 | tf_op jit(solution)/shard_map/ppermute | solution.py:553
  31.3 4.6 %collective-permute-start.10 = (bf16[128,256]{1,0:T(8,128)(2,1)S(1)}, bf16[128,256]{1,0:T(8,128)(2,1)S(1)}, u32[]{:S(2)}, u32[]{:S(2)}) collective-permute-start(bf16[128,256]{1,0:T(8,128)(2,1)S(1)} %row_share.1.refs_0_), channel_id=1, source_target_pairs={{0,4},{4,0},{8,12},{12,8},{1,5},{5,1},{9,13},{13,9},{2,6},{6,2},{1... | collective-permute-start | bytes 196616 | tf_op jit(solution)/shard_map/ppermute | solution.py:659
  34.0 15.3 %collective-permute-start.12 = (bf16[256,1024]{1,0:T(8,128)(2,1)S(1)}, bf16[256,1024]{1,0:T(8,128)(2,1)S(1)}, u32[]{:S(2)}, u32[]{:S(2)}) collective-permute-start(bf16[256,1024]{1,0:T(8,128)(2,1)S(1)} %products.4), channel_id=1, source_target_pairs={{0,4},{4,0},{8,12},{12,8},{1,5},{5,1},{9,13},{13,9},{2,6},{6,2},{1... | collective-permute-start | bytes 1572872 | tf_op jit(solution)/shard_map/ppermute | solution.py:631
  36.9 23.4 %collective-permute-start.14 = (bf16[256,1024]{1,0:T(8,128)(2,1)S(1)}, bf16[256,1024]{1,0:T(8,128)(2,1)S(1)}, u32[]{:S(2)}, u32[]{:S(2)}) collective-permute-start(bf16[256,1024]{1,0:T(8,128)(2,1)S(1)} %products.5), channel_id=1, source_target_pairs={{0,4},{12,8},{1,5},{13,9},{2,6},{14,10},{3,7},{15,11},{16,20},{28,... | collective-permute-start | bytes 1572872 | tf_op jit(solution)/shard_map/ppermute | solution.py:631
  40.4 4.6 %collective-permute-start.11 = (bf16[128,256]{1,0:T(8,128)(2,1)S(1)}, bf16[128,256]{1,0:T(8,128)(2,1)S(1)}, u32[]{:S(2)}, u32[]{:S(2)}) collective-permute-start(bf16[128,256]{1,0:T(8,128)(2,1)S(1)} %hop.3.refs_0_), channel_id=1, source_target_pairs={{4,8},{8,4},{5,9},{9,5},{6,10},{10,6},{7,11},{11,7},{20,24},{24,20... | collective-permute-start | bytes 196616 | tf_op jit(solution)/shard_map/ppermute | solution.py:659
  45.0 15.2 %collective-permute-start.13 = (bf16[128,256]{1,0:T(8,128)(2,1)S(1)}, bf16[128,256]{1,0:T(8,128)(2,1)S(1)}, u32[]{:S(2)}, u32[]{:S(2)}) collective-permute-start(bf16[128,256]{1,0:T(8,128)(2,1)S(1)} %hop.4.refs_0_), channel_id=1, source_target_pairs={{0,4},{4,0},{8,12},{12,8},{1,5},{5,1},{9,13},{13,9},{2,6},{6,2},{1... | collective-permute-start | bytes 196616 | tf_op jit(solution)/shard_map/ppermute | solution.py:659
  47.3 29.2 %collective-permute-start.18 = (bf16[256,1024]{1,0:T(8,128)(2,1)S(1)}, bf16[256,1024]{1,0:T(8,128)(2,1)S(1)}, u32[]{:S(2)}, u32[]{:S(2)}) collective-permute-start(bf16[256,1024]{1,0:T(8,128)(2,1)S(1)} %get-tuple-element.121), channel_id=1, source_target_pairs={{0,4},{12,8},{1,5},{13,9},{2,6},{14,10},{3,7},{15,11},{16,20},{28,... | collective-permute-start | bytes 1572872 | tf_op jit(solution)/shard_map/ppermute | solution.py:631
  49.4 21.8 %collective-permute-start.16 = (bf16[256,1024]{1,0:T(8,128)(2,1)S(1)}, bf16[256,1024]{1,0:T(8,128)(2,1)S(1)}, u32[]{:S(2)}, u32[]{:S(2)}) collective-permute-start(bf16[256,1024]{1,0:T(8,128)(2,1)S(1)} %operand.6), channel_id=1, source_target_pairs={{4,8},{8,4},{5,9},{9,5},{6,10},{10,6},{7,11},{11,7},{20,24},{24,20... | collective-permute-start | bytes 1572872 | tf_op jit(solution)/shard_map/ppermute | solution.py:631
  60.4 16.2 %collective-permute-start.19 = (bf16[256,1024]{1,0:T(8,128)(2,1)S(1)}, bf16[256,1024]{1,0:T(8,128)(2,1)S(1)}, u32[]{:S(2)}, u32[]{:S(2)}) collective-permute-start(bf16[256,1024]{1,0:T(8,128)(2,1)S(1)} %operand.7), channel_id=1, source_target_pairs={{4,8},{8,4},{5,9},{9,5},{6,10},{10,6},{7,11},{11,7},{20,24},{24,20... | collective-permute-start | bytes 1572872 | tf_op jit(solution)/shard_map/ppermute | solution.py:631
  61.1 21.6 %collective-permute-start.20 = (bf16[256,1024]{1,0:T(8,128)(2,1)S(1)}, bf16[256,1024]{1,0:T(8,128)(2,1)S(1)}, u32[]{:S(2)}, u32[]{:S(2)}) collective-permute-start(bf16[256,1024]{1,0:T(8,128)(2,1)S(1)} %get-tuple-element.127), channel_id=1, source_target_pairs={{0,4},{12,8},{1,5},{13,9},{2,6},{14,10},{3,7},{15,11},{16,20},{28,... | collective-permute-start | bytes 1572872 | tf_op jit(solution)/shard_map/ppermute | solution.py:631
  68.6 1.3 %collective-permute-start.15 = (bf16[128,256]{1,0:T(8,128)(2,1)S(1)}, bf16[128,256]{1,0:T(8,128)(2,1)S(1)}, u32[]{:S(2)}, u32[]{:S(2)}) collective-permute-start(bf16[128,256]{1,0:T(8,128)(2,1)S(1)} %hop.5.refs_0_), channel_id=1, source_target_pairs={{0,1},{1,0},{2,3},{3,2},{4,5},{5,4},{6,7},{7,6},{8,9},{9,8},{10,11... | collective-permute-start | bytes 196616 | tf_op jit(solution)/shard_map/ppermute | solution.py:553
  70.0 5.7 %collective-permute-start.17 = (f32[128,256]{1,0:T(8,128)S(1)}, f32[128,256]{1,0:T(8,128)S(1)}, u32[]{:S(2)}, u32[]{:S(2)}) collective-permute-start(f32[128,256]{1,0:T(8,128)S(1)} %plus.5.refs_0_), channel_id=1, source_target_pairs={{0,2},{2,0},{1,3},{3,1},{4,6},{6,4},{5,7},{7,5},{8,10},{10,8},{9,1... | collective-permute-start | bytes 393224 | tf_op jit(solution)/shard_map/ppermute | solution.py:553
  76.4 17.5 %collective-permute-start.21 = (bf16[256,1024]{1,0:T(8,128)(2,1)S(1)}, bf16[256,1024]{1,0:T(8,128)(2,1)S(1)}, u32[]{:S(2)}, u32[]{:S(2)}) collective-permute-start(bf16[256,1024]{1,0:T(8,128)(2,1)S(1)} %operand.8), channel_id=1, source_target_pairs={{0,4},{8,12},{4,0},{12,8},{1,5},{9,13},{5,1},{13,9},{2,6},{10,14},... | collective-permute-start | bytes 1572872 | tf_op jit(solution)/shard_map/ppermute | solution.py:631
  76.7 17.2 %collective-permute-start.22 = (bf16[256,1024]{1,0:T(8,128)(2,1)S(1)}, bf16[256,1024]{1,0:T(8,128)(2,1)S(1)}, u32[]{:S(2)}, u32[]{:S(2)}) collective-permute-start(bf16[256,1024]{1,0:T(8,128)(2,1)S(1)} %operand.9), channel_id=1, source_target_pairs={{4,8},{8,4},{5,9},{9,5},{6,10},{10,6},{7,11},{11,7},{20,24},{24,20... | collective-permute-start | bytes 1572872 | tf_op jit(solution)/shard_map/ppermute | solution.py:631
  82.8 19.5 %collective-permute-start.24 = (bf16[256,1024]{1,0:T(8,128)(2,1)S(1)}, bf16[256,1024]{1,0:T(8,128)(2,1)S(1)}, u32[]{:S(2)}, u32[]{:S(2)}) collective-permute-start(bf16[256,1024]{1,0:T(8,128)(2,1)S(1)} %operand.11), channel_id=1, source_target_pairs={{4,8},{8,4},{5,9},{9,5},{6,10},{10,6},{7,11},{11,7},{20,24},{24,20... | collective-permute-start | bytes 1572872 | tf_op jit(solution)/shard_map/ppermute | solution.py:631
  83.5 18.8 %collective-permute-start.23 = (bf16[256,768]{1,0:T(8,128)(2,1)S(1)}, bf16[256,768]{1,0:T(8,128)(2,1)S(1)}, u32[]{:S(2)}, u32[]{:S(2)}) collective-permute-start(bf16[256,768]{1,0:T(8,128)(2,1)S(1)} %get-tuple-element.132), channel_id=1, source_target_pairs={{0,4},{8,12},{4,0},{12,8},{1,5},{9,13},{5,1},{13,9},{2,6},{10,14},... | collective-permute-start | bytes 1179656 | tf_op jit(solution)/shard_map/ppermute | solution.py:631
  89.2 15.1 %collective-permute-start.25 = (bf16[256,256]{1,0:T(8,128)(2,1)S(1)}, bf16[256,256]{1,0:T(8,128)(2,1)S(1)}, u32[]{:S(2)}, u32[]{:S(2)}) collective-permute-start(bf16[256,256]{1,0:T(8,128)(2,1)S(1)} %get-tuple-element.136), channel_id=1, source_target_pairs={{0,4},{8,12},{4,0},{12,8},{1,5},{9,13},{5,1},{13,9},{2,6},{10,14},... | collective-permute-start | bytes 393224 | tf_op jit(solution)/shard_map/ppermute | solution.py:646

commit v17 on v16

--- a/solution.py
+++ b/solution.py
@@ -155,7 +155,7 @@
 
 def cross_rows(row_tiles, scales, counts, turned, total):
     columns = counts.shape[1]
-    wide = min(1024, columns)
+    wide = min(2048, columns)
     total[...] = jnp.zeros_like(total)
 
     @pl.loop(0, columns // wide)

time: 105 us -> 105 us (level)
  starting transfers between devices: 35.7 us -> 36.9 us
  Pallas kernels: 33.9 us -> 32.8 us
    pallas_call x2, Pallas kernels: 7.74 us -> 6.65 us  [cross(): pl.pallas_call(functools.partial(cross_kernel, bit, kept, rows), out_shap...]
  transfers between devices with their start and end apart: 26 -> 26, of which waited for: 10 -> 11; matrix products, arithmetic and copies ran while one was open for 0% -> 0% of each run, Pallas kernels for 25% -> 24%
where the time goes in v17:
time: 105 us; the launch traced here: 104 us
  starting transfers between devices  36.9 us (35%)
  waiting for transfers between devices  33.7 us (32%)
  Pallas kernels  32.8 us (31%)
    ppermute x10, starting transfers between devices, send(): lax.ppermute(value, 'cell', pairs)  22.9 us
    ppermute x10, waiting for transfers between devices, send(): lax.ppermute(value, 'cell', pairs)  17.2 us
    pallas_call x27, Pallas kernels, call(): pl.pallas_call(lambda token, *refs: kernel(*refs), out_shape=out_shape, i...  16.9 us
    ppermute x12, starting transfers between devices, swap(): return lax.ppermute(value, axis, [(i, i ^ step) for i in range(size)])  9.12 us
    ppermute x12, waiting for transfers between devices, swap(): return lax.ppermute(value, axis, [(i, i ^ step) for i in range(size)])  8.97 us
    pallas_call x2, Pallas kernels, cross(): pl.pallas_call(functools.partial(cross_kernel, bit, kept, rows), out_shap...  6.65 us
    ppermute x3, waiting for transfers between devices, hop_rows(): rows_arrived = lax.ppermute(rows_sum, 'cell', both)  6.6 us
    pallas_call x1, Pallas kernels, load(): pl.pallas_call(functools.partial(load_kernel, bit), out_shape=(jax.ShapeD...  5.81 us
  transfers between devices with their start and end apart: 26, of which 11 were waited for; matrix products, arithmetic and copies ran while one was open for 0% of the time, Pallas kernels for 24%

profile of v17, /device:TPU:0, one launch (start us, length us, event | category | flops | bytes accessed | tf_op | source)
XLA Modules:
  0.0 104.5 jit_solution(14057877628641207773)
XLA Ops:
  0.6 5.8 %load.1 = (f32[256,256]{1,0:T(8,128)S(1)}, f32[32,8192]{1,0:T(8,128)S(1)}, bf16[8192,256]{1,0:T(8,128)(2,1)S(1)}, bf16[512,8192]{1,0:T(8,128)(2,1)S(1)}) custom-call(bf16[256,8192]{1,0:T(8,128)(2,1)} %genes.1, bf16[1024,8192]{1,0:T(8,128)(2,1)} %refs_0_.1, s32[4,32]{1,0:T(4,128)} %tile_mask.1, s32[4,32]{1,0:T(4,128)} %tile_counts.1), custom_call_target="tpu_custom_call" | custom-call | flops 1 | bytes 1 | tf_op jit(solution)/shard_map/load/pallas_call | solution.py:118
  6.4 0.5 collective-permute-start
  7.0 3.5 %cross_sent.1 = (f32[256,128]{1,0:T(8,128)S(1)}, f32[256,128]{1,0:T(8,128)S(1)}, f32[256,256]{1,0:T(8,128)S(1)}, bf16[512,8192]{1,0:T(8,128)(2,1)S(1)}) custom-call(f32[32,8192]{1,0:T(8,128)S(1)} %get-tuple-element.135.scales.token.refs_0_, bf16[512,8192]{1,0:T(8,128)(2,1)S(1)} %get-tuple-element.72.held_rows.refs_1_, ...), custom_call_target="tpu_custom_call" | custom-call | flops 1 | bytes 1 | tf_op jit(solution)/shard_map/cross_sent/pallas_call | solution.py:206
  10.5 0.1 collective-permute-start.2
  10.6 0.5 collective-permute-start.3
  11.1 2.6 %collective-permute-start.1 = (f32[256,128]{1,0:T(8,128)S(1)}, f32[256,128]{1,0:T(8,128)S(1)}, u32[]{:S(2)}, u32[]{:S(2)}) collective-permute-start(f32[256,128]{1,0:T(8,128)S(1)} %half_sum.1), channel_id=1, source_target_pairs={{0,2},{2,0},{1,3},{3,1},{4,6},{6,4},{5,7},{7,5},{8,10},{10,8},{9,1... | collective-permute-start | bytes 393224 | tf_op jit(solution)/shard_map/ppermute | solution.py:553
  13.7 0.0 collective-permute-done.3.refs_2_
  13.7 1.2 %collective-permute-start.7 = (f32[256,256]{1,0:T(8,128)S(1)}, f32[256,256]{1,0:T(8,128)S(1)}, u32[]{:S(2)}, u32[]{:S(2)}) collective-permute-start(f32[256,256]{1,0:T(8,128)S(1)} %plus.3), channel_id=1, source_target_pairs={{0,2},{2,0},{1,3},{3,1},{4,6},{6,4},{5,7},{7,5},{8,10},{10,8},{9,1... | collective-permute-start | bytes 786440 | tf_op jit(solution)/shard_map/ppermute | solution.py:553
  15.0 3.2 %cross_kept.1 = (f32[256,128]{1,0:T(8,128)S(1)}, f32[256,128]{1,0:T(8,128)S(1)}, f32[256,256]{1,0:T(8,128)S(1)}) custom-call(f32[32,8192]{1,0:T(8,128)S(1)} %get-tuple-element.135.scales.token.refs_0_, bf16[512,8192]{1,0:T(8,128)(2,1)S(1)} %get-tuple-element.83.held_rows.refs_2_, bf16[8192,256]{1,0:T(8,128)(2,1)S(1)} %get-tuple-element.73.turned), custom_call_target="tpu_custom_call" | custom-call | flops 1 | bytes 1 | tf_op jit(solution)/shard_map/cross_kept/pallas_call | solution.py:206
  18.1 0.0 copy-start
  18.1 0.0 collective-permute-done.1
  18.2 0.1 collective-permute-start.4
  18.3 0.5 collective-permute-start.5
  18.8 0.1 collective-permute-start.6
  18.8 0.8 collective-permute-done.4.refs_1_
  19.6 3.5 %inverse.1 = (f32[256,256]{1,0:T(8,128)S(1)}, f32[8,128]{1,0:T(8,128)S(1)}) custom-call(f32[256,256]{1,0:T(8,128)S(1)} %side.4.gram_in), custom_call_target="tpu_custom_call" | custom-call | flops 1 | bytes 1 | tf_op jit(solution)/shard_map/inverse/pallas_call | solution.py:359
  23.1 0.0 collective-permute-done.6.refs_2_
  23.2 0.2 collective-permute-done.7.refs_2_
  23.4 1.0 admm.1.refs_0_
  24.5 1.8 %collective-permute-start.8 = (bf16[256,256]{1,0:T(8,128)(2,1)S(1)}, bf16[256,256]{1,0:T(8,128)(2,1)S(1)}, u32[]{:S(2)}, u32[]{:S(2)}) collective-permute-start(bf16[256,256]{1,0:T(8,128)(2,1)S(1)} %admm.1.refs_0_), channel_id=1, source_target_pairs={{0,2},{2,0},{1,3},{3,1},{4,6},{6,4},{5,7},{7,5},{8,10},{10,8},{9,1... | collective-permute-start | bytes 393224 | tf_op jit(solution)/shard_map/ppermute | solution.py:553
  26.3 3.7 %collective-permute-done.8.refs_1_ = bf16[256,256]{1,0:T(8,128)(2,1)S(1)} collective-permute-done((bf16[256,256]{1,0:T(8,128)(2,1)S(1)}, bf16[256,256]{1,0:T(8,128)(2,1)S(1)}, u32[]{:S(2)}, u32[]{:S(2)}) %collective-permute-start.8) | collective-permute-done | bytes 131104 | tf_op jit(solution)/shard_map/ppermute | solution.py:553
  30.0 0.1 collective-permute-start.9
  30.1 0.2 row_share.1.refs_0_
  30.3 1.9 %collective-permute-start.10 = (bf16[128,256]{1,0:T(8,128)(2,1)S(1)}, bf16[128,256]{1,0:T(8,128)(2,1)S(1)}, u32[]{:S(2)}, u32[]{:S(2)}) collective-permute-start(bf16[128,256]{1,0:T(8,128)(2,1)S(1)} %row_share.1.refs_0_), channel_id=1, source_target_pairs={{0,4},{4,0},{8,12},{12,8},{1,5},{5,1},{9,13},{13,9},{2,6},{6,2},{1... | collective-permute-start | bytes 196616 | tf_op jit(solution)/shard_map/ppermute | solution.py:659
  32.3 1.0 products.4
  33.2 1.3 %collective-permute-start.12 = (bf16[256,1024]{1,0:T(8,128)(2,1)S(1)}, bf16[256,1024]{1,0:T(8,128)(2,1)S(1)}, u32[]{:S(2)}, u32[]{:S(2)}) collective-permute-start(bf16[256,1024]{1,0:T(8,128)(2,1)S(1)} %products.4), channel_id=1, source_target_pairs={{0,4},{4,0},{8,12},{12,8},{1,5},{5,1},{9,13},{13,9},{2,6},{6,2},{1... | collective-permute-start | bytes 1572872 | tf_op jit(solution)/shard_map/ppermute | solution.py:631
  34.5 0.4 collective-permute-done.10.refs_1_
  35.0 1.0 products.5
  36.0 3.7 %collective-permute-start.14 = (bf16[256,1024]{1,0:T(8,128)(2,1)S(1)}, bf16[256,1024]{1,0:T(8,128)(2,1)S(1)}, u32[]{:S(2)}, u32[]{:S(2)}) collective-permute-start(bf16[256,1024]{1,0:T(8,128)(2,1)S(1)} %products.5), channel_id=1, source_target_pairs={{0,4},{12,8},{1,5},{13,9},{2,6},{14,10},{3,7},{15,11},{16,20},{28,... | collective-permute-start | bytes 1572872 | tf_op jit(solution)/shard_map/ppermute | solution.py:631
  39.6 0.7 collective-permute-start.11
  40.3 3.9 %products.6 = (bf16[4,256,1024]{2,1,0:T(8,128)(2,1)S(1)}, bf16[256,1024]{1,0:T(8,128)(2,1)S(1)}) custom-call(f32[32,8192]{1,0:T(8,128)S(1)} %get-tuple-element.135.scales.token.refs_0_, f32[32,8192]{1,0:T(8,128)S(1)} %get-tuple-element.135.scales.token.refs_0_, bf16[512,8192]{1,0:T(8,128)(2,1)S(1)} %get-tuple-element.72.held_rows.refs_1_, ...), custom_call_target="tpu_custom_call" | custom-call | flops 1 | bytes 1 | tf_op jit(solution)/shard_map/products/pallas_call | solution.py:232
  44.3 2.2 %collective-permute-start.13 = (bf16[128,256]{1,0:T(8,128)(2,1)S(1)}, bf16[128,256]{1,0:T(8,128)(2,1)S(1)}, u32[]{:S(2)}, u32[]{:S(2)}) collective-permute-start(bf16[128,256]{1,0:T(8,128)(2,1)S(1)} %hop.4.refs_0_), channel_id=1, source_target_pairs={{0,4},{4,0},{8,12},{12,8},{1,5},{5,1},{9,13},{13,9},{2,6},{6,2},{1... | collective-permute-start | bytes 196616 | tf_op jit(solution)/shard_map/ppermute | solution.py:659
  46.5 1.9 %collective-permute-start.18 = (bf16[256,1024]{1,0:T(8,128)(2,1)S(1)}, bf16[256,1024]{1,0:T(8,128)(2,1)S(1)}, u32[]{:S(2)}, u32[]{:S(2)}) collective-permute-start(bf16[256,1024]{1,0:T(8,128)(2,1)S(1)} %get-tuple-element.121), channel_id=1, source_target_pairs={{0,4},{12,8},{1,5},{13,9},{2,6},{14,10},{3,7},{15,11},{16,20},{28,... | collective-permute-start | bytes 1572872 | tf_op jit(solution)/shard_map/ppermute | solution.py:631
  48.5 0.0 collective-permute-done.12.refs_1_
  48.5 0.1 operand.6
  48.6 0.7 collective-permute-start.16
  49.3 3.9 %products.7 = (bf16[4,256,1024]{2,1,0:T(8,128)(2,1)S(1)}, bf16[256,1024]{1,0:T(8,128)(2,1)S(1)}) custom-call(f32[32,8192]{1,0:T(8,128)S(1)} %get-tuple-element.135.scales.token.refs_0_, f32[32,8192]{1,0:T(8,128)S(1)} %get-tuple-element.135.scales.token.refs_0_, bf16[512,8192]{1,0:T(8,128)(2,1)S(1)} %get-tuple-element.72.held_rows.refs_1_, ...), custom_call_target="tpu_custom_call" | custom-call | flops 1 | bytes 1 | tf_op jit(solution)/shard_map/products/pallas_call | solution.py:232
  53.3 6.2 %collective-permute-done.13.refs_1_ = bf16[128,256]{1,0:T(8,128)(2,1)S(1)} collective-permute-done((bf16[128,256]{1,0:T(8,128)(2,1)S(1)}, bf16[128,256]{1,0:T(8,128)(2,1)S(1)}, u32[]{:S(2)}, u32[]{:S(2)}) %collective-permute-start.13) | collective-permute-done | bytes 65568 | tf_op jit(solution)/shard_map/ppermute | solution.py:659
  59.5 0.1 operand.7
  59.6 0.7 collective-permute-start.19
  60.3 7.5 %collective-permute-start.20 = (bf16[256,1024]{1,0:T(8,128)(2,1)S(1)}, bf16[256,1024]{1,0:T(8,128)(2,1)S(1)}, u32[]{:S(2)}, u32[]{:S(2)}) collective-permute-start(bf16[256,1024]{1,0:T(8,128)(2,1)S(1)} %get-tuple-element.127), channel_id=1, source_target_pairs={{0,4},{12,8},{1,5},{13,9},{2,6},{14,10},{3,7},{15,11},{16,20},{28,... | collective-permute-start | bytes 1572872 | tf_op jit(solution)/shard_map/ppermute | solution.py:631
  67.9 0.1 collective-permute-start.15
  68.0 1.0 turn.1
  69.0 0.2 collective-permute-done.15.refs_1_
  69.2 1.6 %collective-permute-start.17 = (f32[128,256]{1,0:T(8,128)S(1)}, f32[128,256]{1,0:T(8,128)S(1)}, u32[]{:S(2)}, u32[]{:S(2)}) collective-permute-start(f32[128,256]{1,0:T(8,128)S(1)} %plus.5.refs_0_), channel_id=1, source_target_pairs={{0,2},{2,0},{1,3},{3,1},{4,6},{6,4},{5,7},{7,5},{8,10},{10,8},{9,1... | collective-permute-start | bytes 393224 | tf_op jit(solution)/shard_map/ppermute | solution.py:553
  70.8 0.1 operand.8
  70.9 4.0 %collective-permute-done.17.refs_1_ = f32[128,256]{1,0:T(8,128)S(1)} collective-permute-done((f32[128,256]{1,0:T(8,128)S(1)}, f32[128,256]{1,0:T(8,128)S(1)}, u32[]{:S(2)}, u32[]{:S(2)}) %collective-permute-start.17) | collective-permute-done | bytes 131104 | tf_op jit(solution)/shard_map/ppermute | solution.py:553
  74.9 0.7 side.7
  75.7 0.1 operand.9
  75.8 0.1 operand.10
  76.0 0.7 collective-permute-start.22
  76.7 5.3 %collective-permute-done.20.refs_1_ = bf16[256,1024]{1,0:T(8,128)(2,1)S(1)} collective-permute-done((bf16[256,1024]{1,0:T(8,128)(2,1)S(1)}, bf16[256,1024]{1,0:T(8,128)(2,1)S(1)}, u32[]{:S(2)}, u32[]{:S(2)}) %collective-permute-start.20) | collective-permute-done | bytes 524320 | tf_op jit(solution)/shard_map/ppermute | solution.py:631
  81.9 0.1 operand.11
  82.1 0.7 collective-permute-start.24
  82.8 5.7 %collective-permute-start.23 = (bf16[256,768]{1,0:T(8,128)(2,1)S(1)}, bf16[256,768]{1,0:T(8,128)(2,1)S(1)}, u32[]{:S(2)}, u32[]{:S(2)}) collective-permute-start(bf16[256,768]{1,0:T(8,128)(2,1)S(1)} %get-tuple-element.132), channel_id=1, source_target_pairs={{0,4},{8,12},{4,0},{12,8},{1,5},{9,13},{5,1},{13,9},{2,6},{10,14},... | collective-permute-start | bytes 1179656 | tf_op jit(solution)/shard_map/ppermute | solution.py:631
  88.4 0.1 collective-permute-start.25
  88.5 4.7 %collective-permute-done.21.refs_1_ = bf16[256,1024]{1,0:T(8,128)(2,1)S(1)} collective-permute-done((bf16[256,1024]{1,0:T(8,128)(2,1)S(1)}, bf16[256,1024]{1,0:T(8,128)(2,1)S(1)}, u32[]{:S(2)}, u32[]{:S(2)}) %collective-permute-start.21) | collective-permute-done | bytes 524320 | tf_op jit(solution)/shard_map/ppermute | solution.py:631
  93.2 0.0 collective-permute-done.22.refs_2_
  93.2 1.1 %keep.3.refs_3_ = f32[2048,256]{1,0:T(8,128)} custom-call(f32[32,8192]{1,0:T(8,128)S(1)} %get-tuple-element.135.scales.token.refs_0_, bf16[4,256,1024]{2,1,0:T(8,128)(2,1)S(1)} %get-tuple-element.102.refs_0_, bf16[256,1024]{1,0:T(8,128)(2,1)S(1)} %collective-permute-done.21.refs_1_, bf16[256,1024]{1,0:T(8,128)(2,1)S(1)} %collective-permute-done.22.refs_2_), custom_call_target="tpu_custom_call" | custom-call | flops 1 | bytes 1 | tf_op jit(solution)/shard_map/keep/pallas_call | solution.py:232
  94.3 7.3 %collective-permute-done.23.refs_1_ = bf16[256,768]{1,0:T(8,128)(2,1)S(1)} collective-permute-done((bf16[256,768]{1,0:T(8,128)(2,1)S(1)}, bf16[256,768]{1,0:T(8,128)(2,1)S(1)}, u32[]{:S(2)}, u32[]{:S(2)}) %collective-permute-start.23) | collective-permute-done | bytes 393248 | tf_op jit(solution)/shard_map/ppermute | solution.py:631
  101.6 0.0 collective-permute-done.24.refs_2_
  101.6 1.0 keep.4.refs_3_
  102.6 1.0 collective-permute-done.25.refs_1_
  103.6 0.9 keep.5
  (22 shorter events, 0.3 us)
Async XLA Ops:
  6.4 4.6 %collective-permute-start = (f32[256,256]{1,0:T(8,128)S(1)}, f32[256,256]{1,0:T(8,128)S(1)}, u32[]{:S(2)}, u32[]{:S(2)}) collective-permute-start(f32[256,256]{1,0:T(8,128)S(1)} %get-tuple-element.76.refs_0_), channel_id=1, source_target_pairs={{0,1},{1,0},{2,3},{3,2},{4,5},{5,4},{6,7},{7,6},{8,9},{9,8},{10,11... | collective-permute-start | bytes 786440 | tf_op jit(solution)/shard_map/ppermute | solution.py:553
  10.5 3.2 %collective-permute-start.2 = (f32[256,128]{1,0:T(8,128)S(1)}, f32[256,128]{1,0:T(8,128)S(1)}, u32[]{:S(2)}, u32[]{:S(2)}) collective-permute-start(f32[256,128]{1,0:T(8,128)S(1)} %get-tuple-element.80), channel_id=1, source_target_pairs={{0,1},{1,0},{2,3},{3,2},{4,5},{5,4},{6,7},{7,6},{8,9},{9,8},{10,11... | collective-permute-start | bytes 393224 | tf_op jit(solution)/shard_map/ppermute | solution.py:553
  10.6 3.1 %collective-permute-start.3 = (f32[256,128]{1,0:T(8,128)S(1)}, f32[256,128]{1,0:T(8,128)S(1)}, u32[]{:S(2)}, u32[]{:S(2)}) collective-permute-start(f32[256,128]{1,0:T(8,128)S(1)} %get-tuple-element.81), channel_id=1, source_target_pairs={{0,1},{1,0},{2,3},{3,2},{4,5},{5,4},{6,7},{7,6},{8,9},{9,8},{10,11... | collective-permute-start | bytes 393224 | tf_op jit(solution)/shard_map/ppermute | solution.py:553
  11.1 7.1 %collective-permute-start.1 = (f32[256,128]{1,0:T(8,128)S(1)}, f32[256,128]{1,0:T(8,128)S(1)}, u32[]{:S(2)}, u32[]{:S(2)}) collective-permute-start(f32[256,128]{1,0:T(8,128)S(1)} %half_sum.1), channel_id=1, source_target_pairs={{0,2},{2,0},{1,3},{3,1},{4,6},{6,4},{5,7},{7,5},{8,10},{10,8},{9,1... | collective-permute-start | bytes 393224 | tf_op jit(solution)/shard_map/ppermute | solution.py:553
  13.7 9.7 %collective-permute-start.7 = (f32[256,256]{1,0:T(8,128)S(1)}, f32[256,256]{1,0:T(8,128)S(1)}, u32[]{:S(2)}, u32[]{:S(2)}) collective-permute-start(f32[256,256]{1,0:T(8,128)S(1)} %plus.3), channel_id=1, source_target_pairs={{0,2},{2,0},{1,3},{3,1},{4,6},{6,4},{5,7},{7,5},{8,10},{10,8},{9,1... | collective-permute-start | bytes 786440 | tf_op jit(solution)/shard_map/ppermute | solution.py:553
  18.1 5.3 %copy-start = (bf16[1024,256]{1,0:T(8,128)(2,1)S(1)}, bf16[1024,256]{1,0:T(8,128)(2,1)}, u32[]{:S(2)}) copy-start(bf16[1024,256]{1,0:T(8,128)(2,1)} %refs_4_.1) | copy-start | bytes 1572868
  18.2 1.4 %collective-permute-start.4 = (f32[256,128]{1,0:T(8,128)S(1)}, f32[256,128]{1,0:T(8,128)S(1)}, u32[]{:S(2)}, u32[]{:S(2)}) collective-permute-start(f32[256,128]{1,0:T(8,128)S(1)} %add.3.refs_0_), channel_id=1, source_target_pairs={{0,1},{1,0},{2,3},{3,2},{4,5},{5,4},{6,7},{7,6},{8,9},{9,8},{10,11... | collective-permute-start | bytes 393224 | tf_op jit(solution)/shard_map/ppermute | solution.py:553
  18.3 4.9 %collective-permute-start.5 = (f32[256,128]{1,0:T(8,128)S(1)}, f32[256,128]{1,0:T(8,128)S(1)}, u32[]{:S(2)}, u32[]{:S(2)}) collective-permute-start(f32[256,128]{1,0:T(8,128)S(1)} %get-tuple-element.90), channel_id=1, source_target_pairs={{0,1},{1,0},{2,3},{3,2},{4,5},{5,4},{6,7},{7,6},{8,9},{9,8},{10,11... | collective-permute-start | bytes 393224 | tf_op jit(solution)/shard_map/ppermute | solution.py:553
  18.8 4.4 %collective-permute-start.6 = (f32[256,128]{1,0:T(8,128)S(1)}, f32[256,128]{1,0:T(8,128)S(1)}, u32[]{:S(2)}, u32[]{:S(2)}) collective-permute-start(f32[256,128]{1,0:T(8,128)S(1)} %get-tuple-element.91), channel_id=1, source_target_pairs={{0,1},{1,0},{2,3},{3,2},{4,5},{5,4},{6,7},{7,6},{8,9},{9,8},{10,11... | collective-permute-start | bytes 393224 | tf_op jit(solution)/shard_map/ppermute | solution.py:553
  24.5 5.5 %collective-permute-start.8 = (bf16[256,256]{1,0:T(8,128)(2,1)S(1)}, bf16[256,256]{1,0:T(8,128)(2,1)S(1)}, u32[]{:S(2)}, u32[]{:S(2)}) collective-permute-start(bf16[256,256]{1,0:T(8,128)(2,1)S(1)} %admm.1.refs_0_), channel_id=1, source_target_pairs={{0,2},{2,0},{1,3},{3,1},{4,6},{6,4},{5,7},{7,5},{8,10},{10,8},{9,1... | collective-permute-start | bytes 393224 | tf_op jit(solution)/shard_map/ppermute | solution.py:553
  30.0 2.2 %collective-permute-start.9 = (bf16[256,512]{1,0:T(8,128)(2,1)S(1)}, bf16[256,512]{1,0:T(8,128)(2,1)S(1)}, u32[]{:S(2)}, u32[]{:S(2)}) collective-permute-start(bf16[256,512]{1,0:T(8,128)(2,1)S(1)} %side.5.refs_0_), channel_id=1, source_target_pairs={{0,1},{1,0},{2,3},{3,2},{4,5},{5,4},{6,7},{7,6},{8,9},{9,8},{10,11... | collective-permute-start | bytes 786440 | tf_op jit(solution)/shard_map/ppermute | solution.py:553
  30.3 4.6 %collective-permute-start.10 = (bf16[128,256]{1,0:T(8,128)(2,1)S(1)}, bf16[128,256]{1,0:T(8,128)(2,1)S(1)}, u32[]{:S(2)}, u32[]{:S(2)}) collective-permute-start(bf16[128,256]{1,0:T(8,128)(2,1)S(1)} %row_share.1.refs_0_), channel_id=1, source_target_pairs={{0,4},{4,0},{8,12},{12,8},{1,5},{5,1},{9,13},{13,9},{2,6},{6,2},{1... | collective-permute-start | bytes 196616 | tf_op jit(solution)/shard_map/ppermute | solution.py:659
  33.2 15.2 %collective-permute-start.12 = (bf16[256,1024]{1,0:T(8,128)(2,1)S(1)}, bf16[256,1024]{1,0:T(8,128)(2,1)S(1)}, u32[]{:S(2)}, u32[]{:S(2)}) collective-permute-start(bf16[256,1024]{1,0:T(8,128)(2,1)S(1)} %products.4), channel_id=1, source_target_pairs={{0,4},{4,0},{8,12},{12,8},{1,5},{5,1},{9,13},{13,9},{2,6},{6,2},{1... | collective-permute-start | bytes 1572872 | tf_op jit(solution)/shard_map/ppermute | solution.py:631
  36.0 23.5 %collective-permute-start.14 = (bf16[256,1024]{1,0:T(8,128)(2,1)S(1)}, bf16[256,1024]{1,0:T(8,128)(2,1)S(1)}, u32[]{:S(2)}, u32[]{:S(2)}) collective-permute-start(bf16[256,1024]{1,0:T(8,128)(2,1)S(1)} %products.5), channel_id=1, source_target_pairs={{0,4},{12,8},{1,5},{13,9},{2,6},{14,10},{3,7},{15,11},{16,20},{28,... | collective-permute-start | bytes 1572872 | tf_op jit(solution)/shard_map/ppermute | solution.py:631
  39.6 4.6 %collective-permute-start.11 = (bf16[128,256]{1,0:T(8,128)(2,1)S(1)}, bf16[128,256]{1,0:T(8,128)(2,1)S(1)}, u32[]{:S(2)}, u32[]{:S(2)}) collective-permute-start(bf16[128,256]{1,0:T(8,128)(2,1)S(1)} %hop.3.refs_0_), channel_id=1, source_target_pairs={{4,8},{8,4},{5,9},{9,5},{6,10},{10,6},{7,11},{11,7},{20,24},{24,20... | collective-permute-start | bytes 196616 | tf_op jit(solution)/shard_map/ppermute | solution.py:659
  44.3 15.2 %collective-permute-start.13 = (bf16[128,256]{1,0:T(8,128)(2,1)S(1)}, bf16[128,256]{1,0:T(8,128)(2,1)S(1)}, u32[]{:S(2)}, u32[]{:S(2)}) collective-permute-start(bf16[128,256]{1,0:T(8,128)(2,1)S(1)} %hop.4.refs_0_), channel_id=1, source_target_pairs={{0,4},{4,0},{8,12},{12,8},{1,5},{5,1},{9,13},{13,9},{2,6},{6,2},{1... | collective-permute-start | bytes 196616 | tf_op jit(solution)/shard_map/ppermute | solution.py:659
  46.5 29.1 %collective-permute-start.18 = (bf16[256,1024]{1,0:T(8,128)(2,1)S(1)}, bf16[256,1024]{1,0:T(8,128)(2,1)S(1)}, u32[]{:S(2)}, u32[]{:S(2)}) collective-permute-start(bf16[256,1024]{1,0:T(8,128)(2,1)S(1)} %get-tuple-element.121), channel_id=1, source_target_pairs={{0,4},{12,8},{1,5},{13,9},{2,6},{14,10},{3,7},{15,11},{16,20},{28,... | collective-permute-start | bytes 1572872 | tf_op jit(solution)/shard_map/ppermute | solution.py:631
  48.6 22.2 %collective-permute-start.16 = (bf16[256,1024]{1,0:T(8,128)(2,1)S(1)}, bf16[256,1024]{1,0:T(8,128)(2,1)S(1)}, u32[]{:S(2)}, u32[]{:S(2)}) collective-permute-start(bf16[256,1024]{1,0:T(8,128)(2,1)S(1)} %operand.6), channel_id=1, source_target_pairs={{4,8},{8,4},{5,9},{9,5},{6,10},{10,6},{7,11},{11,7},{20,24},{24,20... | collective-permute-start | bytes 1572872 | tf_op jit(solution)/shard_map/ppermute | solution.py:631
  59.6 16.2 %collective-permute-start.19 = (bf16[256,1024]{1,0:T(8,128)(2,1)S(1)}, bf16[256,1024]{1,0:T(8,128)(2,1)S(1)}, u32[]{:S(2)}, u32[]{:S(2)}) collective-permute-start(bf16[256,1024]{1,0:T(8,128)(2,1)S(1)} %operand.7), channel_id=1, source_target_pairs={{4,8},{8,4},{5,9},{9,5},{6,10},{10,6},{7,11},{11,7},{20,24},{24,20... | collective-permute-start | bytes 1572872 | tf_op jit(solution)/shard_map/ppermute | solution.py:631
  60.3 21.6 %collective-permute-start.20 = (bf16[256,1024]{1,0:T(8,128)(2,1)S(1)}, bf16[256,1024]{1,0:T(8,128)(2,1)S(1)}, u32[]{:S(2)}, u32[]{:S(2)}) collective-permute-start(bf16[256,1024]{1,0:T(8,128)(2,1)S(1)} %get-tuple-element.127), channel_id=1, source_target_pairs={{0,4},{12,8},{1,5},{13,9},{2,6},{14,10},{3,7},{15,11},{16,20},{28,... | collective-permute-start | bytes 1572872 | tf_op jit(solution)/shard_map/ppermute | solution.py:631
  67.9 1.3 %collective-permute-start.15 = (bf16[128,256]{1,0:T(8,128)(2,1)S(1)}, bf16[128,256]{1,0:T(8,128)(2,1)S(1)}, u32[]{:S(2)}, u32[]{:S(2)}) collective-permute-start(bf16[128,256]{1,0:T(8,128)(2,1)S(1)} %hop.5.refs_0_), channel_id=1, source_target_pairs={{0,1},{1,0},{2,3},{3,2},{4,5},{5,4},{6,7},{7,6},{8,9},{9,8},{10,11... | collective-permute-start | bytes 196616 | tf_op jit(solution)/shard_map/ppermute | solution.py:553
  69.2 5.7 %collective-permute-start.17 = (f32[128,256]{1,0:T(8,128)S(1)}, f32[128,256]{1,0:T(8,128)S(1)}, u32[]{:S(2)}, u32[]{:S(2)}) collective-permute-start(f32[128,256]{1,0:T(8,128)S(1)} %plus.5.refs_0_), channel_id=1, source_target_pairs={{0,2},{2,0},{1,3},{3,1},{4,6},{6,4},{5,7},{7,5},{8,10},{10,8},{9,1... | collective-permute-start | bytes 393224 | tf_op jit(solution)/shard_map/ppermute | solution.py:553
  75.7 17.5 %collective-permute-start.21 = (bf16[256,1024]{1,0:T(8,128)(2,1)S(1)}, bf16[256,1024]{1,0:T(8,128)(2,1)S(1)}, u32[]{:S(2)}, u32[]{:S(2)}) collective-permute-start(bf16[256,1024]{1,0:T(8,128)(2,1)S(1)} %operand.8), channel_id=1, source_target_pairs={{0,4},{8,12},{4,0},{12,8},{1,5},{9,13},{5,1},{13,9},{2,6},{10,14},... | collective-permute-start | bytes 1572872 | tf_op jit(solution)/shard_map/ppermute | solution.py:631
  76.0 17.2 %collective-permute-start.22 = (bf16[256,1024]{1,0:T(8,128)(2,1)S(1)}, bf16[256,1024]{1,0:T(8,128)(2,1)S(1)}, u32[]{:S(2)}, u32[]{:S(2)}) collective-permute-start(bf16[256,1024]{1,0:T(8,128)(2,1)S(1)} %operand.9), channel_id=1, source_target_pairs={{4,8},{8,4},{5,9},{9,5},{6,10},{10,6},{7,11},{11,7},{20,24},{24,20... | collective-permute-start | bytes 1572872 | tf_op jit(solution)/shard_map/ppermute | solution.py:631
  82.1 19.5 %collective-permute-start.24 = (bf16[256,1024]{1,0:T(8,128)(2,1)S(1)}, bf16[256,1024]{1,0:T(8,128)(2,1)S(1)}, u32[]{:S(2)}, u32[]{:S(2)}) collective-permute-start(bf16[256,1024]{1,0:T(8,128)(2,1)S(1)} %operand.11), channel_id=1, source_target_pairs={{4,8},{8,4},{5,9},{9,5},{6,10},{10,6},{7,11},{11,7},{20,24},{24,20... | collective-permute-start | bytes 1572872 | tf_op jit(solution)/shard_map/ppermute | solution.py:631
  82.8 18.8 %collective-permute-start.23 = (bf16[256,768]{1,0:T(8,128)(2,1)S(1)}, bf16[256,768]{1,0:T(8,128)(2,1)S(1)}, u32[]{:S(2)}, u32[]{:S(2)}) collective-permute-start(bf16[256,768]{1,0:T(8,128)(2,1)S(1)} %get-tuple-element.132), channel_id=1, source_target_pairs={{0,4},{8,12},{4,0},{12,8},{1,5},{9,13},{5,1},{13,9},{2,6},{10,14},... | collective-permute-start | bytes 1179656 | tf_op jit(solution)/shard_map/ppermute | solution.py:631
  88.4 15.2 %collective-permute-start.25 = (bf16[256,256]{1,0:T(8,128)(2,1)S(1)}, bf16[256,256]{1,0:T(8,128)(2,1)S(1)}, u32[]{:S(2)}, u32[]{:S(2)}) collective-permute-start(bf16[256,256]{1,0:T(8,128)(2,1)S(1)} %get-tuple-element.136), channel_id=1, source_target_pairs={{0,4},{8,12},{4,0},{12,8},{1,5},{9,13},{5,1},{13,9},{2,6},{10,14},... | collective-permute-start | bytes 393224 | tf_op jit(solution)/shard_map/ppermute | solution.py:646

commit v18 on v17

--- a/solution.py
+++ b/solution.py
@@ -155,7 +155,7 @@
 
 def cross_rows(row_tiles, scales, counts, turned, total):
     columns = counts.shape[1]
-    wide = min(2048, columns)
+    wide = min(4096, columns)
     total[...] = jnp.zeros_like(total)
 
     @pl.loop(0, columns // wide)

time: 105 us -> 105 us (level)
  transfers between devices with their start and end apart: 26 -> 26, of which waited for: 11 -> 12; matrix products, arithmetic and copies ran while one was open for 0% -> 0% of each run, Pallas kernels for 24% -> 24%
where the time goes in v18:
time: 105 us; the launch traced here: 104 us
  starting transfers between devices  36.9 us (35%)
  waiting for transfers between devices  34.1 us (32%)
  Pallas kernels  32.5 us (31%)
    ppermute x10, starting transfers between devices, send(): lax.ppermute(value, 'cell', pairs)  22.9 us
    ppermute x10, waiting for transfers between devices, send(): lax.ppermute(value, 'cell', pairs)  17.2 us
    pallas_call x27, Pallas kernels, call(): pl.pallas_call(lambda token, *refs: kernel(*refs), out_shape=out_shape, i...  16.9 us
    ppermute x12, waiting for transfers between devices, swap(): return lax.ppermute(value, axis, [(i, i ^ step) for i in range(size)])  9.34 us
    ppermute x12, starting transfers between devices, swap(): return lax.ppermute(value, axis, [(i, i ^ step) for i in range(size)])  9.12 us
    ppermute x3, waiting for transfers between devices, hop_rows(): rows_arrived = lax.ppermute(rows_sum, 'cell', both)  6.6 us
    pallas_call x2, Pallas kernels, cross(): pl.pallas_call(functools.partial(cross_kernel, bit, kept, rows), out_shap...  6.29 us
    pallas_call x1, Pallas kernels, load(): pl.pallas_call(functools.partial(load_kernel, bit), out_shape=(jax.ShapeD...  5.81 us
  transfers between devices with their start and end apart: 26, of which 12 were waited for; matrix products, arithmetic and copies ran while one was open for 0% of the time, Pallas kernels for 24%

profile of v18, /device:TPU:0, one launch (start us, length us, event | category | flops | bytes accessed | tf_op | source)
XLA Modules:
  0.0 104.5 jit_solution(10786109781020776711)
XLA Ops:
  0.6 5.8 %load.1 = (f32[256,256]{1,0:T(8,128)S(1)}, f32[32,8192]{1,0:T(8,128)S(1)}, bf16[8192,256]{1,0:T(8,128)(2,1)S(1)}, bf16[512,8192]{1,0:T(8,128)(2,1)S(1)}) custom-call(bf16[256,8192]{1,0:T(8,128)(2,1)} %genes.1, bf16[1024,8192]{1,0:T(8,128)(2,1)} %refs_0_.1, s32[4,32]{1,0:T(4,128)} %tile_mask.1, s32[4,32]{1,0:T(4,128)} %tile_counts.1), custom_call_target="tpu_custom_call" | custom-call | flops 1 | bytes 1 | tf_op jit(solution)/shard_map/load/pallas_call | solution.py:118
  6.4 0.5 collective-permute-start
  7.0 3.5 %cross_sent.1 = (f32[256,128]{1,0:T(8,128)S(1)}, f32[256,128]{1,0:T(8,128)S(1)}, f32[256,256]{1,0:T(8,128)S(1)}, bf16[512,8192]{1,0:T(8,128)(2,1)S(1)}) custom-call(f32[32,8192]{1,0:T(8,128)S(1)} %get-tuple-element.135.scales.token.refs_0_, bf16[512,8192]{1,0:T(8,128)(2,1)S(1)} %get-tuple-element.72.held_rows.refs_1_, ...), custom_call_target="tpu_custom_call" | custom-call | flops 1 | bytes 1 | tf_op jit(solution)/shard_map/cross_sent/pallas_call | solution.py:206
  10.5 0.1 collective-permute-start.2
  10.6 0.5 collective-permute-start.3
  11.1 2.6 %collective-permute-start.1 = (f32[256,128]{1,0:T(8,128)S(1)}, f32[256,128]{1,0:T(8,128)S(1)}, u32[]{:S(2)}, u32[]{:S(2)}) collective-permute-start(f32[256,128]{1,0:T(8,128)S(1)} %half_sum.1), channel_id=1, source_target_pairs={{0,2},{2,0},{1,3},{3,1},{4,6},{6,4},{5,7},{7,5},{8,10},{10,8},{9,1... | collective-permute-start | bytes 393224 | tf_op jit(solution)/shard_map/ppermute | solution.py:553
  13.7 0.0 collective-permute-done.3.refs_2_
  13.7 1.2 %collective-permute-start.7 = (f32[256,256]{1,0:T(8,128)S(1)}, f32[256,256]{1,0:T(8,128)S(1)}, u32[]{:S(2)}, u32[]{:S(2)}) collective-permute-start(f32[256,256]{1,0:T(8,128)S(1)} %plus.3), channel_id=1, source_target_pairs={{0,2},{2,0},{1,3},{3,1},{4,6},{6,4},{5,7},{7,5},{8,10},{10,8},{9,1... | collective-permute-start | bytes 786440 | tf_op jit(solution)/shard_map/ppermute | solution.py:553
  15.0 2.8 %cross_kept.1 = (f32[256,128]{1,0:T(8,128)S(1)}, f32[256,128]{1,0:T(8,128)S(1)}, f32[256,256]{1,0:T(8,128)S(1)}) custom-call(f32[32,8192]{1,0:T(8,128)S(1)} %get-tuple-element.135.scales.token.refs_0_, bf16[512,8192]{1,0:T(8,128)(2,1)S(1)} %get-tuple-element.83.held_rows.refs_2_, bf16[8192,256]{1,0:T(8,128)(2,1)S(1)} %get-tuple-element.73.turned), custom_call_target="tpu_custom_call" | custom-call | flops 1 | bytes 1 | tf_op jit(solution)/shard_map/cross_kept/pallas_call | solution.py:206
  17.8 0.0 copy-start
  17.8 0.3 collective-permute-done.1
  18.1 0.1 collective-permute-start.4
  18.1 0.5 collective-permute-start.5
  18.6 0.1 collective-permute-start.6
  18.7 0.8 collective-permute-done.4.refs_1_
  19.5 3.5 %inverse.1 = (f32[256,256]{1,0:T(8,128)S(1)}, f32[8,128]{1,0:T(8,128)S(1)}) custom-call(f32[256,256]{1,0:T(8,128)S(1)} %side.4.gram_in), custom_call_target="tpu_custom_call" | custom-call | flops 1 | bytes 1 | tf_op jit(solution)/shard_map/inverse/pallas_call | solution.py:359
  23.0 0.0 collective-permute-done.6.refs_2_
  23.1 0.3 collective-permute-done.7.refs_2_
  23.4 1.0 admm.1.refs_0_
  24.5 1.8 %collective-permute-start.8 = (bf16[256,256]{1,0:T(8,128)(2,1)S(1)}, bf16[256,256]{1,0:T(8,128)(2,1)S(1)}, u32[]{:S(2)}, u32[]{:S(2)}) collective-permute-start(bf16[256,256]{1,0:T(8,128)(2,1)S(1)} %admm.1.refs_0_), channel_id=1, source_target_pairs={{0,2},{2,0},{1,3},{3,1},{4,6},{6,4},{5,7},{7,5},{8,10},{10,8},{9,1... | collective-permute-start | bytes 393224 | tf_op jit(solution)/shard_map/ppermute | solution.py:553
  26.3 3.7 %collective-permute-done.8.refs_1_ = bf16[256,256]{1,0:T(8,128)(2,1)S(1)} collective-permute-done((bf16[256,256]{1,0:T(8,128)(2,1)S(1)}, bf16[256,256]{1,0:T(8,128)(2,1)S(1)}, u32[]{:S(2)}, u32[]{:S(2)}) %collective-permute-start.8) | collective-permute-done | bytes 131104 | tf_op jit(solution)/shard_map/ppermute | solution.py:553
  30.0 0.1 collective-permute-start.9
  30.1 0.2 row_share.1.refs_0_
  30.3 1.9 %collective-permute-start.10 = (bf16[128,256]{1,0:T(8,128)(2,1)S(1)}, bf16[128,256]{1,0:T(8,128)(2,1)S(1)}, u32[]{:S(2)}, u32[]{:S(2)}) collective-permute-start(bf16[128,256]{1,0:T(8,128)(2,1)S(1)} %row_share.1.refs_0_), channel_id=1, source_target_pairs={{0,4},{4,0},{8,12},{12,8},{1,5},{5,1},{9,13},{13,9},{2,6},{6,2},{1... | collective-permute-start | bytes 196616 | tf_op jit(solution)/shard_map/ppermute | solution.py:659
  32.3 1.0 products.4
  33.2 1.3 %collective-permute-start.12 = (bf16[256,1024]{1,0:T(8,128)(2,1)S(1)}, bf16[256,1024]{1,0:T(8,128)(2,1)S(1)}, u32[]{:S(2)}, u32[]{:S(2)}) collective-permute-start(bf16[256,1024]{1,0:T(8,128)(2,1)S(1)} %products.4), channel_id=1, source_target_pairs={{0,4},{4,0},{8,12},{12,8},{1,5},{5,1},{9,13},{13,9},{2,6},{6,2},{1... | collective-permute-start | bytes 1572872 | tf_op jit(solution)/shard_map/ppermute | solution.py:631
  34.5 0.4 collective-permute-done.10.refs_1_
  35.0 1.0 products.5
  36.0 3.7 %collective-permute-start.14 = (bf16[256,1024]{1,0:T(8,128)(2,1)S(1)}, bf16[256,1024]{1,0:T(8,128)(2,1)S(1)}, u32[]{:S(2)}, u32[]{:S(2)}) collective-permute-start(bf16[256,1024]{1,0:T(8,128)(2,1)S(1)} %products.5), channel_id=1, source_target_pairs={{0,4},{12,8},{1,5},{13,9},{2,6},{14,10},{3,7},{15,11},{16,20},{28,... | collective-permute-start | bytes 1572872 | tf_op jit(solution)/shard_map/ppermute | solution.py:631
  39.6 0.7 collective-permute-start.11
  40.3 3.9 %products.6 = (bf16[4,256,1024]{2,1,0:T(8,128)(2,1)S(1)}, bf16[256,1024]{1,0:T(8,128)(2,1)S(1)}) custom-call(f32[32,8192]{1,0:T(8,128)S(1)} %get-tuple-element.135.scales.token.refs_0_, f32[32,8192]{1,0:T(8,128)S(1)} %get-tuple-element.135.scales.token.refs_0_, bf16[512,8192]{1,0:T(8,128)(2,1)S(1)} %get-tuple-element.72.held_rows.refs_1_, ...), custom_call_target="tpu_custom_call" | custom-call | flops 1 | bytes 1 | tf_op jit(solution)/shard_map/products/pallas_call | solution.py:232
  44.3 2.2 %collective-permute-start.13 = (bf16[128,256]{1,0:T(8,128)(2,1)S(1)}, bf16[128,256]{1,0:T(8,128)(2,1)S(1)}, u32[]{:S(2)}, u32[]{:S(2)}) collective-permute-start(bf16[128,256]{1,0:T(8,128)(2,1)S(1)} %hop.4.refs_0_), channel_id=1, source_target_pairs={{0,4},{4,0},{8,12},{12,8},{1,5},{5,1},{9,13},{13,9},{2,6},{6,2},{1... | collective-permute-start | bytes 196616 | tf_op jit(solution)/shard_map/ppermute | solution.py:659
  46.5 1.9 %collective-permute-start.18 = (bf16[256,1024]{1,0:T(8,128)(2,1)S(1)}, bf16[256,1024]{1,0:T(8,128)(2,1)S(1)}, u32[]{:S(2)}, u32[]{:S(2)}) collective-permute-start(bf16[256,1024]{1,0:T(8,128)(2,1)S(1)} %get-tuple-element.121), channel_id=1, source_target_pairs={{0,4},{12,8},{1,5},{13,9},{2,6},{14,10},{3,7},{15,11},{16,20},{28,... | collective-permute-start | bytes 1572872 | tf_op jit(solution)/shard_map/ppermute | solution.py:631
  48.5 0.0 collective-permute-done.12.refs_1_
  48.5 0.1 operand.6
  48.6 0.7 collective-permute-start.16
  49.3 3.9 %products.7 = (bf16[4,256,1024]{2,1,0:T(8,128)(2,1)S(1)}, bf16[256,1024]{1,0:T(8,128)(2,1)S(1)}) custom-call(f32[32,8192]{1,0:T(8,128)S(1)} %get-tuple-element.135.scales.token.refs_0_, f32[32,8192]{1,0:T(8,128)S(1)} %get-tuple-element.135.scales.token.refs_0_, bf16[512,8192]{1,0:T(8,128)(2,1)S(1)} %get-tuple-element.72.held_rows.refs_1_, ...), custom_call_target="tpu_custom_call" | custom-call | flops 1 | bytes 1 | tf_op jit(solution)/shard_map/products/pallas_call | solution.py:232
  53.3 6.2 %collective-permute-done.13.refs_1_ = bf16[128,256]{1,0:T(8,128)(2,1)S(1)} collective-permute-done((bf16[128,256]{1,0:T(8,128)(2,1)S(1)}, bf16[128,256]{1,0:T(8,128)(2,1)S(1)}, u32[]{:S(2)}, u32[]{:S(2)}) %collective-permute-start.13) | collective-permute-done | bytes 65568 | tf_op jit(solution)/shard_map/ppermute | solution.py:659
  59.5 0.1 operand.7
  59.6 0.7 collective-permute-start.19
  60.3 7.5 %collective-permute-start.20 = (bf16[256,1024]{1,0:T(8,128)(2,1)S(1)}, bf16[256,1024]{1,0:T(8,128)(2,1)S(1)}, u32[]{:S(2)}, u32[]{:S(2)}) collective-permute-start(bf16[256,1024]{1,0:T(8,128)(2,1)S(1)} %get-tuple-element.127), channel_id=1, source_target_pairs={{0,4},{12,8},{1,5},{13,9},{2,6},{14,10},{3,7},{15,11},{16,20},{28,... | collective-permute-start | bytes 1572872 | tf_op jit(solution)/shard_map/ppermute | solution.py:631
  67.9 0.1 collective-permute-start.15
  68.0 1.0 turn.1
  69.0 0.2 collective-permute-done.15.refs_1_
  69.2 1.6 %collective-permute-start.17 = (f32[128,256]{1,0:T(8,128)S(1)}, f32[128,256]{1,0:T(8,128)S(1)}, u32[]{:S(2)}, u32[]{:S(2)}) collective-permute-start(f32[128,256]{1,0:T(8,128)S(1)} %plus.5.refs_0_), channel_id=1, source_target_pairs={{0,2},{2,0},{1,3},{3,1},{4,6},{6,4},{5,7},{7,5},{8,10},{10,8},{9,1... | collective-permute-start | bytes 393224 | tf_op jit(solution)/shard_map/ppermute | solution.py:553
  70.8 0.1 operand.8
  70.9 4.0 %collective-permute-done.17.refs_1_ = f32[128,256]{1,0:T(8,128)S(1)} collective-permute-done((f32[128,256]{1,0:T(8,128)S(1)}, f32[128,256]{1,0:T(8,128)S(1)}, u32[]{:S(2)}, u32[]{:S(2)}) %collective-permute-start.17) | collective-permute-done | bytes 131104 | tf_op jit(solution)/shard_map/ppermute | solution.py:553
  74.9 0.7 side.7
  75.7 0.1 operand.9
  75.8 0.1 operand.10
  76.0 0.7 collective-permute-start.22
  76.7 5.3 %collective-permute-done.20.refs_1_ = bf16[256,1024]{1,0:T(8,128)(2,1)S(1)} collective-permute-done((bf16[256,1024]{1,0:T(8,128)(2,1)S(1)}, bf16[256,1024]{1,0:T(8,128)(2,1)S(1)}, u32[]{:S(2)}, u32[]{:S(2)}) %collective-permute-start.20) | collective-permute-done | bytes 524320 | tf_op jit(solution)/shard_map/ppermute | solution.py:631
  81.9 0.1 operand.11
  82.1 0.7 collective-permute-start.24
  82.8 5.7 %collective-permute-start.23 = (bf16[256,768]{1,0:T(8,128)(2,1)S(1)}, bf16[256,768]{1,0:T(8,128)(2,1)S(1)}, u32[]{:S(2)}, u32[]{:S(2)}) collective-permute-start(bf16[256,768]{1,0:T(8,128)(2,1)S(1)} %get-tuple-element.132), channel_id=1, source_target_pairs={{0,4},{8,12},{4,0},{12,8},{1,5},{9,13},{5,1},{13,9},{2,6},{10,14},... | collective-permute-start | bytes 1179656 | tf_op jit(solution)/shard_map/ppermute | solution.py:631
  88.4 0.1 collective-permute-start.25
  88.5 4.7 %collective-permute-done.21.refs_1_ = bf16[256,1024]{1,0:T(8,128)(2,1)S(1)} collective-permute-done((bf16[256,1024]{1,0:T(8,128)(2,1)S(1)}, bf16[256,1024]{1,0:T(8,128)(2,1)S(1)}, u32[]{:S(2)}, u32[]{:S(2)}) %collective-permute-start.21) | collective-permute-done | bytes 524320 | tf_op jit(solution)/shard_map/ppermute | solution.py:631
  93.2 0.0 collective-permute-done.22.refs_2_
  93.2 1.1 %keep.3.refs_3_ = f32[2048,256]{1,0:T(8,128)} custom-call(f32[32,8192]{1,0:T(8,128)S(1)} %get-tuple-element.135.scales.token.refs_0_, bf16[4,256,1024]{2,1,0:T(8,128)(2,1)S(1)} %get-tuple-element.102.refs_0_, bf16[256,1024]{1,0:T(8,128)(2,1)S(1)} %collective-permute-done.21.refs_1_, bf16[256,1024]{1,0:T(8,128)(2,1)S(1)} %collective-permute-done.22.refs_2_), custom_call_target="tpu_custom_call" | custom-call | flops 1 | bytes 1 | tf_op jit(solution)/shard_map/keep/pallas_call | solution.py:232
  94.3 7.3 %collective-permute-done.23.refs_1_ = bf16[256,768]{1,0:T(8,128)(2,1)S(1)} collective-permute-done((bf16[256,768]{1,0:T(8,128)(2,1)S(1)}, bf16[256,768]{1,0:T(8,128)(2,1)S(1)}, u32[]{:S(2)}, u32[]{:S(2)}) %collective-permute-start.23) | collective-permute-done | bytes 393248 | tf_op jit(solution)/shard_map/ppermute | solution.py:631
  101.6 0.0 collective-permute-done.24.refs_2_
  101.6 1.0 keep.4.refs_3_
  102.6 1.0 collective-permute-done.25.refs_1_
  103.6 0.9 keep.5
  (22 shorter events, 0.3 us)
Async XLA Ops:
  6.4 4.6 %collective-permute-start = (f32[256,256]{1,0:T(8,128)S(1)}, f32[256,256]{1,0:T(8,128)S(1)}, u32[]{:S(2)}, u32[]{:S(2)}) collective-permute-start(f32[256,256]{1,0:T(8,128)S(1)} %get-tuple-element.76.refs_0_), channel_id=1, source_target_pairs={{0,1},{1,0},{2,3},{3,2},{4,5},{5,4},{6,7},{7,6},{8,9},{9,8},{10,11... | collective-permute-start | bytes 786440 | tf_op jit(solution)/shard_map/ppermute | solution.py:553
  10.5 3.2 %collective-permute-start.2 = (f32[256,128]{1,0:T(8,128)S(1)}, f32[256,128]{1,0:T(8,128)S(1)}, u32[]{:S(2)}, u32[]{:S(2)}) collective-permute-start(f32[256,128]{1,0:T(8,128)S(1)} %get-tuple-element.80), channel_id=1, source_target_pairs={{0,1},{1,0},{2,3},{3,2},{4,5},{5,4},{6,7},{7,6},{8,9},{9,8},{10,11... | collective-permute-start | bytes 393224 | tf_op jit(solution)/shard_map/ppermute | solution.py:553
  10.6 3.1 %collective-permute-start.3 = (f32[256,128]{1,0:T(8,128)S(1)}, f32[256,128]{1,0:T(8,128)S(1)}, u32[]{:S(2)}, u32[]{:S(2)}) collective-permute-start(f32[256,128]{1,0:T(8,128)S(1)} %get-tuple-element.81), channel_id=1, source_target_pairs={{0,1},{1,0},{2,3},{3,2},{4,5},{5,4},{6,7},{7,6},{8,9},{9,8},{10,11... | collective-permute-start | bytes 393224 | tf_op jit(solution)/shard_map/ppermute | solution.py:553
  11.1 7.0 %collective-permute-start.1 = (f32[256,128]{1,0:T(8,128)S(1)}, f32[256,128]{1,0:T(8,128)S(1)}, u32[]{:S(2)}, u32[]{:S(2)}) collective-permute-start(f32[256,128]{1,0:T(8,128)S(1)} %half_sum.1), channel_id=1, source_target_pairs={{0,2},{2,0},{1,3},{3,1},{4,6},{6,4},{5,7},{7,5},{8,10},{10,8},{9,1... | collective-permute-start | bytes 393224 | tf_op jit(solution)/shard_map/ppermute | solution.py:553
  13.7 9.7 %collective-permute-start.7 = (f32[256,256]{1,0:T(8,128)S(1)}, f32[256,256]{1,0:T(8,128)S(1)}, u32[]{:S(2)}, u32[]{:S(2)}) collective-permute-start(f32[256,256]{1,0:T(8,128)S(1)} %plus.3), channel_id=1, source_target_pairs={{0,2},{2,0},{1,3},{3,1},{4,6},{6,4},{5,7},{7,5},{8,10},{10,8},{9,1... | collective-permute-start | bytes 786440 | tf_op jit(solution)/shard_map/ppermute | solution.py:553
  17.8 5.6 %copy-start = (bf16[1024,256]{1,0:T(8,128)(2,1)S(1)}, bf16[1024,256]{1,0:T(8,128)(2,1)}, u32[]{:S(2)}) copy-start(bf16[1024,256]{1,0:T(8,128)(2,1)} %refs_4_.1) | copy-start | bytes 1572868
  18.1 1.4 %collective-permute-start.4 = (f32[256,128]{1,0:T(8,128)S(1)}, f32[256,128]{1,0:T(8,128)S(1)}, u32[]{:S(2)}, u32[]{:S(2)}) collective-permute-start(f32[256,128]{1,0:T(8,128)S(1)} %add.3.refs_0_), channel_id=1, source_target_pairs={{0,1},{1,0},{2,3},{3,2},{4,5},{5,4},{6,7},{7,6},{8,9},{9,8},{10,11... | collective-permute-start | bytes 393224 | tf_op jit(solution)/shard_map/ppermute | solution.py:553
  18.1 4.9 %collective-permute-start.5 = (f32[256,128]{1,0:T(8,128)S(1)}, f32[256,128]{1,0:T(8,128)S(1)}, u32[]{:S(2)}, u32[]{:S(2)}) collective-permute-start(f32[256,128]{1,0:T(8,128)S(1)} %get-tuple-element.90), channel_id=1, source_target_pairs={{0,1},{1,0},{2,3},{3,2},{4,5},{5,4},{6,7},{7,6},{8,9},{9,8},{10,11... | collective-permute-start | bytes 393224 | tf_op jit(solution)/shard_map/ppermute | solution.py:553
  18.6 4.4 %collective-permute-start.6 = (f32[256,128]{1,0:T(8,128)S(1)}, f32[256,128]{1,0:T(8,128)S(1)}, u32[]{:S(2)}, u32[]{:S(2)}) collective-permute-start(f32[256,128]{1,0:T(8,128)S(1)} %get-tuple-element.91), channel_id=1, source_target_pairs={{0,1},{1,0},{2,3},{3,2},{4,5},{5,4},{6,7},{7,6},{8,9},{9,8},{10,11... | collective-permute-start | bytes 393224 | tf_op jit(solution)/shard_map/ppermute | solution.py:553
  24.5 5.5 %collective-permute-start.8 = (bf16[256,256]{1,0:T(8,128)(2,1)S(1)}, bf16[256,256]{1,0:T(8,128)(2,1)S(1)}, u32[]{:S(2)}, u32[]{:S(2)}) collective-permute-start(bf16[256,256]{1,0:T(8,128)(2,1)S(1)} %admm.1.refs_0_), channel_id=1, source_target_pairs={{0,2},{2,0},{1,3},{3,1},{4,6},{6,4},{5,7},{7,5},{8,10},{10,8},{9,1... | collective-permute-start | bytes 393224 | tf_op jit(solution)/shard_map/ppermute | solution.py:553
  30.0 2.2 %collective-permute-start.9 = (bf16[256,512]{1,0:T(8,128)(2,1)S(1)}, bf16[256,512]{1,0:T(8,128)(2,1)S(1)}, u32[]{:S(2)}, u32[]{:S(2)}) collective-permute-start(bf16[256,512]{1,0:T(8,128)(2,1)S(1)} %side.5.refs_0_), channel_id=1, source_target_pairs={{0,1},{1,0},{2,3},{3,2},{4,5},{5,4},{6,7},{7,6},{8,9},{9,8},{10,11... | collective-permute-start | bytes 786440 | tf_op jit(solution)/shard_map/ppermute | solution.py:553
  30.3 4.6 %collective-permute-start.10 = (bf16[128,256]{1,0:T(8,128)(2,1)S(1)}, bf16[128,256]{1,0:T(8,128)(2,1)S(1)}, u32[]{:S(2)}, u32[]{:S(2)}) collective-permute-start(bf16[128,256]{1,0:T(8,128)(2,1)S(1)} %row_share.1.refs_0_), channel_id=1, source_target_pairs={{0,4},{4,0},{8,12},{12,8},{1,5},{5,1},{9,13},{13,9},{2,6},{6,2},{1... | collective-permute-start | bytes 196616 | tf_op jit(solution)/shard_map/ppermute | solution.py:659
  33.2 15.2 %collective-permute-start.12 = (bf16[256,1024]{1,0:T(8,128)(2,1)S(1)}, bf16[256,1024]{1,0:T(8,128)(2,1)S(1)}, u32[]{:S(2)}, u32[]{:S(2)}) collective-permute-start(bf16[256,1024]{1,0:T(8,128)(2,1)S(1)} %products.4), channel_id=1, source_target_pairs={{0,4},{4,0},{8,12},{12,8},{1,5},{5,1},{9,13},{13,9},{2,6},{6,2},{1... | collective-permute-start | bytes 1572872 | tf_op jit(solution)/shard_map/ppermute | solution.py:631
  36.0 23.5 %collective-permute-start.14 = (bf16[256,1024]{1,0:T(8,128)(2,1)S(1)}, bf16[256,1024]{1,0:T(8,128)(2,1)S(1)}, u32[]{:S(2)}, u32[]{:S(2)}) collective-permute-start(bf16[256,1024]{1,0:T(8,128)(2,1)S(1)} %products.5), channel_id=1, source_target_pairs={{0,4},{12,8},{1,5},{13,9},{2,6},{14,10},{3,7},{15,11},{16,20},{28,... | collective-permute-start | bytes 1572872 | tf_op jit(solution)/shard_map/ppermute | solution.py:631
  39.6 4.6 %collective-permute-start.11 = (bf16[128,256]{1,0:T(8,128)(2,1)S(1)}, bf16[128,256]{1,0:T(8,128)(2,1)S(1)}, u32[]{:S(2)}, u32[]{:S(2)}) collective-permute-start(bf16[128,256]{1,0:T(8,128)(2,1)S(1)} %hop.3.refs_0_), channel_id=1, source_target_pairs={{4,8},{8,4},{5,9},{9,5},{6,10},{10,6},{7,11},{11,7},{20,24},{24,20... | collective-permute-start | bytes 196616 | tf_op jit(solution)/shard_map/ppermute | solution.py:659
  44.3 15.2 %collective-permute-start.13 = (bf16[128,256]{1,0:T(8,128)(2,1)S(1)}, bf16[128,256]{1,0:T(8,128)(2,1)S(1)}, u32[]{:S(2)}, u32[]{:S(2)}) collective-permute-start(bf16[128,256]{1,0:T(8,128)(2,1)S(1)} %hop.4.refs_0_), channel_id=1, source_target_pairs={{0,4},{4,0},{8,12},{12,8},{1,5},{5,1},{9,13},{13,9},{2,6},{6,2},{1... | collective-permute-start | bytes 196616 | tf_op jit(solution)/shard_map/ppermute | solution.py:659
  46.5 29.1 %collective-permute-start.18 = (bf16[256,1024]{1,0:T(8,128)(2,1)S(1)}, bf16[256,1024]{1,0:T(8,128)(2,1)S(1)}, u32[]{:S(2)}, u32[]{:S(2)}) collective-permute-start(bf16[256,1024]{1,0:T(8,128)(2,1)S(1)} %get-tuple-element.121), channel_id=1, source_target_pairs={{0,4},{12,8},{1,5},{13,9},{2,6},{14,10},{3,7},{15,11},{16,20},{28,... | collective-permute-start | bytes 1572872 | tf_op jit(solution)/shard_map/ppermute | solution.py:631
  48.6 22.2 %collective-permute-start.16 = (bf16[256,1024]{1,0:T(8,128)(2,1)S(1)}, bf16[256,1024]{1,0:T(8,128)(2,1)S(1)}, u32[]{:S(2)}, u32[]{:S(2)}) collective-permute-start(bf16[256,1024]{1,0:T(8,128)(2,1)S(1)} %operand.6), channel_id=1, source_target_pairs={{4,8},{8,4},{5,9},{9,5},{6,10},{10,6},{7,11},{11,7},{20,24},{24,20... | collective-permute-start | bytes 1572872 | tf_op jit(solution)/shard_map/ppermute | solution.py:631
  59.6 16.2 %collective-permute-start.19 = (bf16[256,1024]{1,0:T(8,128)(2,1)S(1)}, bf16[256,1024]{1,0:T(8,128)(2,1)S(1)}, u32[]{:S(2)}, u32[]{:S(2)}) collective-permute-start(bf16[256,1024]{1,0:T(8,128)(2,1)S(1)} %operand.7), channel_id=1, source_target_pairs={{4,8},{8,4},{5,9},{9,5},{6,10},{10,6},{7,11},{11,7},{20,24},{24,20... | collective-permute-start | bytes 1572872 | tf_op jit(solution)/shard_map/ppermute | solution.py:631
  60.3 21.6 %collective-permute-start.20 = (bf16[256,1024]{1,0:T(8,128)(2,1)S(1)}, bf16[256,1024]{1,0:T(8,128)(2,1)S(1)}, u32[]{:S(2)}, u32[]{:S(2)}) collective-permute-start(bf16[256,1024]{1,0:T(8,128)(2,1)S(1)} %get-tuple-element.127), channel_id=1, source_target_pairs={{0,4},{12,8},{1,5},{13,9},{2,6},{14,10},{3,7},{15,11},{16,20},{28,... | collective-permute-start | bytes 1572872 | tf_op jit(solution)/shard_map/ppermute | solution.py:631
  67.9 1.3 %collective-permute-start.15 = (bf16[128,256]{1,0:T(8,128)(2,1)S(1)}, bf16[128,256]{1,0:T(8,128)(2,1)S(1)}, u32[]{:S(2)}, u32[]{:S(2)}) collective-permute-start(bf16[128,256]{1,0:T(8,128)(2,1)S(1)} %hop.5.refs_0_), channel_id=1, source_target_pairs={{0,1},{1,0},{2,3},{3,2},{4,5},{5,4},{6,7},{7,6},{8,9},{9,8},{10,11... | collective-permute-start | bytes 196616 | tf_op jit(solution)/shard_map/ppermute | solution.py:553
  69.2 5.7 %collective-permute-start.17 = (f32[128,256]{1,0:T(8,128)S(1)}, f32[128,256]{1,0:T(8,128)S(1)}, u32[]{:S(2)}, u32[]{:S(2)}) collective-permute-start(f32[128,256]{1,0:T(8,128)S(1)} %plus.5.refs_0_), channel_id=1, source_target_pairs={{0,2},{2,0},{1,3},{3,1},{4,6},{6,4},{5,7},{7,5},{8,10},{10,8},{9,1... | collective-permute-start | bytes 393224 | tf_op jit(solution)/shard_map/ppermute | solution.py:553
  75.7 17.5 %collective-permute-start.21 = (bf16[256,1024]{1,0:T(8,128)(2,1)S(1)}, bf16[256,1024]{1,0:T(8,128)(2,1)S(1)}, u32[]{:S(2)}, u32[]{:S(2)}) collective-permute-start(bf16[256,1024]{1,0:T(8,128)(2,1)S(1)} %operand.8), channel_id=1, source_target_pairs={{0,4},{8,12},{4,0},{12,8},{1,5},{9,13},{5,1},{13,9},{2,6},{10,14},... | collective-permute-start | bytes 1572872 | tf_op jit(solution)/shard_map/ppermute | solution.py:631
  76.0 17.2 %collective-permute-start.22 = (bf16[256,1024]{1,0:T(8,128)(2,1)S(1)}, bf16[256,1024]{1,0:T(8,128)(2,1)S(1)}, u32[]{:S(2)}, u32[]{:S(2)}) collective-permute-start(bf16[256,1024]{1,0:T(8,128)(2,1)S(1)} %operand.9), channel_id=1, source_target_pairs={{4,8},{8,4},{5,9},{9,5},{6,10},{10,6},{7,11},{11,7},{20,24},{24,20... | collective-permute-start | bytes 1572872 | tf_op jit(solution)/shard_map/ppermute | solution.py:631
  82.1 19.5 %collective-permute-start.24 = (bf16[256,1024]{1,0:T(8,128)(2,1)S(1)}, bf16[256,1024]{1,0:T(8,128)(2,1)S(1)}, u32[]{:S(2)}, u32[]{:S(2)}) collective-permute-start(bf16[256,1024]{1,0:T(8,128)(2,1)S(1)} %operand.11), channel_id=1, source_target_pairs={{4,8},{8,4},{5,9},{9,5},{6,10},{10,6},{7,11},{11,7},{20,24},{24,20... | collective-permute-start | bytes 1572872 | tf_op jit(solution)/shard_map/ppermute | solution.py:631
  82.8 18.8 %collective-permute-start.23 = (bf16[256,768]{1,0:T(8,128)(2,1)S(1)}, bf16[256,768]{1,0:T(8,128)(2,1)S(1)}, u32[]{:S(2)}, u32[]{:S(2)}) collective-permute-start(bf16[256,768]{1,0:T(8,128)(2,1)S(1)} %get-tuple-element.132), channel_id=1, source_target_pairs={{0,4},{8,12},{4,0},{12,8},{1,5},{9,13},{5,1},{13,9},{2,6},{10,14},... | collective-permute-start | bytes 1179656 | tf_op jit(solution)/shard_map/ppermute | solution.py:631
  88.4 15.2 %collective-permute-start.25 = (bf16[256,256]{1,0:T(8,128)(2,1)S(1)}, bf16[256,256]{1,0:T(8,128)(2,1)S(1)}, u32[]{:S(2)}, u32[]{:S(2)}) collective-permute-start(bf16[256,256]{1,0:T(8,128)(2,1)S(1)} %get-tuple-element.136), channel_id=1, source_target_pairs={{0,4},{8,12},{4,0},{12,8},{1,5},{9,13},{5,1},{13,9},{2,6},{10,14},... | collective-permute-start | bytes 393224 | tf_op jit(solution)/shard_map/ppermute | solution.py:646
